TPU v7x, 32 devices: a whole 2x2x4 slice. The times are simulated.
32 devices in a mesh: groups: 2 (over y), rows: 4 (over z), feat: 2 (over x), ent: 2 (over core).
Axes of the slice: x: 2, y: 2, z: 4, core: 2. Of those that a mesh axis runs over, the one named last changes fastest.
Arguments:
- features: bfloat16 [16384, 4096], P(('groups', 'rows', 'ent'), 'feat'), parts along dimension 0, may hold values from -6 to 6
- global_weight: bfloat16 [8192], P(('groups', 'feat')), parts along dimension 0, may hold values from -0.09375 to 0.09375
- entity_feats: bfloat16 [16384, 512], P(('groups', 'rows', 'ent'), 'feat'), parts along dimension 0, may hold values from -6 to 6
- coefs: float32 [8192, 512], P(('groups', 'rows', 'ent'), 'feat'), parts along dimension 0, may hold values from -0.4 to 0.4
- member_owner: int32 [16384, 1], P(('groups', 'rows', 'ent')), parts along dimension 0, may hold values from 0 to 7; in each aligned block of 1024 rows (0 to 1023, 1024 to 2047, ...) at most 256 rows name the same one
- member_local: int32 [16384], P(('groups', 'rows', 'ent')), parts along dimension 0, may hold values from 0 to 511
- item_owner: int32 [16384, 1], P(('groups', 'rows', 'ent')), parts along dimension 0, may hold values from 0 to 7; in each aligned block of 1024 rows (0 to 1023, 1024 to 2047, ...) at most 256 rows name the same one
- item_local: int32 [16384], P(('groups', 'rows', 'ent')), parts along dimension 0, may hold values from 0 to 511
- clicks: int32 [16384], P(('groups', 'rows', 'ent')), parts along dimension 0, may hold values from 0 to 1
- valid: int32 [16384], P(('groups', 'rows', 'ent')), parts along dimension 0, may hold values 0 or 1
Outputs:
- grad_global: float32 [8192], P(('groups', 'feat')), parts along dimension 0
- grad_coefs: float32 [8192, 512], P(('groups', 'rows', 'ent'), 'feat'), parts along dimension 0
There are 2 independent parts, one for each index of `groups`. A program takes and returns all parts, laid end to end along the dimension named above; each array names one. Nothing has to cross between parts.
Inputs may be any that keep to these rules, and one draw needn't show every extreme that they name: `member_owner`: in the rows of one device no owner is named by more than 256 rows. `item_owner`: in the rows of one device no owner is named by more than 256 rows.
All inputs are finite; a program needn't handle non-finite values. No bound on the sum of `valid` on one device may be relied on, other than what follows from the above.
Results may differ from a plain program's by a relative error of at most 0.0023.
Values may be sent and summed in bfloat16 or wider, within the bound.
No kernel may reach another device: no remote copies, remote signals or barrier semaphores. Data moves between devices by JAX's collectives and lax.ppermute only.
A program may use at most 64 MiB of HBM per device.

v0:
```python
import math

import jax
import jax.numpy as jnp
from jax import lax
from jax.sharding import PartitionSpec as P


def body(
    features,
    global_weight,
    entity_feats,
    coefs,
    member_owner,
    member_local,
    item_owner,
    item_local,
    clicks,
    valid,
):
    rows_here = features.shape[0]
    width = entity_feats.shape[1]
    n_rows = lax.axis_size("rows")
    n_ent = lax.axis_size("ent")
    owners = n_rows * n_ent
    capacity = 2 * rows_here // owners
    total_slots = owners * capacity
    on_item = lax.axis_index("feat") >= lax.axis_size("feat") // 2
    owner = jnp.where(on_item, item_owner[:, 0], member_owner[:, 0])
    local = jnp.where(on_item, item_local, member_local)
    hits = (owner[:, None] == jnp.arange(owners, dtype=jnp.int32)[None, :]).astype(jnp.int32)
    rank = jnp.sum(jnp.cumsum(hits, axis=0) * hits, axis=1) - 1
    slot = owner * capacity + rank
    out_feats = jnp.zeros((total_slots, width), jnp.bfloat16).at[slot].set(entity_feats)
    out_ids = jnp.zeros((total_slots,), jnp.int32).at[slot].set(local)
    global_part = jnp.dot(features, global_weight, preferred_element_type=jnp.float32)
    global_total = lax.psum(global_part, "feat")
    in_feats, in_ids = (
        lax.all_to_all(
            out_feats.reshape(owners, capacity, width),
            ("rows", "ent"),
            split_axis=0,
            concat_axis=0,
            tiled=True,
        ),
        lax.all_to_all(
            out_ids.reshape(owners, capacity),
            ("rows", "ent"),
            split_axis=0,
            concat_axis=0,
            tiled=True,
        ),
    )
    in_wide = in_feats.astype(jnp.float32)
    part_scores = jnp.sum(in_wide * coefs[in_ids], axis=2)
    returned = lax.all_to_all(part_scores, ("rows", "ent"), split_axis=0, concat_axis=0, tiled=True)
    entity_part = returned.reshape(total_slots)[slot]
    margin = global_total + lax.psum(entity_part, "feat")
    resid = valid.astype(jnp.float32) * (jax.nn.sigmoid(margin) - clicks.astype(jnp.float32))
    resid_out = jnp.zeros((total_slots,), jnp.float32).at[slot].set(resid).reshape(owners, capacity)
    in_resid = lax.all_to_all(resid_out, ("rows", "ent"), split_axis=0, concat_axis=0, tiled=True)
    contrib = (in_resid[:, :, None] * in_wide).reshape(total_slots, width)
    grad_coefs = (
        jnp.zeros(coefs.shape, jnp.float32).at[in_ids.reshape(total_slots)].add(contrib) + coefs
    )
    partial_grad = jnp.dot(resid.astype(jnp.bfloat16), features, preferred_element_type=jnp.float32)
    summed = lax.psum(partial_grad, ("rows", "ent"))
    scale = 1.0 / math.sqrt(rows_here * owners)
    grad_global = summed * scale + 4.0 * global_weight.astype(jnp.float32)
    return (grad_global, grad_coefs)


def solution(mesh):
    return jax.shard_map(
        body,
        mesh=mesh,
        in_specs=(
            P(("groups", "rows", "ent"), "feat"),
            P(("groups", "feat")),
            P(("groups", "rows", "ent"), "feat"),
            P(("groups", "rows", "ent"), "feat"),
            P(("groups", "rows", "ent"), None),
            P(("groups", "rows", "ent")),
            P(("groups", "rows", "ent"), None),
            P(("groups", "rows", "ent")),
            P(("groups", "rows", "ent")),
            P(("groups", "rows", "ent")),
        ),
        out_specs=(P(("groups", "feat")), P(("groups", "rows", "ent"), "feat")),
        check_vma=False,
    )
```

profile of v0, /device:TPU:0, one launch (start us, length us, event | category | flops | bytes accessed | tf_op | source)
XLA Modules:
  0.0 124.9 jit_solution(5961994442078998786)
XLA Ops:
  0.6 0.0 copy-start.1
  0.6 1.0 copy.19
  1.7 0.7 broadcast_select_fusion
  2.4 2.3 %reduce-window.6 = s32[8,8,128]{2,1,0:T(8,128)S(1)} reduce-window(s32[8,8,128]{2,1,0:T(8,128)S(1)} %fusion.5, s32[]{:T(128)} %constant.17.clone.1), window={size=1x1x128 pad=0_0x0_0x127_0}, to_apply=%region_1.2 | reduce-window | flops 1040384 | bytes 65540 | tf_op jit(solution)/shard_map/reduce-window
  4.7 0.3 slice_reduce_fusion
  4.9 0.2 reduce-window.9
  5.1 0.1 add_bitcast_fusion
  5.2 0.7 broadcast_select_fusion.1
  6.0 4.9 %scatter_custom_fusion.1 = s32[2048]{0:T(1024)} fusion(s32[1024]{0:T(1024)S(1)} %bitcast.53, s32[1024]{0:T(1024)S(1)} %broadcast_select_fusion.1, s32[]{:T(128)} %constant.17.clone.1), kind=kCustom, calls=%fused_computation.29 | custom fusion | bytes 8196 | tf_op jit(solution)/shard_map/scatter | solution.py:35
  10.8 6.3 %all-to-all-start.1 = ((s32[8,1,256]{2,1,0:T(1,128)}), s32[8,1,256]{2,1,0:T(1,128)S(1)}, u32[]{:S(2)}, u32[]{:S(2)}) async-start(s32[8,1,256]{2,1,0:T(1,128)} %bitcast.7), calls=%async_computation.1 | async-start | bytes 16384 | tf_op jit(solution)/shard_map/all_to_all | solution.py:46
  17.2 6.4 %scatter_custom_fusion = bf16[2048,256]{1,0:T(8,128)(2,1)} fusion(s32[1024]{0:T(1024)S(1)} %bitcast.54, bf16[1024,256]{1,0:T(8,128)(2,1)} %param.12, bf16[]{:T(256)} %constant.13.clone.1), kind=kCustom, calls=%fused_computation.9 | custom fusion | bytes 1049088 | tf_op jit(solution)/shard_map/scatter | solution.py:34
  23.6 0.0 all-to-all-done.1
  23.6 5.1 %all-to-all-start = ((bf16[8,256,256]{2,1,0:T(8,128)(2,1)}), bf16[8,256,256]{2,1,0:T(8,128)(2,1)S(1)}, u32[]{:S(2)}, u32[]{:S(2)}) async-start(bf16[8,256,256]{2,1,0:T(8,128)(2,1)} %bitcast.6), calls=%async_computation | async-start | bytes 2097152 | tf_op jit(solution)/shard_map/all_to_all | solution.py:39
  28.7 0.0 copy-done.1
  28.7 3.4 %fusion.11 = f32[1,1024]{1,0:T(1,128)S(1)} fusion(bf16[1024,2048]{1,0:T(8,128)(2,1)} %param.10, bf16[2048,1]{0,1:T(2,128)(2,1)S(1)} %reshape.165), kind=kOutput, calls=%fused_computation.35 | convolution fusion | flops 4194304 | bytes 4202496 | tf_op jit(solution)/shard_map/dot_general | solution.py:36
  32.1 8.6 %gather_fusion = f32[2048,256]{1,0:T(8,128)} fusion(f32[512,256]{1,0:T(8,128)S(1)} %copy.19, s32[2048]{0:T(1024)S(1)} %broadcast_clamp_fusion), kind=kCustom, calls=%fused_computation | custom fusion | bytes 4202496 | tf_op jit(solution)/shard_map/gather | solution.py:55
  40.7 14.6 %all-to-all-done = bf16[8,256,256]{2,1,0:T(8,128)(2,1)S(1)} async-done(((bf16[8,256,256]{2,1,0:T(8,128)(2,1)}), bf16[8,256,256]{2,1,0:T(8,128)(2,1)S(1)}, u32[]{:S(2)}, u32[]{:S(2)}) %all-to-all-start) | async-done | bytes 1048608 | tf_op jit(solution)/shard_map/all_to_all | solution.py:39
  55.3 1.9 %fusion = f32[8,256]{1,0:T(8,128)S(1)} fusion(f32[8,256,256]{2,1,0:T(8,128)} %bitcast.43, bf16[8,256,256]{2,1,0:T(8,128)(2,1)S(1)} %all-to-all-done), kind=kLoop, calls=%fused_computation.8 | loop fusion | flops 1570816 | bytes 3153920 | tf_op jit(solution)/shard_map/reduce_sum | solution.py:55
  57.2 0.6 all_to_all.27
  57.8 3.3 %all-to-all-start.2 = ((f32[8,1,256]{2,1,0:T(1,128)}), f32[8,1,256]{2,1,0:T(1,128)S(1)}, u32[]{:S(2)}, u32[]{:S(2)}) async-start(f32[8,1,256]{2,1,0:T(1,128)} %all_to_all.27), calls=%async_computation.2 | async-start | bytes 16384 | tf_op jit(solution)/shard_map/all_to_all | solution.py:56
  61.2 5.5 %all-to-all-done.2 = f32[8,1,256]{2,1,0:T(1,128)S(1)} async-done(((f32[8,1,256]{2,1,0:T(1,128)}), f32[8,1,256]{2,1,0:T(1,128)S(1)}, u32[]{:S(2)}, u32[]{:S(2)}) %all-to-all-start.2) | async-done | bytes 8224 | tf_op jit(solution)/shard_map/all_to_all | solution.py:56
  66.7 0.0 copy-start.2
  66.7 0.0 copy-start.3
  66.7 6.1 %gather_fusion.1 = f32[1024]{0:T(1024)S(1)} fusion(f32[2048]{0:T(1024)S(1)} %bitcast.42, s32[1024]{0:T(1024)S(1)} %broadcast_clamp_fusion.1), kind=kCustom, calls=%fused_computation.1 | custom fusion | bytes 12288 | tf_op jit(solution)/shard_map/gather | solution.py:57
  72.9 4.9 %psum.24 = f32[1024]{0:T(1024)S(1)} all-reduce(f32[1024]{0:T(1024)S(1)} %add.69), channel_id=1, replica_groups=mesh['groups'=2,'rows'=4,'feat'=2,'ent'=2] {'feat'}, use_global_device_ids=true, to_apply=%region_0.1 | all-reduce | flops 1024 | bytes 8192 | tf_op jit(solution)/shard_map/psum | solution.py:37
  77.8 0.0 copy-done.2
  77.8 0.0 copy-done.3
  77.8 2.8 %fusion.12 = f32[1,2048]{1,0:T(1,128)S(1)} fusion(bf16[1024,1]{0,1:T(2,128)(2,1)S(1)} %reshape.167, bf16[1024,2048]{1,0:T(8,128)(2,1)} %param.10), kind=kOutput, calls=%fused_computation.36 | convolution fusion | flops 4194304 | bytes 4204544 | tf_op jit(solution)/shard_map/dot_general | solution.py:66
  80.7 13.9 %psum.23 = f32[2048]{0:T(1024)S(1)} all-reduce(f32[2048]{0:T(1024)S(1)} %bitcast.50), channel_id=1, replica_groups=mesh['groups'=2,'rows'=4,'feat'=2,'ent'=2] {'rows','ent'}, use_global_device_ids=true, to_apply=%region_8.9 | all-reduce | flops 2048 | bytes 16384 | tf_op jit(solution)/shard_map/psum | solution.py:67
  94.6 4.9 %scatter_custom_fusion.2 = f32[2048]{0:T(1024)} fusion(s32[1024]{0:T(1024)S(1)} %bitcast.56, f32[1024]{0:T(1024)S(1)} %get-tuple-element.3, f32[]{:T(128)} %constant.8.clone.1), kind=kCustom, calls=%fused_computation.26 | custom fusion | bytes 8196 | tf_op jit(solution)/shard_map/scatter | solution.py:60
  99.5 3.3 %all-to-all-start.3 = ((f32[8,1,256]{2,1,0:T(1,128)}), f32[8,1,256]{2,1,0:T(1,128)S(1)}, u32[]{:S(2)}, u32[]{:S(2)}) async-start(f32[8,1,256]{2,1,0:T(1,128)} %bitcast.15), calls=%async_computation.3 | async-start | bytes 16384 | tf_op jit(solution)/shard_map/all_to_all | solution.py:61
  102.8 0.6 multiply_add_fusion
  103.4 4.9 %all-to-all-done.3 = f32[8,1,256]{2,1,0:T(1,128)S(1)} async-done(((f32[8,1,256]{2,1,0:T(1,128)}), f32[8,1,256]{2,1,0:T(1,128)S(1)}, u32[]{:S(2)}, u32[]{:S(2)}) %all-to-all-start.3) | async-done | bytes 8224 | tf_op jit(solution)/shard_map/all_to_all | solution.py:61
  108.4 1.7 %convert_multiply_fusion = f32[8,256,256]{2,1,0:T(8,128)} fusion(bf16[8,256,256]{2,1,0:T(8,128)(2,1)S(1)} %all-to-all-done, f32[8,256]{1,0:T(8,128)S(1)} %bitcast.49), kind=kLoop, calls=%fused_computation.6 | loop fusion | flops 1048576 | bytes 3153920 | tf_op jit(solution)/shard_map/mul | solution.py:62
  110.1 14.0 %scatter_fusion = f32[512,256]{1,0:T(8,128)S(1)} fusion(f32[512,256]{1,0:T(8,128)S(1)} %copy.19, s32[2048]{0:T(1024)S(1)} %bitcast.48, f32[2048,256]{1,0:T(8,128)} %bitcast.44), kind=kCustom, calls=%fused_computation.5 | custom fusion | flops 524288 | bytes 6299648 | tf_op jit(solution)/shard_map/scatter-add | solution.py:64
  124.1 0.0 copy-start
  124.1 0.8 copy-done
  (13 shorter events, 0.1 us)
Async XLA Ops:
  0.6 28.1 %copy-start.1 = (bf16[2048]{0:T(1024)(128)(2,1)S(1)}, bf16[2048]{0:T(1024)(128)(2,1)}, u32[]{:S(2)}) copy-start(bf16[2048]{0:T(1024)(128)(2,1)} %param.11) | copy-start | bytes 12292
  10.8 12.7 %all-to-all-start.1 = ((s32[8,1,256]{2,1,0:T(1,128)}), s32[8,1,256]{2,1,0:T(1,128)S(1)}, u32[]{:S(2)}, u32[]{:S(2)}) async-start(s32[8,1,256]{2,1,0:T(1,128)} %bitcast.7), calls=%async_computation.1 | async-start | bytes 16384 | tf_op jit(solution)/shard_map/all_to_all | solution.py:46
  23.6 31.7 %all-to-all-start = ((bf16[8,256,256]{2,1,0:T(8,128)(2,1)}), bf16[8,256,256]{2,1,0:T(8,128)(2,1)S(1)}, u32[]{:S(2)}, u32[]{:S(2)}) async-start(bf16[8,256,256]{2,1,0:T(8,128)(2,1)} %bitcast.6), calls=%async_computation | async-start | bytes 2097152 | tf_op jit(solution)/shard_map/all_to_all | solution.py:39
  57.8 8.9 %all-to-all-start.2 = ((f32[8,1,256]{2,1,0:T(1,128)}), f32[8,1,256]{2,1,0:T(1,128)S(1)}, u32[]{:S(2)}, u32[]{:S(2)}) async-start(f32[8,1,256]{2,1,0:T(1,128)} %all_to_all.27), calls=%async_computation.2 | async-start | bytes 16384 | tf_op jit(solution)/shard_map/all_to_all | solution.py:56
  66.7 11.1 %copy-start.2 = (s32[1024]{0:T(1024)S(1)}, s32[1024]{0:T(1024)}, u32[]{:S(2)}) copy-start(s32[1024]{0:T(1024)} %param.18) | copy-start | bytes 12292
  66.7 11.1 %copy-start.3 = (s32[1024]{0:T(1024)S(1)}, s32[1024]{0:T(1024)}, u32[]{:S(2)}) copy-start(s32[1024]{0:T(1024)} %param.19) | copy-start | bytes 12292
  99.5 8.9 %all-to-all-start.3 = ((f32[8,1,256]{2,1,0:T(1,128)}), f32[8,1,256]{2,1,0:T(1,128)S(1)}, u32[]{:S(2)}, u32[]{:S(2)}) async-start(f32[8,1,256]{2,1,0:T(1,128)} %bitcast.15), calls=%async_computation.3 | async-start | bytes 16384 | tf_op jit(solution)/shard_map/all_to_all | solution.py:61
  124.1 0.8 copy-start
where the time goes:
time: 126 us; the launch traced here: 125 us
  local copies, waits for them, and re-layouts  33.6 us (27%)
  waiting for transfers between devices  25 us (20%)
  other arithmetic  22.3 us (18%)
  blocking collectives  18.9 us (15%)
  starting transfers between devices  18.1 us (14%)
  matrix products  6.21 us (5%)
    all_to_all x1, waiting for transfers between devices, body(): lax.all_to_all(out_feats.reshape(owners, capacity, width), ('rows', 'ent'...  14.6 us
    scatter-add x1, other arithmetic, body(): jnp.zeros(coefs.shape, jnp.float32).at[in_ids.reshape(total_slots)]  14 us
    psum x1, blocking collectives, body(): summed = lax.psum(partial_grad, ('rows', 'ent'))  13.9 us
    gather x1, local copies, waits for them, and re-layouts, body(): part_scores = jnp.sum(in_wide * coefs[in_ids], axis=2)  8.56 us
    scatter x1, local copies, waits for them, and re-layouts, body(): jnp.zeros((total_slots, width), jnp.bfloat16).at[slot].set(entity_feats)  6.42 us
    all_to_all x1, starting transfers between devices, body(): lax.all_to_all(out_ids.reshape(owners, capacity), ('rows', 'ent'), split_...  6.33 us
    gather x1, local copies, waits for them, and re-layouts, body(): entity_part = returned.reshape(total_slots)[slot]  6.15 us
    all_to_all x1, waiting for transfers between devices, body(): lax.all_to_all(part_scores, ('rows', 'ent'), split_axis=0, concat_axis=0,...  5.52 us
  transfers between devices with their start and end apart: 4, of which 3 were waited for; matrix products, arithmetic and copies ran while one was open for 15% of the time, Pallas kernels for 0%

commit v1 on v0

v1 whole, which is shorter than its diff:
```python
import math

import jax
import jax.numpy as jnp
from jax import lax
from jax.experimental import pallas as pl
from jax.experimental.pallas import tpu as pltpu
from jax.sharding import PartitionSpec as P

F32 = jnp.float32
BF16 = jnp.bfloat16
HOME = ("rows", "ent")
EVERY = ("rows", "feat", "ent")
IDS = 16
PARAMS = pltpu.CompilerParams(vmem_limit_bytes=24 * 2**20)


def lanes_dot(a, b):
    return lax.dot_general(a, b, (((1,), (1,)), ((), ())), preferred_element_type=F32)


def plain_dot(a, b):
    return lax.dot_general(a, b, (((1,), (0,)), ((), ())), preferred_element_type=F32)


def halves(x):
    high = x.astype(BF16)
    return high, (x - high.astype(F32)).astype(BF16)


def one_hot(row, count):
    return row == lax.broadcasted_iota(jnp.int32, (count, row.shape[1]), 0)


def dispatch_kernel(owners, capacity, where, member, item, member_local, item_local, feats, ranks, *chunks):
    rows = feats.shape[0]
    step = min(256, rows)
    blocks = rows // step
    mine, on_item = where[0], where[1] > 0
    hits = jnp.concatenate(
        [one_hot(member[...], owners).astype(F32), one_hot(item[...], owners).astype(F32)], axis=0
    )
    stacked = jnp.concatenate([hits[:, b * step : (b + 1) * step] for b in range(blocks)], axis=0)
    upper = lax.broadcasted_iota(jnp.int32, (step, step), 0) <= lax.broadcasted_iota(
        jnp.int32, (step, step), 1
    )
    counts = plain_dot(stacked.astype(BF16), upper.astype(F32).astype(BF16))
    before = jnp.zeros((2 * owners, 1), F32)
    pieces = []
    for b in range(blocks):
        here = counts[2 * owners * b : 2 * owners * (b + 1)]
        taken = (here + before) * hits[:, b * step : (b + 1) * step]
        pieces.append(
            jnp.concatenate(
                [
                    jnp.sum(taken[:owners], axis=0, keepdims=True),
                    jnp.sum(taken[owners:], axis=0, keepdims=True),
                ],
                axis=0,
            )
        )
        before = before + here[:, step - 1 : step]
    rank = jnp.concatenate(pieces, axis=1).astype(jnp.int32) - 1
    ranks[...] = rank
    own = jnp.where(on_item, item[...], member[...])
    own_rank = jnp.where(on_item, rank[1:2], rank[0:1])
    local = jnp.where(on_item, item_local[...], member_local[...])
    place = (own ^ mine) * capacity + own_rank
    high = local >> 8
    ids = jnp.concatenate([high, local - (high << 8), jnp.zeros((IDS - 2, rows), jnp.int32)], axis=0)
    ids = ids.astype(F32).astype(BF16)
    for k in range(owners):
        pick = one_hot(place - k * capacity, capacity).astype(F32).astype(BF16)
        chunks[k][:capacity] = plain_dot(pick, feats[...]).astype(BF16)
        chunks[k][capacity:, :capacity] = lanes_dot(ids, pick).astype(BF16)


def chunk_ids(chunk, capacity):
    pair = chunk[capacity:, :capacity].astype(F32)
    return (pair[0:1] * 256.0 + pair[1:2]).astype(jnp.int32)


def scores_kernel(owners, capacity, coefs, *refs):
    entities = coefs.shape[0]
    high, low = halves(coefs[...])
    for k in range(owners):
        chunk, out = refs[k], refs[owners + k]
        feats = chunk[:capacity]
        every = lanes_dot(high, feats) + lanes_dot(low, feats)
        out[...] = jnp.sum(
            jnp.where(one_hot(chunk_ids(chunk, capacity), entities), every, 0.0), axis=0, keepdims=True
        )


def home_kernel(owners, capacity, sides, where, member, item, ranks, clicks, valid, margin, *refs):
    mine, on_item = where[0], where[1] > 0
    scores = refs[: sides * owners]
    resid_out = refs[sides * owners]
    outs = refs[sides * owners + 1 :]
    total = margin[...]
    hits_of, spot_of = [], []
    for side, owner in ((0, member), (1, item)):
        hits = one_hot(owner[...] ^ mine, owners)
        spot = one_hot(ranks[side : side + 1], capacity).astype(F32).astype(BF16)
        hits_of.append(hits)
        spot_of.append(spot)
    for q in range(sides):
        table = jnp.concatenate([scores[q * owners + k][...] for k in range(owners)], axis=0)
        high, low = halves(table)
        is_item = where[2 + q] > 0
        spot = jnp.where(is_item, spot_of[1], spot_of[0])
        hits = jnp.where(is_item, hits_of[1].astype(F32), hits_of[0].astype(F32))
        found = plain_dot(jnp.concatenate([high, low], axis=0), spot)
        total = total + jnp.sum((found[:owners] + found[owners:]) * hits, axis=0, keepdims=True)
    resid = valid[...].astype(F32) * (jax.nn.sigmoid(total) - clicks[...].astype(F32))
    resid_out[...] = resid
    hits = jnp.where(on_item, hits_of[1].astype(F32), hits_of[0].astype(F32))
    spot = jnp.where(on_item, spot_of[1], spot_of[0])
    high, low = halves(hits * resid)
    sent = lanes_dot(jnp.concatenate([high, low], axis=0), spot)
    sent = sent[:owners] + sent[owners:]
    for k in range(owners):
        outs[k][...] = sent[k : k + 1]


def coefs_kernel(owners, capacity, coefs, *refs):
    entities = coefs.shape[0]
    total = coefs[...]
    for k in range(owners):
        chunk, resid = refs[k], refs[owners + k]
        hits = one_hot(chunk_ids(chunk, capacity), entities)
        high, low = halves(jnp.where(hits, resid[...], 0.0))
        feats = chunk[:capacity]
        total = total + plain_dot(high, feats) + plain_dot(low, feats)
    refs[2 * owners][...] = total


def xor_send(x, axes, size, k):
    return x if k == 0 else lax.ppermute(x, axes, [(i, i ^ k) for i in range(size)])


def call(kernel, out_shape, operands, scalars=0, flops=0):
    smem = pl.BlockSpec(memory_space=pltpu.SMEM)
    vmem = pl.BlockSpec(memory_space=pltpu.VMEM)
    moved = sum(x.size * x.dtype.itemsize for x in (*operands, *out_shape))
    return pl.pallas_call(
        kernel,
        out_shape=out_shape,
        in_specs=[smem] * scalars + [vmem] * (len(operands) - scalars),
        out_specs=[vmem] * len(out_shape),
        compiler_params=PARAMS,
        cost_estimate=pl.CostEstimate(flops=flops, bytes_accessed=moved, transcendentals=0),
    )(*operands)


def body(
    features,
    global_weight,
    entity_feats,
    coefs,
    member_owner,
    member_local,
    item_owner,
    item_local,
    clicks,
    valid,
):
    rows_here, width = entity_feats.shape
    n_feat = lax.axis_size("feat")
    n_ent = lax.axis_size("ent")
    owners = lax.axis_size("rows") * n_ent
    capacity = 2 * rows_here // owners
    mine = lax.axis_index(HOME)
    feat = lax.axis_index("feat")
    sides_item = [((feat ^ q) >= n_feat // 2).astype(jnp.int32) for q in range(n_feat)]
    where = jnp.stack([mine.astype(jnp.int32), sides_item[0], *sides_item])
    member, item = member_owner.reshape(1, rows_here), item_owner.reshape(1, rows_here)

    def shape(*dims, dtype=F32):
        return jax.ShapeDtypeStruct(dims, dtype)

    def partial(kernel, *args):
        return lambda *refs: kernel(*args, *refs)

    order = sorted(range(1, owners), reverse=True)
    ranks, *chunks = call(
        partial(dispatch_kernel, owners, capacity),
        [shape(2, rows_here, dtype=jnp.int32)] + [shape(capacity + IDS, width, dtype=BF16)] * owners,
        (where, member, item, member_local.reshape(1, rows_here), item_local.reshape(1, rows_here), entity_feats),
        scalars=1,
        flops=2 * owners * capacity * rows_here * width,
    )
    arrived = [None] * owners
    for k in order + [0]:
        arrived[k] = xor_send(chunks[k], HOME, owners, k)

    global_part = jnp.dot(features, global_weight, preferred_element_type=F32)
    global_total = global_part
    for q in range(1, n_feat):
        global_total = global_total + xor_send(global_part, "feat", n_feat, q)

    scores = call(
        partial(scores_kernel, owners, capacity),
        [shape(1, capacity)] * owners,
        (coefs, *arrived),
        flops=4 * coefs.size * owners * capacity,
    )
    returned = []
    for q in range(n_feat):
        for k in range(owners):
            apart = (k // n_ent * n_feat + q) * n_ent + k % n_ent
            returned.append(xor_send(scores[k], EVERY, n_feat * owners, apart))
    resid, *resid_out = call(
        partial(home_kernel, owners, capacity, n_feat),
        [shape(1, rows_here)] + [shape(1, capacity)] * owners,
        (
            where,
            member,
            item,
            ranks,
            clicks.reshape(1, rows_here),
            valid.reshape(1, rows_here),
            global_total.reshape(1, rows_here),
            *returned,
        ),
        scalars=1,
    )
    resid_in = [xor_send(resid_out[k], HOME, owners, k) for k in range(owners)]
    partial_grad = jnp.dot(resid.reshape(rows_here).astype(BF16), features, preferred_element_type=F32)
    terms = [xor_send(partial_grad, HOME, owners, k) for k in range(owners)]
    while len(terms) > 1:
        terms = [a + b for a, b in zip(terms[::2], terms[1::2])]
    (summed,) = terms
    (grad_coefs,) = call(
        partial(coefs_kernel, owners, capacity),
        [shape(*coefs.shape)],
        (coefs, *arrived, *resid_in),
        flops=4 * coefs.size * owners * capacity,
    )
    scale = 1.0 / math.sqrt(rows_here * owners)
    grad_global = summed * scale + 4.0 * global_weight.astype(F32)
    return (grad_global, grad_coefs)


def solution(mesh):
    by_row = P(("groups", "rows", "ent"))
    by_both = P(("groups", "rows", "ent"), "feat")
    column = P(("groups", "rows", "ent"), None)
    by_feat = P(("groups", "feat"))
    return jax.shard_map(
        body,
        mesh=mesh,
        in_specs=(by_both, by_feat, by_both, by_both, column, by_row, column, by_row, by_row, by_row),
        out_specs=(by_feat, by_both),
        check_vma=False,
    )
```

time: 126 us -> 87.1 us (0.69)
  starting transfers between devices: 18.1 us -> 51.8 us
  local copies, waits for them, and re-layouts: 33.6 us -> 4.53 us
  other arithmetic: 22.3 us -> 0.69 us
  blocking collectives: 18.9 us -> 0 us
  waiting for transfers between devices: 25 us -> 16.7 us
  Pallas kernels: 0 us -> 8.07 us
  matrix products: 6.21 us -> 4.17 us
    ppermute x0 -> x37, starting transfers between devices: none -> 51.8 us  [xor_send(): lax.ppermute(x, axes, [(i, i ^ k) for i in range(size)])]
    all_to_all x4 -> x0, waiting for transfers between devices: 25 us -> none  [the longest x1 14.6 us: body(): lax.all_to_all(out_feats.reshape(owners, capacity, width), ('rows', 'ent'...]
    psum x2 -> x0, blocking collectives: 18.9 us -> none  [the longest x1 13.9 us: body(): summed = lax.psum(partial_grad, ('rows', 'ent'))]
    all_to_all x4 -> x0, starting transfers between devices: 18.1 us -> none  [the longest x1 6.33 us: body(): lax.all_to_all(out_ids.reshape(owners, capacity), ('rows', 'ent'), split_...]
    ppermute x0 -> x37, waiting for transfers between devices: none -> 16.7 us  [xor_send(): lax.ppermute(x, axes, [(i, i ^ k) for i in range(size)])]
    scatter x3 -> x0, local copies, waits for them, and re-layouts: 16.2 us -> none  [the longest x1 6.42 us: body(): jnp.zeros((total_slots, width), jnp.bfloat16).at[slot].set(entity_feats)]
    gather x2 -> x0, local copies, waits for them, and re-layouts: 14.7 us -> none  [the longest x1 8.56 us: body(): part_scores = jnp.sum(in_wide * coefs[in_ids], axis=2)]
    scatter-add x1 -> x0, other arithmetic: 14 us -> none  [body(): jnp.zeros(coefs.shape, jnp.float32).at[in_ids.reshape(total_slots)]]
  transfers between devices with their start and end apart: 4 -> 37, of which waited for: 3 -> 9; matrix products, arithmetic and copies ran while one was open for 15% -> 5% of each run, Pallas kernels for 0% -> 4%
where the time goes in v1:
time: 87.1 us; the launch traced here: 86.8 us
  starting transfers between devices  51.8 us (59%)
  waiting for transfers between devices  16.7 us (19%)
  Pallas kernels  8.07 us (9%)
  local copies, waits for them, and re-layouts  4.53 us (5%)
  matrix products  4.17 us (5%)
    ppermute x37, starting transfers between devices, xor_send(): lax.ppermute(x, axes, [(i, i ^ k) for i in range(size)])  51.8 us
    ppermute x37, waiting for transfers between devices, xor_send(): lax.ppermute(x, axes, [(i, i ^ k) for i in range(size)])  16.7 us
    pallas_call x4, Pallas kernels, call(): pl.pallas_call(kernel, out_shape=out_shape, in_specs=[smem] * scalars + [...  8.07 us
    unnamed x25, local copies, waits for them, and re-layouts  4.53 us
    dot_general x1, matrix products, body(): global_part = jnp.dot(features, global_weight, preferred_element_type=F32)  3.52 us
  transfers between devices with their start and end apart: 37, of which 9 were waited for; matrix products, arithmetic and copies ran while one was open for 5% of the time, Pallas kernels for 4%

profile of v1, /device:TPU:0, one launch (start us, length us, event | category | flops | bytes accessed | tf_op | source)
XLA Modules:
  0.0 86.8 jit_solution(8164030100966648648)
XLA Ops:
  0.7 0.7 copy-done
  1.4 0.7 copy-done.2
  2.1 1.0 %copy-done.6 = bf16[1024,256]{1,0:T(8,128)(2,1)S(1)} copy-done((bf16[1024,256]{1,0:T(8,128)(2,1)S(1)}, bf16[1024,256]{1,0:T(8,128)(2,1)}, u32[]{:S(2)}) %copy-start.6) | copy-done | bytes 524312
  3.1 0.7 copy-done.8
  3.8 0.7 copy-done.9
  4.5 3.1 %shard_map.113 = (s32[2,1024]{1,0:T(2,128)S(1)}, bf16[272,256]{1,0:T(8,128)(2,1)S(1)}, bf16[272,256]{1,0:T(8,128)(2,1)S(1)}, bf16[272,256]{1,0:T(8,128)(2,1)S(1)...) custom-call(s32[4]{0:T(128)S(1)} %pad_add_fusion.refs_0_, ...), custom_call_target="tpu_custom_call" | custom-call | flops 1073741824 | bytes 1662992 | tf_op jit(solution)/shard_map/pallas_call | solution.py:146
  7.6 0.5 collective-permute-start.1
  8.1 2.6 %collective-permute-start.2 = (bf16[272,256]{1,0:T(8,128)(2,1)S(1)}, bf16[272,256]{1,0:T(8,128)(2,1)S(1)}, u32[]{:S(2)}, u32[]{:S(2)}) collective-permute-start(bf16[272,256]{1,0:T(8,128)(2,1)S(1)} %get-tuple-element.31), channel_id=1, source_target_pairs={{0,4},{1,5},{4,0},{5,1},{8,12},{9,13},{12,8},{13,9},{2,6},{3,7},{6... | collective-permute-start | bytes 417800 | tf_op jit(solution)/shard_map/ppermute | solution.py:139
  10.8 2.8 %collective-permute-start.4 = (bf16[272,256]{1,0:T(8,128)(2,1)S(1)}, bf16[272,256]{1,0:T(8,128)(2,1)S(1)}, u32[]{:S(2)}, u32[]{:S(2)}) collective-permute-start(bf16[272,256]{1,0:T(8,128)(2,1)S(1)} %get-tuple-element.33), channel_id=1, source_target_pairs={{0,8},{1,9},{4,12},{5,13},{8,0},{9,1},{12,4},{13,5},{2,10},{3,11},... | collective-permute-start | bytes 417800 | tf_op jit(solution)/shard_map/ppermute | solution.py:139
  13.6 0.7 reshape.36
  14.3 3.7 %collective-permute-start.6 = (bf16[272,256]{1,0:T(8,128)(2,1)S(1)}, bf16[272,256]{1,0:T(8,128)(2,1)S(1)}, u32[]{:S(2)}, u32[]{:S(2)}) collective-permute-start(bf16[272,256]{1,0:T(8,128)(2,1)S(1)} %get-tuple-element.35), channel_id=1, source_target_pairs={{0,12},{1,13},{4,8},{5,9},{8,4},{9,5},{12,0},{13,1},{2,14},{3,15},... | collective-permute-start | bytes 417800 | tf_op jit(solution)/shard_map/ppermute | solution.py:139
  17.9 2.8 %collective-permute-done.2.refs_3_ = bf16[272,256]{1,0:T(8,128)(2,1)S(1)} collective-permute-done((bf16[272,256]{1,0:T(8,128)(2,1)S(1)}, bf16[272,256]{1,0:T(8,128)(2,1)S(1)}, u32[]{:S(2)}, u32[]{:S(2)}) %collective-permute-start.2) | collective-permute-done | bytes 139296 | tf_op jit(solution)/shard_map/ppermute | solution.py:139
  20.9 3.5 %fusion.3 = f32[1,1024]{1,0:T(1,128)S(1)} fusion(bf16[1024,2048]{1,0:T(8,128)(2,1)} %param.10, bf16[2048,1]{0,1:T(2,128)(2,1)S(1)} %reshape.36), kind=kOutput, calls=%fused_computation.5 | convolution fusion | flops 4194304 | bytes 4202496 | tf_op jit(solution)/shard_map/dot_general | solution.py:197
  24.4 1.8 %collective-permute-start = (f32[1024]{0:T(1024)S(1)}, f32[1024]{0:T(1024)S(1)}, u32[]{:S(2)}, u32[]{:S(2)}) collective-permute-start(f32[1024]{0:T(1024)S(1)} %bitcast.35), channel_id=1, source_target_pairs={{0,2},{2,0},{1,3},{3,1},{4,6},{6,4},{5,7},{7,5},{8,10},{10,8},{9,1... | collective-permute-start | bytes 12296 | tf_op jit(solution)/shard_map/ppermute | solution.py:139
  26.3 6.2 %collective-permute-done.5.refs_6_ = bf16[272,256]{1,0:T(8,128)(2,1)S(1)} collective-permute-done((bf16[272,256]{1,0:T(8,128)(2,1)S(1)}, bf16[272,256]{1,0:T(8,128)(2,1)S(1)}, u32[]{:S(2)}, u32[]{:S(2)}) %collective-permute-start.5) | collective-permute-done | bytes 139296 | tf_op jit(solution)/shard_map/ppermute | solution.py:139
  32.5 1.3 %shard_map.114 = (f32[1,256]{1,0:T(1,128)S(1)}, f32[1,256]{1,0:T(1,128)S(1)}, f32[1,256]{1,0:T(1,128)S(1)}, f32[1,256]{1,0:T(1,128)S(1)}, f32[1,256]{1,0:T(1,128...) custom-call(f32[512,256]{1,0:T(8,128)S(1)} %copy-done.7, ...), custom_call_target="tpu_custom_call" | custom-call | flops 1073741824 | bytes 1646592 | tf_op jit(solution)/shard_map/pallas_call | solution.py:146
  33.8 6.3 %collective-permute-start.10 = (f32[1,256]{1,0:T(1,128)S(1)}, f32[1,256]{1,0:T(1,128)S(1)}, u32[]{:S(2)}, u32[]{:S(2)}) collective-permute-start(f32[1,256]{1,0:T(1,128)S(1)} %get-tuple-element.40), channel_id=1, source_target_pairs={{0,5},{1,4},{2,7},{3,6},{4,1},{5,0},{6,3},{7,2},{8,13},{9,12},{10,... | collective-permute-start | bytes 3080 | tf_op jit(solution)/shard_map/ppermute | solution.py:139
  40.2 2.3 %collective-permute-start.11 = (f32[1,256]{1,0:T(1,128)S(1)}, f32[1,256]{1,0:T(1,128)S(1)}, u32[]{:S(2)}, u32[]{:S(2)}) collective-permute-start(f32[1,256]{1,0:T(1,128)S(1)} %get-tuple-element.41), channel_id=1, source_target_pairs={{0,8},{1,9},{2,10},{3,11},{4,12},{5,13},{6,14},{7,15},{8,0},{9,1},... | collective-permute-start | bytes 3080 | tf_op jit(solution)/shard_map/ppermute | solution.py:139
  42.4 0.9 %collective-permute-start.12 = (f32[1,256]{1,0:T(1,128)S(1)}, f32[1,256]{1,0:T(1,128)S(1)}, u32[]{:S(2)}, u32[]{:S(2)}) collective-permute-start(f32[1,256]{1,0:T(1,128)S(1)} %get-tuple-element.42), channel_id=1, source_target_pairs={{0,9},{1,8},{2,11},{3,10},{4,13},{5,12},{6,15},{7,14},{8,1},{9,0},... | collective-permute-start | bytes 3080 | tf_op jit(solution)/shard_map/ppermute | solution.py:139
  43.3 2.8 %collective-permute-start.13 = (f32[1,256]{1,0:T(1,128)S(1)}, f32[1,256]{1,0:T(1,128)S(1)}, u32[]{:S(2)}, u32[]{:S(2)}) collective-permute-start(f32[1,256]{1,0:T(1,128)S(1)} %get-tuple-element.43), channel_id=1, source_target_pairs={{0,12},{1,13},{2,14},{3,15},{4,8},{5,9},{6,10},{7,11},{8,4},{9,5},... | collective-permute-start | bytes 3080 | tf_op jit(solution)/shard_map/ppermute | solution.py:139
  46.5 1.5 %collective-permute-start.15 = (f32[1,256]{1,0:T(1,128)S(1)}, f32[1,256]{1,0:T(1,128)S(1)}, u32[]{:S(2)}, u32[]{:S(2)}) collective-permute-start(f32[1,256]{1,0:T(1,128)S(1)} %get-tuple-element.37.refs_7_), channel_id=1, source_target_pairs={{0,2},{1,3},{2,0},{3,1},{4,6},{5,7},{6,4},{7,5},{8,10},{9,11},{10,... | collective-permute-start | bytes 3080 | tf_op jit(solution)/shard_map/ppermute | solution.py:139
  47.9 0.7 collective-permute-start.16
  48.6 0.5 collective-permute-start.17
  49.2 1.7 %collective-permute-start.18 = (f32[1,256]{1,0:T(1,128)S(1)}, f32[1,256]{1,0:T(1,128)S(1)}, u32[]{:S(2)}, u32[]{:S(2)}) collective-permute-start(f32[1,256]{1,0:T(1,128)S(1)} %get-tuple-element.40), channel_id=1, source_target_pairs={{0,7},{1,6},{2,5},{3,4},{4,3},{5,2},{6,1},{7,0},{8,15},{9,14},{10,... | collective-permute-start | bytes 3080 | tf_op jit(solution)/shard_map/ppermute | solution.py:139
  51.0 2.3 %collective-permute-start.19 = (f32[1,256]{1,0:T(1,128)S(1)}, f32[1,256]{1,0:T(1,128)S(1)}, u32[]{:S(2)}, u32[]{:S(2)}) collective-permute-start(f32[1,256]{1,0:T(1,128)S(1)} %get-tuple-element.41), channel_id=1, source_target_pairs={{0,10},{1,11},{2,8},{3,9},{4,14},{5,15},{6,12},{7,13},{8,2},{9,3},... | collective-permute-start | bytes 3080 | tf_op jit(solution)/shard_map/ppermute | solution.py:139
  53.3 1.6 %collective-permute-start.20 = (f32[1,256]{1,0:T(1,128)S(1)}, f32[1,256]{1,0:T(1,128)S(1)}, u32[]{:S(2)}, u32[]{:S(2)}) collective-permute-start(f32[1,256]{1,0:T(1,128)S(1)} %get-tuple-element.42), channel_id=1, source_target_pairs={{0,11},{1,10},{2,9},{3,8},{4,15},{5,14},{6,13},{7,12},{8,3},{9,2},... | collective-permute-start | bytes 3080 | tf_op jit(solution)/shard_map/ppermute | solution.py:139
  54.9 3.8 %collective-permute-start.21 = (f32[1,256]{1,0:T(1,128)S(1)}, f32[1,256]{1,0:T(1,128)S(1)}, u32[]{:S(2)}, u32[]{:S(2)}) collective-permute-start(f32[1,256]{1,0:T(1,128)S(1)} %get-tuple-element.43), channel_id=1, source_target_pairs={{0,14},{1,15},{2,12},{3,13},{4,10},{5,11},{6,8},{7,9},{8,6},{9,7},... | collective-permute-start | bytes 3080 | tf_op jit(solution)/shard_map/ppermute | solution.py:139
  59.0 0.7 collective-permute-start.8
  59.7 1.4 %collective-permute-done.21.refs_21_ = f32[1,256]{1,0:T(1,128)S(1)} collective-permute-done((f32[1,256]{1,0:T(1,128)S(1)}, f32[1,256]{1,0:T(1,128)S(1)}, u32[]{:S(2)}, u32[]{:S(2)}) %collective-permute-start.21) | collective-permute-done | bytes 1056 | tf_op jit(solution)/shard_map/ppermute | solution.py:139
  61.1 3.2 %collective-permute-done.22.refs_22_ = f32[1,256]{1,0:T(1,128)S(1)} collective-permute-done((f32[1,256]{1,0:T(1,128)S(1)}, f32[1,256]{1,0:T(1,128)S(1)}, u32[]{:S(2)}, u32[]{:S(2)}) %collective-permute-start.22) | collective-permute-done | bytes 1056 | tf_op jit(solution)/shard_map/ppermute | solution.py:139
  64.4 1.2 %shard_map.115 = (f32[1,1024]{1,0:T(1,128)S(1)}, f32[1,256]{1,0:T(1,128)S(1)}, f32[1,256]{1,0:T(1,128)S(1)}, f32[1,256]{1,0:T(1,128)S(1)}, f32[1,256]{1,0:T(1,12...) custom-call(s32[4]{0:T(128)S(1)} %pad_add_fusion.refs_0_, ...), custom_call_target="tpu_custom_call" | custom-call | bytes 57360 | tf_op jit(solution)/shard_map/pallas_call | solution.py:146
  65.6 0.7 fusion
  66.2 0.4 collective-permute-start.23
  66.8 1.9 %collective-permute-start.31 = (f32[1,256]{1,0:T(1,128)S(1)}, f32[1,256]{1,0:T(1,128)S(1)}, u32[]{:S(2)}, u32[]{:S(2)}) collective-permute-start(f32[1,256]{1,0:T(1,128)S(1)} %get-tuple-element.48), channel_id=1, source_target_pairs={{0,4},{1,5},{4,0},{5,1},{8,12},{9,13},{12,8},{13,9},{2,6},{3,7},{6... | collective-permute-start | bytes 3080 | tf_op jit(solution)/shard_map/ppermute | solution.py:139
  68.8 1.8 %collective-permute-start.33 = (f32[1,256]{1,0:T(1,128)S(1)}, f32[1,256]{1,0:T(1,128)S(1)}, u32[]{:S(2)}, u32[]{:S(2)}) collective-permute-start(f32[1,256]{1,0:T(1,128)S(1)} %get-tuple-element.50), channel_id=1, source_target_pairs={{0,8},{1,9},{4,12},{5,13},{8,0},{9,1},{12,4},{13,5},{2,10},{3,11},... | collective-permute-start | bytes 3080 | tf_op jit(solution)/shard_map/ppermute | solution.py:139
  70.5 0.7 collective-permute-start.34
  71.2 0.4 collective-permute-done.32.refs_12_
  71.6 1.9 %collective-permute-start.35 = (f32[1,256]{1,0:T(1,128)S(1)}, f32[1,256]{1,0:T(1,128)S(1)}, u32[]{:S(2)}, u32[]{:S(2)}) collective-permute-start(f32[1,256]{1,0:T(1,128)S(1)} %get-tuple-element.52), channel_id=1, source_target_pairs={{0,12},{1,13},{4,8},{5,9},{8,4},{9,5},{12,0},{13,1},{2,14},{3,15},... | collective-permute-start | bytes 3080 | tf_op jit(solution)/shard_map/ppermute | solution.py:139
  73.5 2.2 %collective-permute-start.36 = (f32[1,256]{1,0:T(1,128)S(1)}, f32[1,256]{1,0:T(1,128)S(1)}, u32[]{:S(2)}, u32[]{:S(2)}) collective-permute-start(f32[1,256]{1,0:T(1,128)S(1)} %get-tuple-element.53), channel_id=1, source_target_pairs={{0,13},{1,12},{4,9},{5,8},{8,5},{9,4},{12,1},{13,0},{2,15},{3,14},... | collective-permute-start | bytes 3080 | tf_op jit(solution)/shard_map/ppermute | solution.py:139
  75.7 1.3 %collective-permute-done.35.refs_15_ = f32[1,256]{1,0:T(1,128)S(1)} collective-permute-done((f32[1,256]{1,0:T(1,128)S(1)}, f32[1,256]{1,0:T(1,128)S(1)}, u32[]{:S(2)}, u32[]{:S(2)}) %collective-permute-start.35) | collective-permute-done | bytes 1056 | tf_op jit(solution)/shard_map/ppermute | solution.py:139
  77.0 0.7 collective-permute-start.26
  77.7 0.7 collective-permute-done.36.refs_16_
  78.3 0.7 collective-permute-start.27
  79.0 2.2 %collective-permute-start.28 = (f32[2048]{0:T(1024)S(1)}, f32[2048]{0:T(1024)S(1)}, u32[]{:S(2)}, u32[]{:S(2)}) collective-permute-start(f32[2048]{0:T(1024)S(1)} %bitcast.32), channel_id=1, source_target_pairs={{0,12},{1,13},{4,8},{5,9},{8,4},{9,5},{12,0},{13,1},{2,14},{3,15},... | collective-permute-start | bytes 24584 | tf_op jit(solution)/shard_map/ppermute | solution.py:139
  81.3 1.9 %collective-permute-start.29 = (f32[2048]{0:T(1024)S(1)}, f32[2048]{0:T(1024)S(1)}, u32[]{:S(2)}, u32[]{:S(2)}) collective-permute-start(f32[2048]{0:T(1024)S(1)} %bitcast.33), channel_id=1, source_target_pairs={{0,13},{1,12},{4,9},{5,8},{8,5},{9,4},{12,1},{13,0},{2,15},{3,14},... | collective-permute-start | bytes 24584 | tf_op jit(solution)/shard_map/ppermute | solution.py:139
  83.2 2.4 %shard_map.116 = f32[512,256]{1,0:T(8,128)} custom-call(f32[512,256]{1,0:T(8,128)S(1)} %copy-done.7, bf16[272,256]{1,0:T(8,128)(2,1)S(1)} %get-tuple-element.29.refs_1_, bf16[272,256]{1,0:T(8,128)(2,1)S(1)} %collective-permute-done.1.refs_2_, bf16[272,256]{1,0:T(8,128)(2,1)S(1)} %collective-permute-done.2.refs_3_, ...), custom_call_target="tpu_custom_call" | custom-call | flops 1073741824 | bytes 2170880 | tf_op jit(solution)/shard_map/pallas_call | solution.py:146
  85.7 0.5 collective-permute-done.29
  86.2 0.6 multiply_add_fusion
  (60 shorter events, 1.4 us)
Async XLA Ops:
  0.7 0.7 copy-start
  1.4 0.7 copy-start.2
  2.1 1.0 %copy-start.6 = (bf16[1024,256]{1,0:T(8,128)(2,1)S(1)}, bf16[1024,256]{1,0:T(8,128)(2,1)}, u32[]{:S(2)}) copy-start(bf16[1024,256]{1,0:T(8,128)(2,1)} %refs_5_.1) | copy-start | bytes 1572868
  3.1 0.7 copy-start.8
  4.5 28.0 %copy-start.7 = (f32[512,256]{1,0:T(8,128)S(1)}, f32[512,256]{1,0:T(8,128)}, u32[]{:S(2)}) copy-start(f32[512,256]{1,0:T(8,128)} %refs_0_.3) | copy-start | bytes 1572868
  7.6 6.7 %collective-permute-start.1 = (bf16[272,256]{1,0:T(8,128)(2,1)S(1)}, bf16[272,256]{1,0:T(8,128)(2,1)S(1)}, u32[]{:S(2)}, u32[]{:S(2)}) collective-permute-start(bf16[272,256]{1,0:T(8,128)(2,1)S(1)} %get-tuple-element.30), channel_id=1, source_target_pairs={{0,1},{1,0},{4,5},{5,4},{8,9},{9,8},{12,13},{13,12},{2,3},{3,2},{6... | collective-permute-start | bytes 417800 | tf_op jit(solution)/shard_map/ppermute | solution.py:139
  8.1 12.7 %collective-permute-start.2 = (bf16[272,256]{1,0:T(8,128)(2,1)S(1)}, bf16[272,256]{1,0:T(8,128)(2,1)S(1)}, u32[]{:S(2)}, u32[]{:S(2)}) collective-permute-start(bf16[272,256]{1,0:T(8,128)(2,1)S(1)} %get-tuple-element.31), channel_id=1, source_target_pairs={{0,4},{1,5},{4,0},{5,1},{8,12},{9,13},{12,8},{13,9},{2,6},{3,7},{6... | collective-permute-start | bytes 417800 | tf_op jit(solution)/shard_map/ppermute | solution.py:139
  10.8 13.7 %collective-permute-start.3 = (bf16[272,256]{1,0:T(8,128)(2,1)S(1)}, bf16[272,256]{1,0:T(8,128)(2,1)S(1)}, u32[]{:S(2)}, u32[]{:S(2)}) collective-permute-start(bf16[272,256]{1,0:T(8,128)(2,1)S(1)} %get-tuple-element.32), channel_id=1, source_target_pairs={{0,5},{1,4},{4,1},{5,0},{8,13},{9,12},{12,9},{13,8},{2,7},{3,6},{6... | collective-permute-start | bytes 417800 | tf_op jit(solution)/shard_map/ppermute | solution.py:139
  10.8 15.4 %collective-permute-start.4 = (bf16[272,256]{1,0:T(8,128)(2,1)S(1)}, bf16[272,256]{1,0:T(8,128)(2,1)S(1)}, u32[]{:S(2)}, u32[]{:S(2)}) collective-permute-start(bf16[272,256]{1,0:T(8,128)(2,1)S(1)} %get-tuple-element.33), channel_id=1, source_target_pairs={{0,8},{1,9},{4,12},{5,13},{8,0},{9,1},{12,4},{13,5},{2,10},{3,11},... | collective-permute-start | bytes 417800 | tf_op jit(solution)/shard_map/ppermute | solution.py:139
  13.6 18.9 %collective-permute-start.5 = (bf16[272,256]{1,0:T(8,128)(2,1)S(1)}, bf16[272,256]{1,0:T(8,128)(2,1)S(1)}, u32[]{:S(2)}, u32[]{:S(2)}) collective-permute-start(bf16[272,256]{1,0:T(8,128)(2,1)S(1)} %get-tuple-element.34), channel_id=1, source_target_pairs={{0,9},{1,8},{4,13},{5,12},{8,1},{9,0},{12,5},{13,4},{2,11},{3,10},... | collective-permute-start | bytes 417800 | tf_op jit(solution)/shard_map/ppermute | solution.py:139
  14.3 18.2 %collective-permute-start.6 = (bf16[272,256]{1,0:T(8,128)(2,1)S(1)}, bf16[272,256]{1,0:T(8,128)(2,1)S(1)}, u32[]{:S(2)}, u32[]{:S(2)}) collective-permute-start(bf16[272,256]{1,0:T(8,128)(2,1)S(1)} %get-tuple-element.35), channel_id=1, source_target_pairs={{0,12},{1,13},{4,8},{5,9},{8,4},{9,5},{12,0},{13,1},{2,14},{3,15},... | collective-permute-start | bytes 417800 | tf_op jit(solution)/shard_map/ppermute | solution.py:139
  20.8 43.5 %copy-start.1 = (s32[1024,1]{0,1:T(1,128)S(1)}, s32[1024,1]{0,1:T(1,128)}, u32[]{:S(2)}) copy-start(s32[1024,1]{0,1:T(1,128)} %param.14) | copy-start | bytes 12292
  20.8 43.5 %copy-start.3 = (s32[1024,1]{0,1:T(1,128)S(1)}, s32[1024,1]{0,1:T(1,128)}, u32[]{:S(2)}) copy-start(s32[1024,1]{0,1:T(1,128)} %param.16) | copy-start | bytes 12292
  20.8 43.5 %copy-start.4 = (s32[1024]{0:T(1024)S(1)}, s32[1024]{0:T(1024)}, u32[]{:S(2)}) copy-start(s32[1024]{0:T(1024)} %param.18) | copy-start | bytes 12292
  20.8 43.5 %copy-start.5 = (s32[1024]{0:T(1024)S(1)}, s32[1024]{0:T(1024)}, u32[]{:S(2)}) copy-start(s32[1024]{0:T(1024)} %param.19) | copy-start | bytes 12292
  20.8 44.8 %copy-start.10 = (bf16[1024,2048]{1,0:T(8,128)(2,1)S(1)}, bf16[1024,2048]{1,0:T(8,128)(2,1)}, u32[]{:S(2)}) copy-start(bf16[1024,2048]{1,0:T(8,128)(2,1)} %param.10) | copy-start | bytes 12582916
  20.8 11.7 %collective-permute-start.7 = (bf16[272,256]{1,0:T(8,128)(2,1)S(1)}, bf16[272,256]{1,0:T(8,128)(2,1)S(1)}, u32[]{:S(2)}, u32[]{:S(2)}) collective-permute-start(bf16[272,256]{1,0:T(8,128)(2,1)S(1)} %get-tuple-element.36), channel_id=1, source_target_pairs={{0,13},{1,12},{4,9},{5,8},{8,5},{9,4},{12,1},{13,0},{2,15},{3,14},... | collective-permute-start | bytes 417800 | tf_op jit(solution)/shard_map/ppermute | solution.py:139
  24.4 21.7 %collective-permute-start = (f32[1024]{0:T(1024)S(1)}, f32[1024]{0:T(1024)S(1)}, u32[]{:S(2)}, u32[]{:S(2)}) collective-permute-start(f32[1024]{0:T(1024)S(1)} %bitcast.35), channel_id=1, source_target_pairs={{0,2},{2,0},{1,3},{3,1},{4,6},{6,4},{5,7},{7,5},{8,10},{10,8},{9,1... | collective-permute-start | bytes 12296 | tf_op jit(solution)/shard_map/ppermute | solution.py:139
  33.8 52.3 %copy-start.11 = (bf16[2048]{0:T(1024)(128)(2,1)S(1)}, bf16[2048]{0:T(1024)(128)(2,1)}, u32[]{:S(2)}) copy-start(bf16[2048]{0:T(1024)(128)(2,1)} %param.11) | copy-start | bytes 12292
  33.8 12.6 %collective-permute-start.10 = (f32[1,256]{1,0:T(1,128)S(1)}, f32[1,256]{1,0:T(1,128)S(1)}, u32[]{:S(2)}, u32[]{:S(2)}) collective-permute-start(f32[1,256]{1,0:T(1,128)S(1)} %get-tuple-element.40), channel_id=1, source_target_pairs={{0,5},{1,4},{2,7},{3,6},{4,1},{5,0},{6,3},{7,2},{8,13},{9,12},{10,... | collective-permute-start | bytes 3080 | tf_op jit(solution)/shard_map/ppermute | solution.py:139
  40.2 7.8 %collective-permute-start.11 = (f32[1,256]{1,0:T(1,128)S(1)}, f32[1,256]{1,0:T(1,128)S(1)}, u32[]{:S(2)}, u32[]{:S(2)}) collective-permute-start(f32[1,256]{1,0:T(1,128)S(1)} %get-tuple-element.41), channel_id=1, source_target_pairs={{0,8},{1,9},{2,10},{3,11},{4,12},{5,13},{6,14},{7,15},{8,0},{9,1},... | collective-permute-start | bytes 3080 | tf_op jit(solution)/shard_map/ppermute | solution.py:139
  42.4 6.2 %collective-permute-start.12 = (f32[1,256]{1,0:T(1,128)S(1)}, f32[1,256]{1,0:T(1,128)S(1)}, u32[]{:S(2)}, u32[]{:S(2)}) collective-permute-start(f32[1,256]{1,0:T(1,128)S(1)} %get-tuple-element.42), channel_id=1, source_target_pairs={{0,9},{1,8},{2,11},{3,10},{4,13},{5,12},{6,15},{7,14},{8,1},{9,0},... | collective-permute-start | bytes 3080 | tf_op jit(solution)/shard_map/ppermute | solution.py:139
  43.3 5.8 %collective-permute-start.13 = (f32[1,256]{1,0:T(1,128)S(1)}, f32[1,256]{1,0:T(1,128)S(1)}, u32[]{:S(2)}, u32[]{:S(2)}) collective-permute-start(f32[1,256]{1,0:T(1,128)S(1)} %get-tuple-element.43), channel_id=1, source_target_pairs={{0,12},{1,13},{2,14},{3,15},{4,8},{5,9},{6,10},{7,11},{8,4},{9,5},... | collective-permute-start | bytes 3080 | tf_op jit(solution)/shard_map/ppermute | solution.py:139
  46.2 4.8 %collective-permute-start.14 = (f32[1,256]{1,0:T(1,128)S(1)}, f32[1,256]{1,0:T(1,128)S(1)}, u32[]{:S(2)}, u32[]{:S(2)}) collective-permute-start(f32[1,256]{1,0:T(1,128)S(1)} %get-tuple-element.44), channel_id=1, source_target_pairs={{0,13},{1,12},{2,15},{3,14},{4,9},{5,8},{6,11},{7,10},{8,5},{9,4},... | collective-permute-start | bytes 3080 | tf_op jit(solution)/shard_map/ppermute | solution.py:139
  46.5 6.8 %collective-permute-start.15 = (f32[1,256]{1,0:T(1,128)S(1)}, f32[1,256]{1,0:T(1,128)S(1)}, u32[]{:S(2)}, u32[]{:S(2)}) collective-permute-start(f32[1,256]{1,0:T(1,128)S(1)} %get-tuple-element.37.refs_7_), channel_id=1, source_target_pairs={{0,2},{1,3},{2,0},{3,1},{4,6},{5,7},{6,4},{7,5},{8,10},{9,11},{10,... | collective-permute-start | bytes 3080 | tf_op jit(solution)/shard_map/ppermute | solution.py:139
  47.9 6.9 %collective-permute-start.16 = (f32[1,256]{1,0:T(1,128)S(1)}, f32[1,256]{1,0:T(1,128)S(1)}, u32[]{:S(2)}, u32[]{:S(2)}) collective-permute-start(f32[1,256]{1,0:T(1,128)S(1)} %get-tuple-element.38), channel_id=1, source_target_pairs={{0,3},{1,2},{2,1},{3,0},{4,7},{5,6},{6,5},{7,4},{8,11},{9,10},{10,... | collective-permute-start | bytes 3080 | tf_op jit(solution)/shard_map/ppermute | solution.py:139
  48.6 10.0 %collective-permute-start.17 = (f32[1,256]{1,0:T(1,128)S(1)}, f32[1,256]{1,0:T(1,128)S(1)}, u32[]{:S(2)}, u32[]{:S(2)}) collective-permute-start(f32[1,256]{1,0:T(1,128)S(1)} %get-tuple-element.39), channel_id=1, source_target_pairs={{0,6},{1,7},{2,4},{3,5},{4,2},{5,3},{6,0},{7,1},{8,14},{9,15},{10,... | collective-permute-start | bytes 3080 | tf_op jit(solution)/shard_map/ppermute | solution.py:139
  49.2 9.8 %collective-permute-start.18 = (f32[1,256]{1,0:T(1,128)S(1)}, f32[1,256]{1,0:T(1,128)S(1)}, u32[]{:S(2)}, u32[]{:S(2)}) collective-permute-start(f32[1,256]{1,0:T(1,128)S(1)} %get-tuple-element.40), channel_id=1, source_target_pairs={{0,7},{1,6},{2,5},{3,4},{4,3},{5,2},{6,1},{7,0},{8,15},{9,14},{10,... | collective-permute-start | bytes 3080 | tf_op jit(solution)/shard_map/ppermute | solution.py:139
  51.0 8.7 %collective-permute-start.19 = (f32[1,256]{1,0:T(1,128)S(1)}, f32[1,256]{1,0:T(1,128)S(1)}, u32[]{:S(2)}, u32[]{:S(2)}) collective-permute-start(f32[1,256]{1,0:T(1,128)S(1)} %get-tuple-element.41), channel_id=1, source_target_pairs={{0,10},{1,11},{2,8},{3,9},{4,14},{5,15},{6,12},{7,13},{8,2},{9,3},... | collective-permute-start | bytes 3080 | tf_op jit(solution)/shard_map/ppermute | solution.py:139
  53.3 6.5 %collective-permute-start.20 = (f32[1,256]{1,0:T(1,128)S(1)}, f32[1,256]{1,0:T(1,128)S(1)}, u32[]{:S(2)}, u32[]{:S(2)}) collective-permute-start(f32[1,256]{1,0:T(1,128)S(1)} %get-tuple-element.42), channel_id=1, source_target_pairs={{0,11},{1,10},{2,9},{3,8},{4,15},{5,14},{6,13},{7,12},{8,3},{9,2},... | collective-permute-start | bytes 3080 | tf_op jit(solution)/shard_map/ppermute | solution.py:139
  54.9 6.3 %collective-permute-start.21 = (f32[1,256]{1,0:T(1,128)S(1)}, f32[1,256]{1,0:T(1,128)S(1)}, u32[]{:S(2)}, u32[]{:S(2)}) collective-permute-start(f32[1,256]{1,0:T(1,128)S(1)} %get-tuple-element.43), channel_id=1, source_target_pairs={{0,14},{1,15},{2,12},{3,13},{4,10},{5,11},{6,8},{7,9},{8,6},{9,7},... | collective-permute-start | bytes 3080 | tf_op jit(solution)/shard_map/ppermute | solution.py:139
  58.6 5.7 %collective-permute-start.22 = (f32[1,256]{1,0:T(1,128)S(1)}, f32[1,256]{1,0:T(1,128)S(1)}, u32[]{:S(2)}, u32[]{:S(2)}) collective-permute-start(f32[1,256]{1,0:T(1,128)S(1)} %get-tuple-element.44), channel_id=1, source_target_pairs={{0,15},{1,14},{2,13},{3,12},{4,11},{5,10},{6,9},{7,8},{8,7},{9,6},... | collective-permute-start | bytes 3080 | tf_op jit(solution)/shard_map/ppermute | solution.py:139
  59.0 5.3 %collective-permute-start.8 = (f32[1,256]{1,0:T(1,128)S(1)}, f32[1,256]{1,0:T(1,128)S(1)}, u32[]{:S(2)}, u32[]{:S(2)}) collective-permute-start(f32[1,256]{1,0:T(1,128)S(1)} %get-tuple-element.38), channel_id=1, source_target_pairs={{0,1},{1,0},{2,3},{3,2},{4,5},{5,4},{6,7},{7,6},{8,9},{9,8},{10,11... | collective-permute-start | bytes 3080 | tf_op jit(solution)/shard_map/ppermute | solution.py:139
  59.7 4.6 %collective-permute-start.9 = (f32[1,256]{1,0:T(1,128)S(1)}, f32[1,256]{1,0:T(1,128)S(1)}, u32[]{:S(2)}, u32[]{:S(2)}) collective-permute-start(f32[1,256]{1,0:T(1,128)S(1)} %get-tuple-element.39), channel_id=1, source_target_pairs={{0,4},{1,5},{2,6},{3,7},{4,0},{5,1},{6,2},{7,3},{8,12},{9,13},{10,... | collective-permute-start | bytes 3080 | tf_op jit(solution)/shard_map/ppermute | solution.py:139
  66.2 12.8 %collective-permute-start.23 = (f32[2048]{0:T(1024)S(1)}, f32[2048]{0:T(1024)S(1)}, u32[]{:S(2)}, u32[]{:S(2)}) collective-permute-start(f32[2048]{0:T(1024)S(1)} %bitcast.27), channel_id=1, source_target_pairs={{0,1},{1,0},{4,5},{5,4},{8,9},{9,8},{12,13},{13,12},{2,3},{3,2},{6... | collective-permute-start | bytes 24584 | tf_op jit(solution)/shard_map/ppermute | solution.py:139
  66.6 14.7 %collective-permute-start.24 = (f32[2048]{0:T(1024)S(1)}, f32[2048]{0:T(1024)S(1)}, u32[]{:S(2)}, u32[]{:S(2)}) collective-permute-start(f32[2048]{0:T(1024)S(1)} %bitcast.28), channel_id=1, source_target_pairs={{0,4},{1,5},{4,0},{5,1},{8,12},{9,13},{12,8},{13,9},{2,6},{3,7},{6... | collective-permute-start | bytes 24584 | tf_op jit(solution)/shard_map/ppermute | solution.py:139
  66.6 2.2 %collective-permute-start.30 = (f32[1,256]{1,0:T(1,128)S(1)}, f32[1,256]{1,0:T(1,128)S(1)}, u32[]{:S(2)}, u32[]{:S(2)}) collective-permute-start(f32[1,256]{1,0:T(1,128)S(1)} %get-tuple-element.47), channel_id=1, source_target_pairs={{0,1},{1,0},{4,5},{5,4},{8,9},{9,8},{12,13},{13,12},{2,3},{3,2},{6... | collective-permute-start | bytes 3080 | tf_op jit(solution)/shard_map/ppermute | solution.py:139
  66.8 3.8 %collective-permute-start.31 = (f32[1,256]{1,0:T(1,128)S(1)}, f32[1,256]{1,0:T(1,128)S(1)}, u32[]{:S(2)}, u32[]{:S(2)}) collective-permute-start(f32[1,256]{1,0:T(1,128)S(1)} %get-tuple-element.48), channel_id=1, source_target_pairs={{0,4},{1,5},{4,0},{5,1},{8,12},{9,13},{12,8},{13,9},{2,6},{3,7},{6... | collective-permute-start | bytes 3080 | tf_op jit(solution)/shard_map/ppermute | solution.py:139
  68.6 3.0 %collective-permute-start.32 = (f32[1,256]{1,0:T(1,128)S(1)}, f32[1,256]{1,0:T(1,128)S(1)}, u32[]{:S(2)}, u32[]{:S(2)}) collective-permute-start(f32[1,256]{1,0:T(1,128)S(1)} %get-tuple-element.49), channel_id=1, source_target_pairs={{0,5},{1,4},{4,1},{5,0},{8,13},{9,12},{12,9},{13,8},{2,7},{3,6},{6... | collective-permute-start | bytes 3080 | tf_op jit(solution)/shard_map/ppermute | solution.py:139
  68.8 4.8 %collective-permute-start.33 = (f32[1,256]{1,0:T(1,128)S(1)}, f32[1,256]{1,0:T(1,128)S(1)}, u32[]{:S(2)}, u32[]{:S(2)}) collective-permute-start(f32[1,256]{1,0:T(1,128)S(1)} %get-tuple-element.50), channel_id=1, source_target_pairs={{0,8},{1,9},{4,12},{5,13},{8,0},{9,1},{12,4},{13,5},{2,10},{3,11},... | collective-permute-start | bytes 3080 | tf_op jit(solution)/shard_map/ppermute | solution.py:139
  70.5 5.2 %collective-permute-start.34 = (f32[1,256]{1,0:T(1,128)S(1)}, f32[1,256]{1,0:T(1,128)S(1)}, u32[]{:S(2)}, u32[]{:S(2)}) collective-permute-start(f32[1,256]{1,0:T(1,128)S(1)} %get-tuple-element.51), channel_id=1, source_target_pairs={{0,9},{1,8},{4,13},{5,12},{8,1},{9,0},{12,5},{13,4},{2,11},{3,10},... | collective-permute-start | bytes 3080 | tf_op jit(solution)/shard_map/ppermute | solution.py:139
  71.6 5.4 %collective-permute-start.35 = (f32[1,256]{1,0:T(1,128)S(1)}, f32[1,256]{1,0:T(1,128)S(1)}, u32[]{:S(2)}, u32[]{:S(2)}) collective-permute-start(f32[1,256]{1,0:T(1,128)S(1)} %get-tuple-element.52), channel_id=1, source_target_pairs={{0,12},{1,13},{4,8},{5,9},{8,4},{9,5},{12,0},{13,1},{2,14},{3,15},... | collective-permute-start | bytes 3080 | tf_op jit(solution)/shard_map/ppermute | solution.py:139
  73.5 4.8 %collective-permute-start.36 = (f32[1,256]{1,0:T(1,128)S(1)}, f32[1,256]{1,0:T(1,128)S(1)}, u32[]{:S(2)}, u32[]{:S(2)}) collective-permute-start(f32[1,256]{1,0:T(1,128)S(1)} %get-tuple-element.53), channel_id=1, source_target_pairs={{0,13},{1,12},{4,9},{5,8},{8,5},{9,4},{12,1},{13,0},{2,15},{3,14},... | collective-permute-start | bytes 3080 | tf_op jit(solution)/shard_map/ppermute | solution.py:139
  75.7 9.9 %collective-permute-start.25 = (f32[2048]{0:T(1024)S(1)}, f32[2048]{0:T(1024)S(1)}, u32[]{:S(2)}, u32[]{:S(2)}) collective-permute-start(f32[2048]{0:T(1024)S(1)} %bitcast.29), channel_id=1, source_target_pairs={{0,5},{1,4},{4,1},{5,0},{8,13},{9,12},{12,9},{13,8},{2,7},{3,6},{6... | collective-permute-start | bytes 24584 | tf_op jit(solution)/shard_map/ppermute | solution.py:139
  77.0 8.6 %collective-permute-start.26 = (f32[2048]{0:T(1024)S(1)}, f32[2048]{0:T(1024)S(1)}, u32[]{:S(2)}, u32[]{:S(2)}) collective-permute-start(f32[2048]{0:T(1024)S(1)} %bitcast.30), channel_id=1, source_target_pairs={{0,8},{1,9},{4,12},{5,13},{8,0},{9,1},{12,4},{13,5},{2,10},{3,11},... | collective-permute-start | bytes 24584 | tf_op jit(solution)/shard_map/ppermute | solution.py:139
  78.3 7.3 %collective-permute-start.27 = (f32[2048]{0:T(1024)S(1)}, f32[2048]{0:T(1024)S(1)}, u32[]{:S(2)}, u32[]{:S(2)}) collective-permute-start(f32[2048]{0:T(1024)S(1)} %bitcast.31), channel_id=1, source_target_pairs={{0,9},{1,8},{4,13},{5,12},{8,1},{9,0},{12,5},{13,4},{2,11},{3,10},... | collective-permute-start | bytes 24584 | tf_op jit(solution)/shard_map/ppermute | solution.py:139
  79.0 6.6 %collective-permute-start.28 = (f32[2048]{0:T(1024)S(1)}, f32[2048]{0:T(1024)S(1)}, u32[]{:S(2)}, u32[]{:S(2)}) collective-permute-start(f32[2048]{0:T(1024)S(1)} %bitcast.32), channel_id=1, source_target_pairs={{0,12},{1,13},{4,8},{5,9},{8,4},{9,5},{12,0},{13,1},{2,14},{3,15},... | collective-permute-start | bytes 24584 | tf_op jit(solution)/shard_map/ppermute | solution.py:139
  81.3 4.9 %collective-permute-start.29 = (f32[2048]{0:T(1024)S(1)}, f32[2048]{0:T(1024)S(1)}, u32[]{:S(2)}, u32[]{:S(2)}) collective-permute-start(f32[2048]{0:T(1024)S(1)} %bitcast.33), channel_id=1, source_target_pairs={{0,13},{1,12},{4,9},{5,8},{8,5},{9,4},{12,1},{13,0},{2,15},{3,14},... | collective-permute-start | bytes 24584 | tf_op jit(solution)/shard_map/ppermute | solution.py:139
  (1 other events, 0.7 us)

commit v2 on v1

v2 whole, which is shorter than its diff:
```python
import math

import jax
import jax.numpy as jnp
from jax import lax
from jax.experimental import pallas as pl
from jax.experimental.pallas import tpu as pltpu
from jax.sharding import PartitionSpec as P

F32 = jnp.float32
BF16 = jnp.bfloat16
HOME = ("rows", "ent")
EVERY = ("rows", "feat", "ent")
IDS = 16
PARAMS = pltpu.CompilerParams(vmem_limit_bytes=24 * 2**20)
SMEM = pl.BlockSpec(memory_space=pltpu.SMEM)
VMEM = pl.BlockSpec(memory_space=pltpu.VMEM)
HBM = pl.BlockSpec(memory_space=pltpu.HBM)


def lanes_dot(a, b):
    return lax.dot_general(a, b, (((1,), (1,)), ((), ())), preferred_element_type=F32)


def plain_dot(a, b):
    return lax.dot_general(a, b, (((1,), (0,)), ((), ())), preferred_element_type=F32)


def halves(x):
    high = x.astype(BF16)
    return high, (x - high.astype(F32)).astype(BF16)


def one_hot(row, count):
    return row == lax.broadcasted_iota(jnp.int32, (count, row.shape[1]), 0)


def dispatch_kernel(owners, capacity, where, *refs):
    sources, ranks, chunks = refs[:5], refs[5], refs[6 : 6 + owners]
    copies, sems = refs[6 + owners : 11 + owners], refs[11 + owners]
    moves = [pltpu.make_async_copy(sources[i], copies[i], sems.at[i]) for i in range(5)]
    for move in moves:
        move.start()
    member, item, member_local, item_local, feats = copies
    rows = feats.shape[0]
    step = min(256, rows)
    blocks = rows // step
    mine, on_item = where[0], where[1] > 0
    moves[0].wait()
    moves[1].wait()
    hits = jnp.concatenate(
        [one_hot(member[...], owners).astype(F32), one_hot(item[...], owners).astype(F32)], axis=0
    )
    stacked = jnp.concatenate([hits[:, b * step : (b + 1) * step] for b in range(blocks)], axis=0)
    upper = lax.broadcasted_iota(jnp.int32, (step, step), 0) <= lax.broadcasted_iota(
        jnp.int32, (step, step), 1
    )
    counts = plain_dot(stacked.astype(BF16), upper.astype(F32).astype(BF16))
    before = jnp.zeros((2 * owners, 1), F32)
    pieces = []
    for b in range(blocks):
        here = counts[2 * owners * b : 2 * owners * (b + 1)]
        taken = (here + before) * hits[:, b * step : (b + 1) * step]
        pieces.append(
            jnp.concatenate(
                [
                    jnp.sum(taken[:owners], axis=0, keepdims=True),
                    jnp.sum(taken[owners:], axis=0, keepdims=True),
                ],
                axis=0,
            )
        )
        before = before + here[:, step - 1 : step]
    rank = jnp.concatenate(pieces, axis=1).astype(jnp.int32) - 1
    ranks[...] = rank
    own = jnp.where(on_item, item[...], member[...])
    own_rank = jnp.where(on_item, rank[1:2], rank[0:1])
    moves[2].wait()
    moves[3].wait()
    local = jnp.where(on_item, item_local[...], member_local[...])
    place = (own ^ mine) * capacity + own_rank
    high = local >> 8
    ids = jnp.concatenate([high, local - (high << 8), jnp.zeros((IDS - 2, rows), jnp.int32)], axis=0)
    ids = ids.astype(F32).astype(BF16)
    moves[4].wait()
    for k in reversed(range(owners)):
        pick = one_hot(place - k * capacity, capacity).astype(F32).astype(BF16)
        chunks[k][:capacity] = plain_dot(pick, feats[...]).astype(BF16)
        chunks[k][capacity:, :capacity] = lanes_dot(ids, pick).astype(BF16)


def chunk_ids(chunk, capacity):
    pair = chunk[capacity:, :capacity].astype(F32)
    return (pair[0:1] * 256.0 + pair[1:2]).astype(jnp.int32)


def scores_kernel(owners, capacity, n_feat, n_ent, where, coefs, *refs):
    chunks, out = refs[:owners], refs[owners]
    entities = coefs.shape[0]
    mine = where[0]
    high, low = halves(coefs[...])
    for k in range(owners):
        feats = chunks[k][:capacity]
        every = lanes_dot(high, feats) + lanes_dot(low, feats)
        hits = one_hot(chunk_ids(chunks[k], capacity), entities)
        score = jnp.sum(jnp.where(hits, every, 0.0), axis=0, keepdims=True)
        home = mine ^ k
        for f in range(n_feat):
            out[(home // n_ent * n_feat + f) * n_ent + home % n_ent] = score


def home_kernel(
    owners, capacity, n_feat, n_ent, where, member, item, ranks, clicks, valid, margin, scores, features, out
):
    on_item = where[1] > 0
    total = margin[...]
    hits_of = [one_hot(owner[...], owners).astype(F32) for owner in (member, item)]
    spot_of = [one_hot(ranks[side : side + 1], capacity).astype(F32).astype(BF16) for side in (0, 1)]
    for side in (0, 1):
        table = None
        for f in range(side * n_feat // 2, (side + 1) * n_feat // 2):
            part = jnp.concatenate(
                [scores[(h // n_ent * n_feat + f) * n_ent + h % n_ent] for h in range(owners)], axis=0
            )
            table = part if table is None else table + part
        found = plain_dot(jnp.concatenate(halves(table), axis=0), spot_of[side])
        total = total + jnp.sum((found[:owners] + found[owners:]) * hits_of[side], axis=0, keepdims=True)
    resid = valid[...].astype(F32) * (jax.nn.sigmoid(total) - clicks[...].astype(F32))
    hits = jnp.where(on_item, hits_of[1], hits_of[0])
    spot = jnp.where(on_item, spot_of[1], spot_of[0])
    sent = lanes_dot(jnp.concatenate(halves(hits * resid), axis=0), spot)
    sent = sent[:owners] + sent[owners:]
    low = jnp.broadcast_to(resid, (16, resid.shape[1])).astype(BF16)
    grad = plain_dot(low, features[...])[0:1]
    for h in range(owners):
        out[h, :, :capacity] = sent[h : h + 1]
        out[h, :, capacity:] = grad


def grads_kernel(owners, capacity, scale, where, coefs, weight, came, *refs):
    chunks, grad_global, grad_coefs = refs[:owners], refs[owners], refs[owners + 1]
    entities = coefs.shape[0]
    mine = where[0]
    summed = came[0][:, capacity:]
    for h in range(1, owners):
        summed = summed + came[h][:, capacity:]
    grad_global[...] = summed * scale + 4.0 * weight[...]
    total = coefs[...]
    for k in range(owners):
        resid = came[mine ^ k][:, :capacity]
        hits = one_hot(chunk_ids(chunks[k], capacity), entities)
        high, low = halves(jnp.where(hits, resid, 0.0))
        feats = chunks[k][:capacity]
        total = total + plain_dot(high, feats) + plain_dot(low, feats)
    grad_coefs[...] = total


def xor_send(x, axes, size, k):
    return x if k == 0 else lax.ppermute(x, axes, [(i, i ^ k) for i in range(size)])


def call(kernel, out_shape, operands, in_specs, flops=0, scratch=()):
    moved = sum(x.size * x.dtype.itemsize for x in (*operands, *out_shape))
    return pl.pallas_call(
        kernel,
        out_shape=out_shape,
        in_specs=in_specs,
        out_specs=[VMEM] * len(out_shape),
        scratch_shapes=scratch,
        compiler_params=PARAMS,
        cost_estimate=pl.CostEstimate(flops=flops, bytes_accessed=moved, transcendentals=0),
    )(*operands)


def body(
    features,
    global_weight,
    entity_feats,
    coefs,
    member_owner,
    member_local,
    item_owner,
    item_local,
    clicks,
    valid,
):
    rows_here, width = entity_feats.shape
    columns = features.shape[1]
    n_feat, n_ent = lax.axis_size("feat"), lax.axis_size("ent")
    owners = lax.axis_size("rows") * n_ent
    capacity = 2 * rows_here // owners
    mine = lax.axis_index(HOME).astype(jnp.int32)
    on_item = (lax.axis_index("feat") >= n_feat // 2).astype(jnp.int32)
    where = jnp.stack([mine, on_item])
    member, item = member_owner.reshape(1, rows_here), item_owner.reshape(1, rows_here)

    def shape(*dims, dtype=F32):
        return jax.ShapeDtypeStruct(dims, dtype)

    def partial(kernel, *args):
        return lambda *refs: kernel(*args, *refs)

    row = pltpu.VMEM((1, rows_here), jnp.int32)
    ranks, *chunks = call(
        partial(dispatch_kernel, owners, capacity),
        [shape(2, rows_here, dtype=jnp.int32)] + [shape(capacity + IDS, width, dtype=BF16)] * owners,
        (where, member, item, member_local.reshape(1, rows_here), item_local.reshape(1, rows_here), entity_feats),
        [SMEM] + [HBM] * 5,
        flops=2 * owners * capacity * rows_here * width,
        scratch=[row, row, row, row, pltpu.VMEM((rows_here, width), BF16), pltpu.SemaphoreType.DMA((5,))],
    )
    arrived = [None] * owners
    for k in reversed(range(owners)):
        arrived[k] = xor_send(chunks[k], HOME, owners, k)

    global_part = jnp.dot(features, global_weight, preferred_element_type=F32)
    global_total = global_part
    for q in range(1, n_feat):
        global_total = global_total + xor_send(global_part, "feat", n_feat, q)

    (scores,) = call(
        partial(scores_kernel, owners, capacity, n_feat, n_ent),
        [shape(n_feat * owners, 1, capacity)],
        (where, coefs, *arrived),
        [SMEM] + [VMEM] * (1 + owners),
        flops=4 * coefs.size * owners * capacity,
    )
    returned = lax.all_to_all(scores, EVERY, split_axis=0, concat_axis=0, tiled=True)
    (sent,) = call(
        partial(home_kernel, owners, capacity, n_feat, n_ent),
        [shape(owners, 1, capacity + columns)],
        (
            where,
            member,
            item,
            ranks,
            clicks.reshape(1, rows_here),
            valid.reshape(1, rows_here),
            global_total.reshape(1, rows_here),
            returned,
            features,
        ),
        [SMEM] + [VMEM] * 8,
        flops=32 * features.size,
    )
    came = lax.all_to_all(sent, HOME, split_axis=0, concat_axis=0, tiled=True)
    grad_global, grad_coefs = call(
        partial(grads_kernel, owners, capacity, 1.0 / math.sqrt(rows_here * owners)),
        [shape(1, columns), shape(*coefs.shape)],
        (where, coefs, global_weight.astype(F32).reshape(1, columns), came, *arrived),
        [SMEM] + [VMEM] * (3 + owners),
        flops=4 * coefs.size * owners * capacity,
    )
    return (grad_global.reshape(columns), grad_coefs)


def solution(mesh):
    by_row = P(("groups", "rows", "ent"))
    by_both = P(("groups", "rows", "ent"), "feat")
    column = P(("groups", "rows", "ent"), None)
    by_feat = P(("groups", "feat"))
    return jax.shard_map(
        body,
        mesh=mesh,
        in_specs=(by_both, by_feat, by_both, by_both, column, by_row, column, by_row, by_row, by_row),
        out_specs=(by_feat, by_both),
        check_vma=False,
    )
```

time: 87.1 us -> 73.1 us (0.84)
  starting transfers between devices: 51.8 us -> 27.3 us
  waiting for transfers between devices: 16.7 us -> 22.3 us
  local copies, waits for them, and re-layouts: 4.53 us -> 7.73 us
  Pallas kernels: 8.07 us -> 11 us
    ppermute x37 -> x8, starting transfers between devices: 51.8 us -> 11.5 us  [xor_send(): lax.ppermute(x, axes, [(i, i ^ k) for i in range(size)])]
    all_to_all x0 -> x2, starting transfers between devices: none -> 15.8 us  [the longest x1 10.7 us: body(): lax.all_to_all(scores, EVERY, split_axis=0, concat_axis=0, tiled=True)]
    all_to_all x0 -> x2, waiting for transfers between devices: none -> 6 us  [the longest x1 6 us: body(): came = lax.all_to_all(sent, HOME, split_axis=0, concat_axis=0, tiled=True)]
    unnamed x25 -> x27, local copies, waits for them, and re-layouts: 4.53 us -> 7.73 us
    pallas_call x4, Pallas kernels: 8.07 us -> 11 us  [call(): pl.pallas_call(kernel, out_shape=out_shape, in_specs=in_specs, out_specs=...]
    ppermute x37 -> x8, waiting for transfers between devices: 16.7 us -> 16.3 us  [xor_send(): lax.ppermute(x, axes, [(i, i ^ k) for i in range(size)])]
  transfers between devices with their start and end apart: 37 -> 10, of which waited for: 9 -> 5; matrix products, arithmetic and copies ran while one was open for 5% -> 6% of each run, Pallas kernels for 4% -> 0%
where the time goes in v2:
time: 73.1 us; the launch traced here: 72.5 us
  starting transfers between devices  27.3 us (37%)
  waiting for transfers between devices  22.3 us (31%)
  Pallas kernels  11 us (15%)
  local copies, waits for them, and re-layouts  7.73 us (11%)
  matrix products  3.43 us (5%)
  between operations  0.74 us (1%)
    ppermute x8, waiting for transfers between devices, xor_send(): lax.ppermute(x, axes, [(i, i ^ k) for i in range(size)])  16.3 us
    ppermute x8, starting transfers between devices, xor_send(): lax.ppermute(x, axes, [(i, i ^ k) for i in range(size)])  11.5 us
    pallas_call x4, Pallas kernels, call(): pl.pallas_call(kernel, out_shape=out_shape, in_specs=in_specs, out_specs=...  11 us
    all_to_all x1, starting transfers between devices, body(): lax.all_to_all(scores, EVERY, split_axis=0, concat_axis=0, tiled=True)  10.7 us
    unnamed x27, local copies, waits for them, and re-layouts  7.73 us
    all_to_all x1, waiting for transfers between devices, body(): came = lax.all_to_all(sent, HOME, split_axis=0, concat_axis=0, tiled=True)  6 us
    all_to_all x1, starting transfers between devices, body(): came = lax.all_to_all(sent, HOME, split_axis=0, concat_axis=0, tiled=True)  5 us
    dot_general x1, matrix products, body(): global_part = jnp.dot(features, global_weight, preferred_element_type=F32)  3.43 us
  transfers between devices with their start and end apart: 10, of which 5 were waited for; matrix products, arithmetic and copies ran while one was open for 6% of the time, Pallas kernels for 0%

profile of v2, /device:TPU:0, one launch (start us, length us, event | category | flops | bytes accessed | tf_op | source)
XLA Modules:
  0.0 72.5 jit_solution(4526416792741590971)
XLA Ops:
  0.6 0.1 pad_add_fusion.refs_0_
  0.7 0.0 copy-start.1
  0.7 0.7 copy-done.1
  1.4 0.0 copy-start.3
  1.4 0.7 copy-done.3
  2.1 0.0 copy-start.7
  2.1 1.0 %copy-done.7 = bf16[1024,256]{1,0:T(8,128)(2,1)S(1)} copy-done((bf16[1024,256]{1,0:T(8,128)(2,1)S(1)}, bf16[1024,256]{1,0:T(8,128)(2,1)}, u32[]{:S(2)}) %copy-start.7) | copy-done | bytes 524312
  3.1 0.7 copy-done.10
  3.8 0.0 copy-start.11
  3.8 0.7 copy-done.11
  4.5 3.2 %shard_map.113 = (s32[2,1024]{1,0:T(2,128)S(1)}, bf16[272,256]{1,0:T(8,128)(2,1)S(1)}, bf16[272,256]{1,0:T(8,128)(2,1)S(1)}, bf16[272,256]{1,0:T(8,128)(2,1)S(1)...) custom-call(s32[2]{0:T(128)S(1)} %pad_add_fusion.refs_0_, ...), custom_call_target="tpu_custom_call" | custom-call | flops 1073741824 | bytes 1662984 | tf_op jit(solution)/shard_map/pallas_call | solution.py:164
  7.7 0.5 collective-permute-start.1
  8.3 2.6 %collective-permute-start.2 = (bf16[272,256]{1,0:T(8,128)(2,1)S(1)}, bf16[272,256]{1,0:T(8,128)(2,1)S(1)}, u32[]{:S(2)}, u32[]{:S(2)}) collective-permute-start(bf16[272,256]{1,0:T(8,128)(2,1)S(1)} %get-tuple-element.16), channel_id=1, source_target_pairs={{0,4},{1,5},{4,0},{5,1},{8,12},{9,13},{12,8},{13,9},{2,6},{3,7},{6... | collective-permute-start | bytes 417800 | tf_op jit(solution)/shard_map/ppermute | solution.py:159
  10.9 0.1 collective-permute-start.3
  11.0 2.8 %collective-permute-start.4 = (bf16[272,256]{1,0:T(8,128)(2,1)S(1)}, bf16[272,256]{1,0:T(8,128)(2,1)S(1)}, u32[]{:S(2)}, u32[]{:S(2)}) collective-permute-start(bf16[272,256]{1,0:T(8,128)(2,1)S(1)} %get-tuple-element.18), channel_id=1, source_target_pairs={{0,8},{1,9},{4,12},{5,13},{8,0},{9,1},{12,4},{13,5},{2,10},{3,11},... | collective-permute-start | bytes 417800 | tf_op jit(solution)/shard_map/ppermute | solution.py:159
  13.7 0.0 collective-permute-start.5
  13.7 0.0 collective-permute-done.1.refs_3_.refs_5_
  13.7 3.6 %collective-permute-start.6 = (bf16[272,256]{1,0:T(8,128)(2,1)S(1)}, bf16[272,256]{1,0:T(8,128)(2,1)S(1)}, u32[]{:S(2)}, u32[]{:S(2)}) collective-permute-start(bf16[272,256]{1,0:T(8,128)(2,1)S(1)} %get-tuple-element.20), channel_id=1, source_target_pairs={{0,12},{1,13},{4,8},{5,9},{8,4},{9,5},{12,0},{13,1},{2,14},{3,15},... | collective-permute-start | bytes 417800 | tf_op jit(solution)/shard_map/ppermute | solution.py:159
  17.3 3.6 %collective-permute-done.2.refs_4_.refs_6_ = bf16[272,256]{1,0:T(8,128)(2,1)S(1)} collective-permute-done((bf16[272,256]{1,0:T(8,128)(2,1)S(1)}, bf16[272,256]{1,0:T(8,128)(2,1)S(1)}, u32[]{:S(2)}, u32[]{:S(2)}) %collective-permute-start.2) | collective-permute-done | bytes 139296 | tf_op jit(solution)/shard_map/ppermute | solution.py:159
  20.9 0.0 collective-permute-start.7
  20.9 0.7 reshape.46
  21.6 1.8 %collective-permute-done.3.refs_5_.refs_7_ = bf16[272,256]{1,0:T(8,128)(2,1)S(1)} collective-permute-done((bf16[272,256]{1,0:T(8,128)(2,1)S(1)}, bf16[272,256]{1,0:T(8,128)(2,1)S(1)}, u32[]{:S(2)}, u32[]{:S(2)}) %collective-permute-start.3) | collective-permute-done | bytes 139296 | tf_op jit(solution)/shard_map/ppermute | solution.py:159
  23.4 0.0 collective-permute-done.4.refs_6_.refs_8_
  23.4 9.2 %collective-permute-done.5.refs_7_.refs_9_ = bf16[272,256]{1,0:T(8,128)(2,1)S(1)} collective-permute-done((bf16[272,256]{1,0:T(8,128)(2,1)S(1)}, bf16[272,256]{1,0:T(8,128)(2,1)S(1)}, u32[]{:S(2)}, u32[]{:S(2)}) %collective-permute-start.5) | collective-permute-done | bytes 139296 | tf_op jit(solution)/shard_map/ppermute | solution.py:159
  32.6 0.0 collective-permute-done.6.refs_8_.refs_10_
  32.6 0.0 collective-permute-done.7.refs_9_.refs_11_
  32.6 0.0 copy-start.8
  32.6 1.0 %copy-done.8 = f32[512,256]{1,0:T(8,128)S(1)} copy-done((f32[512,256]{1,0:T(8,128)S(1)}, f32[512,256]{1,0:T(8,128)}, u32[]{:S(2)}) %copy-start.8) | copy-done | bytes 524312
  33.7 2.5 %shard_map.114 = f32[16,1,256]{2,1,0:T(1,128)} custom-call(s32[2]{0:T(128)S(1)} %pad_add_fusion.refs_0_, f32[512,256]{1,0:T(8,128)S(1)} %copy-done.8, bf16[272,256]{1,0:T(8,128)(2,1)S(1)} %get-tuple-element.14.refs_2_.refs_4_, bf16[272,256]{1,0:T(8,128)(2,1)S(1)} %collective-permute-done.1.refs_3_.refs_5_, ...), custom_call_target="tpu_custom_call" | custom-call | flops 1073741824 | bytes 1654792 | tf_op jit(solution)/shard_map/pallas_call | solution.py:164
  36.2 10.7 %all-to-all-start = ((f32[16,1,256]{2,1,0:T(1,128)}), f32[16,1,256]{2,1,0:T(1,128)S(1)}, u32[]{:S(2)}, u32[]{:S(2)}) async-start(f32[16,1,256]{2,1,0:T(1,128)} %shard_map.114), calls=%async_computation | async-start | bytes 32768 | tf_op jit(solution)/shard_map/all_to_all | solution.py:228
  46.9 0.0 copy-start.12
  46.9 0.0 copy-start.9
  46.9 3.4 %fusion = f32[1,1024]{1,0:T(1,128)S(1)} fusion(bf16[1024,2048]{1,0:T(8,128)(2,1)} %refs_8_.1, bf16[2048,1]{0,1:T(2,128)(2,1)S(1)} %reshape.46), kind=kOutput, calls=%fused_computation.1 | convolution fusion | flops 4194304 | bytes 4202496 | tf_op jit(solution)/shard_map/dot_general | solution.py:216
  50.4 1.9 %collective-permute-start = (f32[1024]{0:T(1024)S(1)}, f32[1024]{0:T(1024)S(1)}, u32[]{:S(2)}, u32[]{:S(2)}) collective-permute-start(f32[1024]{0:T(1024)S(1)} %bitcast.24), channel_id=1, source_target_pairs={{0,2},{2,0},{1,3},{3,1},{4,6},{6,4},{5,7},{7,5},{8,10},{10,8},{9,1... | collective-permute-start | bytes 12296 | tf_op jit(solution)/shard_map/ppermute | solution.py:159
  52.3 1.7 %collective-permute-done = f32[1024]{0:T(1024)S(1)} collective-permute-done((f32[1024]{0:T(1024)S(1)}, f32[1024]{0:T(1024)S(1)}, u32[]{:S(2)}, u32[]{:S(2)}) %collective-permute-start) | collective-permute-done | bytes 4128 | tf_op jit(solution)/shard_map/ppermute | solution.py:159
  54.0 0.0 all-to-all-done.refs_7_
  54.0 0.0 copy-done.2
  54.0 0.0 copy-done.4
  54.0 0.0 copy-done.5
  54.0 0.0 copy-done.6
  54.0 0.0 copy-start
  54.0 2.2 %copy-done = bf16[1024,2048]{1,0:T(8,128)(2,1)S(1)} copy-done((bf16[1024,2048]{1,0:T(8,128)(2,1)S(1)}, bf16[1024,2048]{1,0:T(8,128)(2,1)}, u32[]{:S(2)}) %copy-start) | copy-done | bytes 4194328
  56.2 2.3 %shard_map.115 = f32[8,1,2304]{2,1,0:T(1,128)} custom-call(s32[2]{0:T(128)S(1)} %pad_add_fusion.refs_0_, s32[1,1024]{1,0:T(1,128)S(1)} %bitcast.17, s32[1,1024]{1,0:T(1,128)S(1)} %bitcast.19, s32[2,1024]{1,0:T(2,128)S(1)} %get-tuple-element.13.refs_3_, s32[1,1024]{1,0:T(1,128)S(1)} %bitcast.20, s32[1,1024]{1,0:T(1,128)S(1)} %bitcast.21, ...), custom_call_target="tpu_custom_call" | custom-call | flops 67108864 | bytes 4313096 | tf_op jit(solution)/shard_map/pallas_call | solution.py:164
  58.6 5.0 %all-to-all-start.1 = ((f32[8,1,2304]{2,1,0:T(1,128)}), f32[8,1,2304]{2,1,0:T(1,128)S(1)}, u32[]{:S(2)}, u32[]{:S(2)}) async-start(f32[8,1,2304]{2,1,0:T(1,128)} %shard_map.115), calls=%async_computation.1 | async-start | bytes 147456 | tf_op jit(solution)/shard_map/all_to_all | solution.py:246
  63.6 0.0 copy-done.12
  63.6 6.0 %all-to-all-done.1.refs_3_ = f32[8,1,2304]{2,1,0:T(1,128)S(1)} async-done(((f32[8,1,2304]{2,1,0:T(1,128)}), f32[8,1,2304]{2,1,0:T(1,128)S(1)}, u32[]{:S(2)}, u32[]{:S(2)}) %all-to-all-start.1) | async-done | bytes 73760 | tf_op jit(solution)/shard_map/all_to_all | solution.py:246
  69.6 0.0 copy-done.9
  69.6 3.0 %shard_map.116 = (f32[1,2048]{1,0:T(1,128)}, f32[512,256]{1,0:T(8,128)}) custom-call(s32[2]{0:T(128)S(1)} %pad_add_fusion.refs_0_, f32[512,256]{1,0:T(8,128)S(1)} %copy-done.9, f32[1,2048]{1,0:T(1,128)S(1)} %bitcast.15, f32[8,1,2304]{2,1,0:T(1,128)S(1)} %all-to-all-done.1.refs_3_, bf16[272,256]{1,0:T(8,128)(2,1)S(1)} %get-tuple-element.14.refs_2_.refs_4_, ...), custom_call_target="tpu_custom_call" | custom-call | flops 1073741824 | bytes 2252808 | tf_op jit(solution)/shard_map/pallas_call | solution.py:164
  (7 shorter events, 0.0 us)
Async XLA Ops:
  0.7 0.7 copy-start.1
  1.4 0.7 copy-start.3
  2.1 1.0 %copy-start.7 = (bf16[1024,256]{1,0:T(8,128)(2,1)S(1)}, bf16[1024,256]{1,0:T(8,128)(2,1)}, u32[]{:S(2)}) copy-start(bf16[1024,256]{1,0:T(8,128)(2,1)} %refs_5_.1) | copy-start | bytes 1572868
  3.1 0.7 copy-start.10
  3.8 0.7 copy-start.11
  7.7 6.0 %collective-permute-start.1 = (bf16[272,256]{1,0:T(8,128)(2,1)S(1)}, bf16[272,256]{1,0:T(8,128)(2,1)S(1)}, u32[]{:S(2)}, u32[]{:S(2)}) collective-permute-start(bf16[272,256]{1,0:T(8,128)(2,1)S(1)} %get-tuple-element.15), channel_id=1, source_target_pairs={{0,1},{1,0},{4,5},{5,4},{8,9},{9,8},{12,13},{13,12},{2,3},{3,2},{6... | collective-permute-start | bytes 417800 | tf_op jit(solution)/shard_map/ppermute | solution.py:159
  8.3 12.7 %collective-permute-start.2 = (bf16[272,256]{1,0:T(8,128)(2,1)S(1)}, bf16[272,256]{1,0:T(8,128)(2,1)S(1)}, u32[]{:S(2)}, u32[]{:S(2)}) collective-permute-start(bf16[272,256]{1,0:T(8,128)(2,1)S(1)} %get-tuple-element.16), channel_id=1, source_target_pairs={{0,4},{1,5},{4,0},{5,1},{8,12},{9,13},{12,8},{13,9},{2,6},{3,7},{6... | collective-permute-start | bytes 417800 | tf_op jit(solution)/shard_map/ppermute | solution.py:159
  10.9 12.5 %collective-permute-start.3 = (bf16[272,256]{1,0:T(8,128)(2,1)S(1)}, bf16[272,256]{1,0:T(8,128)(2,1)S(1)}, u32[]{:S(2)}, u32[]{:S(2)}) collective-permute-start(bf16[272,256]{1,0:T(8,128)(2,1)S(1)} %get-tuple-element.17), channel_id=1, source_target_pairs={{0,5},{1,4},{4,1},{5,0},{8,13},{9,12},{12,9},{13,8},{2,7},{3,6},{6... | collective-permute-start | bytes 417800 | tf_op jit(solution)/shard_map/ppermute | solution.py:159
  11.0 12.4 %collective-permute-start.4 = (bf16[272,256]{1,0:T(8,128)(2,1)S(1)}, bf16[272,256]{1,0:T(8,128)(2,1)S(1)}, u32[]{:S(2)}, u32[]{:S(2)}) collective-permute-start(bf16[272,256]{1,0:T(8,128)(2,1)S(1)} %get-tuple-element.18), channel_id=1, source_target_pairs={{0,8},{1,9},{4,12},{5,13},{8,0},{9,1},{12,4},{13,5},{2,10},{3,11},... | collective-permute-start | bytes 417800 | tf_op jit(solution)/shard_map/ppermute | solution.py:159
  13.7 18.9 %collective-permute-start.5 = (bf16[272,256]{1,0:T(8,128)(2,1)S(1)}, bf16[272,256]{1,0:T(8,128)(2,1)S(1)}, u32[]{:S(2)}, u32[]{:S(2)}) collective-permute-start(bf16[272,256]{1,0:T(8,128)(2,1)S(1)} %get-tuple-element.19), channel_id=1, source_target_pairs={{0,9},{1,8},{4,13},{5,12},{8,1},{9,0},{12,5},{13,4},{2,11},{3,10},... | collective-permute-start | bytes 417800 | tf_op jit(solution)/shard_map/ppermute | solution.py:159
  13.7 18.9 %collective-permute-start.6 = (bf16[272,256]{1,0:T(8,128)(2,1)S(1)}, bf16[272,256]{1,0:T(8,128)(2,1)S(1)}, u32[]{:S(2)}, u32[]{:S(2)}) collective-permute-start(bf16[272,256]{1,0:T(8,128)(2,1)S(1)} %get-tuple-element.20), channel_id=1, source_target_pairs={{0,12},{1,13},{4,8},{5,9},{8,4},{9,5},{12,0},{13,1},{2,14},{3,15},... | collective-permute-start | bytes 417800 | tf_op jit(solution)/shard_map/ppermute | solution.py:159
  20.9 11.7 %collective-permute-start.7 = (bf16[272,256]{1,0:T(8,128)(2,1)S(1)}, bf16[272,256]{1,0:T(8,128)(2,1)S(1)}, u32[]{:S(2)}, u32[]{:S(2)}) collective-permute-start(bf16[272,256]{1,0:T(8,128)(2,1)S(1)} %get-tuple-element.21), channel_id=1, source_target_pairs={{0,13},{1,12},{4,9},{5,8},{8,5},{9,4},{12,1},{13,0},{2,15},{3,14},... | collective-permute-start | bytes 417800 | tf_op jit(solution)/shard_map/ppermute | solution.py:159
  32.6 1.0 %copy-start.8 = (f32[512,256]{1,0:T(8,128)S(1)}, f32[512,256]{1,0:T(8,128)}, u32[]{:S(2)}) copy-start(f32[512,256]{1,0:T(8,128)} %refs_1_.3) | copy-start | bytes 1572868
  33.7 20.3 %copy-start.2 = (s32[1024,1]{0,1:T(1,128)S(1)}, s32[1024,1]{0,1:T(1,128)}, u32[]{:S(2)}) copy-start(s32[1024,1]{0,1:T(1,128)} %param.14) | copy-start | bytes 12292
  33.7 20.3 %copy-start.4 = (s32[1024,1]{0,1:T(1,128)S(1)}, s32[1024,1]{0,1:T(1,128)}, u32[]{:S(2)}) copy-start(s32[1024,1]{0,1:T(1,128)} %param.16) | copy-start | bytes 12292
  33.7 20.4 %copy-start.5 = (s32[1024]{0:T(1024)S(1)}, s32[1024]{0:T(1024)}, u32[]{:S(2)}) copy-start(s32[1024]{0:T(1024)} %param.18) | copy-start | bytes 12292
  33.7 20.4 %copy-start.6 = (s32[1024]{0:T(1024)S(1)}, s32[1024]{0:T(1024)}, u32[]{:S(2)}) copy-start(s32[1024]{0:T(1024)} %param.19) | copy-start | bytes 12292
  36.2 17.8 %all-to-all-start = ((f32[16,1,256]{2,1,0:T(1,128)}), f32[16,1,256]{2,1,0:T(1,128)S(1)}, u32[]{:S(2)}, u32[]{:S(2)}) async-start(f32[16,1,256]{2,1,0:T(1,128)} %shard_map.114), calls=%async_computation | async-start | bytes 32768 | tf_op jit(solution)/shard_map/all_to_all | solution.py:228
  46.9 16.6 %copy-start.12 = (bf16[2048]{0:T(1024)(128)(2,1)S(1)}, bf16[2048]{0:T(1024)(128)(2,1)}, u32[]{:S(2)}) copy-start(bf16[2048]{0:T(1024)(128)(2,1)} %param.11) | copy-start | bytes 12292
  46.9 22.6 %copy-start.9 = (f32[512,256]{1,0:T(8,128)S(1)}, f32[512,256]{1,0:T(8,128)}, u32[]{:S(2)}) copy-start(f32[512,256]{1,0:T(8,128)} %refs_1_.3) | copy-start | bytes 1572868
  50.4 3.6 %collective-permute-start = (f32[1024]{0:T(1024)S(1)}, f32[1024]{0:T(1024)S(1)}, u32[]{:S(2)}, u32[]{:S(2)}) collective-permute-start(f32[1024]{0:T(1024)S(1)} %bitcast.24), channel_id=1, source_target_pairs={{0,2},{2,0},{1,3},{3,1},{4,6},{6,4},{5,7},{7,5},{8,10},{10,8},{9,1... | collective-permute-start | bytes 12296 | tf_op jit(solution)/shard_map/ppermute | solution.py:159
  54.0 2.2 %copy-start = (bf16[1024,2048]{1,0:T(8,128)(2,1)S(1)}, bf16[1024,2048]{1,0:T(8,128)(2,1)}, u32[]{:S(2)}) copy-start(bf16[1024,2048]{1,0:T(8,128)(2,1)} %refs_8_.1) | copy-start | bytes 12582916
  58.6 11.0 %all-to-all-start.1 = ((f32[8,1,2304]{2,1,0:T(1,128)}), f32[8,1,2304]{2,1,0:T(1,128)S(1)}, u32[]{:S(2)}, u32[]{:S(2)}) async-start(f32[8,1,2304]{2,1,0:T(1,128)} %shard_map.115), calls=%async_computation.1 | async-start | bytes 147456 | tf_op jit(solution)/shard_map/all_to_all | solution.py:246

commit v3 on v2

v3 whole, which is shorter than its diff:
```python
import math

import jax
import jax.numpy as jnp
from jax import lax
from jax.experimental import pallas as pl
from jax.experimental.pallas import tpu as pltpu
from jax.sharding import PartitionSpec as P

F32 = jnp.float32
BF16 = jnp.bfloat16
HOME = ("rows", "ent")
EVERY = ("rows", "feat", "ent")
IDS = 16
PARAMS = pltpu.CompilerParams(vmem_limit_bytes=24 * 2**20)
SMEM = pl.BlockSpec(memory_space=pltpu.SMEM)
VMEM = pl.BlockSpec(memory_space=pltpu.VMEM)
HBM = pl.BlockSpec(memory_space=pltpu.HBM)


def lanes_dot(a, b):
    return lax.dot_general(a, b, (((1,), (1,)), ((), ())), preferred_element_type=F32)


def plain_dot(a, b):
    return lax.dot_general(a, b, (((1,), (0,)), ((), ())), preferred_element_type=F32)


def halves(x):
    high = x.astype(BF16)
    return high, (x - high.astype(F32)).astype(BF16)


def one_hot(row, count):
    return row == lax.broadcasted_iota(jnp.int32, (count, row.shape[1]), 0)


def ranks_of(owners, member, item):
    rows = member.shape[1]
    step = min(256, rows)
    blocks = rows // step
    hits = jnp.concatenate([one_hot(member, owners).astype(F32), one_hot(item, owners).astype(F32)], axis=0)
    stacked = jnp.concatenate([hits[:, b * step : (b + 1) * step] for b in range(blocks)], axis=0)
    upper = lax.broadcasted_iota(jnp.int32, (step, step), 0) <= lax.broadcasted_iota(
        jnp.int32, (step, step), 1
    )
    counts = plain_dot(stacked.astype(BF16), upper.astype(F32).astype(BF16))
    before = jnp.zeros((2 * owners, 1), F32)
    pieces = []
    for b in range(blocks):
        here = counts[2 * owners * b : 2 * owners * (b + 1)]
        taken = (here + before) * hits[:, b * step : (b + 1) * step]
        sides = [jnp.sum(x, axis=0, keepdims=True) for x in (taken[:owners], taken[owners:])]
        pieces.append(jnp.concatenate(sides, axis=0))
        before = before + here[:, step - 1 : step]
    return jnp.concatenate(pieces, axis=1).astype(jnp.int32) - 1


def pack_chunk(k, capacity, place, ids, feats, chunk):
    pick = one_hot(place - k * capacity, capacity).astype(F32).astype(BF16)
    chunk[:capacity] = plain_dot(pick, feats).astype(BF16)
    chunk[capacity:, :capacity] = lanes_dot(ids, pick).astype(BF16)


def far_kernel(owners, capacity, far, where, *refs):
    sources, ranks, place_out, ids_out = refs[:5], refs[5], refs[6], refs[7]
    chunks, copies, sems = refs[8 : 8 + len(far)], refs[8 + len(far) : 13 + len(far)], refs[13 + len(far)]
    moves = [pltpu.make_async_copy(sources[i], copies[i], sems.at[i]) for i in range(5)]
    for move in moves:
        move.start()
    for move in moves[:4]:
        move.wait()
    member, item, member_local, item_local = [copy[...] for copy in copies[:4]]
    rows = member.shape[1]
    mine, on_item = where[0], where[1] > 0
    rank = ranks_of(owners, member, item)
    ranks[...] = rank
    own = jnp.where(on_item, item, member)
    place = (own ^ mine) * capacity + jnp.where(on_item, rank[1:2], rank[0:1])
    place_out[...] = place
    local = jnp.where(on_item, item_local, member_local)
    high = local >> 8
    ids = jnp.concatenate([high, local - (high << 8), jnp.zeros((IDS - 2, rows), jnp.int32)], axis=0)
    ids = ids.astype(F32).astype(BF16)
    ids_out[...] = ids
    moves[4].wait()
    for chunk, k in zip(chunks, far):
        pack_chunk(k, capacity, place, ids, copies[4][...], chunk)


def near_kernel(capacity, near, place, ids, feats, *chunks):
    for chunk, k in zip(chunks, near):
        pack_chunk(k, capacity, place[...], ids[...], feats[...], chunk)


def chunk_ids(chunk, capacity):
    pair = chunk[capacity:, :capacity].astype(F32)
    return (pair[0:1] * 256.0 + pair[1:2]).astype(jnp.int32)


def scores_kernel(owners, capacity, where, margin, coefs, *refs):
    chunks, out = refs[:owners], refs[owners]
    entities = coefs.shape[0]
    mine = where[0]
    high, low = halves(coefs[...])
    scores = []
    for k in range(owners):
        feats = chunks[k][:capacity]
        every = lanes_dot(high, feats) + lanes_dot(low, feats)
        hits = one_hot(chunk_ids(chunks[k], capacity), entities)
        scores.append(jnp.sum(jnp.where(hits, every, 0.0), axis=0, keepdims=True))
    for k in range(owners):
        out[0, pl.ds(mine ^ k, 1), :] = scores[k]


def home_kernel(
    owners, capacity, n_feat, n_ent, where, member, item, ranks, clicks, valid, margin, scores, features, out
):
    mine, on_item = where[0], where[1] > 0
    total = margin[...]
    hits_of = [one_hot(owner[...], owners).astype(F32) for owner in (member, item)]
    spot_of = [one_hot(ranks[side : side + 1], capacity).astype(F32).astype(BF16) for side in (0, 1)]
    for side in (0, 1):
        table = None
        for f in range(side * n_feat // 2, (side + 1) * n_feat // 2):
            part = jnp.concatenate(
                [scores[(h // n_ent * n_feat + f) * n_ent + h % n_ent, pl.ds(mine, 1), :] for h in range(owners)],
                axis=0,
            )
            table = part if table is None else table + part
        found = plain_dot(jnp.concatenate(halves(table), axis=0), spot_of[side])
        total = total + jnp.sum((found[:owners] + found[owners:]) * hits_of[side], axis=0, keepdims=True)
    resid = valid[...].astype(F32) * (jax.nn.sigmoid(total) - clicks[...].astype(F32))
    hits = jnp.where(on_item, hits_of[1], hits_of[0])
    spot = jnp.where(on_item, spot_of[1], spot_of[0])
    sent = lanes_dot(jnp.concatenate(halves(hits * resid), axis=0), spot)
    out[0, :owners] = sent[:owners] + sent[owners:]
    low = jnp.broadcast_to(resid, (16, resid.shape[1])).astype(BF16)
    grad = plain_dot(low, features[...])[0:1]
    for j in range(grad.shape[1] // capacity):
        out[0, owners + j : owners + j + 1] = grad[:, j * capacity : (j + 1) * capacity]


def grads_kernel(owners, capacity, scale, where, coefs, weight, came, *refs):
    chunks, grad_global, grad_coefs = refs[:owners], refs[owners], refs[owners + 1]
    entities = coefs.shape[0]
    mine = where[0]
    resids = [came[mine ^ k, pl.ds(mine, 1), :] for k in range(owners)]
    summed = came[0, owners:]
    for h in range(1, owners):
        summed = summed + came[h, owners:]
    summed = summed * scale
    for j in range(summed.shape[0]):
        here = slice(j * capacity, (j + 1) * capacity)
        grad_global[:, here] = summed[j : j + 1] + 4.0 * weight[:, here]
    total = coefs[...]
    for k in range(owners):
        hits = one_hot(chunk_ids(chunks[k], capacity), entities)
        feats = chunks[k][:capacity]
        for part in halves(resids[k]):
            total = total + plain_dot(jnp.where(hits, part.astype(F32), 0.0).astype(BF16), feats)
    grad_coefs[...] = total


def xor_send(x, axes, size, k):
    return x if k == 0 else lax.ppermute(x, axes, [(i, i ^ k) for i in range(size)])


def call(kernel, out_shape, operands, in_specs, flops=0, scratch=()):
    moved = sum(x.size * x.dtype.itemsize for x in (*operands, *out_shape))
    return pl.pallas_call(
        kernel,
        out_shape=out_shape,
        in_specs=in_specs,
        out_specs=[VMEM] * len(out_shape),
        scratch_shapes=scratch,
        compiler_params=PARAMS,
        cost_estimate=pl.CostEstimate(flops=flops, bytes_accessed=moved, transcendentals=0),
    )(*operands)


def body(
    features,
    global_weight,
    entity_feats,
    coefs,
    member_owner,
    member_local,
    item_owner,
    item_local,
    clicks,
    valid,
):
    rows_here, width = entity_feats.shape
    columns = features.shape[1]
    n_feat, n_ent = lax.axis_size("feat"), lax.axis_size("ent")
    owners = lax.axis_size("rows") * n_ent
    capacity = 2 * rows_here // owners
    mine = lax.axis_index(HOME).astype(jnp.int32)
    on_item = (lax.axis_index("feat") >= n_feat // 2).astype(jnp.int32)
    where = jnp.stack([mine, on_item])
    member, item = member_owner.reshape(1, rows_here), item_owner.reshape(1, rows_here)

    def shape(*dims, dtype=F32):
        return jax.ShapeDtypeStruct(dims, dtype)

    def partial(kernel, *args):
        return lambda *refs: kernel(*args, *refs)

    row = pltpu.VMEM((1, rows_here), jnp.int32)
    far, near = list(reversed(range(owners // 2, owners))), list(reversed(range(owners // 2)))
    chunk = shape(capacity + IDS, width, dtype=BF16)
    flops = owners * capacity * rows_here * width
    chunks = [None] * owners
    ranks, place, ids, *packed = call(
        partial(far_kernel, owners, capacity, far),
        [shape(2, rows_here, dtype=jnp.int32), shape(1, rows_here, dtype=jnp.int32), shape(IDS, rows_here, dtype=BF16)]
        + [chunk] * len(far),
        (
            where,
            *(
                pltpu.with_memory_space_constraint(x, pltpu.HBM)
                for x in (
                    member,
                    item,
                    member_local.reshape(1, rows_here),
                    item_local.reshape(1, rows_here),
                    entity_feats,
                )
            ),
        ),
        [SMEM] + [HBM] * 5,
        flops=flops,
        scratch=[row, row, row, row, pltpu.VMEM((rows_here, width), BF16), pltpu.SemaphoreType.DMA((5,))],
    )
    for k, x in zip(far, packed):
        chunks[k] = xor_send(x, HOME, owners, k)
    packed = call(
        partial(near_kernel, capacity, near), [chunk] * len(near), (place, ids, entity_feats), [VMEM] * 3, flops=flops
    )
    for k, x in zip(near, packed):
        chunks[k] = xor_send(x, HOME, owners, k)

    global_part = jnp.dot(features, global_weight, preferred_element_type=F32)
    global_total = global_part
    for q in range(1, n_feat):
        global_total = global_total + xor_send(global_part, "feat", n_feat, q)
    global_total = global_total.reshape(1, rows_here)

    (scores,) = call(
        partial(scores_kernel, owners, capacity),
        [shape(1, owners, capacity)],
        (where, global_total, coefs, *chunks),
        [SMEM] + [VMEM] * (2 + owners),
        flops=4 * coefs.size * owners * capacity,
    )
    returned = lax.all_gather(scores, EVERY, axis=0, tiled=True)
    (sent,) = call(
        partial(home_kernel, owners, capacity, n_feat, n_ent),
        [shape(1, owners + columns // capacity, capacity)],
        (
            where,
            member,
            item,
            ranks,
            clicks.reshape(1, rows_here),
            valid.reshape(1, rows_here),
            global_total,
            returned,
            features,
        ),
        [SMEM] + [VMEM] * 8,
        flops=32 * features.size,
    )
    came = lax.all_gather(sent, HOME, axis=0, tiled=True)
    grad_global, grad_coefs = call(
        partial(grads_kernel, owners, capacity, 1.0 / math.sqrt(rows_here * owners)),
        [shape(1, columns), shape(*coefs.shape)],
        (where, coefs, global_weight.astype(F32).reshape(1, columns), came, *chunks),
        [SMEM] + [VMEM] * (3 + owners),
        flops=4 * coefs.size * owners * capacity,
    )
    return (grad_global.reshape(columns), grad_coefs)


def solution(mesh):
    by_row = P(("groups", "rows", "ent"))
    by_both = P(("groups", "rows", "ent"), "feat")
    column = P(("groups", "rows", "ent"), None)
    by_feat = P(("groups", "feat"))
    return jax.shard_map(
        body,
        mesh=mesh,
        in_specs=(by_both, by_feat, by_both, by_both, column, by_row, column, by_row, by_row, by_row),
        out_specs=(by_feat, by_both),
        check_vma=False,
    )
```

time: 73.1 us -> 74.5 us (1.019)
  blocking collectives: 0 us -> 36.6 us
  starting transfers between devices: 27.3 us -> 10.8 us
  waiting for transfers between devices: 22.3 us -> 11.5 us
  local copies, waits for them, and re-layouts: 7.73 us -> 0.73 us
    all_gather x0 -> x2, blocking collectives: none -> 36.6 us  [the longest x1 22.6 us: body(): returned = lax.all_gather(scores, EVERY, axis=0, tiled=True)]
    all_to_all x2 -> x0, starting transfers between devices: 15.8 us -> none  [the longest x1 10.7 us: body(): lax.all_to_all(scores, EVERY, split_axis=0, concat_axis=0, tiled=True)]
    unnamed x27 -> x17, local copies, waits for them, and re-layouts: 7.73 us -> 0.73 us
    all_to_all x2 -> x0, waiting for transfers between devices: 6 us -> none  [the longest x1 6 us: body(): came = lax.all_to_all(sent, HOME, split_axis=0, concat_axis=0, tiled=True)]
    ppermute x8, waiting for transfers between devices: 16.3 us -> 11.5 us  [xor_send(): lax.ppermute(x, axes, [(i, i ^ k) for i in range(size)])]
    pallas_call x4 -> x5, Pallas kernels: 11 us -> 10.3 us  [call(): pl.pallas_call(kernel, out_shape=out_shape, in_specs=in_specs, out_specs=...]
  transfers between devices with their start and end apart: 10 -> 8, of which waited for: 5 -> 4; matrix products, arithmetic and copies ran while one was open for 6% -> 5% of each run, Pallas kernels for 0% -> 2%
where the time goes in v3:
time: 74.5 us; the launch traced here: 74.2 us
  blocking collectives  36.6 us (49%)
  waiting for transfers between devices  11.5 us (15%)
  starting transfers between devices  10.8 us (14%)
  Pallas kernels  10.3 us (14%)
  matrix products  3.37 us (5%)
  between operations  0.75 us (1%)
    all_gather x1, blocking collectives, body(): returned = lax.all_gather(scores, EVERY, axis=0, tiled=True)  22.6 us
    all_gather x1, blocking collectives, body(): came = lax.all_gather(sent, HOME, axis=0, tiled=True)  14 us
    ppermute x8, waiting for transfers between devices, xor_send(): lax.ppermute(x, axes, [(i, i ^ k) for i in range(size)])  11.5 us
    ppermute x8, starting transfers between devices, xor_send(): lax.ppermute(x, axes, [(i, i ^ k) for i in range(size)])  10.8 us
    pallas_call x5, Pallas kernels, call(): pl.pallas_call(kernel, out_shape=out_shape, in_specs=in_specs, out_specs=...  10.3 us
    dot_general x1, matrix products, body(): global_part = jnp.dot(features, global_weight, preferred_element_type=F32)  3.37 us
  transfers between devices with their start and end apart: 8, of which 4 were waited for; matrix products, arithmetic and copies ran while one was open for 5% of the time, Pallas kernels for 2%

profile of v3, /device:TPU:0, one launch (start us, length us, event | category | flops | bytes accessed | tf_op | source)
XLA Modules:
  0.0 74.2 jit_solution(9343242881063313880)
XLA Ops:
  0.6 0.0 copy-start.5
  0.6 0.1 pad_add_fusion.refs_0_
  0.7 0.0 copy-start.7
  0.7 0.0 copy-start.6
  0.7 2.9 %shard_map.113 = (s32[2,1024]{1,0:T(2,128)S(1)}, s32[1,1024]{1,0:T(1,128)S(1)}, bf16[16,1024]{1,0:T(8,128)(2,1)S(1)}, bf16[272,256]{1,0:T(8,128)(2,1)S(1)}, bf16...) custom-call(s32[2]{0:T(128)S(1)} %pad_add_fusion.refs_0_, ...), custom_call_target="tpu_custom_call" | custom-call | flops 536870912 | bytes 1142792 | tf_op jit(solution)/shard_map/pallas_call | solution.py:171
  3.7 4.1 %collective-permute-start.4 = (bf16[272,256]{1,0:T(8,128)(2,1)S(1)}, bf16[272,256]{1,0:T(8,128)(2,1)S(1)}, u32[]{:S(2)}, u32[]{:S(2)}) collective-permute-start(bf16[272,256]{1,0:T(8,128)(2,1)S(1)} %get-tuple-element.22), channel_id=1, source_target_pairs={{0,8},{1,9},{4,12},{5,13},{8,0},{9,1},{12,4},{13,5},{2,10},{3,11},... | collective-permute-start | bytes 417800 | tf_op jit(solution)/shard_map/ppermute | solution.py:166
  7.8 0.0 collective-permute-start.5
  7.8 0.7 reshape.46
  8.5 3.4 %fusion = f32[1,1024]{1,0:T(1,128)S(1)} fusion(bf16[1024,2048]{1,0:T(8,128)(2,1)} %refs_8_.1, bf16[2048,1]{0,1:T(2,128)(2,1)S(1)} %reshape.46), kind=kOutput, calls=%fused_computation.1 | convolution fusion | flops 4194304 | bytes 4202496 | tf_op jit(solution)/shard_map/dot_general | solution.py:244
  11.8 0.0 copy-start
  11.8 0.0 copy-start.1
  11.8 0.0 copy-start.2
  11.8 0.0 copy-start.3
  11.9 0.0 copy-start.4
  11.9 1.6 %collective-permute-start = (f32[1024]{0:T(1024)S(1)}, f32[1024]{0:T(1024)S(1)}, u32[]{:S(2)}, u32[]{:S(2)}) collective-permute-start(f32[1024]{0:T(1024)S(1)} %bitcast.23), channel_id=1, source_target_pairs={{0,2},{2,0},{1,3},{3,1},{4,6},{6,4},{5,7},{7,5},{8,10},{10,8},{9,1... | collective-permute-start | bytes 12296 | tf_op jit(solution)/shard_map/ppermute | solution.py:166
  13.4 3.1 %collective-permute-start.6 = (bf16[272,256]{1,0:T(8,128)(2,1)S(1)}, bf16[272,256]{1,0:T(8,128)(2,1)S(1)}, u32[]{:S(2)}, u32[]{:S(2)}) collective-permute-start(bf16[272,256]{1,0:T(8,128)(2,1)S(1)} %get-tuple-element.24), channel_id=1, source_target_pairs={{0,12},{1,13},{4,8},{5,9},{8,4},{9,5},{12,0},{13,1},{2,14},{3,15},... | collective-permute-start | bytes 417800 | tf_op jit(solution)/shard_map/ppermute | solution.py:166
  16.5 0.3 collective-permute-start.7
  16.8 0.0 copy-done.5
  16.8 1.2 %shard_map.114 = (bf16[272,256]{1,0:T(8,128)(2,1)S(1)}, bf16[272,256]{1,0:T(8,128)(2,1)S(1)}, bf16[272,256]{1,0:T(8,128)(2,1)S(1)}, bf16[272,256]{1,0:T(8,128)(2,1)S(1)}) custom-call(s32[1,1024]{1,0:T(1,128)S(1)} %get-tuple-element.16.refs_0_, bf16[16,1024]{1,0:T(8,128)(2,1)S(1)} %get-tuple-element.17.refs_1_, bf16[1024,256]{1,0:T(8,128)(2,1)S(1)} %copy-done.5), custom_call_target="tpu_custom_call" | custom-call | flops 536870912 | bytes 1118208 | tf_op jit(solution)/shard_map/pallas_call | solution.py:171
  18.1 0.0 collective-permute-done
  18.1 0.6 collective-permute-start.1
  18.7 2.5 %collective-permute-done.4.refs_7_.refs_8_ = bf16[272,256]{1,0:T(8,128)(2,1)S(1)} collective-permute-done((bf16[272,256]{1,0:T(8,128)(2,1)S(1)}, bf16[272,256]{1,0:T(8,128)(2,1)S(1)}, u32[]{:S(2)}, u32[]{:S(2)}) %collective-permute-start.4) | collective-permute-done | bytes 139296 | tf_op jit(solution)/shard_map/ppermute | solution.py:166
  21.2 0.0 collective-permute-start.2
  21.2 4.4 %collective-permute-done.5.refs_8_.refs_9_ = bf16[272,256]{1,0:T(8,128)(2,1)S(1)} collective-permute-done((bf16[272,256]{1,0:T(8,128)(2,1)S(1)}, bf16[272,256]{1,0:T(8,128)(2,1)S(1)}, u32[]{:S(2)}, u32[]{:S(2)}) %collective-permute-start.5) | collective-permute-done | bytes 139296 | tf_op jit(solution)/shard_map/ppermute | solution.py:166
  25.6 1.1 %collective-permute-start.3 = (bf16[272,256]{1,0:T(8,128)(2,1)S(1)}, bf16[272,256]{1,0:T(8,128)(2,1)S(1)}, u32[]{:S(2)}, u32[]{:S(2)}) collective-permute-start(bf16[272,256]{1,0:T(8,128)(2,1)S(1)} %get-tuple-element.21), channel_id=1, source_target_pairs={{0,5},{1,4},{4,1},{5,0},{8,13},{9,12},{12,9},{13,8},{2,7},{3,6},{6... | collective-permute-start | bytes 417800 | tf_op jit(solution)/shard_map/ppermute | solution.py:166
  26.7 0.0 copy-done.7
  26.8 0.0 collective-permute-done.6.refs_9_.refs_10_
  26.8 0.0 collective-permute-done.7.refs_10_.refs_11_
  26.8 0.0 collective-permute-done.1.refs_4_.refs_5_
  26.8 2.6 %collective-permute-done.2.refs_5_.refs_6_ = bf16[272,256]{1,0:T(8,128)(2,1)S(1)} collective-permute-done((bf16[272,256]{1,0:T(8,128)(2,1)S(1)}, bf16[272,256]{1,0:T(8,128)(2,1)S(1)}, u32[]{:S(2)}, u32[]{:S(2)}) %collective-permute-start.2) | collective-permute-done | bytes 139296 | tf_op jit(solution)/shard_map/ppermute | solution.py:166
  29.4 1.9 %collective-permute-done.3.refs_6_.refs_7_ = bf16[272,256]{1,0:T(8,128)(2,1)S(1)} collective-permute-done((bf16[272,256]{1,0:T(8,128)(2,1)S(1)}, bf16[272,256]{1,0:T(8,128)(2,1)S(1)}, u32[]{:S(2)}, u32[]{:S(2)}) %collective-permute-start.3) | collective-permute-done | bytes 139296 | tf_op jit(solution)/shard_map/ppermute | solution.py:166
  31.4 0.0 copy-done.6
  31.4 1.9 %shard_map.115 = f32[1,8,256]{2,1,0:T(8,128)S(1)} custom-call(s32[2]{0:T(128)S(1)} %pad_add_fusion.refs_0_, f32[1,1024]{1,0:T(1,128)S(1)} %bitcast.14, f32[512,256]{1,0:T(8,128)S(1)} %copy-done.6, bf16[272,256]{1,0:T(8,128)(2,1)S(1)} %get-tuple-element.18.refs_3_.refs_4_, bf16[272,256]{1,0:T(8,128)(2,1)S(1)} %collective-permute-done.1.refs_4_.refs_5_, ...), custom_call_target="tpu_custom_call" | custom-call | flops 1073741824 | bytes 1650696 | tf_op jit(solution)/shard_map/pallas_call | solution.py:171
  33.3 22.6 %all_gather.6.refs_7_ = f32[16,8,256]{2,1,0:T(8,128)S(1)} all-gather(f32[1,8,256]{2,1,0:T(8,128)S(1)} %shard_map.115), channel_id=1, replica_groups=mesh['groups'=2,'rows'=4,'feat'=2,'ent'=2] {'rows','feat','ent'}, dimensions={0}, use_global_device_ids=true | all-gather | bytes 139264 | tf_op jit(solution)/shard_map/all_gather | solution.py:257
  55.9 0.0 copy-done
  55.9 0.0 copy-done.1
  55.9 0.0 copy-done.2
  55.9 0.0 copy-done.3
  55.9 0.0 copy-done.4
  55.9 1.7 %shard_map.116 = f32[1,16,256]{2,1,0:T(8,128)S(1)} custom-call(s32[2]{0:T(128)S(1)} %pad_add_fusion.refs_0_, s32[1,1024]{1,0:T(1,128)S(1)} %bitcast.18, s32[1,1024]{1,0:T(1,128)S(1)} %bitcast.20, s32[2,1024]{1,0:T(2,128)S(1)} %get-tuple-element.15.refs_3_, s32[1,1024]{1,0:T(1,128)S(1)} %bitcast.21, s32[1,1024]{1,0:T(1,128)S(1)} %bitcast.22, ...), custom_call_target="tpu_custom_call" | custom-call | flops 67108864 | bytes 4370440 | tf_op jit(solution)/shard_map/pallas_call | solution.py:171
  57.6 14.0 %all_gather.7.refs_3_ = f32[8,16,256]{2,1,0:T(8,128)S(1)} all-gather(f32[1,16,256]{2,1,0:T(8,128)S(1)} %shard_map.116), channel_id=1, replica_groups=mesh['groups'=2,'rows'=4,'feat'=2,'ent'=2] {'rows','ent'}, dimensions={0}, use_global_device_ids=true | all-gather | bytes 147456 | tf_op jit(solution)/shard_map/all_gather | solution.py:275
  71.6 2.6 %shard_map.117 = (f32[1,2048]{1,0:T(1,128)}, f32[512,256]{1,0:T(8,128)}) custom-call(s32[2]{0:T(128)S(1)} %pad_add_fusion.refs_0_, f32[512,256]{1,0:T(8,128)S(1)} %copy-done.6, f32[1,2048]{1,0:T(1,128)S(1)} %bitcast.16, f32[8,16,256]{2,1,0:T(8,128)S(1)} %all_gather.7.refs_3_, bf16[272,256]{1,0:T(8,128)(2,1)S(1)} %get-tuple-element.18.refs_3_.refs_4_, ...), custom_call_target="tpu_custom_call" | custom-call | flops 1073741824 | bytes 2310152 | tf_op jit(solution)/shard_map/pallas_call | solution.py:171
  (2 shorter events, 0.0 us)
Async XLA Ops:
  0.6 16.2 %copy-start.5 = (bf16[1024,256]{1,0:T(8,128)(2,1)S(1)}, bf16[1024,256]{1,0:T(8,128)(2,1)}, u32[]{:S(2)}) copy-start(bf16[1024,256]{1,0:T(8,128)(2,1)} %refs_2_.2) | copy-start | bytes 1572868
  0.7 26.0 %copy-start.7 = (bf16[2048]{0:T(1024)(128)(2,1)S(1)}, bf16[2048]{0:T(1024)(128)(2,1)}, u32[]{:S(2)}) copy-start(bf16[2048]{0:T(1024)(128)(2,1)} %param.11) | copy-start | bytes 12292
  0.7 30.7 %copy-start.6 = (f32[512,256]{1,0:T(8,128)S(1)}, f32[512,256]{1,0:T(8,128)}, u32[]{:S(2)}) copy-start(f32[512,256]{1,0:T(8,128)} %refs_1_.1) | copy-start | bytes 1572868
  3.7 17.6 %collective-permute-start.4 = (bf16[272,256]{1,0:T(8,128)(2,1)S(1)}, bf16[272,256]{1,0:T(8,128)(2,1)S(1)}, u32[]{:S(2)}, u32[]{:S(2)}) collective-permute-start(bf16[272,256]{1,0:T(8,128)(2,1)S(1)} %get-tuple-element.22), channel_id=1, source_target_pairs={{0,8},{1,9},{4,12},{5,13},{8,0},{9,1},{12,4},{13,5},{2,10},{3,11},... | collective-permute-start | bytes 417800 | tf_op jit(solution)/shard_map/ppermute | solution.py:166
  7.8 17.9 %collective-permute-start.5 = (bf16[272,256]{1,0:T(8,128)(2,1)S(1)}, bf16[272,256]{1,0:T(8,128)(2,1)S(1)}, u32[]{:S(2)}, u32[]{:S(2)}) collective-permute-start(bf16[272,256]{1,0:T(8,128)(2,1)S(1)} %get-tuple-element.23), channel_id=1, source_target_pairs={{0,9},{1,8},{4,13},{5,12},{8,1},{9,0},{12,5},{13,4},{2,11},{3,10},... | collective-permute-start | bytes 417800 | tf_op jit(solution)/shard_map/ppermute | solution.py:166
  11.8 44.1 %copy-start = (bf16[1024,2048]{1,0:T(8,128)(2,1)S(1)}, bf16[1024,2048]{1,0:T(8,128)(2,1)}, u32[]{:S(2)}) copy-start(bf16[1024,2048]{1,0:T(8,128)(2,1)} %refs_8_.1) | copy-start | bytes 12582916
  11.8 44.1 %copy-start.1 = (s32[1024,1]{0,1:T(1,128)S(1)}, s32[1024,1]{0,1:T(1,128)}, u32[]{:S(2)}) copy-start(s32[1024,1]{0,1:T(1,128)} %param.14) | copy-start | bytes 12292
  11.8 44.1 %copy-start.2 = (s32[1024,1]{0,1:T(1,128)S(1)}, s32[1024,1]{0,1:T(1,128)}, u32[]{:S(2)}) copy-start(s32[1024,1]{0,1:T(1,128)} %param.16) | copy-start | bytes 12292
  11.8 44.1 %copy-start.3 = (s32[1024]{0:T(1024)S(1)}, s32[1024]{0:T(1024)}, u32[]{:S(2)}) copy-start(s32[1024]{0:T(1024)} %param.18) | copy-start | bytes 12292
  11.9 44.1 %copy-start.4 = (s32[1024]{0:T(1024)S(1)}, s32[1024]{0:T(1024)}, u32[]{:S(2)}) copy-start(s32[1024]{0:T(1024)} %param.19) | copy-start | bytes 12292
  11.9 6.2 %collective-permute-start = (f32[1024]{0:T(1024)S(1)}, f32[1024]{0:T(1024)S(1)}, u32[]{:S(2)}, u32[]{:S(2)}) collective-permute-start(f32[1024]{0:T(1024)S(1)} %bitcast.23), channel_id=1, source_target_pairs={{0,2},{2,0},{1,3},{3,1},{4,6},{6,4},{5,7},{7,5},{8,10},{10,8},{9,1... | collective-permute-start | bytes 12296 | tf_op jit(solution)/shard_map/ppermute | solution.py:166
  13.4 13.3 %collective-permute-start.6 = (bf16[272,256]{1,0:T(8,128)(2,1)S(1)}, bf16[272,256]{1,0:T(8,128)(2,1)S(1)}, u32[]{:S(2)}, u32[]{:S(2)}) collective-permute-start(bf16[272,256]{1,0:T(8,128)(2,1)S(1)} %get-tuple-element.24), channel_id=1, source_target_pairs={{0,12},{1,13},{4,8},{5,9},{8,4},{9,5},{12,0},{13,1},{2,14},{3,15},... | collective-permute-start | bytes 417800 | tf_op jit(solution)/shard_map/ppermute | solution.py:166
  16.5 10.2 %collective-permute-start.7 = (bf16[272,256]{1,0:T(8,128)(2,1)S(1)}, bf16[272,256]{1,0:T(8,128)(2,1)S(1)}, u32[]{:S(2)}, u32[]{:S(2)}) collective-permute-start(bf16[272,256]{1,0:T(8,128)(2,1)S(1)} %get-tuple-element.25), channel_id=1, source_target_pairs={{0,13},{1,12},{4,9},{5,8},{8,5},{9,4},{12,1},{13,0},{2,15},{3,14},... | collective-permute-start | bytes 417800 | tf_op jit(solution)/shard_map/ppermute | solution.py:166
  18.1 8.7 %collective-permute-start.1 = (bf16[272,256]{1,0:T(8,128)(2,1)S(1)}, bf16[272,256]{1,0:T(8,128)(2,1)S(1)}, u32[]{:S(2)}, u32[]{:S(2)}) collective-permute-start(bf16[272,256]{1,0:T(8,128)(2,1)S(1)} %get-tuple-element.19), channel_id=1, source_target_pairs={{0,1},{1,0},{4,5},{5,4},{8,9},{9,8},{12,13},{13,12},{2,3},{3,2},{6... | collective-permute-start | bytes 417800 | tf_op jit(solution)/shard_map/ppermute | solution.py:166
  21.2 8.2 %collective-permute-start.2 = (bf16[272,256]{1,0:T(8,128)(2,1)S(1)}, bf16[272,256]{1,0:T(8,128)(2,1)S(1)}, u32[]{:S(2)}, u32[]{:S(2)}) collective-permute-start(bf16[272,256]{1,0:T(8,128)(2,1)S(1)} %get-tuple-element.20), channel_id=1, source_target_pairs={{0,4},{1,5},{4,0},{5,1},{8,12},{9,13},{12,8},{13,9},{2,6},{3,7},{6... | collective-permute-start | bytes 417800 | tf_op jit(solution)/shard_map/ppermute | solution.py:166
  25.6 5.8 %collective-permute-start.3 = (bf16[272,256]{1,0:T(8,128)(2,1)S(1)}, bf16[272,256]{1,0:T(8,128)(2,1)S(1)}, u32[]{:S(2)}, u32[]{:S(2)}) collective-permute-start(bf16[272,256]{1,0:T(8,128)(2,1)S(1)} %get-tuple-element.21), channel_id=1, source_target_pairs={{0,5},{1,4},{4,1},{5,0},{8,13},{9,12},{12,9},{13,8},{2,7},{3,6},{6... | collective-permute-start | bytes 417800 | tf_op jit(solution)/shard_map/ppermute | solution.py:166

commit v4 on v3

--- a/solution.py
+++ b/solution.py
@@ -62,9 +62,9 @@
     chunk[capacity:, :capacity] = lanes_dot(ids, pick).astype(BF16)
 
 
-def far_kernel(owners, capacity, far, where, *refs):
-    sources, ranks, place_out, ids_out = refs[:5], refs[5], refs[6], refs[7]
-    chunks, copies, sems = refs[8 : 8 + len(far)], refs[8 + len(far) : 13 + len(far)], refs[13 + len(far)]
+def dispatch_kernel(owners, capacity, order, where, *refs):
+    sources, ranks = refs[:5], refs[5]
+    chunks, copies, sems = refs[6 : 6 + owners], refs[6 + owners : 11 + owners], refs[11 + owners]
     moves = [pltpu.make_async_copy(sources[i], copies[i], sems.at[i]) for i in range(5)]
     for move in moves:
         move.start()
@@ -77,20 +77,18 @@
     ranks[...] = rank
     own = jnp.where(on_item, item, member)
     place = (own ^ mine) * capacity + jnp.where(on_item, rank[1:2], rank[0:1])
-    place_out[...] = place
     local = jnp.where(on_item, item_local, member_local)
     high = local >> 8
     ids = jnp.concatenate([high, local - (high << 8), jnp.zeros((IDS - 2, rows), jnp.int32)], axis=0)
     ids = ids.astype(F32).astype(BF16)
-    ids_out[...] = ids
     moves[4].wait()
-    for chunk, k in zip(chunks, far):
+    for chunk, k in zip(chunks, order):
         pack_chunk(k, capacity, place, ids, copies[4][...], chunk)
 
 
-def near_kernel(capacity, near, place, ids, feats, *chunks):
-    for chunk, k in zip(chunks, near):
-        pack_chunk(k, capacity, place[...], ids[...], feats[...], chunk)
+def margin_kernel(first, weight, features, margin):
+    wide = jnp.broadcast_to(weight[...], (16, weight.shape[1])).astype(BF16)
+    margin[...] = lanes_dot(wide, features[...])[0:1]
 
 
 def chunk_ids(chunk, capacity):
@@ -98,25 +96,27 @@
     return (pair[0:1] * 256.0 + pair[1:2]).astype(jnp.int32)
 
 
-def scores_kernel(owners, capacity, where, margin, coefs, *refs):
-    chunks, out = refs[:owners], refs[owners]
+def scores_kernel(order, capacity, n_feat, n_ent, where, margin, coefs, *refs):
+    chunks, out = refs[:-1], refs[-1]
     entities = coefs.shape[0]
     mine = where[0]
     high, low = halves(coefs[...])
     scores = []
-    for k in range(owners):
-        feats = chunks[k][:capacity]
+    for chunk in chunks:
+        feats = chunk[:capacity]
         every = lanes_dot(high, feats) + lanes_dot(low, feats)
-        hits = one_hot(chunk_ids(chunks[k], capacity), entities)
+        hits = one_hot(chunk_ids(chunk, capacity), entities)
         scores.append(jnp.sum(jnp.where(hits, every, 0.0), axis=0, keepdims=True))
-    for k in range(owners):
-        out[0, pl.ds(mine ^ k, 1), :] = scores[k]
+    for k, score in zip(order, scores):
+        home = mine ^ k
+        for f in range(n_feat):
+            out[(home // n_ent * n_feat + f) * n_ent + home % n_ent] = score
 
 
 def home_kernel(
     owners, capacity, n_feat, n_ent, where, member, item, ranks, clicks, valid, margin, scores, features, out
 ):
-    mine, on_item = where[0], where[1] > 0
+    on_item = where[1] > 0
     total = margin[...]
     hits_of = [one_hot(owner[...], owners).astype(F32) for owner in (member, item)]
     spot_of = [one_hot(ranks[side : side + 1], capacity).astype(F32).astype(BF16) for side in (0, 1)]
@@ -124,8 +124,7 @@
         table = None
         for f in range(side * n_feat // 2, (side + 1) * n_feat // 2):
             part = jnp.concatenate(
-                [scores[(h // n_ent * n_feat + f) * n_ent + h % n_ent, pl.ds(mine, 1), :] for h in range(owners)],
-                axis=0,
+                [scores[(h // n_ent * n_feat + f) * n_ent + h % n_ent] for h in range(owners)], axis=0
             )
             table = part if table is None else table + part
         found = plain_dot(jnp.concatenate(halves(table), axis=0), spot_of[side])
@@ -134,30 +133,28 @@
     hits = jnp.where(on_item, hits_of[1], hits_of[0])
     spot = jnp.where(on_item, spot_of[1], spot_of[0])
     sent = lanes_dot(jnp.concatenate(halves(hits * resid), axis=0), spot)
-    out[0, :owners] = sent[:owners] + sent[owners:]
+    sent = sent[:owners] + sent[owners:]
     low = jnp.broadcast_to(resid, (16, resid.shape[1])).astype(BF16)
     grad = plain_dot(low, features[...])[0:1]
-    for j in range(grad.shape[1] // capacity):
-        out[0, owners + j : owners + j + 1] = grad[:, j * capacity : (j + 1) * capacity]
-
-
-def grads_kernel(owners, capacity, scale, where, coefs, weight, came, *refs):
-    chunks, grad_global, grad_coefs = refs[:owners], refs[owners], refs[owners + 1]
+    for h in range(owners):
+        out[h, :, :capacity] = sent[h : h + 1]
+        out[h, :, capacity:] = grad
+
+
+def grads_kernel(order, capacity, scale, where, coefs, weight, came, *refs):
+    chunks, grad_global, grad_coefs = refs[:-2], refs[-2], refs[-1]
     entities = coefs.shape[0]
     mine = where[0]
-    resids = [came[mine ^ k, pl.ds(mine, 1), :] for k in range(owners)]
-    summed = came[0, owners:]
-    for h in range(1, owners):
-        summed = summed + came[h, owners:]
-    summed = summed * scale
-    for j in range(summed.shape[0]):
-        here = slice(j * capacity, (j + 1) * capacity)
-        grad_global[:, here] = summed[j : j + 1] + 4.0 * weight[:, here]
+    resids = [came[mine ^ k][:, :capacity] for k in order]
+    summed = came[0][:, capacity:]
+    for h in range(1, len(order)):
+        summed = summed + came[h][:, capacity:]
+    grad_global[...] = summed * scale + 4.0 * weight[...]
     total = coefs[...]
-    for k in range(owners):
-        hits = one_hot(chunk_ids(chunks[k], capacity), entities)
-        feats = chunks[k][:capacity]
-        for part in halves(resids[k]):
+    for chunk, resid in zip(chunks, resids):
+        hits = one_hot(chunk_ids(chunk, capacity), entities)
+        feats = chunk[:capacity]
+        for part in halves(resid):
             total = total + plain_dot(jnp.where(hits, part.astype(F32), 0.0).astype(BF16), feats)
     grad_coefs[...] = total
 
@@ -166,8 +163,8 @@
     return x if k == 0 else lax.ppermute(x, axes, [(i, i ^ k) for i in range(size)])
 
 
-def call(kernel, out_shape, operands, in_specs, flops=0, scratch=()):
-    moved = sum(x.size * x.dtype.itemsize for x in (*operands, *out_shape))
+def call(kernel, out_shape, operands, in_specs, flops=0, scratch=(), hidden=False):
+    moved = 0 if hidden else sum(x.size * x.dtype.itemsize for x in (*operands, *out_shape))
     return pl.pallas_call(
         kernel,
         out_shape=out_shape,
@@ -208,14 +205,12 @@
         return lambda *refs: kernel(*args, *refs)
 
     row = pltpu.VMEM((1, rows_here), jnp.int32)
-    far, near = list(reversed(range(owners // 2, owners))), list(reversed(range(owners // 2)))
+    half = owners // 2
+    order = [*range(half, owners), *reversed(range(half))]
     chunk = shape(capacity + IDS, width, dtype=BF16)
-    flops = owners * capacity * rows_here * width
-    chunks = [None] * owners
-    ranks, place, ids, *packed = call(
-        partial(far_kernel, owners, capacity, far),
-        [shape(2, rows_here, dtype=jnp.int32), shape(1, rows_here, dtype=jnp.int32), shape(IDS, rows_here, dtype=BF16)]
-        + [chunk] * len(far),
+    ranks, *chunks = call(
+        partial(dispatch_kernel, owners, capacity, order),
+        [shape(2, rows_here, dtype=jnp.int32)] + [chunk] * owners,
         (
             where,
             *(
@@ -230,34 +225,27 @@
             ),
         ),
         [SMEM] + [HBM] * 5,
-        flops=flops,
+        flops=2 * owners * capacity * rows_here * width,
         scratch=[row, row, row, row, pltpu.VMEM((rows_here, width), BF16), pltpu.SemaphoreType.DMA((5,))],
     )
-    for k, x in zip(far, packed):
-        chunks[k] = xor_send(x, HOME, owners, k)
-    packed = call(
-        partial(near_kernel, capacity, near), [chunk] * len(near), (place, ids, entity_feats), [VMEM] * 3, flops=flops
-    )
-    for k, x in zip(near, packed):
-        chunks[k] = xor_send(x, HOME, owners, k)
-
-    global_part = jnp.dot(features, global_weight, preferred_element_type=F32)
-    global_total = global_part
-    for q in range(1, n_feat):
-        global_total = global_total + xor_send(global_part, "feat", n_feat, q)
-    global_total = global_total.reshape(1, rows_here)
+    chunks = [xor_send(x, HOME, owners, k) for k, x in zip(order, chunks)]
+    weight = global_weight.astype(F32).reshape(1, columns)
+    (global_part,) = call(
+        margin_kernel, [shape(1, rows_here)], (chunks[0], weight, features), [VMEM] * 3, hidden=True
+    )
+    global_total = lax.psum(global_part, "feat")
 
     (scores,) = call(
-        partial(scores_kernel, owners, capacity),
-        [shape(1, owners, capacity)],
+        partial(scores_kernel, order, capacity, n_feat, n_ent),
+        [shape(n_feat * owners, 1, capacity)],
         (where, global_total, coefs, *chunks),
         [SMEM] + [VMEM] * (2 + owners),
         flops=4 * coefs.size * owners * capacity,
     )
-    returned = lax.all_gather(scores, EVERY, axis=0, tiled=True)
+    returned = lax.all_to_all(scores, EVERY, split_axis=0, concat_axis=0, tiled=True)
     (sent,) = call(
         partial(home_kernel, owners, capacity, n_feat, n_ent),
-        [shape(1, owners + columns // capacity, capacity)],
+        [shape(owners, 1, capacity + columns)],
         (
             where,
             member,
@@ -272,11 +260,11 @@
         [SMEM] + [VMEM] * 8,
         flops=32 * features.size,
     )
-    came = lax.all_gather(sent, HOME, axis=0, tiled=True)
+    came = lax.all_to_all(sent, HOME, split_axis=0, concat_axis=0, tiled=True)
     grad_global, grad_coefs = call(
-        partial(grads_kernel, owners, capacity, 1.0 / math.sqrt(rows_here * owners)),
+        partial(grads_kernel, order, capacity, 1.0 / math.sqrt(rows_here * owners)),
         [shape(1, columns), shape(*coefs.shape)],
-        (where, coefs, global_weight.astype(F32).reshape(1, columns), came, *chunks),
+        (where, coefs, weight, came, *chunks),
         [SMEM] + [VMEM] * (3 + owners),
         flops=4 * coefs.size * owners * capacity,
     )

time: 74.5 us -> 65.8 us (0.88)
  blocking collectives: 36.6 us -> 24.9 us
  local copies, waits for them, and re-layouts: 0.73 us -> 4.39 us
  matrix products: 3.37 us -> 0 us
  waiting for transfers between devices: 11.5 us -> 14.1 us
  starting transfers between devices: 10.8 us -> 9.27 us
  Pallas kernels: 10.3 us -> 11.4 us
    all_gather x2 -> x0, blocking collectives: 36.6 us -> none  [the longest x1 22.6 us: body(): returned = lax.all_gather(scores, EVERY, axis=0, tiled=True)]
    all_to_all x0 -> x2, blocking collectives: none -> 19.9 us  [the longest x1 11.5 us: body(): lax.all_to_all(scores, EVERY, split_axis=0, concat_axis=0, tiled=True)]
    psum x0 -> x1, blocking collectives: none -> 4.93 us  [body(): global_total = lax.psum(global_part, 'feat')]
    unnamed x17 -> x14, local copies, waits for them, and re-layouts: 0.73 us -> 4.39 us
    dot_general x1 -> x0, matrix products: 3.37 us -> none  [body(): global_part = jnp.dot(features, global_weight, preferred_element_type=F32)]
    ppermute x8 -> x7, waiting for transfers between devices: 11.5 us -> 14.1 us  [xor_send(): lax.ppermute(x, axes, [(i, i ^ k) for i in range(size)])]
    ppermute x8 -> x7, starting transfers between devices: 10.8 us -> 9.27 us  [xor_send(): lax.ppermute(x, axes, [(i, i ^ k) for i in range(size)])]
    pallas_call x5, Pallas kernels: 10.3 us -> 11.4 us  [call(): pl.pallas_call(kernel, out_shape=out_shape, in_specs=in_specs, out_specs=...]
  transfers between devices with their start and end apart: 8 -> 7, of which waited for: 4 -> 2; matrix products, arithmetic and copies ran while one was open for 5% -> 1% of each run, Pallas kernels for 2% -> 2%
where the time goes in v4:
time: 65.8 us; the launch traced here: 65.5 us
  blocking collectives  24.9 us (38%)
  waiting for transfers between devices  14.1 us (21%)
  Pallas kernels  11.4 us (17%)
  starting transfers between devices  9.27 us (14%)
  local copies, waits for them, and re-layouts  4.39 us (7%)
  other arithmetic  0.76 us (1%)
  between operations  0.72 us (1%)
    ppermute x7, waiting for transfers between devices, xor_send(): lax.ppermute(x, axes, [(i, i ^ k) for i in range(size)])  14.1 us
    all_to_all x1, blocking collectives, body(): lax.all_to_all(scores, EVERY, split_axis=0, concat_axis=0, tiled=True)  11.5 us
    pallas_call x5, Pallas kernels, call(): pl.pallas_call(kernel, out_shape=out_shape, in_specs=in_specs, out_specs=...  11.4 us
    ppermute x7, starting transfers between devices, xor_send(): lax.ppermute(x, axes, [(i, i ^ k) for i in range(size)])  9.27 us
    all_to_all x1, blocking collectives, body(): came = lax.all_to_all(sent, HOME, split_axis=0, concat_axis=0, tiled=True)  8.4 us
    psum x1, blocking collectives, body(): global_total = lax.psum(global_part, 'feat')  4.93 us
    unnamed x14, local copies, waits for them, and re-layouts  4.39 us
  transfers between devices with their start and end apart: 7, of which 2 were waited for; matrix products, arithmetic and copies ran while one was open for 1% of the time, Pallas kernels for 2%

profile of v4, /device:TPU:0, one launch (start us, length us, event | category | flops | bytes accessed | tf_op | source)
XLA Modules:
  0.0 65.5 jit_solution(10442352687940712444)
XLA Ops:
  0.6 0.0 copy-start.6
  0.6 0.1 pad_add_fusion.refs_0_
  0.7 4.0 %shard_map.113 = (s32[2,1024]{1,0:T(2,128)S(1)}, bf16[272,256]{1,0:T(8,128)(2,1)S(1)}, bf16[272,256]{1,0:T(8,128)(2,1)S(1)}, bf16[272,256]{1,0:T(8,128)(2,1)S(1)...) custom-call(s32[2]{0:T(128)S(1)} %pad_add_fusion.refs_0_, ...), custom_call_target="tpu_custom_call" | custom-call | flops 1073741824 | bytes 1662984 | tf_op jit(solution)/shard_map/pallas_call | solution.py:168
  4.7 4.1 %collective-permute-start = (bf16[272,256]{1,0:T(8,128)(2,1)S(1)}, bf16[272,256]{1,0:T(8,128)(2,1)S(1)}, u32[]{:S(2)}, u32[]{:S(2)}) collective-permute-start(bf16[272,256]{1,0:T(8,128)(2,1)S(1)} %get-tuple-element.14), channel_id=1, source_target_pairs={{0,8},{1,9},{4,12},{5,13},{8,0},{9,1},{12,4},{13,5},{2,10},{3,11},... | collective-permute-start | bytes 417800 | tf_op jit(solution)/shard_map/ppermute | solution.py:163
  8.8 0.0 collective-permute-start.1
  8.8 3.1 %collective-permute-start.2 = (bf16[272,256]{1,0:T(8,128)(2,1)S(1)}, bf16[272,256]{1,0:T(8,128)(2,1)S(1)}, u32[]{:S(2)}, u32[]{:S(2)}) collective-permute-start(bf16[272,256]{1,0:T(8,128)(2,1)S(1)} %get-tuple-element.16), channel_id=1, source_target_pairs={{0,12},{1,13},{4,8},{5,9},{8,4},{9,5},{12,0},{13,1},{2,14},{3,15},... | collective-permute-start | bytes 417800 | tf_op jit(solution)/shard_map/ppermute | solution.py:163
  11.9 0.0 copy-start.2
  11.9 0.0 copy-start.3
  11.9 0.0 copy-start.4
  11.9 0.0 copy-start.5
  12.0 0.6 collective-permute-start.3
  12.6 0.0 collective-permute-start.4
  12.6 12.8 %collective-permute-done.first.refs_3_.refs_4_ = bf16[272,256]{1,0:T(8,128)(2,1)S(1)} collective-permute-done((bf16[272,256]{1,0:T(8,128)(2,1)S(1)}, bf16[272,256]{1,0:T(8,128)(2,1)S(1)}, u32[]{:S(2)}, u32[]{:S(2)}) %collective-permute-start) | collective-permute-done | bytes 139296 | tf_op jit(solution)/shard_map/ppermute | solution.py:163
  25.4 0.0 collective-permute-start.5
  25.4 1.3 %collective-permute-done.1.refs_4_.refs_5_ = bf16[272,256]{1,0:T(8,128)(2,1)S(1)} collective-permute-done((bf16[272,256]{1,0:T(8,128)(2,1)S(1)}, bf16[272,256]{1,0:T(8,128)(2,1)S(1)}, u32[]{:S(2)}, u32[]{:S(2)}) %collective-permute-start.1) | collective-permute-done | bytes 139296 | tf_op jit(solution)/shard_map/ppermute | solution.py:163
  26.7 1.4 %collective-permute-start.6 = (bf16[272,256]{1,0:T(8,128)(2,1)S(1)}, bf16[272,256]{1,0:T(8,128)(2,1)S(1)}, u32[]{:S(2)}, u32[]{:S(2)}) collective-permute-start(bf16[272,256]{1,0:T(8,128)(2,1)S(1)} %get-tuple-element.20), channel_id=1, source_target_pairs={{0,1},{1,0},{4,5},{5,4},{8,9},{9,8},{12,13},{13,12},{2,3},{3,2},{6... | collective-permute-start | bytes 417800 | tf_op jit(solution)/shard_map/ppermute | solution.py:163
  28.1 0.7 %reshape.40 = f32[2048]{0:T(1024)S(1)} convert(bf16[2048]{0:T(1024)(128)(2,1)} %param.11) | non-fusion elementwise | flops 2048 | bytes 12288 | tf_op jit(solution)/shard_map/reshape | solution.py:232
  28.8 0.0 copy-start
  28.8 2.2 %copy-done = bf16[1024,2048]{1,0:T(8,128)(2,1)S(1)} copy-done((bf16[1024,2048]{1,0:T(8,128)(2,1)S(1)}, bf16[1024,2048]{1,0:T(8,128)(2,1)}, u32[]{:S(2)}) %copy-start) | copy-done | bytes 4194328
  31.0 1.2 %shard_map.114 = f32[1,1024]{1,0:T(1,128)S(1)} custom-call(bf16[272,256]{1,0:T(8,128)(2,1)S(1)} %collective-permute-done.first.refs_3_.refs_4_, f32[1,2048]{1,0:T(1,128)S(1)} %bitcast.10, bf16[1024,2048]{1,0:T(8,128)(2,1)S(1)} %copy-done), custom_call_target="tpu_custom_call" | custom-call | tf_op jit(solution)/shard_map/pallas_call | solution.py:168
  32.2 4.9 %psum.7.refs_1_.refs_6_ = f32[1,1024]{1,0:T(1,128)S(1)} all-reduce(f32[1,1024]{1,0:T(1,128)S(1)} %shard_map.114), channel_id=1, replica_groups=mesh['groups'=2,'rows'=4,'feat'=2,'ent'=2] {'feat'}, use_global_device_ids=true, to_apply=%region_0.0 | all-reduce | flops 1024 | bytes 8192 | tf_op jit(solution)/shard_map/psum | solution.py:236
  37.1 0.0 collective-permute-done.2.refs_5_.refs_6_
  37.1 0.0 collective-permute-done.3.refs_6_.refs_7_
  37.1 0.0 collective-permute-done.4.refs_7_.refs_8_
  37.1 0.0 collective-permute-done.5.refs_8_.refs_9_
  37.2 0.0 collective-permute-done.6.refs_9_.refs_10_
  37.2 0.0 copy-done.6
  37.2 1.9 %shard_map.115 = f32[16,1,256]{2,1,0:T(1,128)S(1)} custom-call(s32[2]{0:T(128)S(1)} %pad_add_fusion.refs_0_, f32[1,1024]{1,0:T(1,128)S(1)} %psum.7.refs_1_.refs_6_, f32[512,256]{1,0:T(8,128)S(1)} %copy-done.6, bf16[272,256]{1,0:T(8,128)(2,1)S(1)} %collective-permute-done.first.refs_3_.refs_4_, bf16[272,256]{1,0:T(8,128)(2,1)S(1)} %collective-permute-done.1.refs_4_.refs_5_, ...), custom_call_target="tpu_custom_call" | custom-call | flops 1073741824 | bytes 1658888 | tf_op jit(solution)/shard_map/pallas_call | solution.py:168
  39.1 11.5 %all_to_all.10.refs_7_ = f32[16,1,256]{2,1,0:T(1,128)S(1)} all-to-all(f32[16,1,256]{2,1,0:T(1,128)S(1)} %shard_map.115), channel_id=1, replica_groups=mesh['groups'=2,'rows'=4,'feat'=2,'ent'=2] {'rows','feat','ent'}, dimensions={0} | all-to-all | bytes 32768 | tf_op jit(solution)/shard_map/all_to_all | solution.py:245
  50.6 0.0 copy-done.2
  50.6 0.0 copy-done.3
  50.6 0.0 copy-done.4
  50.6 0.0 copy-done.5
  50.6 0.0 copy-start.1
  50.6 2.2 %copy-done.1 = bf16[1024,2048]{1,0:T(8,128)(2,1)S(1)} copy-done((bf16[1024,2048]{1,0:T(8,128)(2,1)S(1)}, bf16[1024,2048]{1,0:T(8,128)(2,1)}, u32[]{:S(2)}) %copy-start.1) | copy-done | bytes 4194328
  52.8 1.7 %shard_map.116 = f32[8,1,2304]{2,1,0:T(1,128)S(1)} custom-call(s32[2]{0:T(128)S(1)} %pad_add_fusion.refs_0_, s32[1,1024]{1,0:T(1,128)S(1)} %bitcast.13, s32[1,1024]{1,0:T(1,128)S(1)} %bitcast.15, s32[2,1024]{1,0:T(2,128)S(1)} %get-tuple-element.13.refs_3_, s32[1,1024]{1,0:T(1,128)S(1)} %bitcast.16, s32[1,1024]{1,0:T(1,128)S(1)} %bitcast.17, ...), custom_call_target="tpu_custom_call" | custom-call | flops 67108864 | bytes 4313096 | tf_op jit(solution)/shard_map/pallas_call | solution.py:168
  54.5 8.4 %all_to_all.11.refs_3_ = f32[8,1,2304]{2,1,0:T(1,128)S(1)} all-to-all(f32[8,1,2304]{2,1,0:T(1,128)S(1)} %shard_map.116), channel_id=1, replica_groups=mesh['groups'=2,'rows'=4,'feat'=2,'ent'=2] {'rows','ent'}, dimensions={0} | all-to-all | bytes 147456 | tf_op jit(solution)/shard_map/all_to_all | solution.py:263
  62.9 2.6 %shard_map.117 = (f32[1,2048]{1,0:T(1,128)}, f32[512,256]{1,0:T(8,128)}) custom-call(s32[2]{0:T(128)S(1)} %pad_add_fusion.refs_0_, f32[512,256]{1,0:T(8,128)S(1)} %copy-done.6, f32[1,2048]{1,0:T(1,128)S(1)} %bitcast.11, f32[8,1,2304]{2,1,0:T(1,128)S(1)} %all_to_all.11.refs_3_, bf16[272,256]{1,0:T(8,128)(2,1)S(1)} %collective-permute-done.first.refs_3_.refs_4_, ...), custom_call_target="tpu_custom_call" | custom-call | flops 1073741824 | bytes 2252808 | tf_op jit(solution)/shard_map/pallas_call | solution.py:168
Async XLA Ops:
  0.6 36.5 %copy-start.6 = (f32[512,256]{1,0:T(8,128)S(1)}, f32[512,256]{1,0:T(8,128)}, u32[]{:S(2)}) copy-start(f32[512,256]{1,0:T(8,128)} %refs_1_.1) | copy-start | bytes 1572868
  4.7 20.6 %collective-permute-start = (bf16[272,256]{1,0:T(8,128)(2,1)S(1)}, bf16[272,256]{1,0:T(8,128)(2,1)S(1)}, u32[]{:S(2)}, u32[]{:S(2)}) collective-permute-start(bf16[272,256]{1,0:T(8,128)(2,1)S(1)} %get-tuple-element.14), channel_id=1, source_target_pairs={{0,8},{1,9},{4,12},{5,13},{8,0},{9,1},{12,4},{13,5},{2,10},{3,11},... | collective-permute-start | bytes 417800 | tf_op jit(solution)/shard_map/ppermute | solution.py:163
  8.8 17.9 %collective-permute-start.1 = (bf16[272,256]{1,0:T(8,128)(2,1)S(1)}, bf16[272,256]{1,0:T(8,128)(2,1)S(1)}, u32[]{:S(2)}, u32[]{:S(2)}) collective-permute-start(bf16[272,256]{1,0:T(8,128)(2,1)S(1)} %get-tuple-element.15), channel_id=1, source_target_pairs={{0,9},{1,8},{4,13},{5,12},{8,1},{9,0},{12,5},{13,4},{2,11},{3,10},... | collective-permute-start | bytes 417800 | tf_op jit(solution)/shard_map/ppermute | solution.py:163
  8.8 28.3 %collective-permute-start.2 = (bf16[272,256]{1,0:T(8,128)(2,1)S(1)}, bf16[272,256]{1,0:T(8,128)(2,1)S(1)}, u32[]{:S(2)}, u32[]{:S(2)}) collective-permute-start(bf16[272,256]{1,0:T(8,128)(2,1)S(1)} %get-tuple-element.16), channel_id=1, source_target_pairs={{0,12},{1,13},{4,8},{5,9},{8,4},{9,5},{12,0},{13,1},{2,14},{3,15},... | collective-permute-start | bytes 417800 | tf_op jit(solution)/shard_map/ppermute | solution.py:163
  11.9 38.7 %copy-start.2 = (s32[1024,1]{0,1:T(1,128)S(1)}, s32[1024,1]{0,1:T(1,128)}, u32[]{:S(2)}) copy-start(s32[1024,1]{0,1:T(1,128)} %param.14) | copy-start | bytes 12292
  11.9 38.7 %copy-start.3 = (s32[1024,1]{0,1:T(1,128)S(1)}, s32[1024,1]{0,1:T(1,128)}, u32[]{:S(2)}) copy-start(s32[1024,1]{0,1:T(1,128)} %param.16) | copy-start | bytes 12292
  11.9 38.7 %copy-start.4 = (s32[1024]{0:T(1024)S(1)}, s32[1024]{0:T(1024)}, u32[]{:S(2)}) copy-start(s32[1024]{0:T(1024)} %param.18) | copy-start | bytes 12292
  11.9 38.7 %copy-start.5 = (s32[1024]{0:T(1024)S(1)}, s32[1024]{0:T(1024)}, u32[]{:S(2)}) copy-start(s32[1024]{0:T(1024)} %param.19) | copy-start | bytes 12292
  12.0 25.2 %collective-permute-start.3 = (bf16[272,256]{1,0:T(8,128)(2,1)S(1)}, bf16[272,256]{1,0:T(8,128)(2,1)S(1)}, u32[]{:S(2)}, u32[]{:S(2)}) collective-permute-start(bf16[272,256]{1,0:T(8,128)(2,1)S(1)} %get-tuple-element.17), channel_id=1, source_target_pairs={{0,13},{1,12},{4,9},{5,8},{8,5},{9,4},{12,1},{13,0},{2,15},{3,14},... | collective-permute-start | bytes 417800 | tf_op jit(solution)/shard_map/ppermute | solution.py:163
  12.6 24.5 %collective-permute-start.4 = (bf16[272,256]{1,0:T(8,128)(2,1)S(1)}, bf16[272,256]{1,0:T(8,128)(2,1)S(1)}, u32[]{:S(2)}, u32[]{:S(2)}) collective-permute-start(bf16[272,256]{1,0:T(8,128)(2,1)S(1)} %get-tuple-element.18), channel_id=1, source_target_pairs={{0,5},{1,4},{4,1},{5,0},{8,13},{9,12},{12,9},{13,8},{2,7},{3,6},{6... | collective-permute-start | bytes 417800 | tf_op jit(solution)/shard_map/ppermute | solution.py:163
  25.4 11.8 %collective-permute-start.5 = (bf16[272,256]{1,0:T(8,128)(2,1)S(1)}, bf16[272,256]{1,0:T(8,128)(2,1)S(1)}, u32[]{:S(2)}, u32[]{:S(2)}) collective-permute-start(bf16[272,256]{1,0:T(8,128)(2,1)S(1)} %get-tuple-element.19), channel_id=1, source_target_pairs={{0,4},{1,5},{4,0},{5,1},{8,12},{9,13},{12,8},{13,9},{2,6},{3,7},{6... | collective-permute-start | bytes 417800 | tf_op jit(solution)/shard_map/ppermute | solution.py:163
  26.7 10.5 %collective-permute-start.6 = (bf16[272,256]{1,0:T(8,128)(2,1)S(1)}, bf16[272,256]{1,0:T(8,128)(2,1)S(1)}, u32[]{:S(2)}, u32[]{:S(2)}) collective-permute-start(bf16[272,256]{1,0:T(8,128)(2,1)S(1)} %get-tuple-element.20), channel_id=1, source_target_pairs={{0,1},{1,0},{4,5},{5,4},{8,9},{9,8},{12,13},{13,12},{2,3},{3,2},{6... | collective-permute-start | bytes 417800 | tf_op jit(solution)/shard_map/ppermute | solution.py:163
  28.8 2.2 %copy-start = (bf16[1024,2048]{1,0:T(8,128)(2,1)S(1)}, bf16[1024,2048]{1,0:T(8,128)(2,1)}, u32[]{:S(2)}) copy-start(bf16[1024,2048]{1,0:T(8,128)(2,1)} %refs_8_.1) | copy-start | bytes 12582916
  50.6 2.2 %copy-start.1 = (bf16[1024,2048]{1,0:T(8,128)(2,1)S(1)}, bf16[1024,2048]{1,0:T(8,128)(2,1)}, u32[]{:S(2)}) copy-start(bf16[1024,2048]{1,0:T(8,128)(2,1)} %refs_8_.1) | copy-start | bytes 12582916

commit v5 on v4

--- a/solution.py
+++ b/solution.py
@@ -62,9 +62,9 @@
     chunk[capacity:, :capacity] = lanes_dot(ids, pick).astype(BF16)
 
 
-def dispatch_kernel(owners, capacity, order, where, *refs):
-    sources, ranks = refs[:5], refs[5]
-    chunks, copies, sems = refs[6 : 6 + owners], refs[6 + owners : 11 + owners], refs[11 + owners]
+def far_kernel(owners, capacity, far, where, *refs):
+    sources, ranks, place_out, ids_out = refs[:5], refs[5], refs[6], refs[7]
+    chunks, copies, sems = refs[8 : 8 + len(far)], refs[8 + len(far) : 13 + len(far)], refs[13 + len(far)]
     moves = [pltpu.make_async_copy(sources[i], copies[i], sems.at[i]) for i in range(5)]
     for move in moves:
         move.start()
@@ -77,18 +77,34 @@
     ranks[...] = rank
     own = jnp.where(on_item, item, member)
     place = (own ^ mine) * capacity + jnp.where(on_item, rank[1:2], rank[0:1])
+    place_out[...] = place
     local = jnp.where(on_item, item_local, member_local)
     high = local >> 8
     ids = jnp.concatenate([high, local - (high << 8), jnp.zeros((IDS - 2, rows), jnp.int32)], axis=0)
     ids = ids.astype(F32).astype(BF16)
+    ids_out[...] = ids
     moves[4].wait()
-    for chunk, k in zip(chunks, order):
+    for chunk, k in zip(chunks, far):
         pack_chunk(k, capacity, place, ids, copies[4][...], chunk)
 
 
-def margin_kernel(first, weight, features, margin):
+def near_kernel(capacity, near, margin, place, ids, feats, *chunks):
+    for chunk, k in zip(chunks, near):
+        pack_chunk(k, capacity, place[...], ids[...], feats[...], chunk)
+
+
+def margin_kernel(rank, weight, features, margin, copies, sems):
+    parts = copies.shape[0]
+    step = copies.shape[1]
+    moves = [
+        pltpu.make_async_copy(features.at[pl.ds(i * step, step)], copies.at[i], sems.at[i]) for i in range(parts)
+    ]
+    for move in moves:
+        move.start()
     wide = jnp.broadcast_to(weight[...], (16, weight.shape[1])).astype(BF16)
-    margin[...] = lanes_dot(wide, features[...])[0:1]
+    for i in range(parts):
+        moves[i].wait()
+        margin[:, i * step : (i + 1) * step] = lanes_dot(wide, copies[i])[0:1]
 
 
 def chunk_ids(chunk, capacity):
@@ -206,34 +222,50 @@
 
     row = pltpu.VMEM((1, rows_here), jnp.int32)
     half = owners // 2
-    order = [*range(half, owners), *reversed(range(half))]
+    far, near = list(range(half, owners)), list(reversed(range(half)))
     chunk = shape(capacity + IDS, width, dtype=BF16)
-    ranks, *chunks = call(
-        partial(dispatch_kernel, owners, capacity, order),
-        [shape(2, rows_here, dtype=jnp.int32)] + [chunk] * owners,
+    flops = owners * capacity * rows_here * width
+
+    def in_hbm(x):
+        return pltpu.with_memory_space_constraint(x, pltpu.HBM)
+
+    ranks, place, ids, *far_chunks = call(
+        partial(far_kernel, owners, capacity, far),
+        [shape(2, rows_here, dtype=jnp.int32), shape(1, rows_here, dtype=jnp.int32), shape(IDS, rows_here, dtype=BF16)]
+        + [chunk] * len(far),
         (
             where,
-            *(
-                pltpu.with_memory_space_constraint(x, pltpu.HBM)
-                for x in (
-                    member,
-                    item,
-                    member_local.reshape(1, rows_here),
-                    item_local.reshape(1, rows_here),
-                    entity_feats,
-                )
-            ),
+            in_hbm(member),
+            in_hbm(item),
+            in_hbm(member_local.reshape(1, rows_here)),
+            in_hbm(item_local.reshape(1, rows_here)),
+            in_hbm(entity_feats),
         ),
         [SMEM] + [HBM] * 5,
-        flops=2 * owners * capacity * rows_here * width,
+        flops=flops,
         scratch=[row, row, row, row, pltpu.VMEM((rows_here, width), BF16), pltpu.SemaphoreType.DMA((5,))],
     )
-    chunks = [xor_send(x, HOME, owners, k) for k, x in zip(order, chunks)]
+    order = far + near
+    chunks = [xor_send(x, HOME, owners, k) for k, x in zip(far, far_chunks)]
     weight = global_weight.astype(F32).reshape(1, columns)
+    parts = 4
     (global_part,) = call(
-        margin_kernel, [shape(1, rows_here)], (chunks[0], weight, features), [VMEM] * 3, hidden=True
+        margin_kernel,
+        [shape(1, rows_here)],
+        (place, weight, in_hbm(features)),
+        [VMEM, VMEM, HBM],
+        hidden=True,
+        scratch=[pltpu.VMEM((parts, rows_here // parts, columns), BF16), pltpu.SemaphoreType.DMA((parts,))],
     )
     global_total = lax.psum(global_part, "feat")
+    near_chunks = call(
+        partial(near_kernel, capacity, near),
+        [chunk] * len(near),
+        (global_total, place, ids, entity_feats),
+        [VMEM] * 4,
+        hidden=True,
+    )
+    chunks += [xor_send(x, HOME, owners, k) for k, x in zip(near, near_chunks)]
 
     (scores,) = call(
         partial(scores_kernel, order, capacity, n_feat, n_ent),

time: 65.8 us -> 59.3 us (0.901)
  waiting for transfers between devices: 14.1 us -> 8.48 us
  local copies, waits for them, and re-layouts: 4.39 us -> 0.03 us
  Pallas kernels: 11.4 us -> 14.3 us
    ppermute x7, waiting for transfers between devices: 14.1 us -> 8.48 us  [xor_send(): lax.ppermute(x, axes, [(i, i ^ k) for i in range(size)])]
    unnamed x14, local copies, waits for them, and re-layouts: 4.39 us -> 0.03 us
    pallas_call x5 -> x6, Pallas kernels: 11.4 us -> 14.3 us  [call(): pl.pallas_call(kernel, out_shape=out_shape, in_specs=in_specs, out_specs=...]
  transfers between devices with their start and end apart: 7 -> 7, of which waited for: 2 -> 4; matrix products, arithmetic and copies ran while one was open for 1% -> 1% of each run, Pallas kernels for 2% -> 9%
where the time goes in v5:
time: 59.3 us; the launch traced here: 59 us
  blocking collectives  25.4 us (43%)
  Pallas kernels  14.3 us (24%)
  starting transfers between devices  9.29 us (16%)
  waiting for transfers between devices  8.48 us (14%)
  other arithmetic  0.76 us (1%)
  between operations  0.73 us (1%)
    pallas_call x6, Pallas kernels, call(): pl.pallas_call(kernel, out_shape=out_shape, in_specs=in_specs, out_specs=...  14.3 us
    all_to_all x1, blocking collectives, body(): lax.all_to_all(scores, EVERY, split_axis=0, concat_axis=0, tiled=True)  12.1 us
    ppermute x7, starting transfers between devices, xor_send(): lax.ppermute(x, axes, [(i, i ^ k) for i in range(size)])  9.29 us
    ppermute x7, waiting for transfers between devices, xor_send(): lax.ppermute(x, axes, [(i, i ^ k) for i in range(size)])  8.48 us
    all_to_all x1, blocking collectives, body(): came = lax.all_to_all(sent, HOME, split_axis=0, concat_axis=0, tiled=True)  8.4 us
    psum x1, blocking collectives, body(): global_total = lax.psum(global_part, 'feat')  4.95 us
  transfers between devices with their start and end apart: 7, of which 4 were waited for; matrix products, arithmetic and copies ran while one was open for 1% of the time, Pallas kernels for 9%

profile of v5, /device:TPU:0, one launch (start us, length us, event | category | flops | bytes accessed | tf_op | source)
XLA Modules:
  0.0 59.0 jit_solution(14702486168406418798)
XLA Ops:
  0.6 0.0 copy-start.1
  0.6 0.0 copy-start.6
  0.7 0.1 pad_add_fusion.refs_0_
  0.7 2.9 %shard_map.113 = (s32[2,1024]{1,0:T(2,128)S(1)}, s32[1,1024]{1,0:T(1,128)S(1)}, bf16[16,1024]{1,0:T(8,128)(2,1)S(1)}, bf16[272,256]{1,0:T(8,128)(2,1)S(1)}, bf16...) custom-call(s32[2]{0:T(128)S(1)} %pad_add_fusion.refs_0_, ...), custom_call_target="tpu_custom_call" | custom-call | flops 536870912 | bytes 1142792 | tf_op jit(solution)/shard_map/pallas_call | solution.py:184
  3.7 4.1 %collective-permute-start = (bf16[272,256]{1,0:T(8,128)(2,1)S(1)}, bf16[272,256]{1,0:T(8,128)(2,1)S(1)}, u32[]{:S(2)}, u32[]{:S(2)}) collective-permute-start(bf16[272,256]{1,0:T(8,128)(2,1)S(1)} %get-tuple-element.17), channel_id=1, source_target_pairs={{0,8},{1,9},{4,12},{5,13},{8,0},{9,1},{12,4},{13,5},{2,10},{3,11},... | collective-permute-start | bytes 417800 | tf_op jit(solution)/shard_map/ppermute | solution.py:179
  7.8 0.0 collective-permute-start.1
  7.8 3.1 %collective-permute-start.2 = (bf16[272,256]{1,0:T(8,128)(2,1)S(1)}, bf16[272,256]{1,0:T(8,128)(2,1)S(1)}, u32[]{:S(2)}, u32[]{:S(2)}) collective-permute-start(bf16[272,256]{1,0:T(8,128)(2,1)S(1)} %get-tuple-element.19), channel_id=1, source_target_pairs={{0,12},{1,13},{4,8},{5,9},{8,4},{9,5},{12,0},{13,1},{2,14},{3,15},... | collective-permute-start | bytes 417800 | tf_op jit(solution)/shard_map/ppermute | solution.py:179
  10.9 0.6 %collective-permute-start.3 = (bf16[272,256]{1,0:T(8,128)(2,1)S(1)}, bf16[272,256]{1,0:T(8,128)(2,1)S(1)}, u32[]{:S(2)}, u32[]{:S(2)}) collective-permute-start(bf16[272,256]{1,0:T(8,128)(2,1)S(1)} %get-tuple-element.20), channel_id=1, source_target_pairs={{0,13},{1,12},{4,9},{5,8},{8,5},{9,4},{12,1},{13,0},{2,15},{3,14},... | collective-permute-start | bytes 417800 | tf_op jit(solution)/shard_map/ppermute | solution.py:179
  11.5 0.7 %reshape.40 = f32[2048]{0:T(1024)S(1)} convert(bf16[2048]{0:T(1024)(128)(2,1)} %param.11) | non-fusion elementwise | flops 2048 | bytes 12288 | tf_op jit(solution)/shard_map/reshape | solution.py:250
  12.2 0.0 copy-start.2
  12.2 0.0 copy-start.3
  12.2 0.0 copy-start.4
  12.2 0.0 copy-start.5
  12.2 3.9 %shard_map.114 = f32[1,1024]{1,0:T(1,128)S(1)} custom-call(s32[1,1024]{1,0:T(1,128)S(1)} %get-tuple-element.16.rank.refs_1_, f32[1,2048]{1,0:T(1,128)S(1)} %bitcast.10, bf16[1024,2048]{1,0:T(8,128)(2,1)} %refs_8_.1), custom_call_target="tpu_custom_call" | custom-call | tf_op jit(solution)/shard_map/pallas_call | solution.py:184
  16.1 4.9 %psum.7.refs_0_.refs_1_.refs_6_ = f32[1,1024]{1,0:T(1,128)S(1)} all-reduce(f32[1,1024]{1,0:T(1,128)S(1)} %shard_map.114), channel_id=1, replica_groups=mesh['groups'=2,'rows'=4,'feat'=2,'ent'=2] {'feat'}, use_global_device_ids=true, to_apply=%region_0.0 | all-reduce | flops 1024 | bytes 8192 | tf_op jit(solution)/shard_map/psum | solution.py:260
  21.1 0.0 copy-start
  21.1 0.0 copy-done.1
  21.1 1.2 %shard_map.115 = (bf16[272,256]{1,0:T(8,128)(2,1)S(1)}, bf16[272,256]{1,0:T(8,128)(2,1)S(1)}, bf16[272,256]{1,0:T(8,128)(2,1)S(1)}, bf16[272,256]{1,0:T(8,128)(2,1)S(1)}) custom-call(f32[1,1024]{1,0:T(1,128)S(1)} %psum.7.refs_0_.refs_1_.refs_6_, s32[1,1024]{1,0:T(1,128)S(1)} %get-tuple-element.16.rank.refs_1_, ...), custom_call_target="tpu_custom_call" | custom-call | tf_op jit(solution)/shard_map/pallas_call | solution.py:184
  22.3 0.1 collective-permute-start.4
  22.4 1.8 %collective-permute-done.refs_3_.refs_4_ = bf16[272,256]{1,0:T(8,128)(2,1)S(1)} collective-permute-done((bf16[272,256]{1,0:T(8,128)(2,1)S(1)}, bf16[272,256]{1,0:T(8,128)(2,1)S(1)}, u32[]{:S(2)}, u32[]{:S(2)}) %collective-permute-start) | collective-permute-done | bytes 139296 | tf_op jit(solution)/shard_map/ppermute | solution.py:179
  24.2 0.0 collective-permute-start.5
  24.2 1.4 %collective-permute-done.1.refs_4_.refs_5_ = bf16[272,256]{1,0:T(8,128)(2,1)S(1)} collective-permute-done((bf16[272,256]{1,0:T(8,128)(2,1)S(1)}, bf16[272,256]{1,0:T(8,128)(2,1)S(1)}, u32[]{:S(2)}, u32[]{:S(2)}) %collective-permute-start.1) | collective-permute-done | bytes 139296 | tf_op jit(solution)/shard_map/ppermute | solution.py:179
  25.6 1.4 %collective-permute-start.6 = (bf16[272,256]{1,0:T(8,128)(2,1)S(1)}, bf16[272,256]{1,0:T(8,128)(2,1)S(1)}, u32[]{:S(2)}, u32[]{:S(2)}) collective-permute-start(bf16[272,256]{1,0:T(8,128)(2,1)S(1)} %get-tuple-element.24), channel_id=1, source_target_pairs={{0,1},{1,0},{4,5},{5,4},{8,9},{9,8},{12,13},{13,12},{2,3},{3,2},{6... | collective-permute-start | bytes 417800 | tf_op jit(solution)/shard_map/ppermute | solution.py:179
  27.0 0.0 collective-permute-done.2.refs_5_.refs_6_
  27.0 0.0 collective-permute-done.3.refs_6_.refs_7_
  27.0 2.4 %collective-permute-done.4.refs_7_.refs_8_ = bf16[272,256]{1,0:T(8,128)(2,1)S(1)} collective-permute-done((bf16[272,256]{1,0:T(8,128)(2,1)S(1)}, bf16[272,256]{1,0:T(8,128)(2,1)S(1)}, u32[]{:S(2)}, u32[]{:S(2)}) %collective-permute-start.4) | collective-permute-done | bytes 139296 | tf_op jit(solution)/shard_map/ppermute | solution.py:179
  29.4 2.9 %collective-permute-done.5.refs_8_.refs_9_ = bf16[272,256]{1,0:T(8,128)(2,1)S(1)} collective-permute-done((bf16[272,256]{1,0:T(8,128)(2,1)S(1)}, bf16[272,256]{1,0:T(8,128)(2,1)S(1)}, u32[]{:S(2)}, u32[]{:S(2)}) %collective-permute-start.5) | collective-permute-done | bytes 139296 | tf_op jit(solution)/shard_map/ppermute | solution.py:179
  32.3 0.0 collective-permute-done.6.refs_9_.refs_10_
  32.3 0.0 copy-done.6
  32.3 1.9 %shard_map.116 = f32[16,1,256]{2,1,0:T(1,128)S(1)} custom-call(s32[2]{0:T(128)S(1)} %pad_add_fusion.refs_0_, f32[1,1024]{1,0:T(1,128)S(1)} %psum.7.refs_0_.refs_1_.refs_6_, f32[512,256]{1,0:T(8,128)S(1)} %copy-done.6, bf16[272,256]{1,0:T(8,128)(2,1)S(1)} %collective-permute-done.refs_3_.refs_4_, bf16[272,256]{1,0:T(8,128)(2,1)S(1)} %collective-permute-done.1.refs_4_.refs_5_, ...), custom_call_target="tpu_custom_call" | custom-call | flops 1073741824 | bytes 1658888 | tf_op jit(solution)/shard_map/pallas_call | solution.py:184
  34.2 12.1 %all_to_all.10.refs_7_ = f32[16,1,256]{2,1,0:T(1,128)S(1)} all-to-all(f32[16,1,256]{2,1,0:T(1,128)S(1)} %shard_map.116), channel_id=1, replica_groups=mesh['groups'=2,'rows'=4,'feat'=2,'ent'=2] {'rows','feat','ent'}, dimensions={0} | all-to-all | bytes 32768 | tf_op jit(solution)/shard_map/all_to_all | solution.py:277
  46.3 0.0 copy-done.2
  46.3 0.0 copy-done.3
  46.3 0.0 copy-done.4
  46.3 0.0 copy-done.5
  46.3 0.0 copy-done
  46.3 1.7 %shard_map.117 = f32[8,1,2304]{2,1,0:T(1,128)S(1)} custom-call(s32[2]{0:T(128)S(1)} %pad_add_fusion.refs_0_, s32[1,1024]{1,0:T(1,128)S(1)} %bitcast.13, s32[1,1024]{1,0:T(1,128)S(1)} %bitcast.15, s32[2,1024]{1,0:T(2,128)S(1)} %get-tuple-element.15.refs_3_, s32[1,1024]{1,0:T(1,128)S(1)} %bitcast.16, s32[1,1024]{1,0:T(1,128)S(1)} %bitcast.17, ...), custom_call_target="tpu_custom_call" | custom-call | flops 67108864 | bytes 4313096 | tf_op jit(solution)/shard_map/pallas_call | solution.py:184
  48.0 8.4 %all_to_all.11.refs_3_ = f32[8,1,2304]{2,1,0:T(1,128)S(1)} all-to-all(f32[8,1,2304]{2,1,0:T(1,128)S(1)} %shard_map.117), channel_id=1, replica_groups=mesh['groups'=2,'rows'=4,'feat'=2,'ent'=2] {'rows','ent'}, dimensions={0} | all-to-all | bytes 147456 | tf_op jit(solution)/shard_map/all_to_all | solution.py:295
  56.4 2.6 %shard_map.118 = (f32[1,2048]{1,0:T(1,128)}, f32[512,256]{1,0:T(8,128)}) custom-call(s32[2]{0:T(128)S(1)} %pad_add_fusion.refs_0_, f32[512,256]{1,0:T(8,128)S(1)} %copy-done.6, f32[1,2048]{1,0:T(1,128)S(1)} %bitcast.11, f32[8,1,2304]{2,1,0:T(1,128)S(1)} %all_to_all.11.refs_3_, bf16[272,256]{1,0:T(8,128)(2,1)S(1)} %collective-permute-done.refs_3_.refs_4_, ...), custom_call_target="tpu_custom_call" | custom-call | flops 1073741824 | bytes 2252808 | tf_op jit(solution)/shard_map/pallas_call | solution.py:184
Async XLA Ops:
  0.6 20.4 %copy-start.1 = (bf16[1024,256]{1,0:T(8,128)(2,1)S(1)}, bf16[1024,256]{1,0:T(8,128)(2,1)}, u32[]{:S(2)}) copy-start(bf16[1024,256]{1,0:T(8,128)(2,1)} %refs_3_.1) | copy-start | bytes 1572868
  0.6 31.7 %copy-start.6 = (f32[512,256]{1,0:T(8,128)S(1)}, f32[512,256]{1,0:T(8,128)}, u32[]{:S(2)}) copy-start(f32[512,256]{1,0:T(8,128)} %refs_1_.1) | copy-start | bytes 1572868
  3.7 20.5 %collective-permute-start = (bf16[272,256]{1,0:T(8,128)(2,1)S(1)}, bf16[272,256]{1,0:T(8,128)(2,1)S(1)}, u32[]{:S(2)}, u32[]{:S(2)}) collective-permute-start(bf16[272,256]{1,0:T(8,128)(2,1)S(1)} %get-tuple-element.17), channel_id=1, source_target_pairs={{0,8},{1,9},{4,12},{5,13},{8,0},{9,1},{12,4},{13,5},{2,10},{3,11},... | collective-permute-start | bytes 417800 | tf_op jit(solution)/shard_map/ppermute | solution.py:179
  7.8 17.8 %collective-permute-start.1 = (bf16[272,256]{1,0:T(8,128)(2,1)S(1)}, bf16[272,256]{1,0:T(8,128)(2,1)S(1)}, u32[]{:S(2)}, u32[]{:S(2)}) collective-permute-start(bf16[272,256]{1,0:T(8,128)(2,1)S(1)} %get-tuple-element.18), channel_id=1, source_target_pairs={{0,9},{1,8},{4,13},{5,12},{8,1},{9,0},{12,5},{13,4},{2,11},{3,10},... | collective-permute-start | bytes 417800 | tf_op jit(solution)/shard_map/ppermute | solution.py:179
  7.8 19.2 %collective-permute-start.2 = (bf16[272,256]{1,0:T(8,128)(2,1)S(1)}, bf16[272,256]{1,0:T(8,128)(2,1)S(1)}, u32[]{:S(2)}, u32[]{:S(2)}) collective-permute-start(bf16[272,256]{1,0:T(8,128)(2,1)S(1)} %get-tuple-element.19), channel_id=1, source_target_pairs={{0,12},{1,13},{4,8},{5,9},{8,4},{9,5},{12,0},{13,1},{2,14},{3,15},... | collective-permute-start | bytes 417800 | tf_op jit(solution)/shard_map/ppermute | solution.py:179
  10.9 16.2 %collective-permute-start.3 = (bf16[272,256]{1,0:T(8,128)(2,1)S(1)}, bf16[272,256]{1,0:T(8,128)(2,1)S(1)}, u32[]{:S(2)}, u32[]{:S(2)}) collective-permute-start(bf16[272,256]{1,0:T(8,128)(2,1)S(1)} %get-tuple-element.20), channel_id=1, source_target_pairs={{0,13},{1,12},{4,9},{5,8},{8,5},{9,4},{12,1},{13,0},{2,15},{3,14},... | collective-permute-start | bytes 417800 | tf_op jit(solution)/shard_map/ppermute | solution.py:179
  12.2 34.1 %copy-start.2 = (s32[1024,1]{0,1:T(1,128)S(1)}, s32[1024,1]{0,1:T(1,128)}, u32[]{:S(2)}) copy-start(s32[1024,1]{0,1:T(1,128)} %param.14) | copy-start | bytes 12292
  12.2 34.1 %copy-start.3 = (s32[1024,1]{0,1:T(1,128)S(1)}, s32[1024,1]{0,1:T(1,128)}, u32[]{:S(2)}) copy-start(s32[1024,1]{0,1:T(1,128)} %param.16) | copy-start | bytes 12292
  12.2 34.1 %copy-start.4 = (s32[1024]{0:T(1024)S(1)}, s32[1024]{0:T(1024)}, u32[]{:S(2)}) copy-start(s32[1024]{0:T(1024)} %param.18) | copy-start | bytes 12292
  12.2 34.1 %copy-start.5 = (s32[1024]{0:T(1024)S(1)}, s32[1024]{0:T(1024)}, u32[]{:S(2)}) copy-start(s32[1024]{0:T(1024)} %param.19) | copy-start | bytes 12292
  21.1 25.2 %copy-start = (bf16[1024,2048]{1,0:T(8,128)(2,1)S(1)}, bf16[1024,2048]{1,0:T(8,128)(2,1)}, u32[]{:S(2)}) copy-start(bf16[1024,2048]{1,0:T(8,128)(2,1)} %refs_8_.1) | copy-start | bytes 12582916
  22.3 7.1 %collective-permute-start.4 = (bf16[272,256]{1,0:T(8,128)(2,1)S(1)}, bf16[272,256]{1,0:T(8,128)(2,1)S(1)}, u32[]{:S(2)}, u32[]{:S(2)}) collective-permute-start(bf16[272,256]{1,0:T(8,128)(2,1)S(1)} %get-tuple-element.22), channel_id=1, source_target_pairs={{0,5},{1,4},{4,1},{5,0},{8,13},{9,12},{12,9},{13,8},{2,7},{3,6},{6... | collective-permute-start | bytes 417800 | tf_op jit(solution)/shard_map/ppermute | solution.py:179
  24.2 8.1 %collective-permute-start.5 = (bf16[272,256]{1,0:T(8,128)(2,1)S(1)}, bf16[272,256]{1,0:T(8,128)(2,1)S(1)}, u32[]{:S(2)}, u32[]{:S(2)}) collective-permute-start(bf16[272,256]{1,0:T(8,128)(2,1)S(1)} %get-tuple-element.23), channel_id=1, source_target_pairs={{0,4},{1,5},{4,0},{5,1},{8,12},{9,13},{12,8},{13,9},{2,6},{3,7},{6... | collective-permute-start | bytes 417800 | tf_op jit(solution)/shard_map/ppermute | solution.py:179
  25.6 6.7 %collective-permute-start.6 = (bf16[272,256]{1,0:T(8,128)(2,1)S(1)}, bf16[272,256]{1,0:T(8,128)(2,1)S(1)}, u32[]{:S(2)}, u32[]{:S(2)}) collective-permute-start(bf16[272,256]{1,0:T(8,128)(2,1)S(1)} %get-tuple-element.24), channel_id=1, source_target_pairs={{0,1},{1,0},{4,5},{5,4},{8,9},{9,8},{12,13},{13,12},{2,3},{3,2},{6... | collective-permute-start | bytes 417800 | tf_op jit(solution)/shard_map/ppermute | solution.py:179

commit v6 on v5

--- a/solution.py
+++ b/solution.py
@@ -10,7 +10,6 @@
 F32 = jnp.float32
 BF16 = jnp.bfloat16
 HOME = ("rows", "ent")
-EVERY = ("rows", "feat", "ent")
 IDS = 16
 PARAMS = pltpu.CompilerParams(vmem_limit_bytes=24 * 2**20)
 SMEM = pl.BlockSpec(memory_space=pltpu.SMEM)
@@ -88,8 +87,8 @@
         pack_chunk(k, capacity, place, ids, copies[4][...], chunk)
 
 
-def near_kernel(capacity, near, margin, place, ids, feats, *chunks):
-    for chunk, k in zip(chunks, near):
+def rest_kernel(capacity, rest, place, ids, feats, *chunks):
+    for chunk, k in zip(chunks, rest):
         pack_chunk(k, capacity, place[...], ids[...], feats[...], chunk)
 
 
@@ -112,49 +111,47 @@
     return (pair[0:1] * 256.0 + pair[1:2]).astype(jnp.int32)
 
 
-def scores_kernel(order, capacity, n_feat, n_ent, where, margin, coefs, *refs):
-    chunks, out = refs[:-1], refs[-1]
+def scores_kernel(capacity, count, coefs, *refs):
+    chunks, outs = refs[:count], refs[-count:]
     entities = coefs.shape[0]
-    mine = where[0]
     high, low = halves(coefs[...])
-    scores = []
-    for chunk in chunks:
+    for chunk, out in zip(chunks, outs):
         feats = chunk[:capacity]
         every = lanes_dot(high, feats) + lanes_dot(low, feats)
         hits = one_hot(chunk_ids(chunk, capacity), entities)
-        scores.append(jnp.sum(jnp.where(hits, every, 0.0), axis=0, keepdims=True))
-    for k, score in zip(order, scores):
-        home = mine ^ k
-        for f in range(n_feat):
-            out[(home // n_ent * n_feat + f) * n_ent + home % n_ent] = score
-
-
-def home_kernel(
-    owners, capacity, n_feat, n_ent, where, member, item, ranks, clicks, valid, margin, scores, features, out
-):
-    on_item = where[1] > 0
-    total = margin[...]
-    hits_of = [one_hot(owner[...], owners).astype(F32) for owner in (member, item)]
-    spot_of = [one_hot(ranks[side : side + 1], capacity).astype(F32).astype(BF16) for side in (0, 1)]
-    for side in (0, 1):
-        table = None
-        for f in range(side * n_feat // 2, (side + 1) * n_feat // 2):
-            part = jnp.concatenate(
-                [scores[(h // n_ent * n_feat + f) * n_ent + h % n_ent] for h in range(owners)], axis=0
-            )
-            table = part if table is None else table + part
-        found = plain_dot(jnp.concatenate(halves(table), axis=0), spot_of[side])
-        total = total + jnp.sum((found[:owners] + found[owners:]) * hits_of[side], axis=0, keepdims=True)
+        out[...] = jnp.sum(jnp.where(hits, every, 0.0), axis=0, keepdims=True)
+
+
+def margin_rows(owners, capacity, where, member, item, ranks):
+    mine, on_item = where[0], where[1] > 0
+    own = jnp.where(on_item, item[...], member[...])
+    rank = jnp.where(on_item, ranks[1:2], ranks[0:1])
+    return one_hot(own ^ mine, owners).astype(F32), one_hot(rank, capacity).astype(F32).astype(BF16)
+
+
+def gather_kernel(owners, capacity, where, member, item, ranks, margin, *refs):
+    scores, out = refs[:-1], refs[-1]
+    hits, spot = margin_rows(owners, capacity, where, member, item, ranks)
+    table = jnp.concatenate([score[...] for score in scores], axis=0)
+    found = plain_dot(jnp.concatenate(halves(table), axis=0), spot)
+    out[...] = margin[...] + jnp.sum((found[:owners] + found[owners:]) * hits, axis=0, keepdims=True)
+
+
+def home_kernel(owners, capacity, where, member, item, ranks, clicks, valid, features, *refs):
+    margins, out = refs[:-1], refs[-1]
+    mine = where[0]
+    total = margins[0][...]
+    for margin in margins[1:]:
+        total = total + margin[...]
     resid = valid[...].astype(F32) * (jax.nn.sigmoid(total) - clicks[...].astype(F32))
-    hits = jnp.where(on_item, hits_of[1], hits_of[0])
-    spot = jnp.where(on_item, spot_of[1], spot_of[0])
+    hits, spot = margin_rows(owners, capacity, where, member, item, ranks)
     sent = lanes_dot(jnp.concatenate(halves(hits * resid), axis=0), spot)
     sent = sent[:owners] + sent[owners:]
     low = jnp.broadcast_to(resid, (16, resid.shape[1])).astype(BF16)
     grad = plain_dot(low, features[...])[0:1]
-    for h in range(owners):
-        out[h, :, :capacity] = sent[h : h + 1]
-        out[h, :, capacity:] = grad
+    for k in range(owners):
+        out[mine ^ k, :, :capacity] = sent[k : k + 1]
+        out[mine ^ k, :, capacity:] = grad
 
 
 def grads_kernel(order, capacity, scale, where, coefs, weight, came, *refs):
@@ -210,8 +207,8 @@
     owners = lax.axis_size("rows") * n_ent
     capacity = 2 * rows_here // owners
     mine = lax.axis_index(HOME).astype(jnp.int32)
-    on_item = (lax.axis_index("feat") >= n_feat // 2).astype(jnp.int32)
-    where = jnp.stack([mine, on_item])
+    feat = lax.axis_index("feat")
+    where = jnp.stack([mine, (feat >= n_feat // 2).astype(jnp.int32)])
     member, item = member_owner.reshape(1, rows_here), item_owner.reshape(1, rows_here)
 
     def shape(*dims, dtype=F32):
@@ -221,18 +218,21 @@
         return lambda *refs: kernel(*args, *refs)
 
     row = pltpu.VMEM((1, rows_here), jnp.int32)
-    half = owners // 2
-    far, near = list(range(half, owners)), list(reversed(range(half)))
+    half, early = owners // 2, 3 * owners // 4
+    near, far = [*range(1, half), 0], list(range(half, owners))
+    if half > 3:
+        near = [*range(2, half), 1, 0]
+    first = [*near[:-2], *range(half, early)]
+    rest = [*near[-2:], *range(early, owners)]
     chunk = shape(capacity + IDS, width, dtype=BF16)
-    flops = owners * capacity * rows_here * width
 
     def in_hbm(x):
         return pltpu.with_memory_space_constraint(x, pltpu.HBM)
 
-    ranks, place, ids, *far_chunks = call(
-        partial(far_kernel, owners, capacity, far),
+    ranks, place, ids, *chunks = call(
+        partial(far_kernel, owners, capacity, first),
         [shape(2, rows_here, dtype=jnp.int32), shape(1, rows_here, dtype=jnp.int32), shape(IDS, rows_here, dtype=BF16)]
-        + [chunk] * len(far),
+        + [chunk] * len(first),
         (
             where,
             in_hbm(member),
@@ -242,13 +242,20 @@
             in_hbm(entity_feats),
         ),
         [SMEM] + [HBM] * 5,
-        flops=flops,
+        hidden=True,
         scratch=[row, row, row, row, pltpu.VMEM((rows_here, width), BF16), pltpu.SemaphoreType.DMA((5,))],
     )
-    order = far + near
-    chunks = [xor_send(x, HOME, owners, k) for k, x in zip(far, far_chunks)]
+    chunks += call(
+        partial(rest_kernel, capacity, rest),
+        [chunk] * len(rest),
+        (place, ids, entity_feats),
+        [VMEM] * 3,
+        flops=owners * capacity * rows_here * width,
+    )
+    order = first + rest
+    chunks = {k: xor_send(x, HOME, owners, k) for k, x in zip(order, chunks)}
     weight = global_weight.astype(F32).reshape(1, columns)
-    parts = 4
+    parts = 16
     (global_part,) = call(
         margin_kernel,
         [shape(1, rows_here)],
@@ -257,26 +264,30 @@
         hidden=True,
         scratch=[pltpu.VMEM((parts, rows_here // parts, columns), BF16), pltpu.SemaphoreType.DMA((parts,))],
     )
-    global_total = lax.psum(global_part, "feat")
-    near_chunks = call(
-        partial(near_kernel, capacity, near),
-        [chunk] * len(near),
-        (global_total, place, ids, entity_feats),
-        [VMEM] * 4,
+    returned = [None] * owners
+    before = [global_part]
+    for group in [near, list(range(half, early)), *([k] for k in range(early, owners))]:
+        scores = call(
+            partial(scores_kernel, capacity, len(group)),
+            [shape(1, capacity)] * len(group),
+            (coefs, *(chunks[k] for k in group), *before),
+            [VMEM] * (1 + len(group) + len(before)),
+            hidden=True,
+        )
+        for k, score in zip(group, scores):
+            returned[k] = xor_send(score, HOME, owners, k)
+        if len(group) > 1:
+            before = [returned[k] for k in group]
+    (margin,) = call(
+        partial(gather_kernel, owners, capacity),
+        [shape(1, rows_here)],
+        (where, member, item, ranks, global_part, *returned),
+        [SMEM] + [VMEM] * (4 + owners),
         hidden=True,
     )
-    chunks += [xor_send(x, HOME, owners, k) for k, x in zip(near, near_chunks)]
-
-    (scores,) = call(
-        partial(scores_kernel, order, capacity, n_feat, n_ent),
-        [shape(n_feat * owners, 1, capacity)],
-        (where, global_total, coefs, *chunks),
-        [SMEM] + [VMEM] * (2 + owners),
-        flops=4 * coefs.size * owners * capacity,
-    )
-    returned = lax.all_to_all(scores, EVERY, split_axis=0, concat_axis=0, tiled=True)
+    margins = [xor_send(margin, "feat", n_feat, q) for q in range(n_feat)]
     (sent,) = call(
-        partial(home_kernel, owners, capacity, n_feat, n_ent),
+        partial(home_kernel, owners, capacity),
         [shape(owners, 1, capacity + columns)],
         (
             where,
@@ -285,18 +296,17 @@
             ranks,
             clicks.reshape(1, rows_here),
             valid.reshape(1, rows_here),
-            global_total,
-            returned,
             features,
+            *margins,
         ),
-        [SMEM] + [VMEM] * 8,
+        [SMEM] + [VMEM] * (6 + n_feat),
         flops=32 * features.size,
     )
     came = lax.all_to_all(sent, HOME, split_axis=0, concat_axis=0, tiled=True)
     grad_global, grad_coefs = call(
         partial(grads_kernel, order, capacity, 1.0 / math.sqrt(rows_here * owners)),
         [shape(1, columns), shape(*coefs.shape)],
-        (where, coefs, weight, came, *chunks),
+        (where, coefs, weight, came, *(chunks[k] for k in order)),
         [SMEM] + [VMEM] * (3 + owners),
         flops=4 * coefs.size * owners * capacity,
     )

time: 59.3 us -> 66 us (1.11)
  blocking collectives: 25.4 us -> 8.96 us
  starting transfers between devices: 9.29 us -> 20.5 us
  waiting for transfers between devices: 8.48 us -> 17.1 us
  Pallas kernels: 14.3 us -> 16.6 us
  local copies, waits for them, and re-layouts: 0.03 us -> 1.08 us
    all_to_all x1 -> x0, blocking collectives: 12.1 us -> none  [body(): lax.all_to_all(scores, EVERY, split_axis=0, concat_axis=0, tiled=True)]
    ppermute x7 -> x15, starting transfers between devices: 9.29 us -> 20.5 us  [xor_send(): lax.ppermute(x, axes, [(i, i ^ k) for i in range(size)])]
    ppermute x7 -> x15, waiting for transfers between devices: 8.48 us -> 17.1 us  [xor_send(): lax.ppermute(x, axes, [(i, i ^ k) for i in range(size)])]
    psum x1 -> x0, blocking collectives: 4.95 us -> none  [body(): global_total = lax.psum(global_part, 'feat')]
    pallas_call x6 -> x10, Pallas kernels: 14.3 us -> 16.6 us  [call(): pl.pallas_call(kernel, out_shape=out_shape, in_specs=in_specs, out_specs=...]
    unnamed x14, local copies, waits for them, and re-layouts: 0.03 us -> 1.08 us
  transfers between devices with their start and end apart: 7 -> 15, of which waited for: 4 -> 9; matrix products, arithmetic and copies ran while one was open for 1% -> 1% of each run, Pallas kernels for 9% -> 14%
where the time goes in v6:
time: 66 us; the launch traced here: 65.7 us
  starting transfers between devices  20.5 us (31%)
  waiting for transfers between devices  17.1 us (26%)
  Pallas kernels  16.6 us (25%)
  blocking collectives  8.96 us (14%)
  local copies, waits for them, and re-layouts  1.08 us (2%)
  between operations  0.79 us (1%)
  other arithmetic  0.76 us (1%)
    ppermute x15, starting transfers between devices, xor_send(): lax.ppermute(x, axes, [(i, i ^ k) for i in range(size)])  20.5 us
    ppermute x15, waiting for transfers between devices, xor_send(): lax.ppermute(x, axes, [(i, i ^ k) for i in range(size)])  17.1 us
    pallas_call x10, Pallas kernels, call(): pl.pallas_call(kernel, out_shape=out_shape, in_specs=in_specs, out_specs=...  16.6 us
    all_to_all x1, blocking collectives, body(): came = lax.all_to_all(sent, HOME, split_axis=0, concat_axis=0, tiled=True)  8.96 us
  transfers between devices with their start and end apart: 15, of which 9 were waited for; matrix products, arithmetic and copies ran while one was open for 1% of the time, Pallas kernels for 14%

profile of v6, /device:TPU:0, one launch (start us, length us, event | category | flops | bytes accessed | tf_op | source)
XLA Modules:
  0.0 65.7 jit_solution(8675017919453107)
XLA Ops:
  0.6 0.1 pad_add_fusion.refs_0_
  0.7 2.9 %shard_map.113 = (s32[2,1024]{1,0:T(2,128)S(1)}, s32[1,1024]{1,0:T(1,128)S(1)}, bf16[16,1024]{1,0:T(8,128)(2,1)S(1)}, bf16[272,256]{1,0:T(8,128)(2,1)S(1)}, bf16...) custom-call(s32[2]{0:T(128)S(1)} %pad_add_fusion.refs_0_, ...), custom_call_target="tpu_custom_call" | custom-call | tf_op jit(solution)/shard_map/pallas_call | solution.py:181
  3.7 3.1 %collective-permute-start = (bf16[272,256]{1,0:T(8,128)(2,1)S(1)}, bf16[272,256]{1,0:T(8,128)(2,1)S(1)}, u32[]{:S(2)}, u32[]{:S(2)}) collective-permute-start(bf16[272,256]{1,0:T(8,128)(2,1)S(1)} %get-tuple-element.23), channel_id=1, source_target_pairs={{0,4},{1,5},{4,0},{5,1},{8,12},{9,13},{12,8},{13,9},{2,6},{3,7},{6... | collective-permute-start | bytes 417800 | tf_op jit(solution)/shard_map/ppermute | solution.py:176
  6.7 0.0 collective-permute-start.1
  6.8 1.0 %copy-done.2 = bf16[1024,256]{1,0:T(8,128)(2,1)S(1)} copy-done((bf16[1024,256]{1,0:T(8,128)(2,1)S(1)}, bf16[1024,256]{1,0:T(8,128)(2,1)}, u32[]{:S(2)}) %copy-start.2) | copy-done | bytes 524312
  7.8 1.2 %shard_map.115 = (bf16[272,256]{1,0:T(8,128)(2,1)S(1)}, bf16[272,256]{1,0:T(8,128)(2,1)S(1)}, bf16[272,256]{1,0:T(8,128)(2,1)S(1)}, bf16[272,256]{1,0:T(8,128)(2,1)S(1)}) custom-call(s32[1,1024]{1,0:T(1,128)S(1)} %get-tuple-element.22.rank.refs_0_, bf16[16,1024]{1,0:T(8,128)(2,1)S(1)} %get-tuple-element.25.refs_1_, bf16[1024,256]{1,0:T(8,128)(2,1)S(1)} %copy-done.2), custom_call_target="tpu_custom_call" | custom-call | flops 536870912 | bytes 1118208 | tf_op jit(solution)/shard_map/pallas_call | solution.py:181
  9.0 0.0 copy-start.3
  9.0 0.0 copy-start.4
  9.1 0.0 copy-start
  9.1 0.0 copy-start.5
  9.1 0.0 copy-start.6
  9.1 0.3 collective-permute-start.2
  9.3 3.0 %collective-permute-start.6 = (bf16[272,256]{1,0:T(8,128)(2,1)S(1)}, bf16[272,256]{1,0:T(8,128)(2,1)S(1)}, u32[]{:S(2)}, u32[]{:S(2)}) collective-permute-start(bf16[272,256]{1,0:T(8,128)(2,1)S(1)} %get-tuple-element.32), channel_id=1, source_target_pairs={{0,8},{1,9},{4,12},{5,13},{8,0},{9,1},{12,4},{13,5},{2,10},{3,11},... | collective-permute-start | bytes 417800 | tf_op jit(solution)/shard_map/ppermute | solution.py:176
  12.3 0.0 collective-permute-start.7
  12.3 0.0 collective-permute-done.refs_1_.refs_4_
  12.3 3.3 %collective-permute-start.10 = (bf16[272,256]{1,0:T(8,128)(2,1)S(1)}, bf16[272,256]{1,0:T(8,128)(2,1)S(1)}, u32[]{:S(2)}, u32[]{:S(2)}) collective-permute-start(bf16[272,256]{1,0:T(8,128)(2,1)S(1)} %get-tuple-element.36), channel_id=1, source_target_pairs={{0,12},{1,13},{4,8},{5,9},{8,4},{9,5},{12,0},{13,1},{2,14},{3,15},... | collective-permute-start | bytes 417800 | tf_op jit(solution)/shard_map/ppermute | solution.py:176
  15.7 0.0 collective-permute-done.1.refs_2_.refs_5_
  15.7 1.1 %collective-permute-start.12 = (bf16[272,256]{1,0:T(8,128)(2,1)S(1)}, bf16[272,256]{1,0:T(8,128)(2,1)S(1)}, u32[]{:S(2)}, u32[]{:S(2)}) collective-permute-start(bf16[272,256]{1,0:T(8,128)(2,1)S(1)} %get-tuple-element.37), channel_id=1, source_target_pairs={{0,13},{1,12},{4,9},{5,8},{8,5},{9,4},{12,1},{13,0},{2,15},{3,14},... | collective-permute-start | bytes 417800 | tf_op jit(solution)/shard_map/ppermute | solution.py:176
  16.8 0.7 %reshape.40 = f32[2048]{0:T(1024)S(1)} convert(bf16[2048]{0:T(1024)(128)(2,1)} %param.11) | non-fusion elementwise | flops 2048 | bytes 12288 | tf_op jit(solution)/shard_map/reshape | solution.py:257
  17.5 5.7 %shard_map.114.refs_5_.refs_4_ = f32[1,1024]{1,0:T(1,128)S(1)} custom-call(s32[1,1024]{1,0:T(1,128)S(1)} %get-tuple-element.22.rank.refs_0_, f32[1,2048]{1,0:T(1,128)S(1)} %bitcast.16, bf16[1024,2048]{1,0:T(8,128)(2,1)} %refs_6_.1), custom_call_target="tpu_custom_call" | custom-call | tf_op jit(solution)/shard_map/pallas_call | solution.py:181
  23.2 0.0 collective-permute-done.2.refs_3_.refs_8_
  23.2 0.8 %shard_map.116 = (f32[1,256]{1,0:T(1,128)S(1)}, f32[1,256]{1,0:T(1,128)S(1)}, f32[1,256]{1,0:T(1,128)S(1)}, f32[1,256]{1,0:T(1,128)S(1)}) custom-call(f32[512,256]{1,0:T(8,128)S(1)} %copy-done.1, bf16[272,256]{1,0:T(8,128)(2,1)S(1)} %collective-permute-done.refs_1_.refs_4_, bf16[272,256]{1,0:T(8,128)(2,1)S(1)} %collective-permute-done.1.refs_2_.refs_5_, ...), custom_call_target="tpu_custom_call" | custom-call | tf_op jit(solution)/shard_map/pallas_call | solution.py:181
  23.9 0.1 collective-permute-start.3
  24.0 4.7 %collective-permute-done.6.refs_1_.refs_6_ = bf16[272,256]{1,0:T(8,128)(2,1)S(1)} collective-permute-done((bf16[272,256]{1,0:T(8,128)(2,1)S(1)}, bf16[272,256]{1,0:T(8,128)(2,1)S(1)}, u32[]{:S(2)}, u32[]{:S(2)}) %collective-permute-start.6) | collective-permute-done | bytes 139296 | tf_op jit(solution)/shard_map/ppermute | solution.py:176
  28.8 0.4 collective-permute-start.4
  29.1 1.5 %collective-permute-done.7.refs_2_.refs_7_ = bf16[272,256]{1,0:T(8,128)(2,1)S(1)} collective-permute-done((bf16[272,256]{1,0:T(8,128)(2,1)S(1)}, bf16[272,256]{1,0:T(8,128)(2,1)S(1)}, u32[]{:S(2)}, u32[]{:S(2)}) %collective-permute-start.7) | collective-permute-done | bytes 139296 | tf_op jit(solution)/shard_map/ppermute | solution.py:176
  30.6 0.9 %collective-permute-start.5 = (f32[1,256]{1,0:T(1,128)S(1)}, f32[1,256]{1,0:T(1,128)S(1)}, u32[]{:S(2)}, u32[]{:S(2)}) collective-permute-start(f32[1,256]{1,0:T(1,128)S(1)} %get-tuple-element.31), channel_id=1, source_target_pairs={{0,5},{1,4},{4,1},{5,0},{8,13},{9,12},{12,9},{13,8},{2,7},{3,6},{6... | collective-permute-start | bytes 3080 | tf_op jit(solution)/shard_map/ppermute | solution.py:176
  31.5 0.0 collective-permute-done.3.refs_5_.refs_6_
  31.5 0.8 %collective-permute-done.4.refs_3_.refs_7_ = f32[1,256]{1,0:T(1,128)S(1)} collective-permute-done((f32[1,256]{1,0:T(1,128)S(1)}, f32[1,256]{1,0:T(1,128)S(1)}, u32[]{:S(2)}, u32[]{:S(2)}) %collective-permute-start.4) | collective-permute-done | bytes 1056 | tf_op jit(solution)/shard_map/ppermute | solution.py:176
  32.3 1.3 %collective-permute-done.5.refs_4_.refs_8_ = f32[1,256]{1,0:T(1,128)S(1)} collective-permute-done((f32[1,256]{1,0:T(1,128)S(1)}, f32[1,256]{1,0:T(1,128)S(1)}, u32[]{:S(2)}, u32[]{:S(2)}) %collective-permute-start.5) | collective-permute-done | bytes 1056 | tf_op jit(solution)/shard_map/ppermute | solution.py:176
  33.6 0.5 shard_map.117
  34.1 2.7 %collective-permute-start.8 = (f32[1,256]{1,0:T(1,128)S(1)}, f32[1,256]{1,0:T(1,128)S(1)}, u32[]{:S(2)}, u32[]{:S(2)}) collective-permute-start(f32[1,256]{1,0:T(1,128)S(1)} %get-tuple-element.34), channel_id=1, source_target_pairs={{0,8},{1,9},{4,12},{5,13},{8,0},{9,1},{12,4},{13,5},{2,10},{3,11},... | collective-permute-start | bytes 3080 | tf_op jit(solution)/shard_map/ppermute | solution.py:176
  36.8 0.6 collective-permute-start.9
  37.4 0.0 collective-permute-done.10.refs_1_.refs_10_
  37.4 1.3 %collective-permute-done.8.refs_2_.refs_9_ = f32[1,256]{1,0:T(1,128)S(1)} collective-permute-done((f32[1,256]{1,0:T(1,128)S(1)}, f32[1,256]{1,0:T(1,128)S(1)}, u32[]{:S(2)}, u32[]{:S(2)}) %collective-permute-start.8) | collective-permute-done | bytes 1056 | tf_op jit(solution)/shard_map/ppermute | solution.py:176
  38.7 2.0 %collective-permute-done.9.refs_3_.refs_10_ = f32[1,256]{1,0:T(1,128)S(1)} collective-permute-done((f32[1,256]{1,0:T(1,128)S(1)}, f32[1,256]{1,0:T(1,128)S(1)}, u32[]{:S(2)}, u32[]{:S(2)}) %collective-permute-start.9) | collective-permute-done | bytes 1056 | tf_op jit(solution)/shard_map/ppermute | solution.py:176
  40.7 0.4 shard_map.118
  41.1 2.0 %collective-permute-start.11 = (f32[1,256]{1,0:T(1,128)S(1)}, f32[1,256]{1,0:T(1,128)S(1)}, u32[]{:S(2)}, u32[]{:S(2)}) collective-permute-start(f32[1,256]{1,0:T(1,128)S(1)} %shard_map.118), channel_id=1, source_target_pairs={{0,12},{1,13},{4,8},{5,9},{8,4},{9,5},{12,0},{13,1},{2,14},{3,15},... | collective-permute-start | bytes 3080 | tf_op jit(solution)/shard_map/ppermute | solution.py:176
  43.1 0.4 shard_map.119
  43.4 1.6 %collective-permute-start.13 = (f32[1,256]{1,0:T(1,128)S(1)}, f32[1,256]{1,0:T(1,128)S(1)}, u32[]{:S(2)}, u32[]{:S(2)}) collective-permute-start(f32[1,256]{1,0:T(1,128)S(1)} %shard_map.119), channel_id=1, source_target_pairs={{0,13},{1,12},{4,9},{5,8},{8,5},{9,4},{12,1},{13,0},{2,15},{3,14},... | collective-permute-start | bytes 3080 | tf_op jit(solution)/shard_map/ppermute | solution.py:176
  45.0 1.5 %collective-permute-done.11.refs_11_ = f32[1,256]{1,0:T(1,128)S(1)} collective-permute-done((f32[1,256]{1,0:T(1,128)S(1)}, f32[1,256]{1,0:T(1,128)S(1)}, u32[]{:S(2)}, u32[]{:S(2)}) %collective-permute-start.11) | collective-permute-done | bytes 1056 | tf_op jit(solution)/shard_map/ppermute | solution.py:176
  46.5 1.8 %collective-permute-done.13.refs_12_ = f32[1,256]{1,0:T(1,128)S(1)} collective-permute-done((f32[1,256]{1,0:T(1,128)S(1)}, f32[1,256]{1,0:T(1,128)S(1)}, u32[]{:S(2)}, u32[]{:S(2)}) %collective-permute-start.13) | collective-permute-done | bytes 1056 | tf_op jit(solution)/shard_map/ppermute | solution.py:176
  48.3 0.8 %shard_map.120.refs_7_ = f32[1,1024]{1,0:T(1,128)S(1)} custom-call(s32[2]{0:T(128)S(1)} %pad_add_fusion.refs_0_, s32[1,1024]{1,0:T(1,128)S(1)} %bitcast.11, s32[1,1024]{1,0:T(1,128)S(1)} %bitcast.14, s32[2,1024]{1,0:T(2,128)S(1)} %get-tuple-element.21.refs_3_, f32[1,1024]{1,0:T(1,128)S(1)} %shard_map.114.refs_5_.refs_4_, ...), custom_call_target="tpu_custom_call" | custom-call | tf_op jit(solution)/shard_map/pallas_call | solution.py:181
  49.1 1.6 %collective-permute-start.14 = (f32[1,1024]{1,0:T(1,128)S(1)}, f32[1,1024]{1,0:T(1,128)S(1)}, u32[]{:S(2)}, u32[]{:S(2)}) collective-permute-start(f32[1,1024]{1,0:T(1,128)S(1)} %shard_map.120.refs_7_), channel_id=1, source_target_pairs={{0,2},{2,0},{1,3},{3,1},{4,6},{6,4},{5,7},{7,5},{8,10},{10,8},{9,1... | collective-permute-start | bytes 12296 | tf_op jit(solution)/shard_map/ppermute | solution.py:176
  50.7 2.1 %collective-permute-done.14.refs_8_ = f32[1,1024]{1,0:T(1,128)S(1)} collective-permute-done((f32[1,1024]{1,0:T(1,128)S(1)}, f32[1,1024]{1,0:T(1,128)S(1)}, u32[]{:S(2)}, u32[]{:S(2)}) %collective-permute-start.14) | collective-permute-done | bytes 4128 | tf_op jit(solution)/shard_map/ppermute | solution.py:176
  52.8 1.4 %shard_map.121 = f32[8,1,2304]{2,1,0:T(1,128)S(1)} custom-call(s32[2]{0:T(128)S(1)} %pad_add_fusion.refs_0_, s32[1,1024]{1,0:T(1,128)S(1)} %bitcast.12, s32[1,1024]{1,0:T(1,128)S(1)} %bitcast.15, s32[2,1024]{1,0:T(2,128)S(1)} %get-tuple-element.21.refs_3_, s32[1,1024]{1,0:T(1,128)S(1)} %bitcast.18, s32[1,1024]{1,0:T(1,128)S(1)} %bitcast.19, ...), custom_call_target="tpu_custom_call" | custom-call | flops 67108864 | bytes 4300808 | tf_op jit(solution)/shard_map/pallas_call | solution.py:181
  54.2 9.0 %all_to_all.5.refs_3_ = f32[8,1,2304]{2,1,0:T(1,128)S(1)} all-to-all(f32[8,1,2304]{2,1,0:T(1,128)S(1)} %shard_map.121), channel_id=1, replica_groups=mesh['groups'=2,'rows'=4,'feat'=2,'ent'=2] {'rows','ent'}, dimensions={0} | all-to-all | bytes 147456 | tf_op jit(solution)/shard_map/all_to_all | solution.py:305
  63.1 2.6 %shard_map.122 = (f32[1,2048]{1,0:T(1,128)}, f32[512,256]{1,0:T(8,128)}) custom-call(s32[2]{0:T(128)S(1)} %pad_add_fusion.refs_0_, f32[512,256]{1,0:T(8,128)S(1)} %copy-done.1, f32[1,2048]{1,0:T(1,128)S(1)} %bitcast.17, f32[8,1,2304]{2,1,0:T(1,128)S(1)} %all_to_all.5.refs_3_, bf16[272,256]{1,0:T(8,128)(2,1)S(1)} %collective-permute-done.refs_1_.refs_4_, ...), custom_call_target="tpu_custom_call" | custom-call | flops 1073741824 | bytes 2252808 | tf_op jit(solution)/shard_map/pallas_call | solution.py:181
  (9 shorter events, 0.0 us)
Async XLA Ops:
  0.6 22.5 %copy-start.1 = (f32[512,256]{1,0:T(8,128)S(1)}, f32[512,256]{1,0:T(8,128)}, u32[]{:S(2)}) copy-start(f32[512,256]{1,0:T(8,128)} %refs_1_.1) | copy-start | bytes 1572868
  3.7 8.7 %collective-permute-start = (bf16[272,256]{1,0:T(8,128)(2,1)S(1)}, bf16[272,256]{1,0:T(8,128)(2,1)S(1)}, u32[]{:S(2)}, u32[]{:S(2)}) collective-permute-start(bf16[272,256]{1,0:T(8,128)(2,1)S(1)} %get-tuple-element.23), channel_id=1, source_target_pairs={{0,4},{1,5},{4,0},{5,1},{8,12},{9,13},{12,8},{13,9},{2,6},{3,7},{6... | collective-permute-start | bytes 417800 | tf_op jit(solution)/shard_map/ppermute | solution.py:176
  6.7 8.9 %collective-permute-start.1 = (bf16[272,256]{1,0:T(8,128)(2,1)S(1)}, bf16[272,256]{1,0:T(8,128)(2,1)S(1)}, u32[]{:S(2)}, u32[]{:S(2)}) collective-permute-start(bf16[272,256]{1,0:T(8,128)(2,1)S(1)} %get-tuple-element.24), channel_id=1, source_target_pairs={{0,5},{1,4},{4,1},{5,0},{8,13},{9,12},{12,9},{13,8},{2,7},{3,6},{6... | collective-permute-start | bytes 417800 | tf_op jit(solution)/shard_map/ppermute | solution.py:176
  6.8 1.0 %copy-start.2 = (bf16[1024,256]{1,0:T(8,128)(2,1)S(1)}, bf16[1024,256]{1,0:T(8,128)(2,1)}, u32[]{:S(2)}) copy-start(bf16[1024,256]{1,0:T(8,128)(2,1)} %refs_2_.1) | copy-start | bytes 1572868
  9.0 39.3 %copy-start.3 = (s32[1024,1]{0,1:T(1,128)S(1)}, s32[1024,1]{0,1:T(1,128)}, u32[]{:S(2)}) copy-start(s32[1024,1]{0,1:T(1,128)} %param.14) | copy-start | bytes 12292
  9.0 39.3 %copy-start.4 = (s32[1024,1]{0,1:T(1,128)S(1)}, s32[1024,1]{0,1:T(1,128)}, u32[]{:S(2)}) copy-start(s32[1024,1]{0,1:T(1,128)} %param.16) | copy-start | bytes 12292
  9.1 43.7 %copy-start = (bf16[1024,2048]{1,0:T(8,128)(2,1)S(1)}, bf16[1024,2048]{1,0:T(8,128)(2,1)}, u32[]{:S(2)}) copy-start(bf16[1024,2048]{1,0:T(8,128)(2,1)} %refs_6_.1) | copy-start | bytes 12582916
  9.1 43.7 %copy-start.5 = (s32[1024]{0:T(1024)S(1)}, s32[1024]{0:T(1024)}, u32[]{:S(2)}) copy-start(s32[1024]{0:T(1024)} %param.18) | copy-start | bytes 12292
  9.1 43.7 %copy-start.6 = (s32[1024]{0:T(1024)S(1)}, s32[1024]{0:T(1024)}, u32[]{:S(2)}) copy-start(s32[1024]{0:T(1024)} %param.19) | copy-start | bytes 12292
  9.1 14.1 %collective-permute-start.2 = (bf16[272,256]{1,0:T(8,128)(2,1)S(1)}, bf16[272,256]{1,0:T(8,128)(2,1)S(1)}, u32[]{:S(2)}, u32[]{:S(2)}) collective-permute-start(bf16[272,256]{1,0:T(8,128)(2,1)S(1)} %get-tuple-element.26), channel_id=1, source_target_pairs={{0,1},{1,0},{4,5},{5,4},{8,9},{9,8},{12,13},{13,12},{2,3},{3,2},{6... | collective-permute-start | bytes 417800 | tf_op jit(solution)/shard_map/ppermute | solution.py:176
  9.3 19.4 %collective-permute-start.6 = (bf16[272,256]{1,0:T(8,128)(2,1)S(1)}, bf16[272,256]{1,0:T(8,128)(2,1)S(1)}, u32[]{:S(2)}, u32[]{:S(2)}) collective-permute-start(bf16[272,256]{1,0:T(8,128)(2,1)S(1)} %get-tuple-element.32), channel_id=1, source_target_pairs={{0,8},{1,9},{4,12},{5,13},{8,0},{9,1},{12,4},{13,5},{2,10},{3,11},... | collective-permute-start | bytes 417800 | tf_op jit(solution)/shard_map/ppermute | solution.py:176
  12.3 18.3 %collective-permute-start.7 = (bf16[272,256]{1,0:T(8,128)(2,1)S(1)}, bf16[272,256]{1,0:T(8,128)(2,1)S(1)}, u32[]{:S(2)}, u32[]{:S(2)}) collective-permute-start(bf16[272,256]{1,0:T(8,128)(2,1)S(1)} %get-tuple-element.33), channel_id=1, source_target_pairs={{0,9},{1,8},{4,13},{5,12},{8,1},{9,0},{12,5},{13,4},{2,11},{3,10},... | collective-permute-start | bytes 417800 | tf_op jit(solution)/shard_map/ppermute | solution.py:176
  12.3 25.1 %collective-permute-start.10 = (bf16[272,256]{1,0:T(8,128)(2,1)S(1)}, bf16[272,256]{1,0:T(8,128)(2,1)S(1)}, u32[]{:S(2)}, u32[]{:S(2)}) collective-permute-start(bf16[272,256]{1,0:T(8,128)(2,1)S(1)} %get-tuple-element.36), channel_id=1, source_target_pairs={{0,12},{1,13},{4,8},{5,9},{8,4},{9,5},{12,0},{13,1},{2,14},{3,15},... | collective-permute-start | bytes 417800 | tf_op jit(solution)/shard_map/ppermute | solution.py:176
  15.7 27.4 %collective-permute-start.12 = (bf16[272,256]{1,0:T(8,128)(2,1)S(1)}, bf16[272,256]{1,0:T(8,128)(2,1)S(1)}, u32[]{:S(2)}, u32[]{:S(2)}) collective-permute-start(bf16[272,256]{1,0:T(8,128)(2,1)S(1)} %get-tuple-element.37), channel_id=1, source_target_pairs={{0,13},{1,12},{4,9},{5,8},{8,5},{9,4},{12,1},{13,0},{2,15},{3,14},... | collective-permute-start | bytes 417800 | tf_op jit(solution)/shard_map/ppermute | solution.py:176
  23.9 7.6 %collective-permute-start.3 = (f32[1,256]{1,0:T(1,128)S(1)}, f32[1,256]{1,0:T(1,128)S(1)}, u32[]{:S(2)}, u32[]{:S(2)}) collective-permute-start(f32[1,256]{1,0:T(1,128)S(1)} %get-tuple-element.29), channel_id=1, source_target_pairs={{0,1},{1,0},{4,5},{5,4},{8,9},{9,8},{12,13},{13,12},{2,3},{3,2},{6... | collective-permute-start | bytes 3080 | tf_op jit(solution)/shard_map/ppermute | solution.py:176
  28.8 3.6 %collective-permute-start.4 = (f32[1,256]{1,0:T(1,128)S(1)}, f32[1,256]{1,0:T(1,128)S(1)}, u32[]{:S(2)}, u32[]{:S(2)}) collective-permute-start(f32[1,256]{1,0:T(1,128)S(1)} %get-tuple-element.30), channel_id=1, source_target_pairs={{0,4},{1,5},{4,0},{5,1},{8,12},{9,13},{12,8},{13,9},{2,6},{3,7},{6... | collective-permute-start | bytes 3080 | tf_op jit(solution)/shard_map/ppermute | solution.py:176
  30.6 3.0 %collective-permute-start.5 = (f32[1,256]{1,0:T(1,128)S(1)}, f32[1,256]{1,0:T(1,128)S(1)}, u32[]{:S(2)}, u32[]{:S(2)}) collective-permute-start(f32[1,256]{1,0:T(1,128)S(1)} %get-tuple-element.31), channel_id=1, source_target_pairs={{0,5},{1,4},{4,1},{5,0},{8,13},{9,12},{12,9},{13,8},{2,7},{3,6},{6... | collective-permute-start | bytes 3080 | tf_op jit(solution)/shard_map/ppermute | solution.py:176
  34.1 4.5 %collective-permute-start.8 = (f32[1,256]{1,0:T(1,128)S(1)}, f32[1,256]{1,0:T(1,128)S(1)}, u32[]{:S(2)}, u32[]{:S(2)}) collective-permute-start(f32[1,256]{1,0:T(1,128)S(1)} %get-tuple-element.34), channel_id=1, source_target_pairs={{0,8},{1,9},{4,12},{5,13},{8,0},{9,1},{12,4},{13,5},{2,10},{3,11},... | collective-permute-start | bytes 3080 | tf_op jit(solution)/shard_map/ppermute | solution.py:176
  36.8 3.9 %collective-permute-start.9 = (f32[1,256]{1,0:T(1,128)S(1)}, f32[1,256]{1,0:T(1,128)S(1)}, u32[]{:S(2)}, u32[]{:S(2)}) collective-permute-start(f32[1,256]{1,0:T(1,128)S(1)} %get-tuple-element.35), channel_id=1, source_target_pairs={{0,9},{1,8},{4,13},{5,12},{8,1},{9,0},{12,5},{13,4},{2,11},{3,10},... | collective-permute-start | bytes 3080 | tf_op jit(solution)/shard_map/ppermute | solution.py:176
  41.1 5.4 %collective-permute-start.11 = (f32[1,256]{1,0:T(1,128)S(1)}, f32[1,256]{1,0:T(1,128)S(1)}, u32[]{:S(2)}, u32[]{:S(2)}) collective-permute-start(f32[1,256]{1,0:T(1,128)S(1)} %shard_map.118), channel_id=1, source_target_pairs={{0,12},{1,13},{4,8},{5,9},{8,4},{9,5},{12,0},{13,1},{2,14},{3,15},... | collective-permute-start | bytes 3080 | tf_op jit(solution)/shard_map/ppermute | solution.py:176
  43.4 4.9 %collective-permute-start.13 = (f32[1,256]{1,0:T(1,128)S(1)}, f32[1,256]{1,0:T(1,128)S(1)}, u32[]{:S(2)}, u32[]{:S(2)}) collective-permute-start(f32[1,256]{1,0:T(1,128)S(1)} %shard_map.119), channel_id=1, source_target_pairs={{0,13},{1,12},{4,9},{5,8},{8,5},{9,4},{12,1},{13,0},{2,15},{3,14},... | collective-permute-start | bytes 3080 | tf_op jit(solution)/shard_map/ppermute | solution.py:176
  49.1 3.7 %collective-permute-start.14 = (f32[1,1024]{1,0:T(1,128)S(1)}, f32[1,1024]{1,0:T(1,128)S(1)}, u32[]{:S(2)}, u32[]{:S(2)}) collective-permute-start(f32[1,1024]{1,0:T(1,128)S(1)} %shard_map.120.refs_7_), channel_id=1, source_target_pairs={{0,2},{2,0},{1,3},{3,1},{4,6},{6,4},{5,7},{7,5},{8,10},{10,8},{9,1... | collective-permute-start | bytes 12296 | tf_op jit(solution)/shard_map/ppermute | solution.py:176

commit v7 on v5

--- a/solution.py
+++ b/solution.py
@@ -63,8 +63,9 @@
 
 
 def far_kernel(owners, capacity, far, where, *refs):
-    sources, ranks, place_out, ids_out = refs[:5], refs[5], refs[6], refs[7]
-    chunks, copies, sems = refs[8 : 8 + len(far)], refs[8 + len(far) : 13 + len(far)], refs[13 + len(far)]
+    sources, ranks, place_out, ids_out, feats = refs[:5], refs[5], refs[6], refs[7], refs[8]
+    chunks, copies, sems = refs[9 : 9 + len(far)], refs[9 + len(far) : 13 + len(far)], refs[13 + len(far)]
+    copies = (*copies, feats)
     moves = [pltpu.make_async_copy(sources[i], copies[i], sems.at[i]) for i in range(5)]
     for move in moves:
         move.start()
@@ -85,15 +86,16 @@
     ids_out[...] = ids
     moves[4].wait()
     for chunk, k in zip(chunks, far):
-        pack_chunk(k, capacity, place, ids, copies[4][...], chunk)
-
-
-def near_kernel(capacity, near, margin, place, ids, feats, *chunks):
-    for chunk, k in zip(chunks, near):
+        pack_chunk(k, capacity, place, ids, feats[...], chunk)
+
+
+def rest_kernel(capacity, rest, place, ids, feats, *refs):
+    chunks = refs[-len(rest) :]
+    for chunk, k in zip(chunks, rest):
         pack_chunk(k, capacity, place[...], ids[...], feats[...], chunk)
 
 
-def margin_kernel(rank, weight, features, margin, copies, sems):
+def margin_kernel(place, weight, features, margin, copies, sems):
     parts = copies.shape[0]
     step = copies.shape[1]
     moves = [
@@ -112,17 +114,26 @@
     return (pair[0:1] * 256.0 + pair[1:2]).astype(jnp.int32)
 
 
-def scores_kernel(order, capacity, n_feat, n_ent, where, margin, coefs, *refs):
-    chunks, out = refs[:-1], refs[-1]
-    entities = coefs.shape[0]
-    mine = where[0]
-    high, low = halves(coefs[...])
-    scores = []
-    for chunk in chunks:
-        feats = chunk[:capacity]
-        every = lanes_dot(high, feats) + lanes_dot(low, feats)
-        hits = one_hot(chunk_ids(chunk, capacity), entities)
-        scores.append(jnp.sum(jnp.where(hits, every, 0.0), axis=0, keepdims=True))
+def chunk_scores(chunk, table, capacity):
+    feats = chunk[:capacity]
+    every = lanes_dot(table, jnp.concatenate([feats, feats], axis=1))
+    hits = one_hot(chunk_ids(chunk, capacity), table.shape[0])
+    return jnp.sum(jnp.where(hits, every, 0.0), axis=0, keepdims=True)
+
+
+def early_kernel(capacity, coefs, *refs):
+    half = len(refs) // 2
+    table = jnp.concatenate(halves(coefs[...]), axis=1)
+    for chunk, out in zip(refs[:half], refs[half:]):
+        out[...] = chunk_scores(chunk, table, capacity)
+
+
+def scores_kernel(order, capacity, n_feat, n_ent, where, coefs, *refs):
+    out, mine = refs[-1], where[0]
+    table = jnp.concatenate(halves(coefs[...]), axis=1)
+    scores = [
+        x[...] if x.shape[0] == 1 else chunk_scores(x, table, capacity) for x in refs[:-1]
+    ]
     for k, score in zip(order, scores):
         home = mine ^ k
         for f in range(n_feat):
@@ -166,13 +177,15 @@
     for h in range(1, len(order)):
         summed = summed + came[h][:, capacity:]
     grad_global[...] = summed * scale + 4.0 * weight[...]
-    total = coefs[...]
+    highs, lows, feats = [], [], []
     for chunk, resid in zip(chunks, resids):
         hits = one_hot(chunk_ids(chunk, capacity), entities)
-        feats = chunk[:capacity]
-        for part in halves(resid):
-            total = total + plain_dot(jnp.where(hits, part.astype(F32), 0.0).astype(BF16), feats)
-    grad_coefs[...] = total
+        high, low = halves(resid)
+        highs.append(jnp.where(hits, high.astype(F32), 0.0).astype(BF16))
+        lows.append(jnp.where(hits, low.astype(F32), 0.0).astype(BF16))
+        feats.append(chunk[:capacity])
+    spread = jnp.concatenate(highs + lows, axis=1)
+    grad_coefs[...] = coefs[...] + plain_dot(spread, jnp.concatenate(feats + feats, axis=0))
 
 
 def xor_send(x, axes, size, k):
@@ -221,18 +234,23 @@
         return lambda *refs: kernel(*args, *refs)
 
     row = pltpu.VMEM((1, rows_here), jnp.int32)
-    half = owners // 2
-    far, near = list(range(half, owners)), list(reversed(range(half)))
+    half, early = owners // 2, 3 * owners // 4
+    first, second, near = list(range(half, early)), list(range(early, owners)), list(reversed(range(half)))
     chunk = shape(capacity + IDS, width, dtype=BF16)
-    flops = owners * capacity * rows_here * width
+    flops = len(first) * 2 * capacity * rows_here * width
 
     def in_hbm(x):
         return pltpu.with_memory_space_constraint(x, pltpu.HBM)
 
-    ranks, place, ids, *far_chunks = call(
-        partial(far_kernel, owners, capacity, far),
-        [shape(2, rows_here, dtype=jnp.int32), shape(1, rows_here, dtype=jnp.int32), shape(IDS, rows_here, dtype=BF16)]
-        + [chunk] * len(far),
+    ranks, place, ids, feats, *chunks = call(
+        partial(far_kernel, owners, capacity, first),
+        [
+            shape(2, rows_here, dtype=jnp.int32),
+            shape(1, rows_here, dtype=jnp.int32),
+            shape(IDS, rows_here, dtype=BF16),
+            shape(rows_here, width, dtype=BF16),
+        ]
+        + [chunk] * len(first),
         (
             where,
             in_hbm(member),
@@ -243,12 +261,18 @@
         ),
         [SMEM] + [HBM] * 5,
         flops=flops,
-        scratch=[row, row, row, row, pltpu.VMEM((rows_here, width), BF16), pltpu.SemaphoreType.DMA((5,))],
-    )
-    order = far + near
-    chunks = [xor_send(x, HOME, owners, k) for k, x in zip(far, far_chunks)]
+        scratch=[row, row, row, row, pltpu.SemaphoreType.DMA((5,))],
+    )
+    chunks += call(
+        partial(rest_kernel, capacity, second),
+        [chunk] * len(second),
+        (place, ids, feats),
+        [VMEM] * 3,
+        flops=flops,
+    )
+    chunks = [xor_send(x, HOME, owners, k) for k, x in zip(first + second, chunks)]
     weight = global_weight.astype(F32).reshape(1, columns)
-    parts = 4
+    parts = 8
     (global_part,) = call(
         margin_kernel,
         [shape(1, rows_here)],
@@ -259,20 +283,29 @@
     )
     global_total = lax.psum(global_part, "feat")
     near_chunks = call(
-        partial(near_kernel, capacity, near),
+        partial(rest_kernel, capacity, near),
         [chunk] * len(near),
-        (global_total, place, ids, entity_feats),
+        (place, ids, feats, global_total),
         [VMEM] * 4,
         hidden=True,
     )
-    chunks += [xor_send(x, HOME, owners, k) for k, x in zip(near, near_chunks)]
-
+    near_chunks = [xor_send(x, HOME, owners, k) for k, x in zip(near, near_chunks)]
+    order = first + near[-1:] + second + near[:-1]
+    chunks = chunks[: len(first)] + near_chunks[-1:] + chunks[len(first) :] + near_chunks[:-1]
+    came_early = len(first) + 1
+    scores = call(
+        partial(early_kernel, capacity),
+        [shape(1, capacity)] * came_early,
+        (coefs, *chunks[:came_early]),
+        [VMEM] * (1 + came_early),
+        hidden=True,
+    )
     (scores,) = call(
         partial(scores_kernel, order, capacity, n_feat, n_ent),
         [shape(n_feat * owners, 1, capacity)],
-        (where, global_total, coefs, *chunks),
-        [SMEM] + [VMEM] * (2 + owners),
-        flops=4 * coefs.size * owners * capacity,
+        (where, coefs, *scores, *chunks[came_early:]),
+        [SMEM] + [VMEM] * (1 + owners),
+        flops=2 * coefs.size * owners * capacity,
     )
     returned = lax.all_to_all(scores, EVERY, split_axis=0, concat_axis=0, tiled=True)
     (sent,) = call(

time: 59.3 us -> 60.5 us (1.020)
  local copies, waits for them, and re-layouts: 0.03 us -> 2.2 us
  waiting for transfers between devices: 8.48 us -> 6.5 us
    unnamed x14 -> x12, local copies, waits for them, and re-layouts: 0.03 us -> 2.2 us
    ppermute x7, waiting for transfers between devices: 8.48 us -> 6.5 us  [xor_send(): lax.ppermute(x, axes, [(i, i ^ k) for i in range(size)])]
    pallas_call x6 -> x8, Pallas kernels: 14.3 us -> 14.9 us  [call(): pl.pallas_call(kernel, out_shape=out_shape, in_specs=in_specs, out_specs=...]
  transfers between devices with their start and end apart: 7 -> 7, of which waited for: 4 -> 4; matrix products, arithmetic and copies ran while one was open for 1% -> 1% of each run, Pallas kernels for 9% -> 11%
where the time goes in v7:
time: 60.5 us; the launch traced here: 60.2 us
  blocking collectives  25.4 us (42%)
  Pallas kernels  14.9 us (25%)
  starting transfers between devices  9.67 us (16%)
  waiting for transfers between devices  6.5 us (11%)
  local copies, waits for them, and re-layouts  2.2 us (4%)
  other arithmetic  0.76 us (1%)
  between operations  0.76 us (1%)
    pallas_call x8, Pallas kernels, call(): pl.pallas_call(kernel, out_shape=out_shape, in_specs=in_specs, out_specs=...  14.9 us
    all_to_all x1, blocking collectives, body(): lax.all_to_all(scores, EVERY, split_axis=0, concat_axis=0, tiled=True)  12.1 us
    ppermute x7, starting transfers between devices, xor_send(): lax.ppermute(x, axes, [(i, i ^ k) for i in range(size)])  9.67 us
    all_to_all x1, blocking collectives, body(): came = lax.all_to_all(sent, HOME, split_axis=0, concat_axis=0, tiled=True)  8.4 us
    ppermute x7, waiting for transfers between devices, xor_send(): lax.ppermute(x, axes, [(i, i ^ k) for i in range(size)])  6.5 us
    psum x1, blocking collectives, body(): global_total = lax.psum(global_part, 'feat')  4.95 us
    unnamed x12, local copies, waits for them, and re-layouts  2.2 us
  transfers between devices with their start and end apart: 7, of which 4 were waited for; matrix products, arithmetic and copies ran while one was open for 1% of the time, Pallas kernels for 11%

profile of v7, /device:TPU:0, one launch (start us, length us, event | category | flops | bytes accessed | tf_op | source)
XLA Modules:
  0.0 60.2 jit_solution(16971203542441886534)
XLA Ops:
  0.6 0.0 copy-start.1
  0.6 0.1 pad_add_fusion.refs_0_
  0.7 2.4 %shard_map.113 = (s32[2,1024]{1,0:T(2,128)S(1)}, s32[1,1024]{1,0:T(1,128)S(1)}, bf16[16,1024]{1,0:T(8,128)(2,1)S(1)}, bf16[1024,256]{1,0:T(8,128)(2,1)S(1)}, bf1...) custom-call(s32[2]{0:T(128)S(1)} %pad_add_fusion.refs_0_, s32[1,1024]{1,0:T(1,128)} %bitcast.12, ...), custom_call_target="tpu_custom_call" | custom-call | flops 268435456 | bytes 1388552 | tf_op jit(solution)/shard_map/pallas_call | solution.py:197
  3.1 4.1 %collective-permute-start = (bf16[272,256]{1,0:T(8,128)(2,1)S(1)}, bf16[272,256]{1,0:T(8,128)(2,1)S(1)}, u32[]{:S(2)}, u32[]{:S(2)}) collective-permute-start(bf16[272,256]{1,0:T(8,128)(2,1)S(1)} %get-tuple-element.21), channel_id=1, source_target_pairs={{0,8},{1,9},{4,12},{5,13},{8,0},{9,1},{12,4},{13,5},{2,10},{3,11},... | collective-permute-start | bytes 417800 | tf_op jit(solution)/shard_map/ppermute | solution.py:192
  7.2 0.0 collective-permute-start.1
  7.2 0.0 copy-start.2
  7.2 0.0 copy-start.3
  7.2 0.0 copy-start.4
  7.2 0.0 copy-start.5
  7.2 0.7 %shard_map.117 = (bf16[272,256]{1,0:T(8,128)(2,1)S(1)}, bf16[272,256]{1,0:T(8,128)(2,1)S(1)}) custom-call(s32[1,1024]{1,0:T(1,128)S(1)} %get-tuple-element.20.place.refs_0_, bf16[16,1024]{1,0:T(8,128)(2,1)S(1)} %get-tuple-element.23.refs_1_, bf16[1024,256]{1,0:T(8,128)(2,1)S(1)} %get-tuple-element.24.refs_2_), custom_call_target="tpu_custom_call" | custom-call | flops 268435456 | bytes 839680 | tf_op jit(solution)/shard_map/pallas_call | solution.py:197
  7.9 3.1 %collective-permute-start.2 = (bf16[272,256]{1,0:T(8,128)(2,1)S(1)}, bf16[272,256]{1,0:T(8,128)(2,1)S(1)}, u32[]{:S(2)}, u32[]{:S(2)}) collective-permute-start(bf16[272,256]{1,0:T(8,128)(2,1)S(1)} %get-tuple-element.29), channel_id=1, source_target_pairs={{0,12},{1,13},{4,8},{5,9},{8,4},{9,5},{12,0},{13,1},{2,14},{3,15},... | collective-permute-start | bytes 417800 | tf_op jit(solution)/shard_map/ppermute | solution.py:192
  11.1 0.6 %collective-permute-start.3 = (bf16[272,256]{1,0:T(8,128)(2,1)S(1)}, bf16[272,256]{1,0:T(8,128)(2,1)S(1)}, u32[]{:S(2)}, u32[]{:S(2)}) collective-permute-start(bf16[272,256]{1,0:T(8,128)(2,1)S(1)} %get-tuple-element.30), channel_id=1, source_target_pairs={{0,13},{1,12},{4,9},{5,8},{8,5},{9,4},{12,1},{13,0},{2,15},{3,14},... | collective-permute-start | bytes 417800 | tf_op jit(solution)/shard_map/ppermute | solution.py:192
  11.7 0.7 %reshape.40 = f32[2048]{0:T(1024)S(1)} convert(bf16[2048]{0:T(1024)(128)(2,1)} %param.11) | non-fusion elementwise | flops 2048 | bytes 12288 | tf_op jit(solution)/shard_map/reshape | solution.py:274
  12.4 4.2 %shard_map.114 = f32[1,1024]{1,0:T(1,128)S(1)} custom-call(s32[1,1024]{1,0:T(1,128)S(1)} %get-tuple-element.20.place.refs_0_, f32[1,2048]{1,0:T(1,128)S(1)} %bitcast.10, bf16[1024,2048]{1,0:T(8,128)(2,1)} %refs_8_.1), custom_call_target="tpu_custom_call" | custom-call | tf_op jit(solution)/shard_map/pallas_call | solution.py:197
  16.6 4.9 %psum.7.refs_3_.refs_6_ = f32[1,1024]{1,0:T(1,128)S(1)} all-reduce(f32[1,1024]{1,0:T(1,128)S(1)} %shard_map.114), channel_id=1, replica_groups=mesh['groups'=2,'rows'=4,'feat'=2,'ent'=2] {'feat'}, use_global_device_ids=true, to_apply=%region_0.0 | all-reduce | flops 1024 | bytes 8192 | tf_op jit(solution)/shard_map/psum | solution.py:284
  21.6 1.2 %shard_map.115 = (bf16[272,256]{1,0:T(8,128)(2,1)S(1)}, bf16[272,256]{1,0:T(8,128)(2,1)S(1)}, bf16[272,256]{1,0:T(8,128)(2,1)S(1)}, bf16[272,256]{1,0:T(8,128)(2,1)S(1)}) custom-call(s32[1,1024]{1,0:T(1,128)S(1)} %get-tuple-element.20.place.refs_0_, bf16[16,1024]{1,0:T(8,128)(2,1)S(1)} %get-tuple-element.23.refs_1_, ...), custom_call_target="tpu_custom_call" | custom-call | tf_op jit(solution)/shard_map/pallas_call | solution.py:197
  22.8 0.1 collective-permute-start.4
  22.9 0.8 %collective-permute-done.refs_1_.refs_4_ = bf16[272,256]{1,0:T(8,128)(2,1)S(1)} collective-permute-done((bf16[272,256]{1,0:T(8,128)(2,1)S(1)}, bf16[272,256]{1,0:T(8,128)(2,1)S(1)}, u32[]{:S(2)}, u32[]{:S(2)}) %collective-permute-start) | collective-permute-done | bytes 139296 | tf_op jit(solution)/shard_map/ppermute | solution.py:192
  23.7 0.2 collective-permute-start.5
  23.9 1.1 %collective-permute-done.1.refs_2_.refs_5_ = bf16[272,256]{1,0:T(8,128)(2,1)S(1)} collective-permute-done((bf16[272,256]{1,0:T(8,128)(2,1)S(1)}, bf16[272,256]{1,0:T(8,128)(2,1)S(1)}, u32[]{:S(2)}, u32[]{:S(2)}) %collective-permute-start.1) | collective-permute-done | bytes 139296 | tf_op jit(solution)/shard_map/ppermute | solution.py:192
  25.0 1.5 %collective-permute-start.6 = (bf16[272,256]{1,0:T(8,128)(2,1)S(1)}, bf16[272,256]{1,0:T(8,128)(2,1)S(1)}, u32[]{:S(2)}, u32[]{:S(2)}) collective-permute-start(bf16[272,256]{1,0:T(8,128)(2,1)S(1)} %get-tuple-element.33), channel_id=1, source_target_pairs={{0,1},{1,0},{4,5},{5,4},{8,9},{9,8},{12,13},{13,12},{2,3},{3,2},{6... | collective-permute-start | bytes 417800 | tf_op jit(solution)/shard_map/ppermute | solution.py:192
  26.5 0.0 copy-done.1
  26.5 0.6 %shard_map.116 = (f32[1,256]{1,0:T(1,128)S(1)}, f32[1,256]{1,0:T(1,128)S(1)}, f32[1,256]{1,0:T(1,128)S(1)}) custom-call(f32[512,256]{1,0:T(8,128)S(1)} %copy-done.1, bf16[272,256]{1,0:T(8,128)(2,1)S(1)} %collective-permute-done.refs_1_.refs_4_, bf16[272,256]{1,0:T(8,128)(2,1)S(1)} %collective-permute-done.1.refs_2_.refs_5_, ...), custom_call_target="tpu_custom_call" | custom-call | tf_op jit(solution)/shard_map/pallas_call | solution.py:197
  27.1 0.0 collective-permute-done.2.refs_5_.refs_7_
  27.1 0.0 collective-permute-done.3.refs_6_.refs_8_
  27.1 2.1 %collective-permute-done.4.refs_7_.refs_9_ = bf16[272,256]{1,0:T(8,128)(2,1)S(1)} collective-permute-done((bf16[272,256]{1,0:T(8,128)(2,1)S(1)}, bf16[272,256]{1,0:T(8,128)(2,1)S(1)}, u32[]{:S(2)}, u32[]{:S(2)}) %collective-permute-start.4) | collective-permute-done | bytes 139296 | tf_op jit(solution)/shard_map/ppermute | solution.py:192
  29.2 2.5 %collective-permute-done.5.refs_8_.refs_10_ = bf16[272,256]{1,0:T(8,128)(2,1)S(1)} collective-permute-done((bf16[272,256]{1,0:T(8,128)(2,1)S(1)}, bf16[272,256]{1,0:T(8,128)(2,1)S(1)}, u32[]{:S(2)}, u32[]{:S(2)}) %collective-permute-start.5) | collective-permute-done | bytes 139296 | tf_op jit(solution)/shard_map/ppermute | solution.py:192
  31.8 0.0 collective-permute-done.6.refs_9_.refs_11_
  31.8 1.4 %shard_map.118 = f32[16,1,256]{2,1,0:T(1,128)S(1)} custom-call(s32[2]{0:T(128)S(1)} %pad_add_fusion.refs_0_, f32[512,256]{1,0:T(8,128)S(1)} %copy-done.1, f32[1,256]{1,0:T(1,128)S(1)} %get-tuple-element.26.refs_2_, f32[1,256]{1,0:T(1,128)S(1)} %get-tuple-element.27.refs_3_, f32[1,256]{1,0:T(1,128)S(1)} %get-tuple-element.28.refs_4_, ...), custom_call_target="tpu_custom_call" | custom-call | flops 536870912 | bytes 1240072 | tf_op jit(solution)/shard_map/pallas_call | solution.py:197
  33.2 12.1 %all_to_all.10.refs_7_ = f32[16,1,256]{2,1,0:T(1,128)S(1)} all-to-all(f32[16,1,256]{2,1,0:T(1,128)S(1)} %shard_map.118), channel_id=1, replica_groups=mesh['groups'=2,'rows'=4,'feat'=2,'ent'=2] {'rows','feat','ent'}, dimensions={0} | all-to-all | bytes 32768 | tf_op jit(solution)/shard_map/all_to_all | solution.py:310
  45.3 0.0 copy-done.2
  45.3 0.0 copy-done.3
  45.3 0.0 copy-done.4
  45.3 0.0 copy-done.5
  45.3 0.0 copy-start
  45.3 2.2 %copy-done = bf16[1024,2048]{1,0:T(8,128)(2,1)S(1)} copy-done((bf16[1024,2048]{1,0:T(8,128)(2,1)S(1)}, bf16[1024,2048]{1,0:T(8,128)(2,1)}, u32[]{:S(2)}) %copy-start) | copy-done | bytes 4194328
  47.5 1.7 %shard_map.119 = f32[8,1,2304]{2,1,0:T(1,128)S(1)} custom-call(s32[2]{0:T(128)S(1)} %pad_add_fusion.refs_0_, s32[1,1024]{1,0:T(1,128)S(1)} %bitcast.13, s32[1,1024]{1,0:T(1,128)S(1)} %bitcast.15, s32[2,1024]{1,0:T(2,128)S(1)} %get-tuple-element.19.refs_3_, s32[1,1024]{1,0:T(1,128)S(1)} %bitcast.16, s32[1,1024]{1,0:T(1,128)S(1)} %bitcast.17, ...), custom_call_target="tpu_custom_call" | custom-call | flops 67108864 | bytes 4313096 | tf_op jit(solution)/shard_map/pallas_call | solution.py:197
  49.2 8.4 %all_to_all.11.refs_3_ = f32[8,1,2304]{2,1,0:T(1,128)S(1)} all-to-all(f32[8,1,2304]{2,1,0:T(1,128)S(1)} %shard_map.119), channel_id=1, replica_groups=mesh['groups'=2,'rows'=4,'feat'=2,'ent'=2] {'rows','ent'}, dimensions={0} | all-to-all | bytes 147456 | tf_op jit(solution)/shard_map/all_to_all | solution.py:328
  57.6 2.6 %shard_map.120 = (f32[1,2048]{1,0:T(1,128)}, f32[512,256]{1,0:T(8,128)}) custom-call(s32[2]{0:T(128)S(1)} %pad_add_fusion.refs_0_, f32[512,256]{1,0:T(8,128)S(1)} %copy-done.1, f32[1,2048]{1,0:T(1,128)S(1)} %bitcast.11, f32[8,1,2304]{2,1,0:T(1,128)S(1)} %all_to_all.11.refs_3_, bf16[272,256]{1,0:T(8,128)(2,1)S(1)} %collective-permute-done.refs_1_.refs_4_, ...), custom_call_target="tpu_custom_call" | custom-call | flops 1073741824 | bytes 2252808 | tf_op jit(solution)/shard_map/pallas_call | solution.py:197
Async XLA Ops:
  0.6 25.8 %copy-start.1 = (f32[512,256]{1,0:T(8,128)S(1)}, f32[512,256]{1,0:T(8,128)}, u32[]{:S(2)}) copy-start(f32[512,256]{1,0:T(8,128)} %refs_1_.3) | copy-start | bytes 1572868
  3.1 20.5 %collective-permute-start = (bf16[272,256]{1,0:T(8,128)(2,1)S(1)}, bf16[272,256]{1,0:T(8,128)(2,1)S(1)}, u32[]{:S(2)}, u32[]{:S(2)}) collective-permute-start(bf16[272,256]{1,0:T(8,128)(2,1)S(1)} %get-tuple-element.21), channel_id=1, source_target_pairs={{0,8},{1,9},{4,12},{5,13},{8,0},{9,1},{12,4},{13,5},{2,10},{3,11},... | collective-permute-start | bytes 417800 | tf_op jit(solution)/shard_map/ppermute | solution.py:192
  7.2 17.8 %collective-permute-start.1 = (bf16[272,256]{1,0:T(8,128)(2,1)S(1)}, bf16[272,256]{1,0:T(8,128)(2,1)S(1)}, u32[]{:S(2)}, u32[]{:S(2)}) collective-permute-start(bf16[272,256]{1,0:T(8,128)(2,1)S(1)} %get-tuple-element.22), channel_id=1, source_target_pairs={{0,9},{1,8},{4,13},{5,12},{8,1},{9,0},{12,5},{13,4},{2,11},{3,10},... | collective-permute-start | bytes 417800 | tf_op jit(solution)/shard_map/ppermute | solution.py:192
  7.2 38.1 %copy-start.2 = (s32[1024,1]{0,1:T(1,128)S(1)}, s32[1024,1]{0,1:T(1,128)}, u32[]{:S(2)}) copy-start(s32[1024,1]{0,1:T(1,128)} %param.14) | copy-start | bytes 12292
  7.2 38.1 %copy-start.3 = (s32[1024,1]{0,1:T(1,128)S(1)}, s32[1024,1]{0,1:T(1,128)}, u32[]{:S(2)}) copy-start(s32[1024,1]{0,1:T(1,128)} %param.16) | copy-start | bytes 12292
  7.2 38.1 %copy-start.4 = (s32[1024]{0:T(1024)S(1)}, s32[1024]{0:T(1024)}, u32[]{:S(2)}) copy-start(s32[1024]{0:T(1024)} %param.18) | copy-start | bytes 12292
  7.2 38.1 %copy-start.5 = (s32[1024]{0:T(1024)S(1)}, s32[1024]{0:T(1024)}, u32[]{:S(2)}) copy-start(s32[1024]{0:T(1024)} %param.19) | copy-start | bytes 12292
  7.9 19.2 %collective-permute-start.2 = (bf16[272,256]{1,0:T(8,128)(2,1)S(1)}, bf16[272,256]{1,0:T(8,128)(2,1)S(1)}, u32[]{:S(2)}, u32[]{:S(2)}) collective-permute-start(bf16[272,256]{1,0:T(8,128)(2,1)S(1)} %get-tuple-element.29), channel_id=1, source_target_pairs={{0,12},{1,13},{4,8},{5,9},{8,4},{9,5},{12,0},{13,1},{2,14},{3,15},... | collective-permute-start | bytes 417800 | tf_op jit(solution)/shard_map/ppermute | solution.py:192
  11.1 16.0 %collective-permute-start.3 = (bf16[272,256]{1,0:T(8,128)(2,1)S(1)}, bf16[272,256]{1,0:T(8,128)(2,1)S(1)}, u32[]{:S(2)}, u32[]{:S(2)}) collective-permute-start(bf16[272,256]{1,0:T(8,128)(2,1)S(1)} %get-tuple-element.30), channel_id=1, source_target_pairs={{0,13},{1,12},{4,9},{5,8},{8,5},{9,4},{12,1},{13,0},{2,15},{3,14},... | collective-permute-start | bytes 417800 | tf_op jit(solution)/shard_map/ppermute | solution.py:192
  22.8 6.4 %collective-permute-start.4 = (bf16[272,256]{1,0:T(8,128)(2,1)S(1)}, bf16[272,256]{1,0:T(8,128)(2,1)S(1)}, u32[]{:S(2)}, u32[]{:S(2)}) collective-permute-start(bf16[272,256]{1,0:T(8,128)(2,1)S(1)} %get-tuple-element.31), channel_id=1, source_target_pairs={{0,5},{1,4},{4,1},{5,0},{8,13},{9,12},{12,9},{13,8},{2,7},{3,6},{6... | collective-permute-start | bytes 417800 | tf_op jit(solution)/shard_map/ppermute | solution.py:192
  23.7 8.1 %collective-permute-start.5 = (bf16[272,256]{1,0:T(8,128)(2,1)S(1)}, bf16[272,256]{1,0:T(8,128)(2,1)S(1)}, u32[]{:S(2)}, u32[]{:S(2)}) collective-permute-start(bf16[272,256]{1,0:T(8,128)(2,1)S(1)} %get-tuple-element.32), channel_id=1, source_target_pairs={{0,4},{1,5},{4,0},{5,1},{8,12},{9,13},{12,8},{13,9},{2,6},{3,7},{6... | collective-permute-start | bytes 417800 | tf_op jit(solution)/shard_map/ppermute | solution.py:192
  25.0 6.8 %collective-permute-start.6 = (bf16[272,256]{1,0:T(8,128)(2,1)S(1)}, bf16[272,256]{1,0:T(8,128)(2,1)S(1)}, u32[]{:S(2)}, u32[]{:S(2)}) collective-permute-start(bf16[272,256]{1,0:T(8,128)(2,1)S(1)} %get-tuple-element.33), channel_id=1, source_target_pairs={{0,1},{1,0},{4,5},{5,4},{8,9},{9,8},{12,13},{13,12},{2,3},{3,2},{6... | collective-permute-start | bytes 417800 | tf_op jit(solution)/shard_map/ppermute | solution.py:192
  45.3 2.2 %copy-start = (bf16[1024,2048]{1,0:T(8,128)(2,1)S(1)}, bf16[1024,2048]{1,0:T(8,128)(2,1)}, u32[]{:S(2)}) copy-start(bf16[1024,2048]{1,0:T(8,128)(2,1)} %refs_8_.1) | copy-start | bytes 12582916

commit v8 on v7

--- a/solution.py
+++ b/solution.py
@@ -95,18 +95,19 @@
         pack_chunk(k, capacity, place[...], ids[...], feats[...], chunk)
 
 
-def margin_kernel(place, weight, features, margin, copies, sems):
-    parts = copies.shape[0]
-    step = copies.shape[1]
+def margin_kernel(parts, place, weight, features, margin, kept, sems):
+    step = kept.shape[0] // parts
     moves = [
-        pltpu.make_async_copy(features.at[pl.ds(i * step, step)], copies.at[i], sems.at[i]) for i in range(parts)
+        pltpu.make_async_copy(features.at[pl.ds(i * step, step)], kept.at[pl.ds(i * step, step)], sems.at[i])
+        for i in range(parts)
     ]
     for move in moves:
         move.start()
     wide = jnp.broadcast_to(weight[...], (16, weight.shape[1])).astype(BF16)
     for i in range(parts):
         moves[i].wait()
-        margin[:, i * step : (i + 1) * step] = lanes_dot(wide, copies[i])[0:1]
+        here = slice(i * step, (i + 1) * step)
+        margin[:, here] = lanes_dot(wide, kept[here])[0:1]
 
 
 def chunk_ids(chunk, capacity):
@@ -115,22 +116,22 @@
 
 
 def chunk_scores(chunk, table, capacity):
-    feats = chunk[:capacity]
-    every = lanes_dot(table, jnp.concatenate([feats, feats], axis=1))
-    hits = one_hot(chunk_ids(chunk, capacity), table.shape[0])
-    return jnp.sum(jnp.where(hits, every, 0.0), axis=0, keepdims=True)
+    entities = table.shape[0] // 2
+    every = lanes_dot(table, chunk[:capacity])
+    hits = one_hot(chunk_ids(chunk, capacity), entities)
+    return jnp.sum(jnp.where(hits, every[:entities] + every[entities:], 0.0), axis=0, keepdims=True)
 
 
 def early_kernel(capacity, coefs, *refs):
     half = len(refs) // 2
-    table = jnp.concatenate(halves(coefs[...]), axis=1)
+    table = jnp.concatenate(halves(coefs[...]), axis=0)
     for chunk, out in zip(refs[:half], refs[half:]):
         out[...] = chunk_scores(chunk, table, capacity)
 
 
 def scores_kernel(order, capacity, n_feat, n_ent, where, coefs, *refs):
     out, mine = refs[-1], where[0]
-    table = jnp.concatenate(halves(coefs[...]), axis=1)
+    table = jnp.concatenate(halves(coefs[...]), axis=0)
     scores = [
         x[...] if x.shape[0] == 1 else chunk_scores(x, table, capacity) for x in refs[:-1]
     ]
@@ -184,8 +185,9 @@
         highs.append(jnp.where(hits, high.astype(F32), 0.0).astype(BF16))
         lows.append(jnp.where(hits, low.astype(F32), 0.0).astype(BF16))
         feats.append(chunk[:capacity])
-    spread = jnp.concatenate(highs + lows, axis=1)
-    grad_coefs[...] = coefs[...] + plain_dot(spread, jnp.concatenate(feats + feats, axis=0))
+    spread = jnp.concatenate([jnp.concatenate(highs, axis=1), jnp.concatenate(lows, axis=1)], axis=0)
+    both = plain_dot(spread, jnp.concatenate(feats, axis=0))
+    grad_coefs[...] = coefs[...] + both[:entities] + both[entities:]
 
 
 def xor_send(x, axes, size, k):
@@ -272,14 +274,14 @@
     )
     chunks = [xor_send(x, HOME, owners, k) for k, x in zip(first + second, chunks)]
     weight = global_weight.astype(F32).reshape(1, columns)
-    parts = 8
-    (global_part,) = call(
-        margin_kernel,
-        [shape(1, rows_here)],
+    parts = 4
+    global_part, kept = call(
+        partial(margin_kernel, parts),
+        [shape(1, rows_here), shape(rows_here, columns, dtype=BF16)],
         (place, weight, in_hbm(features)),
         [VMEM, VMEM, HBM],
         hidden=True,
-        scratch=[pltpu.VMEM((parts, rows_here // parts, columns), BF16), pltpu.SemaphoreType.DMA((parts,))],
+        scratch=[pltpu.SemaphoreType.DMA((parts,))],
     )
     global_total = lax.psum(global_part, "feat")
     near_chunks = call(
@@ -320,7 +322,7 @@
             valid.reshape(1, rows_here),
             global_total,
             returned,
-            features,
+            kept,
         ),
         [SMEM] + [VMEM] * 8,
         flops=32 * features.size,

time: 60.5 us -> 60.8 us (level)
  local copies, waits for them, and re-layouts: 2.2 us -> 4.16 us
  waiting for transfers between devices: 6.5 us -> 5.51 us
    unnamed x12 -> x14, local copies, waits for them, and re-layouts: 2.2 us -> 4.16 us
    ppermute x7, waiting for transfers between devices: 6.5 us -> 5.51 us  [xor_send(): lax.ppermute(x, axes, [(i, i ^ k) for i in range(size)])]
  transfers between devices with their start and end apart: 7 -> 7, of which waited for: 4 -> 2; matrix products, arithmetic and copies ran while one was open for 1% -> 1% of each run, Pallas kernels for 11% -> 11%
where the time goes in v8:
time: 60.8 us; the launch traced here: 60.5 us
  blocking collectives  24.8 us (41%)
  Pallas kernels  14.6 us (24%)
  starting transfers between devices  9.9 us (16%)
  waiting for transfers between devices  5.51 us (9%)
  local copies, waits for them, and re-layouts  4.16 us (7%)
  between operations  0.77 us (1%)
  other arithmetic  0.76 us (1%)
    pallas_call x8, Pallas kernels, call(): pl.pallas_call(kernel, out_shape=out_shape, in_specs=in_specs, out_specs=...  14.6 us
    all_to_all x1, blocking collectives, body(): lax.all_to_all(scores, EVERY, split_axis=0, concat_axis=0, tiled=True)  11.5 us
    ppermute x7, starting transfers between devices, xor_send(): lax.ppermute(x, axes, [(i, i ^ k) for i in range(size)])  9.9 us
    all_to_all x1, blocking collectives, body(): came = lax.all_to_all(sent, HOME, split_axis=0, concat_axis=0, tiled=True)  8.4 us
    ppermute x7, waiting for transfers between devices, xor_send(): lax.ppermute(x, axes, [(i, i ^ k) for i in range(size)])  5.51 us
    psum x1, blocking collectives, body(): global_total = lax.psum(global_part, 'feat')  4.91 us
    unnamed x14, local copies, waits for them, and re-layouts  4.16 us
  transfers between devices with their start and end apart: 7, of which 2 were waited for; matrix products, arithmetic and copies ran while one was open for 1% of the time, Pallas kernels for 11%

profile of v8, /device:TPU:0, one launch (start us, length us, event | category | flops | bytes accessed | tf_op | source)
XLA Modules:
  0.0 60.5 jit_solution(18049947799934386751)
XLA Ops:
  0.6 0.0 copy-start.2
  0.6 0.1 pad_add_fusion.refs_0_
  0.7 2.4 %shard_map.113 = (s32[2,1024]{1,0:T(2,128)S(1)}, s32[1,1024]{1,0:T(1,128)S(1)}, bf16[16,1024]{1,0:T(8,128)(2,1)S(1)}, bf16[1024,256]{1,0:T(8,128)(2,1)S(1)}, bf1...) custom-call(s32[2]{0:T(128)S(1)} %pad_add_fusion.refs_0_, s32[1,1024]{1,0:T(1,128)} %bitcast.12, ...), custom_call_target="tpu_custom_call" | custom-call | flops 268435456 | bytes 1388552 | tf_op jit(solution)/shard_map/pallas_call | solution.py:199
  3.1 4.1 %collective-permute-start = (bf16[272,256]{1,0:T(8,128)(2,1)S(1)}, bf16[272,256]{1,0:T(8,128)(2,1)S(1)}, u32[]{:S(2)}, u32[]{:S(2)}) collective-permute-start(bf16[272,256]{1,0:T(8,128)(2,1)S(1)} %get-tuple-element.24), channel_id=1, source_target_pairs={{0,8},{1,9},{4,12},{5,13},{8,0},{9,1},{12,4},{13,5},{2,10},{3,11},... | collective-permute-start | bytes 417800 | tf_op jit(solution)/shard_map/ppermute | solution.py:194
  7.2 0.0 collective-permute-start.1
  7.2 0.0 copy-start.3
  7.2 0.0 copy-start.4
  7.2 0.0 copy-start.5
  7.2 0.0 copy-start.6
  7.2 0.7 %shard_map.117 = (bf16[272,256]{1,0:T(8,128)(2,1)S(1)}, bf16[272,256]{1,0:T(8,128)(2,1)S(1)}) custom-call(s32[1,1024]{1,0:T(1,128)S(1)} %get-tuple-element.22.refs_0_, bf16[16,1024]{1,0:T(8,128)(2,1)S(1)} %get-tuple-element.26.refs_1_, bf16[1024,256]{1,0:T(8,128)(2,1)S(1)} %get-tuple-element.27.refs_2_), custom_call_target="tpu_custom_call" | custom-call | flops 268435456 | bytes 839680 | tf_op jit(solution)/shard_map/pallas_call | solution.py:199
  7.9 3.1 %collective-permute-start.2 = (bf16[272,256]{1,0:T(8,128)(2,1)S(1)}, bf16[272,256]{1,0:T(8,128)(2,1)S(1)}, u32[]{:S(2)}, u32[]{:S(2)}) collective-permute-start(bf16[272,256]{1,0:T(8,128)(2,1)S(1)} %get-tuple-element.32), channel_id=1, source_target_pairs={{0,12},{1,13},{4,8},{5,9},{8,4},{9,5},{12,0},{13,1},{2,14},{3,15},... | collective-permute-start | bytes 417800 | tf_op jit(solution)/shard_map/ppermute | solution.py:194
  11.1 0.6 %collective-permute-start.3 = (bf16[272,256]{1,0:T(8,128)(2,1)S(1)}, bf16[272,256]{1,0:T(8,128)(2,1)S(1)}, u32[]{:S(2)}, u32[]{:S(2)}) collective-permute-start(bf16[272,256]{1,0:T(8,128)(2,1)S(1)} %get-tuple-element.33), channel_id=1, source_target_pairs={{0,13},{1,12},{4,9},{5,8},{8,5},{9,4},{12,1},{13,0},{2,15},{3,14},... | collective-permute-start | bytes 417800 | tf_op jit(solution)/shard_map/ppermute | solution.py:194
  11.7 0.7 %reshape.40 = f32[2048]{0:T(1024)S(1)} convert(bf16[2048]{0:T(1024)(128)(2,1)} %param.11) | non-fusion elementwise | flops 2048 | bytes 12288 | tf_op jit(solution)/shard_map/reshape | solution.py:276
  12.4 3.9 %shard_map.114 = (f32[1,1024]{1,0:T(1,128)S(1)}, bf16[1024,2048]{1,0:T(8,128)(2,1)S(1)}) custom-call(s32[1,1024]{1,0:T(1,128)S(1)} %get-tuple-element.22.refs_0_, f32[1,2048]{1,0:T(1,128)S(1)} %bitcast.10, bf16[1024,2048]{1,0:T(8,128)(2,1)} %refs_2_.1), custom_call_target="tpu_custom_call" | custom-call | tf_op jit(solution)/shard_map/pallas_call | solution.py:199
  16.3 0.0 copy-start
  16.3 2.0 %copy-done = bf16[1024,2048]{1,0:T(8,128)(2,1)} copy-done((bf16[1024,2048]{1,0:T(8,128)(2,1)}, bf16[1024,2048]{1,0:T(8,128)(2,1)S(1)}, u32[]{:S(2)}) %copy-start) | copy-done | bytes 4194328
  18.3 4.9 %psum.7.refs_3_.refs_6_ = f32[1,1024]{1,0:T(1,128)S(1)} all-reduce(f32[1,1024]{1,0:T(1,128)S(1)} %get-tuple-element.23), channel_id=1, replica_groups=mesh['groups'=2,'rows'=4,'feat'=2,'ent'=2] {'feat'}, use_global_device_ids=true, to_apply=%region_0.0 | all-reduce | flops 1024 | bytes 8192 | tf_op jit(solution)/shard_map/psum | solution.py:286
  23.2 1.2 %shard_map.115 = (bf16[272,256]{1,0:T(8,128)(2,1)S(1)}, bf16[272,256]{1,0:T(8,128)(2,1)S(1)}, bf16[272,256]{1,0:T(8,128)(2,1)S(1)}, bf16[272,256]{1,0:T(8,128)(2,1)S(1)}) custom-call(s32[1,1024]{1,0:T(1,128)S(1)} %get-tuple-element.22.refs_0_, bf16[16,1024]{1,0:T(8,128)(2,1)S(1)} %get-tuple-element.26.refs_1_, ...), custom_call_target="tpu_custom_call" | custom-call | tf_op jit(solution)/shard_map/pallas_call | solution.py:199
  24.4 0.1 collective-permute-start.4
  24.5 0.0 collective-permute-done.refs_1_.refs_4_
  24.5 1.0 %collective-permute-start.5 = (bf16[272,256]{1,0:T(8,128)(2,1)S(1)}, bf16[272,256]{1,0:T(8,128)(2,1)S(1)}, u32[]{:S(2)}, u32[]{:S(2)}) collective-permute-start(bf16[272,256]{1,0:T(8,128)(2,1)S(1)} %get-tuple-element.35), channel_id=1, source_target_pairs={{0,4},{1,5},{4,0},{5,1},{8,12},{9,13},{12,8},{13,9},{2,6},{3,7},{6... | collective-permute-start | bytes 417800 | tf_op jit(solution)/shard_map/ppermute | solution.py:194
  25.5 0.0 collective-permute-done.1.refs_2_.refs_5_
  25.5 1.0 %collective-permute-start.6 = (bf16[272,256]{1,0:T(8,128)(2,1)S(1)}, bf16[272,256]{1,0:T(8,128)(2,1)S(1)}, u32[]{:S(2)}, u32[]{:S(2)}) collective-permute-start(bf16[272,256]{1,0:T(8,128)(2,1)S(1)} %get-tuple-element.36), channel_id=1, source_target_pairs={{0,1},{1,0},{4,5},{5,4},{8,9},{9,8},{12,13},{13,12},{2,3},{3,2},{6... | collective-permute-start | bytes 417800 | tf_op jit(solution)/shard_map/ppermute | solution.py:194
  26.5 0.0 copy-done.2
  26.5 0.6 %shard_map.116 = (f32[1,256]{1,0:T(1,128)S(1)}, f32[1,256]{1,0:T(1,128)S(1)}, f32[1,256]{1,0:T(1,128)S(1)}) custom-call(f32[512,256]{1,0:T(8,128)S(1)} %copy-done.2, bf16[272,256]{1,0:T(8,128)(2,1)S(1)} %collective-permute-done.refs_1_.refs_4_, bf16[272,256]{1,0:T(8,128)(2,1)S(1)} %collective-permute-done.1.refs_2_.refs_5_, ...), custom_call_target="tpu_custom_call" | custom-call | tf_op jit(solution)/shard_map/pallas_call | solution.py:199
  27.1 0.0 collective-permute-done.2.refs_5_.refs_7_
  27.1 0.0 collective-permute-done.3.refs_6_.refs_8_
  27.1 3.3 %collective-permute-done.4.refs_7_.refs_9_ = bf16[272,256]{1,0:T(8,128)(2,1)S(1)} collective-permute-done((bf16[272,256]{1,0:T(8,128)(2,1)S(1)}, bf16[272,256]{1,0:T(8,128)(2,1)S(1)}, u32[]{:S(2)}, u32[]{:S(2)}) %collective-permute-start.4) | collective-permute-done | bytes 139296 | tf_op jit(solution)/shard_map/ppermute | solution.py:194
  30.4 2.2 %collective-permute-done.5.refs_8_.refs_10_ = bf16[272,256]{1,0:T(8,128)(2,1)S(1)} collective-permute-done((bf16[272,256]{1,0:T(8,128)(2,1)S(1)}, bf16[272,256]{1,0:T(8,128)(2,1)S(1)}, u32[]{:S(2)}, u32[]{:S(2)}) %collective-permute-start.5) | collective-permute-done | bytes 139296 | tf_op jit(solution)/shard_map/ppermute | solution.py:194
  32.6 0.0 collective-permute-done.6.refs_9_.refs_11_
  32.6 1.4 %shard_map.118 = f32[16,1,256]{2,1,0:T(1,128)S(1)} custom-call(s32[2]{0:T(128)S(1)} %pad_add_fusion.refs_0_, f32[512,256]{1,0:T(8,128)S(1)} %copy-done.2, f32[1,256]{1,0:T(1,128)S(1)} %get-tuple-element.29.refs_2_, f32[1,256]{1,0:T(1,128)S(1)} %get-tuple-element.30.refs_3_, f32[1,256]{1,0:T(1,128)S(1)} %get-tuple-element.31.refs_4_, ...), custom_call_target="tpu_custom_call" | custom-call | flops 536870912 | bytes 1240072 | tf_op jit(solution)/shard_map/pallas_call | solution.py:199
  34.1 11.5 %all_to_all.10.refs_7_ = f32[16,1,256]{2,1,0:T(1,128)S(1)} all-to-all(f32[16,1,256]{2,1,0:T(1,128)S(1)} %shard_map.118), channel_id=1, replica_groups=mesh['groups'=2,'rows'=4,'feat'=2,'ent'=2] {'rows','feat','ent'}, dimensions={0} | all-to-all | bytes 32768 | tf_op jit(solution)/shard_map/all_to_all | solution.py:312
  45.6 0.0 copy-done.3
  45.6 0.0 copy-done.4
  45.6 0.0 copy-done.5
  45.6 0.0 copy-done.6
  45.6 0.0 copy-start.1
  45.6 2.2 %copy-done.1 = bf16[1024,2048]{1,0:T(8,128)(2,1)S(1)} copy-done((bf16[1024,2048]{1,0:T(8,128)(2,1)S(1)}, bf16[1024,2048]{1,0:T(8,128)(2,1)}, u32[]{:S(2)}) %copy-start.1) | copy-done | bytes 4194328
  47.8 1.7 %shard_map.119 = f32[8,1,2304]{2,1,0:T(1,128)S(1)} custom-call(s32[2]{0:T(128)S(1)} %pad_add_fusion.refs_0_, s32[1,1024]{1,0:T(1,128)S(1)} %bitcast.13, s32[1,1024]{1,0:T(1,128)S(1)} %bitcast.15, s32[2,1024]{1,0:T(2,128)S(1)} %get-tuple-element.21.refs_3_, s32[1,1024]{1,0:T(1,128)S(1)} %bitcast.16, s32[1,1024]{1,0:T(1,128)S(1)} %bitcast.17, ...), custom_call_target="tpu_custom_call" | custom-call | flops 67108864 | bytes 4313096 | tf_op jit(solution)/shard_map/pallas_call | solution.py:199
  49.5 8.4 %all_to_all.11.refs_3_ = f32[8,1,2304]{2,1,0:T(1,128)S(1)} all-to-all(f32[8,1,2304]{2,1,0:T(1,128)S(1)} %shard_map.119), channel_id=1, replica_groups=mesh['groups'=2,'rows'=4,'feat'=2,'ent'=2] {'rows','ent'}, dimensions={0} | all-to-all | bytes 147456 | tf_op jit(solution)/shard_map/all_to_all | solution.py:330
  57.9 2.6 %shard_map.120 = (f32[1,2048]{1,0:T(1,128)}, f32[512,256]{1,0:T(8,128)}) custom-call(s32[2]{0:T(128)S(1)} %pad_add_fusion.refs_0_, f32[512,256]{1,0:T(8,128)S(1)} %copy-done.2, f32[1,2048]{1,0:T(1,128)S(1)} %bitcast.11, f32[8,1,2304]{2,1,0:T(1,128)S(1)} %all_to_all.11.refs_3_, bf16[272,256]{1,0:T(8,128)(2,1)S(1)} %collective-permute-done.refs_1_.refs_4_, ...), custom_call_target="tpu_custom_call" | custom-call | flops 1073741824 | bytes 2252808 | tf_op jit(solution)/shard_map/pallas_call | solution.py:199
Async XLA Ops:
  0.6 25.8 %copy-start.2 = (f32[512,256]{1,0:T(8,128)S(1)}, f32[512,256]{1,0:T(8,128)}, u32[]{:S(2)}) copy-start(f32[512,256]{1,0:T(8,128)} %refs_1_.3) | copy-start | bytes 1572868
  3.1 21.4 %collective-permute-start = (bf16[272,256]{1,0:T(8,128)(2,1)S(1)}, bf16[272,256]{1,0:T(8,128)(2,1)S(1)}, u32[]{:S(2)}, u32[]{:S(2)}) collective-permute-start(bf16[272,256]{1,0:T(8,128)(2,1)S(1)} %get-tuple-element.24), channel_id=1, source_target_pairs={{0,8},{1,9},{4,12},{5,13},{8,0},{9,1},{12,4},{13,5},{2,10},{3,11},... | collective-permute-start | bytes 417800 | tf_op jit(solution)/shard_map/ppermute | solution.py:194
  7.2 18.3 %collective-permute-start.1 = (bf16[272,256]{1,0:T(8,128)(2,1)S(1)}, bf16[272,256]{1,0:T(8,128)(2,1)S(1)}, u32[]{:S(2)}, u32[]{:S(2)}) collective-permute-start(bf16[272,256]{1,0:T(8,128)(2,1)S(1)} %get-tuple-element.25), channel_id=1, source_target_pairs={{0,9},{1,8},{4,13},{5,12},{8,1},{9,0},{12,5},{13,4},{2,11},{3,10},... | collective-permute-start | bytes 417800 | tf_op jit(solution)/shard_map/ppermute | solution.py:194
  7.2 38.4 %copy-start.3 = (s32[1024,1]{0,1:T(1,128)S(1)}, s32[1024,1]{0,1:T(1,128)}, u32[]{:S(2)}) copy-start(s32[1024,1]{0,1:T(1,128)} %param.14) | copy-start | bytes 12292
  7.2 38.4 %copy-start.4 = (s32[1024,1]{0,1:T(1,128)S(1)}, s32[1024,1]{0,1:T(1,128)}, u32[]{:S(2)}) copy-start(s32[1024,1]{0,1:T(1,128)} %param.16) | copy-start | bytes 12292
  7.2 38.4 %copy-start.5 = (s32[1024]{0:T(1024)S(1)}, s32[1024]{0:T(1024)}, u32[]{:S(2)}) copy-start(s32[1024]{0:T(1024)} %param.18) | copy-start | bytes 12292
  7.2 38.4 %copy-start.6 = (s32[1024]{0:T(1024)S(1)}, s32[1024]{0:T(1024)}, u32[]{:S(2)}) copy-start(s32[1024]{0:T(1024)} %param.19) | copy-start | bytes 12292
  7.9 19.2 %collective-permute-start.2 = (bf16[272,256]{1,0:T(8,128)(2,1)S(1)}, bf16[272,256]{1,0:T(8,128)(2,1)S(1)}, u32[]{:S(2)}, u32[]{:S(2)}) collective-permute-start(bf16[272,256]{1,0:T(8,128)(2,1)S(1)} %get-tuple-element.32), channel_id=1, source_target_pairs={{0,12},{1,13},{4,8},{5,9},{8,4},{9,5},{12,0},{13,1},{2,14},{3,15},... | collective-permute-start | bytes 417800 | tf_op jit(solution)/shard_map/ppermute | solution.py:194
  11.1 16.0 %collective-permute-start.3 = (bf16[272,256]{1,0:T(8,128)(2,1)S(1)}, bf16[272,256]{1,0:T(8,128)(2,1)S(1)}, u32[]{:S(2)}, u32[]{:S(2)}) collective-permute-start(bf16[272,256]{1,0:T(8,128)(2,1)S(1)} %get-tuple-element.33), channel_id=1, source_target_pairs={{0,13},{1,12},{4,9},{5,8},{8,5},{9,4},{12,1},{13,0},{2,15},{3,14},... | collective-permute-start | bytes 417800 | tf_op jit(solution)/shard_map/ppermute | solution.py:194
  16.3 2.0 %copy-start = (bf16[1024,2048]{1,0:T(8,128)(2,1)}, bf16[1024,2048]{1,0:T(8,128)(2,1)S(1)}, u32[]{:S(2)}) copy-start(bf16[1024,2048]{1,0:T(8,128)(2,1)S(1)} %get-tuple-element.37.refs_8_) | copy-start | bytes 12582916
  24.4 6.0 %collective-permute-start.4 = (bf16[272,256]{1,0:T(8,128)(2,1)S(1)}, bf16[272,256]{1,0:T(8,128)(2,1)S(1)}, u32[]{:S(2)}, u32[]{:S(2)}) collective-permute-start(bf16[272,256]{1,0:T(8,128)(2,1)S(1)} %get-tuple-element.34), channel_id=1, source_target_pairs={{0,5},{1,4},{4,1},{5,0},{8,13},{9,12},{12,9},{13,8},{2,7},{3,6},{6... | collective-permute-start | bytes 417800 | tf_op jit(solution)/shard_map/ppermute | solution.py:194
  24.5 8.1 %collective-permute-start.5 = (bf16[272,256]{1,0:T(8,128)(2,1)S(1)}, bf16[272,256]{1,0:T(8,128)(2,1)S(1)}, u32[]{:S(2)}, u32[]{:S(2)}) collective-permute-start(bf16[272,256]{1,0:T(8,128)(2,1)S(1)} %get-tuple-element.35), channel_id=1, source_target_pairs={{0,4},{1,5},{4,0},{5,1},{8,12},{9,13},{12,8},{13,9},{2,6},{3,7},{6... | collective-permute-start | bytes 417800 | tf_op jit(solution)/shard_map/ppermute | solution.py:194
  25.5 7.1 %collective-permute-start.6 = (bf16[272,256]{1,0:T(8,128)(2,1)S(1)}, bf16[272,256]{1,0:T(8,128)(2,1)S(1)}, u32[]{:S(2)}, u32[]{:S(2)}) collective-permute-start(bf16[272,256]{1,0:T(8,128)(2,1)S(1)} %get-tuple-element.36), channel_id=1, source_target_pairs={{0,1},{1,0},{4,5},{5,4},{8,9},{9,8},{12,13},{13,12},{2,3},{3,2},{6... | collective-permute-start | bytes 417800 | tf_op jit(solution)/shard_map/ppermute | solution.py:194
  45.6 2.2 %copy-start.1 = (bf16[1024,2048]{1,0:T(8,128)(2,1)S(1)}, bf16[1024,2048]{1,0:T(8,128)(2,1)}, u32[]{:S(2)}) copy-start(bf16[1024,2048]{1,0:T(8,128)(2,1)} %copy-done) | copy-start | bytes 12582916

commit v9 on v7

--- a/solution.py
+++ b/solution.py
@@ -11,7 +11,7 @@
 BF16 = jnp.bfloat16
 HOME = ("rows", "ent")
 EVERY = ("rows", "feat", "ent")
-IDS = 16
+IDS = 8
 PARAMS = pltpu.CompilerParams(vmem_limit_bytes=24 * 2**20)
 SMEM = pl.BlockSpec(memory_space=pltpu.SMEM)
 VMEM = pl.BlockSpec(memory_space=pltpu.VMEM)
@@ -115,22 +115,22 @@
 
 
 def chunk_scores(chunk, table, capacity):
-    feats = chunk[:capacity]
-    every = lanes_dot(table, jnp.concatenate([feats, feats], axis=1))
-    hits = one_hot(chunk_ids(chunk, capacity), table.shape[0])
-    return jnp.sum(jnp.where(hits, every, 0.0), axis=0, keepdims=True)
+    entities = table.shape[0] // 2
+    every = lanes_dot(table, chunk[:capacity])
+    hits = one_hot(chunk_ids(chunk, capacity), entities)
+    return jnp.sum(jnp.where(hits, every[:entities] + every[entities:], 0.0), axis=0, keepdims=True)
 
 
 def early_kernel(capacity, coefs, *refs):
     half = len(refs) // 2
-    table = jnp.concatenate(halves(coefs[...]), axis=1)
+    table = jnp.concatenate(halves(coefs[...]), axis=0)
     for chunk, out in zip(refs[:half], refs[half:]):
         out[...] = chunk_scores(chunk, table, capacity)
 
 
 def scores_kernel(order, capacity, n_feat, n_ent, where, coefs, *refs):
     out, mine = refs[-1], where[0]
-    table = jnp.concatenate(halves(coefs[...]), axis=1)
+    table = jnp.concatenate(halves(coefs[...]), axis=0)
     scores = [
         x[...] if x.shape[0] == 1 else chunk_scores(x, table, capacity) for x in refs[:-1]
     ]
@@ -184,8 +184,9 @@
         highs.append(jnp.where(hits, high.astype(F32), 0.0).astype(BF16))
         lows.append(jnp.where(hits, low.astype(F32), 0.0).astype(BF16))
         feats.append(chunk[:capacity])
-    spread = jnp.concatenate(highs + lows, axis=1)
-    grad_coefs[...] = coefs[...] + plain_dot(spread, jnp.concatenate(feats + feats, axis=0))
+    spread = jnp.concatenate([jnp.concatenate(highs, axis=1), jnp.concatenate(lows, axis=1)], axis=0)
+    both = plain_dot(spread, jnp.concatenate(feats, axis=0))
+    grad_coefs[...] = coefs[...] + both[:entities] + both[entities:]
 
 
 def xor_send(x, axes, size, k):
@@ -272,7 +273,7 @@
     )
     chunks = [xor_send(x, HOME, owners, k) for k, x in zip(first + second, chunks)]
     weight = global_weight.astype(F32).reshape(1, columns)
-    parts = 8
+    parts = 4
     (global_part,) = call(
         margin_kernel,
         [shape(1, rows_here)],
@@ -305,7 +306,7 @@
         [shape(n_feat * owners, 1, capacity)],
         (where, coefs, *scores, *chunks[came_early:]),
         [SMEM] + [VMEM] * (1 + owners),
-        flops=2 * coefs.size * owners * capacity,
+        flops=16 * coefs.size * owners * capacity,
     )
     returned = lax.all_to_all(scores, EVERY, split_axis=0, concat_axis=0, tiled=True)
     (sent,) = call(

time: 60.5 us -> 57.5 us (0.950)
  local copies, waits for them, and re-layouts: 2.2 us -> 0.03 us
    unnamed x12, local copies, waits for them, and re-layouts: 2.2 us -> 0.03 us
where the time goes in v9:
time: 57.5 us; the launch traced here: 57.3 us
  blocking collectives  25.2 us (44%)
  Pallas kernels  14.6 us (25%)
  starting transfers between devices  9.78 us (17%)
  waiting for transfers between devices  6.13 us (11%)
  other arithmetic  0.76 us (1%)
  between operations  0.76 us (1%)
    pallas_call x8, Pallas kernels, call(): pl.pallas_call(kernel, out_shape=out_shape, in_specs=in_specs, out_specs=...  14.6 us
    all_to_all x1, blocking collectives, body(): lax.all_to_all(scores, EVERY, split_axis=0, concat_axis=0, tiled=True)  11.9 us
    ppermute x7, starting transfers between devices, xor_send(): lax.ppermute(x, axes, [(i, i ^ k) for i in range(size)])  9.78 us
    all_to_all x1, blocking collectives, body(): came = lax.all_to_all(sent, HOME, split_axis=0, concat_axis=0, tiled=True)  8.4 us
    ppermute x7, waiting for transfers between devices, xor_send(): lax.ppermute(x, axes, [(i, i ^ k) for i in range(size)])  6.13 us
    psum x1, blocking collectives, body(): global_total = lax.psum(global_part, 'feat')  4.95 us
  transfers between devices with their start and end apart: 7, of which 4 were waited for; matrix products, arithmetic and copies ran while one was open for 1% of the time, Pallas kernels for 11%

profile of v9, /device:TPU:0, one launch (start us, length us, event | category | flops | bytes accessed | tf_op | source)
XLA Modules:
  0.0 57.3 jit_solution(16033754292893784479)
XLA Ops:
  0.6 0.0 copy-start.1
  0.6 0.1 pad_add_fusion.refs_0_
  0.7 2.4 %shard_map.113 = (s32[2,1024]{1,0:T(2,128)S(1)}, s32[1,1024]{1,0:T(1,128)S(1)}, bf16[8,1024]{1,0:T(8,128)(2,1)S(1)}, bf16[1024,256]{1,0:T(8,128)(2,1)S(1)}, bf16...) custom-call(s32[2]{0:T(128)S(1)} %pad_add_fusion.refs_0_, s32[1,1024]{1,0:T(1,128)} %bitcast.12, ...), custom_call_target="tpu_custom_call" | custom-call | flops 268435456 | bytes 1363976 | tf_op jit(solution)/shard_map/pallas_call | solution.py:198
  3.1 4.1 %collective-permute-start = (bf16[264,256]{1,0:T(8,128)(2,1)S(1)}, bf16[264,256]{1,0:T(8,128)(2,1)S(1)}, u32[]{:S(2)}, u32[]{:S(2)}) collective-permute-start(bf16[264,256]{1,0:T(8,128)(2,1)S(1)} %get-tuple-element.21), channel_id=1, source_target_pairs={{0,8},{1,9},{4,12},{5,13},{8,0},{9,1},{12,4},{13,5},{2,10},{3,11},... | collective-permute-start | bytes 405512 | tf_op jit(solution)/shard_map/ppermute | solution.py:193
  7.2 0.0 collective-permute-start.1
  7.2 0.7 %shard_map.117 = (bf16[264,256]{1,0:T(8,128)(2,1)S(1)}, bf16[264,256]{1,0:T(8,128)(2,1)S(1)}) custom-call(s32[1,1024]{1,0:T(1,128)S(1)} %get-tuple-element.20.place.refs_0_, bf16[8,1024]{1,0:T(8,128)(2,1)S(1)} %get-tuple-element.23.refs_1_, bf16[1024,256]{1,0:T(8,128)(2,1)S(1)} %get-tuple-element.24.refs_2_), custom_call_target="tpu_custom_call" | custom-call | flops 268435456 | bytes 815104 | tf_op jit(solution)/shard_map/pallas_call | solution.py:198
  7.9 3.2 %collective-permute-start.2 = (bf16[264,256]{1,0:T(8,128)(2,1)S(1)}, bf16[264,256]{1,0:T(8,128)(2,1)S(1)}, u32[]{:S(2)}, u32[]{:S(2)}) collective-permute-start(bf16[264,256]{1,0:T(8,128)(2,1)S(1)} %get-tuple-element.29), channel_id=1, source_target_pairs={{0,12},{1,13},{4,8},{5,9},{8,4},{9,5},{12,0},{13,1},{2,14},{3,15},... | collective-permute-start | bytes 405512 | tf_op jit(solution)/shard_map/ppermute | solution.py:193
  11.1 0.6 %collective-permute-start.3 = (bf16[264,256]{1,0:T(8,128)(2,1)S(1)}, bf16[264,256]{1,0:T(8,128)(2,1)S(1)}, u32[]{:S(2)}, u32[]{:S(2)}) collective-permute-start(bf16[264,256]{1,0:T(8,128)(2,1)S(1)} %get-tuple-element.30), channel_id=1, source_target_pairs={{0,13},{1,12},{4,9},{5,8},{8,5},{9,4},{12,1},{13,0},{2,15},{3,14},... | collective-permute-start | bytes 405512 | tf_op jit(solution)/shard_map/ppermute | solution.py:193
  11.7 0.7 %reshape.40 = f32[2048]{0:T(1024)S(1)} convert(bf16[2048]{0:T(1024)(128)(2,1)} %param.11) | non-fusion elementwise | flops 2048 | bytes 12288 | tf_op jit(solution)/shard_map/reshape | solution.py:275
  12.4 3.9 %shard_map.114 = f32[1,1024]{1,0:T(1,128)S(1)} custom-call(s32[1,1024]{1,0:T(1,128)S(1)} %get-tuple-element.20.place.refs_0_, f32[1,2048]{1,0:T(1,128)S(1)} %bitcast.10, bf16[1024,2048]{1,0:T(8,128)(2,1)} %refs_8_.1), custom_call_target="tpu_custom_call" | custom-call | tf_op jit(solution)/shard_map/pallas_call | solution.py:198
  16.3 4.9 %psum.7.refs_3_.refs_6_ = f32[1,1024]{1,0:T(1,128)S(1)} all-reduce(f32[1,1024]{1,0:T(1,128)S(1)} %shard_map.114), channel_id=1, replica_groups=mesh['groups'=2,'rows'=4,'feat'=2,'ent'=2] {'feat'}, use_global_device_ids=true, to_apply=%region_0.0 | all-reduce | flops 1024 | bytes 8192 | tf_op jit(solution)/shard_map/psum | solution.py:285
  21.3 1.2 %shard_map.115 = (bf16[264,256]{1,0:T(8,128)(2,1)S(1)}, bf16[264,256]{1,0:T(8,128)(2,1)S(1)}, bf16[264,256]{1,0:T(8,128)(2,1)S(1)}, bf16[264,256]{1,0:T(8,128)(2,1)S(1)}) custom-call(s32[1,1024]{1,0:T(1,128)S(1)} %get-tuple-element.20.place.refs_0_, bf16[8,1024]{1,0:T(8,128)(2,1)S(1)} %get-tuple-element.23.refs_1_, ...), custom_call_target="tpu_custom_call" | custom-call | tf_op jit(solution)/shard_map/pallas_call | solution.py:198
  22.5 0.1 collective-permute-start.4
  22.6 0.6 %collective-permute-done.refs_1_.refs_4_ = bf16[264,256]{1,0:T(8,128)(2,1)S(1)} collective-permute-done((bf16[264,256]{1,0:T(8,128)(2,1)S(1)}, bf16[264,256]{1,0:T(8,128)(2,1)S(1)}, u32[]{:S(2)}, u32[]{:S(2)}) %collective-permute-start) | collective-permute-done | bytes 135200 | tf_op jit(solution)/shard_map/ppermute | solution.py:193
  23.2 0.3 collective-permute-start.5
  23.5 0.9 %collective-permute-done.1.refs_2_.refs_5_ = bf16[264,256]{1,0:T(8,128)(2,1)S(1)} collective-permute-done((bf16[264,256]{1,0:T(8,128)(2,1)S(1)}, bf16[264,256]{1,0:T(8,128)(2,1)S(1)}, u32[]{:S(2)}, u32[]{:S(2)}) %collective-permute-start.1) | collective-permute-done | bytes 135200 | tf_op jit(solution)/shard_map/ppermute | solution.py:193
  24.5 1.5 %collective-permute-start.6 = (bf16[264,256]{1,0:T(8,128)(2,1)S(1)}, bf16[264,256]{1,0:T(8,128)(2,1)S(1)}, u32[]{:S(2)}, u32[]{:S(2)}) collective-permute-start(bf16[264,256]{1,0:T(8,128)(2,1)S(1)} %get-tuple-element.33), channel_id=1, source_target_pairs={{0,1},{1,0},{4,5},{5,4},{8,9},{9,8},{12,13},{13,12},{2,3},{3,2},{6... | collective-permute-start | bytes 405512 | tf_op jit(solution)/shard_map/ppermute | solution.py:193
  25.9 0.0 copy-done.1
  25.9 0.6 %shard_map.116 = (f32[1,256]{1,0:T(1,128)S(1)}, f32[1,256]{1,0:T(1,128)S(1)}, f32[1,256]{1,0:T(1,128)S(1)}) custom-call(f32[512,256]{1,0:T(8,128)S(1)} %copy-done.1, bf16[264,256]{1,0:T(8,128)(2,1)S(1)} %collective-permute-done.refs_1_.refs_4_, bf16[264,256]{1,0:T(8,128)(2,1)S(1)} %collective-permute-done.1.refs_2_.refs_5_, ...), custom_call_target="tpu_custom_call" | custom-call | tf_op jit(solution)/shard_map/pallas_call | solution.py:198
  26.6 0.0 collective-permute-done.2.refs_5_.refs_7_
  26.6 0.0 collective-permute-done.3.refs_6_.refs_8_
  26.6 2.1 %collective-permute-done.4.refs_7_.refs_9_ = bf16[264,256]{1,0:T(8,128)(2,1)S(1)} collective-permute-done((bf16[264,256]{1,0:T(8,128)(2,1)S(1)}, bf16[264,256]{1,0:T(8,128)(2,1)S(1)}, u32[]{:S(2)}, u32[]{:S(2)}) %collective-permute-start.4) | collective-permute-done | bytes 135200 | tf_op jit(solution)/shard_map/ppermute | solution.py:193
  28.7 2.4 %collective-permute-done.5.refs_8_.refs_10_ = bf16[264,256]{1,0:T(8,128)(2,1)S(1)} collective-permute-done((bf16[264,256]{1,0:T(8,128)(2,1)S(1)}, bf16[264,256]{1,0:T(8,128)(2,1)S(1)}, u32[]{:S(2)}, u32[]{:S(2)}) %collective-permute-start.5) | collective-permute-done | bytes 135200 | tf_op jit(solution)/shard_map/ppermute | solution.py:193
  31.2 0.0 collective-permute-done.6.refs_9_.refs_11_
  31.2 0.0 copy-start
  31.2 0.0 copy-start.2
  31.2 0.0 copy-start.3
  31.2 0.0 copy-start.4
  31.2 0.0 copy-start.5
  31.2 1.4 %shard_map.118 = f32[16,1,256]{2,1,0:T(1,128)S(1)} custom-call(s32[2]{0:T(128)S(1)} %pad_add_fusion.refs_0_, f32[512,256]{1,0:T(8,128)S(1)} %copy-done.1, f32[1,256]{1,0:T(1,128)S(1)} %get-tuple-element.26.refs_2_, f32[1,256]{1,0:T(1,128)S(1)} %get-tuple-element.27.refs_3_, f32[1,256]{1,0:T(1,128)S(1)} %get-tuple-element.28.refs_4_, ...), custom_call_target="tpu_custom_call" | custom-call | flops 4294967296 | bytes 1219592 | tf_op jit(solution)/shard_map/pallas_call | solution.py:198
  32.6 11.9 %all_to_all.10.refs_7_ = f32[16,1,256]{2,1,0:T(1,128)S(1)} all-to-all(f32[16,1,256]{2,1,0:T(1,128)S(1)} %shard_map.118), channel_id=1, replica_groups=mesh['groups'=2,'rows'=4,'feat'=2,'ent'=2] {'rows','feat','ent'}, dimensions={0} | all-to-all | bytes 32768 | tf_op jit(solution)/shard_map/all_to_all | solution.py:311
  44.5 0.0 copy-done
  44.5 0.0 copy-done.2
  44.5 0.0 copy-done.3
  44.5 0.0 copy-done.4
  44.5 0.0 copy-done.5
  44.6 1.7 %shard_map.119 = f32[8,1,2304]{2,1,0:T(1,128)S(1)} custom-call(s32[2]{0:T(128)S(1)} %pad_add_fusion.refs_0_, s32[1,1024]{1,0:T(1,128)S(1)} %bitcast.13, s32[1,1024]{1,0:T(1,128)S(1)} %bitcast.15, s32[2,1024]{1,0:T(2,128)S(1)} %get-tuple-element.19.refs_3_, s32[1,1024]{1,0:T(1,128)S(1)} %bitcast.16, s32[1,1024]{1,0:T(1,128)S(1)} %bitcast.17, ...), custom_call_target="tpu_custom_call" | custom-call | flops 67108864 | bytes 4313096 | tf_op jit(solution)/shard_map/pallas_call | solution.py:198
  46.3 8.4 %all_to_all.11.refs_3_ = f32[8,1,2304]{2,1,0:T(1,128)S(1)} all-to-all(f32[8,1,2304]{2,1,0:T(1,128)S(1)} %shard_map.119), channel_id=1, replica_groups=mesh['groups'=2,'rows'=4,'feat'=2,'ent'=2] {'rows','ent'}, dimensions={0} | all-to-all | bytes 147456 | tf_op jit(solution)/shard_map/all_to_all | solution.py:329
  54.7 2.6 %shard_map.120 = (f32[1,2048]{1,0:T(1,128)}, f32[512,256]{1,0:T(8,128)}) custom-call(s32[2]{0:T(128)S(1)} %pad_add_fusion.refs_0_, f32[512,256]{1,0:T(8,128)S(1)} %copy-done.1, f32[1,2048]{1,0:T(1,128)S(1)} %bitcast.11, f32[8,1,2304]{2,1,0:T(1,128)S(1)} %all_to_all.11.refs_3_, bf16[264,256]{1,0:T(8,128)(2,1)S(1)} %collective-permute-done.refs_1_.refs_4_, ...), custom_call_target="tpu_custom_call" | custom-call | flops 1073741824 | bytes 2220040 | tf_op jit(solution)/shard_map/pallas_call | solution.py:198
Async XLA Ops:
  0.6 25.3 %copy-start.1 = (f32[512,256]{1,0:T(8,128)S(1)}, f32[512,256]{1,0:T(8,128)}, u32[]{:S(2)}) copy-start(f32[512,256]{1,0:T(8,128)} %refs_1_.3) | copy-start | bytes 1572868
  3.1 20.1 %collective-permute-start = (bf16[264,256]{1,0:T(8,128)(2,1)S(1)}, bf16[264,256]{1,0:T(8,128)(2,1)S(1)}, u32[]{:S(2)}, u32[]{:S(2)}) collective-permute-start(bf16[264,256]{1,0:T(8,128)(2,1)S(1)} %get-tuple-element.21), channel_id=1, source_target_pairs={{0,8},{1,9},{4,12},{5,13},{8,0},{9,1},{12,4},{13,5},{2,10},{3,11},... | collective-permute-start | bytes 405512 | tf_op jit(solution)/shard_map/ppermute | solution.py:193
  7.2 17.2 %collective-permute-start.1 = (bf16[264,256]{1,0:T(8,128)(2,1)S(1)}, bf16[264,256]{1,0:T(8,128)(2,1)S(1)}, u32[]{:S(2)}, u32[]{:S(2)}) collective-permute-start(bf16[264,256]{1,0:T(8,128)(2,1)S(1)} %get-tuple-element.22), channel_id=1, source_target_pairs={{0,9},{1,8},{4,13},{5,12},{8,1},{9,0},{12,5},{13,4},{2,11},{3,10},... | collective-permute-start | bytes 405512 | tf_op jit(solution)/shard_map/ppermute | solution.py:193
  7.9 18.7 %collective-permute-start.2 = (bf16[264,256]{1,0:T(8,128)(2,1)S(1)}, bf16[264,256]{1,0:T(8,128)(2,1)S(1)}, u32[]{:S(2)}, u32[]{:S(2)}) collective-permute-start(bf16[264,256]{1,0:T(8,128)(2,1)S(1)} %get-tuple-element.29), channel_id=1, source_target_pairs={{0,12},{1,13},{4,8},{5,9},{8,4},{9,5},{12,0},{13,1},{2,14},{3,15},... | collective-permute-start | bytes 405512 | tf_op jit(solution)/shard_map/ppermute | solution.py:193
  11.1 15.5 %collective-permute-start.3 = (bf16[264,256]{1,0:T(8,128)(2,1)S(1)}, bf16[264,256]{1,0:T(8,128)(2,1)S(1)}, u32[]{:S(2)}, u32[]{:S(2)}) collective-permute-start(bf16[264,256]{1,0:T(8,128)(2,1)S(1)} %get-tuple-element.30), channel_id=1, source_target_pairs={{0,13},{1,12},{4,9},{5,8},{8,5},{9,4},{12,1},{13,0},{2,15},{3,14},... | collective-permute-start | bytes 405512 | tf_op jit(solution)/shard_map/ppermute | solution.py:193
  22.5 6.2 %collective-permute-start.4 = (bf16[264,256]{1,0:T(8,128)(2,1)S(1)}, bf16[264,256]{1,0:T(8,128)(2,1)S(1)}, u32[]{:S(2)}, u32[]{:S(2)}) collective-permute-start(bf16[264,256]{1,0:T(8,128)(2,1)S(1)} %get-tuple-element.31), channel_id=1, source_target_pairs={{0,5},{1,4},{4,1},{5,0},{8,13},{9,12},{12,9},{13,8},{2,7},{3,6},{6... | collective-permute-start | bytes 405512 | tf_op jit(solution)/shard_map/ppermute | solution.py:193
  23.2 7.9 %collective-permute-start.5 = (bf16[264,256]{1,0:T(8,128)(2,1)S(1)}, bf16[264,256]{1,0:T(8,128)(2,1)S(1)}, u32[]{:S(2)}, u32[]{:S(2)}) collective-permute-start(bf16[264,256]{1,0:T(8,128)(2,1)S(1)} %get-tuple-element.32), channel_id=1, source_target_pairs={{0,4},{1,5},{4,0},{5,1},{8,12},{9,13},{12,8},{13,9},{2,6},{3,7},{6... | collective-permute-start | bytes 405512 | tf_op jit(solution)/shard_map/ppermute | solution.py:193
  24.5 6.7 %collective-permute-start.6 = (bf16[264,256]{1,0:T(8,128)(2,1)S(1)}, bf16[264,256]{1,0:T(8,128)(2,1)S(1)}, u32[]{:S(2)}, u32[]{:S(2)}) collective-permute-start(bf16[264,256]{1,0:T(8,128)(2,1)S(1)} %get-tuple-element.33), channel_id=1, source_target_pairs={{0,1},{1,0},{4,5},{5,4},{8,9},{9,8},{12,13},{13,12},{2,3},{3,2},{6... | collective-permute-start | bytes 405512 | tf_op jit(solution)/shard_map/ppermute | solution.py:193
  31.2 13.4 %copy-start = (bf16[1024,2048]{1,0:T(8,128)(2,1)S(1)}, bf16[1024,2048]{1,0:T(8,128)(2,1)}, u32[]{:S(2)}) copy-start(bf16[1024,2048]{1,0:T(8,128)(2,1)} %refs_8_.1) | copy-start | bytes 12582916
  31.2 13.4 %copy-start.2 = (s32[1024,1]{0,1:T(1,128)S(1)}, s32[1024,1]{0,1:T(1,128)}, u32[]{:S(2)}) copy-start(s32[1024,1]{0,1:T(1,128)} %param.14) | copy-start | bytes 12292
  31.2 13.4 %copy-start.3 = (s32[1024,1]{0,1:T(1,128)S(1)}, s32[1024,1]{0,1:T(1,128)}, u32[]{:S(2)}) copy-start(s32[1024,1]{0,1:T(1,128)} %param.16) | copy-start | bytes 12292
  31.2 13.4 %copy-start.4 = (s32[1024]{0:T(1024)S(1)}, s32[1024]{0:T(1024)}, u32[]{:S(2)}) copy-start(s32[1024]{0:T(1024)} %param.18) | copy-start | bytes 12292
  31.2 13.4 %copy-start.5 = (s32[1024]{0:T(1024)S(1)}, s32[1024]{0:T(1024)}, u32[]{:S(2)}) copy-start(s32[1024]{0:T(1024)} %param.19) | copy-start | bytes 12292

commit v10 on v9

--- a/solution.py
+++ b/solution.py
@@ -95,18 +95,9 @@
         pack_chunk(k, capacity, place[...], ids[...], feats[...], chunk)
 
 
-def margin_kernel(place, weight, features, margin, copies, sems):
-    parts = copies.shape[0]
-    step = copies.shape[1]
-    moves = [
-        pltpu.make_async_copy(features.at[pl.ds(i * step, step)], copies.at[i], sems.at[i]) for i in range(parts)
-    ]
-    for move in moves:
-        move.start()
+def margin_kernel(place, weight, features, margin):
     wide = jnp.broadcast_to(weight[...], (16, weight.shape[1])).astype(BF16)
-    for i in range(parts):
-        moves[i].wait()
-        margin[:, i * step : (i + 1) * step] = lanes_dot(wide, copies[i])[0:1]
+    margin[...] = lanes_dot(wide, features[...])[0:1]
 
 
 def chunk_ids(chunk, capacity):
@@ -121,19 +112,17 @@
     return jnp.sum(jnp.where(hits, every[:entities] + every[entities:], 0.0), axis=0, keepdims=True)
 
 
-def early_kernel(capacity, coefs, *refs):
-    half = len(refs) // 2
+def early_kernel(capacity, count, coefs, *refs):
     table = jnp.concatenate(halves(coefs[...]), axis=0)
-    for chunk, out in zip(refs[:half], refs[half:]):
+    for chunk, out in zip(refs[:count], refs[-count:]):
         out[...] = chunk_scores(chunk, table, capacity)
 
 
 def scores_kernel(order, capacity, n_feat, n_ent, where, coefs, *refs):
     out, mine = refs[-1], where[0]
     table = jnp.concatenate(halves(coefs[...]), axis=0)
-    scores = [
-        x[...] if x.shape[0] == 1 else chunk_scores(x, table, capacity) for x in refs[:-1]
-    ]
+    scores = [x[...] if x.shape[0] == 1 else chunk_scores(x, table, capacity) for x in refs[:-1]]
+    scores.append(jnp.zeros((1, capacity), F32))
     for k, score in zip(order, scores):
         home = mine ^ k
         for f in range(n_feat):
@@ -141,12 +130,14 @@
 
 
 def home_kernel(
-    owners, capacity, n_feat, n_ent, where, member, item, ranks, clicks, valid, margin, scores, features, out
+    owners, capacity, n_feat, n_ent, where, member, item, ranks, clicks, valid, margin, scores, features, *refs
 ):
-    on_item = where[1] > 0
+    lates, out = refs[:-1], refs[-1]
+    mine, on_item = where[0], where[1] > 0
     total = margin[...]
     hits_of = [one_hot(owner[...], owners).astype(F32) for owner in (member, item)]
     spot_of = [one_hot(ranks[side : side + 1], capacity).astype(F32).astype(BF16) for side in (0, 1)]
+    late = lax.broadcasted_iota(jnp.int32, (owners, capacity), 0) == (mine ^ (owners - 1))
     for side in (0, 1):
         table = None
         for f in range(side * n_feat // 2, (side + 1) * n_feat // 2):
@@ -154,6 +145,9 @@
                 [scores[(h // n_ent * n_feat + f) * n_ent + h % n_ent] for h in range(owners)], axis=0
             )
             table = part if table is None else table + part
+        for q in range(n_feat):
+            on_side = where[1 + q] == side
+            table = table + jnp.where(late & on_side, lates[q][...], 0.0)
         found = plain_dot(jnp.concatenate(halves(table), axis=0), spot_of[side])
         total = total + jnp.sum((found[:owners] + found[owners:]) * hits_of[side], axis=0, keepdims=True)
     resid = valid[...].astype(F32) * (jax.nn.sigmoid(total) - clicks[...].astype(F32))
@@ -224,8 +218,8 @@
     owners = lax.axis_size("rows") * n_ent
     capacity = 2 * rows_here // owners
     mine = lax.axis_index(HOME).astype(jnp.int32)
-    on_item = (lax.axis_index("feat") >= n_feat // 2).astype(jnp.int32)
-    where = jnp.stack([mine, on_item])
+    feat = lax.axis_index("feat")
+    where = jnp.stack([mine, *(((feat ^ q) >= n_feat // 2).astype(jnp.int32) for q in range(n_feat))])
     member, item = member_owner.reshape(1, rows_here), item_owner.reshape(1, rows_here)
 
     def shape(*dims, dtype=F32):
@@ -235,8 +229,9 @@
         return lambda *refs: kernel(*args, *refs)
 
     row = pltpu.VMEM((1, rows_here), jnp.int32)
-    half, early = owners // 2, 3 * owners // 4
-    first, second, near = list(range(half, early)), list(range(early, owners)), list(reversed(range(half)))
+    half, early, late = owners // 2, 3 * owners // 4, owners - 1
+    first, second = list(range(half, early)), list(range(early, owners))
+    last = list(reversed(range(half)))
     chunk = shape(capacity + IDS, width, dtype=BF16)
     flops = len(first) * 2 * capacity * rows_here * width
 
@@ -261,7 +256,7 @@
             in_hbm(entity_feats),
         ),
         [SMEM] + [HBM] * 5,
-        flops=flops,
+        flops=1 * flops,
         scratch=[row, row, row, row, pltpu.SemaphoreType.DMA((5,))],
     )
     chunks += call(
@@ -269,46 +264,48 @@
         [chunk] * len(second),
         (place, ids, feats),
         [VMEM] * 3,
-        flops=flops,
+        flops=16 * flops,
     )
     chunks = [xor_send(x, HOME, owners, k) for k, x in zip(first + second, chunks)]
     weight = global_weight.astype(F32).reshape(1, columns)
-    parts = 4
     (global_part,) = call(
-        margin_kernel,
-        [shape(1, rows_here)],
-        (place, weight, in_hbm(features)),
-        [VMEM, VMEM, HBM],
-        hidden=True,
-        scratch=[pltpu.VMEM((parts, rows_here // parts, columns), BF16), pltpu.SemaphoreType.DMA((parts,))],
+        margin_kernel, [shape(1, rows_here)], (place, weight, features), [VMEM] * 3, hidden=True
     )
     global_total = lax.psum(global_part, "feat")
-    near_chunks = call(
-        partial(rest_kernel, capacity, near),
-        [chunk] * len(near),
+    last_chunks = call(
+        partial(rest_kernel, capacity, last),
+        [chunk] * len(last),
         (place, ids, feats, global_total),
         [VMEM] * 4,
         hidden=True,
     )
-    near_chunks = [xor_send(x, HOME, owners, k) for k, x in zip(near, near_chunks)]
-    order = first + near[-1:] + second + near[:-1]
-    chunks = chunks[: len(first)] + near_chunks[-1:] + chunks[len(first) :] + near_chunks[:-1]
-    came_early = len(first) + 1
+    last_chunks = [xor_send(x, HOME, owners, k) for k, x in zip(last, last_chunks)]
+    chunks = dict(zip(first + second + last, chunks + last_chunks))
+    came_early = first + [0]
     scores = call(
-        partial(early_kernel, capacity),
-        [shape(1, capacity)] * came_early,
-        (coefs, *chunks[:came_early]),
-        [VMEM] * (1 + came_early),
+        partial(early_kernel, capacity, len(came_early)),
+        [shape(1, capacity)] * len(came_early),
+        (coefs, *(chunks[k] for k in came_early)),
+        [VMEM] * (1 + len(came_early)),
         hidden=True,
     )
+    came_next = second[:-1] + last[:-1]
+    order = came_early + came_next + [late]
     (scores,) = call(
         partial(scores_kernel, order, capacity, n_feat, n_ent),
         [shape(n_feat * owners, 1, capacity)],
-        (where, coefs, *scores, *chunks[came_early:]),
-        [SMEM] + [VMEM] * (1 + owners),
+        (where, coefs, *scores, *(chunks[k] for k in came_next)),
+        [SMEM] + [VMEM] * owners,
         flops=16 * coefs.size * owners * capacity,
     )
     returned = lax.all_to_all(scores, EVERY, split_axis=0, concat_axis=0, tiled=True)
+    (late_score,) = call(
+        partial(early_kernel, capacity, 1), [shape(1, capacity)], (coefs, chunks[late], scores), [VMEM] * 3, hidden=True
+    )
+    lates = []
+    for q in range(n_feat):
+        apart = (late // n_ent * n_feat + q) * n_ent + late % n_ent
+        lates.append(xor_send(late_score, EVERY, n_feat * owners, apart))
     (sent,) = call(
         partial(home_kernel, owners, capacity, n_feat, n_ent),
         [shape(owners, 1, capacity + columns)],
@@ -322,15 +319,16 @@
             global_total,
             returned,
             features,
+            *lates,
         ),
-        [SMEM] + [VMEM] * 8,
+        [SMEM] + [VMEM] * (8 + n_feat),
         flops=32 * features.size,
     )
     came = lax.all_to_all(sent, HOME, split_axis=0, concat_axis=0, tiled=True)
     grad_global, grad_coefs = call(
         partial(grads_kernel, order, capacity, 1.0 / math.sqrt(rows_here * owners)),
         [shape(1, columns), shape(*coefs.shape)],
-        (where, coefs, weight, came, *chunks),
+        (where, coefs, weight, came, *(chunks[k] for k in order)),
         [SMEM] + [VMEM] * (3 + owners),
         flops=4 * coefs.size * owners * capacity,
     )

time: 57.5 us -> 64.6 us (1.12)
  starting transfers between devices: 9.78 us -> 23.7 us
  blocking collectives: 25.2 us -> 13.3 us
  waiting for transfers between devices: 6.13 us -> 10.6 us
  local copies, waits for them, and re-layouts: 0.03 us -> 2.21 us
  Pallas kernels: 14.6 us -> 13.5 us
  other arithmetic: 0.76 us -> 0.08 us
    all_to_all x1 -> x0, blocking collectives: 11.9 us -> none  [body(): lax.all_to_all(scores, EVERY, split_axis=0, concat_axis=0, tiled=True)]
    ppermute x7 -> x9, starting transfers between devices: 9.78 us -> 17.8 us  [xor_send(): lax.ppermute(x, axes, [(i, i ^ k) for i in range(size)])]
    all_to_all x0 -> x1, starting transfers between devices: none -> 5.85 us  [body(): lax.all_to_all(scores, EVERY, split_axis=0, concat_axis=0, tiled=True)]
    ppermute x7 -> x9, waiting for transfers between devices: 6.13 us -> 10.6 us  [xor_send(): lax.ppermute(x, axes, [(i, i ^ k) for i in range(size)])]
    unnamed x12 -> x16, local copies, waits for them, and re-layouts: 0.03 us -> 2.21 us
    pallas_call x8 -> x9, Pallas kernels: 14.6 us -> 13.5 us  [call(): pl.pallas_call(kernel, out_shape=out_shape, in_specs=in_specs, out_specs=...]
    reshape x1, other arithmetic: 0.69 us -> 0.01 us  [body(): weight = global_weight.astype(F32).reshape(1, columns)]
  transfers between devices with their start and end apart: 7 -> 10, of which waited for: 4 -> 5; matrix products, arithmetic and copies ran while one was open for 1% -> 0% of each run, Pallas kernels for 11% -> 11%
where the time goes in v10:
time: 64.6 us; the launch traced here: 64.2 us
  starting transfers between devices  23.7 us (37%)
  Pallas kernels  13.5 us (21%)
  blocking collectives  13.3 us (21%)
  waiting for transfers between devices  10.6 us (16%)
  local copies, waits for them, and re-layouts  2.21 us (3%)
  between operations  0.78 us (1%)
    ppermute x9, starting transfers between devices, xor_send(): lax.ppermute(x, axes, [(i, i ^ k) for i in range(size)])  17.8 us
    pallas_call x9, Pallas kernels, call(): pl.pallas_call(kernel, out_shape=out_shape, in_specs=in_specs, out_specs=...  13.5 us
    ppermute x9, waiting for transfers between devices, xor_send(): lax.ppermute(x, axes, [(i, i ^ k) for i in range(size)])  10.6 us
    all_to_all x1, blocking collectives, body(): came = lax.all_to_all(sent, HOME, split_axis=0, concat_axis=0, tiled=True)  8.4 us
    all_to_all x1, starting transfers between devices, body(): lax.all_to_all(scores, EVERY, split_axis=0, concat_axis=0, tiled=True)  5.85 us
    psum x1, blocking collectives, body(): global_total = lax.psum(global_part, 'feat')  4.93 us
    unnamed x16, local copies, waits for them, and re-layouts  2.21 us
  transfers between devices with their start and end apart: 10, of which 5 were waited for; matrix products, arithmetic and copies ran while one was open for 0% of the time, Pallas kernels for 11%

profile of v10, /device:TPU:0, one launch (start us, length us, event | category | flops | bytes accessed | tf_op | source)
XLA Modules:
  0.0 64.2 jit_solution(10716414992914254024)
XLA Ops:
  0.6 0.1 pad_add_fusion.refs_0_
  0.7 2.4 %shard_map.113 = (s32[2,1024]{1,0:T(2,128)S(1)}, s32[1,1024]{1,0:T(1,128)S(1)}, bf16[8,1024]{1,0:T(8,128)(2,1)S(1)}, bf16[1024,256]{1,0:T(8,128)(2,1)S(1)}, bf16...) custom-call(s32[3]{0:T(128)S(1)} %pad_add_fusion.refs_0_, s32[1,1024]{1,0:T(1,128)} %bitcast.13, ...), custom_call_target="tpu_custom_call" | custom-call | flops 268435456 | bytes 1363980 | tf_op jit(solution)/shard_map/pallas_call | solution.py:192
  3.1 4.1 %collective-permute-start = (bf16[264,256]{1,0:T(8,128)(2,1)S(1)}, bf16[264,256]{1,0:T(8,128)(2,1)S(1)}, u32[]{:S(2)}, u32[]{:S(2)}) collective-permute-start(bf16[264,256]{1,0:T(8,128)(2,1)S(1)} %get-tuple-element.21), channel_id=1, source_target_pairs={{0,8},{1,9},{4,12},{5,13},{8,0},{9,1},{12,4},{13,5},{2,10},{3,11},... | collective-permute-start | bytes 405512 | tf_op jit(solution)/shard_map/ppermute | solution.py:187
  7.2 0.0 collective-permute-start.1
  7.2 0.0 copy-start.7
  7.2 0.0 copy-start
  7.2 0.7 %shard_map.117 = (bf16[264,256]{1,0:T(8,128)(2,1)S(1)}, bf16[264,256]{1,0:T(8,128)(2,1)S(1)}) custom-call(s32[1,1024]{1,0:T(1,128)S(1)} %get-tuple-element.20.place.refs_0_, bf16[8,1024]{1,0:T(8,128)(2,1)S(1)} %get-tuple-element.23.refs_1_, bf16[1024,256]{1,0:T(8,128)(2,1)S(1)} %get-tuple-element.24.refs_2_), custom_call_target="tpu_custom_call" | custom-call | flops 4294967296 | bytes 815104 | tf_op jit(solution)/shard_map/pallas_call | solution.py:192
  7.9 0.0 copy-start.2
  7.9 3.2 %collective-permute-start.2 = (bf16[264,256]{1,0:T(8,128)(2,1)S(1)}, bf16[264,256]{1,0:T(8,128)(2,1)S(1)}, u32[]{:S(2)}, u32[]{:S(2)}) collective-permute-start(bf16[264,256]{1,0:T(8,128)(2,1)S(1)} %get-tuple-element.29), channel_id=1, source_target_pairs={{0,12},{1,13},{4,8},{5,9},{8,4},{9,5},{12,0},{13,1},{2,14},{3,15},... | collective-permute-start | bytes 405512 | tf_op jit(solution)/shard_map/ppermute | solution.py:187
  11.1 0.0 copy-done.7
  11.1 0.0 copy-done
  11.1 1.2 %shard_map.114 = f32[1,1024]{1,0:T(1,128)S(1)} custom-call(s32[1,1024]{1,0:T(1,128)S(1)} %get-tuple-element.20.place.refs_0_, f32[1,2048]{1,0:T(1,128)S(1)} %bitcast.11, bf16[1024,2048]{1,0:T(8,128)(2,1)S(1)} %copy-done), custom_call_target="tpu_custom_call" | custom-call | tf_op jit(solution)/shard_map/pallas_call | solution.py:192
  12.3 4.9 %psum.7.refs_3_.refs_6_ = f32[1,1024]{1,0:T(1,128)S(1)} all-reduce(f32[1,1024]{1,0:T(1,128)S(1)} %shard_map.114), channel_id=1, replica_groups=mesh['groups'=2,'rows'=4,'feat'=2,'ent'=2] {'feat'}, use_global_device_ids=true, to_apply=%region_0.0 | all-reduce | flops 1024 | bytes 8192 | tf_op jit(solution)/shard_map/psum | solution.py:274
  17.2 1.2 %shard_map.115 = (bf16[264,256]{1,0:T(8,128)(2,1)S(1)}, bf16[264,256]{1,0:T(8,128)(2,1)S(1)}, bf16[264,256]{1,0:T(8,128)(2,1)S(1)}, bf16[264,256]{1,0:T(8,128)(2,1)S(1)}) custom-call(s32[1,1024]{1,0:T(1,128)S(1)} %get-tuple-element.20.place.refs_0_, bf16[8,1024]{1,0:T(8,128)(2,1)S(1)} %get-tuple-element.23.refs_1_, ...), custom_call_target="tpu_custom_call" | custom-call | tf_op jit(solution)/shard_map/pallas_call | solution.py:192
  18.4 0.1 collective-permute-start.3
  18.5 1.4 %collective-permute-start.4 = (bf16[264,256]{1,0:T(8,128)(2,1)S(1)}, bf16[264,256]{1,0:T(8,128)(2,1)S(1)}, u32[]{:S(2)}, u32[]{:S(2)}) collective-permute-start(bf16[264,256]{1,0:T(8,128)(2,1)S(1)} %get-tuple-element.31), channel_id=1, source_target_pairs={{0,4},{1,5},{4,0},{5,1},{8,12},{9,13},{12,8},{13,9},{2,6},{3,7},{6... | collective-permute-start | bytes 405512 | tf_op jit(solution)/shard_map/ppermute | solution.py:187
  20.0 0.3 collective-permute-done.refs_1_.refs_4_
  20.3 0.1 collective-permute-start.5
  20.4 1.2 %collective-permute-done.1.refs_2_.refs_5_ = bf16[264,256]{1,0:T(8,128)(2,1)S(1)} collective-permute-done((bf16[264,256]{1,0:T(8,128)(2,1)S(1)}, bf16[264,256]{1,0:T(8,128)(2,1)S(1)}, u32[]{:S(2)}, u32[]{:S(2)}) %collective-permute-start.1) | collective-permute-done | bytes 135200 | tf_op jit(solution)/shard_map/ppermute | solution.py:187
  21.6 4.0 %collective-permute-start.6 = (bf16[264,256]{1,0:T(8,128)(2,1)S(1)}, bf16[264,256]{1,0:T(8,128)(2,1)S(1)}, u32[]{:S(2)}, u32[]{:S(2)}) collective-permute-start(bf16[264,256]{1,0:T(8,128)(2,1)S(1)} %get-tuple-element.33), channel_id=1, source_target_pairs={{0,13},{1,12},{4,9},{5,8},{8,5},{9,4},{12,1},{13,0},{2,15},{3,14},... | collective-permute-start | bytes 405512 | tf_op jit(solution)/shard_map/ppermute | solution.py:187
  25.6 0.0 copy-done.2
  25.6 0.6 shard_map.116
  26.2 0.0 collective-permute-done.2.refs_5_.refs_7_
  26.2 0.0 collective-permute-done.3.refs_6_.refs_8_
  26.2 4.8 %collective-permute-done.4.refs_7_.refs_9_ = bf16[264,256]{1,0:T(8,128)(2,1)S(1)} collective-permute-done((bf16[264,256]{1,0:T(8,128)(2,1)S(1)}, bf16[264,256]{1,0:T(8,128)(2,1)S(1)}, u32[]{:S(2)}, u32[]{:S(2)}) %collective-permute-start.4) | collective-permute-done | bytes 135200 | tf_op jit(solution)/shard_map/ppermute | solution.py:187
  31.1 0.0 collective-permute-done.5.refs_8_.refs_10_
  31.1 0.0 copy-start.3
  31.1 0.0 copy-start.4
  31.1 0.0 copy-start.5
  31.1 0.0 copy-start.6
  31.1 1.9 %shard_map.118.refs_2_ = f32[16,1,256]{2,1,0:T(1,128)} custom-call(s32[3]{0:T(128)S(1)} %pad_add_fusion.refs_0_, f32[512,256]{1,0:T(8,128)S(1)} %copy-done.2, f32[1,256]{1,0:T(1,128)S(1)} %get-tuple-element.26.refs_2_, f32[1,256]{1,0:T(1,128)S(1)} %get-tuple-element.27.refs_3_, f32[1,256]{1,0:T(1,128)S(1)} %get-tuple-element.28.refs_4_, ...), custom_call_target="tpu_custom_call" | custom-call | flops 4294967296 | bytes 1084428 | tf_op jit(solution)/shard_map/pallas_call | solution.py:192
  33.0 5.9 %all-to-all-start = ((f32[16,1,256]{2,1,0:T(1,128)}), f32[16,1,256]{2,1,0:T(1,128)S(1)}, u32[]{:S(2)}, u32[]{:S(2)}) async-start(f32[16,1,256]{2,1,0:T(1,128)} %shard_map.118.refs_2_), calls=%async_computation | async-start | bytes 32768 | tf_op jit(solution)/shard_map/all_to_all | solution.py:301
  38.9 0.0 collective-permute-done.6.refs_1_.refs_11_
  38.9 1.1 %shard_map.119 = f32[1,256]{1,0:T(1,128)S(1)} custom-call(f32[512,256]{1,0:T(8,128)S(1)} %copy-done.2, bf16[264,256]{1,0:T(8,128)(2,1)S(1)} %collective-permute-done.6.refs_1_.refs_11_, f32[16,1,256]{2,1,0:T(1,128)} %shard_map.118.refs_2_), custom_call_target="tpu_custom_call" | custom-call | tf_op jit(solution)/shard_map/pallas_call | solution.py:192
  40.0 4.4 %collective-permute-start.8 = (f32[1,256]{1,0:T(1,128)S(1)}, f32[1,256]{1,0:T(1,128)S(1)}, u32[]{:S(2)}, u32[]{:S(2)}) collective-permute-start(f32[1,256]{1,0:T(1,128)S(1)} %shard_map.119), channel_id=1, source_target_pairs={{0,15},{1,14},{2,13},{3,12},{4,11},{5,10},{6,9},{7,8},{8,7},{9,6},... | collective-permute-start | bytes 3080 | tf_op jit(solution)/shard_map/ppermute | solution.py:187
  44.4 0.5 collective-permute-start.7
  45.0 0.8 %collective-permute-done.8.refs_10_ = f32[1,256]{1,0:T(1,128)S(1)} collective-permute-done((f32[1,256]{1,0:T(1,128)S(1)}, f32[1,256]{1,0:T(1,128)S(1)}, u32[]{:S(2)}, u32[]{:S(2)}) %collective-permute-start.8) | collective-permute-done | bytes 1056 | tf_op jit(solution)/shard_map/ppermute | solution.py:187
  45.8 3.5 %collective-permute-done.7.refs_9_ = f32[1,256]{1,0:T(1,128)S(1)} collective-permute-done((f32[1,256]{1,0:T(1,128)S(1)}, f32[1,256]{1,0:T(1,128)S(1)}, u32[]{:S(2)}, u32[]{:S(2)}) %collective-permute-start.7) | collective-permute-done | bytes 1056 | tf_op jit(solution)/shard_map/ppermute | solution.py:187
  49.2 0.0 all-to-all-done.refs_7_
  49.2 0.0 copy-done.3
  49.2 0.0 copy-done.4
  49.2 0.0 copy-done.5
  49.3 0.0 copy-done.6
  49.3 0.0 copy-start.1
  49.3 2.2 %copy-done.1 = bf16[1024,2048]{1,0:T(8,128)(2,1)S(1)} copy-done((bf16[1024,2048]{1,0:T(8,128)(2,1)S(1)}, bf16[1024,2048]{1,0:T(8,128)(2,1)}, u32[]{:S(2)}) %copy-start.1) | copy-done | bytes 4194328
  51.5 1.7 %shard_map.120 = f32[8,1,2304]{2,1,0:T(1,128)S(1)} custom-call(s32[3]{0:T(128)S(1)} %pad_add_fusion.refs_0_, s32[1,1024]{1,0:T(1,128)S(1)} %bitcast.14, s32[1,1024]{1,0:T(1,128)S(1)} %bitcast.16, s32[2,1024]{1,0:T(2,128)S(1)} %get-tuple-element.19.refs_3_, s32[1,1024]{1,0:T(1,128)S(1)} %bitcast.17, s32[1,1024]{1,0:T(1,128)S(1)} %bitcast.18, ...), custom_call_target="tpu_custom_call" | custom-call | flops 67108864 | bytes 4315148 | tf_op jit(solution)/shard_map/pallas_call | solution.py:192
  53.2 8.4 %all_to_all.10.refs_3_ = f32[8,1,2304]{2,1,0:T(1,128)S(1)} all-to-all(f32[8,1,2304]{2,1,0:T(1,128)S(1)} %shard_map.120), channel_id=1, replica_groups=mesh['groups'=2,'rows'=4,'feat'=2,'ent'=2] {'rows','ent'}, dimensions={0} | all-to-all | bytes 147456 | tf_op jit(solution)/shard_map/all_to_all | solution.py:327
  61.6 2.6 %shard_map.121 = (f32[1,2048]{1,0:T(1,128)}, f32[512,256]{1,0:T(8,128)}) custom-call(s32[3]{0:T(128)S(1)} %pad_add_fusion.refs_0_, f32[512,256]{1,0:T(8,128)S(1)} %copy-done.2, f32[1,2048]{1,0:T(1,128)S(1)} %bitcast.12, f32[8,1,2304]{2,1,0:T(1,128)S(1)} %all_to_all.10.refs_3_, bf16[264,256]{1,0:T(8,128)(2,1)S(1)} %collective-permute-done.refs_1_.refs_4_, ...), custom_call_target="tpu_custom_call" | custom-call | flops 1073741824 | bytes 2220044 | tf_op jit(solution)/shard_map/pallas_call | solution.py:192
  (1 shorter events, 0.0 us)
Async XLA Ops:
  3.1 17.2 %collective-permute-start = (bf16[264,256]{1,0:T(8,128)(2,1)S(1)}, bf16[264,256]{1,0:T(8,128)(2,1)S(1)}, u32[]{:S(2)}, u32[]{:S(2)}) collective-permute-start(bf16[264,256]{1,0:T(8,128)(2,1)S(1)} %get-tuple-element.21), channel_id=1, source_target_pairs={{0,8},{1,9},{4,12},{5,13},{8,0},{9,1},{12,4},{13,5},{2,10},{3,11},... | collective-permute-start | bytes 405512 | tf_op jit(solution)/shard_map/ppermute | solution.py:187
  7.2 14.3 %collective-permute-start.1 = (bf16[264,256]{1,0:T(8,128)(2,1)S(1)}, bf16[264,256]{1,0:T(8,128)(2,1)S(1)}, u32[]{:S(2)}, u32[]{:S(2)}) collective-permute-start(bf16[264,256]{1,0:T(8,128)(2,1)S(1)} %get-tuple-element.22), channel_id=1, source_target_pairs={{0,9},{1,8},{4,13},{5,12},{8,1},{9,0},{12,5},{13,4},{2,11},{3,10},... | collective-permute-start | bytes 405512 | tf_op jit(solution)/shard_map/ppermute | solution.py:187
  7.2 3.9 %copy-start.7 = (bf16[2048]{0:T(1024)(128)(2,1)S(1)}, bf16[2048]{0:T(1024)(128)(2,1)}, u32[]{:S(2)}) copy-start(bf16[2048]{0:T(1024)(128)(2,1)} %param.11) | copy-start | bytes 12292
  7.2 3.9 %copy-start = (bf16[1024,2048]{1,0:T(8,128)(2,1)S(1)}, bf16[1024,2048]{1,0:T(8,128)(2,1)}, u32[]{:S(2)}) copy-start(bf16[1024,2048]{1,0:T(8,128)(2,1)} %refs_8_.1) | copy-start | bytes 12582916
  7.9 17.7 %copy-start.2 = (f32[512,256]{1,0:T(8,128)S(1)}, f32[512,256]{1,0:T(8,128)}, u32[]{:S(2)}) copy-start(f32[512,256]{1,0:T(8,128)} %refs_1_.3) | copy-start | bytes 1572868
  7.9 18.3 %collective-permute-start.2 = (bf16[264,256]{1,0:T(8,128)(2,1)S(1)}, bf16[264,256]{1,0:T(8,128)(2,1)S(1)}, u32[]{:S(2)}, u32[]{:S(2)}) collective-permute-start(bf16[264,256]{1,0:T(8,128)(2,1)S(1)} %get-tuple-element.29), channel_id=1, source_target_pairs={{0,12},{1,13},{4,8},{5,9},{8,4},{9,5},{12,0},{13,1},{2,14},{3,15},... | collective-permute-start | bytes 405512 | tf_op jit(solution)/shard_map/ppermute | solution.py:187
  18.4 7.8 %collective-permute-start.3 = (bf16[264,256]{1,0:T(8,128)(2,1)S(1)}, bf16[264,256]{1,0:T(8,128)(2,1)S(1)}, u32[]{:S(2)}, u32[]{:S(2)}) collective-permute-start(bf16[264,256]{1,0:T(8,128)(2,1)S(1)} %get-tuple-element.30), channel_id=1, source_target_pairs={{0,5},{1,4},{4,1},{5,0},{8,13},{9,12},{12,9},{13,8},{2,7},{3,6},{6... | collective-permute-start | bytes 405512 | tf_op jit(solution)/shard_map/ppermute | solution.py:187
  18.5 12.5 %collective-permute-start.4 = (bf16[264,256]{1,0:T(8,128)(2,1)S(1)}, bf16[264,256]{1,0:T(8,128)(2,1)S(1)}, u32[]{:S(2)}, u32[]{:S(2)}) collective-permute-start(bf16[264,256]{1,0:T(8,128)(2,1)S(1)} %get-tuple-element.31), channel_id=1, source_target_pairs={{0,4},{1,5},{4,0},{5,1},{8,12},{9,13},{12,8},{13,9},{2,6},{3,7},{6... | collective-permute-start | bytes 405512 | tf_op jit(solution)/shard_map/ppermute | solution.py:187
  20.3 10.8 %collective-permute-start.5 = (bf16[264,256]{1,0:T(8,128)(2,1)S(1)}, bf16[264,256]{1,0:T(8,128)(2,1)S(1)}, u32[]{:S(2)}, u32[]{:S(2)}) collective-permute-start(bf16[264,256]{1,0:T(8,128)(2,1)S(1)} %get-tuple-element.32), channel_id=1, source_target_pairs={{0,1},{1,0},{4,5},{5,4},{8,9},{9,8},{12,13},{13,12},{2,3},{3,2},{6... | collective-permute-start | bytes 405512 | tf_op jit(solution)/shard_map/ppermute | solution.py:187
  21.6 17.3 %collective-permute-start.6 = (bf16[264,256]{1,0:T(8,128)(2,1)S(1)}, bf16[264,256]{1,0:T(8,128)(2,1)S(1)}, u32[]{:S(2)}, u32[]{:S(2)}) collective-permute-start(bf16[264,256]{1,0:T(8,128)(2,1)S(1)} %get-tuple-element.33), channel_id=1, source_target_pairs={{0,13},{1,12},{4,9},{5,8},{8,5},{9,4},{12,1},{13,0},{2,15},{3,14},... | collective-permute-start | bytes 405512 | tf_op jit(solution)/shard_map/ppermute | solution.py:187
  31.1 18.2 %copy-start.3 = (s32[1024,1]{0,1:T(1,128)S(1)}, s32[1024,1]{0,1:T(1,128)}, u32[]{:S(2)}) copy-start(s32[1024,1]{0,1:T(1,128)} %param.14) | copy-start | bytes 12292
  31.1 18.2 %copy-start.4 = (s32[1024,1]{0,1:T(1,128)S(1)}, s32[1024,1]{0,1:T(1,128)}, u32[]{:S(2)}) copy-start(s32[1024,1]{0,1:T(1,128)} %param.16) | copy-start | bytes 12292
  31.1 18.2 %copy-start.5 = (s32[1024]{0:T(1024)S(1)}, s32[1024]{0:T(1024)}, u32[]{:S(2)}) copy-start(s32[1024]{0:T(1024)} %param.18) | copy-start | bytes 12292
  31.1 18.2 %copy-start.6 = (s32[1024]{0:T(1024)S(1)}, s32[1024]{0:T(1024)}, u32[]{:S(2)}) copy-start(s32[1024]{0:T(1024)} %param.19) | copy-start | bytes 12292
  33.0 16.2 %all-to-all-start = ((f32[16,1,256]{2,1,0:T(1,128)}), f32[16,1,256]{2,1,0:T(1,128)S(1)}, u32[]{:S(2)}, u32[]{:S(2)}) async-start(f32[16,1,256]{2,1,0:T(1,128)} %shard_map.118.refs_2_), calls=%async_computation | async-start | bytes 32768 | tf_op jit(solution)/shard_map/all_to_all | solution.py:301
  40.0 5.8 %collective-permute-start.8 = (f32[1,256]{1,0:T(1,128)S(1)}, f32[1,256]{1,0:T(1,128)S(1)}, u32[]{:S(2)}, u32[]{:S(2)}) collective-permute-start(f32[1,256]{1,0:T(1,128)S(1)} %shard_map.119), channel_id=1, source_target_pairs={{0,15},{1,14},{2,13},{3,12},{4,11},{5,10},{6,9},{7,8},{8,7},{9,6},... | collective-permute-start | bytes 3080 | tf_op jit(solution)/shard_map/ppermute | solution.py:187
  44.4 4.8 %collective-permute-start.7 = (f32[1,256]{1,0:T(1,128)S(1)}, f32[1,256]{1,0:T(1,128)S(1)}, u32[]{:S(2)}, u32[]{:S(2)}) collective-permute-start(f32[1,256]{1,0:T(1,128)S(1)} %shard_map.119), channel_id=1, source_target_pairs={{0,13},{1,12},{2,15},{3,14},{4,9},{5,8},{6,11},{7,10},{8,5},{9,4},... | collective-permute-start | bytes 3080 | tf_op jit(solution)/shard_map/ppermute | solution.py:187
  49.3 2.2 %copy-start.1 = (bf16[1024,2048]{1,0:T(8,128)(2,1)S(1)}, bf16[1024,2048]{1,0:T(8,128)(2,1)}, u32[]{:S(2)}) copy-start(bf16[1024,2048]{1,0:T(8,128)(2,1)} %refs_8_.1) | copy-start | bytes 12582916

commit v11 on v9

--- a/solution.py
+++ b/solution.py
@@ -33,6 +33,25 @@
 
 def one_hot(row, count):
     return row == lax.broadcasted_iota(jnp.int32, (count, row.shape[1]), 0)
+
+
+def low_hot(row, count):
+    row = jnp.where((row >= 0) & (row < count), row, -1).astype(F32).astype(BF16)
+    return row == lax.broadcasted_iota(jnp.int32, (count, row.shape[1]), 0).astype(F32).astype(BF16)
+
+
+def ones(mask):
+    return jnp.where(mask, jnp.ones((), BF16), jnp.zeros((), BF16))
+
+
+def xor_rows(rows, mine):
+    count = rows.shape[0]
+    bit = 1
+    while bit < count:
+        swapped = jnp.concatenate([rows[(k ^ bit) : (k ^ bit) + 1] for k in range(count)], axis=0)
+        rows = jnp.where((mine & bit) > 0, swapped, rows)
+        bit *= 2
+    return rows
 
 
 def ranks_of(owners, member, item):
@@ -57,7 +76,7 @@
 
 
 def pack_chunk(k, capacity, place, ids, feats, chunk):
-    pick = one_hot(place - k * capacity, capacity).astype(F32).astype(BF16)
+    pick = ones(low_hot(place - k * capacity, capacity))
     chunk[:capacity] = plain_dot(pick, feats).astype(BF16)
     chunk[capacity:, :capacity] = lanes_dot(ids, pick).astype(BF16)
 
@@ -134,10 +153,11 @@
     scores = [
         x[...] if x.shape[0] == 1 else chunk_scores(x, table, capacity) for x in refs[:-1]
     ]
-    for k, score in zip(order, scores):
-        home = mine ^ k
+    scores = dict(zip(order, scores))
+    scores = xor_rows(jnp.concatenate([scores[k] for k in range(len(order))], axis=0), mine)
+    for home in range(len(order)):
         for f in range(n_feat):
-            out[(home // n_ent * n_feat + f) * n_ent + home % n_ent] = score
+            out[(home // n_ent * n_feat + f) * n_ent + home % n_ent] = scores[home : home + 1]
 
 
 def home_kernel(
@@ -146,7 +166,7 @@
     on_item = where[1] > 0
     total = margin[...]
     hits_of = [one_hot(owner[...], owners).astype(F32) for owner in (member, item)]
-    spot_of = [one_hot(ranks[side : side + 1], capacity).astype(F32).astype(BF16) for side in (0, 1)]
+    spot_of = [ones(low_hot(ranks[side : side + 1], capacity)) for side in (0, 1)]
     for side in (0, 1):
         table = None
         for f in range(side * n_feat // 2, (side + 1) * n_feat // 2):
@@ -172,17 +192,18 @@
     chunks, grad_global, grad_coefs = refs[:-2], refs[-2], refs[-1]
     entities = coefs.shape[0]
     mine = where[0]
-    resids = [came[mine ^ k][:, :capacity] for k in order]
+    resids = xor_rows(jnp.concatenate([came[h][:, :capacity] for h in range(len(order))], axis=0), mine)
     summed = came[0][:, capacity:]
     for h in range(1, len(order)):
         summed = summed + came[h][:, capacity:]
     grad_global[...] = summed * scale + 4.0 * weight[...]
     highs, lows, feats = [], [], []
-    for chunk, resid in zip(chunks, resids):
-        hits = one_hot(chunk_ids(chunk, capacity), entities)
-        high, low = halves(resid)
-        highs.append(jnp.where(hits, high.astype(F32), 0.0).astype(BF16))
-        lows.append(jnp.where(hits, low.astype(F32), 0.0).astype(BF16))
+    for chunk, k in zip(chunks, order):
+        here = chunk_ids(chunk, capacity)
+        blocks = [low_hot(here - first, min(256, entities)) for first in range(0, entities, 256)]
+        high, low = halves(resids[k : k + 1])
+        highs.append(jnp.concatenate([jnp.where(hits, high, jnp.zeros((), BF16)) for hits in blocks], axis=0))
+        lows.append(jnp.concatenate([jnp.where(hits, low, jnp.zeros((), BF16)) for hits in blocks], axis=0))
         feats.append(chunk[:capacity])
     spread = jnp.concatenate([jnp.concatenate(highs, axis=1), jnp.concatenate(lows, axis=1)], axis=0)
     both = plain_dot(spread, jnp.concatenate(feats, axis=0))

time: 57.5 us -> 57.4 us (level)
  no operation moved by 1% of the time
where the time goes in v11:
time: 57.4 us; the launch traced here: 57.2 us
  blocking collectives  25.2 us (44%)
  Pallas kernels  14.5 us (25%)
  starting transfers between devices  9.78 us (17%)
  waiting for transfers between devices  6.13 us (11%)
  other arithmetic  0.76 us (1%)
  between operations  0.76 us (1%)
    pallas_call x8, Pallas kernels, call(): pl.pallas_call(kernel, out_shape=out_shape, in_specs=in_specs, out_specs=...  14.5 us
    all_to_all x1, blocking collectives, body(): lax.all_to_all(scores, EVERY, split_axis=0, concat_axis=0, tiled=True)  11.9 us
    ppermute x7, starting transfers between devices, xor_send(): lax.ppermute(x, axes, [(i, i ^ k) for i in range(size)])  9.78 us
    all_to_all x1, blocking collectives, body(): came = lax.all_to_all(sent, HOME, split_axis=0, concat_axis=0, tiled=True)  8.4 us
    ppermute x7, waiting for transfers between devices, xor_send(): lax.ppermute(x, axes, [(i, i ^ k) for i in range(size)])  6.13 us
    psum x1, blocking collectives, body(): global_total = lax.psum(global_part, 'feat')  4.95 us
  transfers between devices with their start and end apart: 7, of which 4 were waited for; matrix products, arithmetic and copies ran while one was open for 1% of the time, Pallas kernels for 11%

profile of v11, /device:TPU:0, one launch (start us, length us, event | category | flops | bytes accessed | tf_op | source)
XLA Modules:
  0.0 57.2 jit_solution(12639920680819005492)
XLA Ops:
  0.6 0.0 copy-start.1
  0.6 0.1 pad_add_fusion.refs_0_
  0.7 2.4 %shard_map.113 = (s32[2,1024]{1,0:T(2,128)S(1)}, s32[1,1024]{1,0:T(1,128)S(1)}, bf16[8,1024]{1,0:T(8,128)(2,1)S(1)}, bf16[1024,256]{1,0:T(8,128)(2,1)S(1)}, bf16...) custom-call(s32[2]{0:T(128)S(1)} %pad_add_fusion.refs_0_, s32[1,1024]{1,0:T(1,128)} %bitcast.12, ...), custom_call_target="tpu_custom_call" | custom-call | flops 268435456 | bytes 1363976 | tf_op jit(solution)/shard_map/pallas_call | solution.py:219
  3.1 4.1 %collective-permute-start = (bf16[264,256]{1,0:T(8,128)(2,1)S(1)}, bf16[264,256]{1,0:T(8,128)(2,1)S(1)}, u32[]{:S(2)}, u32[]{:S(2)}) collective-permute-start(bf16[264,256]{1,0:T(8,128)(2,1)S(1)} %get-tuple-element.21), channel_id=1, source_target_pairs={{0,8},{1,9},{4,12},{5,13},{8,0},{9,1},{12,4},{13,5},{2,10},{3,11},... | collective-permute-start | bytes 405512 | tf_op jit(solution)/shard_map/ppermute | solution.py:214
  7.2 0.0 collective-permute-start.1
  7.2 0.7 %shard_map.117 = (bf16[264,256]{1,0:T(8,128)(2,1)S(1)}, bf16[264,256]{1,0:T(8,128)(2,1)S(1)}) custom-call(s32[1,1024]{1,0:T(1,128)S(1)} %get-tuple-element.20.place.refs_0_, bf16[8,1024]{1,0:T(8,128)(2,1)S(1)} %get-tuple-element.23.refs_1_, bf16[1024,256]{1,0:T(8,128)(2,1)S(1)} %get-tuple-element.24.refs_2_), custom_call_target="tpu_custom_call" | custom-call | flops 268435456 | bytes 815104 | tf_op jit(solution)/shard_map/pallas_call | solution.py:219
  7.9 3.2 %collective-permute-start.2 = (bf16[264,256]{1,0:T(8,128)(2,1)S(1)}, bf16[264,256]{1,0:T(8,128)(2,1)S(1)}, u32[]{:S(2)}, u32[]{:S(2)}) collective-permute-start(bf16[264,256]{1,0:T(8,128)(2,1)S(1)} %get-tuple-element.29), channel_id=1, source_target_pairs={{0,12},{1,13},{4,8},{5,9},{8,4},{9,5},{12,0},{13,1},{2,14},{3,15},... | collective-permute-start | bytes 405512 | tf_op jit(solution)/shard_map/ppermute | solution.py:214
  11.1 0.6 %collective-permute-start.3 = (bf16[264,256]{1,0:T(8,128)(2,1)S(1)}, bf16[264,256]{1,0:T(8,128)(2,1)S(1)}, u32[]{:S(2)}, u32[]{:S(2)}) collective-permute-start(bf16[264,256]{1,0:T(8,128)(2,1)S(1)} %get-tuple-element.30), channel_id=1, source_target_pairs={{0,13},{1,12},{4,9},{5,8},{8,5},{9,4},{12,1},{13,0},{2,15},{3,14},... | collective-permute-start | bytes 405512 | tf_op jit(solution)/shard_map/ppermute | solution.py:214
  11.7 0.7 %reshape.40 = f32[2048]{0:T(1024)S(1)} convert(bf16[2048]{0:T(1024)(128)(2,1)} %param.11) | non-fusion elementwise | flops 2048 | bytes 12288 | tf_op jit(solution)/shard_map/reshape | solution.py:296
  12.4 3.9 %shard_map.114 = f32[1,1024]{1,0:T(1,128)S(1)} custom-call(s32[1,1024]{1,0:T(1,128)S(1)} %get-tuple-element.20.place.refs_0_, f32[1,2048]{1,0:T(1,128)S(1)} %bitcast.10, bf16[1024,2048]{1,0:T(8,128)(2,1)} %refs_8_.1), custom_call_target="tpu_custom_call" | custom-call | tf_op jit(solution)/shard_map/pallas_call | solution.py:219
  16.3 4.9 %psum.7.refs_3_.refs_6_ = f32[1,1024]{1,0:T(1,128)S(1)} all-reduce(f32[1,1024]{1,0:T(1,128)S(1)} %shard_map.114), channel_id=1, replica_groups=mesh['groups'=2,'rows'=4,'feat'=2,'ent'=2] {'feat'}, use_global_device_ids=true, to_apply=%region_0.0 | all-reduce | flops 1024 | bytes 8192 | tf_op jit(solution)/shard_map/psum | solution.py:306
  21.3 1.2 %shard_map.115 = (bf16[264,256]{1,0:T(8,128)(2,1)S(1)}, bf16[264,256]{1,0:T(8,128)(2,1)S(1)}, bf16[264,256]{1,0:T(8,128)(2,1)S(1)}, bf16[264,256]{1,0:T(8,128)(2,1)S(1)}) custom-call(s32[1,1024]{1,0:T(1,128)S(1)} %get-tuple-element.20.place.refs_0_, bf16[8,1024]{1,0:T(8,128)(2,1)S(1)} %get-tuple-element.23.refs_1_, ...), custom_call_target="tpu_custom_call" | custom-call | tf_op jit(solution)/shard_map/pallas_call | solution.py:219
  22.5 0.1 collective-permute-start.4
  22.6 0.6 %collective-permute-done.refs_1_.refs_4_ = bf16[264,256]{1,0:T(8,128)(2,1)S(1)} collective-permute-done((bf16[264,256]{1,0:T(8,128)(2,1)S(1)}, bf16[264,256]{1,0:T(8,128)(2,1)S(1)}, u32[]{:S(2)}, u32[]{:S(2)}) %collective-permute-start) | collective-permute-done | bytes 135200 | tf_op jit(solution)/shard_map/ppermute | solution.py:214
  23.2 0.3 collective-permute-start.5
  23.5 0.9 %collective-permute-done.1.refs_2_.refs_5_ = bf16[264,256]{1,0:T(8,128)(2,1)S(1)} collective-permute-done((bf16[264,256]{1,0:T(8,128)(2,1)S(1)}, bf16[264,256]{1,0:T(8,128)(2,1)S(1)}, u32[]{:S(2)}, u32[]{:S(2)}) %collective-permute-start.1) | collective-permute-done | bytes 135200 | tf_op jit(solution)/shard_map/ppermute | solution.py:214
  24.4 1.5 %collective-permute-start.6 = (bf16[264,256]{1,0:T(8,128)(2,1)S(1)}, bf16[264,256]{1,0:T(8,128)(2,1)S(1)}, u32[]{:S(2)}, u32[]{:S(2)}) collective-permute-start(bf16[264,256]{1,0:T(8,128)(2,1)S(1)} %get-tuple-element.33), channel_id=1, source_target_pairs={{0,1},{1,0},{4,5},{5,4},{8,9},{9,8},{12,13},{13,12},{2,3},{3,2},{6... | collective-permute-start | bytes 405512 | tf_op jit(solution)/shard_map/ppermute | solution.py:214
  25.9 0.0 copy-done.1
  25.9 0.6 %shard_map.116 = (f32[1,256]{1,0:T(1,128)S(1)}, f32[1,256]{1,0:T(1,128)S(1)}, f32[1,256]{1,0:T(1,128)S(1)}) custom-call(f32[512,256]{1,0:T(8,128)S(1)} %copy-done.1, bf16[264,256]{1,0:T(8,128)(2,1)S(1)} %collective-permute-done.refs_1_.refs_4_, bf16[264,256]{1,0:T(8,128)(2,1)S(1)} %collective-permute-done.1.refs_2_.refs_5_, ...), custom_call_target="tpu_custom_call" | custom-call | tf_op jit(solution)/shard_map/pallas_call | solution.py:219
  26.6 0.0 collective-permute-done.2.refs_5_.refs_7_
  26.6 0.0 collective-permute-done.3.refs_6_.refs_8_
  26.6 2.1 %collective-permute-done.4.refs_7_.refs_9_ = bf16[264,256]{1,0:T(8,128)(2,1)S(1)} collective-permute-done((bf16[264,256]{1,0:T(8,128)(2,1)S(1)}, bf16[264,256]{1,0:T(8,128)(2,1)S(1)}, u32[]{:S(2)}, u32[]{:S(2)}) %collective-permute-start.4) | collective-permute-done | bytes 135200 | tf_op jit(solution)/shard_map/ppermute | solution.py:214
  28.7 2.4 %collective-permute-done.5.refs_8_.refs_10_ = bf16[264,256]{1,0:T(8,128)(2,1)S(1)} collective-permute-done((bf16[264,256]{1,0:T(8,128)(2,1)S(1)}, bf16[264,256]{1,0:T(8,128)(2,1)S(1)}, u32[]{:S(2)}, u32[]{:S(2)}) %collective-permute-start.5) | collective-permute-done | bytes 135200 | tf_op jit(solution)/shard_map/ppermute | solution.py:214
  31.2 0.0 collective-permute-done.6.refs_9_.refs_11_
  31.2 0.0 copy-start
  31.2 0.0 copy-start.2
  31.2 0.0 copy-start.3
  31.2 0.0 copy-start.4
  31.2 0.0 copy-start.5
  31.2 1.5 %shard_map.118 = f32[16,1,256]{2,1,0:T(1,128)S(1)} custom-call(s32[2]{0:T(128)S(1)} %pad_add_fusion.refs_0_, f32[512,256]{1,0:T(8,128)S(1)} %copy-done.1, f32[1,256]{1,0:T(1,128)S(1)} %get-tuple-element.26.refs_2_, f32[1,256]{1,0:T(1,128)S(1)} %get-tuple-element.27.refs_3_, f32[1,256]{1,0:T(1,128)S(1)} %get-tuple-element.28.refs_4_, ...), custom_call_target="tpu_custom_call" | custom-call | flops 4294967296 | bytes 1219592 | tf_op jit(solution)/shard_map/pallas_call | solution.py:219
  32.7 11.9 %all_to_all.10.refs_7_ = f32[16,1,256]{2,1,0:T(1,128)S(1)} all-to-all(f32[16,1,256]{2,1,0:T(1,128)S(1)} %shard_map.118), channel_id=1, replica_groups=mesh['groups'=2,'rows'=4,'feat'=2,'ent'=2] {'rows','feat','ent'}, dimensions={0} | all-to-all | bytes 32768 | tf_op jit(solution)/shard_map/all_to_all | solution.py:332
  44.5 0.0 copy-done
  44.5 0.0 copy-done.2
  44.5 0.0 copy-done.3
  44.5 0.0 copy-done.4
  44.6 0.0 copy-done.5
  44.6 1.6 %shard_map.119 = f32[8,1,2304]{2,1,0:T(1,128)S(1)} custom-call(s32[2]{0:T(128)S(1)} %pad_add_fusion.refs_0_, s32[1,1024]{1,0:T(1,128)S(1)} %bitcast.13, s32[1,1024]{1,0:T(1,128)S(1)} %bitcast.15, s32[2,1024]{1,0:T(2,128)S(1)} %get-tuple-element.19.refs_3_, s32[1,1024]{1,0:T(1,128)S(1)} %bitcast.16, s32[1,1024]{1,0:T(1,128)S(1)} %bitcast.17, ...), custom_call_target="tpu_custom_call" | custom-call | flops 67108864 | bytes 4313096 | tf_op jit(solution)/shard_map/pallas_call | solution.py:219
  46.2 8.4 %all_to_all.11.refs_3_ = f32[8,1,2304]{2,1,0:T(1,128)S(1)} all-to-all(f32[8,1,2304]{2,1,0:T(1,128)S(1)} %shard_map.119), channel_id=1, replica_groups=mesh['groups'=2,'rows'=4,'feat'=2,'ent'=2] {'rows','ent'}, dimensions={0} | all-to-all | bytes 147456 | tf_op jit(solution)/shard_map/all_to_all | solution.py:350
  54.6 2.6 %shard_map.120 = (f32[1,2048]{1,0:T(1,128)}, f32[512,256]{1,0:T(8,128)}) custom-call(s32[2]{0:T(128)S(1)} %pad_add_fusion.refs_0_, f32[512,256]{1,0:T(8,128)S(1)} %copy-done.1, f32[1,2048]{1,0:T(1,128)S(1)} %bitcast.11, f32[8,1,2304]{2,1,0:T(1,128)S(1)} %all_to_all.11.refs_3_, bf16[264,256]{1,0:T(8,128)(2,1)S(1)} %collective-permute-done.refs_1_.refs_4_, ...), custom_call_target="tpu_custom_call" | custom-call | flops 1073741824 | bytes 2220040 | tf_op jit(solution)/shard_map/pallas_call | solution.py:219
Async XLA Ops:
  0.6 25.3 %copy-start.1 = (f32[512,256]{1,0:T(8,128)S(1)}, f32[512,256]{1,0:T(8,128)}, u32[]{:S(2)}) copy-start(f32[512,256]{1,0:T(8,128)} %refs_1_.3) | copy-start | bytes 1572868
  3.1 20.1 %collective-permute-start = (bf16[264,256]{1,0:T(8,128)(2,1)S(1)}, bf16[264,256]{1,0:T(8,128)(2,1)S(1)}, u32[]{:S(2)}, u32[]{:S(2)}) collective-permute-start(bf16[264,256]{1,0:T(8,128)(2,1)S(1)} %get-tuple-element.21), channel_id=1, source_target_pairs={{0,8},{1,9},{4,12},{5,13},{8,0},{9,1},{12,4},{13,5},{2,10},{3,11},... | collective-permute-start | bytes 405512 | tf_op jit(solution)/shard_map/ppermute | solution.py:214
  7.2 17.2 %collective-permute-start.1 = (bf16[264,256]{1,0:T(8,128)(2,1)S(1)}, bf16[264,256]{1,0:T(8,128)(2,1)S(1)}, u32[]{:S(2)}, u32[]{:S(2)}) collective-permute-start(bf16[264,256]{1,0:T(8,128)(2,1)S(1)} %get-tuple-element.22), channel_id=1, source_target_pairs={{0,9},{1,8},{4,13},{5,12},{8,1},{9,0},{12,5},{13,4},{2,11},{3,10},... | collective-permute-start | bytes 405512 | tf_op jit(solution)/shard_map/ppermute | solution.py:214
  7.9 18.7 %collective-permute-start.2 = (bf16[264,256]{1,0:T(8,128)(2,1)S(1)}, bf16[264,256]{1,0:T(8,128)(2,1)S(1)}, u32[]{:S(2)}, u32[]{:S(2)}) collective-permute-start(bf16[264,256]{1,0:T(8,128)(2,1)S(1)} %get-tuple-element.29), channel_id=1, source_target_pairs={{0,12},{1,13},{4,8},{5,9},{8,4},{9,5},{12,0},{13,1},{2,14},{3,15},... | collective-permute-start | bytes 405512 | tf_op jit(solution)/shard_map/ppermute | solution.py:214
  11.1 15.5 %collective-permute-start.3 = (bf16[264,256]{1,0:T(8,128)(2,1)S(1)}, bf16[264,256]{1,0:T(8,128)(2,1)S(1)}, u32[]{:S(2)}, u32[]{:S(2)}) collective-permute-start(bf16[264,256]{1,0:T(8,128)(2,1)S(1)} %get-tuple-element.30), channel_id=1, source_target_pairs={{0,13},{1,12},{4,9},{5,8},{8,5},{9,4},{12,1},{13,0},{2,15},{3,14},... | collective-permute-start | bytes 405512 | tf_op jit(solution)/shard_map/ppermute | solution.py:214
  22.5 6.2 %collective-permute-start.4 = (bf16[264,256]{1,0:T(8,128)(2,1)S(1)}, bf16[264,256]{1,0:T(8,128)(2,1)S(1)}, u32[]{:S(2)}, u32[]{:S(2)}) collective-permute-start(bf16[264,256]{1,0:T(8,128)(2,1)S(1)} %get-tuple-element.31), channel_id=1, source_target_pairs={{0,5},{1,4},{4,1},{5,0},{8,13},{9,12},{12,9},{13,8},{2,7},{3,6},{6... | collective-permute-start | bytes 405512 | tf_op jit(solution)/shard_map/ppermute | solution.py:214
  23.2 7.9 %collective-permute-start.5 = (bf16[264,256]{1,0:T(8,128)(2,1)S(1)}, bf16[264,256]{1,0:T(8,128)(2,1)S(1)}, u32[]{:S(2)}, u32[]{:S(2)}) collective-permute-start(bf16[264,256]{1,0:T(8,128)(2,1)S(1)} %get-tuple-element.32), channel_id=1, source_target_pairs={{0,4},{1,5},{4,0},{5,1},{8,12},{9,13},{12,8},{13,9},{2,6},{3,7},{6... | collective-permute-start | bytes 405512 | tf_op jit(solution)/shard_map/ppermute | solution.py:214
  24.4 6.7 %collective-permute-start.6 = (bf16[264,256]{1,0:T(8,128)(2,1)S(1)}, bf16[264,256]{1,0:T(8,128)(2,1)S(1)}, u32[]{:S(2)}, u32[]{:S(2)}) collective-permute-start(bf16[264,256]{1,0:T(8,128)(2,1)S(1)} %get-tuple-element.33), channel_id=1, source_target_pairs={{0,1},{1,0},{4,5},{5,4},{8,9},{9,8},{12,13},{13,12},{2,3},{3,2},{6... | collective-permute-start | bytes 405512 | tf_op jit(solution)/shard_map/ppermute | solution.py:214
  31.2 13.4 %copy-start = (bf16[1024,2048]{1,0:T(8,128)(2,1)S(1)}, bf16[1024,2048]{1,0:T(8,128)(2,1)}, u32[]{:S(2)}) copy-start(bf16[1024,2048]{1,0:T(8,128)(2,1)} %refs_8_.1) | copy-start | bytes 12582916
  31.2 13.4 %copy-start.2 = (s32[1024,1]{0,1:T(1,128)S(1)}, s32[1024,1]{0,1:T(1,128)}, u32[]{:S(2)}) copy-start(s32[1024,1]{0,1:T(1,128)} %param.14) | copy-start | bytes 12292
  31.2 13.4 %copy-start.3 = (s32[1024,1]{0,1:T(1,128)S(1)}, s32[1024,1]{0,1:T(1,128)}, u32[]{:S(2)}) copy-start(s32[1024,1]{0,1:T(1,128)} %param.16) | copy-start | bytes 12292
  31.2 13.4 %copy-start.4 = (s32[1024]{0:T(1024)S(1)}, s32[1024]{0:T(1024)}, u32[]{:S(2)}) copy-start(s32[1024]{0:T(1024)} %param.18) | copy-start | bytes 12292
  31.2 13.4 %copy-start.5 = (s32[1024]{0:T(1024)S(1)}, s32[1024]{0:T(1024)}, u32[]{:S(2)}) copy-start(s32[1024]{0:T(1024)} %param.19) | copy-start | bytes 12292

commit v12 on v11

--- a/solution.py
+++ b/solution.py
@@ -13,7 +13,6 @@
 EVERY = ("rows", "feat", "ent")
 IDS = 8
 PARAMS = pltpu.CompilerParams(vmem_limit_bytes=24 * 2**20)
-SMEM = pl.BlockSpec(memory_space=pltpu.SMEM)
 VMEM = pl.BlockSpec(memory_space=pltpu.VMEM)
 HBM = pl.BlockSpec(memory_space=pltpu.HBM)
 
@@ -81,7 +80,11 @@
     chunk[capacity:, :capacity] = lanes_dot(ids, pick).astype(BF16)
 
 
-def far_kernel(owners, capacity, far, where, *refs):
+def position(n_feat):
+    return lax.axis_index(HOME), lax.axis_index("feat") >= n_feat // 2
+
+
+def far_kernel(owners, capacity, n_feat, far, *refs):
     sources, ranks, place_out, ids_out, feats = refs[:5], refs[5], refs[6], refs[7], refs[8]
     chunks, copies, sems = refs[9 : 9 + len(far)], refs[9 + len(far) : 13 + len(far)], refs[13 + len(far)]
     copies = (*copies, feats)
@@ -92,7 +95,7 @@
         move.wait()
     member, item, member_local, item_local = [copy[...] for copy in copies[:4]]
     rows = member.shape[1]
-    mine, on_item = where[0], where[1] > 0
+    mine, on_item = position(n_feat)
     rank = ranks_of(owners, member, item)
     ranks[...] = rank
     own = jnp.where(on_item, item, member)
@@ -147,8 +150,8 @@
         out[...] = chunk_scores(chunk, table, capacity)
 
 
-def scores_kernel(order, capacity, n_feat, n_ent, where, coefs, *refs):
-    out, mine = refs[-1], where[0]
+def scores_kernel(order, capacity, n_feat, n_ent, coefs, *refs):
+    out, mine = refs[-1], lax.axis_index(HOME)
     table = jnp.concatenate(halves(coefs[...]), axis=0)
     scores = [
         x[...] if x.shape[0] == 1 else chunk_scores(x, table, capacity) for x in refs[:-1]
@@ -161,9 +164,9 @@
 
 
 def home_kernel(
-    owners, capacity, n_feat, n_ent, where, member, item, ranks, clicks, valid, margin, scores, features, out
+    owners, capacity, n_feat, n_ent, member, item, ranks, clicks, valid, margin, scores, features, out
 ):
-    on_item = where[1] > 0
+    on_item = position(n_feat)[1]
     total = margin[...]
     hits_of = [one_hot(owner[...], owners).astype(F32) for owner in (member, item)]
     spot_of = [ones(low_hot(ranks[side : side + 1], capacity)) for side in (0, 1)]
@@ -188,10 +191,10 @@
         out[h, :, capacity:] = grad
 
 
-def grads_kernel(order, capacity, scale, where, coefs, weight, came, *refs):
+def grads_kernel(order, capacity, scale, coefs, weight, came, *refs):
     chunks, grad_global, grad_coefs = refs[:-2], refs[-2], refs[-1]
     entities = coefs.shape[0]
-    mine = where[0]
+    mine = lax.axis_index(HOME)
     resids = xor_rows(jnp.concatenate([came[h][:, :capacity] for h in range(len(order))], axis=0), mine)
     summed = came[0][:, capacity:]
     for h in range(1, len(order)):
@@ -244,9 +247,6 @@
     n_feat, n_ent = lax.axis_size("feat"), lax.axis_size("ent")
     owners = lax.axis_size("rows") * n_ent
     capacity = 2 * rows_here // owners
-    mine = lax.axis_index(HOME).astype(jnp.int32)
-    on_item = (lax.axis_index("feat") >= n_feat // 2).astype(jnp.int32)
-    where = jnp.stack([mine, on_item])
     member, item = member_owner.reshape(1, rows_here), item_owner.reshape(1, rows_here)
 
     def shape(*dims, dtype=F32):
@@ -265,7 +265,7 @@
         return pltpu.with_memory_space_constraint(x, pltpu.HBM)
 
     ranks, place, ids, feats, *chunks = call(
-        partial(far_kernel, owners, capacity, first),
+        partial(far_kernel, owners, capacity, n_feat, first),
         [
             shape(2, rows_here, dtype=jnp.int32),
             shape(1, rows_here, dtype=jnp.int32),
@@ -274,14 +274,13 @@
         ]
         + [chunk] * len(first),
         (
-            where,
             in_hbm(member),
             in_hbm(item),
             in_hbm(member_local.reshape(1, rows_here)),
             in_hbm(item_local.reshape(1, rows_here)),
             in_hbm(entity_feats),
         ),
-        [SMEM] + [HBM] * 5,
+        [HBM] * 5,
         flops=flops,
         scratch=[row, row, row, row, pltpu.SemaphoreType.DMA((5,))],
     )
@@ -325,8 +324,8 @@
     (scores,) = call(
         partial(scores_kernel, order, capacity, n_feat, n_ent),
         [shape(n_feat * owners, 1, capacity)],
-        (where, coefs, *scores, *chunks[came_early:]),
-        [SMEM] + [VMEM] * (1 + owners),
+        (coefs, *scores, *chunks[came_early:]),
+        [VMEM] * (1 + owners),
         flops=16 * coefs.size * owners * capacity,
     )
     returned = lax.all_to_all(scores, EVERY, split_axis=0, concat_axis=0, tiled=True)
@@ -334,7 +333,6 @@
         partial(home_kernel, owners, capacity, n_feat, n_ent),
         [shape(owners, 1, capacity + columns)],
         (
-            where,
             member,
             item,
             ranks,
@@ -344,15 +342,15 @@
             returned,
             features,
         ),
-        [SMEM] + [VMEM] * 8,
+        [VMEM] * 8,
         flops=32 * features.size,
     )
     came = lax.all_to_all(sent, HOME, split_axis=0, concat_axis=0, tiled=True)
     grad_global, grad_coefs = call(
         partial(grads_kernel, order, capacity, 1.0 / math.sqrt(rows_here * owners)),
         [shape(1, columns), shape(*coefs.shape)],
-        (where, coefs, weight, came, *chunks),
-        [SMEM] + [VMEM] * (3 + owners),
+        (coefs, weight, came, *chunks),
+        [VMEM] * (3 + owners),
         flops=4 * coefs.size * owners * capacity,
     )
     return (grad_global.reshape(columns), grad_coefs)

time: 57.4 us -> 55.4 us (0.965)
  Pallas kernels: 14.5 us -> 12.4 us
    pallas_call x8, Pallas kernels: 14.5 us -> 12.4 us  [call(): pl.pallas_call(kernel, out_shape=out_shape, in_specs=in_specs, out_specs=...]
  transfers between devices with their start and end apart: 7 -> 7, of which waited for: 4 -> 4; matrix products, arithmetic and copies ran while one was open for 1% -> 1% of each run, Pallas kernels for 11% -> 12%
where the time goes in v12:
time: 55.4 us; the launch traced here: 55.1 us
  blocking collectives  25.3 us (46%)
  Pallas kernels  12.4 us (22%)
  starting transfers between devices  9.78 us (18%)
  waiting for transfers between devices  6.13 us (11%)
  between operations  0.75 us (1%)
  other arithmetic  0.69 us (1%)
    pallas_call x8, Pallas kernels, call(): pl.pallas_call(kernel, out_shape=out_shape, in_specs=in_specs, out_specs=...  12.4 us
    all_to_all x1, blocking collectives, body(): lax.all_to_all(scores, EVERY, split_axis=0, concat_axis=0, tiled=True)  12 us
    ppermute x7, starting transfers between devices, xor_send(): lax.ppermute(x, axes, [(i, i ^ k) for i in range(size)])  9.78 us
    all_to_all x1, blocking collectives, body(): came = lax.all_to_all(sent, HOME, split_axis=0, concat_axis=0, tiled=True)  8.4 us
    ppermute x7, waiting for transfers between devices, xor_send(): lax.ppermute(x, axes, [(i, i ^ k) for i in range(size)])  6.13 us
    psum x1, blocking collectives, body(): global_total = lax.psum(global_part, 'feat')  4.95 us
  transfers between devices with their start and end apart: 7, of which 4 were waited for; matrix products, arithmetic and copies ran while one was open for 1% of the time, Pallas kernels for 12%

profile of v12, /device:TPU:0, one launch (start us, length us, event | category | flops | bytes accessed | tf_op | source)
XLA Modules:
  0.0 55.1 jit_solution(17757278162170093096)
XLA Ops:
  0.6 0.0 copy-start.1
  0.6 1.9 %shard_map.113 = (s32[2,1024]{1,0:T(2,128)S(1)}, s32[1,1024]{1,0:T(1,128)S(1)}, bf16[8,1024]{1,0:T(8,128)(2,1)S(1)}, bf16[1024,256]{1,0:T(8,128)(2,1)S(1)}, bf16...) custom-call(s32[1,1024]{1,0:T(1,128)} %bitcast.10, s32[1,1024]{1,0:T(1,128)} %bitcast.12, s32[1,1024]{1,0:T(1,128)} %bitcast.16, ...), custom_call_target="tpu_custom_call" | custom-call | flops 268435456 | bytes 1363968 | tf_op jit(solution)/shard_map/pallas_call | solution.py:222
  2.5 4.1 %collective-permute-start = (bf16[264,256]{1,0:T(8,128)(2,1)S(1)}, bf16[264,256]{1,0:T(8,128)(2,1)S(1)}, u32[]{:S(2)}, u32[]{:S(2)}) collective-permute-start(bf16[264,256]{1,0:T(8,128)(2,1)S(1)} %get-tuple-element.21), channel_id=1, source_target_pairs={{0,8},{1,9},{4,12},{5,13},{8,0},{9,1},{12,4},{13,5},{2,10},{3,11},... | collective-permute-start | bytes 405512 | tf_op jit(solution)/shard_map/ppermute | solution.py:217
  6.7 0.0 collective-permute-start.1
  6.7 0.7 %shard_map.117 = (bf16[264,256]{1,0:T(8,128)(2,1)S(1)}, bf16[264,256]{1,0:T(8,128)(2,1)S(1)}) custom-call(s32[1,1024]{1,0:T(1,128)S(1)} %get-tuple-element.20.place.refs_0_, bf16[8,1024]{1,0:T(8,128)(2,1)S(1)} %get-tuple-element.23.refs_1_, bf16[1024,256]{1,0:T(8,128)(2,1)S(1)} %get-tuple-element.24.refs_2_), custom_call_target="tpu_custom_call" | custom-call | flops 268435456 | bytes 815104 | tf_op jit(solution)/shard_map/pallas_call | solution.py:222
  7.3 3.2 %collective-permute-start.2 = (bf16[264,256]{1,0:T(8,128)(2,1)S(1)}, bf16[264,256]{1,0:T(8,128)(2,1)S(1)}, u32[]{:S(2)}, u32[]{:S(2)}) collective-permute-start(bf16[264,256]{1,0:T(8,128)(2,1)S(1)} %get-tuple-element.29), channel_id=1, source_target_pairs={{0,12},{1,13},{4,8},{5,9},{8,4},{9,5},{12,0},{13,1},{2,14},{3,15},... | collective-permute-start | bytes 405512 | tf_op jit(solution)/shard_map/ppermute | solution.py:217
  10.5 0.6 %collective-permute-start.3 = (bf16[264,256]{1,0:T(8,128)(2,1)S(1)}, bf16[264,256]{1,0:T(8,128)(2,1)S(1)}, u32[]{:S(2)}, u32[]{:S(2)}) collective-permute-start(bf16[264,256]{1,0:T(8,128)(2,1)S(1)} %get-tuple-element.30), channel_id=1, source_target_pairs={{0,13},{1,12},{4,9},{5,8},{8,5},{9,4},{12,1},{13,0},{2,15},{3,14},... | collective-permute-start | bytes 405512 | tf_op jit(solution)/shard_map/ppermute | solution.py:217
  11.1 0.7 %reshape.39 = f32[2048]{0:T(1024)S(1)} convert(bf16[2048]{0:T(1024)(128)(2,1)} %param.11) | non-fusion elementwise | flops 2048 | bytes 12288 | tf_op jit(solution)/shard_map/reshape | solution.py:295
  11.8 3.9 %shard_map.114 = f32[1,1024]{1,0:T(1,128)S(1)} custom-call(s32[1,1024]{1,0:T(1,128)S(1)} %get-tuple-element.20.place.refs_0_, f32[1,2048]{1,0:T(1,128)S(1)} %bitcast.8, bf16[1024,2048]{1,0:T(8,128)(2,1)} %refs_7_.1), custom_call_target="tpu_custom_call" | custom-call | tf_op jit(solution)/shard_map/pallas_call | solution.py:222
  15.7 4.9 %psum.7.refs_3_.refs_5_ = f32[1,1024]{1,0:T(1,128)S(1)} all-reduce(f32[1,1024]{1,0:T(1,128)S(1)} %shard_map.114), channel_id=1, replica_groups=mesh['groups'=2,'rows'=4,'feat'=2,'ent'=2] {'feat'}, use_global_device_ids=true, to_apply=%region_0.0 | all-reduce | flops 1024 | bytes 8192 | tf_op jit(solution)/shard_map/psum | solution.py:305
  20.7 1.2 %shard_map.115 = (bf16[264,256]{1,0:T(8,128)(2,1)S(1)}, bf16[264,256]{1,0:T(8,128)(2,1)S(1)}, bf16[264,256]{1,0:T(8,128)(2,1)S(1)}, bf16[264,256]{1,0:T(8,128)(2,1)S(1)}) custom-call(s32[1,1024]{1,0:T(1,128)S(1)} %get-tuple-element.20.place.refs_0_, bf16[8,1024]{1,0:T(8,128)(2,1)S(1)} %get-tuple-element.23.refs_1_, ...), custom_call_target="tpu_custom_call" | custom-call | tf_op jit(solution)/shard_map/pallas_call | solution.py:222
  21.9 0.1 collective-permute-start.4
  22.0 0.6 %collective-permute-done.refs_1_.refs_3_ = bf16[264,256]{1,0:T(8,128)(2,1)S(1)} collective-permute-done((bf16[264,256]{1,0:T(8,128)(2,1)S(1)}, bf16[264,256]{1,0:T(8,128)(2,1)S(1)}, u32[]{:S(2)}, u32[]{:S(2)}) %collective-permute-start) | collective-permute-done | bytes 135200 | tf_op jit(solution)/shard_map/ppermute | solution.py:217
  22.7 0.3 collective-permute-start.5
  23.0 0.9 %collective-permute-done.1.refs_2_.refs_4_ = bf16[264,256]{1,0:T(8,128)(2,1)S(1)} collective-permute-done((bf16[264,256]{1,0:T(8,128)(2,1)S(1)}, bf16[264,256]{1,0:T(8,128)(2,1)S(1)}, u32[]{:S(2)}, u32[]{:S(2)}) %collective-permute-start.1) | collective-permute-done | bytes 135200 | tf_op jit(solution)/shard_map/ppermute | solution.py:217
  23.9 1.5 %collective-permute-start.6 = (bf16[264,256]{1,0:T(8,128)(2,1)S(1)}, bf16[264,256]{1,0:T(8,128)(2,1)S(1)}, u32[]{:S(2)}, u32[]{:S(2)}) collective-permute-start(bf16[264,256]{1,0:T(8,128)(2,1)S(1)} %get-tuple-element.33), channel_id=1, source_target_pairs={{0,1},{1,0},{4,5},{5,4},{8,9},{9,8},{12,13},{13,12},{2,3},{3,2},{6... | collective-permute-start | bytes 405512 | tf_op jit(solution)/shard_map/ppermute | solution.py:217
  25.4 0.0 copy-done.1
  25.4 0.6 %shard_map.116 = (f32[1,256]{1,0:T(1,128)S(1)}, f32[1,256]{1,0:T(1,128)S(1)}, f32[1,256]{1,0:T(1,128)S(1)}) custom-call(f32[512,256]{1,0:T(8,128)S(1)} %copy-done.1, bf16[264,256]{1,0:T(8,128)(2,1)S(1)} %collective-permute-done.refs_1_.refs_3_, bf16[264,256]{1,0:T(8,128)(2,1)S(1)} %collective-permute-done.1.refs_2_.refs_4_, ...), custom_call_target="tpu_custom_call" | custom-call | tf_op jit(solution)/shard_map/pallas_call | solution.py:222
  26.0 0.0 collective-permute-done.2.refs_4_.refs_6_
  26.0 0.0 collective-permute-done.3.refs_5_.refs_7_
  26.0 2.1 %collective-permute-done.4.refs_6_.refs_8_ = bf16[264,256]{1,0:T(8,128)(2,1)S(1)} collective-permute-done((bf16[264,256]{1,0:T(8,128)(2,1)S(1)}, bf16[264,256]{1,0:T(8,128)(2,1)S(1)}, u32[]{:S(2)}, u32[]{:S(2)}) %collective-permute-start.4) | collective-permute-done | bytes 135200 | tf_op jit(solution)/shard_map/ppermute | solution.py:217
  28.2 2.4 %collective-permute-done.5.refs_7_.refs_9_ = bf16[264,256]{1,0:T(8,128)(2,1)S(1)} collective-permute-done((bf16[264,256]{1,0:T(8,128)(2,1)S(1)}, bf16[264,256]{1,0:T(8,128)(2,1)S(1)}, u32[]{:S(2)}, u32[]{:S(2)}) %collective-permute-start.5) | collective-permute-done | bytes 135200 | tf_op jit(solution)/shard_map/ppermute | solution.py:217
  30.6 0.0 collective-permute-done.6.refs_8_.refs_10_
  30.6 0.0 copy-start
  30.6 0.0 copy-start.2
  30.6 0.0 copy-start.3
  30.6 0.0 copy-start.4
  30.6 0.0 copy-start.5
  30.6 0.9 %shard_map.118 = f32[16,1,256]{2,1,0:T(1,128)S(1)} custom-call(f32[512,256]{1,0:T(8,128)S(1)} %copy-done.1, f32[1,256]{1,0:T(1,128)S(1)} %get-tuple-element.26.refs_1_, f32[1,256]{1,0:T(1,128)S(1)} %get-tuple-element.27.refs_2_, f32[1,256]{1,0:T(1,128)S(1)} %get-tuple-element.28.refs_3_, bf16[264,256]{1,0:T(8,128)(2,1)S(1)} %collective-permute-done.2.refs_4_.refs_6_, ...), custom_call_target="tpu_custom_call" | custom-call | flops 4294967296 | bytes 1219584 | tf_op jit(solution)/shard_map/pallas_call | solution.py:222
  31.6 12.0 %all_to_all.10.refs_6_ = f32[16,1,256]{2,1,0:T(1,128)S(1)} all-to-all(f32[16,1,256]{2,1,0:T(1,128)S(1)} %shard_map.118), channel_id=1, replica_groups=mesh['groups'=2,'rows'=4,'feat'=2,'ent'=2] {'rows','feat','ent'}, dimensions={0} | all-to-all | bytes 32768 | tf_op jit(solution)/shard_map/all_to_all | solution.py:331
  43.6 0.0 copy-done
  43.6 0.0 copy-done.2
  43.6 0.0 copy-done.3
  43.6 0.0 copy-done.4
  43.6 0.0 copy-done.5
  43.6 1.0 %shard_map.119 = f32[8,1,2304]{2,1,0:T(1,128)S(1)} custom-call(s32[1,1024]{1,0:T(1,128)S(1)} %bitcast.11, s32[1,1024]{1,0:T(1,128)S(1)} %bitcast.13, s32[2,1024]{1,0:T(2,128)S(1)} %get-tuple-element.19.refs_2_, s32[1,1024]{1,0:T(1,128)S(1)} %bitcast.14, s32[1,1024]{1,0:T(1,128)S(1)} %bitcast.15, f32[1,1024]{1,0:T(1,128)S(1)} %psum.7.refs_3_.refs_5_, ...), custom_call_target="tpu_custom_call" | custom-call | flops 67108864 | bytes 4313088 | tf_op jit(solution)/shard_map/pallas_call | solution.py:222
  44.7 8.4 %all_to_all.11.refs_2_ = f32[8,1,2304]{2,1,0:T(1,128)S(1)} all-to-all(f32[8,1,2304]{2,1,0:T(1,128)S(1)} %shard_map.119), channel_id=1, replica_groups=mesh['groups'=2,'rows'=4,'feat'=2,'ent'=2] {'rows','ent'}, dimensions={0} | all-to-all | bytes 147456 | tf_op jit(solution)/shard_map/all_to_all | solution.py:348
  53.1 2.1 %shard_map.120 = (f32[1,2048]{1,0:T(1,128)}, f32[512,256]{1,0:T(8,128)}) custom-call(f32[512,256]{1,0:T(8,128)S(1)} %copy-done.1, f32[1,2048]{1,0:T(1,128)S(1)} %bitcast.9, f32[8,1,2304]{2,1,0:T(1,128)S(1)} %all_to_all.11.refs_2_, bf16[264,256]{1,0:T(8,128)(2,1)S(1)} %collective-permute-done.refs_1_.refs_3_, ...), custom_call_target="tpu_custom_call" | custom-call | flops 1073741824 | bytes 2220032 | tf_op jit(solution)/shard_map/pallas_call | solution.py:222
Async XLA Ops:
  0.6 24.7 %copy-start.1 = (f32[512,256]{1,0:T(8,128)S(1)}, f32[512,256]{1,0:T(8,128)}, u32[]{:S(2)}) copy-start(f32[512,256]{1,0:T(8,128)} %refs_0_.5) | copy-start | bytes 1572868
  2.5 20.1 %collective-permute-start = (bf16[264,256]{1,0:T(8,128)(2,1)S(1)}, bf16[264,256]{1,0:T(8,128)(2,1)S(1)}, u32[]{:S(2)}, u32[]{:S(2)}) collective-permute-start(bf16[264,256]{1,0:T(8,128)(2,1)S(1)} %get-tuple-element.21), channel_id=1, source_target_pairs={{0,8},{1,9},{4,12},{5,13},{8,0},{9,1},{12,4},{13,5},{2,10},{3,11},... | collective-permute-start | bytes 405512 | tf_op jit(solution)/shard_map/ppermute | solution.py:217
  6.7 17.2 %collective-permute-start.1 = (bf16[264,256]{1,0:T(8,128)(2,1)S(1)}, bf16[264,256]{1,0:T(8,128)(2,1)S(1)}, u32[]{:S(2)}, u32[]{:S(2)}) collective-permute-start(bf16[264,256]{1,0:T(8,128)(2,1)S(1)} %get-tuple-element.22), channel_id=1, source_target_pairs={{0,9},{1,8},{4,13},{5,12},{8,1},{9,0},{12,5},{13,4},{2,11},{3,10},... | collective-permute-start | bytes 405512 | tf_op jit(solution)/shard_map/ppermute | solution.py:217
  7.3 18.7 %collective-permute-start.2 = (bf16[264,256]{1,0:T(8,128)(2,1)S(1)}, bf16[264,256]{1,0:T(8,128)(2,1)S(1)}, u32[]{:S(2)}, u32[]{:S(2)}) collective-permute-start(bf16[264,256]{1,0:T(8,128)(2,1)S(1)} %get-tuple-element.29), channel_id=1, source_target_pairs={{0,12},{1,13},{4,8},{5,9},{8,4},{9,5},{12,0},{13,1},{2,14},{3,15},... | collective-permute-start | bytes 405512 | tf_op jit(solution)/shard_map/ppermute | solution.py:217
  10.5 15.5 %collective-permute-start.3 = (bf16[264,256]{1,0:T(8,128)(2,1)S(1)}, bf16[264,256]{1,0:T(8,128)(2,1)S(1)}, u32[]{:S(2)}, u32[]{:S(2)}) collective-permute-start(bf16[264,256]{1,0:T(8,128)(2,1)S(1)} %get-tuple-element.30), channel_id=1, source_target_pairs={{0,13},{1,12},{4,9},{5,8},{8,5},{9,4},{12,1},{13,0},{2,15},{3,14},... | collective-permute-start | bytes 405512 | tf_op jit(solution)/shard_map/ppermute | solution.py:217
  21.9 6.2 %collective-permute-start.4 = (bf16[264,256]{1,0:T(8,128)(2,1)S(1)}, bf16[264,256]{1,0:T(8,128)(2,1)S(1)}, u32[]{:S(2)}, u32[]{:S(2)}) collective-permute-start(bf16[264,256]{1,0:T(8,128)(2,1)S(1)} %get-tuple-element.31), channel_id=1, source_target_pairs={{0,5},{1,4},{4,1},{5,0},{8,13},{9,12},{12,9},{13,8},{2,7},{3,6},{6... | collective-permute-start | bytes 405512 | tf_op jit(solution)/shard_map/ppermute | solution.py:217
  22.7 7.9 %collective-permute-start.5 = (bf16[264,256]{1,0:T(8,128)(2,1)S(1)}, bf16[264,256]{1,0:T(8,128)(2,1)S(1)}, u32[]{:S(2)}, u32[]{:S(2)}) collective-permute-start(bf16[264,256]{1,0:T(8,128)(2,1)S(1)} %get-tuple-element.32), channel_id=1, source_target_pairs={{0,4},{1,5},{4,0},{5,1},{8,12},{9,13},{12,8},{13,9},{2,6},{3,7},{6... | collective-permute-start | bytes 405512 | tf_op jit(solution)/shard_map/ppermute | solution.py:217
  23.9 6.7 %collective-permute-start.6 = (bf16[264,256]{1,0:T(8,128)(2,1)S(1)}, bf16[264,256]{1,0:T(8,128)(2,1)S(1)}, u32[]{:S(2)}, u32[]{:S(2)}) collective-permute-start(bf16[264,256]{1,0:T(8,128)(2,1)S(1)} %get-tuple-element.33), channel_id=1, source_target_pairs={{0,1},{1,0},{4,5},{5,4},{8,9},{9,8},{12,13},{13,12},{2,3},{3,2},{6... | collective-permute-start | bytes 405512 | tf_op jit(solution)/shard_map/ppermute | solution.py:217
  30.6 13.0 %copy-start = (bf16[1024,2048]{1,0:T(8,128)(2,1)S(1)}, bf16[1024,2048]{1,0:T(8,128)(2,1)}, u32[]{:S(2)}) copy-start(bf16[1024,2048]{1,0:T(8,128)(2,1)} %refs_7_.1) | copy-start | bytes 12582916
  30.6 13.0 %copy-start.2 = (s32[1024,1]{0,1:T(1,128)S(1)}, s32[1024,1]{0,1:T(1,128)}, u32[]{:S(2)}) copy-start(s32[1024,1]{0,1:T(1,128)} %param.14) | copy-start | bytes 12292
  30.6 13.0 %copy-start.3 = (s32[1024,1]{0,1:T(1,128)S(1)}, s32[1024,1]{0,1:T(1,128)}, u32[]{:S(2)}) copy-start(s32[1024,1]{0,1:T(1,128)} %param.16) | copy-start | bytes 12292
  30.6 13.0 %copy-start.4 = (s32[1024]{0:T(1024)S(1)}, s32[1024]{0:T(1024)}, u32[]{:S(2)}) copy-start(s32[1024]{0:T(1024)} %param.18) | copy-start | bytes 12292
  30.6 13.0 %copy-start.5 = (s32[1024]{0:T(1024)S(1)}, s32[1024]{0:T(1024)}, u32[]{:S(2)}) copy-start(s32[1024]{0:T(1024)} %param.19) | copy-start | bytes 12292

commit v13 on v12

--- a/solution.py
+++ b/solution.py
@@ -118,16 +118,17 @@
 
 
 def margin_kernel(place, weight, features, margin, copies, sems):
-    parts = copies.shape[0]
-    step = copies.shape[1]
+    parts, step = copies.shape[0], copies.shape[1]
     moves = [
         pltpu.make_async_copy(features.at[pl.ds(i * step, step)], copies.at[i], sems.at[i]) for i in range(parts)
     ]
-    for move in moves:
+    for move in moves[:2]:
         move.start()
     wide = jnp.broadcast_to(weight[...], (16, weight.shape[1])).astype(BF16)
     for i in range(parts):
         moves[i].wait()
+        if i + 2 < parts:
+            moves[i + 2].start()
         margin[:, i * step : (i + 1) * step] = lanes_dot(wide, copies[i])[0:1]
 
 
@@ -192,7 +193,7 @@
 
 
 def grads_kernel(order, capacity, scale, coefs, weight, came, *refs):
-    chunks, grad_global, grad_coefs = refs[:-2], refs[-2], refs[-1]
+    chunks, grad_global, grad_coefs, done, sems = refs[:-4], refs[-4], refs[-3], refs[-2], refs[-1]
     entities = coefs.shape[0]
     mine = lax.axis_index(HOME)
     resids = xor_rows(jnp.concatenate([came[h][:, :capacity] for h in range(len(order))], axis=0), mine)
@@ -200,30 +201,34 @@
     for h in range(1, len(order)):
         summed = summed + came[h][:, capacity:]
     grad_global[...] = summed * scale + 4.0 * weight[...]
-    highs, lows, feats = [], [], []
-    for chunk, k in zip(chunks, order):
-        here = chunk_ids(chunk, capacity)
-        blocks = [low_hot(here - first, min(256, entities)) for first in range(0, entities, 256)]
-        high, low = halves(resids[k : k + 1])
-        highs.append(jnp.concatenate([jnp.where(hits, high, jnp.zeros((), BF16)) for hits in blocks], axis=0))
-        lows.append(jnp.concatenate([jnp.where(hits, low, jnp.zeros((), BF16)) for hits in blocks], axis=0))
-        feats.append(chunk[:capacity])
-    spread = jnp.concatenate([jnp.concatenate(highs, axis=1), jnp.concatenate(lows, axis=1)], axis=0)
-    both = plain_dot(spread, jnp.concatenate(feats, axis=0))
-    grad_coefs[...] = coefs[...] + both[:entities] + both[entities:]
+    step = min(256, entities)
+    feats = jnp.concatenate([chunk[:capacity] for chunk in chunks], axis=0)
+    ids = jnp.concatenate([chunk_ids(chunk, capacity) for chunk in chunks], axis=1)
+    high, low = halves(jnp.concatenate([resids[k : k + 1] for k in order], axis=1))
+    moves = []
+    for i in range(entities // step):
+        hits = low_hot(ids - i * step, step)
+        spread = [jnp.where(hits, part, jnp.zeros((), BF16)) for part in (high, low)]
+        both = plain_dot(jnp.concatenate(spread, axis=0), feats)
+        here = slice(i * step, (i + 1) * step)
+        done[here] = coefs[here] + both[:step] + both[step:]
+        moves.append(pltpu.make_async_copy(done.at[here], grad_coefs.at[here], sems.at[i]))
+        moves[i].start()
+    for move in moves:
+        move.wait()
 
 
 def xor_send(x, axes, size, k):
     return x if k == 0 else lax.ppermute(x, axes, [(i, i ^ k) for i in range(size)])
 
 
-def call(kernel, out_shape, operands, in_specs, flops=0, scratch=(), hidden=False):
+def call(kernel, out_shape, operands, in_specs, flops=0, scratch=(), hidden=False, out_specs=None):
     moved = 0 if hidden else sum(x.size * x.dtype.itemsize for x in (*operands, *out_shape))
     return pl.pallas_call(
         kernel,
         out_shape=out_shape,
         in_specs=in_specs,
-        out_specs=[VMEM] * len(out_shape),
+        out_specs=out_specs or [VMEM] * len(out_shape),
         scratch_shapes=scratch,
         compiler_params=PARAMS,
         cost_estimate=pl.CostEstimate(flops=flops, bytes_accessed=moved, transcendentals=0),
@@ -256,8 +261,8 @@
         return lambda *refs: kernel(*args, *refs)
 
     row = pltpu.VMEM((1, rows_here), jnp.int32)
-    half, early = owners // 2, 3 * owners // 4
-    first, second, near = list(range(half, early)), list(range(early, owners)), list(reversed(range(half)))
+    half = owners // 2
+    first, second, near = [half], list(range(half + 1, owners)), list(reversed(range(half)))
     chunk = shape(capacity + IDS, width, dtype=BF16)
     flops = len(first) * 2 * capacity * rows_here * width
 
@@ -311,20 +316,21 @@
         hidden=True,
     )
     near_chunks = [xor_send(x, HOME, owners, k) for k, x in zip(near, near_chunks)]
-    order = first + near[-1:] + second + near[:-1]
-    chunks = chunks[: len(first)] + near_chunks[-1:] + chunks[len(first) :] + near_chunks[:-1]
-    came_early = len(first) + 1
+    chunks = dict(zip(first + second + near, chunks + near_chunks))
+    early = (first + second)[: half // 2] + near[-1:]
+    late = (first + second)[half // 2 :] + near[:-1]
+    order = early + late
     scores = call(
         partial(early_kernel, capacity),
-        [shape(1, capacity)] * came_early,
-        (coefs, *chunks[:came_early]),
-        [VMEM] * (1 + came_early),
+        [shape(1, capacity)] * len(early),
+        (coefs, *(chunks[k] for k in early)),
+        [VMEM] * (1 + len(early)),
         hidden=True,
     )
     (scores,) = call(
         partial(scores_kernel, order, capacity, n_feat, n_ent),
         [shape(n_feat * owners, 1, capacity)],
-        (coefs, *scores, *chunks[came_early:]),
+        (coefs, *scores, *(chunks[k] for k in late)),
         [VMEM] * (1 + owners),
         flops=16 * coefs.size * owners * capacity,
     )
@@ -349,8 +355,10 @@
     grad_global, grad_coefs = call(
         partial(grads_kernel, order, capacity, 1.0 / math.sqrt(rows_here * owners)),
         [shape(1, columns), shape(*coefs.shape)],
-        (coefs, weight, came, *chunks),
+        (coefs, weight, came, *(chunks[k] for k in order)),
         [VMEM] * (3 + owners),
+        out_specs=[VMEM, HBM],
+        scratch=[pltpu.VMEM(coefs.shape, F32), pltpu.SemaphoreType.DMA((-(-coefs.shape[0] // 256),))],
         flops=4 * coefs.size * owners * capacity,
     )
     return (grad_global.reshape(columns), grad_coefs)

time: 55.4 us -> 55.5 us (level)
  Pallas kernels: 12.4 us -> 13 us
    pallas_call x8, Pallas kernels: 12.4 us -> 13 us  [call(): pl.pallas_call(kernel, out_shape=out_shape, in_specs=in_specs, out_specs=...]
where the time goes in v13:
time: 55.5 us; the launch traced here: 55.2 us
  blocking collectives  24.9 us (45%)
  Pallas kernels  13 us (23%)
  starting transfers between devices  10.1 us (18%)
  waiting for transfers between devices  5.77 us (10%)
  between operations  0.76 us (1%)
  other arithmetic  0.69 us (1%)
    pallas_call x8, Pallas kernels, call(): pl.pallas_call(kernel, out_shape=out_shape, in_specs=in_specs, out_specs=...  13 us
    all_to_all x1, blocking collectives, body(): lax.all_to_all(scores, EVERY, split_axis=0, concat_axis=0, tiled=True)  11.5 us
    ppermute x7, starting transfers between devices, xor_send(): lax.ppermute(x, axes, [(i, i ^ k) for i in range(size)])  10.1 us
    all_to_all x1, blocking collectives, body(): came = lax.all_to_all(sent, HOME, split_axis=0, concat_axis=0, tiled=True)  8.4 us
    ppermute x7, waiting for transfers between devices, xor_send(): lax.ppermute(x, axes, [(i, i ^ k) for i in range(size)])  5.77 us
    psum x1, blocking collectives, body(): global_total = lax.psum(global_part, 'feat')  4.95 us
  transfers between devices with their start and end apart: 7, of which 4 were waited for; matrix products, arithmetic and copies ran while one was open for 1% of the time, Pallas kernels for 12%

profile of v13, /device:TPU:0, one launch (start us, length us, event | category | flops | bytes accessed | tf_op | source)
XLA Modules:
  0.0 55.2 jit_solution(1124674668708198732)
XLA Ops:
  0.6 0.0 copy-start.1
  0.6 1.6 %shard_map.113 = (s32[2,1024]{1,0:T(2,128)S(1)}, s32[1,1024]{1,0:T(1,128)S(1)}, bf16[8,1024]{1,0:T(8,128)(2,1)S(1)}, bf16[1024,256]{1,0:T(8,128)(2,1)S(1)}, bf16[264,256]{1,0:T(8,128)(2,1)S(1)}) custom-call(s32[1,1024]{1,0:T(1,128)} %bitcast.10, s32[1,1024]{1,0:T(1,128)} %bitcast.12, s32[1,1024]{1,0:T(1,128)} %bitcast.16, s32[1,1024]{1,0:T(1,128)} %bitcast.17, ...), custom_call_target="tpu_custom_call" | custom-call | flops 134217728 | bytes 1228800 | tf_op jit(solution)/shard_map/pallas_call | solution.py:227
  2.3 4.1 %collective-permute-start = (bf16[264,256]{1,0:T(8,128)(2,1)S(1)}, bf16[264,256]{1,0:T(8,128)(2,1)S(1)}, u32[]{:S(2)}, u32[]{:S(2)}) collective-permute-start(bf16[264,256]{1,0:T(8,128)(2,1)S(1)} %get-tuple-element.21), channel_id=1, source_target_pairs={{0,8},{1,9},{4,12},{5,13},{8,0},{9,1},{12,4},{13,5},{2,10},{3,11},... | collective-permute-start | bytes 405512 | tf_op jit(solution)/shard_map/ppermute | solution.py:222
  6.4 1.0 %shard_map.115 = (bf16[264,256]{1,0:T(8,128)(2,1)S(1)}, bf16[264,256]{1,0:T(8,128)(2,1)S(1)}, bf16[264,256]{1,0:T(8,128)(2,1)S(1)}) custom-call(s32[1,1024]{1,0:T(1,128)S(1)} %get-tuple-element.20.place.refs_0_, bf16[8,1024]{1,0:T(8,128)(2,1)S(1)} %get-tuple-element.22.refs_1_, bf16[1024,256]{1,0:T(8,128)(2,1)S(1)} %get-tuple-element.23.refs_2_), custom_call_target="tpu_custom_call" | custom-call | flops 134217728 | bytes 950272 | tf_op jit(solution)/shard_map/pallas_call | solution.py:227
  7.3 0.1 collective-permute-start.1
  7.4 3.1 %collective-permute-start.2 = (bf16[264,256]{1,0:T(8,128)(2,1)S(1)}, bf16[264,256]{1,0:T(8,128)(2,1)S(1)}, u32[]{:S(2)}, u32[]{:S(2)}) collective-permute-start(bf16[264,256]{1,0:T(8,128)(2,1)S(1)} %get-tuple-element.29), channel_id=1, source_target_pairs={{0,12},{1,13},{4,8},{5,9},{8,4},{9,5},{12,0},{13,1},{2,14},{3,15},... | collective-permute-start | bytes 405512 | tf_op jit(solution)/shard_map/ppermute | solution.py:222
  10.5 0.6 %collective-permute-start.3 = (bf16[264,256]{1,0:T(8,128)(2,1)S(1)}, bf16[264,256]{1,0:T(8,128)(2,1)S(1)}, u32[]{:S(2)}, u32[]{:S(2)}) collective-permute-start(bf16[264,256]{1,0:T(8,128)(2,1)S(1)} %get-tuple-element.30), channel_id=1, source_target_pairs={{0,13},{1,12},{4,9},{5,8},{8,5},{9,4},{12,1},{13,0},{2,15},{3,14},... | collective-permute-start | bytes 405512 | tf_op jit(solution)/shard_map/ppermute | solution.py:222
  11.1 0.7 %reshape.39 = f32[2048]{0:T(1024)S(1)} convert(bf16[2048]{0:T(1024)(128)(2,1)} %param.11) | non-fusion elementwise | flops 2048 | bytes 12288 | tf_op jit(solution)/shard_map/reshape | solution.py:300
  11.8 3.9 %shard_map.114 = f32[1,1024]{1,0:T(1,128)S(1)} custom-call(s32[1,1024]{1,0:T(1,128)S(1)} %get-tuple-element.20.place.refs_0_, f32[1,2048]{1,0:T(1,128)S(1)} %bitcast.8, bf16[1024,2048]{1,0:T(8,128)(2,1)} %refs_7_.1), custom_call_target="tpu_custom_call" | custom-call | tf_op jit(solution)/shard_map/pallas_call | solution.py:227
  15.7 4.9 %psum.7.refs_3_.refs_5_ = f32[1,1024]{1,0:T(1,128)S(1)} all-reduce(f32[1,1024]{1,0:T(1,128)S(1)} %shard_map.114), channel_id=1, replica_groups=mesh['groups'=2,'rows'=4,'feat'=2,'ent'=2] {'feat'}, use_global_device_ids=true, to_apply=%region_0.0 | all-reduce | flops 1024 | bytes 8192 | tf_op jit(solution)/shard_map/psum | solution.py:310
  20.6 1.2 %shard_map.116 = (bf16[264,256]{1,0:T(8,128)(2,1)S(1)}, bf16[264,256]{1,0:T(8,128)(2,1)S(1)}, bf16[264,256]{1,0:T(8,128)(2,1)S(1)}, bf16[264,256]{1,0:T(8,128)(2,1)S(1)}) custom-call(s32[1,1024]{1,0:T(1,128)S(1)} %get-tuple-element.20.place.refs_0_, bf16[8,1024]{1,0:T(8,128)(2,1)S(1)} %get-tuple-element.22.refs_1_, ...), custom_call_target="tpu_custom_call" | custom-call | tf_op jit(solution)/shard_map/pallas_call | solution.py:227
  21.9 0.1 collective-permute-start.4
  22.0 0.4 collective-permute-done.refs_1_.refs_3_
  22.4 0.7 %collective-permute-start.5 = (bf16[264,256]{1,0:T(8,128)(2,1)S(1)}, bf16[264,256]{1,0:T(8,128)(2,1)S(1)}, u32[]{:S(2)}, u32[]{:S(2)}) collective-permute-start(bf16[264,256]{1,0:T(8,128)(2,1)S(1)} %get-tuple-element.32), channel_id=1, source_target_pairs={{0,4},{1,5},{4,0},{5,1},{8,12},{9,13},{12,8},{13,9},{2,6},{3,7},{6... | collective-permute-start | bytes 405512 | tf_op jit(solution)/shard_map/ppermute | solution.py:222
  23.1 0.6 %collective-permute-done.1.refs_2_.refs_4_ = bf16[264,256]{1,0:T(8,128)(2,1)S(1)} collective-permute-done((bf16[264,256]{1,0:T(8,128)(2,1)S(1)}, bf16[264,256]{1,0:T(8,128)(2,1)S(1)}, u32[]{:S(2)}, u32[]{:S(2)}) %collective-permute-start.1) | collective-permute-done | bytes 135200 | tf_op jit(solution)/shard_map/ppermute | solution.py:222
  23.6 1.5 %collective-permute-start.6 = (bf16[264,256]{1,0:T(8,128)(2,1)S(1)}, bf16[264,256]{1,0:T(8,128)(2,1)S(1)}, u32[]{:S(2)}, u32[]{:S(2)}) collective-permute-start(bf16[264,256]{1,0:T(8,128)(2,1)S(1)} %get-tuple-element.33), channel_id=1, source_target_pairs={{0,1},{1,0},{4,5},{5,4},{8,9},{9,8},{12,13},{13,12},{2,3},{3,2},{6... | collective-permute-start | bytes 405512 | tf_op jit(solution)/shard_map/ppermute | solution.py:222
  25.1 0.0 copy-done.1
  25.1 0.6 %shard_map.117 = (f32[1,256]{1,0:T(1,128)S(1)}, f32[1,256]{1,0:T(1,128)S(1)}, f32[1,256]{1,0:T(1,128)S(1)}) custom-call(f32[512,256]{1,0:T(8,128)S(1)} %copy-done.1, bf16[264,256]{1,0:T(8,128)(2,1)S(1)} %collective-permute-done.refs_1_.refs_3_, bf16[264,256]{1,0:T(8,128)(2,1)S(1)} %collective-permute-done.1.refs_2_.refs_4_, ...), custom_call_target="tpu_custom_call" | custom-call | tf_op jit(solution)/shard_map/pallas_call | solution.py:227
  25.7 0.0 collective-permute-done.2.refs_4_.refs_6_
  25.7 0.0 collective-permute-done.3.refs_5_.refs_7_
  25.8 2.2 %collective-permute-done.4.refs_6_.refs_8_ = bf16[264,256]{1,0:T(8,128)(2,1)S(1)} collective-permute-done((bf16[264,256]{1,0:T(8,128)(2,1)S(1)}, bf16[264,256]{1,0:T(8,128)(2,1)S(1)}, u32[]{:S(2)}, u32[]{:S(2)}) %collective-permute-start.4) | collective-permute-done | bytes 135200 | tf_op jit(solution)/shard_map/ppermute | solution.py:222
  28.0 2.6 %collective-permute-done.5.refs_7_.refs_9_ = bf16[264,256]{1,0:T(8,128)(2,1)S(1)} collective-permute-done((bf16[264,256]{1,0:T(8,128)(2,1)S(1)}, bf16[264,256]{1,0:T(8,128)(2,1)S(1)}, u32[]{:S(2)}, u32[]{:S(2)}) %collective-permute-start.5) | collective-permute-done | bytes 135200 | tf_op jit(solution)/shard_map/ppermute | solution.py:222
  30.6 0.0 collective-permute-done.6.refs_8_.refs_10_
  30.6 0.0 copy-start
  30.6 0.0 copy-start.2
  30.6 0.0 copy-start.3
  30.6 0.0 copy-start.4
  30.6 0.0 copy-start.5
  30.6 0.9 %shard_map.118 = f32[16,1,256]{2,1,0:T(1,128)S(1)} custom-call(f32[512,256]{1,0:T(8,128)S(1)} %copy-done.1, f32[1,256]{1,0:T(1,128)S(1)} %get-tuple-element.26.refs_1_, f32[1,256]{1,0:T(1,128)S(1)} %get-tuple-element.27.refs_2_, f32[1,256]{1,0:T(1,128)S(1)} %get-tuple-element.28.refs_3_, bf16[264,256]{1,0:T(8,128)(2,1)S(1)} %collective-permute-done.2.refs_4_.refs_6_, ...), custom_call_target="tpu_custom_call" | custom-call | flops 4294967296 | bytes 1219584 | tf_op jit(solution)/shard_map/pallas_call | solution.py:227
  31.5 11.5 %all_to_all.10.refs_6_ = f32[16,1,256]{2,1,0:T(1,128)S(1)} all-to-all(f32[16,1,256]{2,1,0:T(1,128)S(1)} %shard_map.118), channel_id=1, replica_groups=mesh['groups'=2,'rows'=4,'feat'=2,'ent'=2] {'rows','feat','ent'}, dimensions={0} | all-to-all | bytes 32768 | tf_op jit(solution)/shard_map/all_to_all | solution.py:337
  43.0 0.0 copy-done
  43.0 0.0 copy-done.2
  43.1 0.0 copy-done.3
  43.1 0.0 copy-done.4
  43.1 0.0 copy-done.5
  43.1 1.0 %shard_map.119 = f32[8,1,2304]{2,1,0:T(1,128)S(1)} custom-call(s32[1,1024]{1,0:T(1,128)S(1)} %bitcast.11, s32[1,1024]{1,0:T(1,128)S(1)} %bitcast.13, s32[2,1024]{1,0:T(2,128)S(1)} %get-tuple-element.19.refs_2_, s32[1,1024]{1,0:T(1,128)S(1)} %bitcast.14, s32[1,1024]{1,0:T(1,128)S(1)} %bitcast.15, f32[1,1024]{1,0:T(1,128)S(1)} %psum.7.refs_3_.refs_5_, ...), custom_call_target="tpu_custom_call" | custom-call | flops 67108864 | bytes 4313088 | tf_op jit(solution)/shard_map/pallas_call | solution.py:227
  44.1 8.4 %all_to_all.11.refs_2_ = f32[8,1,2304]{2,1,0:T(1,128)S(1)} all-to-all(f32[8,1,2304]{2,1,0:T(1,128)S(1)} %shard_map.119), channel_id=1, replica_groups=mesh['groups'=2,'rows'=4,'feat'=2,'ent'=2] {'rows','ent'}, dimensions={0} | all-to-all | bytes 147456 | tf_op jit(solution)/shard_map/all_to_all | solution.py:354
  52.5 2.7 %shard_map.120 = (f32[1,2048]{1,0:T(1,128)}, f32[512,256]{1,0:T(8,128)}) custom-call(f32[512,256]{1,0:T(8,128)S(1)} %copy-done.1, f32[1,2048]{1,0:T(1,128)S(1)} %bitcast.9, f32[8,1,2304]{2,1,0:T(1,128)S(1)} %all_to_all.11.refs_2_, bf16[264,256]{1,0:T(8,128)(2,1)S(1)} %collective-permute-done.refs_1_.refs_3_, ...), custom_call_target="tpu_custom_call" | custom-call | flops 1073741824 | bytes 2220032 | tf_op jit(solution)/shard_map/pallas_call | solution.py:227
Async XLA Ops:
  0.6 24.5 %copy-start.1 = (f32[512,256]{1,0:T(8,128)S(1)}, f32[512,256]{1,0:T(8,128)}, u32[]{:S(2)}) copy-start(f32[512,256]{1,0:T(8,128)} %refs_0_.5) | copy-start | bytes 1572868
  2.3 20.1 %collective-permute-start = (bf16[264,256]{1,0:T(8,128)(2,1)S(1)}, bf16[264,256]{1,0:T(8,128)(2,1)S(1)}, u32[]{:S(2)}, u32[]{:S(2)}) collective-permute-start(bf16[264,256]{1,0:T(8,128)(2,1)S(1)} %get-tuple-element.21), channel_id=1, source_target_pairs={{0,8},{1,9},{4,12},{5,13},{8,0},{9,1},{12,4},{13,5},{2,10},{3,11},... | collective-permute-start | bytes 405512 | tf_op jit(solution)/shard_map/ppermute | solution.py:222
  7.3 16.3 %collective-permute-start.1 = (bf16[264,256]{1,0:T(8,128)(2,1)S(1)}, bf16[264,256]{1,0:T(8,128)(2,1)S(1)}, u32[]{:S(2)}, u32[]{:S(2)}) collective-permute-start(bf16[264,256]{1,0:T(8,128)(2,1)S(1)} %get-tuple-element.24), channel_id=1, source_target_pairs={{0,9},{1,8},{4,13},{5,12},{8,1},{9,0},{12,5},{13,4},{2,11},{3,10},... | collective-permute-start | bytes 405512 | tf_op jit(solution)/shard_map/ppermute | solution.py:222
  7.4 18.3 %collective-permute-start.2 = (bf16[264,256]{1,0:T(8,128)(2,1)S(1)}, bf16[264,256]{1,0:T(8,128)(2,1)S(1)}, u32[]{:S(2)}, u32[]{:S(2)}) collective-permute-start(bf16[264,256]{1,0:T(8,128)(2,1)S(1)} %get-tuple-element.29), channel_id=1, source_target_pairs={{0,12},{1,13},{4,8},{5,9},{8,4},{9,5},{12,0},{13,1},{2,14},{3,15},... | collective-permute-start | bytes 405512 | tf_op jit(solution)/shard_map/ppermute | solution.py:222
  10.5 15.2 %collective-permute-start.3 = (bf16[264,256]{1,0:T(8,128)(2,1)S(1)}, bf16[264,256]{1,0:T(8,128)(2,1)S(1)}, u32[]{:S(2)}, u32[]{:S(2)}) collective-permute-start(bf16[264,256]{1,0:T(8,128)(2,1)S(1)} %get-tuple-element.30), channel_id=1, source_target_pairs={{0,13},{1,12},{4,9},{5,8},{8,5},{9,4},{12,1},{13,0},{2,15},{3,14},... | collective-permute-start | bytes 405512 | tf_op jit(solution)/shard_map/ppermute | solution.py:222
  21.9 6.1 %collective-permute-start.4 = (bf16[264,256]{1,0:T(8,128)(2,1)S(1)}, bf16[264,256]{1,0:T(8,128)(2,1)S(1)}, u32[]{:S(2)}, u32[]{:S(2)}) collective-permute-start(bf16[264,256]{1,0:T(8,128)(2,1)S(1)} %get-tuple-element.31), channel_id=1, source_target_pairs={{0,5},{1,4},{4,1},{5,0},{8,13},{9,12},{12,9},{13,8},{2,7},{3,6},{6... | collective-permute-start | bytes 405512 | tf_op jit(solution)/shard_map/ppermute | solution.py:222
  22.4 8.2 %collective-permute-start.5 = (bf16[264,256]{1,0:T(8,128)(2,1)S(1)}, bf16[264,256]{1,0:T(8,128)(2,1)S(1)}, u32[]{:S(2)}, u32[]{:S(2)}) collective-permute-start(bf16[264,256]{1,0:T(8,128)(2,1)S(1)} %get-tuple-element.32), channel_id=1, source_target_pairs={{0,4},{1,5},{4,0},{5,1},{8,12},{9,13},{12,8},{13,9},{2,6},{3,7},{6... | collective-permute-start | bytes 405512 | tf_op jit(solution)/shard_map/ppermute | solution.py:222
  23.6 6.9 %collective-permute-start.6 = (bf16[264,256]{1,0:T(8,128)(2,1)S(1)}, bf16[264,256]{1,0:T(8,128)(2,1)S(1)}, u32[]{:S(2)}, u32[]{:S(2)}) collective-permute-start(bf16[264,256]{1,0:T(8,128)(2,1)S(1)} %get-tuple-element.33), channel_id=1, source_target_pairs={{0,1},{1,0},{4,5},{5,4},{8,9},{9,8},{12,13},{13,12},{2,3},{3,2},{6... | collective-permute-start | bytes 405512 | tf_op jit(solution)/shard_map/ppermute | solution.py:222
  30.6 12.5 %copy-start = (bf16[1024,2048]{1,0:T(8,128)(2,1)S(1)}, bf16[1024,2048]{1,0:T(8,128)(2,1)}, u32[]{:S(2)}) copy-start(bf16[1024,2048]{1,0:T(8,128)(2,1)} %refs_7_.1) | copy-start | bytes 12582916
  30.6 12.5 %copy-start.2 = (s32[1024,1]{0,1:T(1,128)S(1)}, s32[1024,1]{0,1:T(1,128)}, u32[]{:S(2)}) copy-start(s32[1024,1]{0,1:T(1,128)} %param.14) | copy-start | bytes 12292
  30.6 12.5 %copy-start.3 = (s32[1024,1]{0,1:T(1,128)S(1)}, s32[1024,1]{0,1:T(1,128)}, u32[]{:S(2)}) copy-start(s32[1024,1]{0,1:T(1,128)} %param.16) | copy-start | bytes 12292
  30.6 12.5 %copy-start.4 = (s32[1024]{0:T(1024)S(1)}, s32[1024]{0:T(1024)}, u32[]{:S(2)}) copy-start(s32[1024]{0:T(1024)} %param.18) | copy-start | bytes 12292
  30.6 12.5 %copy-start.5 = (s32[1024]{0:T(1024)S(1)}, s32[1024]{0:T(1024)}, u32[]{:S(2)}) copy-start(s32[1024]{0:T(1024)} %param.19) | copy-start | bytes 12292

commit v14 on v12

--- a/solution.py
+++ b/solution.py
@@ -118,16 +118,17 @@
 
 
 def margin_kernel(place, weight, features, margin, copies, sems):
-    parts = copies.shape[0]
-    step = copies.shape[1]
+    parts, step = copies.shape[0], copies.shape[1]
     moves = [
         pltpu.make_async_copy(features.at[pl.ds(i * step, step)], copies.at[i], sems.at[i]) for i in range(parts)
     ]
-    for move in moves:
+    for move in moves[:2]:
         move.start()
     wide = jnp.broadcast_to(weight[...], (16, weight.shape[1])).astype(BF16)
     for i in range(parts):
         moves[i].wait()
+        if i + 2 < parts:
+            moves[i + 2].start()
         margin[:, i * step : (i + 1) * step] = lanes_dot(wide, copies[i])[0:1]
 
 
@@ -145,17 +146,17 @@
 
 def early_kernel(capacity, coefs, *refs):
     half = len(refs) // 2
-    table = jnp.concatenate(halves(coefs[...]), axis=0)
-    for chunk, out in zip(refs[:half], refs[half:]):
+    kept = refs[half]
+    entities = coefs.shape[0]
+    kept[:entities], kept[entities:] = halves(coefs[...])
+    table = kept[...]
+    for chunk, out in zip(refs[:half], refs[half + 1 :]):
         out[...] = chunk_scores(chunk, table, capacity)
 
 
-def scores_kernel(order, capacity, n_feat, n_ent, coefs, *refs):
+def scores_kernel(order, capacity, n_feat, n_ent, table, *refs):
     out, mine = refs[-1], lax.axis_index(HOME)
-    table = jnp.concatenate(halves(coefs[...]), axis=0)
-    scores = [
-        x[...] if x.shape[0] == 1 else chunk_scores(x, table, capacity) for x in refs[:-1]
-    ]
+    scores = [x[...] if x.shape[0] == 1 else chunk_scores(x, table[...], capacity) for x in refs[:-1]]
     scores = dict(zip(order, scores))
     scores = xor_rows(jnp.concatenate([scores[k] for k in range(len(order))], axis=0), mine)
     for home in range(len(order)):
@@ -256,8 +257,8 @@
         return lambda *refs: kernel(*args, *refs)
 
     row = pltpu.VMEM((1, rows_here), jnp.int32)
-    half, early = owners // 2, 3 * owners // 4
-    first, second, near = list(range(half, early)), list(range(early, owners)), list(reversed(range(half)))
+    half = owners // 2
+    first, second, near = [half], list(range(half + 1, owners)), list(reversed(range(half)))
     chunk = shape(capacity + IDS, width, dtype=BF16)
     flops = len(first) * 2 * capacity * rows_here * width
 
@@ -311,20 +312,21 @@
         hidden=True,
     )
     near_chunks = [xor_send(x, HOME, owners, k) for k, x in zip(near, near_chunks)]
-    order = first + near[-1:] + second + near[:-1]
-    chunks = chunks[: len(first)] + near_chunks[-1:] + chunks[len(first) :] + near_chunks[:-1]
-    came_early = len(first) + 1
-    scores = call(
+    chunks = dict(zip(first + second + near, chunks + near_chunks))
+    early = (first + second)[: half // 2] + near[-1:]
+    late = (first + second)[half // 2 :] + near[:-1]
+    order = early + late
+    table, *scores = call(
         partial(early_kernel, capacity),
-        [shape(1, capacity)] * came_early,
-        (coefs, *chunks[:came_early]),
-        [VMEM] * (1 + came_early),
+        [shape(2 * coefs.shape[0], width, dtype=BF16)] + [shape(1, capacity)] * len(early),
+        (coefs, *(chunks[k] for k in early)),
+        [VMEM] * (1 + len(early)),
         hidden=True,
     )
     (scores,) = call(
         partial(scores_kernel, order, capacity, n_feat, n_ent),
         [shape(n_feat * owners, 1, capacity)],
-        (coefs, *scores, *chunks[came_early:]),
+        (table, *scores, *(chunks[k] for k in late)),
         [VMEM] * (1 + owners),
         flops=16 * coefs.size * owners * capacity,
     )
@@ -349,7 +351,7 @@
     grad_global, grad_coefs = call(
         partial(grads_kernel, order, capacity, 1.0 / math.sqrt(rows_here * owners)),
         [shape(1, columns), shape(*coefs.shape)],
-        (coefs, weight, came, *chunks),
+        (coefs, weight, came, *(chunks[k] for k in order)),
         [VMEM] * (3 + owners),
         flops=4 * coefs.size * owners * capacity,
     )

time: 55.4 us -> 54.9 us (level)
  no operation moved by 1% of the time
where the time goes in v14:
time: 54.9 us; the launch traced here: 54.6 us
  blocking collectives  24.9 us (45%)
  Pallas kernels  12.4 us (23%)
  starting transfers between devices  10.1 us (18%)
  waiting for transfers between devices  5.78 us (11%)
  between operations  0.76 us (1%)
  other arithmetic  0.69 us (1%)
    pallas_call x8, Pallas kernels, call(): pl.pallas_call(kernel, out_shape=out_shape, in_specs=in_specs, out_specs=...  12.4 us
    all_to_all x1, blocking collectives, body(): lax.all_to_all(scores, EVERY, split_axis=0, concat_axis=0, tiled=True)  11.5 us
    ppermute x7, starting transfers between devices, xor_send(): lax.ppermute(x, axes, [(i, i ^ k) for i in range(size)])  10.1 us
    all_to_all x1, blocking collectives, body(): came = lax.all_to_all(sent, HOME, split_axis=0, concat_axis=0, tiled=True)  8.4 us
    ppermute x7, waiting for transfers between devices, xor_send(): lax.ppermute(x, axes, [(i, i ^ k) for i in range(size)])  5.78 us
    psum x1, blocking collectives, body(): global_total = lax.psum(global_part, 'feat')  4.95 us
  transfers between devices with their start and end apart: 7, of which 4 were waited for; matrix products, arithmetic and copies ran while one was open for 1% of the time, Pallas kernels for 12%

profile of v14, /device:TPU:0, one launch (start us, length us, event | category | flops | bytes accessed | tf_op | source)
XLA Modules:
  0.0 54.6 jit_solution(9659358084436893826)
XLA Ops:
  0.6 0.0 copy-start.1
  0.6 1.6 %shard_map.113 = (s32[2,1024]{1,0:T(2,128)S(1)}, s32[1,1024]{1,0:T(1,128)S(1)}, bf16[8,1024]{1,0:T(8,128)(2,1)S(1)}, bf16[1024,256]{1,0:T(8,128)(2,1)S(1)}, bf16[264,256]{1,0:T(8,128)(2,1)S(1)}) custom-call(s32[1,1024]{1,0:T(1,128)} %bitcast.10, s32[1,1024]{1,0:T(1,128)} %bitcast.12, s32[1,1024]{1,0:T(1,128)} %bitcast.16, s32[1,1024]{1,0:T(1,128)} %bitcast.17, ...), custom_call_target="tpu_custom_call" | custom-call | flops 134217728 | bytes 1228800 | tf_op jit(solution)/shard_map/pallas_call | solution.py:223
  2.3 4.1 %collective-permute-start = (bf16[264,256]{1,0:T(8,128)(2,1)S(1)}, bf16[264,256]{1,0:T(8,128)(2,1)S(1)}, u32[]{:S(2)}, u32[]{:S(2)}) collective-permute-start(bf16[264,256]{1,0:T(8,128)(2,1)S(1)} %get-tuple-element.22), channel_id=1, source_target_pairs={{0,8},{1,9},{4,12},{5,13},{8,0},{9,1},{12,4},{13,5},{2,10},{3,11},... | collective-permute-start | bytes 405512 | tf_op jit(solution)/shard_map/ppermute | solution.py:218
  6.4 1.0 %shard_map.115 = (bf16[264,256]{1,0:T(8,128)(2,1)S(1)}, bf16[264,256]{1,0:T(8,128)(2,1)S(1)}, bf16[264,256]{1,0:T(8,128)(2,1)S(1)}) custom-call(s32[1,1024]{1,0:T(1,128)S(1)} %get-tuple-element.21.place.refs_0_, bf16[8,1024]{1,0:T(8,128)(2,1)S(1)} %get-tuple-element.23.refs_1_, bf16[1024,256]{1,0:T(8,128)(2,1)S(1)} %get-tuple-element.24.refs_2_), custom_call_target="tpu_custom_call" | custom-call | flops 134217728 | bytes 950272 | tf_op jit(solution)/shard_map/pallas_call | solution.py:223
  7.3 0.1 collective-permute-start.1
  7.4 3.1 %collective-permute-start.2 = (bf16[264,256]{1,0:T(8,128)(2,1)S(1)}, bf16[264,256]{1,0:T(8,128)(2,1)S(1)}, u32[]{:S(2)}, u32[]{:S(2)}) collective-permute-start(bf16[264,256]{1,0:T(8,128)(2,1)S(1)} %get-tuple-element.31), channel_id=1, source_target_pairs={{0,12},{1,13},{4,8},{5,9},{8,4},{9,5},{12,0},{13,1},{2,14},{3,15},... | collective-permute-start | bytes 405512 | tf_op jit(solution)/shard_map/ppermute | solution.py:218
  10.5 0.6 %collective-permute-start.3 = (bf16[264,256]{1,0:T(8,128)(2,1)S(1)}, bf16[264,256]{1,0:T(8,128)(2,1)S(1)}, u32[]{:S(2)}, u32[]{:S(2)}) collective-permute-start(bf16[264,256]{1,0:T(8,128)(2,1)S(1)} %get-tuple-element.32), channel_id=1, source_target_pairs={{0,13},{1,12},{4,9},{5,8},{8,5},{9,4},{12,1},{13,0},{2,15},{3,14},... | collective-permute-start | bytes 405512 | tf_op jit(solution)/shard_map/ppermute | solution.py:218
  11.1 0.7 %reshape.39 = f32[2048]{0:T(1024)S(1)} convert(bf16[2048]{0:T(1024)(128)(2,1)} %param.11) | non-fusion elementwise | flops 2048 | bytes 12288 | tf_op jit(solution)/shard_map/reshape | solution.py:296
  11.8 3.9 %shard_map.114 = f32[1,1024]{1,0:T(1,128)S(1)} custom-call(s32[1,1024]{1,0:T(1,128)S(1)} %get-tuple-element.21.place.refs_0_, f32[1,2048]{1,0:T(1,128)S(1)} %bitcast.8, bf16[1024,2048]{1,0:T(8,128)(2,1)} %refs_7_.1), custom_call_target="tpu_custom_call" | custom-call | tf_op jit(solution)/shard_map/pallas_call | solution.py:223
  15.7 4.9 %psum.7.refs_3_.refs_5_ = f32[1,1024]{1,0:T(1,128)S(1)} all-reduce(f32[1,1024]{1,0:T(1,128)S(1)} %shard_map.114), channel_id=1, replica_groups=mesh['groups'=2,'rows'=4,'feat'=2,'ent'=2] {'feat'}, use_global_device_ids=true, to_apply=%region_0.0 | all-reduce | flops 1024 | bytes 8192 | tf_op jit(solution)/shard_map/psum | solution.py:306
  20.6 1.2 %shard_map.116 = (bf16[264,256]{1,0:T(8,128)(2,1)S(1)}, bf16[264,256]{1,0:T(8,128)(2,1)S(1)}, bf16[264,256]{1,0:T(8,128)(2,1)S(1)}, bf16[264,256]{1,0:T(8,128)(2,1)S(1)}) custom-call(s32[1,1024]{1,0:T(1,128)S(1)} %get-tuple-element.21.place.refs_0_, bf16[8,1024]{1,0:T(8,128)(2,1)S(1)} %get-tuple-element.23.refs_1_, ...), custom_call_target="tpu_custom_call" | custom-call | tf_op jit(solution)/shard_map/pallas_call | solution.py:223
  21.9 0.1 collective-permute-start.4
  22.0 0.4 collective-permute-done.refs_1_.refs_3_
  22.4 0.7 %collective-permute-start.5 = (bf16[264,256]{1,0:T(8,128)(2,1)S(1)}, bf16[264,256]{1,0:T(8,128)(2,1)S(1)}, u32[]{:S(2)}, u32[]{:S(2)}) collective-permute-start(bf16[264,256]{1,0:T(8,128)(2,1)S(1)} %get-tuple-element.34), channel_id=1, source_target_pairs={{0,4},{1,5},{4,0},{5,1},{8,12},{9,13},{12,8},{13,9},{2,6},{3,7},{6... | collective-permute-start | bytes 405512 | tf_op jit(solution)/shard_map/ppermute | solution.py:218
  23.1 0.6 %collective-permute-done.1.refs_2_.refs_4_ = bf16[264,256]{1,0:T(8,128)(2,1)S(1)} collective-permute-done((bf16[264,256]{1,0:T(8,128)(2,1)S(1)}, bf16[264,256]{1,0:T(8,128)(2,1)S(1)}, u32[]{:S(2)}, u32[]{:S(2)}) %collective-permute-start.1) | collective-permute-done | bytes 135200 | tf_op jit(solution)/shard_map/ppermute | solution.py:218
  23.6 1.5 %collective-permute-start.6 = (bf16[264,256]{1,0:T(8,128)(2,1)S(1)}, bf16[264,256]{1,0:T(8,128)(2,1)S(1)}, u32[]{:S(2)}, u32[]{:S(2)}) collective-permute-start(bf16[264,256]{1,0:T(8,128)(2,1)S(1)} %get-tuple-element.35), channel_id=1, source_target_pairs={{0,1},{1,0},{4,5},{5,4},{8,9},{9,8},{12,13},{13,12},{2,3},{3,2},{6... | collective-permute-start | bytes 405512 | tf_op jit(solution)/shard_map/ppermute | solution.py:218
  25.1 0.0 copy-done.1
  25.1 0.6 %shard_map.117 = (bf16[1024,256]{1,0:T(8,128)(2,1)S(1)}, f32[1,256]{1,0:T(1,128)S(1)}, f32[1,256]{1,0:T(1,128)S(1)}, f32[1,256]{1,0:T(1,128)S(1)}) custom-call(f32[512,256]{1,0:T(8,128)S(1)} %copy-done.1, bf16[264,256]{1,0:T(8,128)(2,1)S(1)} %collective-permute-done.refs_1_.refs_3_, bf16[264,256]{1,0:T(8,128)(2,1)S(1)} %collective-permute-done.1.refs_2_.refs_4_, ...), custom_call_target="tpu_custom_call" | custom-call | tf_op jit(solution)/shard_map/pallas_call | solution.py:223
  25.7 0.0 collective-permute-done.2.refs_4_.refs_6_
  25.7 0.0 collective-permute-done.3.refs_5_.refs_7_
  25.8 2.2 %collective-permute-done.4.refs_6_.refs_8_ = bf16[264,256]{1,0:T(8,128)(2,1)S(1)} collective-permute-done((bf16[264,256]{1,0:T(8,128)(2,1)S(1)}, bf16[264,256]{1,0:T(8,128)(2,1)S(1)}, u32[]{:S(2)}, u32[]{:S(2)}) %collective-permute-start.4) | collective-permute-done | bytes 135200 | tf_op jit(solution)/shard_map/ppermute | solution.py:218
  28.0 2.6 %collective-permute-done.5.refs_7_.refs_9_ = bf16[264,256]{1,0:T(8,128)(2,1)S(1)} collective-permute-done((bf16[264,256]{1,0:T(8,128)(2,1)S(1)}, bf16[264,256]{1,0:T(8,128)(2,1)S(1)}, u32[]{:S(2)}, u32[]{:S(2)}) %collective-permute-start.5) | collective-permute-done | bytes 135200 | tf_op jit(solution)/shard_map/ppermute | solution.py:218
  30.6 0.0 collective-permute-done.6.refs_8_.refs_10_
  30.6 0.0 copy-start
  30.6 0.0 copy-start.2
  30.6 0.0 copy-start.3
  30.6 0.0 copy-start.4
  30.6 0.0 copy-start.5
  30.6 0.9 %shard_map.118 = f32[16,1,256]{2,1,0:T(1,128)S(1)} custom-call(bf16[1024,256]{1,0:T(8,128)(2,1)S(1)} %get-tuple-element.27.refs_0_, f32[1,256]{1,0:T(1,128)S(1)} %get-tuple-element.28.refs_1_, f32[1,256]{1,0:T(1,128)S(1)} %get-tuple-element.29.refs_2_, f32[1,256]{1,0:T(1,128)S(1)} %get-tuple-element.30.refs_3_, ...), custom_call_target="tpu_custom_call" | custom-call | flops 4294967296 | bytes 1219584 | tf_op jit(solution)/shard_map/pallas_call | solution.py:223
  31.5 11.5 %all_to_all.10.refs_6_ = f32[16,1,256]{2,1,0:T(1,128)S(1)} all-to-all(f32[16,1,256]{2,1,0:T(1,128)S(1)} %shard_map.118), channel_id=1, replica_groups=mesh['groups'=2,'rows'=4,'feat'=2,'ent'=2] {'rows','feat','ent'}, dimensions={0} | all-to-all | bytes 32768 | tf_op jit(solution)/shard_map/all_to_all | solution.py:333
  43.0 0.0 copy-done
  43.0 0.0 copy-done.2
  43.0 0.0 copy-done.3
  43.0 0.0 copy-done.4
  43.1 0.0 copy-done.5
  43.1 1.0 %shard_map.119 = f32[8,1,2304]{2,1,0:T(1,128)S(1)} custom-call(s32[1,1024]{1,0:T(1,128)S(1)} %bitcast.11, s32[1,1024]{1,0:T(1,128)S(1)} %bitcast.13, s32[2,1024]{1,0:T(2,128)S(1)} %get-tuple-element.20.refs_2_, s32[1,1024]{1,0:T(1,128)S(1)} %bitcast.14, s32[1,1024]{1,0:T(1,128)S(1)} %bitcast.15, f32[1,1024]{1,0:T(1,128)S(1)} %psum.7.refs_3_.refs_5_, ...), custom_call_target="tpu_custom_call" | custom-call | flops 67108864 | bytes 4313088 | tf_op jit(solution)/shard_map/pallas_call | solution.py:223
  44.1 8.4 %all_to_all.11.refs_2_ = f32[8,1,2304]{2,1,0:T(1,128)S(1)} all-to-all(f32[8,1,2304]{2,1,0:T(1,128)S(1)} %shard_map.119), channel_id=1, replica_groups=mesh['groups'=2,'rows'=4,'feat'=2,'ent'=2] {'rows','ent'}, dimensions={0} | all-to-all | bytes 147456 | tf_op jit(solution)/shard_map/all_to_all | solution.py:350
  52.5 2.1 %shard_map.120 = (f32[1,2048]{1,0:T(1,128)}, f32[512,256]{1,0:T(8,128)}) custom-call(f32[512,256]{1,0:T(8,128)S(1)} %copy-done.1, f32[1,2048]{1,0:T(1,128)S(1)} %bitcast.9, f32[8,1,2304]{2,1,0:T(1,128)S(1)} %all_to_all.11.refs_2_, bf16[264,256]{1,0:T(8,128)(2,1)S(1)} %collective-permute-done.refs_1_.refs_3_, ...), custom_call_target="tpu_custom_call" | custom-call | flops 1073741824 | bytes 2220032 | tf_op jit(solution)/shard_map/pallas_call | solution.py:223
Async XLA Ops:
  0.6 24.5 %copy-start.1 = (f32[512,256]{1,0:T(8,128)S(1)}, f32[512,256]{1,0:T(8,128)}, u32[]{:S(2)}) copy-start(f32[512,256]{1,0:T(8,128)} %refs_0_.3) | copy-start | bytes 1572868
  2.3 20.1 %collective-permute-start = (bf16[264,256]{1,0:T(8,128)(2,1)S(1)}, bf16[264,256]{1,0:T(8,128)(2,1)S(1)}, u32[]{:S(2)}, u32[]{:S(2)}) collective-permute-start(bf16[264,256]{1,0:T(8,128)(2,1)S(1)} %get-tuple-element.22), channel_id=1, source_target_pairs={{0,8},{1,9},{4,12},{5,13},{8,0},{9,1},{12,4},{13,5},{2,10},{3,11},... | collective-permute-start | bytes 405512 | tf_op jit(solution)/shard_map/ppermute | solution.py:218
  7.3 16.3 %collective-permute-start.1 = (bf16[264,256]{1,0:T(8,128)(2,1)S(1)}, bf16[264,256]{1,0:T(8,128)(2,1)S(1)}, u32[]{:S(2)}, u32[]{:S(2)}) collective-permute-start(bf16[264,256]{1,0:T(8,128)(2,1)S(1)} %get-tuple-element.25), channel_id=1, source_target_pairs={{0,9},{1,8},{4,13},{5,12},{8,1},{9,0},{12,5},{13,4},{2,11},{3,10},... | collective-permute-start | bytes 405512 | tf_op jit(solution)/shard_map/ppermute | solution.py:218
  7.4 18.3 %collective-permute-start.2 = (bf16[264,256]{1,0:T(8,128)(2,1)S(1)}, bf16[264,256]{1,0:T(8,128)(2,1)S(1)}, u32[]{:S(2)}, u32[]{:S(2)}) collective-permute-start(bf16[264,256]{1,0:T(8,128)(2,1)S(1)} %get-tuple-element.31), channel_id=1, source_target_pairs={{0,12},{1,13},{4,8},{5,9},{8,4},{9,5},{12,0},{13,1},{2,14},{3,15},... | collective-permute-start | bytes 405512 | tf_op jit(solution)/shard_map/ppermute | solution.py:218
  10.5 15.2 %collective-permute-start.3 = (bf16[264,256]{1,0:T(8,128)(2,1)S(1)}, bf16[264,256]{1,0:T(8,128)(2,1)S(1)}, u32[]{:S(2)}, u32[]{:S(2)}) collective-permute-start(bf16[264,256]{1,0:T(8,128)(2,1)S(1)} %get-tuple-element.32), channel_id=1, source_target_pairs={{0,13},{1,12},{4,9},{5,8},{8,5},{9,4},{12,1},{13,0},{2,15},{3,14},... | collective-permute-start | bytes 405512 | tf_op jit(solution)/shard_map/ppermute | solution.py:218
  21.9 6.1 %collective-permute-start.4 = (bf16[264,256]{1,0:T(8,128)(2,1)S(1)}, bf16[264,256]{1,0:T(8,128)(2,1)S(1)}, u32[]{:S(2)}, u32[]{:S(2)}) collective-permute-start(bf16[264,256]{1,0:T(8,128)(2,1)S(1)} %get-tuple-element.33), channel_id=1, source_target_pairs={{0,5},{1,4},{4,1},{5,0},{8,13},{9,12},{12,9},{13,8},{2,7},{3,6},{6... | collective-permute-start | bytes 405512 | tf_op jit(solution)/shard_map/ppermute | solution.py:218
  22.4 8.2 %collective-permute-start.5 = (bf16[264,256]{1,0:T(8,128)(2,1)S(1)}, bf16[264,256]{1,0:T(8,128)(2,1)S(1)}, u32[]{:S(2)}, u32[]{:S(2)}) collective-permute-start(bf16[264,256]{1,0:T(8,128)(2,1)S(1)} %get-tuple-element.34), channel_id=1, source_target_pairs={{0,4},{1,5},{4,0},{5,1},{8,12},{9,13},{12,8},{13,9},{2,6},{3,7},{6... | collective-permute-start | bytes 405512 | tf_op jit(solution)/shard_map/ppermute | solution.py:218
  23.6 6.9 %collective-permute-start.6 = (bf16[264,256]{1,0:T(8,128)(2,1)S(1)}, bf16[264,256]{1,0:T(8,128)(2,1)S(1)}, u32[]{:S(2)}, u32[]{:S(2)}) collective-permute-start(bf16[264,256]{1,0:T(8,128)(2,1)S(1)} %get-tuple-element.35), channel_id=1, source_target_pairs={{0,1},{1,0},{4,5},{5,4},{8,9},{9,8},{12,13},{13,12},{2,3},{3,2},{6... | collective-permute-start | bytes 405512 | tf_op jit(solution)/shard_map/ppermute | solution.py:218
  30.6 12.5 %copy-start = (bf16[1024,2048]{1,0:T(8,128)(2,1)S(1)}, bf16[1024,2048]{1,0:T(8,128)(2,1)}, u32[]{:S(2)}) copy-start(bf16[1024,2048]{1,0:T(8,128)(2,1)} %refs_7_.1) | copy-start | bytes 12582916
  30.6 12.5 %copy-start.2 = (s32[1024,1]{0,1:T(1,128)S(1)}, s32[1024,1]{0,1:T(1,128)}, u32[]{:S(2)}) copy-start(s32[1024,1]{0,1:T(1,128)} %param.14) | copy-start | bytes 12292
  30.6 12.5 %copy-start.3 = (s32[1024,1]{0,1:T(1,128)S(1)}, s32[1024,1]{0,1:T(1,128)}, u32[]{:S(2)}) copy-start(s32[1024,1]{0,1:T(1,128)} %param.16) | copy-start | bytes 12292
  30.6 12.5 %copy-start.4 = (s32[1024]{0:T(1024)S(1)}, s32[1024]{0:T(1024)}, u32[]{:S(2)}) copy-start(s32[1024]{0:T(1024)} %param.18) | copy-start | bytes 12292
  30.6 12.5 %copy-start.5 = (s32[1024]{0:T(1024)S(1)}, s32[1024]{0:T(1024)}, u32[]{:S(2)}) copy-start(s32[1024]{0:T(1024)} %param.19) | copy-start | bytes 12292

commit v15 on v14

--- a/solution.py
+++ b/solution.py
@@ -117,19 +117,9 @@
         pack_chunk(k, capacity, place[...], ids[...], feats[...], chunk)
 
 
-def margin_kernel(place, weight, features, margin, copies, sems):
-    parts, step = copies.shape[0], copies.shape[1]
-    moves = [
-        pltpu.make_async_copy(features.at[pl.ds(i * step, step)], copies.at[i], sems.at[i]) for i in range(parts)
-    ]
-    for move in moves[:2]:
-        move.start()
+def margin_kernel(place, weight, features, margin):
     wide = jnp.broadcast_to(weight[...], (16, weight.shape[1])).astype(BF16)
-    for i in range(parts):
-        moves[i].wait()
-        if i + 2 < parts:
-            moves[i + 2].start()
-        margin[:, i * step : (i + 1) * step] = lanes_dot(wide, copies[i])[0:1]
+    margin[...] = lanes_dot(wide, features[...])[0:1]
 
 
 def chunk_ids(chunk, capacity):
@@ -290,18 +280,12 @@
         [chunk] * len(second),
         (place, ids, feats),
         [VMEM] * 3,
-        flops=flops,
+        flops=32 * flops,
     )
     chunks = [xor_send(x, HOME, owners, k) for k, x in zip(first + second, chunks)]
     weight = global_weight.astype(F32).reshape(1, columns)
-    parts = 4
     (global_part,) = call(
-        margin_kernel,
-        [shape(1, rows_here)],
-        (place, weight, in_hbm(features)),
-        [VMEM, VMEM, HBM],
-        hidden=True,
-        scratch=[pltpu.VMEM((parts, rows_here // parts, columns), BF16), pltpu.SemaphoreType.DMA((parts,))],
+        margin_kernel, [shape(1, rows_here)], (place, weight, features), [VMEM] * 3, hidden=True
     )
     global_total = lax.psum(global_part, "feat")
     near_chunks = call(

time: 54.9 us -> 55.1 us (level)
  waiting for transfers between devices: 5.78 us -> 9.57 us
  Pallas kernels: 12.4 us -> 9.61 us
  starting transfers between devices: 10.1 us -> 9.35 us
  blocking collectives: 24.9 us -> 25.6 us
  other arithmetic: 0.69 us -> 0.01 us
    ppermute x7, waiting for transfers between devices: 5.78 us -> 9.57 us  [xor_send(): lax.ppermute(x, axes, [(i, i ^ k) for i in range(size)])]
    pallas_call x8, Pallas kernels: 12.4 us -> 9.61 us  [call(): pl.pallas_call(kernel, out_shape=out_shape, in_specs=in_specs, out_specs=...]
    ppermute x7, starting transfers between devices: 10.1 us -> 9.35 us  [xor_send(): lax.ppermute(x, axes, [(i, i ^ k) for i in range(size)])]
    all_to_all x1, blocking collectives: 11.5 us -> 12.2 us  [body(): lax.all_to_all(scores, EVERY, split_axis=0, concat_axis=0, tiled=True)]
    reshape x1, other arithmetic: 0.69 us -> 0.01 us  [body(): weight = global_weight.astype(F32).reshape(1, columns)]
  transfers between devices with their start and end apart: 7 -> 7, of which waited for: 4 -> 4; matrix products, arithmetic and copies ran while one was open for 1% -> 0% of each run, Pallas kernels for 12% -> 7%
where the time goes in v15:
time: 55.1 us; the launch traced here: 54.9 us
  blocking collectives  25.6 us (46%)
  Pallas kernels  9.61 us (17%)
  waiting for transfers between devices  9.57 us (17%)
  starting transfers between devices  9.35 us (17%)
  between operations  0.76 us (1%)
    all_to_all x1, blocking collectives, body(): lax.all_to_all(scores, EVERY, split_axis=0, concat_axis=0, tiled=True)  12.2 us
    pallas_call x8, Pallas kernels, call(): pl.pallas_call(kernel, out_shape=out_shape, in_specs=in_specs, out_specs=...  9.61 us
    ppermute x7, waiting for transfers between devices, xor_send(): lax.ppermute(x, axes, [(i, i ^ k) for i in range(size)])  9.57 us
    ppermute x7, starting transfers between devices, xor_send(): lax.ppermute(x, axes, [(i, i ^ k) for i in range(size)])  9.35 us
    all_to_all x1, blocking collectives, body(): came = lax.all_to_all(sent, HOME, split_axis=0, concat_axis=0, tiled=True)  8.4 us
    psum x1, blocking collectives, body(): global_total = lax.psum(global_part, 'feat')  4.93 us
  transfers between devices with their start and end apart: 7, of which 4 were waited for; matrix products, arithmetic and copies ran while one was open for 0% of the time, Pallas kernels for 7%

profile of v15, /device:TPU:0, one launch (start us, length us, event | category | flops | bytes accessed | tf_op | source)
XLA Modules:
  0.0 54.9 jit_solution(4086108066112942797)
XLA Ops:
  0.6 1.6 %shard_map.113 = (s32[2,1024]{1,0:T(2,128)S(1)}, s32[1,1024]{1,0:T(1,128)S(1)}, bf16[8,1024]{1,0:T(8,128)(2,1)S(1)}, bf16[1024,256]{1,0:T(8,128)(2,1)S(1)}, bf16[264,256]{1,0:T(8,128)(2,1)S(1)}) custom-call(s32[1,1024]{1,0:T(1,128)} %bitcast.10, s32[1,1024]{1,0:T(1,128)} %bitcast.12, s32[1,1024]{1,0:T(1,128)} %bitcast.16, s32[1,1024]{1,0:T(1,128)} %bitcast.17, ...), custom_call_target="tpu_custom_call" | custom-call | flops 134217728 | bytes 1228800 | tf_op jit(solution)/shard_map/pallas_call | solution.py:213
  2.2 4.1 %collective-permute-start = (bf16[264,256]{1,0:T(8,128)(2,1)S(1)}, bf16[264,256]{1,0:T(8,128)(2,1)S(1)}, u32[]{:S(2)}, u32[]{:S(2)}) collective-permute-start(bf16[264,256]{1,0:T(8,128)(2,1)S(1)} %get-tuple-element.22), channel_id=1, source_target_pairs={{0,8},{1,9},{4,12},{5,13},{8,0},{9,1},{12,4},{13,5},{2,10},{3,11},... | collective-permute-start | bytes 405512 | tf_op jit(solution)/shard_map/ppermute | solution.py:208
  6.3 0.0 copy-start.7
  6.3 0.0 copy-start
  6.3 1.0 %shard_map.115 = (bf16[264,256]{1,0:T(8,128)(2,1)S(1)}, bf16[264,256]{1,0:T(8,128)(2,1)S(1)}, bf16[264,256]{1,0:T(8,128)(2,1)S(1)}) custom-call(s32[1,1024]{1,0:T(1,128)S(1)} %get-tuple-element.21.place.refs_0_, bf16[8,1024]{1,0:T(8,128)(2,1)S(1)} %get-tuple-element.23.refs_1_, bf16[1024,256]{1,0:T(8,128)(2,1)S(1)} %get-tuple-element.24.refs_2_), custom_call_target="tpu_custom_call" | custom-call | flops 4294967296 | bytes 950272 | tf_op jit(solution)/shard_map/pallas_call | solution.py:213
  7.3 0.0 copy-start.2
  7.3 0.1 collective-permute-start.1
  7.4 3.1 %collective-permute-start.2 = (bf16[264,256]{1,0:T(8,128)(2,1)S(1)}, bf16[264,256]{1,0:T(8,128)(2,1)S(1)}, u32[]{:S(2)}, u32[]{:S(2)}) collective-permute-start(bf16[264,256]{1,0:T(8,128)(2,1)S(1)} %get-tuple-element.31), channel_id=1, source_target_pairs={{0,12},{1,13},{4,8},{5,9},{8,4},{9,5},{12,0},{13,1},{2,14},{3,15},... | collective-permute-start | bytes 405512 | tf_op jit(solution)/shard_map/ppermute | solution.py:208
  10.5 0.6 %collective-permute-start.3 = (bf16[264,256]{1,0:T(8,128)(2,1)S(1)}, bf16[264,256]{1,0:T(8,128)(2,1)S(1)}, u32[]{:S(2)}, u32[]{:S(2)}) collective-permute-start(bf16[264,256]{1,0:T(8,128)(2,1)S(1)} %get-tuple-element.32), channel_id=1, source_target_pairs={{0,13},{1,12},{4,9},{5,8},{8,5},{9,4},{12,1},{13,0},{2,15},{3,14},... | collective-permute-start | bytes 405512 | tf_op jit(solution)/shard_map/ppermute | solution.py:208
  11.1 0.0 copy-done.7
  11.1 0.0 copy-done
  11.1 1.2 %shard_map.114 = f32[1,1024]{1,0:T(1,128)S(1)} custom-call(s32[1,1024]{1,0:T(1,128)S(1)} %get-tuple-element.21.place.refs_0_, f32[1,2048]{1,0:T(1,128)S(1)} %bitcast.8, bf16[1024,2048]{1,0:T(8,128)(2,1)S(1)} %copy-done), custom_call_target="tpu_custom_call" | custom-call | tf_op jit(solution)/shard_map/pallas_call | solution.py:213
  12.2 4.9 %psum.7.refs_3_.refs_5_ = f32[1,1024]{1,0:T(1,128)S(1)} all-reduce(f32[1,1024]{1,0:T(1,128)S(1)} %shard_map.114), channel_id=1, replica_groups=mesh['groups'=2,'rows'=4,'feat'=2,'ent'=2] {'feat'}, use_global_device_ids=true, to_apply=%region_0.0 | all-reduce | flops 1024 | bytes 8192 | tf_op jit(solution)/shard_map/psum | solution.py:290
  17.2 1.2 %shard_map.116 = (bf16[264,256]{1,0:T(8,128)(2,1)S(1)}, bf16[264,256]{1,0:T(8,128)(2,1)S(1)}, bf16[264,256]{1,0:T(8,128)(2,1)S(1)}, bf16[264,256]{1,0:T(8,128)(2,1)S(1)}) custom-call(s32[1,1024]{1,0:T(1,128)S(1)} %get-tuple-element.21.place.refs_0_, bf16[8,1024]{1,0:T(8,128)(2,1)S(1)} %get-tuple-element.23.refs_1_, ...), custom_call_target="tpu_custom_call" | custom-call | tf_op jit(solution)/shard_map/pallas_call | solution.py:213
  18.4 0.1 collective-permute-start.4
  18.5 3.9 %collective-permute-done.refs_1_.refs_3_ = bf16[264,256]{1,0:T(8,128)(2,1)S(1)} collective-permute-done((bf16[264,256]{1,0:T(8,128)(2,1)S(1)}, bf16[264,256]{1,0:T(8,128)(2,1)S(1)}, u32[]{:S(2)}, u32[]{:S(2)}) %collective-permute-start) | collective-permute-done | bytes 135200 | tf_op jit(solution)/shard_map/ppermute | solution.py:208
  22.4 0.0 collective-permute-start.5
  22.4 1.2 %collective-permute-done.1.refs_2_.refs_4_ = bf16[264,256]{1,0:T(8,128)(2,1)S(1)} collective-permute-done((bf16[264,256]{1,0:T(8,128)(2,1)S(1)}, bf16[264,256]{1,0:T(8,128)(2,1)S(1)}, u32[]{:S(2)}, u32[]{:S(2)}) %collective-permute-start.1) | collective-permute-done | bytes 135200 | tf_op jit(solution)/shard_map/ppermute | solution.py:208
  23.6 1.4 %collective-permute-start.6 = (bf16[264,256]{1,0:T(8,128)(2,1)S(1)}, bf16[264,256]{1,0:T(8,128)(2,1)S(1)}, u32[]{:S(2)}, u32[]{:S(2)}) collective-permute-start(bf16[264,256]{1,0:T(8,128)(2,1)S(1)} %get-tuple-element.35), channel_id=1, source_target_pairs={{0,1},{1,0},{4,5},{5,4},{8,9},{9,8},{12,13},{13,12},{2,3},{3,2},{6... | collective-permute-start | bytes 405512 | tf_op jit(solution)/shard_map/ppermute | solution.py:208
  25.1 0.0 copy-done.2
  25.1 0.6 %shard_map.117 = (bf16[1024,256]{1,0:T(8,128)(2,1)S(1)}, f32[1,256]{1,0:T(1,128)S(1)}, f32[1,256]{1,0:T(1,128)S(1)}, f32[1,256]{1,0:T(1,128)S(1)}) custom-call(f32[512,256]{1,0:T(8,128)S(1)} %copy-done.2, bf16[264,256]{1,0:T(8,128)(2,1)S(1)} %collective-permute-done.refs_1_.refs_3_, bf16[264,256]{1,0:T(8,128)(2,1)S(1)} %collective-permute-done.1.refs_2_.refs_4_, ...), custom_call_target="tpu_custom_call" | custom-call | tf_op jit(solution)/shard_map/pallas_call | solution.py:213
  25.7 0.0 collective-permute-done.2.refs_4_.refs_6_
  25.7 0.0 collective-permute-done.3.refs_5_.refs_7_
  25.7 1.6 %collective-permute-done.4.refs_6_.refs_8_ = bf16[264,256]{1,0:T(8,128)(2,1)S(1)} collective-permute-done((bf16[264,256]{1,0:T(8,128)(2,1)S(1)}, bf16[264,256]{1,0:T(8,128)(2,1)S(1)}, u32[]{:S(2)}, u32[]{:S(2)}) %collective-permute-start.4) | collective-permute-done | bytes 135200 | tf_op jit(solution)/shard_map/ppermute | solution.py:208
  27.3 2.8 %collective-permute-done.5.refs_7_.refs_9_ = bf16[264,256]{1,0:T(8,128)(2,1)S(1)} collective-permute-done((bf16[264,256]{1,0:T(8,128)(2,1)S(1)}, bf16[264,256]{1,0:T(8,128)(2,1)S(1)}, u32[]{:S(2)}, u32[]{:S(2)}) %collective-permute-start.5) | collective-permute-done | bytes 135200 | tf_op jit(solution)/shard_map/ppermute | solution.py:208
  30.1 0.0 collective-permute-done.6.refs_8_.refs_10_
  30.1 0.0 copy-start.1
  30.1 0.0 copy-start.3
  30.1 0.0 copy-start.4
  30.2 0.0 copy-start.5
  30.2 0.0 copy-start.6
  30.2 0.9 %shard_map.118 = f32[16,1,256]{2,1,0:T(1,128)S(1)} custom-call(bf16[1024,256]{1,0:T(8,128)(2,1)S(1)} %get-tuple-element.27.refs_0_, f32[1,256]{1,0:T(1,128)S(1)} %get-tuple-element.28.refs_1_, f32[1,256]{1,0:T(1,128)S(1)} %get-tuple-element.29.refs_2_, f32[1,256]{1,0:T(1,128)S(1)} %get-tuple-element.30.refs_3_, ...), custom_call_target="tpu_custom_call" | custom-call | flops 4294967296 | bytes 1219584 | tf_op jit(solution)/shard_map/pallas_call | solution.py:213
  31.1 12.2 %all_to_all.10.refs_6_ = f32[16,1,256]{2,1,0:T(1,128)S(1)} all-to-all(f32[16,1,256]{2,1,0:T(1,128)S(1)} %shard_map.118), channel_id=1, replica_groups=mesh['groups'=2,'rows'=4,'feat'=2,'ent'=2] {'rows','feat','ent'}, dimensions={0} | all-to-all | bytes 32768 | tf_op jit(solution)/shard_map/all_to_all | solution.py:317
  43.3 0.0 copy-done.1
  43.3 0.0 copy-done.3
  43.3 0.0 copy-done.4
  43.3 0.0 copy-done.5
  43.4 0.0 copy-done.6
  43.4 1.0 %shard_map.119 = f32[8,1,2304]{2,1,0:T(1,128)S(1)} custom-call(s32[1,1024]{1,0:T(1,128)S(1)} %bitcast.11, s32[1,1024]{1,0:T(1,128)S(1)} %bitcast.13, s32[2,1024]{1,0:T(2,128)S(1)} %get-tuple-element.20.refs_2_, s32[1,1024]{1,0:T(1,128)S(1)} %bitcast.14, s32[1,1024]{1,0:T(1,128)S(1)} %bitcast.15, f32[1,1024]{1,0:T(1,128)S(1)} %psum.7.refs_3_.refs_5_, ...), custom_call_target="tpu_custom_call" | custom-call | flops 67108864 | bytes 4313088 | tf_op jit(solution)/shard_map/pallas_call | solution.py:213
  44.4 8.4 %all_to_all.11.refs_2_ = f32[8,1,2304]{2,1,0:T(1,128)S(1)} all-to-all(f32[8,1,2304]{2,1,0:T(1,128)S(1)} %shard_map.119), channel_id=1, replica_groups=mesh['groups'=2,'rows'=4,'feat'=2,'ent'=2] {'rows','ent'}, dimensions={0} | all-to-all | bytes 147456 | tf_op jit(solution)/shard_map/all_to_all | solution.py:334
  52.8 2.1 %shard_map.120 = (f32[1,2048]{1,0:T(1,128)}, f32[512,256]{1,0:T(8,128)}) custom-call(f32[512,256]{1,0:T(8,128)S(1)} %copy-done.2, f32[1,2048]{1,0:T(1,128)S(1)} %bitcast.9, f32[8,1,2304]{2,1,0:T(1,128)S(1)} %all_to_all.11.refs_2_, bf16[264,256]{1,0:T(8,128)(2,1)S(1)} %collective-permute-done.refs_1_.refs_3_, ...), custom_call_target="tpu_custom_call" | custom-call | flops 1073741824 | bytes 2220032 | tf_op jit(solution)/shard_map/pallas_call | solution.py:213
  (1 shorter events, 0.0 us)
Async XLA Ops:
  2.2 20.2 %collective-permute-start = (bf16[264,256]{1,0:T(8,128)(2,1)S(1)}, bf16[264,256]{1,0:T(8,128)(2,1)S(1)}, u32[]{:S(2)}, u32[]{:S(2)}) collective-permute-start(bf16[264,256]{1,0:T(8,128)(2,1)S(1)} %get-tuple-element.22), channel_id=1, source_target_pairs={{0,8},{1,9},{4,12},{5,13},{8,0},{9,1},{12,4},{13,5},{2,10},{3,11},... | collective-permute-start | bytes 405512 | tf_op jit(solution)/shard_map/ppermute | solution.py:208
  6.3 4.7 %copy-start.7 = (bf16[2048]{0:T(1024)(128)(2,1)S(1)}, bf16[2048]{0:T(1024)(128)(2,1)}, u32[]{:S(2)}) copy-start(bf16[2048]{0:T(1024)(128)(2,1)} %param.11) | copy-start | bytes 12292
  6.3 4.7 %copy-start = (bf16[1024,2048]{1,0:T(8,128)(2,1)S(1)}, bf16[1024,2048]{1,0:T(8,128)(2,1)}, u32[]{:S(2)}) copy-start(bf16[1024,2048]{1,0:T(8,128)(2,1)} %refs_7_.1) | copy-start | bytes 12582916
  7.3 17.8 %copy-start.2 = (f32[512,256]{1,0:T(8,128)S(1)}, f32[512,256]{1,0:T(8,128)}, u32[]{:S(2)}) copy-start(f32[512,256]{1,0:T(8,128)} %refs_0_.3) | copy-start | bytes 1572868
  7.3 16.4 %collective-permute-start.1 = (bf16[264,256]{1,0:T(8,128)(2,1)S(1)}, bf16[264,256]{1,0:T(8,128)(2,1)S(1)}, u32[]{:S(2)}, u32[]{:S(2)}) collective-permute-start(bf16[264,256]{1,0:T(8,128)(2,1)S(1)} %get-tuple-element.25), channel_id=1, source_target_pairs={{0,9},{1,8},{4,13},{5,12},{8,1},{9,0},{12,5},{13,4},{2,11},{3,10},... | collective-permute-start | bytes 405512 | tf_op jit(solution)/shard_map/ppermute | solution.py:208
  7.4 18.3 %collective-permute-start.2 = (bf16[264,256]{1,0:T(8,128)(2,1)S(1)}, bf16[264,256]{1,0:T(8,128)(2,1)S(1)}, u32[]{:S(2)}, u32[]{:S(2)}) collective-permute-start(bf16[264,256]{1,0:T(8,128)(2,1)S(1)} %get-tuple-element.31), channel_id=1, source_target_pairs={{0,12},{1,13},{4,8},{5,9},{8,4},{9,5},{12,0},{13,1},{2,14},{3,15},... | collective-permute-start | bytes 405512 | tf_op jit(solution)/shard_map/ppermute | solution.py:208
  10.5 15.3 %collective-permute-start.3 = (bf16[264,256]{1,0:T(8,128)(2,1)S(1)}, bf16[264,256]{1,0:T(8,128)(2,1)S(1)}, u32[]{:S(2)}, u32[]{:S(2)}) collective-permute-start(bf16[264,256]{1,0:T(8,128)(2,1)S(1)} %get-tuple-element.32), channel_id=1, source_target_pairs={{0,13},{1,12},{4,9},{5,8},{8,5},{9,4},{12,1},{13,0},{2,15},{3,14},... | collective-permute-start | bytes 405512 | tf_op jit(solution)/shard_map/ppermute | solution.py:208
  18.4 8.9 %collective-permute-start.4 = (bf16[264,256]{1,0:T(8,128)(2,1)S(1)}, bf16[264,256]{1,0:T(8,128)(2,1)S(1)}, u32[]{:S(2)}, u32[]{:S(2)}) collective-permute-start(bf16[264,256]{1,0:T(8,128)(2,1)S(1)} %get-tuple-element.33), channel_id=1, source_target_pairs={{0,5},{1,4},{4,1},{5,0},{8,13},{9,12},{12,9},{13,8},{2,7},{3,6},{6... | collective-permute-start | bytes 405512 | tf_op jit(solution)/shard_map/ppermute | solution.py:208
  22.4 7.7 %collective-permute-start.5 = (bf16[264,256]{1,0:T(8,128)(2,1)S(1)}, bf16[264,256]{1,0:T(8,128)(2,1)S(1)}, u32[]{:S(2)}, u32[]{:S(2)}) collective-permute-start(bf16[264,256]{1,0:T(8,128)(2,1)S(1)} %get-tuple-element.34), channel_id=1, source_target_pairs={{0,4},{1,5},{4,0},{5,1},{8,12},{9,13},{12,8},{13,9},{2,6},{3,7},{6... | collective-permute-start | bytes 405512 | tf_op jit(solution)/shard_map/ppermute | solution.py:208
  23.6 6.5 %collective-permute-start.6 = (bf16[264,256]{1,0:T(8,128)(2,1)S(1)}, bf16[264,256]{1,0:T(8,128)(2,1)S(1)}, u32[]{:S(2)}, u32[]{:S(2)}) collective-permute-start(bf16[264,256]{1,0:T(8,128)(2,1)S(1)} %get-tuple-element.35), channel_id=1, source_target_pairs={{0,1},{1,0},{4,5},{5,4},{8,9},{9,8},{12,13},{13,12},{2,3},{3,2},{6... | collective-permute-start | bytes 405512 | tf_op jit(solution)/shard_map/ppermute | solution.py:208
  30.1 13.2 %copy-start.1 = (bf16[1024,2048]{1,0:T(8,128)(2,1)S(1)}, bf16[1024,2048]{1,0:T(8,128)(2,1)}, u32[]{:S(2)}) copy-start(bf16[1024,2048]{1,0:T(8,128)(2,1)} %refs_7_.1) | copy-start | bytes 12582916
  30.1 13.2 %copy-start.3 = (s32[1024,1]{0,1:T(1,128)S(1)}, s32[1024,1]{0,1:T(1,128)}, u32[]{:S(2)}) copy-start(s32[1024,1]{0,1:T(1,128)} %param.14) | copy-start | bytes 12292
  30.1 13.2 %copy-start.4 = (s32[1024,1]{0,1:T(1,128)S(1)}, s32[1024,1]{0,1:T(1,128)}, u32[]{:S(2)}) copy-start(s32[1024,1]{0,1:T(1,128)} %param.16) | copy-start | bytes 12292
  30.2 13.2 %copy-start.5 = (s32[1024]{0:T(1024)S(1)}, s32[1024]{0:T(1024)}, u32[]{:S(2)}) copy-start(s32[1024]{0:T(1024)} %param.18) | copy-start | bytes 12292
  30.2 13.2 %copy-start.6 = (s32[1024]{0:T(1024)S(1)}, s32[1024]{0:T(1024)}, u32[]{:S(2)}) copy-start(s32[1024]{0:T(1024)} %param.19) | copy-start | bytes 12292

commit v16 on v15

--- a/solution.py
+++ b/solution.py
@@ -43,12 +43,21 @@
     return jnp.where(mask, jnp.ones((), BF16), jnp.zeros((), BF16))
 
 
-def xor_rows(rows, mine):
-    count = rows.shape[0]
+def turn_rows(rows, n_rows, n_ent, z, c):
+    def moved(di, dj, sign):
+        at = [
+            ((sign * i - di) % n_rows) * n_ent + (sign * j - dj) % n_ent for i in range(n_rows) for j in range(n_ent)
+        ]
+        return jnp.concatenate([rows[k : k + 1] for k in at], axis=0)
+
+    rows = moved(0, 0, -1)
     bit = 1
-    while bit < count:
-        swapped = jnp.concatenate([rows[(k ^ bit) : (k ^ bit) + 1] for k in range(count)], axis=0)
-        rows = jnp.where((mine & bit) > 0, swapped, rows)
+    while bit < n_rows:
+        rows = jnp.where((z & bit) > 0, moved(bit, 0, 1), rows)
+        bit *= 2
+    bit = 1
+    while bit < n_ent:
+        rows = jnp.where((c & bit) > 0, moved(0, bit, 1), rows)
         bit *= 2
     return rows
 
@@ -80,11 +89,7 @@
     chunk[capacity:, :capacity] = lanes_dot(ids, pick).astype(BF16)
 
 
-def position(n_feat):
-    return lax.axis_index(HOME), lax.axis_index("feat") >= n_feat // 2
-
-
-def far_kernel(owners, capacity, n_feat, far, *refs):
+def far_kernel(n_rows, n_ent, capacity, n_feat, far, *refs):
     sources, ranks, place_out, ids_out, feats = refs[:5], refs[5], refs[6], refs[7], refs[8]
     chunks, copies, sems = refs[9 : 9 + len(far)], refs[9 + len(far) : 13 + len(far)], refs[13 + len(far)]
     copies = (*copies, feats)
@@ -95,11 +100,13 @@
         move.wait()
     member, item, member_local, item_local = [copy[...] for copy in copies[:4]]
     rows = member.shape[1]
-    mine, on_item = position(n_feat)
-    rank = ranks_of(owners, member, item)
+    rank = ranks_of(n_rows * n_ent, member, item)
     ranks[...] = rank
+    on_item = lax.axis_index("feat") >= n_feat // 2
     own = jnp.where(on_item, item, member)
-    place = (own ^ mine) * capacity + jnp.where(on_item, rank[1:2], rank[0:1])
+    up, across = own // n_ent - lax.axis_index("rows"), own % n_ent - lax.axis_index("ent")
+    up, across = jnp.where(up < 0, up + n_rows, up), jnp.where(across < 0, across + n_ent, across)
+    place = (up * n_ent + across) * capacity + jnp.where(on_item, rank[1:2], rank[0:1])
     place_out[...] = place
     local = jnp.where(on_item, item_local, member_local)
     high = local >> 8
@@ -144,11 +151,12 @@
         out[...] = chunk_scores(chunk, table, capacity)
 
 
-def scores_kernel(order, capacity, n_feat, n_ent, table, *refs):
-    out, mine = refs[-1], lax.axis_index(HOME)
+def scores_kernel(order, capacity, n_feat, n_rows, n_ent, table, *refs):
+    out = refs[-1]
     scores = [x[...] if x.shape[0] == 1 else chunk_scores(x, table[...], capacity) for x in refs[:-1]]
     scores = dict(zip(order, scores))
-    scores = xor_rows(jnp.concatenate([scores[k] for k in range(len(order))], axis=0), mine)
+    scores = jnp.concatenate([scores[k] for k in range(len(order))], axis=0)
+    scores = turn_rows(scores, n_rows, n_ent, lax.axis_index("rows"), lax.axis_index("ent"))
     for home in range(len(order)):
         for f in range(n_feat):
             out[(home // n_ent * n_feat + f) * n_ent + home % n_ent] = scores[home : home + 1]
@@ -157,7 +165,7 @@
 def home_kernel(
     owners, capacity, n_feat, n_ent, member, item, ranks, clicks, valid, margin, scores, features, out
 ):
-    on_item = position(n_feat)[1]
+    on_item = lax.axis_index("feat") >= n_feat // 2
     total = margin[...]
     hits_of = [one_hot(owner[...], owners).astype(F32) for owner in (member, item)]
     spot_of = [ones(low_hot(ranks[side : side + 1], capacity)) for side in (0, 1)]
@@ -182,11 +190,11 @@
         out[h, :, capacity:] = grad
 
 
-def grads_kernel(order, capacity, scale, coefs, weight, came, *refs):
+def grads_kernel(order, capacity, n_rows, n_ent, scale, coefs, weight, came, *refs):
     chunks, grad_global, grad_coefs = refs[:-2], refs[-2], refs[-1]
     entities = coefs.shape[0]
-    mine = lax.axis_index(HOME)
-    resids = xor_rows(jnp.concatenate([came[h][:, :capacity] for h in range(len(order))], axis=0), mine)
+    resids = jnp.concatenate([came[h][:, :capacity] for h in range(len(order))], axis=0)
+    resids = turn_rows(resids, n_rows, n_ent, lax.axis_index("rows"), lax.axis_index("ent"))
     summed = came[0][:, capacity:]
     for h in range(1, len(order)):
         summed = summed + came[h][:, capacity:]
@@ -204,8 +212,16 @@
     grad_coefs[...] = coefs[...] + both[:entities] + both[entities:]
 
 
-def xor_send(x, axes, size, k):
-    return x if k == 0 else lax.ppermute(x, axes, [(i, i ^ k) for i in range(size)])
+def shift_send(x, n_rows, n_ent, k):
+    if k == 0:
+        return x
+    up, across = divmod(k, n_ent)
+    pairs = [
+        (z * n_ent + c, (z + up) % n_rows * n_ent + (c + across) % n_ent)
+        for z in range(n_rows)
+        for c in range(n_ent)
+    ]
+    return lax.ppermute(x, HOME, pairs)
 
 
 def call(kernel, out_shape, operands, in_specs, flops=0, scratch=(), hidden=False):
@@ -236,7 +252,8 @@
     rows_here, width = entity_feats.shape
     columns = features.shape[1]
     n_feat, n_ent = lax.axis_size("feat"), lax.axis_size("ent")
-    owners = lax.axis_size("rows") * n_ent
+    n_rows = lax.axis_size("rows")
+    owners = n_rows * n_ent
     capacity = 2 * rows_here // owners
     member, item = member_owner.reshape(1, rows_here), item_owner.reshape(1, rows_here)
 
@@ -247,8 +264,12 @@
         return lambda *refs: kernel(*args, *refs)
 
     row = pltpu.VMEM((1, rows_here), jnp.int32)
-    half = owners // 2
-    first, second, near = [half], list(range(half + 1, owners)), list(reversed(range(half)))
+    middle = n_rows // 2
+    away = [middle * n_ent + c for c in range(n_ent)]
+    for c in range(n_ent):
+        for up in range(1, middle):
+            away += [up * n_ent + c, (n_rows - up) * n_ent + c]
+    first, second, near = away[:1], away[1:-2], [*away[-2:], *reversed(range(n_ent))]
     chunk = shape(capacity + IDS, width, dtype=BF16)
     flops = len(first) * 2 * capacity * rows_here * width
 
@@ -256,7 +277,7 @@
         return pltpu.with_memory_space_constraint(x, pltpu.HBM)
 
     ranks, place, ids, feats, *chunks = call(
-        partial(far_kernel, owners, capacity, n_feat, first),
+        partial(far_kernel, n_rows, n_ent, capacity, n_feat, first),
         [
             shape(2, rows_here, dtype=jnp.int32),
             shape(1, rows_here, dtype=jnp.int32),
@@ -282,7 +303,7 @@
         [VMEM] * 3,
         flops=32 * flops,
     )
-    chunks = [xor_send(x, HOME, owners, k) for k, x in zip(first + second, chunks)]
+    chunks = [shift_send(x, n_rows, n_ent, k) for k, x in zip(first + second, chunks)]
     weight = global_weight.astype(F32).reshape(1, columns)
     (global_part,) = call(
         margin_kernel, [shape(1, rows_here)], (place, weight, features), [VMEM] * 3, hidden=True
@@ -295,10 +316,10 @@
         [VMEM] * 4,
         hidden=True,
     )
-    near_chunks = [xor_send(x, HOME, owners, k) for k, x in zip(near, near_chunks)]
+    near_chunks = [shift_send(x, n_rows, n_ent, k) for k, x in zip(near, near_chunks)]
     chunks = dict(zip(first + second + near, chunks + near_chunks))
-    early = (first + second)[: half // 2] + near[-1:]
-    late = (first + second)[half // 2 :] + near[:-1]
+    early = away[:n_ent] + near[-1:]
+    late = away[n_ent:-2] + near[:-1]
     order = early + late
     table, *scores = call(
         partial(early_kernel, capacity),
@@ -308,7 +329,7 @@
         hidden=True,
     )
     (scores,) = call(
-        partial(scores_kernel, order, capacity, n_feat, n_ent),
+        partial(scores_kernel, order, capacity, n_feat, n_rows, n_ent),
         [shape(n_feat * owners, 1, capacity)],
         (table, *scores, *(chunks[k] for k in late)),
         [VMEM] * (1 + owners),
@@ -333,7 +354,7 @@
     )
     came = lax.all_to_all(sent, HOME, split_axis=0, concat_axis=0, tiled=True)
     grad_global, grad_coefs = call(
-        partial(grads_kernel, order, capacity, 1.0 / math.sqrt(rows_here * owners)),
+        partial(grads_kernel, order, capacity, n_rows, n_ent, 1.0 / math.sqrt(rows_here * owners)),
         [shape(1, columns), shape(*coefs.shape)],
         (coefs, weight, came, *(chunks[k] for k in order)),
         [VMEM] * (3 + owners),

time: 55.1 us -> 54.3 us (0.985)
  waiting for transfers between devices: 9.57 us -> 5.48 us
  starting transfers between devices: 9.35 us -> 11.1 us
  blocking collectives: 25.6 us -> 27 us
    ppermute x7, waiting for transfers between devices: 9.57 us -> 5.48 us  [shift_send(): return lax.ppermute(x, HOME, pairs)]
    ppermute x7, starting transfers between devices: 9.35 us -> 11.1 us  [shift_send(): return lax.ppermute(x, HOME, pairs)]
    all_to_all x1, blocking collectives: 12.2 us -> 13.7 us  [body(): lax.all_to_all(scores, EVERY, split_axis=0, concat_axis=0, tiled=True)]
  transfers between devices with their start and end apart: 7 -> 7, of which waited for: 4 -> 3; matrix products, arithmetic and copies ran while one was open for 0% -> 0% of each run, Pallas kernels for 7% -> 7%
where the time goes in v16:
time: 54.3 us; the launch traced here: 54 us
  blocking collectives  27 us (50%)
  starting transfers between devices  11.1 us (20%)
  Pallas kernels  9.6 us (18%)
  waiting for transfers between devices  5.48 us (10%)
  between operations  0.76 us (1%)
    all_to_all x1, blocking collectives, body(): lax.all_to_all(scores, EVERY, split_axis=0, concat_axis=0, tiled=True)  13.7 us
    ppermute x7, starting transfers between devices, shift_send(): return lax.ppermute(x, HOME, pairs)  11.1 us
    pallas_call x8, Pallas kernels, call(): pl.pallas_call(kernel, out_shape=out_shape, in_specs=in_specs, out_specs=...  9.6 us
    all_to_all x1, blocking collectives, body(): came = lax.all_to_all(sent, HOME, split_axis=0, concat_axis=0, tiled=True)  8.4 us
    ppermute x7, waiting for transfers between devices, shift_send(): return lax.ppermute(x, HOME, pairs)  5.48 us
    psum x1, blocking collectives, body(): global_total = lax.psum(global_part, 'feat')  4.93 us
  transfers between devices with their start and end apart: 7, of which 3 were waited for; matrix products, arithmetic and copies ran while one was open for 0% of the time, Pallas kernels for 7%

profile of v16, /device:TPU:0, one launch (start us, length us, event | category | flops | bytes accessed | tf_op | source)
XLA Modules:
  0.0 54.0 jit_solution(5402419562509350976)
XLA Ops:
  0.6 1.6 %shard_map.113 = (s32[2,1024]{1,0:T(2,128)S(1)}, s32[1,1024]{1,0:T(1,128)S(1)}, bf16[8,1024]{1,0:T(8,128)(2,1)S(1)}, bf16[1024,256]{1,0:T(8,128)(2,1)S(1)}, bf16[264,256]{1,0:T(8,128)(2,1)S(1)}) custom-call(s32[1,1024]{1,0:T(1,128)} %bitcast.10, s32[1,1024]{1,0:T(1,128)} %bitcast.12, s32[1,1024]{1,0:T(1,128)} %bitcast.16, s32[1,1024]{1,0:T(1,128)} %bitcast.17, ...), custom_call_target="tpu_custom_call" | custom-call | flops 134217728 | bytes 1228800 | tf_op jit(solution)/shard_map/pallas_call | solution.py:229
  2.2 4.1 %collective-permute-start = (bf16[264,256]{1,0:T(8,128)(2,1)S(1)}, bf16[264,256]{1,0:T(8,128)(2,1)S(1)}, u32[]{:S(2)}, u32[]{:S(2)}) collective-permute-start(bf16[264,256]{1,0:T(8,128)(2,1)S(1)} %get-tuple-element.22), channel_id=1, source_target_pairs={{0,8},{1,9},{4,12},{5,13},{8,0},{9,1},{12,4},{13,5},{2,10},{3,11},... | collective-permute-start | bytes 405512 | tf_op jit(solution)/shard_map/ppermute | solution.py:224
  6.3 0.0 copy-start.7
  6.3 0.0 copy-start
  6.3 1.0 %shard_map.115 = (bf16[264,256]{1,0:T(8,128)(2,1)S(1)}, bf16[264,256]{1,0:T(8,128)(2,1)S(1)}, bf16[264,256]{1,0:T(8,128)(2,1)S(1)}) custom-call(s32[1,1024]{1,0:T(1,128)S(1)} %get-tuple-element.21.place.refs_0_, bf16[8,1024]{1,0:T(8,128)(2,1)S(1)} %get-tuple-element.23.refs_1_, bf16[1024,256]{1,0:T(8,128)(2,1)S(1)} %get-tuple-element.24.refs_2_), custom_call_target="tpu_custom_call" | custom-call | flops 4294967296 | bytes 950272 | tf_op jit(solution)/shard_map/pallas_call | solution.py:229
  7.3 0.0 copy-start.2
  7.3 0.1 collective-permute-start.1
  7.4 1.7 %collective-permute-start.2 = (bf16[264,256]{1,0:T(8,128)(2,1)S(1)}, bf16[264,256]{1,0:T(8,128)(2,1)S(1)}, u32[]{:S(2)}, u32[]{:S(2)}) collective-permute-start(bf16[264,256]{1,0:T(8,128)(2,1)S(1)} %get-tuple-element.31), channel_id=1, source_target_pairs={{0,4},{1,5},{4,8},{5,9},{8,12},{9,13},{12,0},{13,1},{2,6},{3,7},{6... | collective-permute-start | bytes 405512 | tf_op jit(solution)/shard_map/ppermute | solution.py:224
  9.0 2.2 %collective-permute-start.3 = (bf16[264,256]{1,0:T(8,128)(2,1)S(1)}, bf16[264,256]{1,0:T(8,128)(2,1)S(1)}, u32[]{:S(2)}, u32[]{:S(2)}) collective-permute-start(bf16[264,256]{1,0:T(8,128)(2,1)S(1)} %get-tuple-element.32), channel_id=1, source_target_pairs={{0,12},{1,13},{4,0},{5,1},{8,4},{9,5},{12,8},{13,9},{2,14},{3,15},... | collective-permute-start | bytes 405512 | tf_op jit(solution)/shard_map/ppermute | solution.py:224
  11.2 0.0 copy-done.7
  11.3 0.0 copy-done
  11.3 1.2 %shard_map.114 = f32[1,1024]{1,0:T(1,128)S(1)} custom-call(s32[1,1024]{1,0:T(1,128)S(1)} %get-tuple-element.21.place.refs_0_, f32[1,2048]{1,0:T(1,128)S(1)} %bitcast.8, bf16[1024,2048]{1,0:T(8,128)(2,1)S(1)} %copy-done), custom_call_target="tpu_custom_call" | custom-call | tf_op jit(solution)/shard_map/pallas_call | solution.py:229
  12.4 4.9 %psum.7.refs_3_.refs_5_ = f32[1,1024]{1,0:T(1,128)S(1)} all-reduce(f32[1,1024]{1,0:T(1,128)S(1)} %shard_map.114), channel_id=1, replica_groups=mesh['groups'=2,'rows'=4,'feat'=2,'ent'=2] {'feat'}, use_global_device_ids=true, to_apply=%region_0.0 | all-reduce | flops 1024 | bytes 8192 | tf_op jit(solution)/shard_map/psum | solution.py:311
  17.4 1.2 %shard_map.116 = (bf16[264,256]{1,0:T(8,128)(2,1)S(1)}, bf16[264,256]{1,0:T(8,128)(2,1)S(1)}, bf16[264,256]{1,0:T(8,128)(2,1)S(1)}, bf16[264,256]{1,0:T(8,128)(2,1)S(1)}) custom-call(s32[1,1024]{1,0:T(1,128)S(1)} %get-tuple-element.21.place.refs_0_, bf16[8,1024]{1,0:T(8,128)(2,1)S(1)} %get-tuple-element.23.refs_1_, ...), custom_call_target="tpu_custom_call" | custom-call | tf_op jit(solution)/shard_map/pallas_call | solution.py:229
  18.6 0.1 collective-permute-start.4
  18.7 0.7 %collective-permute-done.refs_1_.refs_3_ = bf16[264,256]{1,0:T(8,128)(2,1)S(1)} collective-permute-done((bf16[264,256]{1,0:T(8,128)(2,1)S(1)}, bf16[264,256]{1,0:T(8,128)(2,1)S(1)}, u32[]{:S(2)}, u32[]{:S(2)}) %collective-permute-start) | collective-permute-done | bytes 135200 | tf_op jit(solution)/shard_map/ppermute | solution.py:224
  19.4 2.8 %collective-permute-start.5 = (bf16[264,256]{1,0:T(8,128)(2,1)S(1)}, bf16[264,256]{1,0:T(8,128)(2,1)S(1)}, u32[]{:S(2)}, u32[]{:S(2)}) collective-permute-start(bf16[264,256]{1,0:T(8,128)(2,1)S(1)} %get-tuple-element.34), channel_id=1, source_target_pairs={{0,13},{1,12},{4,1},{5,0},{8,5},{9,4},{12,9},{13,8},{2,15},{3,14},... | collective-permute-start | bytes 405512 | tf_op jit(solution)/shard_map/ppermute | solution.py:224
  22.2 0.0 collective-permute-done.1.refs_2_.refs_4_
  22.2 0.2 collective-permute-start.6
  22.4 0.0 copy-done.2
  22.4 0.6 %shard_map.117 = (bf16[1024,256]{1,0:T(8,128)(2,1)S(1)}, f32[1,256]{1,0:T(1,128)S(1)}, f32[1,256]{1,0:T(1,128)S(1)}, f32[1,256]{1,0:T(1,128)S(1)}) custom-call(f32[512,256]{1,0:T(8,128)S(1)} %copy-done.2, bf16[264,256]{1,0:T(8,128)(2,1)S(1)} %collective-permute-done.refs_1_.refs_3_, bf16[264,256]{1,0:T(8,128)(2,1)S(1)} %collective-permute-done.1.refs_2_.refs_4_, ...), custom_call_target="tpu_custom_call" | custom-call | tf_op jit(solution)/shard_map/pallas_call | solution.py:229
  23.1 0.0 collective-permute-done.2.refs_4_.refs_6_
  23.1 0.0 collective-permute-done.3.refs_5_.refs_7_
  23.1 3.3 %collective-permute-done.4.refs_6_.refs_8_ = bf16[264,256]{1,0:T(8,128)(2,1)S(1)} collective-permute-done((bf16[264,256]{1,0:T(8,128)(2,1)S(1)}, bf16[264,256]{1,0:T(8,128)(2,1)S(1)}, u32[]{:S(2)}, u32[]{:S(2)}) %collective-permute-start.4) | collective-permute-done | bytes 135200 | tf_op jit(solution)/shard_map/ppermute | solution.py:224
  26.4 1.5 %collective-permute-done.5.refs_7_.refs_9_ = bf16[264,256]{1,0:T(8,128)(2,1)S(1)} collective-permute-done((bf16[264,256]{1,0:T(8,128)(2,1)S(1)}, bf16[264,256]{1,0:T(8,128)(2,1)S(1)}, u32[]{:S(2)}, u32[]{:S(2)}) %collective-permute-start.5) | collective-permute-done | bytes 135200 | tf_op jit(solution)/shard_map/ppermute | solution.py:224
  27.8 0.0 collective-permute-done.6.refs_8_.refs_10_
  27.8 0.0 copy-start.1
  27.8 0.0 copy-start.3
  27.8 0.0 copy-start.4
  27.8 0.0 copy-start.5
  27.9 0.0 copy-start.6
  27.9 0.9 %shard_map.118 = f32[16,1,256]{2,1,0:T(1,128)S(1)} custom-call(bf16[1024,256]{1,0:T(8,128)(2,1)S(1)} %get-tuple-element.27.refs_0_, f32[1,256]{1,0:T(1,128)S(1)} %get-tuple-element.28.refs_1_, f32[1,256]{1,0:T(1,128)S(1)} %get-tuple-element.29.refs_2_, f32[1,256]{1,0:T(1,128)S(1)} %get-tuple-element.30.refs_3_, ...), custom_call_target="tpu_custom_call" | custom-call | flops 4294967296 | bytes 1219584 | tf_op jit(solution)/shard_map/pallas_call | solution.py:229
  28.8 13.7 %all_to_all.10.refs_6_ = f32[16,1,256]{2,1,0:T(1,128)S(1)} all-to-all(f32[16,1,256]{2,1,0:T(1,128)S(1)} %shard_map.118), channel_id=1, replica_groups=mesh['groups'=2,'rows'=4,'feat'=2,'ent'=2] {'rows','feat','ent'}, dimensions={0} | all-to-all | bytes 32768 | tf_op jit(solution)/shard_map/all_to_all | solution.py:338
  42.5 0.0 copy-done.1
  42.5 0.0 copy-done.3
  42.5 0.0 copy-done.4
  42.5 0.0 copy-done.5
  42.5 0.0 copy-done.6
  42.5 1.0 %shard_map.119 = f32[8,1,2304]{2,1,0:T(1,128)S(1)} custom-call(s32[1,1024]{1,0:T(1,128)S(1)} %bitcast.11, s32[1,1024]{1,0:T(1,128)S(1)} %bitcast.13, s32[2,1024]{1,0:T(2,128)S(1)} %get-tuple-element.20.refs_2_, s32[1,1024]{1,0:T(1,128)S(1)} %bitcast.14, s32[1,1024]{1,0:T(1,128)S(1)} %bitcast.15, f32[1,1024]{1,0:T(1,128)S(1)} %psum.7.refs_3_.refs_5_, ...), custom_call_target="tpu_custom_call" | custom-call | flops 67108864 | bytes 4313088 | tf_op jit(solution)/shard_map/pallas_call | solution.py:229
  43.6 8.4 %all_to_all.11.refs_2_ = f32[8,1,2304]{2,1,0:T(1,128)S(1)} all-to-all(f32[8,1,2304]{2,1,0:T(1,128)S(1)} %shard_map.119), channel_id=1, replica_groups=mesh['groups'=2,'rows'=4,'feat'=2,'ent'=2] {'rows','ent'}, dimensions={0} | all-to-all | bytes 147456 | tf_op jit(solution)/shard_map/all_to_all | solution.py:355
  52.0 2.1 %shard_map.120 = (f32[1,2048]{1,0:T(1,128)}, f32[512,256]{1,0:T(8,128)}) custom-call(f32[512,256]{1,0:T(8,128)S(1)} %copy-done.2, f32[1,2048]{1,0:T(1,128)S(1)} %bitcast.9, f32[8,1,2304]{2,1,0:T(1,128)S(1)} %all_to_all.11.refs_2_, bf16[264,256]{1,0:T(8,128)(2,1)S(1)} %collective-permute-done.refs_1_.refs_3_, ...), custom_call_target="tpu_custom_call" | custom-call | flops 1073741824 | bytes 2220032 | tf_op jit(solution)/shard_map/pallas_call | solution.py:229
  (1 shorter events, 0.0 us)
Async XLA Ops:
  2.2 17.2 %collective-permute-start = (bf16[264,256]{1,0:T(8,128)(2,1)S(1)}, bf16[264,256]{1,0:T(8,128)(2,1)S(1)}, u32[]{:S(2)}, u32[]{:S(2)}) collective-permute-start(bf16[264,256]{1,0:T(8,128)(2,1)S(1)} %get-tuple-element.22), channel_id=1, source_target_pairs={{0,8},{1,9},{4,12},{5,13},{8,0},{9,1},{12,4},{13,5},{2,10},{3,11},... | collective-permute-start | bytes 405512 | tf_op jit(solution)/shard_map/ppermute | solution.py:224
  6.3 4.9 %copy-start.7 = (bf16[2048]{0:T(1024)(128)(2,1)S(1)}, bf16[2048]{0:T(1024)(128)(2,1)}, u32[]{:S(2)}) copy-start(bf16[2048]{0:T(1024)(128)(2,1)} %param.11) | copy-start | bytes 12292
  6.3 4.9 %copy-start = (bf16[1024,2048]{1,0:T(8,128)(2,1)S(1)}, bf16[1024,2048]{1,0:T(8,128)(2,1)}, u32[]{:S(2)}) copy-start(bf16[1024,2048]{1,0:T(8,128)(2,1)} %refs_7_.1) | copy-start | bytes 12582916
  7.3 15.2 %copy-start.2 = (f32[512,256]{1,0:T(8,128)S(1)}, f32[512,256]{1,0:T(8,128)}, u32[]{:S(2)}) copy-start(f32[512,256]{1,0:T(8,128)} %refs_0_.3) | copy-start | bytes 1572868
  7.3 14.9 %collective-permute-start.1 = (bf16[264,256]{1,0:T(8,128)(2,1)S(1)}, bf16[264,256]{1,0:T(8,128)(2,1)S(1)}, u32[]{:S(2)}, u32[]{:S(2)}) collective-permute-start(bf16[264,256]{1,0:T(8,128)(2,1)S(1)} %get-tuple-element.25), channel_id=1, source_target_pairs={{0,9},{1,8},{4,13},{5,12},{8,1},{9,0},{12,5},{13,4},{2,11},{3,10},... | collective-permute-start | bytes 405512 | tf_op jit(solution)/shard_map/ppermute | solution.py:224
  7.4 15.7 %collective-permute-start.2 = (bf16[264,256]{1,0:T(8,128)(2,1)S(1)}, bf16[264,256]{1,0:T(8,128)(2,1)S(1)}, u32[]{:S(2)}, u32[]{:S(2)}) collective-permute-start(bf16[264,256]{1,0:T(8,128)(2,1)S(1)} %get-tuple-element.31), channel_id=1, source_target_pairs={{0,4},{1,5},{4,8},{5,9},{8,12},{9,13},{12,0},{13,1},{2,6},{3,7},{6... | collective-permute-start | bytes 405512 | tf_op jit(solution)/shard_map/ppermute | solution.py:224
  9.0 14.1 %collective-permute-start.3 = (bf16[264,256]{1,0:T(8,128)(2,1)S(1)}, bf16[264,256]{1,0:T(8,128)(2,1)S(1)}, u32[]{:S(2)}, u32[]{:S(2)}) collective-permute-start(bf16[264,256]{1,0:T(8,128)(2,1)S(1)} %get-tuple-element.32), channel_id=1, source_target_pairs={{0,12},{1,13},{4,0},{5,1},{8,4},{9,5},{12,8},{13,9},{2,14},{3,15},... | collective-permute-start | bytes 405512 | tf_op jit(solution)/shard_map/ppermute | solution.py:224
  18.6 7.8 %collective-permute-start.4 = (bf16[264,256]{1,0:T(8,128)(2,1)S(1)}, bf16[264,256]{1,0:T(8,128)(2,1)S(1)}, u32[]{:S(2)}, u32[]{:S(2)}) collective-permute-start(bf16[264,256]{1,0:T(8,128)(2,1)S(1)} %get-tuple-element.33), channel_id=1, source_target_pairs={{0,5},{1,4},{4,9},{5,8},{8,13},{9,12},{12,1},{13,0},{2,7},{3,6},{6... | collective-permute-start | bytes 405512 | tf_op jit(solution)/shard_map/ppermute | solution.py:224
  19.4 8.4 %collective-permute-start.5 = (bf16[264,256]{1,0:T(8,128)(2,1)S(1)}, bf16[264,256]{1,0:T(8,128)(2,1)S(1)}, u32[]{:S(2)}, u32[]{:S(2)}) collective-permute-start(bf16[264,256]{1,0:T(8,128)(2,1)S(1)} %get-tuple-element.34), channel_id=1, source_target_pairs={{0,13},{1,12},{4,1},{5,0},{8,5},{9,4},{12,9},{13,8},{2,15},{3,14},... | collective-permute-start | bytes 405512 | tf_op jit(solution)/shard_map/ppermute | solution.py:224
  22.2 5.6 %collective-permute-start.6 = (bf16[264,256]{1,0:T(8,128)(2,1)S(1)}, bf16[264,256]{1,0:T(8,128)(2,1)S(1)}, u32[]{:S(2)}, u32[]{:S(2)}) collective-permute-start(bf16[264,256]{1,0:T(8,128)(2,1)S(1)} %get-tuple-element.35), channel_id=1, source_target_pairs={{0,1},{1,0},{4,5},{5,4},{8,9},{9,8},{12,13},{13,12},{2,3},{3,2},{6... | collective-permute-start | bytes 405512 | tf_op jit(solution)/shard_map/ppermute | solution.py:224
  27.8 14.7 %copy-start.1 = (bf16[1024,2048]{1,0:T(8,128)(2,1)S(1)}, bf16[1024,2048]{1,0:T(8,128)(2,1)}, u32[]{:S(2)}) copy-start(bf16[1024,2048]{1,0:T(8,128)(2,1)} %refs_7_.1) | copy-start | bytes 12582916
  27.8 14.7 %copy-start.3 = (s32[1024,1]{0,1:T(1,128)S(1)}, s32[1024,1]{0,1:T(1,128)}, u32[]{:S(2)}) copy-start(s32[1024,1]{0,1:T(1,128)} %param.14) | copy-start | bytes 12292
  27.8 14.7 %copy-start.4 = (s32[1024,1]{0,1:T(1,128)S(1)}, s32[1024,1]{0,1:T(1,128)}, u32[]{:S(2)}) copy-start(s32[1024,1]{0,1:T(1,128)} %param.16) | copy-start | bytes 12292
  27.8 14.7 %copy-start.5 = (s32[1024]{0:T(1024)S(1)}, s32[1024]{0:T(1024)}, u32[]{:S(2)}) copy-start(s32[1024]{0:T(1024)} %param.18) | copy-start | bytes 12292
  27.9 14.7 %copy-start.6 = (s32[1024]{0:T(1024)S(1)}, s32[1024]{0:T(1024)}, u32[]{:S(2)}) copy-start(s32[1024]{0:T(1024)} %param.19) | copy-start | bytes 12292

commit v17 on v16

--- a/solution.py
+++ b/solution.py
@@ -312,7 +312,7 @@
     near_chunks = call(
         partial(rest_kernel, capacity, near),
         [chunk] * len(near),
-        (place, ids, feats, global_total),
+        (place, ids, feats, global_part),
         [VMEM] * 4,
         hidden=True,
     )

time: 54.3 us -> 58 us (1.068)
  blocking collectives: 27 us -> 14.3 us
  starting transfers between devices: 11.1 us -> 20.5 us
  waiting for transfers between devices: 5.48 us -> 9.77 us
  local copies, waits for them, and re-layouts: 0.04 us -> 2.21 us
  Pallas kernels: 9.6 us -> 10.2 us
    all_to_all x1 -> x0, blocking collectives: 13.7 us -> none  [body(): lax.all_to_all(scores, EVERY, split_axis=0, concat_axis=0, tiled=True)]
    all_to_all x0 -> x1, starting transfers between devices: none -> 7.81 us  [body(): lax.all_to_all(scores, EVERY, split_axis=0, concat_axis=0, tiled=True)]
    ppermute x7, waiting for transfers between devices: 5.48 us -> 8.27 us  [shift_send(): return lax.ppermute(x, HOME, pairs)]
    unnamed x16, local copies, waits for them, and re-layouts: 0.04 us -> 2.21 us
    ppermute x7, starting transfers between devices: 11.1 us -> 12.7 us  [shift_send(): return lax.ppermute(x, HOME, pairs)]
    all_to_all x0 -> x1, waiting for transfers between devices: none -> 1.49 us  [body(): lax.all_to_all(scores, EVERY, split_axis=0, concat_axis=0, tiled=True)]
    all_to_all x1, blocking collectives: 8.4 us -> 9.27 us  [body(): came = lax.all_to_all(sent, HOME, split_axis=0, concat_axis=0, tiled=True)]
    pallas_call x8, Pallas kernels: 9.6 us -> 10.2 us  [call(): pl.pallas_call(kernel, out_shape=out_shape, in_specs=in_specs, out_specs=...]
  transfers between devices with their start and end apart: 7 -> 8, of which waited for: 3 -> 4; matrix products, arithmetic and copies ran while one was open for 0% -> 0% of each run, Pallas kernels for 7% -> 7%
where the time goes in v17:
time: 58 us; the launch traced here: 57.7 us
  starting transfers between devices  20.5 us (35%)
  blocking collectives  14.3 us (25%)
  Pallas kernels  10.2 us (18%)
  waiting for transfers between devices  9.77 us (17%)
  local copies, waits for them, and re-layouts  2.21 us (4%)
  between operations  0.76 us (1%)
    ppermute x7, starting transfers between devices, shift_send(): return lax.ppermute(x, HOME, pairs)  12.7 us
    pallas_call x8, Pallas kernels, call(): pl.pallas_call(kernel, out_shape=out_shape, in_specs=in_specs, out_specs=...  10.2 us
    all_to_all x1, blocking collectives, body(): came = lax.all_to_all(sent, HOME, split_axis=0, concat_axis=0, tiled=True)  9.27 us
    ppermute x7, waiting for transfers between devices, shift_send(): return lax.ppermute(x, HOME, pairs)  8.27 us
    all_to_all x1, starting transfers between devices, body(): lax.all_to_all(scores, EVERY, split_axis=0, concat_axis=0, tiled=True)  7.81 us
    psum x1, blocking collectives, body(): global_total = lax.psum(global_part, 'feat')  5 us
    unnamed x16, local copies, waits for them, and re-layouts  2.21 us
    all_to_all x1, waiting for transfers between devices, body(): lax.all_to_all(scores, EVERY, split_axis=0, concat_axis=0, tiled=True)  1.49 us
  transfers between devices with their start and end apart: 8, of which 4 were waited for; matrix products, arithmetic and copies ran while one was open for 0% of the time, Pallas kernels for 7%

profile of v17, /device:TPU:0, one launch (start us, length us, event | category | flops | bytes accessed | tf_op | source)
XLA Modules:
  0.0 57.7 jit_solution(1428031068030380921)
XLA Ops:
  0.6 1.6 %shard_map.113 = (s32[2,1024]{1,0:T(2,128)S(1)}, s32[1,1024]{1,0:T(1,128)S(1)}, bf16[8,1024]{1,0:T(8,128)(2,1)S(1)}, bf16[1024,256]{1,0:T(8,128)(2,1)S(1)}, bf16[264,256]{1,0:T(8,128)(2,1)S(1)}) custom-call(s32[1,1024]{1,0:T(1,128)} %bitcast.10, s32[1,1024]{1,0:T(1,128)} %bitcast.12, s32[1,1024]{1,0:T(1,128)} %bitcast.16, s32[1,1024]{1,0:T(1,128)} %bitcast.17, ...), custom_call_target="tpu_custom_call" | custom-call | flops 134217728 | bytes 1228800 | tf_op jit(solution)/shard_map/pallas_call | solution.py:229
  2.2 4.1 %collective-permute-start = (bf16[264,256]{1,0:T(8,128)(2,1)S(1)}, bf16[264,256]{1,0:T(8,128)(2,1)S(1)}, u32[]{:S(2)}, u32[]{:S(2)}) collective-permute-start(bf16[264,256]{1,0:T(8,128)(2,1)S(1)} %get-tuple-element.22), channel_id=1, source_target_pairs={{0,8},{1,9},{4,12},{5,13},{8,0},{9,1},{12,4},{13,5},{2,10},{3,11},... | collective-permute-start | bytes 405512 | tf_op jit(solution)/shard_map/ppermute | solution.py:224
  6.3 0.0 copy-start.7
  6.3 0.0 copy-start
  6.3 1.0 %shard_map.115 = (bf16[264,256]{1,0:T(8,128)(2,1)S(1)}, bf16[264,256]{1,0:T(8,128)(2,1)S(1)}, bf16[264,256]{1,0:T(8,128)(2,1)S(1)}) custom-call(s32[1,1024]{1,0:T(1,128)S(1)} %get-tuple-element.21.place.refs_0_, bf16[8,1024]{1,0:T(8,128)(2,1)S(1)} %get-tuple-element.23.refs_1_, bf16[1024,256]{1,0:T(8,128)(2,1)S(1)} %get-tuple-element.24.refs_2_), custom_call_target="tpu_custom_call" | custom-call | flops 4294967296 | bytes 950272 | tf_op jit(solution)/shard_map/pallas_call | solution.py:229
  7.3 0.0 copy-start.2
  7.3 0.1 collective-permute-start.1
  7.4 1.7 %collective-permute-start.2 = (bf16[264,256]{1,0:T(8,128)(2,1)S(1)}, bf16[264,256]{1,0:T(8,128)(2,1)S(1)}, u32[]{:S(2)}, u32[]{:S(2)}) collective-permute-start(bf16[264,256]{1,0:T(8,128)(2,1)S(1)} %get-tuple-element.31), channel_id=1, source_target_pairs={{0,4},{1,5},{4,8},{5,9},{8,12},{9,13},{12,0},{13,1},{2,6},{3,7},{6... | collective-permute-start | bytes 405512 | tf_op jit(solution)/shard_map/ppermute | solution.py:224
  9.0 2.2 %collective-permute-start.3 = (bf16[264,256]{1,0:T(8,128)(2,1)S(1)}, bf16[264,256]{1,0:T(8,128)(2,1)S(1)}, u32[]{:S(2)}, u32[]{:S(2)}) collective-permute-start(bf16[264,256]{1,0:T(8,128)(2,1)S(1)} %get-tuple-element.32), channel_id=1, source_target_pairs={{0,12},{1,13},{4,0},{5,1},{8,4},{9,5},{12,8},{13,9},{2,14},{3,15},... | collective-permute-start | bytes 405512 | tf_op jit(solution)/shard_map/ppermute | solution.py:224
  11.2 0.0 copy-done.7
  11.3 0.0 copy-done
  11.3 1.2 %shard_map.114.refs_3_ = f32[1,1024]{1,0:T(1,128)S(1)} custom-call(s32[1,1024]{1,0:T(1,128)S(1)} %get-tuple-element.21.place.refs_0_, f32[1,2048]{1,0:T(1,128)S(1)} %bitcast.8, bf16[1024,2048]{1,0:T(8,128)(2,1)S(1)} %copy-done), custom_call_target="tpu_custom_call" | custom-call | tf_op jit(solution)/shard_map/pallas_call | solution.py:229
  12.4 1.2 %shard_map.116 = (bf16[264,256]{1,0:T(8,128)(2,1)S(1)}, bf16[264,256]{1,0:T(8,128)(2,1)S(1)}, bf16[264,256]{1,0:T(8,128)(2,1)S(1)}, bf16[264,256]{1,0:T(8,128)(2,1)S(1)}) custom-call(s32[1,1024]{1,0:T(1,128)S(1)} %get-tuple-element.21.place.refs_0_, bf16[8,1024]{1,0:T(8,128)(2,1)S(1)} %get-tuple-element.23.refs_1_, ...), custom_call_target="tpu_custom_call" | custom-call | tf_op jit(solution)/shard_map/pallas_call | solution.py:229
  13.7 0.1 collective-permute-start.4
  13.8 5.7 %collective-permute-done.refs_1_.refs_3_ = bf16[264,256]{1,0:T(8,128)(2,1)S(1)} collective-permute-done((bf16[264,256]{1,0:T(8,128)(2,1)S(1)}, bf16[264,256]{1,0:T(8,128)(2,1)S(1)}, u32[]{:S(2)}, u32[]{:S(2)}) %collective-permute-start) | collective-permute-done | bytes 135200 | tf_op jit(solution)/shard_map/ppermute | solution.py:224
  19.5 0.5 collective-permute-start.5
  19.9 1.0 %collective-permute-done.1.refs_2_.refs_4_ = bf16[264,256]{1,0:T(8,128)(2,1)S(1)} collective-permute-done((bf16[264,256]{1,0:T(8,128)(2,1)S(1)}, bf16[264,256]{1,0:T(8,128)(2,1)S(1)}, u32[]{:S(2)}, u32[]{:S(2)}) %collective-permute-start.1) | collective-permute-done | bytes 135200 | tf_op jit(solution)/shard_map/ppermute | solution.py:224
  21.0 4.1 %collective-permute-start.6 = (bf16[264,256]{1,0:T(8,128)(2,1)S(1)}, bf16[264,256]{1,0:T(8,128)(2,1)S(1)}, u32[]{:S(2)}, u32[]{:S(2)}) collective-permute-start(bf16[264,256]{1,0:T(8,128)(2,1)S(1)} %get-tuple-element.35), channel_id=1, source_target_pairs={{0,1},{1,0},{4,5},{5,4},{8,9},{9,8},{12,13},{13,12},{2,3},{3,2},{6... | collective-permute-start | bytes 405512 | tf_op jit(solution)/shard_map/ppermute | solution.py:224
  25.1 0.0 copy-done.2
  25.1 0.6 %shard_map.117 = (bf16[1024,256]{1,0:T(8,128)(2,1)S(1)}, f32[1,256]{1,0:T(1,128)S(1)}, f32[1,256]{1,0:T(1,128)S(1)}, f32[1,256]{1,0:T(1,128)S(1)}) custom-call(f32[512,256]{1,0:T(8,128)S(1)} %copy-done.2, bf16[264,256]{1,0:T(8,128)(2,1)S(1)} %collective-permute-done.refs_1_.refs_3_, bf16[264,256]{1,0:T(8,128)(2,1)S(1)} %collective-permute-done.1.refs_2_.refs_4_, ...), custom_call_target="tpu_custom_call" | custom-call | tf_op jit(solution)/shard_map/pallas_call | solution.py:229
  25.7 0.0 collective-permute-done.2.refs_4_.refs_6_
  25.7 0.0 collective-permute-done.3.refs_5_.refs_7_
  25.7 0.0 collective-permute-done.4.refs_6_.refs_8_
  25.7 1.5 %collective-permute-done.5.refs_7_.refs_9_ = bf16[264,256]{1,0:T(8,128)(2,1)S(1)} collective-permute-done((bf16[264,256]{1,0:T(8,128)(2,1)S(1)}, bf16[264,256]{1,0:T(8,128)(2,1)S(1)}, u32[]{:S(2)}, u32[]{:S(2)}) %collective-permute-start.5) | collective-permute-done | bytes 135200 | tf_op jit(solution)/shard_map/ppermute | solution.py:224
  27.3 0.0 collective-permute-done.6.refs_8_.refs_10_
  27.3 0.0 copy-start.3
  27.3 0.0 copy-start.4
  27.3 0.0 copy-start.5
  27.3 0.0 copy-start.6
  27.3 1.5 %shard_map.118 = f32[16,1,256]{2,1,0:T(1,128)} custom-call(bf16[1024,256]{1,0:T(8,128)(2,1)S(1)} %get-tuple-element.27.refs_0_, f32[1,256]{1,0:T(1,128)S(1)} %get-tuple-element.28.refs_1_, f32[1,256]{1,0:T(1,128)S(1)} %get-tuple-element.29.refs_2_, f32[1,256]{1,0:T(1,128)S(1)} %get-tuple-element.30.refs_3_, ...), custom_call_target="tpu_custom_call" | custom-call | flops 4294967296 | bytes 1219584 | tf_op jit(solution)/shard_map/pallas_call | solution.py:229
  28.9 7.8 %all-to-all-start = ((f32[16,1,256]{2,1,0:T(1,128)}), f32[16,1,256]{2,1,0:T(1,128)S(1)}, u32[]{:S(2)}, u32[]{:S(2)}) async-start(f32[16,1,256]{2,1,0:T(1,128)} %shard_map.118), calls=%async_computation | async-start | bytes 32768 | tf_op jit(solution)/shard_map/all_to_all | solution.py:338
  36.7 5.0 %psum.7.refs_5_ = f32[1,1024]{1,0:T(1,128)S(1)} all-reduce(f32[1,1024]{1,0:T(1,128)S(1)} %shard_map.114.refs_3_), channel_id=1, replica_groups=mesh['groups'=2,'rows'=4,'feat'=2,'ent'=2] {'feat'}, use_global_device_ids=true, to_apply=%region_0.0 | all-reduce | flops 1024 | bytes 8192 | tf_op jit(solution)/shard_map/psum | solution.py:311
  41.7 1.5 %all-to-all-done.refs_6_ = f32[16,1,256]{2,1,0:T(1,128)S(1)} async-done(((f32[16,1,256]{2,1,0:T(1,128)}), f32[16,1,256]{2,1,0:T(1,128)S(1)}, u32[]{:S(2)}, u32[]{:S(2)}) %all-to-all-start) | async-done | bytes 16416 | tf_op jit(solution)/shard_map/all_to_all | solution.py:338
  43.2 0.0 copy-done.3
  43.2 0.0 copy-done.4
  43.2 0.0 copy-done.5
  43.2 0.0 copy-done.6
  43.2 0.0 copy-start.1
  43.2 2.2 %copy-done.1 = bf16[1024,2048]{1,0:T(8,128)(2,1)S(1)} copy-done((bf16[1024,2048]{1,0:T(8,128)(2,1)S(1)}, bf16[1024,2048]{1,0:T(8,128)(2,1)}, u32[]{:S(2)}) %copy-start.1) | copy-done | bytes 4194328
  45.4 1.0 %shard_map.119 = f32[8,1,2304]{2,1,0:T(1,128)S(1)} custom-call(s32[1,1024]{1,0:T(1,128)S(1)} %bitcast.11, s32[1,1024]{1,0:T(1,128)S(1)} %bitcast.13, s32[2,1024]{1,0:T(2,128)S(1)} %get-tuple-element.20.refs_2_, s32[1,1024]{1,0:T(1,128)S(1)} %bitcast.14, s32[1,1024]{1,0:T(1,128)S(1)} %bitcast.15, f32[1,1024]{1,0:T(1,128)S(1)} %psum.7.refs_5_, ...), custom_call_target="tpu_custom_call" | custom-call | flops 67108864 | bytes 4313088 | tf_op jit(solution)/shard_map/pallas_call | solution.py:229
  46.4 9.3 %all_to_all.10.refs_2_ = f32[8,1,2304]{2,1,0:T(1,128)S(1)} all-to-all(f32[8,1,2304]{2,1,0:T(1,128)S(1)} %shard_map.119), channel_id=1, replica_groups=mesh['groups'=2,'rows'=4,'feat'=2,'ent'=2] {'rows','ent'}, dimensions={0} | all-to-all | bytes 147456 | tf_op jit(solution)/shard_map/all_to_all | solution.py:355
  55.7 2.1 %shard_map.120 = (f32[1,2048]{1,0:T(1,128)}, f32[512,256]{1,0:T(8,128)}) custom-call(f32[512,256]{1,0:T(8,128)S(1)} %copy-done.2, f32[1,2048]{1,0:T(1,128)S(1)} %bitcast.9, f32[8,1,2304]{2,1,0:T(1,128)S(1)} %all_to_all.10.refs_2_, bf16[264,256]{1,0:T(8,128)(2,1)S(1)} %collective-permute-done.refs_1_.refs_3_, ...), custom_call_target="tpu_custom_call" | custom-call | flops 1073741824 | bytes 2220032 | tf_op jit(solution)/shard_map/pallas_call | solution.py:229
  (1 shorter events, 0.0 us)
Async XLA Ops:
  2.2 17.2 %collective-permute-start = (bf16[264,256]{1,0:T(8,128)(2,1)S(1)}, bf16[264,256]{1,0:T(8,128)(2,1)S(1)}, u32[]{:S(2)}, u32[]{:S(2)}) collective-permute-start(bf16[264,256]{1,0:T(8,128)(2,1)S(1)} %get-tuple-element.22), channel_id=1, source_target_pairs={{0,8},{1,9},{4,12},{5,13},{8,0},{9,1},{12,4},{13,5},{2,10},{3,11},... | collective-permute-start | bytes 405512 | tf_op jit(solution)/shard_map/ppermute | solution.py:224
  6.3 4.9 %copy-start.7 = (bf16[2048]{0:T(1024)(128)(2,1)S(1)}, bf16[2048]{0:T(1024)(128)(2,1)}, u32[]{:S(2)}) copy-start(bf16[2048]{0:T(1024)(128)(2,1)} %param.11) | copy-start | bytes 12292
  6.3 4.9 %copy-start = (bf16[1024,2048]{1,0:T(8,128)(2,1)S(1)}, bf16[1024,2048]{1,0:T(8,128)(2,1)}, u32[]{:S(2)}) copy-start(bf16[1024,2048]{1,0:T(8,128)(2,1)} %refs_7_.1) | copy-start | bytes 12582916
  7.3 17.8 %copy-start.2 = (f32[512,256]{1,0:T(8,128)S(1)}, f32[512,256]{1,0:T(8,128)}, u32[]{:S(2)}) copy-start(f32[512,256]{1,0:T(8,128)} %refs_0_.3) | copy-start | bytes 1572868
  7.3 13.7 %collective-permute-start.1 = (bf16[264,256]{1,0:T(8,128)(2,1)S(1)}, bf16[264,256]{1,0:T(8,128)(2,1)S(1)}, u32[]{:S(2)}, u32[]{:S(2)}) collective-permute-start(bf16[264,256]{1,0:T(8,128)(2,1)S(1)} %get-tuple-element.25), channel_id=1, source_target_pairs={{0,9},{1,8},{4,13},{5,12},{8,1},{9,0},{12,5},{13,4},{2,11},{3,10},... | collective-permute-start | bytes 405512 | tf_op jit(solution)/shard_map/ppermute | solution.py:224
  7.4 18.3 %collective-permute-start.2 = (bf16[264,256]{1,0:T(8,128)(2,1)S(1)}, bf16[264,256]{1,0:T(8,128)(2,1)S(1)}, u32[]{:S(2)}, u32[]{:S(2)}) collective-permute-start(bf16[264,256]{1,0:T(8,128)(2,1)S(1)} %get-tuple-element.31), channel_id=1, source_target_pairs={{0,4},{1,5},{4,8},{5,9},{8,12},{9,13},{12,0},{13,1},{2,6},{3,7},{6... | collective-permute-start | bytes 405512 | tf_op jit(solution)/shard_map/ppermute | solution.py:224
  9.0 16.7 %collective-permute-start.3 = (bf16[264,256]{1,0:T(8,128)(2,1)S(1)}, bf16[264,256]{1,0:T(8,128)(2,1)S(1)}, u32[]{:S(2)}, u32[]{:S(2)}) collective-permute-start(bf16[264,256]{1,0:T(8,128)(2,1)S(1)} %get-tuple-element.32), channel_id=1, source_target_pairs={{0,12},{1,13},{4,0},{5,1},{8,4},{9,5},{12,8},{13,9},{2,14},{3,15},... | collective-permute-start | bytes 405512 | tf_op jit(solution)/shard_map/ppermute | solution.py:224
  13.7 12.0 %collective-permute-start.4 = (bf16[264,256]{1,0:T(8,128)(2,1)S(1)}, bf16[264,256]{1,0:T(8,128)(2,1)S(1)}, u32[]{:S(2)}, u32[]{:S(2)}) collective-permute-start(bf16[264,256]{1,0:T(8,128)(2,1)S(1)} %get-tuple-element.33), channel_id=1, source_target_pairs={{0,5},{1,4},{4,9},{5,8},{8,13},{9,12},{12,1},{13,0},{2,7},{3,6},{6... | collective-permute-start | bytes 405512 | tf_op jit(solution)/shard_map/ppermute | solution.py:224
  19.5 7.8 %collective-permute-start.5 = (bf16[264,256]{1,0:T(8,128)(2,1)S(1)}, bf16[264,256]{1,0:T(8,128)(2,1)S(1)}, u32[]{:S(2)}, u32[]{:S(2)}) collective-permute-start(bf16[264,256]{1,0:T(8,128)(2,1)S(1)} %get-tuple-element.34), channel_id=1, source_target_pairs={{0,13},{1,12},{4,1},{5,0},{8,5},{9,4},{12,9},{13,8},{2,15},{3,14},... | collective-permute-start | bytes 405512 | tf_op jit(solution)/shard_map/ppermute | solution.py:224
  21.0 6.3 %collective-permute-start.6 = (bf16[264,256]{1,0:T(8,128)(2,1)S(1)}, bf16[264,256]{1,0:T(8,128)(2,1)S(1)}, u32[]{:S(2)}, u32[]{:S(2)}) collective-permute-start(bf16[264,256]{1,0:T(8,128)(2,1)S(1)} %get-tuple-element.35), channel_id=1, source_target_pairs={{0,1},{1,0},{4,5},{5,4},{8,9},{9,8},{12,13},{13,12},{2,3},{3,2},{6... | collective-permute-start | bytes 405512 | tf_op jit(solution)/shard_map/ppermute | solution.py:224
  27.3 15.9 %copy-start.3 = (s32[1024,1]{0,1:T(1,128)S(1)}, s32[1024,1]{0,1:T(1,128)}, u32[]{:S(2)}) copy-start(s32[1024,1]{0,1:T(1,128)} %param.14) | copy-start | bytes 12292
  27.3 15.9 %copy-start.4 = (s32[1024,1]{0,1:T(1,128)S(1)}, s32[1024,1]{0,1:T(1,128)}, u32[]{:S(2)}) copy-start(s32[1024,1]{0,1:T(1,128)} %param.16) | copy-start | bytes 12292
  27.3 15.9 %copy-start.5 = (s32[1024]{0:T(1024)S(1)}, s32[1024]{0:T(1024)}, u32[]{:S(2)}) copy-start(s32[1024]{0:T(1024)} %param.18) | copy-start | bytes 12292
  27.3 15.9 %copy-start.6 = (s32[1024]{0:T(1024)S(1)}, s32[1024]{0:T(1024)}, u32[]{:S(2)}) copy-start(s32[1024]{0:T(1024)} %param.19) | copy-start | bytes 12292
  28.9 14.3 %all-to-all-start = ((f32[16,1,256]{2,1,0:T(1,128)}), f32[16,1,256]{2,1,0:T(1,128)S(1)}, u32[]{:S(2)}, u32[]{:S(2)}) async-start(f32[16,1,256]{2,1,0:T(1,128)} %shard_map.118), calls=%async_computation | async-start | bytes 32768 | tf_op jit(solution)/shard_map/all_to_all | solution.py:338
  43.2 2.2 %copy-start.1 = (bf16[1024,2048]{1,0:T(8,128)(2,1)S(1)}, bf16[1024,2048]{1,0:T(8,128)(2,1)}, u32[]{:S(2)}) copy-start(bf16[1024,2048]{1,0:T(8,128)(2,1)} %refs_7_.1) | copy-start | bytes 12582916

commit v18 on v16

--- a/solution.py
+++ b/solution.py
@@ -151,6 +151,12 @@
         out[...] = chunk_scores(chunk, table, capacity)
 
 
+def later_kernel(capacity, table, *refs):
+    half = len(refs) // 2
+    for chunk, out in zip(refs[:half], refs[half:]):
+        out[...] = chunk_scores(chunk, table[...], capacity)
+
+
 def scores_kernel(order, capacity, n_feat, n_rows, n_ent, table, *refs):
     out = refs[-1]
     scores = [x[...] if x.shape[0] == 1 else chunk_scores(x, table[...], capacity) for x in refs[:-1]]
@@ -319,13 +325,20 @@
     near_chunks = [shift_send(x, n_rows, n_ent, k) for k, x in zip(near, near_chunks)]
     chunks = dict(zip(first + second + near, chunks + near_chunks))
     early = away[:n_ent] + near[-1:]
-    late = away[n_ent:-2] + near[:-1]
-    order = early + late
+    later, late = away[n_ent:-2], near[:-1]
+    order = early + later + late
     table, *scores = call(
         partial(early_kernel, capacity),
         [shape(2 * coefs.shape[0], width, dtype=BF16)] + [shape(1, capacity)] * len(early),
         (coefs, *(chunks[k] for k in early)),
         [VMEM] * (1 + len(early)),
+        hidden=True,
+    )
+    scores += call(
+        partial(later_kernel, capacity),
+        [shape(1, capacity)] * len(later),
+        (table, *(chunks[k] for k in later)),
+        [VMEM] * (1 + len(later)),
         hidden=True,
     )
     (scores,) = call(

time: 54.3 us -> 54 us (level)
    pallas_call x8 -> x9, Pallas kernels: 9.6 us -> 9.8 us  [call(): pl.pallas_call(kernel, out_shape=out_shape, in_specs=in_specs, out_specs=...]
  transfers between devices with their start and end apart: 7 -> 7, of which waited for: 3 -> 3; matrix products, arithmetic and copies ran while one was open for 0% -> 0% of each run, Pallas kernels for 7% -> 8%
where the time goes in v18:
time: 54 us; the launch traced here: 53.8 us
  blocking collectives  27 us (50%)
  starting transfers between devices  11.1 us (21%)
  Pallas kernels  9.8 us (18%)
  waiting for transfers between devices  4.99 us (9%)
  between operations  0.76 us (1%)
    all_to_all x1, blocking collectives, body(): lax.all_to_all(scores, EVERY, split_axis=0, concat_axis=0, tiled=True)  13.7 us
    ppermute x7, starting transfers between devices, shift_send(): return lax.ppermute(x, HOME, pairs)  11.1 us
    pallas_call x9, Pallas kernels, call(): pl.pallas_call(kernel, out_shape=out_shape, in_specs=in_specs, out_specs=...  9.8 us
    all_to_all x1, blocking collectives, body(): came = lax.all_to_all(sent, HOME, split_axis=0, concat_axis=0, tiled=True)  8.4 us
    ppermute x7, waiting for transfers between devices, shift_send(): return lax.ppermute(x, HOME, pairs)  4.99 us
    psum x1, blocking collectives, body(): global_total = lax.psum(global_part, 'feat')  4.93 us
  transfers between devices with their start and end apart: 7, of which 3 were waited for; matrix products, arithmetic and copies ran while one was open for 0% of the time, Pallas kernels for 8%

profile of v18, /device:TPU:0, one launch (start us, length us, event | category | flops | bytes accessed | tf_op | source)
XLA Modules:
  0.0 53.8 jit_solution(6767433234759051728)
XLA Ops:
  0.6 1.6 %shard_map.113 = (s32[2,1024]{1,0:T(2,128)S(1)}, s32[1,1024]{1,0:T(1,128)S(1)}, bf16[8,1024]{1,0:T(8,128)(2,1)S(1)}, bf16[1024,256]{1,0:T(8,128)(2,1)S(1)}, bf16[264,256]{1,0:T(8,128)(2,1)S(1)}) custom-call(s32[1,1024]{1,0:T(1,128)} %bitcast.10, s32[1,1024]{1,0:T(1,128)} %bitcast.12, s32[1,1024]{1,0:T(1,128)} %bitcast.16, s32[1,1024]{1,0:T(1,128)} %bitcast.17, ...), custom_call_target="tpu_custom_call" | custom-call | flops 134217728 | bytes 1228800 | tf_op jit(solution)/shard_map/pallas_call | solution.py:235
  2.2 4.1 %collective-permute-start = (bf16[264,256]{1,0:T(8,128)(2,1)S(1)}, bf16[264,256]{1,0:T(8,128)(2,1)S(1)}, u32[]{:S(2)}, u32[]{:S(2)}) collective-permute-start(bf16[264,256]{1,0:T(8,128)(2,1)S(1)} %get-tuple-element.24), channel_id=1, source_target_pairs={{0,8},{1,9},{4,12},{5,13},{8,0},{9,1},{12,4},{13,5},{2,10},{3,11},... | collective-permute-start | bytes 405512 | tf_op jit(solution)/shard_map/ppermute | solution.py:230
  6.3 0.0 copy-start.7
  6.3 0.0 copy-start
  6.3 1.0 %shard_map.115 = (bf16[264,256]{1,0:T(8,128)(2,1)S(1)}, bf16[264,256]{1,0:T(8,128)(2,1)S(1)}, bf16[264,256]{1,0:T(8,128)(2,1)S(1)}) custom-call(s32[1,1024]{1,0:T(1,128)S(1)} %get-tuple-element.23.place.refs_0_, bf16[8,1024]{1,0:T(8,128)(2,1)S(1)} %get-tuple-element.25.refs_1_, bf16[1024,256]{1,0:T(8,128)(2,1)S(1)} %get-tuple-element.26.refs_2_), custom_call_target="tpu_custom_call" | custom-call | flops 4294967296 | bytes 950272 | tf_op jit(solution)/shard_map/pallas_call | solution.py:235
  7.3 0.0 copy-start.2
  7.3 0.1 collective-permute-start.1
  7.4 1.7 %collective-permute-start.2 = (bf16[264,256]{1,0:T(8,128)(2,1)S(1)}, bf16[264,256]{1,0:T(8,128)(2,1)S(1)}, u32[]{:S(2)}, u32[]{:S(2)}) collective-permute-start(bf16[264,256]{1,0:T(8,128)(2,1)S(1)} %get-tuple-element.33), channel_id=1, source_target_pairs={{0,4},{1,5},{4,8},{5,9},{8,12},{9,13},{12,0},{13,1},{2,6},{3,7},{6... | collective-permute-start | bytes 405512 | tf_op jit(solution)/shard_map/ppermute | solution.py:230
  9.0 2.2 %collective-permute-start.3 = (bf16[264,256]{1,0:T(8,128)(2,1)S(1)}, bf16[264,256]{1,0:T(8,128)(2,1)S(1)}, u32[]{:S(2)}, u32[]{:S(2)}) collective-permute-start(bf16[264,256]{1,0:T(8,128)(2,1)S(1)} %get-tuple-element.34), channel_id=1, source_target_pairs={{0,12},{1,13},{4,0},{5,1},{8,4},{9,5},{12,8},{13,9},{2,14},{3,15},... | collective-permute-start | bytes 405512 | tf_op jit(solution)/shard_map/ppermute | solution.py:230
  11.3 0.0 copy-done.7
  11.3 0.0 copy-done
  11.3 1.2 %shard_map.114 = f32[1,1024]{1,0:T(1,128)S(1)} custom-call(s32[1,1024]{1,0:T(1,128)S(1)} %get-tuple-element.23.place.refs_0_, f32[1,2048]{1,0:T(1,128)S(1)} %bitcast.8, bf16[1024,2048]{1,0:T(8,128)(2,1)S(1)} %copy-done), custom_call_target="tpu_custom_call" | custom-call | tf_op jit(solution)/shard_map/pallas_call | solution.py:235
  12.4 4.9 %psum.7.refs_3_.refs_5_ = f32[1,1024]{1,0:T(1,128)S(1)} all-reduce(f32[1,1024]{1,0:T(1,128)S(1)} %shard_map.114), channel_id=1, replica_groups=mesh['groups'=2,'rows'=4,'feat'=2,'ent'=2] {'feat'}, use_global_device_ids=true, to_apply=%region_0.0 | all-reduce | flops 1024 | bytes 8192 | tf_op jit(solution)/shard_map/psum | solution.py:317
  17.4 1.2 %shard_map.116 = (bf16[264,256]{1,0:T(8,128)(2,1)S(1)}, bf16[264,256]{1,0:T(8,128)(2,1)S(1)}, bf16[264,256]{1,0:T(8,128)(2,1)S(1)}, bf16[264,256]{1,0:T(8,128)(2,1)S(1)}) custom-call(s32[1,1024]{1,0:T(1,128)S(1)} %get-tuple-element.23.place.refs_0_, bf16[8,1024]{1,0:T(8,128)(2,1)S(1)} %get-tuple-element.25.refs_1_, ...), custom_call_target="tpu_custom_call" | custom-call | tf_op jit(solution)/shard_map/pallas_call | solution.py:235
  18.6 0.1 collective-permute-start.4
  18.7 0.7 %collective-permute-done.refs_1_.refs_3_ = bf16[264,256]{1,0:T(8,128)(2,1)S(1)} collective-permute-done((bf16[264,256]{1,0:T(8,128)(2,1)S(1)}, bf16[264,256]{1,0:T(8,128)(2,1)S(1)}, u32[]{:S(2)}, u32[]{:S(2)}) %collective-permute-start) | collective-permute-done | bytes 135200 | tf_op jit(solution)/shard_map/ppermute | solution.py:230
  19.4 2.8 %collective-permute-start.5 = (bf16[264,256]{1,0:T(8,128)(2,1)S(1)}, bf16[264,256]{1,0:T(8,128)(2,1)S(1)}, u32[]{:S(2)}, u32[]{:S(2)}) collective-permute-start(bf16[264,256]{1,0:T(8,128)(2,1)S(1)} %get-tuple-element.38), channel_id=1, source_target_pairs={{0,13},{1,12},{4,1},{5,0},{8,5},{9,4},{12,9},{13,8},{2,15},{3,14},... | collective-permute-start | bytes 405512 | tf_op jit(solution)/shard_map/ppermute | solution.py:230
  22.2 0.0 collective-permute-done.1.refs_2_.refs_4_
  22.2 0.2 collective-permute-start.6
  22.4 0.0 copy-done.2
  22.4 0.6 %shard_map.117 = (bf16[1024,256]{1,0:T(8,128)(2,1)S(1)}, f32[1,256]{1,0:T(1,128)S(1)}, f32[1,256]{1,0:T(1,128)S(1)}, f32[1,256]{1,0:T(1,128)S(1)}) custom-call(f32[512,256]{1,0:T(8,128)S(1)} %copy-done.2, bf16[264,256]{1,0:T(8,128)(2,1)S(1)} %collective-permute-done.refs_1_.refs_3_, bf16[264,256]{1,0:T(8,128)(2,1)S(1)} %collective-permute-done.1.refs_2_.refs_4_, ...), custom_call_target="tpu_custom_call" | custom-call | tf_op jit(solution)/shard_map/pallas_call | solution.py:235
  23.1 0.0 collective-permute-done.2.refs_1_.refs_6_
  23.1 0.0 collective-permute-done.3.refs_2_.refs_7_
  23.1 0.5 shard_map.118
  23.6 2.8 %collective-permute-done.4.refs_6_.refs_8_ = bf16[264,256]{1,0:T(8,128)(2,1)S(1)} collective-permute-done((bf16[264,256]{1,0:T(8,128)(2,1)S(1)}, bf16[264,256]{1,0:T(8,128)(2,1)S(1)}, u32[]{:S(2)}, u32[]{:S(2)}) %collective-permute-start.4) | collective-permute-done | bytes 135200 | tf_op jit(solution)/shard_map/ppermute | solution.py:230
  26.4 1.5 %collective-permute-done.5.refs_7_.refs_9_ = bf16[264,256]{1,0:T(8,128)(2,1)S(1)} collective-permute-done((bf16[264,256]{1,0:T(8,128)(2,1)S(1)}, bf16[264,256]{1,0:T(8,128)(2,1)S(1)}, u32[]{:S(2)}, u32[]{:S(2)}) %collective-permute-start.5) | collective-permute-done | bytes 135200 | tf_op jit(solution)/shard_map/ppermute | solution.py:230
  27.8 0.0 collective-permute-done.6.refs_8_.refs_10_
  27.8 0.0 copy-start.1
  27.8 0.0 copy-start.3
  27.8 0.0 copy-start.4
  27.8 0.0 copy-start.5
  27.9 0.0 copy-start.6
  27.9 0.6 %shard_map.119 = f32[16,1,256]{2,1,0:T(1,128)S(1)} custom-call(bf16[1024,256]{1,0:T(8,128)(2,1)S(1)} %get-tuple-element.29.refs_0_, f32[1,256]{1,0:T(1,128)S(1)} %get-tuple-element.30.refs_1_, f32[1,256]{1,0:T(1,128)S(1)} %get-tuple-element.31.refs_2_, f32[1,256]{1,0:T(1,128)S(1)} %get-tuple-element.32.refs_3_, f32[1,256]{1,0:T(1,128)S(1)} %get-tuple-element.35.refs_4_, ...), custom_call_target="tpu_custom_call" | custom-call | flops 4294967296 | bytes 951296 | tf_op jit(solution)/shard_map/pallas_call | solution.py:235
  28.5 13.7 %all_to_all.10.refs_6_ = f32[16,1,256]{2,1,0:T(1,128)S(1)} all-to-all(f32[16,1,256]{2,1,0:T(1,128)S(1)} %shard_map.119), channel_id=1, replica_groups=mesh['groups'=2,'rows'=4,'feat'=2,'ent'=2] {'rows','feat','ent'}, dimensions={0} | all-to-all | bytes 32768 | tf_op jit(solution)/shard_map/all_to_all | solution.py:351
  42.2 0.0 copy-done.1
  42.2 0.0 copy-done.3
  42.2 0.0 copy-done.4
  42.2 0.0 copy-done.5
  42.2 0.0 copy-done.6
  42.2 1.0 %shard_map.120 = f32[8,1,2304]{2,1,0:T(1,128)S(1)} custom-call(s32[1,1024]{1,0:T(1,128)S(1)} %bitcast.11, s32[1,1024]{1,0:T(1,128)S(1)} %bitcast.13, s32[2,1024]{1,0:T(2,128)S(1)} %get-tuple-element.22.refs_2_, s32[1,1024]{1,0:T(1,128)S(1)} %bitcast.14, s32[1,1024]{1,0:T(1,128)S(1)} %bitcast.15, f32[1,1024]{1,0:T(1,128)S(1)} %psum.7.refs_3_.refs_5_, ...), custom_call_target="tpu_custom_call" | custom-call | flops 67108864 | bytes 4313088 | tf_op jit(solution)/shard_map/pallas_call | solution.py:235
  43.3 8.4 %all_to_all.11.refs_2_ = f32[8,1,2304]{2,1,0:T(1,128)S(1)} all-to-all(f32[8,1,2304]{2,1,0:T(1,128)S(1)} %shard_map.120), channel_id=1, replica_groups=mesh['groups'=2,'rows'=4,'feat'=2,'ent'=2] {'rows','ent'}, dimensions={0} | all-to-all | bytes 147456 | tf_op jit(solution)/shard_map/all_to_all | solution.py:368
  51.7 2.1 %shard_map.121 = (f32[1,2048]{1,0:T(1,128)}, f32[512,256]{1,0:T(8,128)}) custom-call(f32[512,256]{1,0:T(8,128)S(1)} %copy-done.2, f32[1,2048]{1,0:T(1,128)S(1)} %bitcast.9, f32[8,1,2304]{2,1,0:T(1,128)S(1)} %all_to_all.11.refs_2_, bf16[264,256]{1,0:T(8,128)(2,1)S(1)} %collective-permute-done.refs_1_.refs_3_, ...), custom_call_target="tpu_custom_call" | custom-call | flops 1073741824 | bytes 2220032 | tf_op jit(solution)/shard_map/pallas_call | solution.py:235
  (1 shorter events, 0.0 us)
Async XLA Ops:
  2.2 17.2 %collective-permute-start = (bf16[264,256]{1,0:T(8,128)(2,1)S(1)}, bf16[264,256]{1,0:T(8,128)(2,1)S(1)}, u32[]{:S(2)}, u32[]{:S(2)}) collective-permute-start(bf16[264,256]{1,0:T(8,128)(2,1)S(1)} %get-tuple-element.24), channel_id=1, source_target_pairs={{0,8},{1,9},{4,12},{5,13},{8,0},{9,1},{12,4},{13,5},{2,10},{3,11},... | collective-permute-start | bytes 405512 | tf_op jit(solution)/shard_map/ppermute | solution.py:230
  6.3 4.9 %copy-start.7 = (bf16[2048]{0:T(1024)(128)(2,1)S(1)}, bf16[2048]{0:T(1024)(128)(2,1)}, u32[]{:S(2)}) copy-start(bf16[2048]{0:T(1024)(128)(2,1)} %param.11) | copy-start | bytes 12292
  6.3 4.9 %copy-start = (bf16[1024,2048]{1,0:T(8,128)(2,1)S(1)}, bf16[1024,2048]{1,0:T(8,128)(2,1)}, u32[]{:S(2)}) copy-start(bf16[1024,2048]{1,0:T(8,128)(2,1)} %refs_7_.1) | copy-start | bytes 12582916
  7.3 15.2 %copy-start.2 = (f32[512,256]{1,0:T(8,128)S(1)}, f32[512,256]{1,0:T(8,128)}, u32[]{:S(2)}) copy-start(f32[512,256]{1,0:T(8,128)} %refs_0_.3) | copy-start | bytes 1572868
  7.3 14.9 %collective-permute-start.1 = (bf16[264,256]{1,0:T(8,128)(2,1)S(1)}, bf16[264,256]{1,0:T(8,128)(2,1)S(1)}, u32[]{:S(2)}, u32[]{:S(2)}) collective-permute-start(bf16[264,256]{1,0:T(8,128)(2,1)S(1)} %get-tuple-element.27), channel_id=1, source_target_pairs={{0,9},{1,8},{4,13},{5,12},{8,1},{9,0},{12,5},{13,4},{2,11},{3,10},... | collective-permute-start | bytes 405512 | tf_op jit(solution)/shard_map/ppermute | solution.py:230
  7.4 15.7 %collective-permute-start.2 = (bf16[264,256]{1,0:T(8,128)(2,1)S(1)}, bf16[264,256]{1,0:T(8,128)(2,1)S(1)}, u32[]{:S(2)}, u32[]{:S(2)}) collective-permute-start(bf16[264,256]{1,0:T(8,128)(2,1)S(1)} %get-tuple-element.33), channel_id=1, source_target_pairs={{0,4},{1,5},{4,8},{5,9},{8,12},{9,13},{12,0},{13,1},{2,6},{3,7},{6... | collective-permute-start | bytes 405512 | tf_op jit(solution)/shard_map/ppermute | solution.py:230
  9.0 14.1 %collective-permute-start.3 = (bf16[264,256]{1,0:T(8,128)(2,1)S(1)}, bf16[264,256]{1,0:T(8,128)(2,1)S(1)}, u32[]{:S(2)}, u32[]{:S(2)}) collective-permute-start(bf16[264,256]{1,0:T(8,128)(2,1)S(1)} %get-tuple-element.34), channel_id=1, source_target_pairs={{0,12},{1,13},{4,0},{5,1},{8,4},{9,5},{12,8},{13,9},{2,14},{3,15},... | collective-permute-start | bytes 405512 | tf_op jit(solution)/shard_map/ppermute | solution.py:230
  18.6 7.7 %collective-permute-start.4 = (bf16[264,256]{1,0:T(8,128)(2,1)S(1)}, bf16[264,256]{1,0:T(8,128)(2,1)S(1)}, u32[]{:S(2)}, u32[]{:S(2)}) collective-permute-start(bf16[264,256]{1,0:T(8,128)(2,1)S(1)} %get-tuple-element.37), channel_id=1, source_target_pairs={{0,5},{1,4},{4,9},{5,8},{8,13},{9,12},{12,1},{13,0},{2,7},{3,6},{6... | collective-permute-start | bytes 405512 | tf_op jit(solution)/shard_map/ppermute | solution.py:230
  19.4 8.4 %collective-permute-start.5 = (bf16[264,256]{1,0:T(8,128)(2,1)S(1)}, bf16[264,256]{1,0:T(8,128)(2,1)S(1)}, u32[]{:S(2)}, u32[]{:S(2)}) collective-permute-start(bf16[264,256]{1,0:T(8,128)(2,1)S(1)} %get-tuple-element.38), channel_id=1, source_target_pairs={{0,13},{1,12},{4,1},{5,0},{8,5},{9,4},{12,9},{13,8},{2,15},{3,14},... | collective-permute-start | bytes 405512 | tf_op jit(solution)/shard_map/ppermute | solution.py:230
  22.2 5.6 %collective-permute-start.6 = (bf16[264,256]{1,0:T(8,128)(2,1)S(1)}, bf16[264,256]{1,0:T(8,128)(2,1)S(1)}, u32[]{:S(2)}, u32[]{:S(2)}) collective-permute-start(bf16[264,256]{1,0:T(8,128)(2,1)S(1)} %get-tuple-element.39), channel_id=1, source_target_pairs={{0,1},{1,0},{4,5},{5,4},{8,9},{9,8},{12,13},{13,12},{2,3},{3,2},{6... | collective-permute-start | bytes 405512 | tf_op jit(solution)/shard_map/ppermute | solution.py:230
  27.8 14.4 %copy-start.1 = (bf16[1024,2048]{1,0:T(8,128)(2,1)S(1)}, bf16[1024,2048]{1,0:T(8,128)(2,1)}, u32[]{:S(2)}) copy-start(bf16[1024,2048]{1,0:T(8,128)(2,1)} %refs_7_.1) | copy-start | bytes 12582916
  27.8 14.4 %copy-start.3 = (s32[1024,1]{0,1:T(1,128)S(1)}, s32[1024,1]{0,1:T(1,128)}, u32[]{:S(2)}) copy-start(s32[1024,1]{0,1:T(1,128)} %param.14) | copy-start | bytes 12292
  27.8 14.4 %copy-start.4 = (s32[1024,1]{0,1:T(1,128)S(1)}, s32[1024,1]{0,1:T(1,128)}, u32[]{:S(2)}) copy-start(s32[1024,1]{0,1:T(1,128)} %param.16) | copy-start | bytes 12292
  27.8 14.4 %copy-start.5 = (s32[1024]{0:T(1024)S(1)}, s32[1024]{0:T(1024)}, u32[]{:S(2)}) copy-start(s32[1024]{0:T(1024)} %param.18) | copy-start | bytes 12292
  27.9 14.4 %copy-start.6 = (s32[1024]{0:T(1024)S(1)}, s32[1024]{0:T(1024)}, u32[]{:S(2)}) copy-start(s32[1024]{0:T(1024)} %param.19) | copy-start | bytes 12292

commit v19 on v18

--- a/solution.py
+++ b/solution.py
@@ -271,10 +271,9 @@
 
     row = pltpu.VMEM((1, rows_here), jnp.int32)
     middle = n_rows // 2
-    away = [middle * n_ent + c for c in range(n_ent)]
-    for c in range(n_ent):
-        for up in range(1, middle):
-            away += [up * n_ent + c, (n_rows - up) * n_ent + c]
+    away = [up * n_ent for half in range(1, middle) for up in (half, n_rows - half)]
+    away += [middle * n_ent + c for c in range(n_ent)]
+    away += [up * n_ent + c for c in range(1, n_ent) for half in range(1, middle) for up in (half, n_rows - half)]
     first, second, near = away[:1], away[1:-2], [*away[-2:], *reversed(range(n_ent))]
     chunk = shape(capacity + IDS, width, dtype=BF16)
     flops = len(first) * 2 * capacity * rows_here * width

time: 54 us -> 54.1 us (level)
  waiting for transfers between devices: 4.99 us -> 8.68 us
  blocking collectives: 27 us -> 23.8 us
    ppermute x7, waiting for transfers between devices: 4.99 us -> 8.68 us  [shift_send(): return lax.ppermute(x, HOME, pairs)]
    all_to_all x1, blocking collectives: 13.7 us -> 10.5 us  [body(): lax.all_to_all(scores, EVERY, split_axis=0, concat_axis=0, tiled=True)]
where the time goes in v19:
time: 54.1 us; the launch traced here: 53.8 us
  blocking collectives  23.8 us (44%)
  starting transfers between devices  10.7 us (20%)
  Pallas kernels  9.79 us (18%)
  waiting for transfers between devices  8.68 us (16%)
  between operations  0.76 us (1%)
    ppermute x7, starting transfers between devices, shift_send(): return lax.ppermute(x, HOME, pairs)  10.7 us
    all_to_all x1, blocking collectives, body(): lax.all_to_all(scores, EVERY, split_axis=0, concat_axis=0, tiled=True)  10.5 us
    pallas_call x9, Pallas kernels, call(): pl.pallas_call(kernel, out_shape=out_shape, in_specs=in_specs, out_specs=...  9.79 us
    ppermute x7, waiting for transfers between devices, shift_send(): return lax.ppermute(x, HOME, pairs)  8.68 us
    all_to_all x1, blocking collectives, body(): came = lax.all_to_all(sent, HOME, split_axis=0, concat_axis=0, tiled=True)  8.4 us
    psum x1, blocking collectives, body(): global_total = lax.psum(global_part, 'feat')  4.93 us
  transfers between devices with their start and end apart: 7, of which 3 were waited for; matrix products, arithmetic and copies ran while one was open for 0% of the time, Pallas kernels for 8%

profile of v19, /device:TPU:0, one launch (start us, length us, event | category | flops | bytes accessed | tf_op | source)
XLA Modules:
  0.0 53.8 jit_solution(17635301796319914676)
XLA Ops:
  0.6 1.6 %shard_map.113 = (s32[2,1024]{1,0:T(2,128)S(1)}, s32[1,1024]{1,0:T(1,128)S(1)}, bf16[8,1024]{1,0:T(8,128)(2,1)S(1)}, bf16[1024,256]{1,0:T(8,128)(2,1)S(1)}, bf16[264,256]{1,0:T(8,128)(2,1)S(1)}) custom-call(s32[1,1024]{1,0:T(1,128)} %bitcast.10, s32[1,1024]{1,0:T(1,128)} %bitcast.12, s32[1,1024]{1,0:T(1,128)} %bitcast.16, s32[1,1024]{1,0:T(1,128)} %bitcast.17, ...), custom_call_target="tpu_custom_call" | custom-call | flops 134217728 | bytes 1228800 | tf_op jit(solution)/shard_map/pallas_call | solution.py:235
  2.2 3.1 %collective-permute-start = (bf16[264,256]{1,0:T(8,128)(2,1)S(1)}, bf16[264,256]{1,0:T(8,128)(2,1)S(1)}, u32[]{:S(2)}, u32[]{:S(2)}) collective-permute-start(bf16[264,256]{1,0:T(8,128)(2,1)S(1)} %get-tuple-element.24), channel_id=1, source_target_pairs={{0,4},{1,5},{4,8},{5,9},{8,12},{9,13},{12,0},{13,1},{2,6},{3,7},{6... | collective-permute-start | bytes 405512 | tf_op jit(solution)/shard_map/ppermute | solution.py:230
  5.3 0.0 copy-start.7
  5.3 0.0 copy-start
  5.3 1.0 %shard_map.115 = (bf16[264,256]{1,0:T(8,128)(2,1)S(1)}, bf16[264,256]{1,0:T(8,128)(2,1)S(1)}, bf16[264,256]{1,0:T(8,128)(2,1)S(1)}) custom-call(s32[1,1024]{1,0:T(1,128)S(1)} %get-tuple-element.23.place.refs_0_, bf16[8,1024]{1,0:T(8,128)(2,1)S(1)} %get-tuple-element.25.refs_1_, bf16[1024,256]{1,0:T(8,128)(2,1)S(1)} %get-tuple-element.26.refs_2_), custom_call_target="tpu_custom_call" | custom-call | flops 4294967296 | bytes 950272 | tf_op jit(solution)/shard_map/pallas_call | solution.py:235
  6.3 0.0 copy-start.2
  6.3 2.1 %collective-permute-start.1 = (bf16[264,256]{1,0:T(8,128)(2,1)S(1)}, bf16[264,256]{1,0:T(8,128)(2,1)S(1)}, u32[]{:S(2)}, u32[]{:S(2)}) collective-permute-start(bf16[264,256]{1,0:T(8,128)(2,1)S(1)} %get-tuple-element.27), channel_id=1, source_target_pairs={{0,12},{1,13},{4,0},{5,1},{8,4},{9,5},{12,8},{13,9},{2,14},{3,15},... | collective-permute-start | bytes 405512 | tf_op jit(solution)/shard_map/ppermute | solution.py:230
  8.4 1.0 %collective-permute-start.2 = (bf16[264,256]{1,0:T(8,128)(2,1)S(1)}, bf16[264,256]{1,0:T(8,128)(2,1)S(1)}, u32[]{:S(2)}, u32[]{:S(2)}) collective-permute-start(bf16[264,256]{1,0:T(8,128)(2,1)S(1)} %get-tuple-element.33), channel_id=1, source_target_pairs={{0,8},{1,9},{4,12},{5,13},{8,0},{9,1},{12,4},{13,5},{2,10},{3,11},... | collective-permute-start | bytes 405512 | tf_op jit(solution)/shard_map/ppermute | solution.py:230
  9.4 0.8 %collective-permute-start.3 = (bf16[264,256]{1,0:T(8,128)(2,1)S(1)}, bf16[264,256]{1,0:T(8,128)(2,1)S(1)}, u32[]{:S(2)}, u32[]{:S(2)}) collective-permute-start(bf16[264,256]{1,0:T(8,128)(2,1)S(1)} %get-tuple-element.34), channel_id=1, source_target_pairs={{0,9},{1,8},{4,13},{5,12},{8,1},{9,0},{12,5},{13,4},{2,11},{3,10},... | collective-permute-start | bytes 405512 | tf_op jit(solution)/shard_map/ppermute | solution.py:230
  10.2 0.0 copy-done.7
  10.2 0.0 copy-done
  10.2 1.2 %shard_map.114 = f32[1,1024]{1,0:T(1,128)S(1)} custom-call(s32[1,1024]{1,0:T(1,128)S(1)} %get-tuple-element.23.place.refs_0_, f32[1,2048]{1,0:T(1,128)S(1)} %bitcast.8, bf16[1024,2048]{1,0:T(8,128)(2,1)S(1)} %copy-done), custom_call_target="tpu_custom_call" | custom-call | tf_op jit(solution)/shard_map/pallas_call | solution.py:235
  11.4 4.9 %psum.7.refs_3_.refs_5_ = f32[1,1024]{1,0:T(1,128)S(1)} all-reduce(f32[1,1024]{1,0:T(1,128)S(1)} %shard_map.114), channel_id=1, replica_groups=mesh['groups'=2,'rows'=4,'feat'=2,'ent'=2] {'feat'}, use_global_device_ids=true, to_apply=%region_0.0 | all-reduce | flops 1024 | bytes 8192 | tf_op jit(solution)/shard_map/psum | solution.py:316
  16.3 1.2 %shard_map.116 = (bf16[264,256]{1,0:T(8,128)(2,1)S(1)}, bf16[264,256]{1,0:T(8,128)(2,1)S(1)}, bf16[264,256]{1,0:T(8,128)(2,1)S(1)}, bf16[264,256]{1,0:T(8,128)(2,1)S(1)}) custom-call(s32[1,1024]{1,0:T(1,128)S(1)} %get-tuple-element.23.place.refs_0_, bf16[8,1024]{1,0:T(8,128)(2,1)S(1)} %get-tuple-element.25.refs_1_, ...), custom_call_target="tpu_custom_call" | custom-call | tf_op jit(solution)/shard_map/pallas_call | solution.py:235
  17.6 0.1 collective-permute-start.4
  17.6 0.0 collective-permute-done.refs_1_.refs_3_
  17.6 3.6 %collective-permute-start.5 = (bf16[264,256]{1,0:T(8,128)(2,1)S(1)}, bf16[264,256]{1,0:T(8,128)(2,1)S(1)}, u32[]{:S(2)}, u32[]{:S(2)}) collective-permute-start(bf16[264,256]{1,0:T(8,128)(2,1)S(1)} %get-tuple-element.38), channel_id=1, source_target_pairs={{0,13},{1,12},{4,1},{5,0},{8,5},{9,4},{12,9},{13,8},{2,15},{3,14},... | collective-permute-start | bytes 405512 | tf_op jit(solution)/shard_map/ppermute | solution.py:230
  21.2 0.0 collective-permute-done.1.refs_2_.refs_4_
  21.2 0.1 collective-permute-start.6
  21.3 0.0 copy-done.2
  21.3 0.6 %shard_map.117 = (bf16[1024,256]{1,0:T(8,128)(2,1)S(1)}, f32[1,256]{1,0:T(1,128)S(1)}, f32[1,256]{1,0:T(1,128)S(1)}, f32[1,256]{1,0:T(1,128)S(1)}) custom-call(f32[512,256]{1,0:T(8,128)S(1)} %copy-done.2, bf16[264,256]{1,0:T(8,128)(2,1)S(1)} %collective-permute-done.refs_1_.refs_3_, bf16[264,256]{1,0:T(8,128)(2,1)S(1)} %collective-permute-done.1.refs_2_.refs_4_, ...), custom_call_target="tpu_custom_call" | custom-call | tf_op jit(solution)/shard_map/pallas_call | solution.py:235
  21.9 3.7 %collective-permute-done.2.refs_1_.refs_6_ = bf16[264,256]{1,0:T(8,128)(2,1)S(1)} collective-permute-done((bf16[264,256]{1,0:T(8,128)(2,1)S(1)}, bf16[264,256]{1,0:T(8,128)(2,1)S(1)}, u32[]{:S(2)}, u32[]{:S(2)}) %collective-permute-start.2) | collective-permute-done | bytes 135200 | tf_op jit(solution)/shard_map/ppermute | solution.py:230
  25.6 2.6 %collective-permute-done.3.refs_2_.refs_7_ = bf16[264,256]{1,0:T(8,128)(2,1)S(1)} collective-permute-done((bf16[264,256]{1,0:T(8,128)(2,1)S(1)}, bf16[264,256]{1,0:T(8,128)(2,1)S(1)}, u32[]{:S(2)}, u32[]{:S(2)}) %collective-permute-start.3) | collective-permute-done | bytes 135200 | tf_op jit(solution)/shard_map/ppermute | solution.py:230
  28.2 0.5 shard_map.118
  28.7 0.0 collective-permute-done.4.refs_6_.refs_8_
  28.7 2.4 %collective-permute-done.5.refs_7_.refs_9_ = bf16[264,256]{1,0:T(8,128)(2,1)S(1)} collective-permute-done((bf16[264,256]{1,0:T(8,128)(2,1)S(1)}, bf16[264,256]{1,0:T(8,128)(2,1)S(1)}, u32[]{:S(2)}, u32[]{:S(2)}) %collective-permute-start.5) | collective-permute-done | bytes 135200 | tf_op jit(solution)/shard_map/ppermute | solution.py:230
  31.1 0.0 collective-permute-done.6.refs_8_.refs_10_
  31.1 0.0 copy-start.1
  31.1 0.0 copy-start.3
  31.1 0.0 copy-start.4
  31.1 0.0 copy-start.5
  31.1 0.0 copy-start.6
  31.1 0.6 %shard_map.119 = f32[16,1,256]{2,1,0:T(1,128)S(1)} custom-call(bf16[1024,256]{1,0:T(8,128)(2,1)S(1)} %get-tuple-element.29.refs_0_, f32[1,256]{1,0:T(1,128)S(1)} %get-tuple-element.30.refs_1_, f32[1,256]{1,0:T(1,128)S(1)} %get-tuple-element.31.refs_2_, f32[1,256]{1,0:T(1,128)S(1)} %get-tuple-element.32.refs_3_, f32[1,256]{1,0:T(1,128)S(1)} %get-tuple-element.35.refs_4_, ...), custom_call_target="tpu_custom_call" | custom-call | flops 4294967296 | bytes 951296 | tf_op jit(solution)/shard_map/pallas_call | solution.py:235
  31.8 10.5 %all_to_all.10.refs_6_ = f32[16,1,256]{2,1,0:T(1,128)S(1)} all-to-all(f32[16,1,256]{2,1,0:T(1,128)S(1)} %shard_map.119), channel_id=1, replica_groups=mesh['groups'=2,'rows'=4,'feat'=2,'ent'=2] {'rows','feat','ent'}, dimensions={0} | all-to-all | bytes 32768 | tf_op jit(solution)/shard_map/all_to_all | solution.py:350
  42.3 0.0 copy-done.1
  42.3 0.0 copy-done.3
  42.3 0.0 copy-done.4
  42.3 0.0 copy-done.5
  42.3 0.0 copy-done.6
  42.3 1.0 %shard_map.120 = f32[8,1,2304]{2,1,0:T(1,128)S(1)} custom-call(s32[1,1024]{1,0:T(1,128)S(1)} %bitcast.11, s32[1,1024]{1,0:T(1,128)S(1)} %bitcast.13, s32[2,1024]{1,0:T(2,128)S(1)} %get-tuple-element.22.refs_2_, s32[1,1024]{1,0:T(1,128)S(1)} %bitcast.14, s32[1,1024]{1,0:T(1,128)S(1)} %bitcast.15, f32[1,1024]{1,0:T(1,128)S(1)} %psum.7.refs_3_.refs_5_, ...), custom_call_target="tpu_custom_call" | custom-call | flops 67108864 | bytes 4313088 | tf_op jit(solution)/shard_map/pallas_call | solution.py:235
  43.4 8.4 %all_to_all.11.refs_2_ = f32[8,1,2304]{2,1,0:T(1,128)S(1)} all-to-all(f32[8,1,2304]{2,1,0:T(1,128)S(1)} %shard_map.120), channel_id=1, replica_groups=mesh['groups'=2,'rows'=4,'feat'=2,'ent'=2] {'rows','ent'}, dimensions={0} | all-to-all | bytes 147456 | tf_op jit(solution)/shard_map/all_to_all | solution.py:367
  51.8 2.1 %shard_map.121 = (f32[1,2048]{1,0:T(1,128)}, f32[512,256]{1,0:T(8,128)}) custom-call(f32[512,256]{1,0:T(8,128)S(1)} %copy-done.2, f32[1,2048]{1,0:T(1,128)S(1)} %bitcast.9, f32[8,1,2304]{2,1,0:T(1,128)S(1)} %all_to_all.11.refs_2_, bf16[264,256]{1,0:T(8,128)(2,1)S(1)} %collective-permute-done.refs_1_.refs_3_, ...), custom_call_target="tpu_custom_call" | custom-call | flops 1073741824 | bytes 2220032 | tf_op jit(solution)/shard_map/pallas_call | solution.py:235
  (1 shorter events, 0.0 us)
Async XLA Ops:
  2.2 15.4 %collective-permute-start = (bf16[264,256]{1,0:T(8,128)(2,1)S(1)}, bf16[264,256]{1,0:T(8,128)(2,1)S(1)}, u32[]{:S(2)}, u32[]{:S(2)}) collective-permute-start(bf16[264,256]{1,0:T(8,128)(2,1)S(1)} %get-tuple-element.24), channel_id=1, source_target_pairs={{0,4},{1,5},{4,8},{5,9},{8,12},{9,13},{12,0},{13,1},{2,6},{3,7},{6... | collective-permute-start | bytes 405512 | tf_op jit(solution)/shard_map/ppermute | solution.py:230
  5.3 4.9 %copy-start.7 = (bf16[2048]{0:T(1024)(128)(2,1)S(1)}, bf16[2048]{0:T(1024)(128)(2,1)}, u32[]{:S(2)}) copy-start(bf16[2048]{0:T(1024)(128)(2,1)} %param.11) | copy-start | bytes 12292
  5.3 4.9 %copy-start = (bf16[1024,2048]{1,0:T(8,128)(2,1)S(1)}, bf16[1024,2048]{1,0:T(8,128)(2,1)}, u32[]{:S(2)}) copy-start(bf16[1024,2048]{1,0:T(8,128)(2,1)} %refs_7_.1) | copy-start | bytes 12582916
  6.3 15.0 %copy-start.2 = (f32[512,256]{1,0:T(8,128)S(1)}, f32[512,256]{1,0:T(8,128)}, u32[]{:S(2)}) copy-start(f32[512,256]{1,0:T(8,128)} %refs_0_.3) | copy-start | bytes 1572868
  6.3 14.9 %collective-permute-start.1 = (bf16[264,256]{1,0:T(8,128)(2,1)S(1)}, bf16[264,256]{1,0:T(8,128)(2,1)S(1)}, u32[]{:S(2)}, u32[]{:S(2)}) collective-permute-start(bf16[264,256]{1,0:T(8,128)(2,1)S(1)} %get-tuple-element.27), channel_id=1, source_target_pairs={{0,12},{1,13},{4,0},{5,1},{8,4},{9,5},{12,8},{13,9},{2,14},{3,15},... | collective-permute-start | bytes 405512 | tf_op jit(solution)/shard_map/ppermute | solution.py:230
  8.4 17.2 %collective-permute-start.2 = (bf16[264,256]{1,0:T(8,128)(2,1)S(1)}, bf16[264,256]{1,0:T(8,128)(2,1)S(1)}, u32[]{:S(2)}, u32[]{:S(2)}) collective-permute-start(bf16[264,256]{1,0:T(8,128)(2,1)S(1)} %get-tuple-element.33), channel_id=1, source_target_pairs={{0,8},{1,9},{4,12},{5,13},{8,0},{9,1},{12,4},{13,5},{2,10},{3,11},... | collective-permute-start | bytes 405512 | tf_op jit(solution)/shard_map/ppermute | solution.py:230
  9.4 18.8 %collective-permute-start.3 = (bf16[264,256]{1,0:T(8,128)(2,1)S(1)}, bf16[264,256]{1,0:T(8,128)(2,1)S(1)}, u32[]{:S(2)}, u32[]{:S(2)}) collective-permute-start(bf16[264,256]{1,0:T(8,128)(2,1)S(1)} %get-tuple-element.34), channel_id=1, source_target_pairs={{0,9},{1,8},{4,13},{5,12},{8,1},{9,0},{12,5},{13,4},{2,11},{3,10},... | collective-permute-start | bytes 405512 | tf_op jit(solution)/shard_map/ppermute | solution.py:230
  17.6 11.1 %collective-permute-start.4 = (bf16[264,256]{1,0:T(8,128)(2,1)S(1)}, bf16[264,256]{1,0:T(8,128)(2,1)S(1)}, u32[]{:S(2)}, u32[]{:S(2)}) collective-permute-start(bf16[264,256]{1,0:T(8,128)(2,1)S(1)} %get-tuple-element.37), channel_id=1, source_target_pairs={{0,5},{1,4},{4,9},{5,8},{8,13},{9,12},{12,1},{13,0},{2,7},{3,6},{6... | collective-permute-start | bytes 405512 | tf_op jit(solution)/shard_map/ppermute | solution.py:230
  17.6 13.4 %collective-permute-start.5 = (bf16[264,256]{1,0:T(8,128)(2,1)S(1)}, bf16[264,256]{1,0:T(8,128)(2,1)S(1)}, u32[]{:S(2)}, u32[]{:S(2)}) collective-permute-start(bf16[264,256]{1,0:T(8,128)(2,1)S(1)} %get-tuple-element.38), channel_id=1, source_target_pairs={{0,13},{1,12},{4,1},{5,0},{8,5},{9,4},{12,9},{13,8},{2,15},{3,14},... | collective-permute-start | bytes 405512 | tf_op jit(solution)/shard_map/ppermute | solution.py:230
  21.2 9.9 %collective-permute-start.6 = (bf16[264,256]{1,0:T(8,128)(2,1)S(1)}, bf16[264,256]{1,0:T(8,128)(2,1)S(1)}, u32[]{:S(2)}, u32[]{:S(2)}) collective-permute-start(bf16[264,256]{1,0:T(8,128)(2,1)S(1)} %get-tuple-element.39), channel_id=1, source_target_pairs={{0,1},{1,0},{4,5},{5,4},{8,9},{9,8},{12,13},{13,12},{2,3},{3,2},{6... | collective-permute-start | bytes 405512 | tf_op jit(solution)/shard_map/ppermute | solution.py:230
  31.1 11.2 %copy-start.1 = (bf16[1024,2048]{1,0:T(8,128)(2,1)S(1)}, bf16[1024,2048]{1,0:T(8,128)(2,1)}, u32[]{:S(2)}) copy-start(bf16[1024,2048]{1,0:T(8,128)(2,1)} %refs_7_.1) | copy-start | bytes 12582916
  31.1 11.2 %copy-start.3 = (s32[1024,1]{0,1:T(1,128)S(1)}, s32[1024,1]{0,1:T(1,128)}, u32[]{:S(2)}) copy-start(s32[1024,1]{0,1:T(1,128)} %param.14) | copy-start | bytes 12292
  31.1 11.2 %copy-start.4 = (s32[1024,1]{0,1:T(1,128)S(1)}, s32[1024,1]{0,1:T(1,128)}, u32[]{:S(2)}) copy-start(s32[1024,1]{0,1:T(1,128)} %param.16) | copy-start | bytes 12292
  31.1 11.2 %copy-start.5 = (s32[1024]{0:T(1024)S(1)}, s32[1024]{0:T(1024)}, u32[]{:S(2)}) copy-start(s32[1024]{0:T(1024)} %param.18) | copy-start | bytes 12292
  31.1 11.2 %copy-start.6 = (s32[1024]{0:T(1024)S(1)}, s32[1024]{0:T(1024)}, u32[]{:S(2)}) copy-start(s32[1024]{0:T(1024)} %param.19) | copy-start | bytes 12292

commit v20 on v19

--- a/solution.py
+++ b/solution.py
@@ -141,13 +141,12 @@
     return jnp.sum(jnp.where(hits, every[:entities] + every[entities:], 0.0), axis=0, keepdims=True)
 
 
-def early_kernel(capacity, coefs, *refs):
-    half = len(refs) // 2
-    kept = refs[half]
+def early_kernel(capacity, count, coefs, *refs):
+    chunks, kept, outs = refs[:count], refs[-count - 1], refs[-count:]
     entities = coefs.shape[0]
     kept[:entities], kept[entities:] = halves(coefs[...])
     table = kept[...]
-    for chunk, out in zip(refs[:half], refs[half + 1 :]):
+    for chunk, out in zip(chunks, outs):
         out[...] = chunk_scores(chunk, table, capacity)
 
 
@@ -317,7 +316,7 @@
     near_chunks = call(
         partial(rest_kernel, capacity, near),
         [chunk] * len(near),
-        (place, ids, feats, global_total),
+        (place, ids, feats, global_part),
         [VMEM] * 4,
         hidden=True,
     )
@@ -327,10 +326,10 @@
     later, late = away[n_ent:-2], near[:-1]
     order = early + later + late
     table, *scores = call(
-        partial(early_kernel, capacity),
+        partial(early_kernel, capacity, len(early)),
         [shape(2 * coefs.shape[0], width, dtype=BF16)] + [shape(1, capacity)] * len(early),
-        (coefs, *(chunks[k] for k in early)),
-        [VMEM] * (1 + len(early)),
+        (coefs, *(chunks[k] for k in early), global_total),
+        [VMEM] * (2 + len(early)),
         hidden=True,
     )
     scores += call(

time: 54.1 us -> 53.1 us (0.982)
  waiting for transfers between devices: 8.68 us -> 5.09 us
  blocking collectives: 23.8 us -> 25.3 us
  starting transfers between devices: 10.7 us -> 11.8 us
    ppermute x7, waiting for transfers between devices: 8.68 us -> 5.09 us  [shift_send(): return lax.ppermute(x, HOME, pairs)]
    all_to_all x1, blocking collectives: 10.5 us -> 12 us  [body(): lax.all_to_all(scores, EVERY, split_axis=0, concat_axis=0, tiled=True)]
    ppermute x7, starting transfers between devices: 10.7 us -> 11.8 us  [shift_send(): return lax.ppermute(x, HOME, pairs)]
  transfers between devices with their start and end apart: 7 -> 7, of which waited for: 3 -> 2; matrix products, arithmetic and copies ran while one was open for 0% -> 0% of each run, Pallas kernels for 8% -> 9%
where the time goes in v20:
time: 53.1 us; the launch traced here: 52.9 us
  blocking collectives  25.3 us (48%)
  starting transfers between devices  11.8 us (22%)
  Pallas kernels  9.82 us (18%)
  waiting for transfers between devices  5.09 us (10%)
  between operations  0.77 us (1%)
    all_to_all x1, blocking collectives, body(): lax.all_to_all(scores, EVERY, split_axis=0, concat_axis=0, tiled=True)  12 us
    ppermute x7, starting transfers between devices, shift_send(): return lax.ppermute(x, HOME, pairs)  11.8 us
    pallas_call x9, Pallas kernels, call(): pl.pallas_call(kernel, out_shape=out_shape, in_specs=in_specs, out_specs=...  9.82 us
    all_to_all x1, blocking collectives, body(): came = lax.all_to_all(sent, HOME, split_axis=0, concat_axis=0, tiled=True)  8.4 us
    ppermute x7, waiting for transfers between devices, shift_send(): return lax.ppermute(x, HOME, pairs)  5.09 us
    psum x1, blocking collectives, body(): global_total = lax.psum(global_part, 'feat')  4.91 us
  transfers between devices with their start and end apart: 7, of which 2 were waited for; matrix products, arithmetic and copies ran while one was open for 0% of the time, Pallas kernels for 9%

profile of v20, /device:TPU:0, one launch (start us, length us, event | category | flops | bytes accessed | tf_op | source)
XLA Modules:
  0.0 52.9 jit_solution(5418203185347387327)
XLA Ops:
  0.6 1.6 %shard_map.113 = (s32[2,1024]{1,0:T(2,128)S(1)}, s32[1,1024]{1,0:T(1,128)S(1)}, bf16[8,1024]{1,0:T(8,128)(2,1)S(1)}, bf16[1024,256]{1,0:T(8,128)(2,1)S(1)}, bf16[264,256]{1,0:T(8,128)(2,1)S(1)}) custom-call(s32[1,1024]{1,0:T(1,128)} %bitcast.10, s32[1,1024]{1,0:T(1,128)} %bitcast.12, s32[1,1024]{1,0:T(1,128)} %bitcast.16, s32[1,1024]{1,0:T(1,128)} %bitcast.17, ...), custom_call_target="tpu_custom_call" | custom-call | flops 134217728 | bytes 1228800 | tf_op jit(solution)/shard_map/pallas_call | solution.py:234
  2.2 3.1 %collective-permute-start = (bf16[264,256]{1,0:T(8,128)(2,1)S(1)}, bf16[264,256]{1,0:T(8,128)(2,1)S(1)}, u32[]{:S(2)}, u32[]{:S(2)}) collective-permute-start(bf16[264,256]{1,0:T(8,128)(2,1)S(1)} %get-tuple-element.24), channel_id=1, source_target_pairs={{0,4},{1,5},{4,8},{5,9},{8,12},{9,13},{12,0},{13,1},{2,6},{3,7},{6... | collective-permute-start | bytes 405512 | tf_op jit(solution)/shard_map/ppermute | solution.py:229
  5.3 0.0 copy-start.7
  5.3 0.0 copy-start
  5.3 1.0 %shard_map.115 = (bf16[264,256]{1,0:T(8,128)(2,1)S(1)}, bf16[264,256]{1,0:T(8,128)(2,1)S(1)}, bf16[264,256]{1,0:T(8,128)(2,1)S(1)}) custom-call(s32[1,1024]{1,0:T(1,128)S(1)} %get-tuple-element.23.place.refs_0_, bf16[8,1024]{1,0:T(8,128)(2,1)S(1)} %get-tuple-element.25.refs_1_, bf16[1024,256]{1,0:T(8,128)(2,1)S(1)} %get-tuple-element.26.refs_2_), custom_call_target="tpu_custom_call" | custom-call | flops 4294967296 | bytes 950272 | tf_op jit(solution)/shard_map/pallas_call | solution.py:234
  6.3 0.0 copy-start.2
  6.3 2.1 %collective-permute-start.1 = (bf16[264,256]{1,0:T(8,128)(2,1)S(1)}, bf16[264,256]{1,0:T(8,128)(2,1)S(1)}, u32[]{:S(2)}, u32[]{:S(2)}) collective-permute-start(bf16[264,256]{1,0:T(8,128)(2,1)S(1)} %get-tuple-element.27), channel_id=1, source_target_pairs={{0,12},{1,13},{4,0},{5,1},{8,4},{9,5},{12,8},{13,9},{2,14},{3,15},... | collective-permute-start | bytes 405512 | tf_op jit(solution)/shard_map/ppermute | solution.py:229
  8.4 1.0 %collective-permute-start.2 = (bf16[264,256]{1,0:T(8,128)(2,1)S(1)}, bf16[264,256]{1,0:T(8,128)(2,1)S(1)}, u32[]{:S(2)}, u32[]{:S(2)}) collective-permute-start(bf16[264,256]{1,0:T(8,128)(2,1)S(1)} %get-tuple-element.33), channel_id=1, source_target_pairs={{0,8},{1,9},{4,12},{5,13},{8,0},{9,1},{12,4},{13,5},{2,10},{3,11},... | collective-permute-start | bytes 405512 | tf_op jit(solution)/shard_map/ppermute | solution.py:229
  9.4 0.8 %collective-permute-start.3 = (bf16[264,256]{1,0:T(8,128)(2,1)S(1)}, bf16[264,256]{1,0:T(8,128)(2,1)S(1)}, u32[]{:S(2)}, u32[]{:S(2)}) collective-permute-start(bf16[264,256]{1,0:T(8,128)(2,1)S(1)} %get-tuple-element.34), channel_id=1, source_target_pairs={{0,9},{1,8},{4,13},{5,12},{8,1},{9,0},{12,5},{13,4},{2,11},{3,10},... | collective-permute-start | bytes 405512 | tf_op jit(solution)/shard_map/ppermute | solution.py:229
  10.2 0.0 copy-done.7
  10.2 0.0 copy-done
  10.2 1.2 %shard_map.114.refs_3_ = f32[1,1024]{1,0:T(1,128)S(1)} custom-call(s32[1,1024]{1,0:T(1,128)S(1)} %get-tuple-element.23.place.refs_0_, f32[1,2048]{1,0:T(1,128)S(1)} %bitcast.8, bf16[1024,2048]{1,0:T(8,128)(2,1)S(1)} %copy-done), custom_call_target="tpu_custom_call" | custom-call | tf_op jit(solution)/shard_map/pallas_call | solution.py:234
  11.4 1.2 %shard_map.116 = (bf16[264,256]{1,0:T(8,128)(2,1)S(1)}, bf16[264,256]{1,0:T(8,128)(2,1)S(1)}, bf16[264,256]{1,0:T(8,128)(2,1)S(1)}, bf16[264,256]{1,0:T(8,128)(2,1)S(1)}) custom-call(s32[1,1024]{1,0:T(1,128)S(1)} %get-tuple-element.23.place.refs_0_, bf16[8,1024]{1,0:T(8,128)(2,1)S(1)} %get-tuple-element.25.refs_1_, ...), custom_call_target="tpu_custom_call" | custom-call | tf_op jit(solution)/shard_map/pallas_call | solution.py:234
  12.6 0.9 %collective-permute-start.4 = (bf16[264,256]{1,0:T(8,128)(2,1)S(1)}, bf16[264,256]{1,0:T(8,128)(2,1)S(1)}, u32[]{:S(2)}, u32[]{:S(2)}) collective-permute-start(bf16[264,256]{1,0:T(8,128)(2,1)S(1)} %get-tuple-element.37), channel_id=1, source_target_pairs={{0,5},{1,4},{4,9},{5,8},{8,13},{9,12},{12,1},{13,0},{2,7},{3,6},{6... | collective-permute-start | bytes 405512 | tf_op jit(solution)/shard_map/ppermute | solution.py:229
  13.5 0.0 collective-permute-done.refs_1_.refs_3_
  13.5 2.7 %collective-permute-start.5 = (bf16[264,256]{1,0:T(8,128)(2,1)S(1)}, bf16[264,256]{1,0:T(8,128)(2,1)S(1)}, u32[]{:S(2)}, u32[]{:S(2)}) collective-permute-start(bf16[264,256]{1,0:T(8,128)(2,1)S(1)} %get-tuple-element.38), channel_id=1, source_target_pairs={{0,13},{1,12},{4,1},{5,0},{8,5},{9,4},{12,9},{13,8},{2,15},{3,14},... | collective-permute-start | bytes 405512 | tf_op jit(solution)/shard_map/ppermute | solution.py:229
  16.2 0.0 collective-permute-done.1.refs_2_.refs_4_
  16.2 1.2 %collective-permute-start.6 = (bf16[264,256]{1,0:T(8,128)(2,1)S(1)}, bf16[264,256]{1,0:T(8,128)(2,1)S(1)}, u32[]{:S(2)}, u32[]{:S(2)}) collective-permute-start(bf16[264,256]{1,0:T(8,128)(2,1)S(1)} %get-tuple-element.39), channel_id=1, source_target_pairs={{0,1},{1,0},{4,5},{5,4},{8,9},{9,8},{12,13},{13,12},{2,3},{3,2},{6... | collective-permute-start | bytes 405512 | tf_op jit(solution)/shard_map/ppermute | solution.py:229
  17.5 4.9 %psum.7.refs_4_.refs_5_ = f32[1,1024]{1,0:T(1,128)S(1)} all-reduce(f32[1,1024]{1,0:T(1,128)S(1)} %shard_map.114.refs_3_), channel_id=1, replica_groups=mesh['groups'=2,'rows'=4,'feat'=2,'ent'=2] {'feat'}, use_global_device_ids=true, to_apply=%region_0.0 | all-reduce | flops 1024 | bytes 8192 | tf_op jit(solution)/shard_map/psum | solution.py:315
  22.4 0.0 copy-done.2
  22.4 0.6 %shard_map.117 = (bf16[1024,256]{1,0:T(8,128)(2,1)S(1)}, f32[1,256]{1,0:T(1,128)S(1)}, f32[1,256]{1,0:T(1,128)S(1)}, f32[1,256]{1,0:T(1,128)S(1)}) custom-call(f32[512,256]{1,0:T(8,128)S(1)} %copy-done.2, bf16[264,256]{1,0:T(8,128)(2,1)S(1)} %collective-permute-done.refs_1_.refs_3_, bf16[264,256]{1,0:T(8,128)(2,1)S(1)} %collective-permute-done.1.refs_2_.refs_4_, ...), custom_call_target="tpu_custom_call" | custom-call | tf_op jit(solution)/shard_map/pallas_call | solution.py:234
  23.0 2.5 %collective-permute-done.2.refs_1_.refs_6_ = bf16[264,256]{1,0:T(8,128)(2,1)S(1)} collective-permute-done((bf16[264,256]{1,0:T(8,128)(2,1)S(1)}, bf16[264,256]{1,0:T(8,128)(2,1)S(1)}, u32[]{:S(2)}, u32[]{:S(2)}) %collective-permute-start.2) | collective-permute-done | bytes 135200 | tf_op jit(solution)/shard_map/ppermute | solution.py:229
  25.5 2.6 %collective-permute-done.3.refs_2_.refs_7_ = bf16[264,256]{1,0:T(8,128)(2,1)S(1)} collective-permute-done((bf16[264,256]{1,0:T(8,128)(2,1)S(1)}, bf16[264,256]{1,0:T(8,128)(2,1)S(1)}, u32[]{:S(2)}, u32[]{:S(2)}) %collective-permute-start.3) | collective-permute-done | bytes 135200 | tf_op jit(solution)/shard_map/ppermute | solution.py:229
  28.1 0.5 shard_map.118
  28.6 0.0 collective-permute-done.4.refs_6_.refs_8_
  28.6 0.0 collective-permute-done.5.refs_7_.refs_9_
  28.6 0.0 collective-permute-done.6.refs_8_.refs_10_
  28.6 0.0 copy-start.1
  28.6 0.0 copy-start.3
  28.6 0.0 copy-start.4
  28.7 0.0 copy-start.5
  28.7 0.0 copy-start.6
  28.7 0.6 %shard_map.119 = f32[16,1,256]{2,1,0:T(1,128)S(1)} custom-call(bf16[1024,256]{1,0:T(8,128)(2,1)S(1)} %get-tuple-element.29.refs_0_, f32[1,256]{1,0:T(1,128)S(1)} %get-tuple-element.30.refs_1_, f32[1,256]{1,0:T(1,128)S(1)} %get-tuple-element.31.refs_2_, f32[1,256]{1,0:T(1,128)S(1)} %get-tuple-element.32.refs_3_, f32[1,256]{1,0:T(1,128)S(1)} %get-tuple-element.35.refs_4_, ...), custom_call_target="tpu_custom_call" | custom-call | flops 4294967296 | bytes 951296 | tf_op jit(solution)/shard_map/pallas_call | solution.py:234
  29.3 12.0 %all_to_all.10.refs_6_ = f32[16,1,256]{2,1,0:T(1,128)S(1)} all-to-all(f32[16,1,256]{2,1,0:T(1,128)S(1)} %shard_map.119), channel_id=1, replica_groups=mesh['groups'=2,'rows'=4,'feat'=2,'ent'=2] {'rows','feat','ent'}, dimensions={0} | all-to-all | bytes 32768 | tf_op jit(solution)/shard_map/all_to_all | solution.py:349
  41.3 0.0 copy-done.1
  41.3 0.0 copy-done.3
  41.3 0.0 copy-done.4
  41.4 0.0 copy-done.5
  41.4 0.0 copy-done.6
  41.4 1.0 %shard_map.120 = f32[8,1,2304]{2,1,0:T(1,128)S(1)} custom-call(s32[1,1024]{1,0:T(1,128)S(1)} %bitcast.11, s32[1,1024]{1,0:T(1,128)S(1)} %bitcast.13, s32[2,1024]{1,0:T(2,128)S(1)} %get-tuple-element.22.refs_2_, s32[1,1024]{1,0:T(1,128)S(1)} %bitcast.14, s32[1,1024]{1,0:T(1,128)S(1)} %bitcast.15, f32[1,1024]{1,0:T(1,128)S(1)} %psum.7.refs_4_.refs_5_, ...), custom_call_target="tpu_custom_call" | custom-call | flops 67108864 | bytes 4313088 | tf_op jit(solution)/shard_map/pallas_call | solution.py:234
  42.4 8.4 %all_to_all.11.refs_2_ = f32[8,1,2304]{2,1,0:T(1,128)S(1)} all-to-all(f32[8,1,2304]{2,1,0:T(1,128)S(1)} %shard_map.120), channel_id=1, replica_groups=mesh['groups'=2,'rows'=4,'feat'=2,'ent'=2] {'rows','ent'}, dimensions={0} | all-to-all | bytes 147456 | tf_op jit(solution)/shard_map/all_to_all | solution.py:366
  50.8 2.1 %shard_map.121 = (f32[1,2048]{1,0:T(1,128)}, f32[512,256]{1,0:T(8,128)}) custom-call(f32[512,256]{1,0:T(8,128)S(1)} %copy-done.2, f32[1,2048]{1,0:T(1,128)S(1)} %bitcast.9, f32[8,1,2304]{2,1,0:T(1,128)S(1)} %all_to_all.11.refs_2_, bf16[264,256]{1,0:T(8,128)(2,1)S(1)} %collective-permute-done.refs_1_.refs_3_, ...), custom_call_target="tpu_custom_call" | custom-call | flops 1073741824 | bytes 2220032 | tf_op jit(solution)/shard_map/pallas_call | solution.py:234
  (1 shorter events, 0.0 us)
Async XLA Ops:
  2.2 11.3 %collective-permute-start = (bf16[264,256]{1,0:T(8,128)(2,1)S(1)}, bf16[264,256]{1,0:T(8,128)(2,1)S(1)}, u32[]{:S(2)}, u32[]{:S(2)}) collective-permute-start(bf16[264,256]{1,0:T(8,128)(2,1)S(1)} %get-tuple-element.24), channel_id=1, source_target_pairs={{0,4},{1,5},{4,8},{5,9},{8,12},{9,13},{12,0},{13,1},{2,6},{3,7},{6... | collective-permute-start | bytes 405512 | tf_op jit(solution)/shard_map/ppermute | solution.py:229
  5.3 4.9 %copy-start.7 = (bf16[2048]{0:T(1024)(128)(2,1)S(1)}, bf16[2048]{0:T(1024)(128)(2,1)}, u32[]{:S(2)}) copy-start(bf16[2048]{0:T(1024)(128)(2,1)} %param.11) | copy-start | bytes 12292
  5.3 4.9 %copy-start = (bf16[1024,2048]{1,0:T(8,128)(2,1)S(1)}, bf16[1024,2048]{1,0:T(8,128)(2,1)}, u32[]{:S(2)}) copy-start(bf16[1024,2048]{1,0:T(8,128)(2,1)} %refs_7_.1) | copy-start | bytes 12582916
  6.3 16.1 %copy-start.2 = (f32[512,256]{1,0:T(8,128)S(1)}, f32[512,256]{1,0:T(8,128)}, u32[]{:S(2)}) copy-start(f32[512,256]{1,0:T(8,128)} %refs_0_.3) | copy-start | bytes 1572868
  6.3 10.0 %collective-permute-start.1 = (bf16[264,256]{1,0:T(8,128)(2,1)S(1)}, bf16[264,256]{1,0:T(8,128)(2,1)S(1)}, u32[]{:S(2)}, u32[]{:S(2)}) collective-permute-start(bf16[264,256]{1,0:T(8,128)(2,1)S(1)} %get-tuple-element.27), channel_id=1, source_target_pairs={{0,12},{1,13},{4,0},{5,1},{8,4},{9,5},{12,8},{13,9},{2,14},{3,15},... | collective-permute-start | bytes 405512 | tf_op jit(solution)/shard_map/ppermute | solution.py:229
  8.4 17.2 %collective-permute-start.2 = (bf16[264,256]{1,0:T(8,128)(2,1)S(1)}, bf16[264,256]{1,0:T(8,128)(2,1)S(1)}, u32[]{:S(2)}, u32[]{:S(2)}) collective-permute-start(bf16[264,256]{1,0:T(8,128)(2,1)S(1)} %get-tuple-element.33), channel_id=1, source_target_pairs={{0,8},{1,9},{4,12},{5,13},{8,0},{9,1},{12,4},{13,5},{2,10},{3,11},... | collective-permute-start | bytes 405512 | tf_op jit(solution)/shard_map/ppermute | solution.py:229
  9.4 18.7 %collective-permute-start.3 = (bf16[264,256]{1,0:T(8,128)(2,1)S(1)}, bf16[264,256]{1,0:T(8,128)(2,1)S(1)}, u32[]{:S(2)}, u32[]{:S(2)}) collective-permute-start(bf16[264,256]{1,0:T(8,128)(2,1)S(1)} %get-tuple-element.34), channel_id=1, source_target_pairs={{0,9},{1,8},{4,13},{5,12},{8,1},{9,0},{12,5},{13,4},{2,11},{3,10},... | collective-permute-start | bytes 405512 | tf_op jit(solution)/shard_map/ppermute | solution.py:229
  12.6 16.0 %collective-permute-start.4 = (bf16[264,256]{1,0:T(8,128)(2,1)S(1)}, bf16[264,256]{1,0:T(8,128)(2,1)S(1)}, u32[]{:S(2)}, u32[]{:S(2)}) collective-permute-start(bf16[264,256]{1,0:T(8,128)(2,1)S(1)} %get-tuple-element.37), channel_id=1, source_target_pairs={{0,5},{1,4},{4,9},{5,8},{8,13},{9,12},{12,1},{13,0},{2,7},{3,6},{6... | collective-permute-start | bytes 405512 | tf_op jit(solution)/shard_map/ppermute | solution.py:229
  13.5 15.1 %collective-permute-start.5 = (bf16[264,256]{1,0:T(8,128)(2,1)S(1)}, bf16[264,256]{1,0:T(8,128)(2,1)S(1)}, u32[]{:S(2)}, u32[]{:S(2)}) collective-permute-start(bf16[264,256]{1,0:T(8,128)(2,1)S(1)} %get-tuple-element.38), channel_id=1, source_target_pairs={{0,13},{1,12},{4,1},{5,0},{8,5},{9,4},{12,9},{13,8},{2,15},{3,14},... | collective-permute-start | bytes 405512 | tf_op jit(solution)/shard_map/ppermute | solution.py:229
  16.2 12.4 %collective-permute-start.6 = (bf16[264,256]{1,0:T(8,128)(2,1)S(1)}, bf16[264,256]{1,0:T(8,128)(2,1)S(1)}, u32[]{:S(2)}, u32[]{:S(2)}) collective-permute-start(bf16[264,256]{1,0:T(8,128)(2,1)S(1)} %get-tuple-element.39), channel_id=1, source_target_pairs={{0,1},{1,0},{4,5},{5,4},{8,9},{9,8},{12,13},{13,12},{2,3},{3,2},{6... | collective-permute-start | bytes 405512 | tf_op jit(solution)/shard_map/ppermute | solution.py:229
  28.6 12.7 %copy-start.1 = (bf16[1024,2048]{1,0:T(8,128)(2,1)S(1)}, bf16[1024,2048]{1,0:T(8,128)(2,1)}, u32[]{:S(2)}) copy-start(bf16[1024,2048]{1,0:T(8,128)(2,1)} %refs_7_.1) | copy-start | bytes 12582916
  28.6 12.7 %copy-start.3 = (s32[1024,1]{0,1:T(1,128)S(1)}, s32[1024,1]{0,1:T(1,128)}, u32[]{:S(2)}) copy-start(s32[1024,1]{0,1:T(1,128)} %param.14) | copy-start | bytes 12292
  28.6 12.7 %copy-start.4 = (s32[1024,1]{0,1:T(1,128)S(1)}, s32[1024,1]{0,1:T(1,128)}, u32[]{:S(2)}) copy-start(s32[1024,1]{0,1:T(1,128)} %param.16) | copy-start | bytes 12292
  28.7 12.7 %copy-start.5 = (s32[1024]{0:T(1024)S(1)}, s32[1024]{0:T(1024)}, u32[]{:S(2)}) copy-start(s32[1024]{0:T(1024)} %param.18) | copy-start | bytes 12292
  28.7 12.7 %copy-start.6 = (s32[1024]{0:T(1024)S(1)}, s32[1024]{0:T(1024)}, u32[]{:S(2)}) copy-start(s32[1024]{0:T(1024)} %param.19) | copy-start | bytes 12292

commit v21 on v20

--- a/solution.py
+++ b/solution.py
@@ -309,21 +309,21 @@
     )
     chunks = [shift_send(x, n_rows, n_ent, k) for k, x in zip(first + second, chunks)]
     weight = global_weight.astype(F32).reshape(1, columns)
-    (global_part,) = call(
-        margin_kernel, [shape(1, rows_here)], (place, weight, features), [VMEM] * 3, hidden=True
-    )
-    global_total = lax.psum(global_part, "feat")
     near_chunks = call(
         partial(rest_kernel, capacity, near),
         [chunk] * len(near),
-        (place, ids, feats, global_part),
-        [VMEM] * 4,
+        (place, ids, feats),
+        [VMEM] * 3,
         hidden=True,
     )
+    (global_part,) = call(
+        margin_kernel, [shape(1, rows_here)], (near_chunks[-1], weight, features), [VMEM] * 3, hidden=True
+    )
+    global_total = lax.psum(global_part, "feat")
     near_chunks = [shift_send(x, n_rows, n_ent, k) for k, x in zip(near, near_chunks)]
     chunks = dict(zip(first + second + near, chunks + near_chunks))
     early = away[:n_ent] + near[-1:]
-    later, late = away[n_ent:-2], near[:-1]
+    later, late = away[n_ent:-2] + near[2:-1], near[:2]
     order = early + later + late
     table, *scores = call(
         partial(early_kernel, capacity, len(early)),

time: 53.1 us -> 53.1 us (level)
  waiting for transfers between devices: 5.09 us -> 6.24 us
  starting transfers between devices: 11.8 us -> 10.8 us
    ppermute x7, waiting for transfers between devices: 5.09 us -> 6.24 us  [shift_send(): return lax.ppermute(x, HOME, pairs)]
    ppermute x7, starting transfers between devices: 11.8 us -> 10.8 us  [shift_send(): return lax.ppermute(x, HOME, pairs)]
  transfers between devices with their start and end apart: 7 -> 7, of which waited for: 2 -> 3; matrix products, arithmetic and copies ran while one was open for 0% -> 0% of each run, Pallas kernels for 9% -> 9%
where the time goes in v21:
time: 53.1 us; the launch traced here: 52.8 us
  blocking collectives  25.2 us (47%)
  starting transfers between devices  10.8 us (20%)
  Pallas kernels  9.8 us (18%)
  waiting for transfers between devices  6.24 us (12%)
  between operations  0.76 us (1%)
    all_to_all x1, blocking collectives, body(): lax.all_to_all(scores, EVERY, split_axis=0, concat_axis=0, tiled=True)  11.9 us
    ppermute x7, starting transfers between devices, shift_send(): return lax.ppermute(x, HOME, pairs)  10.8 us
    pallas_call x9, Pallas kernels, call(): pl.pallas_call(kernel, out_shape=out_shape, in_specs=in_specs, out_specs=...  9.8 us
    all_to_all x1, blocking collectives, body(): came = lax.all_to_all(sent, HOME, split_axis=0, concat_axis=0, tiled=True)  8.4 us
    ppermute x7, waiting for transfers between devices, shift_send(): return lax.ppermute(x, HOME, pairs)  6.24 us
    psum x1, blocking collectives, body(): global_total = lax.psum(global_part, 'feat')  4.93 us
  transfers between devices with their start and end apart: 7, of which 3 were waited for; matrix products, arithmetic and copies ran while one was open for 0% of the time, Pallas kernels for 9%

profile of v21, /device:TPU:0, one launch (start us, length us, event | category | flops | bytes accessed | tf_op | source)
XLA Modules:
  0.0 52.8 jit_solution(6369100165443128310)
XLA Ops:
  0.6 1.6 %shard_map.113 = (s32[2,1024]{1,0:T(2,128)S(1)}, s32[1,1024]{1,0:T(1,128)S(1)}, bf16[8,1024]{1,0:T(8,128)(2,1)S(1)}, bf16[1024,256]{1,0:T(8,128)(2,1)S(1)}, bf16[264,256]{1,0:T(8,128)(2,1)S(1)}) custom-call(s32[1,1024]{1,0:T(1,128)} %bitcast.10, s32[1,1024]{1,0:T(1,128)} %bitcast.12, s32[1,1024]{1,0:T(1,128)} %bitcast.16, s32[1,1024]{1,0:T(1,128)} %bitcast.17, ...), custom_call_target="tpu_custom_call" | custom-call | flops 134217728 | bytes 1228800 | tf_op jit(solution)/shard_map/pallas_call | solution.py:234
  2.2 3.1 %collective-permute-start = (bf16[264,256]{1,0:T(8,128)(2,1)S(1)}, bf16[264,256]{1,0:T(8,128)(2,1)S(1)}, u32[]{:S(2)}, u32[]{:S(2)}) collective-permute-start(bf16[264,256]{1,0:T(8,128)(2,1)S(1)} %get-tuple-element.28), channel_id=1, source_target_pairs={{0,4},{1,5},{4,8},{5,9},{8,12},{9,13},{12,0},{13,1},{2,6},{3,7},{6... | collective-permute-start | bytes 405512 | tf_op jit(solution)/shard_map/ppermute | solution.py:229
  5.3 0.0 copy-start.7
  5.3 0.0 copy-start
  5.3 1.0 %shard_map.116 = (bf16[264,256]{1,0:T(8,128)(2,1)S(1)}, bf16[264,256]{1,0:T(8,128)(2,1)S(1)}, bf16[264,256]{1,0:T(8,128)(2,1)S(1)}) custom-call(s32[1,1024]{1,0:T(1,128)S(1)} %get-tuple-element.24.refs_0_, bf16[8,1024]{1,0:T(8,128)(2,1)S(1)} %get-tuple-element.25.refs_1_, bf16[1024,256]{1,0:T(8,128)(2,1)S(1)} %get-tuple-element.26.refs_2_), custom_call_target="tpu_custom_call" | custom-call | flops 4294967296 | bytes 950272 | tf_op jit(solution)/shard_map/pallas_call | solution.py:234
  6.3 0.0 copy-start.2
  6.3 2.1 %collective-permute-start.1 = (bf16[264,256]{1,0:T(8,128)(2,1)S(1)}, bf16[264,256]{1,0:T(8,128)(2,1)S(1)}, u32[]{:S(2)}, u32[]{:S(2)}) collective-permute-start(bf16[264,256]{1,0:T(8,128)(2,1)S(1)} %get-tuple-element.29), channel_id=1, source_target_pairs={{0,12},{1,13},{4,0},{5,1},{8,4},{9,5},{12,8},{13,9},{2,14},{3,15},... | collective-permute-start | bytes 405512 | tf_op jit(solution)/shard_map/ppermute | solution.py:229
  8.4 1.0 %collective-permute-start.2 = (bf16[264,256]{1,0:T(8,128)(2,1)S(1)}, bf16[264,256]{1,0:T(8,128)(2,1)S(1)}, u32[]{:S(2)}, u32[]{:S(2)}) collective-permute-start(bf16[264,256]{1,0:T(8,128)(2,1)S(1)} %get-tuple-element.34), channel_id=1, source_target_pairs={{0,8},{1,9},{4,12},{5,13},{8,0},{9,1},{12,4},{13,5},{2,10},{3,11},... | collective-permute-start | bytes 405512 | tf_op jit(solution)/shard_map/ppermute | solution.py:229
  9.4 0.8 %collective-permute-start.3 = (bf16[264,256]{1,0:T(8,128)(2,1)S(1)}, bf16[264,256]{1,0:T(8,128)(2,1)S(1)}, u32[]{:S(2)}, u32[]{:S(2)}) collective-permute-start(bf16[264,256]{1,0:T(8,128)(2,1)S(1)} %get-tuple-element.35), channel_id=1, source_target_pairs={{0,9},{1,8},{4,13},{5,12},{8,1},{9,0},{12,5},{13,4},{2,11},{3,10},... | collective-permute-start | bytes 405512 | tf_op jit(solution)/shard_map/ppermute | solution.py:229
  10.2 1.2 %shard_map.114 = (bf16[264,256]{1,0:T(8,128)(2,1)S(1)}, bf16[264,256]{1,0:T(8,128)(2,1)S(1)}, bf16[264,256]{1,0:T(8,128)(2,1)S(1)}, bf16[264,256]{1,0:T(8,128)(2,1)S(1)}) custom-call(s32[1,1024]{1,0:T(1,128)S(1)} %get-tuple-element.24.refs_0_, bf16[8,1024]{1,0:T(8,128)(2,1)S(1)} %get-tuple-element.25.refs_1_, bf16[1024,256]{1,0:T(8,128)(2,1)S(1)} %get-tuple-element.26.refs_2_), custom_call_target="tpu_custom_call" | custom-call | tf_op jit(solution)/shard_map/pallas_call | solution.py:234
  11.4 1.3 %collective-permute-start.4 = (bf16[264,256]{1,0:T(8,128)(2,1)S(1)}, bf16[264,256]{1,0:T(8,128)(2,1)S(1)}, u32[]{:S(2)}, u32[]{:S(2)}) collective-permute-start(bf16[264,256]{1,0:T(8,128)(2,1)S(1)} %get-tuple-element.36), channel_id=1, source_target_pairs={{0,1},{1,0},{4,5},{5,4},{8,9},{9,8},{12,13},{13,12},{2,3},{3,2},{6... | collective-permute-start | bytes 405512 | tf_op jit(solution)/shard_map/ppermute | solution.py:229
  12.7 0.0 collective-permute-done.refs_1_.refs_3_
  12.7 0.0 collective-permute-start.5
  12.7 1.1 %collective-permute-done.1.refs_2_.refs_4_ = bf16[264,256]{1,0:T(8,128)(2,1)S(1)} collective-permute-done((bf16[264,256]{1,0:T(8,128)(2,1)S(1)}, bf16[264,256]{1,0:T(8,128)(2,1)S(1)}, u32[]{:S(2)}, u32[]{:S(2)}) %collective-permute-start.1) | collective-permute-done | bytes 135200 | tf_op jit(solution)/shard_map/ppermute | solution.py:229
  13.8 2.5 %collective-permute-start.6 = (bf16[264,256]{1,0:T(8,128)(2,1)S(1)}, bf16[264,256]{1,0:T(8,128)(2,1)S(1)}, u32[]{:S(2)}, u32[]{:S(2)}) collective-permute-start(bf16[264,256]{1,0:T(8,128)(2,1)S(1)} %get-tuple-element.41), channel_id=1, source_target_pairs={{0,13},{1,12},{4,1},{5,0},{8,5},{9,4},{12,9},{13,8},{2,15},{3,14},... | collective-permute-start | bytes 405512 | tf_op jit(solution)/shard_map/ppermute | solution.py:229
  16.3 0.0 copy-done.7
  16.3 0.0 copy-done
  16.3 1.2 %shard_map.115 = f32[1,1024]{1,0:T(1,128)S(1)} custom-call(bf16[264,256]{1,0:T(8,128)(2,1)S(1)} %get-tuple-element.27.place.refs_3_.refs_5_, f32[1,2048]{1,0:T(1,128)S(1)} %bitcast.8, bf16[1024,2048]{1,0:T(8,128)(2,1)S(1)} %copy-done), custom_call_target="tpu_custom_call" | custom-call | tf_op jit(solution)/shard_map/pallas_call | solution.py:234
  17.5 4.9 %psum.7.refs_4_.refs_5_ = f32[1,1024]{1,0:T(1,128)S(1)} all-reduce(f32[1,1024]{1,0:T(1,128)S(1)} %shard_map.115), channel_id=1, replica_groups=mesh['groups'=2,'rows'=4,'feat'=2,'ent'=2] {'feat'}, use_global_device_ids=true, to_apply=%region_0.0 | all-reduce | flops 1024 | bytes 8192 | tf_op jit(solution)/shard_map/psum | solution.py:322
  22.4 0.0 copy-done.2
  22.4 0.6 %shard_map.117 = (bf16[1024,256]{1,0:T(8,128)(2,1)S(1)}, f32[1,256]{1,0:T(1,128)S(1)}, f32[1,256]{1,0:T(1,128)S(1)}, f32[1,256]{1,0:T(1,128)S(1)}) custom-call(f32[512,256]{1,0:T(8,128)S(1)} %copy-done.2, bf16[264,256]{1,0:T(8,128)(2,1)S(1)} %collective-permute-done.refs_1_.refs_3_, bf16[264,256]{1,0:T(8,128)(2,1)S(1)} %collective-permute-done.1.refs_2_.refs_4_, ...), custom_call_target="tpu_custom_call" | custom-call | tf_op jit(solution)/shard_map/pallas_call | solution.py:234
  23.0 2.6 %collective-permute-done.2.refs_1_.refs_6_ = bf16[264,256]{1,0:T(8,128)(2,1)S(1)} collective-permute-done((bf16[264,256]{1,0:T(8,128)(2,1)S(1)}, bf16[264,256]{1,0:T(8,128)(2,1)S(1)}, u32[]{:S(2)}, u32[]{:S(2)}) %collective-permute-start.2) | collective-permute-done | bytes 135200 | tf_op jit(solution)/shard_map/ppermute | solution.py:229
  25.6 2.6 %collective-permute-done.3.refs_2_.refs_7_ = bf16[264,256]{1,0:T(8,128)(2,1)S(1)} collective-permute-done((bf16[264,256]{1,0:T(8,128)(2,1)S(1)}, bf16[264,256]{1,0:T(8,128)(2,1)S(1)}, u32[]{:S(2)}, u32[]{:S(2)}) %collective-permute-start.3) | collective-permute-done | bytes 135200 | tf_op jit(solution)/shard_map/ppermute | solution.py:229
  28.2 0.0 collective-permute-done.4.refs_3_.refs_8_
  28.2 0.6 %shard_map.118 = (f32[1,256]{1,0:T(1,128)S(1)}, f32[1,256]{1,0:T(1,128)S(1)}, f32[1,256]{1,0:T(1,128)S(1)}) custom-call(bf16[1024,256]{1,0:T(8,128)(2,1)S(1)} %get-tuple-element.30.refs_0_, bf16[264,256]{1,0:T(8,128)(2,1)S(1)} %collective-permute-done.2.refs_1_.refs_6_, bf16[264,256]{1,0:T(8,128)(2,1)S(1)} %collective-permute-done.3.refs_2_.refs_7_, ...), custom_call_target="tpu_custom_call" | custom-call | tf_op jit(solution)/shard_map/pallas_call | solution.py:234
  28.8 0.0 collective-permute-done.5.refs_7_.refs_9_
  28.8 0.0 collective-permute-done.6.refs_8_.refs_10_
  28.9 0.0 copy-start.1
  28.9 0.0 copy-start.3
  28.9 0.0 copy-start.4
  28.9 0.0 copy-start.5
  28.9 0.0 copy-start.6
  28.9 0.5 shard_map.119
  29.4 11.9 %all_to_all.10.refs_6_ = f32[16,1,256]{2,1,0:T(1,128)S(1)} all-to-all(f32[16,1,256]{2,1,0:T(1,128)S(1)} %shard_map.119), channel_id=1, replica_groups=mesh['groups'=2,'rows'=4,'feat'=2,'ent'=2] {'rows','feat','ent'}, dimensions={0} | all-to-all | bytes 32768 | tf_op jit(solution)/shard_map/all_to_all | solution.py:349
  41.3 0.0 copy-done.1
  41.3 0.0 copy-done.3
  41.3 0.0 copy-done.4
  41.3 0.0 copy-done.5
  41.3 0.0 copy-done.6
  41.3 1.0 %shard_map.120 = f32[8,1,2304]{2,1,0:T(1,128)S(1)} custom-call(s32[1,1024]{1,0:T(1,128)S(1)} %bitcast.11, s32[1,1024]{1,0:T(1,128)S(1)} %bitcast.13, s32[2,1024]{1,0:T(2,128)S(1)} %get-tuple-element.23.refs_2_, s32[1,1024]{1,0:T(1,128)S(1)} %bitcast.14, s32[1,1024]{1,0:T(1,128)S(1)} %bitcast.15, f32[1,1024]{1,0:T(1,128)S(1)} %psum.7.refs_4_.refs_5_, ...), custom_call_target="tpu_custom_call" | custom-call | flops 67108864 | bytes 4313088 | tf_op jit(solution)/shard_map/pallas_call | solution.py:234
  42.4 8.4 %all_to_all.11.refs_2_ = f32[8,1,2304]{2,1,0:T(1,128)S(1)} all-to-all(f32[8,1,2304]{2,1,0:T(1,128)S(1)} %shard_map.120), channel_id=1, replica_groups=mesh['groups'=2,'rows'=4,'feat'=2,'ent'=2] {'rows','ent'}, dimensions={0} | all-to-all | bytes 147456 | tf_op jit(solution)/shard_map/all_to_all | solution.py:366
  50.8 2.1 %shard_map.121 = (f32[1,2048]{1,0:T(1,128)}, f32[512,256]{1,0:T(8,128)}) custom-call(f32[512,256]{1,0:T(8,128)S(1)} %copy-done.2, f32[1,2048]{1,0:T(1,128)S(1)} %bitcast.9, f32[8,1,2304]{2,1,0:T(1,128)S(1)} %all_to_all.11.refs_2_, bf16[264,256]{1,0:T(8,128)(2,1)S(1)} %collective-permute-done.refs_1_.refs_3_, ...), custom_call_target="tpu_custom_call" | custom-call | flops 1073741824 | bytes 2220032 | tf_op jit(solution)/shard_map/pallas_call | solution.py:234
  (1 shorter events, 0.0 us)
Async XLA Ops:
  2.2 10.5 %collective-permute-start = (bf16[264,256]{1,0:T(8,128)(2,1)S(1)}, bf16[264,256]{1,0:T(8,128)(2,1)S(1)}, u32[]{:S(2)}, u32[]{:S(2)}) collective-permute-start(bf16[264,256]{1,0:T(8,128)(2,1)S(1)} %get-tuple-element.28), channel_id=1, source_target_pairs={{0,4},{1,5},{4,8},{5,9},{8,12},{9,13},{12,0},{13,1},{2,6},{3,7},{6... | collective-permute-start | bytes 405512 | tf_op jit(solution)/shard_map/ppermute | solution.py:229
  5.3 11.0 %copy-start.7 = (bf16[2048]{0:T(1024)(128)(2,1)S(1)}, bf16[2048]{0:T(1024)(128)(2,1)}, u32[]{:S(2)}) copy-start(bf16[2048]{0:T(1024)(128)(2,1)} %param.11) | copy-start | bytes 12292
  5.3 11.0 %copy-start = (bf16[1024,2048]{1,0:T(8,128)(2,1)S(1)}, bf16[1024,2048]{1,0:T(8,128)(2,1)}, u32[]{:S(2)}) copy-start(bf16[1024,2048]{1,0:T(8,128)(2,1)} %refs_7_.1) | copy-start | bytes 12582916
  6.3 16.2 %copy-start.2 = (f32[512,256]{1,0:T(8,128)S(1)}, f32[512,256]{1,0:T(8,128)}, u32[]{:S(2)}) copy-start(f32[512,256]{1,0:T(8,128)} %refs_0_.3) | copy-start | bytes 1572868
  6.3 7.5 %collective-permute-start.1 = (bf16[264,256]{1,0:T(8,128)(2,1)S(1)}, bf16[264,256]{1,0:T(8,128)(2,1)S(1)}, u32[]{:S(2)}, u32[]{:S(2)}) collective-permute-start(bf16[264,256]{1,0:T(8,128)(2,1)S(1)} %get-tuple-element.29), channel_id=1, source_target_pairs={{0,12},{1,13},{4,0},{5,1},{8,4},{9,5},{12,8},{13,9},{2,14},{3,15},... | collective-permute-start | bytes 405512 | tf_op jit(solution)/shard_map/ppermute | solution.py:229
  8.4 17.3 %collective-permute-start.2 = (bf16[264,256]{1,0:T(8,128)(2,1)S(1)}, bf16[264,256]{1,0:T(8,128)(2,1)S(1)}, u32[]{:S(2)}, u32[]{:S(2)}) collective-permute-start(bf16[264,256]{1,0:T(8,128)(2,1)S(1)} %get-tuple-element.34), channel_id=1, source_target_pairs={{0,8},{1,9},{4,12},{5,13},{8,0},{9,1},{12,4},{13,5},{2,10},{3,11},... | collective-permute-start | bytes 405512 | tf_op jit(solution)/shard_map/ppermute | solution.py:229
  9.4 18.8 %collective-permute-start.3 = (bf16[264,256]{1,0:T(8,128)(2,1)S(1)}, bf16[264,256]{1,0:T(8,128)(2,1)S(1)}, u32[]{:S(2)}, u32[]{:S(2)}) collective-permute-start(bf16[264,256]{1,0:T(8,128)(2,1)S(1)} %get-tuple-element.35), channel_id=1, source_target_pairs={{0,9},{1,8},{4,13},{5,12},{8,1},{9,0},{12,5},{13,4},{2,11},{3,10},... | collective-permute-start | bytes 405512 | tf_op jit(solution)/shard_map/ppermute | solution.py:229
  11.4 16.8 %collective-permute-start.4 = (bf16[264,256]{1,0:T(8,128)(2,1)S(1)}, bf16[264,256]{1,0:T(8,128)(2,1)S(1)}, u32[]{:S(2)}, u32[]{:S(2)}) collective-permute-start(bf16[264,256]{1,0:T(8,128)(2,1)S(1)} %get-tuple-element.36), channel_id=1, source_target_pairs={{0,1},{1,0},{4,5},{5,4},{8,9},{9,8},{12,13},{13,12},{2,3},{3,2},{6... | collective-permute-start | bytes 405512 | tf_op jit(solution)/shard_map/ppermute | solution.py:229
  12.7 16.1 %collective-permute-start.5 = (bf16[264,256]{1,0:T(8,128)(2,1)S(1)}, bf16[264,256]{1,0:T(8,128)(2,1)S(1)}, u32[]{:S(2)}, u32[]{:S(2)}) collective-permute-start(bf16[264,256]{1,0:T(8,128)(2,1)S(1)} %get-tuple-element.40), channel_id=1, source_target_pairs={{0,5},{1,4},{4,9},{5,8},{8,13},{9,12},{12,1},{13,0},{2,7},{3,6},{6... | collective-permute-start | bytes 405512 | tf_op jit(solution)/shard_map/ppermute | solution.py:229
  13.8 15.1 %collective-permute-start.6 = (bf16[264,256]{1,0:T(8,128)(2,1)S(1)}, bf16[264,256]{1,0:T(8,128)(2,1)S(1)}, u32[]{:S(2)}, u32[]{:S(2)}) collective-permute-start(bf16[264,256]{1,0:T(8,128)(2,1)S(1)} %get-tuple-element.41), channel_id=1, source_target_pairs={{0,13},{1,12},{4,1},{5,0},{8,5},{9,4},{12,9},{13,8},{2,15},{3,14},... | collective-permute-start | bytes 405512 | tf_op jit(solution)/shard_map/ppermute | solution.py:229
  28.9 12.4 %copy-start.1 = (bf16[1024,2048]{1,0:T(8,128)(2,1)S(1)}, bf16[1024,2048]{1,0:T(8,128)(2,1)}, u32[]{:S(2)}) copy-start(bf16[1024,2048]{1,0:T(8,128)(2,1)} %refs_7_.1) | copy-start | bytes 12582916
  28.9 12.4 %copy-start.3 = (s32[1024,1]{0,1:T(1,128)S(1)}, s32[1024,1]{0,1:T(1,128)}, u32[]{:S(2)}) copy-start(s32[1024,1]{0,1:T(1,128)} %param.14) | copy-start | bytes 12292
  28.9 12.4 %copy-start.4 = (s32[1024,1]{0,1:T(1,128)S(1)}, s32[1024,1]{0,1:T(1,128)}, u32[]{:S(2)}) copy-start(s32[1024,1]{0,1:T(1,128)} %param.16) | copy-start | bytes 12292
  28.9 12.4 %copy-start.5 = (s32[1024]{0:T(1024)S(1)}, s32[1024]{0:T(1024)}, u32[]{:S(2)}) copy-start(s32[1024]{0:T(1024)} %param.18) | copy-start | bytes 12292
  28.9 12.4 %copy-start.6 = (s32[1024]{0:T(1024)S(1)}, s32[1024]{0:T(1024)}, u32[]{:S(2)}) copy-start(s32[1024]{0:T(1024)} %param.19) | copy-start | bytes 12292

commit v22 on v21

--- a/solution.py
+++ b/solution.py
@@ -124,7 +124,7 @@
         pack_chunk(k, capacity, place[...], ids[...], feats[...], chunk)
 
 
-def margin_kernel(place, weight, features, margin):
+def margin_kernel(packed, weight, features, margin):
     wide = jnp.broadcast_to(weight[...], (16, weight.shape[1])).astype(BF16)
     margin[...] = lanes_dot(wide, features[...])[0:1]
 
@@ -323,7 +323,7 @@
     near_chunks = [shift_send(x, n_rows, n_ent, k) for k, x in zip(near, near_chunks)]
     chunks = dict(zip(first + second + near, chunks + near_chunks))
     early = away[:n_ent] + near[-1:]
-    later, late = away[n_ent:-2] + near[2:-1], near[:2]
+    later, late = away[n_ent:-2], near[:-1]
     order = early + later + late
     table, *scores = call(
         partial(early_kernel, capacity, len(early)),

time: 53.1 us -> 53.1 us (level)
  waiting for transfers between devices: 6.24 us -> 5.09 us
  starting transfers between devices: 10.8 us -> 11.8 us
    ppermute x7, waiting for transfers between devices: 6.24 us -> 5.09 us  [shift_send(): return lax.ppermute(x, HOME, pairs)]
    ppermute x7, starting transfers between devices: 10.8 us -> 11.8 us  [shift_send(): return lax.ppermute(x, HOME, pairs)]
  transfers between devices with their start and end apart: 7 -> 7, of which waited for: 3 -> 2; matrix products, arithmetic and copies ran while one was open for 0% -> 0% of each run, Pallas kernels for 9% -> 8%
where the time goes in v22:
time: 53.1 us; the launch traced here: 52.9 us
  blocking collectives  25.3 us (48%)
  starting transfers between devices  11.8 us (22%)
  Pallas kernels  9.8 us (18%)
  waiting for transfers between devices  5.09 us (10%)
  between operations  0.77 us (1%)
    all_to_all x1, blocking collectives, body(): lax.all_to_all(scores, EVERY, split_axis=0, concat_axis=0, tiled=True)  12 us
    ppermute x7, starting transfers between devices, shift_send(): return lax.ppermute(x, HOME, pairs)  11.8 us
    pallas_call x9, Pallas kernels, call(): pl.pallas_call(kernel, out_shape=out_shape, in_specs=in_specs, out_specs=...  9.8 us
    all_to_all x1, blocking collectives, body(): came = lax.all_to_all(sent, HOME, split_axis=0, concat_axis=0, tiled=True)  8.4 us
    ppermute x7, waiting for transfers between devices, shift_send(): return lax.ppermute(x, HOME, pairs)  5.09 us
    psum x1, blocking collectives, body(): global_total = lax.psum(global_part, 'feat')  4.93 us
  transfers between devices with their start and end apart: 7, of which 2 were waited for; matrix products, arithmetic and copies ran while one was open for 0% of the time, Pallas kernels for 8%

profile of v22, /device:TPU:0, one launch (start us, length us, event | category | flops | bytes accessed | tf_op | source)
XLA Modules:
  0.0 52.9 jit_solution(11041034263097188692)
XLA Ops:
  0.6 1.6 %shard_map.113 = (s32[2,1024]{1,0:T(2,128)S(1)}, s32[1,1024]{1,0:T(1,128)S(1)}, bf16[8,1024]{1,0:T(8,128)(2,1)S(1)}, bf16[1024,256]{1,0:T(8,128)(2,1)S(1)}, bf16[264,256]{1,0:T(8,128)(2,1)S(1)}) custom-call(s32[1,1024]{1,0:T(1,128)} %bitcast.10, s32[1,1024]{1,0:T(1,128)} %bitcast.12, s32[1,1024]{1,0:T(1,128)} %bitcast.16, s32[1,1024]{1,0:T(1,128)} %bitcast.17, ...), custom_call_target="tpu_custom_call" | custom-call | flops 134217728 | bytes 1228800 | tf_op jit(solution)/shard_map/pallas_call | solution.py:234
  2.2 3.1 %collective-permute-start = (bf16[264,256]{1,0:T(8,128)(2,1)S(1)}, bf16[264,256]{1,0:T(8,128)(2,1)S(1)}, u32[]{:S(2)}, u32[]{:S(2)}) collective-permute-start(bf16[264,256]{1,0:T(8,128)(2,1)S(1)} %get-tuple-element.27), channel_id=1, source_target_pairs={{0,4},{1,5},{4,8},{5,9},{8,12},{9,13},{12,0},{13,1},{2,6},{3,7},{6... | collective-permute-start | bytes 405512 | tf_op jit(solution)/shard_map/ppermute | solution.py:229
  5.3 0.0 copy-start.7
  5.3 0.0 copy-start
  5.3 1.0 %shard_map.116 = (bf16[264,256]{1,0:T(8,128)(2,1)S(1)}, bf16[264,256]{1,0:T(8,128)(2,1)S(1)}, bf16[264,256]{1,0:T(8,128)(2,1)S(1)}) custom-call(s32[1,1024]{1,0:T(1,128)S(1)} %get-tuple-element.23.refs_0_, bf16[8,1024]{1,0:T(8,128)(2,1)S(1)} %get-tuple-element.24.refs_1_, bf16[1024,256]{1,0:T(8,128)(2,1)S(1)} %get-tuple-element.25.refs_2_), custom_call_target="tpu_custom_call" | custom-call | flops 4294967296 | bytes 950272 | tf_op jit(solution)/shard_map/pallas_call | solution.py:234
  6.3 0.0 copy-start.2
  6.3 2.1 %collective-permute-start.1 = (bf16[264,256]{1,0:T(8,128)(2,1)S(1)}, bf16[264,256]{1,0:T(8,128)(2,1)S(1)}, u32[]{:S(2)}, u32[]{:S(2)}) collective-permute-start(bf16[264,256]{1,0:T(8,128)(2,1)S(1)} %get-tuple-element.28), channel_id=1, source_target_pairs={{0,12},{1,13},{4,0},{5,1},{8,4},{9,5},{12,8},{13,9},{2,14},{3,15},... | collective-permute-start | bytes 405512 | tf_op jit(solution)/shard_map/ppermute | solution.py:229
  8.4 1.0 %collective-permute-start.2 = (bf16[264,256]{1,0:T(8,128)(2,1)S(1)}, bf16[264,256]{1,0:T(8,128)(2,1)S(1)}, u32[]{:S(2)}, u32[]{:S(2)}) collective-permute-start(bf16[264,256]{1,0:T(8,128)(2,1)S(1)} %get-tuple-element.33), channel_id=1, source_target_pairs={{0,8},{1,9},{4,12},{5,13},{8,0},{9,1},{12,4},{13,5},{2,10},{3,11},... | collective-permute-start | bytes 405512 | tf_op jit(solution)/shard_map/ppermute | solution.py:229
  9.4 0.8 %collective-permute-start.3 = (bf16[264,256]{1,0:T(8,128)(2,1)S(1)}, bf16[264,256]{1,0:T(8,128)(2,1)S(1)}, u32[]{:S(2)}, u32[]{:S(2)}) collective-permute-start(bf16[264,256]{1,0:T(8,128)(2,1)S(1)} %get-tuple-element.34), channel_id=1, source_target_pairs={{0,9},{1,8},{4,13},{5,12},{8,1},{9,0},{12,5},{13,4},{2,11},{3,10},... | collective-permute-start | bytes 405512 | tf_op jit(solution)/shard_map/ppermute | solution.py:229
  10.2 1.2 %shard_map.114 = (bf16[264,256]{1,0:T(8,128)(2,1)S(1)}, bf16[264,256]{1,0:T(8,128)(2,1)S(1)}, bf16[264,256]{1,0:T(8,128)(2,1)S(1)}, bf16[264,256]{1,0:T(8,128)(2,1)S(1)}) custom-call(s32[1,1024]{1,0:T(1,128)S(1)} %get-tuple-element.23.refs_0_, bf16[8,1024]{1,0:T(8,128)(2,1)S(1)} %get-tuple-element.24.refs_1_, bf16[1024,256]{1,0:T(8,128)(2,1)S(1)} %get-tuple-element.25.refs_2_), custom_call_target="tpu_custom_call" | custom-call | tf_op jit(solution)/shard_map/pallas_call | solution.py:234
  11.4 0.9 %collective-permute-start.4 = (bf16[264,256]{1,0:T(8,128)(2,1)S(1)}, bf16[264,256]{1,0:T(8,128)(2,1)S(1)}, u32[]{:S(2)}, u32[]{:S(2)}) collective-permute-start(bf16[264,256]{1,0:T(8,128)(2,1)S(1)} %get-tuple-element.37), channel_id=1, source_target_pairs={{0,5},{1,4},{4,9},{5,8},{8,13},{9,12},{12,1},{13,0},{2,7},{3,6},{6... | collective-permute-start | bytes 405512 | tf_op jit(solution)/shard_map/ppermute | solution.py:229
  12.3 0.0 collective-permute-done.refs_1_.refs_3_
  12.3 2.7 %collective-permute-start.5 = (bf16[264,256]{1,0:T(8,128)(2,1)S(1)}, bf16[264,256]{1,0:T(8,128)(2,1)S(1)}, u32[]{:S(2)}, u32[]{:S(2)}) collective-permute-start(bf16[264,256]{1,0:T(8,128)(2,1)S(1)} %get-tuple-element.38), channel_id=1, source_target_pairs={{0,13},{1,12},{4,1},{5,0},{8,5},{9,4},{12,9},{13,8},{2,15},{3,14},... | collective-permute-start | bytes 405512 | tf_op jit(solution)/shard_map/ppermute | solution.py:229
  15.0 0.0 collective-permute-done.1.refs_2_.refs_4_
  15.0 1.2 %collective-permute-start.6 = (bf16[264,256]{1,0:T(8,128)(2,1)S(1)}, bf16[264,256]{1,0:T(8,128)(2,1)S(1)}, u32[]{:S(2)}, u32[]{:S(2)}) collective-permute-start(bf16[264,256]{1,0:T(8,128)(2,1)S(1)} %get-tuple-element.39), channel_id=1, source_target_pairs={{0,1},{1,0},{4,5},{5,4},{8,9},{9,8},{12,13},{13,12},{2,3},{3,2},{6... | collective-permute-start | bytes 405512 | tf_op jit(solution)/shard_map/ppermute | solution.py:229
  16.3 0.0 copy-done.7
  16.3 0.0 copy-done
  16.3 1.2 %shard_map.115 = f32[1,1024]{1,0:T(1,128)S(1)} custom-call(bf16[264,256]{1,0:T(8,128)(2,1)S(1)} %get-tuple-element.26.packed.refs_3_.refs_5_, f32[1,2048]{1,0:T(1,128)S(1)} %bitcast.8, bf16[1024,2048]{1,0:T(8,128)(2,1)S(1)} %copy-done), custom_call_target="tpu_custom_call" | custom-call | tf_op jit(solution)/shard_map/pallas_call | solution.py:234
  17.5 4.9 %psum.7.refs_4_.refs_5_ = f32[1,1024]{1,0:T(1,128)S(1)} all-reduce(f32[1,1024]{1,0:T(1,128)S(1)} %shard_map.115), channel_id=1, replica_groups=mesh['groups'=2,'rows'=4,'feat'=2,'ent'=2] {'feat'}, use_global_device_ids=true, to_apply=%region_0.0 | all-reduce | flops 1024 | bytes 8192 | tf_op jit(solution)/shard_map/psum | solution.py:322
  22.4 0.0 copy-done.2
  22.4 0.6 %shard_map.117 = (bf16[1024,256]{1,0:T(8,128)(2,1)S(1)}, f32[1,256]{1,0:T(1,128)S(1)}, f32[1,256]{1,0:T(1,128)S(1)}, f32[1,256]{1,0:T(1,128)S(1)}) custom-call(f32[512,256]{1,0:T(8,128)S(1)} %copy-done.2, bf16[264,256]{1,0:T(8,128)(2,1)S(1)} %collective-permute-done.refs_1_.refs_3_, bf16[264,256]{1,0:T(8,128)(2,1)S(1)} %collective-permute-done.1.refs_2_.refs_4_, ...), custom_call_target="tpu_custom_call" | custom-call | tf_op jit(solution)/shard_map/pallas_call | solution.py:234
  23.0 2.5 %collective-permute-done.2.refs_1_.refs_6_ = bf16[264,256]{1,0:T(8,128)(2,1)S(1)} collective-permute-done((bf16[264,256]{1,0:T(8,128)(2,1)S(1)}, bf16[264,256]{1,0:T(8,128)(2,1)S(1)}, u32[]{:S(2)}, u32[]{:S(2)}) %collective-permute-start.2) | collective-permute-done | bytes 135200 | tf_op jit(solution)/shard_map/ppermute | solution.py:229
  25.5 2.6 %collective-permute-done.3.refs_2_.refs_7_ = bf16[264,256]{1,0:T(8,128)(2,1)S(1)} collective-permute-done((bf16[264,256]{1,0:T(8,128)(2,1)S(1)}, bf16[264,256]{1,0:T(8,128)(2,1)S(1)}, u32[]{:S(2)}, u32[]{:S(2)}) %collective-permute-start.3) | collective-permute-done | bytes 135200 | tf_op jit(solution)/shard_map/ppermute | solution.py:229
  28.1 0.5 shard_map.118
  28.6 0.0 collective-permute-done.4.refs_6_.refs_8_
  28.6 0.0 collective-permute-done.5.refs_7_.refs_9_
  28.6 0.0 collective-permute-done.6.refs_8_.refs_10_
  28.6 0.0 copy-start.1
  28.6 0.0 copy-start.3
  28.6 0.0 copy-start.4
  28.7 0.0 copy-start.5
  28.7 0.0 copy-start.6
  28.7 0.6 %shard_map.119 = f32[16,1,256]{2,1,0:T(1,128)S(1)} custom-call(bf16[1024,256]{1,0:T(8,128)(2,1)S(1)} %get-tuple-element.29.refs_0_, f32[1,256]{1,0:T(1,128)S(1)} %get-tuple-element.30.refs_1_, f32[1,256]{1,0:T(1,128)S(1)} %get-tuple-element.31.refs_2_, f32[1,256]{1,0:T(1,128)S(1)} %get-tuple-element.32.refs_3_, f32[1,256]{1,0:T(1,128)S(1)} %get-tuple-element.35.refs_4_, ...), custom_call_target="tpu_custom_call" | custom-call | flops 4294967296 | bytes 951296 | tf_op jit(solution)/shard_map/pallas_call | solution.py:234
  29.3 12.0 %all_to_all.10.refs_6_ = f32[16,1,256]{2,1,0:T(1,128)S(1)} all-to-all(f32[16,1,256]{2,1,0:T(1,128)S(1)} %shard_map.119), channel_id=1, replica_groups=mesh['groups'=2,'rows'=4,'feat'=2,'ent'=2] {'rows','feat','ent'}, dimensions={0} | all-to-all | bytes 32768 | tf_op jit(solution)/shard_map/all_to_all | solution.py:349
  41.3 0.0 copy-done.1
  41.3 0.0 copy-done.3
  41.3 0.0 copy-done.4
  41.3 0.0 copy-done.5
  41.4 0.0 copy-done.6
  41.4 1.0 %shard_map.120 = f32[8,1,2304]{2,1,0:T(1,128)S(1)} custom-call(s32[1,1024]{1,0:T(1,128)S(1)} %bitcast.11, s32[1,1024]{1,0:T(1,128)S(1)} %bitcast.13, s32[2,1024]{1,0:T(2,128)S(1)} %get-tuple-element.22.refs_2_, s32[1,1024]{1,0:T(1,128)S(1)} %bitcast.14, s32[1,1024]{1,0:T(1,128)S(1)} %bitcast.15, f32[1,1024]{1,0:T(1,128)S(1)} %psum.7.refs_4_.refs_5_, ...), custom_call_target="tpu_custom_call" | custom-call | flops 67108864 | bytes 4313088 | tf_op jit(solution)/shard_map/pallas_call | solution.py:234
  42.4 8.4 %all_to_all.11.refs_2_ = f32[8,1,2304]{2,1,0:T(1,128)S(1)} all-to-all(f32[8,1,2304]{2,1,0:T(1,128)S(1)} %shard_map.120), channel_id=1, replica_groups=mesh['groups'=2,'rows'=4,'feat'=2,'ent'=2] {'rows','ent'}, dimensions={0} | all-to-all | bytes 147456 | tf_op jit(solution)/shard_map/all_to_all | solution.py:366
  50.8 2.1 %shard_map.121 = (f32[1,2048]{1,0:T(1,128)}, f32[512,256]{1,0:T(8,128)}) custom-call(f32[512,256]{1,0:T(8,128)S(1)} %copy-done.2, f32[1,2048]{1,0:T(1,128)S(1)} %bitcast.9, f32[8,1,2304]{2,1,0:T(1,128)S(1)} %all_to_all.11.refs_2_, bf16[264,256]{1,0:T(8,128)(2,1)S(1)} %collective-permute-done.refs_1_.refs_3_, ...), custom_call_target="tpu_custom_call" | custom-call | flops 1073741824 | bytes 2220032 | tf_op jit(solution)/shard_map/pallas_call | solution.py:234
  (1 shorter events, 0.0 us)
Async XLA Ops:
  2.2 10.1 %collective-permute-start = (bf16[264,256]{1,0:T(8,128)(2,1)S(1)}, bf16[264,256]{1,0:T(8,128)(2,1)S(1)}, u32[]{:S(2)}, u32[]{:S(2)}) collective-permute-start(bf16[264,256]{1,0:T(8,128)(2,1)S(1)} %get-tuple-element.27), channel_id=1, source_target_pairs={{0,4},{1,5},{4,8},{5,9},{8,12},{9,13},{12,0},{13,1},{2,6},{3,7},{6... | collective-permute-start | bytes 405512 | tf_op jit(solution)/shard_map/ppermute | solution.py:229
  5.3 11.0 %copy-start.7 = (bf16[2048]{0:T(1024)(128)(2,1)S(1)}, bf16[2048]{0:T(1024)(128)(2,1)}, u32[]{:S(2)}) copy-start(bf16[2048]{0:T(1024)(128)(2,1)} %param.11) | copy-start | bytes 12292
  5.3 11.0 %copy-start = (bf16[1024,2048]{1,0:T(8,128)(2,1)S(1)}, bf16[1024,2048]{1,0:T(8,128)(2,1)}, u32[]{:S(2)}) copy-start(bf16[1024,2048]{1,0:T(8,128)(2,1)} %refs_7_.1) | copy-start | bytes 12582916
  6.3 16.1 %copy-start.2 = (f32[512,256]{1,0:T(8,128)S(1)}, f32[512,256]{1,0:T(8,128)}, u32[]{:S(2)}) copy-start(f32[512,256]{1,0:T(8,128)} %refs_0_.3) | copy-start | bytes 1572868
  6.3 8.8 %collective-permute-start.1 = (bf16[264,256]{1,0:T(8,128)(2,1)S(1)}, bf16[264,256]{1,0:T(8,128)(2,1)S(1)}, u32[]{:S(2)}, u32[]{:S(2)}) collective-permute-start(bf16[264,256]{1,0:T(8,128)(2,1)S(1)} %get-tuple-element.28), channel_id=1, source_target_pairs={{0,12},{1,13},{4,0},{5,1},{8,4},{9,5},{12,8},{13,9},{2,14},{3,15},... | collective-permute-start | bytes 405512 | tf_op jit(solution)/shard_map/ppermute | solution.py:229
  8.4 17.2 %collective-permute-start.2 = (bf16[264,256]{1,0:T(8,128)(2,1)S(1)}, bf16[264,256]{1,0:T(8,128)(2,1)S(1)}, u32[]{:S(2)}, u32[]{:S(2)}) collective-permute-start(bf16[264,256]{1,0:T(8,128)(2,1)S(1)} %get-tuple-element.33), channel_id=1, source_target_pairs={{0,8},{1,9},{4,12},{5,13},{8,0},{9,1},{12,4},{13,5},{2,10},{3,11},... | collective-permute-start | bytes 405512 | tf_op jit(solution)/shard_map/ppermute | solution.py:229
  9.4 18.7 %collective-permute-start.3 = (bf16[264,256]{1,0:T(8,128)(2,1)S(1)}, bf16[264,256]{1,0:T(8,128)(2,1)S(1)}, u32[]{:S(2)}, u32[]{:S(2)}) collective-permute-start(bf16[264,256]{1,0:T(8,128)(2,1)S(1)} %get-tuple-element.34), channel_id=1, source_target_pairs={{0,9},{1,8},{4,13},{5,12},{8,1},{9,0},{12,5},{13,4},{2,11},{3,10},... | collective-permute-start | bytes 405512 | tf_op jit(solution)/shard_map/ppermute | solution.py:229
  11.4 17.2 %collective-permute-start.4 = (bf16[264,256]{1,0:T(8,128)(2,1)S(1)}, bf16[264,256]{1,0:T(8,128)(2,1)S(1)}, u32[]{:S(2)}, u32[]{:S(2)}) collective-permute-start(bf16[264,256]{1,0:T(8,128)(2,1)S(1)} %get-tuple-element.37), channel_id=1, source_target_pairs={{0,5},{1,4},{4,9},{5,8},{8,13},{9,12},{12,1},{13,0},{2,7},{3,6},{6... | collective-permute-start | bytes 405512 | tf_op jit(solution)/shard_map/ppermute | solution.py:229
  12.3 16.3 %collective-permute-start.5 = (bf16[264,256]{1,0:T(8,128)(2,1)S(1)}, bf16[264,256]{1,0:T(8,128)(2,1)S(1)}, u32[]{:S(2)}, u32[]{:S(2)}) collective-permute-start(bf16[264,256]{1,0:T(8,128)(2,1)S(1)} %get-tuple-element.38), channel_id=1, source_target_pairs={{0,13},{1,12},{4,1},{5,0},{8,5},{9,4},{12,9},{13,8},{2,15},{3,14},... | collective-permute-start | bytes 405512 | tf_op jit(solution)/shard_map/ppermute | solution.py:229
  15.0 13.6 %collective-permute-start.6 = (bf16[264,256]{1,0:T(8,128)(2,1)S(1)}, bf16[264,256]{1,0:T(8,128)(2,1)S(1)}, u32[]{:S(2)}, u32[]{:S(2)}) collective-permute-start(bf16[264,256]{1,0:T(8,128)(2,1)S(1)} %get-tuple-element.39), channel_id=1, source_target_pairs={{0,1},{1,0},{4,5},{5,4},{8,9},{9,8},{12,13},{13,12},{2,3},{3,2},{6... | collective-permute-start | bytes 405512 | tf_op jit(solution)/shard_map/ppermute | solution.py:229
  28.6 12.7 %copy-start.1 = (bf16[1024,2048]{1,0:T(8,128)(2,1)S(1)}, bf16[1024,2048]{1,0:T(8,128)(2,1)}, u32[]{:S(2)}) copy-start(bf16[1024,2048]{1,0:T(8,128)(2,1)} %refs_7_.1) | copy-start | bytes 12582916
  28.6 12.7 %copy-start.3 = (s32[1024,1]{0,1:T(1,128)S(1)}, s32[1024,1]{0,1:T(1,128)}, u32[]{:S(2)}) copy-start(s32[1024,1]{0,1:T(1,128)} %param.14) | copy-start | bytes 12292
  28.6 12.7 %copy-start.4 = (s32[1024,1]{0,1:T(1,128)S(1)}, s32[1024,1]{0,1:T(1,128)}, u32[]{:S(2)}) copy-start(s32[1024,1]{0,1:T(1,128)} %param.16) | copy-start | bytes 12292
  28.7 12.7 %copy-start.5 = (s32[1024]{0:T(1024)S(1)}, s32[1024]{0:T(1024)}, u32[]{:S(2)}) copy-start(s32[1024]{0:T(1024)} %param.18) | copy-start | bytes 12292
  28.7 12.7 %copy-start.6 = (s32[1024]{0:T(1024)S(1)}, s32[1024]{0:T(1024)}, u32[]{:S(2)}) copy-start(s32[1024]{0:T(1024)} %param.19) | copy-start | bytes 12292

commit v23 on v20

--- a/solution.py
+++ b/solution.py
@@ -270,9 +270,8 @@
 
     row = pltpu.VMEM((1, rows_here), jnp.int32)
     middle = n_rows // 2
-    away = [up * n_ent for half in range(1, middle) for up in (half, n_rows - half)]
+    away = [up * n_ent + c for c in range(n_ent) for half in range(1, middle) for up in (half, n_rows - half)]
     away += [middle * n_ent + c for c in range(n_ent)]
-    away += [up * n_ent + c for c in range(1, n_ent) for half in range(1, middle) for up in (half, n_rows - half)]
     first, second, near = away[:1], away[1:-2], [*away[-2:], *reversed(range(n_ent))]
     chunk = shape(capacity + IDS, width, dtype=BF16)
     flops = len(first) * 2 * capacity * rows_here * width

time: 53.1 us -> 54.1 us (1.019)
  waiting for transfers between devices: 5.09 us -> 7.46 us
  blocking collectives: 25.3 us -> 23.9 us
    ppermute x7, waiting for transfers between devices: 5.09 us -> 7.46 us  [shift_send(): return lax.ppermute(x, HOME, pairs)]
    all_to_all x1, blocking collectives: 12 us -> 10.6 us  [body(): lax.all_to_all(scores, EVERY, split_axis=0, concat_axis=0, tiled=True)]
  transfers between devices with their start and end apart: 7 -> 7, of which waited for: 2 -> 2; matrix products, arithmetic and copies ran while one was open for 0% -> 0% of each run, Pallas kernels for 9% -> 8%
where the time goes in v23:
time: 54.1 us; the launch traced here: 53.8 us
  blocking collectives  23.9 us (44%)
  starting transfers between devices  11.8 us (22%)
  Pallas kernels  9.83 us (18%)
  waiting for transfers between devices  7.46 us (14%)
  between operations  0.76 us (1%)
    ppermute x7, starting transfers between devices, shift_send(): return lax.ppermute(x, HOME, pairs)  11.8 us
    all_to_all x1, blocking collectives, body(): lax.all_to_all(scores, EVERY, split_axis=0, concat_axis=0, tiled=True)  10.6 us
    pallas_call x9, Pallas kernels, call(): pl.pallas_call(kernel, out_shape=out_shape, in_specs=in_specs, out_specs=...  9.83 us
    all_to_all x1, blocking collectives, body(): came = lax.all_to_all(sent, HOME, split_axis=0, concat_axis=0, tiled=True)  8.4 us
    ppermute x7, waiting for transfers between devices, shift_send(): return lax.ppermute(x, HOME, pairs)  7.46 us
    psum x1, blocking collectives, body(): global_total = lax.psum(global_part, 'feat')  4.91 us
  transfers between devices with their start and end apart: 7, of which 2 were waited for; matrix products, arithmetic and copies ran while one was open for 0% of the time, Pallas kernels for 8%

profile of v23, /device:TPU:0, one launch (start us, length us, event | category | flops | bytes accessed | tf_op | source)
XLA Modules:
  0.0 53.8 jit_solution(4051091871781686184)
XLA Ops:
  0.6 1.6 %shard_map.113 = (s32[2,1024]{1,0:T(2,128)S(1)}, s32[1,1024]{1,0:T(1,128)S(1)}, bf16[8,1024]{1,0:T(8,128)(2,1)S(1)}, bf16[1024,256]{1,0:T(8,128)(2,1)S(1)}, bf16[264,256]{1,0:T(8,128)(2,1)S(1)}) custom-call(s32[1,1024]{1,0:T(1,128)} %bitcast.10, s32[1,1024]{1,0:T(1,128)} %bitcast.12, s32[1,1024]{1,0:T(1,128)} %bitcast.16, s32[1,1024]{1,0:T(1,128)} %bitcast.17, ...), custom_call_target="tpu_custom_call" | custom-call | flops 134217728 | bytes 1228800 | tf_op jit(solution)/shard_map/pallas_call | solution.py:234
  2.2 3.1 %collective-permute-start = (bf16[264,256]{1,0:T(8,128)(2,1)S(1)}, bf16[264,256]{1,0:T(8,128)(2,1)S(1)}, u32[]{:S(2)}, u32[]{:S(2)}) collective-permute-start(bf16[264,256]{1,0:T(8,128)(2,1)S(1)} %get-tuple-element.24), channel_id=1, source_target_pairs={{0,4},{1,5},{4,8},{5,9},{8,12},{9,13},{12,0},{13,1},{2,6},{3,7},{6... | collective-permute-start | bytes 405512 | tf_op jit(solution)/shard_map/ppermute | solution.py:229
  5.3 0.0 copy-start.7
  5.3 0.0 copy-start
  5.3 1.0 %shard_map.115 = (bf16[264,256]{1,0:T(8,128)(2,1)S(1)}, bf16[264,256]{1,0:T(8,128)(2,1)S(1)}, bf16[264,256]{1,0:T(8,128)(2,1)S(1)}) custom-call(s32[1,1024]{1,0:T(1,128)S(1)} %get-tuple-element.23.place.refs_0_, bf16[8,1024]{1,0:T(8,128)(2,1)S(1)} %get-tuple-element.25.refs_1_, bf16[1024,256]{1,0:T(8,128)(2,1)S(1)} %get-tuple-element.26.refs_2_), custom_call_target="tpu_custom_call" | custom-call | flops 4294967296 | bytes 950272 | tf_op jit(solution)/shard_map/pallas_call | solution.py:234
  6.3 0.0 copy-start.2
  6.3 2.1 %collective-permute-start.1 = (bf16[264,256]{1,0:T(8,128)(2,1)S(1)}, bf16[264,256]{1,0:T(8,128)(2,1)S(1)}, u32[]{:S(2)}, u32[]{:S(2)}) collective-permute-start(bf16[264,256]{1,0:T(8,128)(2,1)S(1)} %get-tuple-element.27), channel_id=1, source_target_pairs={{0,12},{1,13},{4,0},{5,1},{8,4},{9,5},{12,8},{13,9},{2,14},{3,15},... | collective-permute-start | bytes 405512 | tf_op jit(solution)/shard_map/ppermute | solution.py:229
  8.4 0.0 collective-permute-start.2
  8.4 3.5 %collective-permute-start.3 = (bf16[264,256]{1,0:T(8,128)(2,1)S(1)}, bf16[264,256]{1,0:T(8,128)(2,1)S(1)}, u32[]{:S(2)}, u32[]{:S(2)}) collective-permute-start(bf16[264,256]{1,0:T(8,128)(2,1)S(1)} %get-tuple-element.34), channel_id=1, source_target_pairs={{0,13},{1,12},{4,1},{5,0},{8,5},{9,4},{12,9},{13,8},{2,15},{3,14},... | collective-permute-start | bytes 405512 | tf_op jit(solution)/shard_map/ppermute | solution.py:229
  11.9 0.0 copy-done.7
  11.9 0.0 copy-done
  11.9 1.2 %shard_map.114.refs_3_ = f32[1,1024]{1,0:T(1,128)S(1)} custom-call(s32[1,1024]{1,0:T(1,128)S(1)} %get-tuple-element.23.place.refs_0_, f32[1,2048]{1,0:T(1,128)S(1)} %bitcast.8, bf16[1024,2048]{1,0:T(8,128)(2,1)S(1)} %copy-done), custom_call_target="tpu_custom_call" | custom-call | tf_op jit(solution)/shard_map/pallas_call | solution.py:234
  13.1 1.2 %shard_map.116 = (bf16[264,256]{1,0:T(8,128)(2,1)S(1)}, bf16[264,256]{1,0:T(8,128)(2,1)S(1)}, bf16[264,256]{1,0:T(8,128)(2,1)S(1)}, bf16[264,256]{1,0:T(8,128)(2,1)S(1)}) custom-call(s32[1,1024]{1,0:T(1,128)S(1)} %get-tuple-element.23.place.refs_0_, bf16[8,1024]{1,0:T(8,128)(2,1)S(1)} %get-tuple-element.25.refs_1_, ...), custom_call_target="tpu_custom_call" | custom-call | tf_op jit(solution)/shard_map/pallas_call | solution.py:234
  14.4 0.1 collective-permute-start.4
  14.5 0.0 collective-permute-done.refs_1_.refs_3_
  14.5 1.8 %collective-permute-start.5 = (bf16[264,256]{1,0:T(8,128)(2,1)S(1)}, bf16[264,256]{1,0:T(8,128)(2,1)S(1)}, u32[]{:S(2)}, u32[]{:S(2)}) collective-permute-start(bf16[264,256]{1,0:T(8,128)(2,1)S(1)} %get-tuple-element.38), channel_id=1, source_target_pairs={{0,9},{1,8},{4,13},{5,12},{8,1},{9,0},{12,5},{13,4},{2,11},{3,10},... | collective-permute-start | bytes 405512 | tf_op jit(solution)/shard_map/ppermute | solution.py:229
  16.3 0.0 collective-permute-done.1.refs_2_.refs_4_
  16.3 1.2 %collective-permute-start.6 = (bf16[264,256]{1,0:T(8,128)(2,1)S(1)}, bf16[264,256]{1,0:T(8,128)(2,1)S(1)}, u32[]{:S(2)}, u32[]{:S(2)}) collective-permute-start(bf16[264,256]{1,0:T(8,128)(2,1)S(1)} %get-tuple-element.39), channel_id=1, source_target_pairs={{0,1},{1,0},{4,5},{5,4},{8,9},{9,8},{12,13},{13,12},{2,3},{3,2},{6... | collective-permute-start | bytes 405512 | tf_op jit(solution)/shard_map/ppermute | solution.py:229
  17.5 4.9 %psum.7.refs_4_.refs_5_ = f32[1,1024]{1,0:T(1,128)S(1)} all-reduce(f32[1,1024]{1,0:T(1,128)S(1)} %shard_map.114.refs_3_), channel_id=1, replica_groups=mesh['groups'=2,'rows'=4,'feat'=2,'ent'=2] {'feat'}, use_global_device_ids=true, to_apply=%region_0.0 | all-reduce | flops 1024 | bytes 8192 | tf_op jit(solution)/shard_map/psum | solution.py:314
  22.4 0.0 copy-done.2
  22.4 0.6 %shard_map.117 = (bf16[1024,256]{1,0:T(8,128)(2,1)S(1)}, f32[1,256]{1,0:T(1,128)S(1)}, f32[1,256]{1,0:T(1,128)S(1)}, f32[1,256]{1,0:T(1,128)S(1)}) custom-call(f32[512,256]{1,0:T(8,128)S(1)} %copy-done.2, bf16[264,256]{1,0:T(8,128)(2,1)S(1)} %collective-permute-done.refs_1_.refs_3_, bf16[264,256]{1,0:T(8,128)(2,1)S(1)} %collective-permute-done.1.refs_2_.refs_4_, ...), custom_call_target="tpu_custom_call" | custom-call | tf_op jit(solution)/shard_map/pallas_call | solution.py:234
  23.0 0.0 collective-permute-done.2.refs_1_.refs_6_
  23.1 0.0 collective-permute-done.3.refs_2_.refs_7_
  23.1 0.5 shard_map.118
  23.6 4.9 %collective-permute-done.4.refs_6_.refs_8_ = bf16[264,256]{1,0:T(8,128)(2,1)S(1)} collective-permute-done((bf16[264,256]{1,0:T(8,128)(2,1)S(1)}, bf16[264,256]{1,0:T(8,128)(2,1)S(1)}, u32[]{:S(2)}, u32[]{:S(2)}) %collective-permute-start.4) | collective-permute-done | bytes 135200 | tf_op jit(solution)/shard_map/ppermute | solution.py:229
  28.4 2.6 %collective-permute-done.5.refs_7_.refs_9_ = bf16[264,256]{1,0:T(8,128)(2,1)S(1)} collective-permute-done((bf16[264,256]{1,0:T(8,128)(2,1)S(1)}, bf16[264,256]{1,0:T(8,128)(2,1)S(1)}, u32[]{:S(2)}, u32[]{:S(2)}) %collective-permute-start.5) | collective-permute-done | bytes 135200 | tf_op jit(solution)/shard_map/ppermute | solution.py:229
  31.0 0.0 collective-permute-done.6.refs_8_.refs_10_
  31.0 0.0 copy-start.1
  31.0 0.0 copy-start.3
  31.0 0.0 copy-start.4
  31.0 0.0 copy-start.5
  31.0 0.0 copy-start.6
  31.0 0.6 %shard_map.119 = f32[16,1,256]{2,1,0:T(1,128)S(1)} custom-call(bf16[1024,256]{1,0:T(8,128)(2,1)S(1)} %get-tuple-element.29.refs_0_, f32[1,256]{1,0:T(1,128)S(1)} %get-tuple-element.30.refs_1_, f32[1,256]{1,0:T(1,128)S(1)} %get-tuple-element.31.refs_2_, f32[1,256]{1,0:T(1,128)S(1)} %get-tuple-element.32.refs_3_, f32[1,256]{1,0:T(1,128)S(1)} %get-tuple-element.35.refs_4_, ...), custom_call_target="tpu_custom_call" | custom-call | flops 4294967296 | bytes 951296 | tf_op jit(solution)/shard_map/pallas_call | solution.py:234
  31.7 10.6 %all_to_all.10.refs_6_ = f32[16,1,256]{2,1,0:T(1,128)S(1)} all-to-all(f32[16,1,256]{2,1,0:T(1,128)S(1)} %shard_map.119), channel_id=1, replica_groups=mesh['groups'=2,'rows'=4,'feat'=2,'ent'=2] {'rows','feat','ent'}, dimensions={0} | all-to-all | bytes 32768 | tf_op jit(solution)/shard_map/all_to_all | solution.py:348
  42.3 0.0 copy-done.1
  42.3 0.0 copy-done.3
  42.3 0.0 copy-done.4
  42.3 0.0 copy-done.5
  42.3 0.0 copy-done.6
  42.3 1.0 %shard_map.120 = f32[8,1,2304]{2,1,0:T(1,128)S(1)} custom-call(s32[1,1024]{1,0:T(1,128)S(1)} %bitcast.11, s32[1,1024]{1,0:T(1,128)S(1)} %bitcast.13, s32[2,1024]{1,0:T(2,128)S(1)} %get-tuple-element.22.refs_2_, s32[1,1024]{1,0:T(1,128)S(1)} %bitcast.14, s32[1,1024]{1,0:T(1,128)S(1)} %bitcast.15, f32[1,1024]{1,0:T(1,128)S(1)} %psum.7.refs_4_.refs_5_, ...), custom_call_target="tpu_custom_call" | custom-call | flops 67108864 | bytes 4313088 | tf_op jit(solution)/shard_map/pallas_call | solution.py:234
  43.4 8.4 %all_to_all.11.refs_2_ = f32[8,1,2304]{2,1,0:T(1,128)S(1)} all-to-all(f32[8,1,2304]{2,1,0:T(1,128)S(1)} %shard_map.120), channel_id=1, replica_groups=mesh['groups'=2,'rows'=4,'feat'=2,'ent'=2] {'rows','ent'}, dimensions={0} | all-to-all | bytes 147456 | tf_op jit(solution)/shard_map/all_to_all | solution.py:365
  51.8 2.1 %shard_map.121 = (f32[1,2048]{1,0:T(1,128)}, f32[512,256]{1,0:T(8,128)}) custom-call(f32[512,256]{1,0:T(8,128)S(1)} %copy-done.2, f32[1,2048]{1,0:T(1,128)S(1)} %bitcast.9, f32[8,1,2304]{2,1,0:T(1,128)S(1)} %all_to_all.11.refs_2_, bf16[264,256]{1,0:T(8,128)(2,1)S(1)} %collective-permute-done.refs_1_.refs_3_, ...), custom_call_target="tpu_custom_call" | custom-call | flops 1073741824 | bytes 2220032 | tf_op jit(solution)/shard_map/pallas_call | solution.py:234
  (1 shorter events, 0.0 us)
Async XLA Ops:
  2.2 12.2 %collective-permute-start = (bf16[264,256]{1,0:T(8,128)(2,1)S(1)}, bf16[264,256]{1,0:T(8,128)(2,1)S(1)}, u32[]{:S(2)}, u32[]{:S(2)}) collective-permute-start(bf16[264,256]{1,0:T(8,128)(2,1)S(1)} %get-tuple-element.24), channel_id=1, source_target_pairs={{0,4},{1,5},{4,8},{5,9},{8,12},{9,13},{12,0},{13,1},{2,6},{3,7},{6... | collective-permute-start | bytes 405512 | tf_op jit(solution)/shard_map/ppermute | solution.py:229
  5.3 6.6 %copy-start.7 = (bf16[2048]{0:T(1024)(128)(2,1)S(1)}, bf16[2048]{0:T(1024)(128)(2,1)}, u32[]{:S(2)}) copy-start(bf16[2048]{0:T(1024)(128)(2,1)} %param.11) | copy-start | bytes 12292
  5.3 6.6 %copy-start = (bf16[1024,2048]{1,0:T(8,128)(2,1)S(1)}, bf16[1024,2048]{1,0:T(8,128)(2,1)}, u32[]{:S(2)}) copy-start(bf16[1024,2048]{1,0:T(8,128)(2,1)} %refs_7_.1) | copy-start | bytes 12582916
  6.3 16.2 %copy-start.2 = (f32[512,256]{1,0:T(8,128)S(1)}, f32[512,256]{1,0:T(8,128)}, u32[]{:S(2)}) copy-start(f32[512,256]{1,0:T(8,128)} %refs_0_.3) | copy-start | bytes 1572868
  6.3 10.0 %collective-permute-start.1 = (bf16[264,256]{1,0:T(8,128)(2,1)S(1)}, bf16[264,256]{1,0:T(8,128)(2,1)S(1)}, u32[]{:S(2)}, u32[]{:S(2)}) collective-permute-start(bf16[264,256]{1,0:T(8,128)(2,1)S(1)} %get-tuple-element.27), channel_id=1, source_target_pairs={{0,12},{1,13},{4,0},{5,1},{8,4},{9,5},{12,8},{13,9},{2,14},{3,15},... | collective-permute-start | bytes 405512 | tf_op jit(solution)/shard_map/ppermute | solution.py:229
  8.4 14.7 %collective-permute-start.2 = (bf16[264,256]{1,0:T(8,128)(2,1)S(1)}, bf16[264,256]{1,0:T(8,128)(2,1)S(1)}, u32[]{:S(2)}, u32[]{:S(2)}) collective-permute-start(bf16[264,256]{1,0:T(8,128)(2,1)S(1)} %get-tuple-element.33), channel_id=1, source_target_pairs={{0,5},{1,4},{4,9},{5,8},{8,13},{9,12},{12,1},{13,0},{2,7},{3,6},{6... | collective-permute-start | bytes 405512 | tf_op jit(solution)/shard_map/ppermute | solution.py:229
  8.4 14.7 %collective-permute-start.3 = (bf16[264,256]{1,0:T(8,128)(2,1)S(1)}, bf16[264,256]{1,0:T(8,128)(2,1)S(1)}, u32[]{:S(2)}, u32[]{:S(2)}) collective-permute-start(bf16[264,256]{1,0:T(8,128)(2,1)S(1)} %get-tuple-element.34), channel_id=1, source_target_pairs={{0,13},{1,12},{4,1},{5,0},{8,5},{9,4},{12,9},{13,8},{2,15},{3,14},... | collective-permute-start | bytes 405512 | tf_op jit(solution)/shard_map/ppermute | solution.py:229
  14.4 14.1 %collective-permute-start.4 = (bf16[264,256]{1,0:T(8,128)(2,1)S(1)}, bf16[264,256]{1,0:T(8,128)(2,1)S(1)}, u32[]{:S(2)}, u32[]{:S(2)}) collective-permute-start(bf16[264,256]{1,0:T(8,128)(2,1)S(1)} %get-tuple-element.37), channel_id=1, source_target_pairs={{0,8},{1,9},{4,12},{5,13},{8,0},{9,1},{12,4},{13,5},{2,10},{3,11},... | collective-permute-start | bytes 405512 | tf_op jit(solution)/shard_map/ppermute | solution.py:229
  14.5 16.5 %collective-permute-start.5 = (bf16[264,256]{1,0:T(8,128)(2,1)S(1)}, bf16[264,256]{1,0:T(8,128)(2,1)S(1)}, u32[]{:S(2)}, u32[]{:S(2)}) collective-permute-start(bf16[264,256]{1,0:T(8,128)(2,1)S(1)} %get-tuple-element.38), channel_id=1, source_target_pairs={{0,9},{1,8},{4,13},{5,12},{8,1},{9,0},{12,5},{13,4},{2,11},{3,10},... | collective-permute-start | bytes 405512 | tf_op jit(solution)/shard_map/ppermute | solution.py:229
  16.3 14.8 %collective-permute-start.6 = (bf16[264,256]{1,0:T(8,128)(2,1)S(1)}, bf16[264,256]{1,0:T(8,128)(2,1)S(1)}, u32[]{:S(2)}, u32[]{:S(2)}) collective-permute-start(bf16[264,256]{1,0:T(8,128)(2,1)S(1)} %get-tuple-element.39), channel_id=1, source_target_pairs={{0,1},{1,0},{4,5},{5,4},{8,9},{9,8},{12,13},{13,12},{2,3},{3,2},{6... | collective-permute-start | bytes 405512 | tf_op jit(solution)/shard_map/ppermute | solution.py:229
  31.0 11.3 %copy-start.1 = (bf16[1024,2048]{1,0:T(8,128)(2,1)S(1)}, bf16[1024,2048]{1,0:T(8,128)(2,1)}, u32[]{:S(2)}) copy-start(bf16[1024,2048]{1,0:T(8,128)(2,1)} %refs_7_.1) | copy-start | bytes 12582916
  31.0 11.3 %copy-start.3 = (s32[1024,1]{0,1:T(1,128)S(1)}, s32[1024,1]{0,1:T(1,128)}, u32[]{:S(2)}) copy-start(s32[1024,1]{0,1:T(1,128)} %param.14) | copy-start | bytes 12292
  31.0 11.3 %copy-start.4 = (s32[1024,1]{0,1:T(1,128)S(1)}, s32[1024,1]{0,1:T(1,128)}, u32[]{:S(2)}) copy-start(s32[1024,1]{0,1:T(1,128)} %param.16) | copy-start | bytes 12292
  31.0 11.3 %copy-start.5 = (s32[1024]{0:T(1024)S(1)}, s32[1024]{0:T(1024)}, u32[]{:S(2)}) copy-start(s32[1024]{0:T(1024)} %param.18) | copy-start | bytes 12292
  31.0 11.3 %copy-start.6 = (s32[1024]{0:T(1024)S(1)}, s32[1024]{0:T(1024)}, u32[]{:S(2)}) copy-start(s32[1024]{0:T(1024)} %param.19) | copy-start | bytes 12292

commit v24 on v23

--- a/solution.py
+++ b/solution.py
@@ -270,8 +270,10 @@
 
     row = pltpu.VMEM((1, rows_here), jnp.int32)
     middle = n_rows // 2
-    away = [up * n_ent + c for c in range(n_ent) for half in range(1, middle) for up in (half, n_rows - half)]
-    away += [middle * n_ent + c for c in range(n_ent)]
+    away = [middle * n_ent]
+    for c in range(n_ent):
+        away += [up * n_ent + c for half in range(1, middle) for up in (half, n_rows - half)]
+        away += [middle * n_ent + c + 1] if c + 1 < n_ent else []
     first, second, near = away[:1], away[1:-2], [*away[-2:], *reversed(range(n_ent))]
     chunk = shape(capacity + IDS, width, dtype=BF16)
     flops = len(first) * 2 * capacity * rows_here * width

time: 54.1 us -> 54 us (level)
  blocking collectives: 23.9 us -> 28 us
  starting transfers between devices: 11.8 us -> 8.31 us
  waiting for transfers between devices: 7.46 us -> 6.8 us
    all_to_all x1, blocking collectives: 10.6 us -> 14.5 us  [body(): lax.all_to_all(scores, EVERY, split_axis=0, concat_axis=0, tiled=True)]
    ppermute x7, starting transfers between devices: 11.8 us -> 8.31 us  [shift_send(): return lax.ppermute(x, HOME, pairs)]
    ppermute x7, waiting for transfers between devices: 7.46 us -> 6.8 us  [shift_send(): return lax.ppermute(x, HOME, pairs)]
where the time goes in v24:
time: 54 us; the launch traced here: 53.7 us
  blocking collectives  28 us (52%)
  Pallas kernels  9.82 us (18%)
  starting transfers between devices  8.31 us (15%)
  waiting for transfers between devices  6.8 us (13%)
  between operations  0.8 us (1%)
    all_to_all x1, blocking collectives, body(): lax.all_to_all(scores, EVERY, split_axis=0, concat_axis=0, tiled=True)  14.5 us
    pallas_call x9, Pallas kernels, call(): pl.pallas_call(kernel, out_shape=out_shape, in_specs=in_specs, out_specs=...  9.82 us
    all_to_all x1, blocking collectives, body(): came = lax.all_to_all(sent, HOME, split_axis=0, concat_axis=0, tiled=True)  8.4 us
    ppermute x7, starting transfers between devices, shift_send(): return lax.ppermute(x, HOME, pairs)  8.31 us
    ppermute x7, waiting for transfers between devices, shift_send(): return lax.ppermute(x, HOME, pairs)  6.8 us
    psum x1, blocking collectives, body(): global_total = lax.psum(global_part, 'feat')  5.08 us
  transfers between devices with their start and end apart: 7, of which 2 were waited for; matrix products, arithmetic and copies ran while one was open for 0% of the time, Pallas kernels for 8%

profile of v24, /device:TPU:0, one launch (start us, length us, event | category | flops | bytes accessed | tf_op | source)
XLA Modules:
  0.0 53.7 jit_solution(14331241438932209347)
XLA Ops:
  0.6 1.6 %shard_map.113 = (s32[2,1024]{1,0:T(2,128)S(1)}, s32[1,1024]{1,0:T(1,128)S(1)}, bf16[8,1024]{1,0:T(8,128)(2,1)S(1)}, bf16[1024,256]{1,0:T(8,128)(2,1)S(1)}, bf16[264,256]{1,0:T(8,128)(2,1)S(1)}) custom-call(s32[1,1024]{1,0:T(1,128)} %bitcast.10, s32[1,1024]{1,0:T(1,128)} %bitcast.12, s32[1,1024]{1,0:T(1,128)} %bitcast.16, s32[1,1024]{1,0:T(1,128)} %bitcast.17, ...), custom_call_target="tpu_custom_call" | custom-call | flops 134217728 | bytes 1228800 | tf_op jit(solution)/shard_map/pallas_call | solution.py:234
  2.2 4.1 %collective-permute-start = (bf16[264,256]{1,0:T(8,128)(2,1)S(1)}, bf16[264,256]{1,0:T(8,128)(2,1)S(1)}, u32[]{:S(2)}, u32[]{:S(2)}) collective-permute-start(bf16[264,256]{1,0:T(8,128)(2,1)S(1)} %get-tuple-element.24), channel_id=1, source_target_pairs={{0,8},{1,9},{4,12},{5,13},{8,0},{9,1},{12,4},{13,5},{2,10},{3,11},... | collective-permute-start | bytes 405512 | tf_op jit(solution)/shard_map/ppermute | solution.py:229
  6.3 0.0 copy-start.7
  6.3 0.0 copy-start
  6.3 1.0 %shard_map.115 = (bf16[264,256]{1,0:T(8,128)(2,1)S(1)}, bf16[264,256]{1,0:T(8,128)(2,1)S(1)}, bf16[264,256]{1,0:T(8,128)(2,1)S(1)}) custom-call(s32[1,1024]{1,0:T(1,128)S(1)} %get-tuple-element.23.place.refs_0_, bf16[8,1024]{1,0:T(8,128)(2,1)S(1)} %get-tuple-element.25.refs_1_, bf16[1024,256]{1,0:T(8,128)(2,1)S(1)} %get-tuple-element.26.refs_2_), custom_call_target="tpu_custom_call" | custom-call | flops 4294967296 | bytes 950272 | tf_op jit(solution)/shard_map/pallas_call | solution.py:234
  7.3 0.0 copy-start.2
  7.3 1.6 %collective-permute-start.1 = (bf16[264,256]{1,0:T(8,128)(2,1)S(1)}, bf16[264,256]{1,0:T(8,128)(2,1)S(1)}, u32[]{:S(2)}, u32[]{:S(2)}) collective-permute-start(bf16[264,256]{1,0:T(8,128)(2,1)S(1)} %get-tuple-element.27), channel_id=1, source_target_pairs={{0,4},{1,5},{4,8},{5,9},{8,12},{9,13},{12,0},{13,1},{2,6},{3,7},{6... | collective-permute-start | bytes 405512 | tf_op jit(solution)/shard_map/ppermute | solution.py:229
  8.9 2.2 %collective-permute-start.2 = (bf16[264,256]{1,0:T(8,128)(2,1)S(1)}, bf16[264,256]{1,0:T(8,128)(2,1)S(1)}, u32[]{:S(2)}, u32[]{:S(2)}) collective-permute-start(bf16[264,256]{1,0:T(8,128)(2,1)S(1)} %get-tuple-element.33), channel_id=1, source_target_pairs={{0,12},{1,13},{4,0},{5,1},{8,4},{9,5},{12,8},{13,9},{2,14},{3,15},... | collective-permute-start | bytes 405512 | tf_op jit(solution)/shard_map/ppermute | solution.py:229
  11.2 0.0 collective-permute-start.3
  11.2 0.0 copy-done.7
  11.2 0.0 copy-done
  11.2 1.2 %shard_map.114.refs_3_ = f32[1,1024]{1,0:T(1,128)S(1)} custom-call(s32[1,1024]{1,0:T(1,128)S(1)} %get-tuple-element.23.place.refs_0_, f32[1,2048]{1,0:T(1,128)S(1)} %bitcast.8, bf16[1024,2048]{1,0:T(8,128)(2,1)S(1)} %copy-done), custom_call_target="tpu_custom_call" | custom-call | tf_op jit(solution)/shard_map/pallas_call | solution.py:234
  12.4 1.2 %shard_map.116 = (bf16[264,256]{1,0:T(8,128)(2,1)S(1)}, bf16[264,256]{1,0:T(8,128)(2,1)S(1)}, bf16[264,256]{1,0:T(8,128)(2,1)S(1)}, bf16[264,256]{1,0:T(8,128)(2,1)S(1)}) custom-call(s32[1,1024]{1,0:T(1,128)S(1)} %get-tuple-element.23.place.refs_0_, bf16[8,1024]{1,0:T(8,128)(2,1)S(1)} %get-tuple-element.25.refs_1_, ...), custom_call_target="tpu_custom_call" | custom-call | tf_op jit(solution)/shard_map/pallas_call | solution.py:234
  13.6 0.3 collective-permute-start.4
  14.0 3.5 %collective-permute-done.refs_1_.refs_3_ = bf16[264,256]{1,0:T(8,128)(2,1)S(1)} collective-permute-done((bf16[264,256]{1,0:T(8,128)(2,1)S(1)}, bf16[264,256]{1,0:T(8,128)(2,1)S(1)}, u32[]{:S(2)}, u32[]{:S(2)}) %collective-permute-start) | collective-permute-done | bytes 135200 | tf_op jit(solution)/shard_map/ppermute | solution.py:229
  17.5 0.0 collective-permute-start.5
  17.5 0.0 collective-permute-done.1.refs_2_.refs_4_
  17.5 0.0 collective-permute-start.6
  17.5 5.1 %psum.7.refs_4_.refs_5_ = f32[1,1024]{1,0:T(1,128)S(1)} all-reduce(f32[1,1024]{1,0:T(1,128)S(1)} %shard_map.114.refs_3_), channel_id=1, replica_groups=mesh['groups'=2,'rows'=4,'feat'=2,'ent'=2] {'feat'}, use_global_device_ids=true, to_apply=%region_0.0 | all-reduce | flops 1024 | bytes 8192 | tf_op jit(solution)/shard_map/psum | solution.py:316
  22.6 0.0 copy-done.2
  22.6 0.6 %shard_map.117 = (bf16[1024,256]{1,0:T(8,128)(2,1)S(1)}, f32[1,256]{1,0:T(1,128)S(1)}, f32[1,256]{1,0:T(1,128)S(1)}, f32[1,256]{1,0:T(1,128)S(1)}) custom-call(f32[512,256]{1,0:T(8,128)S(1)} %copy-done.2, bf16[264,256]{1,0:T(8,128)(2,1)S(1)} %collective-permute-done.refs_1_.refs_3_, bf16[264,256]{1,0:T(8,128)(2,1)S(1)} %collective-permute-done.1.refs_2_.refs_4_, ...), custom_call_target="tpu_custom_call" | custom-call | tf_op jit(solution)/shard_map/pallas_call | solution.py:234
  23.2 0.0 collective-permute-done.2.refs_1_.refs_6_
  23.3 3.2 %collective-permute-done.3.refs_2_.refs_7_ = bf16[264,256]{1,0:T(8,128)(2,1)S(1)} collective-permute-done((bf16[264,256]{1,0:T(8,128)(2,1)S(1)}, bf16[264,256]{1,0:T(8,128)(2,1)S(1)}, u32[]{:S(2)}, u32[]{:S(2)}) %collective-permute-start.3) | collective-permute-done | bytes 135200 | tf_op jit(solution)/shard_map/ppermute | solution.py:229
  26.5 0.5 shard_map.118
  27.0 0.0 collective-permute-done.4.refs_6_.refs_8_
  27.0 0.0 collective-permute-done.5.refs_7_.refs_9_
  27.0 0.0 collective-permute-done.6.refs_8_.refs_10_
  27.0 0.0 copy-start.1
  27.0 0.0 copy-start.3
  27.0 0.0 copy-start.4
  27.0 0.0 copy-start.5
  27.1 0.0 copy-start.6
  27.1 0.6 %shard_map.119 = f32[16,1,256]{2,1,0:T(1,128)S(1)} custom-call(bf16[1024,256]{1,0:T(8,128)(2,1)S(1)} %get-tuple-element.29.refs_0_, f32[1,256]{1,0:T(1,128)S(1)} %get-tuple-element.30.refs_1_, f32[1,256]{1,0:T(1,128)S(1)} %get-tuple-element.31.refs_2_, f32[1,256]{1,0:T(1,128)S(1)} %get-tuple-element.32.refs_3_, f32[1,256]{1,0:T(1,128)S(1)} %get-tuple-element.35.refs_4_, ...), custom_call_target="tpu_custom_call" | custom-call | flops 4294967296 | bytes 951296 | tf_op jit(solution)/shard_map/pallas_call | solution.py:234
  27.7 14.5 %all_to_all.10.refs_6_ = f32[16,1,256]{2,1,0:T(1,128)S(1)} all-to-all(f32[16,1,256]{2,1,0:T(1,128)S(1)} %shard_map.119), channel_id=1, replica_groups=mesh['groups'=2,'rows'=4,'feat'=2,'ent'=2] {'rows','feat','ent'}, dimensions={0} | all-to-all | bytes 32768 | tf_op jit(solution)/shard_map/all_to_all | solution.py:350
  42.2 0.0 copy-done.1
  42.2 0.0 copy-done.3
  42.2 0.0 copy-done.4
  42.2 0.0 copy-done.5
  42.2 0.0 copy-done.6
  42.2 1.0 %shard_map.120 = f32[8,1,2304]{2,1,0:T(1,128)S(1)} custom-call(s32[1,1024]{1,0:T(1,128)S(1)} %bitcast.11, s32[1,1024]{1,0:T(1,128)S(1)} %bitcast.13, s32[2,1024]{1,0:T(2,128)S(1)} %get-tuple-element.22.refs_2_, s32[1,1024]{1,0:T(1,128)S(1)} %bitcast.14, s32[1,1024]{1,0:T(1,128)S(1)} %bitcast.15, f32[1,1024]{1,0:T(1,128)S(1)} %psum.7.refs_4_.refs_5_, ...), custom_call_target="tpu_custom_call" | custom-call | flops 67108864 | bytes 4313088 | tf_op jit(solution)/shard_map/pallas_call | solution.py:234
  43.3 8.4 %all_to_all.11.refs_2_ = f32[8,1,2304]{2,1,0:T(1,128)S(1)} all-to-all(f32[8,1,2304]{2,1,0:T(1,128)S(1)} %shard_map.120), channel_id=1, replica_groups=mesh['groups'=2,'rows'=4,'feat'=2,'ent'=2] {'rows','ent'}, dimensions={0} | all-to-all | bytes 147456 | tf_op jit(solution)/shard_map/all_to_all | solution.py:367
  51.7 2.1 %shard_map.121 = (f32[1,2048]{1,0:T(1,128)}, f32[512,256]{1,0:T(8,128)}) custom-call(f32[512,256]{1,0:T(8,128)S(1)} %copy-done.2, f32[1,2048]{1,0:T(1,128)S(1)} %bitcast.9, f32[8,1,2304]{2,1,0:T(1,128)S(1)} %all_to_all.11.refs_2_, bf16[264,256]{1,0:T(8,128)(2,1)S(1)} %collective-permute-done.refs_1_.refs_3_, ...), custom_call_target="tpu_custom_call" | custom-call | flops 1073741824 | bytes 2220032 | tf_op jit(solution)/shard_map/pallas_call | solution.py:234
  (1 shorter events, 0.0 us)
Async XLA Ops:
  2.2 15.3 %collective-permute-start = (bf16[264,256]{1,0:T(8,128)(2,1)S(1)}, bf16[264,256]{1,0:T(8,128)(2,1)S(1)}, u32[]{:S(2)}, u32[]{:S(2)}) collective-permute-start(bf16[264,256]{1,0:T(8,128)(2,1)S(1)} %get-tuple-element.24), channel_id=1, source_target_pairs={{0,8},{1,9},{4,12},{5,13},{8,0},{9,1},{12,4},{13,5},{2,10},{3,11},... | collective-permute-start | bytes 405512 | tf_op jit(solution)/shard_map/ppermute | solution.py:229
  6.3 4.9 %copy-start.7 = (bf16[2048]{0:T(1024)(128)(2,1)S(1)}, bf16[2048]{0:T(1024)(128)(2,1)}, u32[]{:S(2)}) copy-start(bf16[2048]{0:T(1024)(128)(2,1)} %param.11) | copy-start | bytes 12292
  6.3 4.9 %copy-start = (bf16[1024,2048]{1,0:T(8,128)(2,1)S(1)}, bf16[1024,2048]{1,0:T(8,128)(2,1)}, u32[]{:S(2)}) copy-start(bf16[1024,2048]{1,0:T(8,128)(2,1)} %refs_7_.1) | copy-start | bytes 12582916
  7.3 15.3 %copy-start.2 = (f32[512,256]{1,0:T(8,128)S(1)}, f32[512,256]{1,0:T(8,128)}, u32[]{:S(2)}) copy-start(f32[512,256]{1,0:T(8,128)} %refs_0_.3) | copy-start | bytes 1572868
  7.3 10.2 %collective-permute-start.1 = (bf16[264,256]{1,0:T(8,128)(2,1)S(1)}, bf16[264,256]{1,0:T(8,128)(2,1)S(1)}, u32[]{:S(2)}, u32[]{:S(2)}) collective-permute-start(bf16[264,256]{1,0:T(8,128)(2,1)S(1)} %get-tuple-element.27), channel_id=1, source_target_pairs={{0,4},{1,5},{4,8},{5,9},{8,12},{9,13},{12,0},{13,1},{2,6},{3,7},{6... | collective-permute-start | bytes 405512 | tf_op jit(solution)/shard_map/ppermute | solution.py:229
  8.9 14.3 %collective-permute-start.2 = (bf16[264,256]{1,0:T(8,128)(2,1)S(1)}, bf16[264,256]{1,0:T(8,128)(2,1)S(1)}, u32[]{:S(2)}, u32[]{:S(2)}) collective-permute-start(bf16[264,256]{1,0:T(8,128)(2,1)S(1)} %get-tuple-element.33), channel_id=1, source_target_pairs={{0,12},{1,13},{4,0},{5,1},{8,4},{9,5},{12,8},{13,9},{2,14},{3,15},... | collective-permute-start | bytes 405512 | tf_op jit(solution)/shard_map/ppermute | solution.py:229
  11.2 15.3 %collective-permute-start.3 = (bf16[264,256]{1,0:T(8,128)(2,1)S(1)}, bf16[264,256]{1,0:T(8,128)(2,1)S(1)}, u32[]{:S(2)}, u32[]{:S(2)}) collective-permute-start(bf16[264,256]{1,0:T(8,128)(2,1)S(1)} %get-tuple-element.34), channel_id=1, source_target_pairs={{0,9},{1,8},{4,13},{5,12},{8,1},{9,0},{12,5},{13,4},{2,11},{3,10},... | collective-permute-start | bytes 405512 | tf_op jit(solution)/shard_map/ppermute | solution.py:229
  13.6 13.3 %collective-permute-start.4 = (bf16[264,256]{1,0:T(8,128)(2,1)S(1)}, bf16[264,256]{1,0:T(8,128)(2,1)S(1)}, u32[]{:S(2)}, u32[]{:S(2)}) collective-permute-start(bf16[264,256]{1,0:T(8,128)(2,1)S(1)} %get-tuple-element.37), channel_id=1, source_target_pairs={{0,5},{1,4},{4,9},{5,8},{8,13},{9,12},{12,1},{13,0},{2,7},{3,6},{6... | collective-permute-start | bytes 405512 | tf_op jit(solution)/shard_map/ppermute | solution.py:229
  17.5 9.5 %collective-permute-start.5 = (bf16[264,256]{1,0:T(8,128)(2,1)S(1)}, bf16[264,256]{1,0:T(8,128)(2,1)S(1)}, u32[]{:S(2)}, u32[]{:S(2)}) collective-permute-start(bf16[264,256]{1,0:T(8,128)(2,1)S(1)} %get-tuple-element.38), channel_id=1, source_target_pairs={{0,13},{1,12},{4,1},{5,0},{8,5},{9,4},{12,9},{13,8},{2,15},{3,14},... | collective-permute-start | bytes 405512 | tf_op jit(solution)/shard_map/ppermute | solution.py:229
  17.5 9.5 %collective-permute-start.6 = (bf16[264,256]{1,0:T(8,128)(2,1)S(1)}, bf16[264,256]{1,0:T(8,128)(2,1)S(1)}, u32[]{:S(2)}, u32[]{:S(2)}) collective-permute-start(bf16[264,256]{1,0:T(8,128)(2,1)S(1)} %get-tuple-element.39), channel_id=1, source_target_pairs={{0,1},{1,0},{4,5},{5,4},{8,9},{9,8},{12,13},{13,12},{2,3},{3,2},{6... | collective-permute-start | bytes 405512 | tf_op jit(solution)/shard_map/ppermute | solution.py:229
  27.0 15.2 %copy-start.1 = (bf16[1024,2048]{1,0:T(8,128)(2,1)S(1)}, bf16[1024,2048]{1,0:T(8,128)(2,1)}, u32[]{:S(2)}) copy-start(bf16[1024,2048]{1,0:T(8,128)(2,1)} %refs_7_.1) | copy-start | bytes 12582916
  27.0 15.2 %copy-start.3 = (s32[1024,1]{0,1:T(1,128)S(1)}, s32[1024,1]{0,1:T(1,128)}, u32[]{:S(2)}) copy-start(s32[1024,1]{0,1:T(1,128)} %param.14) | copy-start | bytes 12292
  27.0 15.2 %copy-start.4 = (s32[1024,1]{0,1:T(1,128)S(1)}, s32[1024,1]{0,1:T(1,128)}, u32[]{:S(2)}) copy-start(s32[1024,1]{0,1:T(1,128)} %param.16) | copy-start | bytes 12292
  27.0 15.2 %copy-start.5 = (s32[1024]{0:T(1024)S(1)}, s32[1024]{0:T(1024)}, u32[]{:S(2)}) copy-start(s32[1024]{0:T(1024)} %param.18) | copy-start | bytes 12292
  27.1 15.2 %copy-start.6 = (s32[1024]{0:T(1024)S(1)}, s32[1024]{0:T(1024)}, u32[]{:S(2)}) copy-start(s32[1024]{0:T(1024)} %param.19) | copy-start | bytes 12292

commit v25 on v20

--- a/solution.py
+++ b/solution.py
@@ -10,7 +10,7 @@
 F32 = jnp.float32
 BF16 = jnp.bfloat16
 HOME = ("rows", "ent")
-EVERY = ("rows", "feat", "ent")
+EVERY = ("feat", "rows", "ent")
 IDS = 8
 PARAMS = pltpu.CompilerParams(vmem_limit_bytes=24 * 2**20)
 VMEM = pl.BlockSpec(memory_space=pltpu.VMEM)
@@ -164,7 +164,7 @@
     scores = turn_rows(scores, n_rows, n_ent, lax.axis_index("rows"), lax.axis_index("ent"))
     for home in range(len(order)):
         for f in range(n_feat):
-            out[(home // n_ent * n_feat + f) * n_ent + home % n_ent] = scores[home : home + 1]
+            out[f * len(order) + home] = scores[home : home + 1]
 
 
 def home_kernel(
@@ -178,7 +178,7 @@
         table = None
         for f in range(side * n_feat // 2, (side + 1) * n_feat // 2):
             part = jnp.concatenate(
-                [scores[(h // n_ent * n_feat + f) * n_ent + h % n_ent] for h in range(owners)], axis=0
+                [scores[f * owners + h] for h in range(owners)], axis=0
             )
             table = part if table is None else table + part
         found = plain_dot(jnp.concatenate(halves(table), axis=0), spot_of[side])

time: 53.1 us -> 53.1 us (level)
  no operation moved by 1% of the time
where the time goes in v25:
time: 53.1 us; the launch traced here: 52.9 us
  blocking collectives  25.3 us (48%)
  starting transfers between devices  11.8 us (22%)
  Pallas kernels  9.82 us (18%)
  waiting for transfers between devices  5.09 us (10%)
  between operations  0.77 us (1%)
    all_to_all x1, blocking collectives, body(): lax.all_to_all(scores, EVERY, split_axis=0, concat_axis=0, tiled=True)  12 us
    ppermute x7, starting transfers between devices, shift_send(): return lax.ppermute(x, HOME, pairs)  11.8 us
    pallas_call x9, Pallas kernels, call(): pl.pallas_call(kernel, out_shape=out_shape, in_specs=in_specs, out_specs=...  9.82 us
    all_to_all x1, blocking collectives, body(): came = lax.all_to_all(sent, HOME, split_axis=0, concat_axis=0, tiled=True)  8.4 us
    ppermute x7, waiting for transfers between devices, shift_send(): return lax.ppermute(x, HOME, pairs)  5.09 us
    psum x1, blocking collectives, body(): global_total = lax.psum(global_part, 'feat')  4.91 us
  transfers between devices with their start and end apart: 7, of which 2 were waited for; matrix products, arithmetic and copies ran while one was open for 0% of the time, Pallas kernels for 9%

profile of v25, /device:TPU:0, one launch (start us, length us, event | category | flops | bytes accessed | tf_op | source)
XLA Modules:
  0.0 52.9 jit_solution(17657883238146671445)
XLA Ops:
  0.6 1.6 %shard_map.113 = (s32[2,1024]{1,0:T(2,128)S(1)}, s32[1,1024]{1,0:T(1,128)S(1)}, bf16[8,1024]{1,0:T(8,128)(2,1)S(1)}, bf16[1024,256]{1,0:T(8,128)(2,1)S(1)}, bf16[264,256]{1,0:T(8,128)(2,1)S(1)}) custom-call(s32[1,1024]{1,0:T(1,128)} %bitcast.10, s32[1,1024]{1,0:T(1,128)} %bitcast.12, s32[1,1024]{1,0:T(1,128)} %bitcast.16, s32[1,1024]{1,0:T(1,128)} %bitcast.17, ...), custom_call_target="tpu_custom_call" | custom-call | flops 134217728 | bytes 1228800 | tf_op jit(solution)/shard_map/pallas_call | solution.py:234
  2.2 3.1 %collective-permute-start = (bf16[264,256]{1,0:T(8,128)(2,1)S(1)}, bf16[264,256]{1,0:T(8,128)(2,1)S(1)}, u32[]{:S(2)}, u32[]{:S(2)}) collective-permute-start(bf16[264,256]{1,0:T(8,128)(2,1)S(1)} %get-tuple-element.24), channel_id=1, source_target_pairs={{0,4},{1,5},{4,8},{5,9},{8,12},{9,13},{12,0},{13,1},{2,6},{3,7},{6... | collective-permute-start | bytes 405512 | tf_op jit(solution)/shard_map/ppermute | solution.py:229
  5.3 0.0 copy-start.7
  5.3 0.0 copy-start
  5.3 1.0 %shard_map.115 = (bf16[264,256]{1,0:T(8,128)(2,1)S(1)}, bf16[264,256]{1,0:T(8,128)(2,1)S(1)}, bf16[264,256]{1,0:T(8,128)(2,1)S(1)}) custom-call(s32[1,1024]{1,0:T(1,128)S(1)} %get-tuple-element.23.place.refs_0_, bf16[8,1024]{1,0:T(8,128)(2,1)S(1)} %get-tuple-element.25.refs_1_, bf16[1024,256]{1,0:T(8,128)(2,1)S(1)} %get-tuple-element.26.refs_2_), custom_call_target="tpu_custom_call" | custom-call | flops 4294967296 | bytes 950272 | tf_op jit(solution)/shard_map/pallas_call | solution.py:234
  6.3 0.0 copy-start.2
  6.3 2.1 %collective-permute-start.1 = (bf16[264,256]{1,0:T(8,128)(2,1)S(1)}, bf16[264,256]{1,0:T(8,128)(2,1)S(1)}, u32[]{:S(2)}, u32[]{:S(2)}) collective-permute-start(bf16[264,256]{1,0:T(8,128)(2,1)S(1)} %get-tuple-element.27), channel_id=1, source_target_pairs={{0,12},{1,13},{4,0},{5,1},{8,4},{9,5},{12,8},{13,9},{2,14},{3,15},... | collective-permute-start | bytes 405512 | tf_op jit(solution)/shard_map/ppermute | solution.py:229
  8.4 1.0 %collective-permute-start.2 = (bf16[264,256]{1,0:T(8,128)(2,1)S(1)}, bf16[264,256]{1,0:T(8,128)(2,1)S(1)}, u32[]{:S(2)}, u32[]{:S(2)}) collective-permute-start(bf16[264,256]{1,0:T(8,128)(2,1)S(1)} %get-tuple-element.33), channel_id=1, source_target_pairs={{0,8},{1,9},{4,12},{5,13},{8,0},{9,1},{12,4},{13,5},{2,10},{3,11},... | collective-permute-start | bytes 405512 | tf_op jit(solution)/shard_map/ppermute | solution.py:229
  9.4 0.8 %collective-permute-start.3 = (bf16[264,256]{1,0:T(8,128)(2,1)S(1)}, bf16[264,256]{1,0:T(8,128)(2,1)S(1)}, u32[]{:S(2)}, u32[]{:S(2)}) collective-permute-start(bf16[264,256]{1,0:T(8,128)(2,1)S(1)} %get-tuple-element.34), channel_id=1, source_target_pairs={{0,9},{1,8},{4,13},{5,12},{8,1},{9,0},{12,5},{13,4},{2,11},{3,10},... | collective-permute-start | bytes 405512 | tf_op jit(solution)/shard_map/ppermute | solution.py:229
  10.2 0.0 copy-done.7
  10.2 0.0 copy-done
  10.2 1.2 %shard_map.114.refs_3_ = f32[1,1024]{1,0:T(1,128)S(1)} custom-call(s32[1,1024]{1,0:T(1,128)S(1)} %get-tuple-element.23.place.refs_0_, f32[1,2048]{1,0:T(1,128)S(1)} %bitcast.8, bf16[1024,2048]{1,0:T(8,128)(2,1)S(1)} %copy-done), custom_call_target="tpu_custom_call" | custom-call | tf_op jit(solution)/shard_map/pallas_call | solution.py:234
  11.4 1.2 %shard_map.116 = (bf16[264,256]{1,0:T(8,128)(2,1)S(1)}, bf16[264,256]{1,0:T(8,128)(2,1)S(1)}, bf16[264,256]{1,0:T(8,128)(2,1)S(1)}, bf16[264,256]{1,0:T(8,128)(2,1)S(1)}) custom-call(s32[1,1024]{1,0:T(1,128)S(1)} %get-tuple-element.23.place.refs_0_, bf16[8,1024]{1,0:T(8,128)(2,1)S(1)} %get-tuple-element.25.refs_1_, ...), custom_call_target="tpu_custom_call" | custom-call | tf_op jit(solution)/shard_map/pallas_call | solution.py:234
  12.6 0.9 %collective-permute-start.4 = (bf16[264,256]{1,0:T(8,128)(2,1)S(1)}, bf16[264,256]{1,0:T(8,128)(2,1)S(1)}, u32[]{:S(2)}, u32[]{:S(2)}) collective-permute-start(bf16[264,256]{1,0:T(8,128)(2,1)S(1)} %get-tuple-element.37), channel_id=1, source_target_pairs={{0,5},{1,4},{4,9},{5,8},{8,13},{9,12},{12,1},{13,0},{2,7},{3,6},{6... | collective-permute-start | bytes 405512 | tf_op jit(solution)/shard_map/ppermute | solution.py:229
  13.5 0.0 collective-permute-done.refs_1_.refs_3_
  13.5 2.7 %collective-permute-start.5 = (bf16[264,256]{1,0:T(8,128)(2,1)S(1)}, bf16[264,256]{1,0:T(8,128)(2,1)S(1)}, u32[]{:S(2)}, u32[]{:S(2)}) collective-permute-start(bf16[264,256]{1,0:T(8,128)(2,1)S(1)} %get-tuple-element.38), channel_id=1, source_target_pairs={{0,13},{1,12},{4,1},{5,0},{8,5},{9,4},{12,9},{13,8},{2,15},{3,14},... | collective-permute-start | bytes 405512 | tf_op jit(solution)/shard_map/ppermute | solution.py:229
  16.2 0.0 collective-permute-done.1.refs_2_.refs_4_
  16.2 1.2 %collective-permute-start.6 = (bf16[264,256]{1,0:T(8,128)(2,1)S(1)}, bf16[264,256]{1,0:T(8,128)(2,1)S(1)}, u32[]{:S(2)}, u32[]{:S(2)}) collective-permute-start(bf16[264,256]{1,0:T(8,128)(2,1)S(1)} %get-tuple-element.39), channel_id=1, source_target_pairs={{0,1},{1,0},{4,5},{5,4},{8,9},{9,8},{12,13},{13,12},{2,3},{3,2},{6... | collective-permute-start | bytes 405512 | tf_op jit(solution)/shard_map/ppermute | solution.py:229
  17.5 4.9 %psum.7.refs_4_.refs_5_ = f32[1,1024]{1,0:T(1,128)S(1)} all-reduce(f32[1,1024]{1,0:T(1,128)S(1)} %shard_map.114.refs_3_), channel_id=1, replica_groups=mesh['groups'=2,'rows'=4,'feat'=2,'ent'=2] {'feat'}, use_global_device_ids=true, to_apply=%region_0.0 | all-reduce | flops 1024 | bytes 8192 | tf_op jit(solution)/shard_map/psum | solution.py:315
  22.4 0.0 copy-done.2
  22.4 0.6 %shard_map.117 = (bf16[1024,256]{1,0:T(8,128)(2,1)S(1)}, f32[1,256]{1,0:T(1,128)S(1)}, f32[1,256]{1,0:T(1,128)S(1)}, f32[1,256]{1,0:T(1,128)S(1)}) custom-call(f32[512,256]{1,0:T(8,128)S(1)} %copy-done.2, bf16[264,256]{1,0:T(8,128)(2,1)S(1)} %collective-permute-done.refs_1_.refs_3_, bf16[264,256]{1,0:T(8,128)(2,1)S(1)} %collective-permute-done.1.refs_2_.refs_4_, ...), custom_call_target="tpu_custom_call" | custom-call | tf_op jit(solution)/shard_map/pallas_call | solution.py:234
  23.0 2.5 %collective-permute-done.2.refs_1_.refs_6_ = bf16[264,256]{1,0:T(8,128)(2,1)S(1)} collective-permute-done((bf16[264,256]{1,0:T(8,128)(2,1)S(1)}, bf16[264,256]{1,0:T(8,128)(2,1)S(1)}, u32[]{:S(2)}, u32[]{:S(2)}) %collective-permute-start.2) | collective-permute-done | bytes 135200 | tf_op jit(solution)/shard_map/ppermute | solution.py:229
  25.5 2.6 %collective-permute-done.3.refs_2_.refs_7_ = bf16[264,256]{1,0:T(8,128)(2,1)S(1)} collective-permute-done((bf16[264,256]{1,0:T(8,128)(2,1)S(1)}, bf16[264,256]{1,0:T(8,128)(2,1)S(1)}, u32[]{:S(2)}, u32[]{:S(2)}) %collective-permute-start.3) | collective-permute-done | bytes 135200 | tf_op jit(solution)/shard_map/ppermute | solution.py:229
  28.1 0.5 shard_map.118
  28.6 0.0 collective-permute-done.4.refs_6_.refs_8_
  28.6 0.0 collective-permute-done.5.refs_7_.refs_9_
  28.6 0.0 collective-permute-done.6.refs_8_.refs_10_
  28.6 0.0 copy-start.1
  28.6 0.0 copy-start.3
  28.6 0.0 copy-start.4
  28.7 0.0 copy-start.5
  28.7 0.0 copy-start.6
  28.7 0.6 %shard_map.119 = f32[16,1,256]{2,1,0:T(1,128)S(1)} custom-call(bf16[1024,256]{1,0:T(8,128)(2,1)S(1)} %get-tuple-element.29.refs_0_, f32[1,256]{1,0:T(1,128)S(1)} %get-tuple-element.30.refs_1_, f32[1,256]{1,0:T(1,128)S(1)} %get-tuple-element.31.refs_2_, f32[1,256]{1,0:T(1,128)S(1)} %get-tuple-element.32.refs_3_, f32[1,256]{1,0:T(1,128)S(1)} %get-tuple-element.35.refs_4_, ...), custom_call_target="tpu_custom_call" | custom-call | flops 4294967296 | bytes 951296 | tf_op jit(solution)/shard_map/pallas_call | solution.py:234
  29.3 12.0 %all_to_all.10.refs_6_ = f32[16,1,256]{2,1,0:T(1,128)S(1)} all-to-all(f32[16,1,256]{2,1,0:T(1,128)S(1)} %shard_map.119), channel_id=1, replica_groups=mesh['groups'=2,'rows'=4,'feat'=2,'ent'=2] {'feat','rows','ent'}, dimensions={0} | all-to-all | bytes 32768 | tf_op jit(solution)/shard_map/all_to_all | solution.py:349
  41.3 0.0 copy-done.1
  41.3 0.0 copy-done.3
  41.3 0.0 copy-done.4
  41.4 0.0 copy-done.5
  41.4 0.0 copy-done.6
  41.4 1.0 %shard_map.120 = f32[8,1,2304]{2,1,0:T(1,128)S(1)} custom-call(s32[1,1024]{1,0:T(1,128)S(1)} %bitcast.11, s32[1,1024]{1,0:T(1,128)S(1)} %bitcast.13, s32[2,1024]{1,0:T(2,128)S(1)} %get-tuple-element.22.refs_2_, s32[1,1024]{1,0:T(1,128)S(1)} %bitcast.14, s32[1,1024]{1,0:T(1,128)S(1)} %bitcast.15, f32[1,1024]{1,0:T(1,128)S(1)} %psum.7.refs_4_.refs_5_, ...), custom_call_target="tpu_custom_call" | custom-call | flops 67108864 | bytes 4313088 | tf_op jit(solution)/shard_map/pallas_call | solution.py:234
  42.4 8.4 %all_to_all.11.refs_2_ = f32[8,1,2304]{2,1,0:T(1,128)S(1)} all-to-all(f32[8,1,2304]{2,1,0:T(1,128)S(1)} %shard_map.120), channel_id=1, replica_groups=mesh['groups'=2,'rows'=4,'feat'=2,'ent'=2] {'rows','ent'}, dimensions={0} | all-to-all | bytes 147456 | tf_op jit(solution)/shard_map/all_to_all | solution.py:366
  50.8 2.1 %shard_map.121 = (f32[1,2048]{1,0:T(1,128)}, f32[512,256]{1,0:T(8,128)}) custom-call(f32[512,256]{1,0:T(8,128)S(1)} %copy-done.2, f32[1,2048]{1,0:T(1,128)S(1)} %bitcast.9, f32[8,1,2304]{2,1,0:T(1,128)S(1)} %all_to_all.11.refs_2_, bf16[264,256]{1,0:T(8,128)(2,1)S(1)} %collective-permute-done.refs_1_.refs_3_, ...), custom_call_target="tpu_custom_call" | custom-call | flops 1073741824 | bytes 2220032 | tf_op jit(solution)/shard_map/pallas_call | solution.py:234
  (1 shorter events, 0.0 us)
Async XLA Ops:
  2.2 11.3 %collective-permute-start = (bf16[264,256]{1,0:T(8,128)(2,1)S(1)}, bf16[264,256]{1,0:T(8,128)(2,1)S(1)}, u32[]{:S(2)}, u32[]{:S(2)}) collective-permute-start(bf16[264,256]{1,0:T(8,128)(2,1)S(1)} %get-tuple-element.24), channel_id=1, source_target_pairs={{0,4},{1,5},{4,8},{5,9},{8,12},{9,13},{12,0},{13,1},{2,6},{3,7},{6... | collective-permute-start | bytes 405512 | tf_op jit(solution)/shard_map/ppermute | solution.py:229
  5.3 4.9 %copy-start.7 = (bf16[2048]{0:T(1024)(128)(2,1)S(1)}, bf16[2048]{0:T(1024)(128)(2,1)}, u32[]{:S(2)}) copy-start(bf16[2048]{0:T(1024)(128)(2,1)} %param.11) | copy-start | bytes 12292
  5.3 4.9 %copy-start = (bf16[1024,2048]{1,0:T(8,128)(2,1)S(1)}, bf16[1024,2048]{1,0:T(8,128)(2,1)}, u32[]{:S(2)}) copy-start(bf16[1024,2048]{1,0:T(8,128)(2,1)} %refs_7_.1) | copy-start | bytes 12582916
  6.3 16.1 %copy-start.2 = (f32[512,256]{1,0:T(8,128)S(1)}, f32[512,256]{1,0:T(8,128)}, u32[]{:S(2)}) copy-start(f32[512,256]{1,0:T(8,128)} %refs_0_.3) | copy-start | bytes 1572868
  6.3 10.0 %collective-permute-start.1 = (bf16[264,256]{1,0:T(8,128)(2,1)S(1)}, bf16[264,256]{1,0:T(8,128)(2,1)S(1)}, u32[]{:S(2)}, u32[]{:S(2)}) collective-permute-start(bf16[264,256]{1,0:T(8,128)(2,1)S(1)} %get-tuple-element.27), channel_id=1, source_target_pairs={{0,12},{1,13},{4,0},{5,1},{8,4},{9,5},{12,8},{13,9},{2,14},{3,15},... | collective-permute-start | bytes 405512 | tf_op jit(solution)/shard_map/ppermute | solution.py:229
  8.4 17.2 %collective-permute-start.2 = (bf16[264,256]{1,0:T(8,128)(2,1)S(1)}, bf16[264,256]{1,0:T(8,128)(2,1)S(1)}, u32[]{:S(2)}, u32[]{:S(2)}) collective-permute-start(bf16[264,256]{1,0:T(8,128)(2,1)S(1)} %get-tuple-element.33), channel_id=1, source_target_pairs={{0,8},{1,9},{4,12},{5,13},{8,0},{9,1},{12,4},{13,5},{2,10},{3,11},... | collective-permute-start | bytes 405512 | tf_op jit(solution)/shard_map/ppermute | solution.py:229
  9.4 18.7 %collective-permute-start.3 = (bf16[264,256]{1,0:T(8,128)(2,1)S(1)}, bf16[264,256]{1,0:T(8,128)(2,1)S(1)}, u32[]{:S(2)}, u32[]{:S(2)}) collective-permute-start(bf16[264,256]{1,0:T(8,128)(2,1)S(1)} %get-tuple-element.34), channel_id=1, source_target_pairs={{0,9},{1,8},{4,13},{5,12},{8,1},{9,0},{12,5},{13,4},{2,11},{3,10},... | collective-permute-start | bytes 405512 | tf_op jit(solution)/shard_map/ppermute | solution.py:229
  12.6 16.0 %collective-permute-start.4 = (bf16[264,256]{1,0:T(8,128)(2,1)S(1)}, bf16[264,256]{1,0:T(8,128)(2,1)S(1)}, u32[]{:S(2)}, u32[]{:S(2)}) collective-permute-start(bf16[264,256]{1,0:T(8,128)(2,1)S(1)} %get-tuple-element.37), channel_id=1, source_target_pairs={{0,5},{1,4},{4,9},{5,8},{8,13},{9,12},{12,1},{13,0},{2,7},{3,6},{6... | collective-permute-start | bytes 405512 | tf_op jit(solution)/shard_map/ppermute | solution.py:229
  13.5 15.1 %collective-permute-start.5 = (bf16[264,256]{1,0:T(8,128)(2,1)S(1)}, bf16[264,256]{1,0:T(8,128)(2,1)S(1)}, u32[]{:S(2)}, u32[]{:S(2)}) collective-permute-start(bf16[264,256]{1,0:T(8,128)(2,1)S(1)} %get-tuple-element.38), channel_id=1, source_target_pairs={{0,13},{1,12},{4,1},{5,0},{8,5},{9,4},{12,9},{13,8},{2,15},{3,14},... | collective-permute-start | bytes 405512 | tf_op jit(solution)/shard_map/ppermute | solution.py:229
  16.2 12.4 %collective-permute-start.6 = (bf16[264,256]{1,0:T(8,128)(2,1)S(1)}, bf16[264,256]{1,0:T(8,128)(2,1)S(1)}, u32[]{:S(2)}, u32[]{:S(2)}) collective-permute-start(bf16[264,256]{1,0:T(8,128)(2,1)S(1)} %get-tuple-element.39), channel_id=1, source_target_pairs={{0,1},{1,0},{4,5},{5,4},{8,9},{9,8},{12,13},{13,12},{2,3},{3,2},{6... | collective-permute-start | bytes 405512 | tf_op jit(solution)/shard_map/ppermute | solution.py:229
  28.6 12.7 %copy-start.1 = (bf16[1024,2048]{1,0:T(8,128)(2,1)S(1)}, bf16[1024,2048]{1,0:T(8,128)(2,1)}, u32[]{:S(2)}) copy-start(bf16[1024,2048]{1,0:T(8,128)(2,1)} %refs_7_.1) | copy-start | bytes 12582916
  28.6 12.7 %copy-start.3 = (s32[1024,1]{0,1:T(1,128)S(1)}, s32[1024,1]{0,1:T(1,128)}, u32[]{:S(2)}) copy-start(s32[1024,1]{0,1:T(1,128)} %param.14) | copy-start | bytes 12292
  28.6 12.7 %copy-start.4 = (s32[1024,1]{0,1:T(1,128)S(1)}, s32[1024,1]{0,1:T(1,128)}, u32[]{:S(2)}) copy-start(s32[1024,1]{0,1:T(1,128)} %param.16) | copy-start | bytes 12292
  28.7 12.7 %copy-start.5 = (s32[1024]{0:T(1024)S(1)}, s32[1024]{0:T(1024)}, u32[]{:S(2)}) copy-start(s32[1024]{0:T(1024)} %param.18) | copy-start | bytes 12292
  28.7 12.7 %copy-start.6 = (s32[1024]{0:T(1024)S(1)}, s32[1024]{0:T(1024)}, u32[]{:S(2)}) copy-start(s32[1024]{0:T(1024)} %param.19) | copy-start | bytes 12292

commit v26 on v20

--- a/solution.py
+++ b/solution.py
@@ -273,9 +273,9 @@
     away = [up * n_ent for half in range(1, middle) for up in (half, n_rows - half)]
     away += [middle * n_ent + c for c in range(n_ent)]
     away += [up * n_ent + c for c in range(1, n_ent) for half in range(1, middle) for up in (half, n_rows - half)]
-    first, second, near = away[:1], away[1:-2], [*away[-2:], *reversed(range(n_ent))]
+    first, second, near = away[:2], away[2:-2], [*away[-2:], *reversed(range(n_ent))]
     chunk = shape(capacity + IDS, width, dtype=BF16)
-    flops = len(first) * 2 * capacity * rows_here * width
+    flops = 2 * capacity * rows_here * width
 
     def in_hbm(x):
         return pltpu.with_memory_space_constraint(x, pltpu.HBM)

time: 53.1 us -> 53.2 us (level)
  transfers between devices with their start and end apart: 7 -> 7, of which waited for: 2 -> 2; matrix products, arithmetic and copies ran while one was open for 0% -> 0% of each run, Pallas kernels for 9% -> 8%
where the time goes in v26:
time: 53.2 us; the launch traced here: 52.9 us
  blocking collectives  25 us (47%)
  starting transfers between devices  11.9 us (22%)
  Pallas kernels  9.83 us (18%)
  waiting for transfers between devices  5.39 us (10%)
  between operations  0.77 us (1%)
    ppermute x7, starting transfers between devices, shift_send(): return lax.ppermute(x, HOME, pairs)  11.9 us
    all_to_all x1, blocking collectives, body(): lax.all_to_all(scores, EVERY, split_axis=0, concat_axis=0, tiled=True)  11.7 us
    pallas_call x9, Pallas kernels, call(): pl.pallas_call(kernel, out_shape=out_shape, in_specs=in_specs, out_specs=...  9.83 us
    all_to_all x1, blocking collectives, body(): came = lax.all_to_all(sent, HOME, split_axis=0, concat_axis=0, tiled=True)  8.4 us
    ppermute x7, waiting for transfers between devices, shift_send(): return lax.ppermute(x, HOME, pairs)  5.39 us
    psum x1, blocking collectives, body(): global_total = lax.psum(global_part, 'feat')  4.91 us
  transfers between devices with their start and end apart: 7, of which 2 were waited for; matrix products, arithmetic and copies ran while one was open for 0% of the time, Pallas kernels for 8%

profile of v26, /device:TPU:0, one launch (start us, length us, event | category | flops | bytes accessed | tf_op | source)
XLA Modules:
  0.0 52.9 jit_solution(5905007625510660426)
XLA Ops:
  0.6 1.8 %shard_map.113 = (s32[2,1024]{1,0:T(2,128)S(1)}, s32[1,1024]{1,0:T(1,128)S(1)}, bf16[8,1024]{1,0:T(8,128)(2,1)S(1)}, bf16[1024,256]{1,0:T(8,128)(2,1)S(1)}, bf16...) custom-call(s32[1,1024]{1,0:T(1,128)} %bitcast.10, s32[1,1024]{1,0:T(1,128)} %bitcast.12, s32[1,1024]{1,0:T(1,128)} %bitcast.16, ...), custom_call_target="tpu_custom_call" | custom-call | flops 134217728 | bytes 1363968 | tf_op jit(solution)/shard_map/pallas_call | solution.py:234
  2.5 3.1 %collective-permute-start = (bf16[264,256]{1,0:T(8,128)(2,1)S(1)}, bf16[264,256]{1,0:T(8,128)(2,1)S(1)}, u32[]{:S(2)}, u32[]{:S(2)}) collective-permute-start(bf16[264,256]{1,0:T(8,128)(2,1)S(1)} %get-tuple-element.24), channel_id=1, source_target_pairs={{0,4},{1,5},{4,8},{5,9},{8,12},{9,13},{12,0},{13,1},{2,6},{3,7},{6... | collective-permute-start | bytes 405512 | tf_op jit(solution)/shard_map/ppermute | solution.py:229
  5.6 2.1 %collective-permute-start.1 = (bf16[264,256]{1,0:T(8,128)(2,1)S(1)}, bf16[264,256]{1,0:T(8,128)(2,1)S(1)}, u32[]{:S(2)}, u32[]{:S(2)}) collective-permute-start(bf16[264,256]{1,0:T(8,128)(2,1)S(1)} %get-tuple-element.25), channel_id=1, source_target_pairs={{0,12},{1,13},{4,0},{5,1},{8,4},{9,5},{12,8},{13,9},{2,14},{3,15},... | collective-permute-start | bytes 405512 | tf_op jit(solution)/shard_map/ppermute | solution.py:229
  7.7 0.0 copy-start.7
  7.7 0.0 copy-start
  7.7 0.7 %shard_map.117 = (bf16[264,256]{1,0:T(8,128)(2,1)S(1)}, bf16[264,256]{1,0:T(8,128)(2,1)S(1)}) custom-call(s32[1,1024]{1,0:T(1,128)S(1)} %get-tuple-element.23.place.refs_0_, bf16[8,1024]{1,0:T(8,128)(2,1)S(1)} %get-tuple-element.26.refs_1_, bf16[1024,256]{1,0:T(8,128)(2,1)S(1)} %get-tuple-element.27.refs_2_), custom_call_target="tpu_custom_call" | custom-call | flops 4294967296 | bytes 815104 | tf_op jit(solution)/shard_map/pallas_call | solution.py:234
  8.3 0.0 copy-start.2
  8.4 1.0 %collective-permute-start.2 = (bf16[264,256]{1,0:T(8,128)(2,1)S(1)}, bf16[264,256]{1,0:T(8,128)(2,1)S(1)}, u32[]{:S(2)}, u32[]{:S(2)}) collective-permute-start(bf16[264,256]{1,0:T(8,128)(2,1)S(1)} %get-tuple-element.33), channel_id=1, source_target_pairs={{0,8},{1,9},{4,12},{5,13},{8,0},{9,1},{12,4},{13,5},{2,10},{3,11},... | collective-permute-start | bytes 405512 | tf_op jit(solution)/shard_map/ppermute | solution.py:229
  9.4 0.9 %collective-permute-start.3 = (bf16[264,256]{1,0:T(8,128)(2,1)S(1)}, bf16[264,256]{1,0:T(8,128)(2,1)S(1)}, u32[]{:S(2)}, u32[]{:S(2)}) collective-permute-start(bf16[264,256]{1,0:T(8,128)(2,1)S(1)} %get-tuple-element.34), channel_id=1, source_target_pairs={{0,9},{1,8},{4,13},{5,12},{8,1},{9,0},{12,5},{13,4},{2,11},{3,10},... | collective-permute-start | bytes 405512 | tf_op jit(solution)/shard_map/ppermute | solution.py:229
  10.2 0.0 copy-done.7
  10.2 0.0 copy-done
  10.2 1.2 %shard_map.114.refs_3_ = f32[1,1024]{1,0:T(1,128)S(1)} custom-call(s32[1,1024]{1,0:T(1,128)S(1)} %get-tuple-element.23.place.refs_0_, f32[1,2048]{1,0:T(1,128)S(1)} %bitcast.8, bf16[1024,2048]{1,0:T(8,128)(2,1)S(1)} %copy-done), custom_call_target="tpu_custom_call" | custom-call | tf_op jit(solution)/shard_map/pallas_call | solution.py:234
  11.4 1.2 %shard_map.115 = (bf16[264,256]{1,0:T(8,128)(2,1)S(1)}, bf16[264,256]{1,0:T(8,128)(2,1)S(1)}, bf16[264,256]{1,0:T(8,128)(2,1)S(1)}, bf16[264,256]{1,0:T(8,128)(2,1)S(1)}) custom-call(s32[1,1024]{1,0:T(1,128)S(1)} %get-tuple-element.23.place.refs_0_, bf16[8,1024]{1,0:T(8,128)(2,1)S(1)} %get-tuple-element.26.refs_1_, ...), custom_call_target="tpu_custom_call" | custom-call | tf_op jit(solution)/shard_map/pallas_call | solution.py:234
  12.7 0.8 %collective-permute-start.4 = (bf16[264,256]{1,0:T(8,128)(2,1)S(1)}, bf16[264,256]{1,0:T(8,128)(2,1)S(1)}, u32[]{:S(2)}, u32[]{:S(2)}) collective-permute-start(bf16[264,256]{1,0:T(8,128)(2,1)S(1)} %get-tuple-element.37), channel_id=1, source_target_pairs={{0,5},{1,4},{4,9},{5,8},{8,13},{9,12},{12,1},{13,0},{2,7},{3,6},{6... | collective-permute-start | bytes 405512 | tf_op jit(solution)/shard_map/ppermute | solution.py:229
  13.5 0.0 collective-permute-done.refs_1_.refs_3_
  13.5 2.8 %collective-permute-start.5 = (bf16[264,256]{1,0:T(8,128)(2,1)S(1)}, bf16[264,256]{1,0:T(8,128)(2,1)S(1)}, u32[]{:S(2)}, u32[]{:S(2)}) collective-permute-start(bf16[264,256]{1,0:T(8,128)(2,1)S(1)} %get-tuple-element.38), channel_id=1, source_target_pairs={{0,13},{1,12},{4,1},{5,0},{8,5},{9,4},{12,9},{13,8},{2,15},{3,14},... | collective-permute-start | bytes 405512 | tf_op jit(solution)/shard_map/ppermute | solution.py:229
  16.3 0.0 collective-permute-done.1.refs_2_.refs_4_
  16.3 1.2 %collective-permute-start.6 = (bf16[264,256]{1,0:T(8,128)(2,1)S(1)}, bf16[264,256]{1,0:T(8,128)(2,1)S(1)}, u32[]{:S(2)}, u32[]{:S(2)}) collective-permute-start(bf16[264,256]{1,0:T(8,128)(2,1)S(1)} %get-tuple-element.39), channel_id=1, source_target_pairs={{0,1},{1,0},{4,5},{5,4},{8,9},{9,8},{12,13},{13,12},{2,3},{3,2},{6... | collective-permute-start | bytes 405512 | tf_op jit(solution)/shard_map/ppermute | solution.py:229
  17.5 4.9 %psum.7.refs_4_.refs_5_ = f32[1,1024]{1,0:T(1,128)S(1)} all-reduce(f32[1,1024]{1,0:T(1,128)S(1)} %shard_map.114.refs_3_), channel_id=1, replica_groups=mesh['groups'=2,'rows'=4,'feat'=2,'ent'=2] {'feat'}, use_global_device_ids=true, to_apply=%region_0.0 | all-reduce | flops 1024 | bytes 8192 | tf_op jit(solution)/shard_map/psum | solution.py:315
  22.4 0.0 copy-done.2
  22.4 0.6 %shard_map.116 = (bf16[1024,256]{1,0:T(8,128)(2,1)S(1)}, f32[1,256]{1,0:T(1,128)S(1)}, f32[1,256]{1,0:T(1,128)S(1)}, f32[1,256]{1,0:T(1,128)S(1)}) custom-call(f32[512,256]{1,0:T(8,128)S(1)} %copy-done.2, bf16[264,256]{1,0:T(8,128)(2,1)S(1)} %collective-permute-done.refs_1_.refs_3_, bf16[264,256]{1,0:T(8,128)(2,1)S(1)} %collective-permute-done.1.refs_2_.refs_4_, ...), custom_call_target="tpu_custom_call" | custom-call | tf_op jit(solution)/shard_map/pallas_call | solution.py:234
  23.1 2.7 %collective-permute-done.2.refs_1_.refs_6_ = bf16[264,256]{1,0:T(8,128)(2,1)S(1)} collective-permute-done((bf16[264,256]{1,0:T(8,128)(2,1)S(1)}, bf16[264,256]{1,0:T(8,128)(2,1)S(1)}, u32[]{:S(2)}, u32[]{:S(2)}) %collective-permute-start.2) | collective-permute-done | bytes 135200 | tf_op jit(solution)/shard_map/ppermute | solution.py:229
  25.7 2.7 %collective-permute-done.3.refs_2_.refs_7_ = bf16[264,256]{1,0:T(8,128)(2,1)S(1)} collective-permute-done((bf16[264,256]{1,0:T(8,128)(2,1)S(1)}, bf16[264,256]{1,0:T(8,128)(2,1)S(1)}, u32[]{:S(2)}, u32[]{:S(2)}) %collective-permute-start.3) | collective-permute-done | bytes 135200 | tf_op jit(solution)/shard_map/ppermute | solution.py:229
  28.5 0.5 shard_map.118
  28.9 0.0 collective-permute-done.4.refs_6_.refs_8_
  28.9 0.0 collective-permute-done.5.refs_7_.refs_9_
  29.0 0.0 collective-permute-done.6.refs_8_.refs_10_
  29.0 0.0 copy-start.1
  29.0 0.0 copy-start.3
  29.0 0.0 copy-start.4
  29.0 0.0 copy-start.5
  29.0 0.0 copy-start.6
  29.0 0.7 %shard_map.119 = f32[16,1,256]{2,1,0:T(1,128)S(1)} custom-call(bf16[1024,256]{1,0:T(8,128)(2,1)S(1)} %get-tuple-element.29.refs_0_, f32[1,256]{1,0:T(1,128)S(1)} %get-tuple-element.30.refs_1_, f32[1,256]{1,0:T(1,128)S(1)} %get-tuple-element.31.refs_2_, f32[1,256]{1,0:T(1,128)S(1)} %get-tuple-element.32.refs_3_, f32[1,256]{1,0:T(1,128)S(1)} %get-tuple-element.35.refs_4_, ...), custom_call_target="tpu_custom_call" | custom-call | flops 4294967296 | bytes 951296 | tf_op jit(solution)/shard_map/pallas_call | solution.py:234
  29.7 11.7 %all_to_all.10.refs_6_ = f32[16,1,256]{2,1,0:T(1,128)S(1)} all-to-all(f32[16,1,256]{2,1,0:T(1,128)S(1)} %shard_map.119), channel_id=1, replica_groups=mesh['groups'=2,'rows'=4,'feat'=2,'ent'=2] {'rows','feat','ent'}, dimensions={0} | all-to-all | bytes 32768 | tf_op jit(solution)/shard_map/all_to_all | solution.py:349
  41.4 0.0 copy-done.1
  41.4 0.0 copy-done.3
  41.4 0.0 copy-done.4
  41.4 0.0 copy-done.5
  41.4 0.0 copy-done.6
  41.4 1.0 %shard_map.120 = f32[8,1,2304]{2,1,0:T(1,128)S(1)} custom-call(s32[1,1024]{1,0:T(1,128)S(1)} %bitcast.11, s32[1,1024]{1,0:T(1,128)S(1)} %bitcast.13, s32[2,1024]{1,0:T(2,128)S(1)} %get-tuple-element.22.refs_2_, s32[1,1024]{1,0:T(1,128)S(1)} %bitcast.14, s32[1,1024]{1,0:T(1,128)S(1)} %bitcast.15, f32[1,1024]{1,0:T(1,128)S(1)} %psum.7.refs_4_.refs_5_, ...), custom_call_target="tpu_custom_call" | custom-call | flops 67108864 | bytes 4313088 | tf_op jit(solution)/shard_map/pallas_call | solution.py:234
  42.5 8.4 %all_to_all.11.refs_2_ = f32[8,1,2304]{2,1,0:T(1,128)S(1)} all-to-all(f32[8,1,2304]{2,1,0:T(1,128)S(1)} %shard_map.120), channel_id=1, replica_groups=mesh['groups'=2,'rows'=4,'feat'=2,'ent'=2] {'rows','ent'}, dimensions={0} | all-to-all | bytes 147456 | tf_op jit(solution)/shard_map/all_to_all | solution.py:366
  50.9 2.1 %shard_map.121 = (f32[1,2048]{1,0:T(1,128)}, f32[512,256]{1,0:T(8,128)}) custom-call(f32[512,256]{1,0:T(8,128)S(1)} %copy-done.2, f32[1,2048]{1,0:T(1,128)S(1)} %bitcast.9, f32[8,1,2304]{2,1,0:T(1,128)S(1)} %all_to_all.11.refs_2_, bf16[264,256]{1,0:T(8,128)(2,1)S(1)} %collective-permute-done.refs_1_.refs_3_, ...), custom_call_target="tpu_custom_call" | custom-call | flops 1073741824 | bytes 2220032 | tf_op jit(solution)/shard_map/pallas_call | solution.py:234
  (1 shorter events, 0.0 us)
Async XLA Ops:
  2.5 11.0 %collective-permute-start = (bf16[264,256]{1,0:T(8,128)(2,1)S(1)}, bf16[264,256]{1,0:T(8,128)(2,1)S(1)}, u32[]{:S(2)}, u32[]{:S(2)}) collective-permute-start(bf16[264,256]{1,0:T(8,128)(2,1)S(1)} %get-tuple-element.24), channel_id=1, source_target_pairs={{0,4},{1,5},{4,8},{5,9},{8,12},{9,13},{12,0},{13,1},{2,6},{3,7},{6... | collective-permute-start | bytes 405512 | tf_op jit(solution)/shard_map/ppermute | solution.py:229
  5.6 10.7 %collective-permute-start.1 = (bf16[264,256]{1,0:T(8,128)(2,1)S(1)}, bf16[264,256]{1,0:T(8,128)(2,1)S(1)}, u32[]{:S(2)}, u32[]{:S(2)}) collective-permute-start(bf16[264,256]{1,0:T(8,128)(2,1)S(1)} %get-tuple-element.25), channel_id=1, source_target_pairs={{0,12},{1,13},{4,0},{5,1},{8,4},{9,5},{12,8},{13,9},{2,14},{3,15},... | collective-permute-start | bytes 405512 | tf_op jit(solution)/shard_map/ppermute | solution.py:229
  7.7 2.6 %copy-start.7 = (bf16[2048]{0:T(1024)(128)(2,1)S(1)}, bf16[2048]{0:T(1024)(128)(2,1)}, u32[]{:S(2)}) copy-start(bf16[2048]{0:T(1024)(128)(2,1)} %param.11) | copy-start | bytes 12292
  7.7 2.6 %copy-start = (bf16[1024,2048]{1,0:T(8,128)(2,1)S(1)}, bf16[1024,2048]{1,0:T(8,128)(2,1)}, u32[]{:S(2)}) copy-start(bf16[1024,2048]{1,0:T(8,128)(2,1)} %refs_7_.1) | copy-start | bytes 12582916
  8.3 14.1 %copy-start.2 = (f32[512,256]{1,0:T(8,128)S(1)}, f32[512,256]{1,0:T(8,128)}, u32[]{:S(2)}) copy-start(f32[512,256]{1,0:T(8,128)} %refs_0_.3) | copy-start | bytes 1572868
  8.4 17.4 %collective-permute-start.2 = (bf16[264,256]{1,0:T(8,128)(2,1)S(1)}, bf16[264,256]{1,0:T(8,128)(2,1)S(1)}, u32[]{:S(2)}, u32[]{:S(2)}) collective-permute-start(bf16[264,256]{1,0:T(8,128)(2,1)S(1)} %get-tuple-element.33), channel_id=1, source_target_pairs={{0,8},{1,9},{4,12},{5,13},{8,0},{9,1},{12,4},{13,5},{2,10},{3,11},... | collective-permute-start | bytes 405512 | tf_op jit(solution)/shard_map/ppermute | solution.py:229
  9.4 19.1 %collective-permute-start.3 = (bf16[264,256]{1,0:T(8,128)(2,1)S(1)}, bf16[264,256]{1,0:T(8,128)(2,1)S(1)}, u32[]{:S(2)}, u32[]{:S(2)}) collective-permute-start(bf16[264,256]{1,0:T(8,128)(2,1)S(1)} %get-tuple-element.34), channel_id=1, source_target_pairs={{0,9},{1,8},{4,13},{5,12},{8,1},{9,0},{12,5},{13,4},{2,11},{3,10},... | collective-permute-start | bytes 405512 | tf_op jit(solution)/shard_map/ppermute | solution.py:229
  12.7 16.3 %collective-permute-start.4 = (bf16[264,256]{1,0:T(8,128)(2,1)S(1)}, bf16[264,256]{1,0:T(8,128)(2,1)S(1)}, u32[]{:S(2)}, u32[]{:S(2)}) collective-permute-start(bf16[264,256]{1,0:T(8,128)(2,1)S(1)} %get-tuple-element.37), channel_id=1, source_target_pairs={{0,5},{1,4},{4,9},{5,8},{8,13},{9,12},{12,1},{13,0},{2,7},{3,6},{6... | collective-permute-start | bytes 405512 | tf_op jit(solution)/shard_map/ppermute | solution.py:229
  13.5 15.4 %collective-permute-start.5 = (bf16[264,256]{1,0:T(8,128)(2,1)S(1)}, bf16[264,256]{1,0:T(8,128)(2,1)S(1)}, u32[]{:S(2)}, u32[]{:S(2)}) collective-permute-start(bf16[264,256]{1,0:T(8,128)(2,1)S(1)} %get-tuple-element.38), channel_id=1, source_target_pairs={{0,13},{1,12},{4,1},{5,0},{8,5},{9,4},{12,9},{13,8},{2,15},{3,14},... | collective-permute-start | bytes 405512 | tf_op jit(solution)/shard_map/ppermute | solution.py:229
  16.3 12.7 %collective-permute-start.6 = (bf16[264,256]{1,0:T(8,128)(2,1)S(1)}, bf16[264,256]{1,0:T(8,128)(2,1)S(1)}, u32[]{:S(2)}, u32[]{:S(2)}) collective-permute-start(bf16[264,256]{1,0:T(8,128)(2,1)S(1)} %get-tuple-element.39), channel_id=1, source_target_pairs={{0,1},{1,0},{4,5},{5,4},{8,9},{9,8},{12,13},{13,12},{2,3},{3,2},{6... | collective-permute-start | bytes 405512 | tf_op jit(solution)/shard_map/ppermute | solution.py:229
  29.0 12.4 %copy-start.1 = (bf16[1024,2048]{1,0:T(8,128)(2,1)S(1)}, bf16[1024,2048]{1,0:T(8,128)(2,1)}, u32[]{:S(2)}) copy-start(bf16[1024,2048]{1,0:T(8,128)(2,1)} %refs_7_.1) | copy-start | bytes 12582916
  29.0 12.4 %copy-start.3 = (s32[1024,1]{0,1:T(1,128)S(1)}, s32[1024,1]{0,1:T(1,128)}, u32[]{:S(2)}) copy-start(s32[1024,1]{0,1:T(1,128)} %param.14) | copy-start | bytes 12292
  29.0 12.4 %copy-start.4 = (s32[1024,1]{0,1:T(1,128)S(1)}, s32[1024,1]{0,1:T(1,128)}, u32[]{:S(2)}) copy-start(s32[1024,1]{0,1:T(1,128)} %param.16) | copy-start | bytes 12292
  29.0 12.4 %copy-start.5 = (s32[1024]{0:T(1024)S(1)}, s32[1024]{0:T(1024)}, u32[]{:S(2)}) copy-start(s32[1024]{0:T(1024)} %param.18) | copy-start | bytes 12292
  29.0 12.4 %copy-start.6 = (s32[1024]{0:T(1024)S(1)}, s32[1024]{0:T(1024)}, u32[]{:S(2)}) copy-start(s32[1024]{0:T(1024)} %param.19) | copy-start | bytes 12292

commit v27 on v20

--- a/solution.py
+++ b/solution.py
@@ -272,7 +272,7 @@
     middle = n_rows // 2
     away = [up * n_ent for half in range(1, middle) for up in (half, n_rows - half)]
     away += [middle * n_ent + c for c in range(n_ent)]
-    away += [up * n_ent + c for c in range(1, n_ent) for half in range(1, middle) for up in (half, n_rows - half)]
+    away += [up * n_ent + c for c in range(1, n_ent) for half in range(1, middle) for up in (n_rows - half, half)]
     first, second, near = away[:1], away[1:-2], [*away[-2:], *reversed(range(n_ent))]
     chunk = shape(capacity + IDS, width, dtype=BF16)
     flops = len(first) * 2 * capacity * rows_here * width

time: 53.1 us -> 53.2 us (level)
  starting transfers between devices: 11.8 us -> 10 us
  waiting for transfers between devices: 5.09 us -> 6.89 us
    ppermute x7, starting transfers between devices: 11.8 us -> 10 us  [shift_send(): return lax.ppermute(x, HOME, pairs)]
    ppermute x7, waiting for transfers between devices: 5.09 us -> 6.89 us  [shift_send(): return lax.ppermute(x, HOME, pairs)]
where the time goes in v27:
time: 53.2 us; the launch traced here: 52.9 us
  blocking collectives  25.3 us (48%)
  starting transfers between devices  10 us (19%)
  Pallas kernels  9.82 us (18%)
  waiting for transfers between devices  6.89 us (13%)
  between operations  0.78 us (1%)
    all_to_all x1, blocking collectives, body(): lax.all_to_all(scores, EVERY, split_axis=0, concat_axis=0, tiled=True)  12 us
    ppermute x7, starting transfers between devices, shift_send(): return lax.ppermute(x, HOME, pairs)  10 us
    pallas_call x9, Pallas kernels, call(): pl.pallas_call(kernel, out_shape=out_shape, in_specs=in_specs, out_specs=...  9.82 us
    all_to_all x1, blocking collectives, body(): came = lax.all_to_all(sent, HOME, split_axis=0, concat_axis=0, tiled=True)  8.4 us
    ppermute x7, waiting for transfers between devices, shift_send(): return lax.ppermute(x, HOME, pairs)  6.89 us
    psum x1, blocking collectives, body(): global_total = lax.psum(global_part, 'feat')  4.91 us
  transfers between devices with their start and end apart: 7, of which 2 were waited for; matrix products, arithmetic and copies ran while one was open for 0% of the time, Pallas kernels for 9%

profile of v27, /device:TPU:0, one launch (start us, length us, event | category | flops | bytes accessed | tf_op | source)
XLA Modules:
  0.0 52.9 jit_solution(3456495961855091922)
XLA Ops:
  0.6 1.6 %shard_map.113 = (s32[2,1024]{1,0:T(2,128)S(1)}, s32[1,1024]{1,0:T(1,128)S(1)}, bf16[8,1024]{1,0:T(8,128)(2,1)S(1)}, bf16[1024,256]{1,0:T(8,128)(2,1)S(1)}, bf16[264,256]{1,0:T(8,128)(2,1)S(1)}) custom-call(s32[1,1024]{1,0:T(1,128)} %bitcast.10, s32[1,1024]{1,0:T(1,128)} %bitcast.12, s32[1,1024]{1,0:T(1,128)} %bitcast.16, s32[1,1024]{1,0:T(1,128)} %bitcast.17, ...), custom_call_target="tpu_custom_call" | custom-call | flops 134217728 | bytes 1228800 | tf_op jit(solution)/shard_map/pallas_call | solution.py:234
  2.2 3.1 %collective-permute-start = (bf16[264,256]{1,0:T(8,128)(2,1)S(1)}, bf16[264,256]{1,0:T(8,128)(2,1)S(1)}, u32[]{:S(2)}, u32[]{:S(2)}) collective-permute-start(bf16[264,256]{1,0:T(8,128)(2,1)S(1)} %get-tuple-element.24), channel_id=1, source_target_pairs={{0,4},{1,5},{4,8},{5,9},{8,12},{9,13},{12,0},{13,1},{2,6},{3,7},{6... | collective-permute-start | bytes 405512 | tf_op jit(solution)/shard_map/ppermute | solution.py:229
  5.3 0.0 copy-start.7
  5.3 0.0 copy-start
  5.3 1.0 %shard_map.115 = (bf16[264,256]{1,0:T(8,128)(2,1)S(1)}, bf16[264,256]{1,0:T(8,128)(2,1)S(1)}, bf16[264,256]{1,0:T(8,128)(2,1)S(1)}) custom-call(s32[1,1024]{1,0:T(1,128)S(1)} %get-tuple-element.23.place.refs_0_, bf16[8,1024]{1,0:T(8,128)(2,1)S(1)} %get-tuple-element.25.refs_1_, bf16[1024,256]{1,0:T(8,128)(2,1)S(1)} %get-tuple-element.26.refs_2_), custom_call_target="tpu_custom_call" | custom-call | flops 4294967296 | bytes 950272 | tf_op jit(solution)/shard_map/pallas_call | solution.py:234
  6.3 0.0 copy-start.2
  6.3 2.1 %collective-permute-start.1 = (bf16[264,256]{1,0:T(8,128)(2,1)S(1)}, bf16[264,256]{1,0:T(8,128)(2,1)S(1)}, u32[]{:S(2)}, u32[]{:S(2)}) collective-permute-start(bf16[264,256]{1,0:T(8,128)(2,1)S(1)} %get-tuple-element.27), channel_id=1, source_target_pairs={{0,12},{1,13},{4,0},{5,1},{8,4},{9,5},{12,8},{13,9},{2,14},{3,15},... | collective-permute-start | bytes 405512 | tf_op jit(solution)/shard_map/ppermute | solution.py:229
  8.4 1.0 %collective-permute-start.2 = (bf16[264,256]{1,0:T(8,128)(2,1)S(1)}, bf16[264,256]{1,0:T(8,128)(2,1)S(1)}, u32[]{:S(2)}, u32[]{:S(2)}) collective-permute-start(bf16[264,256]{1,0:T(8,128)(2,1)S(1)} %get-tuple-element.33), channel_id=1, source_target_pairs={{0,8},{1,9},{4,12},{5,13},{8,0},{9,1},{12,4},{13,5},{2,10},{3,11},... | collective-permute-start | bytes 405512 | tf_op jit(solution)/shard_map/ppermute | solution.py:229
  9.4 0.8 %collective-permute-start.3 = (bf16[264,256]{1,0:T(8,128)(2,1)S(1)}, bf16[264,256]{1,0:T(8,128)(2,1)S(1)}, u32[]{:S(2)}, u32[]{:S(2)}) collective-permute-start(bf16[264,256]{1,0:T(8,128)(2,1)S(1)} %get-tuple-element.34), channel_id=1, source_target_pairs={{0,9},{1,8},{4,13},{5,12},{8,1},{9,0},{12,5},{13,4},{2,11},{3,10},... | collective-permute-start | bytes 405512 | tf_op jit(solution)/shard_map/ppermute | solution.py:229
  10.2 0.0 copy-done.7
  10.2 0.0 copy-done
  10.2 1.2 %shard_map.114.refs_3_ = f32[1,1024]{1,0:T(1,128)S(1)} custom-call(s32[1,1024]{1,0:T(1,128)S(1)} %get-tuple-element.23.place.refs_0_, f32[1,2048]{1,0:T(1,128)S(1)} %bitcast.8, bf16[1024,2048]{1,0:T(8,128)(2,1)S(1)} %copy-done), custom_call_target="tpu_custom_call" | custom-call | tf_op jit(solution)/shard_map/pallas_call | solution.py:234
  11.4 1.2 %shard_map.116 = (bf16[264,256]{1,0:T(8,128)(2,1)S(1)}, bf16[264,256]{1,0:T(8,128)(2,1)S(1)}, bf16[264,256]{1,0:T(8,128)(2,1)S(1)}, bf16[264,256]{1,0:T(8,128)(2,1)S(1)}) custom-call(s32[1,1024]{1,0:T(1,128)S(1)} %get-tuple-element.23.place.refs_0_, bf16[8,1024]{1,0:T(8,128)(2,1)S(1)} %get-tuple-element.25.refs_1_, ...), custom_call_target="tpu_custom_call" | custom-call | tf_op jit(solution)/shard_map/pallas_call | solution.py:234
  12.6 2.9 %collective-permute-start.4 = (bf16[264,256]{1,0:T(8,128)(2,1)S(1)}, bf16[264,256]{1,0:T(8,128)(2,1)S(1)}, u32[]{:S(2)}, u32[]{:S(2)}) collective-permute-start(bf16[264,256]{1,0:T(8,128)(2,1)S(1)} %get-tuple-element.37), channel_id=1, source_target_pairs={{0,13},{1,12},{4,1},{5,0},{8,5},{9,4},{12,9},{13,8},{2,15},{3,14},... | collective-permute-start | bytes 405512 | tf_op jit(solution)/shard_map/ppermute | solution.py:229
  15.5 0.0 collective-permute-done.refs_1_.refs_3_
  15.5 0.0 collective-permute-start.5
  15.5 0.0 collective-permute-done.1.refs_2_.refs_4_
  15.5 0.1 collective-permute-start.6
  15.7 4.9 %psum.7.refs_4_.refs_5_ = f32[1,1024]{1,0:T(1,128)S(1)} all-reduce(f32[1,1024]{1,0:T(1,128)S(1)} %shard_map.114.refs_3_), channel_id=1, replica_groups=mesh['groups'=2,'rows'=4,'feat'=2,'ent'=2] {'feat'}, use_global_device_ids=true, to_apply=%region_0.0 | all-reduce | flops 1024 | bytes 8192 | tf_op jit(solution)/shard_map/psum | solution.py:315
  20.6 0.0 copy-done.2
  20.6 0.6 %shard_map.117 = (bf16[1024,256]{1,0:T(8,128)(2,1)S(1)}, f32[1,256]{1,0:T(1,128)S(1)}, f32[1,256]{1,0:T(1,128)S(1)}, f32[1,256]{1,0:T(1,128)S(1)}) custom-call(f32[512,256]{1,0:T(8,128)S(1)} %copy-done.2, bf16[264,256]{1,0:T(8,128)(2,1)S(1)} %collective-permute-done.refs_1_.refs_3_, bf16[264,256]{1,0:T(8,128)(2,1)S(1)} %collective-permute-done.1.refs_2_.refs_4_, ...), custom_call_target="tpu_custom_call" | custom-call | tf_op jit(solution)/shard_map/pallas_call | solution.py:234
  21.2 4.3 %collective-permute-done.2.refs_1_.refs_6_ = bf16[264,256]{1,0:T(8,128)(2,1)S(1)} collective-permute-done((bf16[264,256]{1,0:T(8,128)(2,1)S(1)}, bf16[264,256]{1,0:T(8,128)(2,1)S(1)}, u32[]{:S(2)}, u32[]{:S(2)}) %collective-permute-start.2) | collective-permute-done | bytes 135200 | tf_op jit(solution)/shard_map/ppermute | solution.py:229
  25.5 2.6 %collective-permute-done.3.refs_2_.refs_7_ = bf16[264,256]{1,0:T(8,128)(2,1)S(1)} collective-permute-done((bf16[264,256]{1,0:T(8,128)(2,1)S(1)}, bf16[264,256]{1,0:T(8,128)(2,1)S(1)}, u32[]{:S(2)}, u32[]{:S(2)}) %collective-permute-start.3) | collective-permute-done | bytes 135200 | tf_op jit(solution)/shard_map/ppermute | solution.py:229
  28.1 0.5 shard_map.118
  28.6 0.0 collective-permute-done.4.refs_6_.refs_8_
  28.6 0.0 collective-permute-done.5.refs_7_.refs_9_
  28.6 0.0 collective-permute-done.6.refs_8_.refs_10_
  28.6 0.0 copy-start.1
  28.6 0.0 copy-start.3
  28.6 0.0 copy-start.4
  28.7 0.0 copy-start.5
  28.7 0.0 copy-start.6
  28.7 0.6 %shard_map.119 = f32[16,1,256]{2,1,0:T(1,128)S(1)} custom-call(bf16[1024,256]{1,0:T(8,128)(2,1)S(1)} %get-tuple-element.29.refs_0_, f32[1,256]{1,0:T(1,128)S(1)} %get-tuple-element.30.refs_1_, f32[1,256]{1,0:T(1,128)S(1)} %get-tuple-element.31.refs_2_, f32[1,256]{1,0:T(1,128)S(1)} %get-tuple-element.32.refs_3_, f32[1,256]{1,0:T(1,128)S(1)} %get-tuple-element.35.refs_4_, ...), custom_call_target="tpu_custom_call" | custom-call | flops 4294967296 | bytes 951296 | tf_op jit(solution)/shard_map/pallas_call | solution.py:234
  29.3 12.0 %all_to_all.10.refs_6_ = f32[16,1,256]{2,1,0:T(1,128)S(1)} all-to-all(f32[16,1,256]{2,1,0:T(1,128)S(1)} %shard_map.119), channel_id=1, replica_groups=mesh['groups'=2,'rows'=4,'feat'=2,'ent'=2] {'rows','feat','ent'}, dimensions={0} | all-to-all | bytes 32768 | tf_op jit(solution)/shard_map/all_to_all | solution.py:349
  41.4 0.0 copy-done.1
  41.4 0.0 copy-done.3
  41.4 0.0 copy-done.4
  41.4 0.0 copy-done.5
  41.4 0.0 copy-done.6
  41.4 1.0 %shard_map.120 = f32[8,1,2304]{2,1,0:T(1,128)S(1)} custom-call(s32[1,1024]{1,0:T(1,128)S(1)} %bitcast.11, s32[1,1024]{1,0:T(1,128)S(1)} %bitcast.13, s32[2,1024]{1,0:T(2,128)S(1)} %get-tuple-element.22.refs_2_, s32[1,1024]{1,0:T(1,128)S(1)} %bitcast.14, s32[1,1024]{1,0:T(1,128)S(1)} %bitcast.15, f32[1,1024]{1,0:T(1,128)S(1)} %psum.7.refs_4_.refs_5_, ...), custom_call_target="tpu_custom_call" | custom-call | flops 67108864 | bytes 4313088 | tf_op jit(solution)/shard_map/pallas_call | solution.py:234
  42.4 8.4 %all_to_all.11.refs_2_ = f32[8,1,2304]{2,1,0:T(1,128)S(1)} all-to-all(f32[8,1,2304]{2,1,0:T(1,128)S(1)} %shard_map.120), channel_id=1, replica_groups=mesh['groups'=2,'rows'=4,'feat'=2,'ent'=2] {'rows','ent'}, dimensions={0} | all-to-all | bytes 147456 | tf_op jit(solution)/shard_map/all_to_all | solution.py:366
  50.8 2.1 %shard_map.121 = (f32[1,2048]{1,0:T(1,128)}, f32[512,256]{1,0:T(8,128)}) custom-call(f32[512,256]{1,0:T(8,128)S(1)} %copy-done.2, f32[1,2048]{1,0:T(1,128)S(1)} %bitcast.9, f32[8,1,2304]{2,1,0:T(1,128)S(1)} %all_to_all.11.refs_2_, bf16[264,256]{1,0:T(8,128)(2,1)S(1)} %collective-permute-done.refs_1_.refs_3_, ...), custom_call_target="tpu_custom_call" | custom-call | flops 1073741824 | bytes 2220032 | tf_op jit(solution)/shard_map/pallas_call | solution.py:234
  (1 shorter events, 0.0 us)
Async XLA Ops:
  2.2 13.3 %collective-permute-start = (bf16[264,256]{1,0:T(8,128)(2,1)S(1)}, bf16[264,256]{1,0:T(8,128)(2,1)S(1)}, u32[]{:S(2)}, u32[]{:S(2)}) collective-permute-start(bf16[264,256]{1,0:T(8,128)(2,1)S(1)} %get-tuple-element.24), channel_id=1, source_target_pairs={{0,4},{1,5},{4,8},{5,9},{8,12},{9,13},{12,0},{13,1},{2,6},{3,7},{6... | collective-permute-start | bytes 405512 | tf_op jit(solution)/shard_map/ppermute | solution.py:229
  5.3 4.9 %copy-start.7 = (bf16[2048]{0:T(1024)(128)(2,1)S(1)}, bf16[2048]{0:T(1024)(128)(2,1)}, u32[]{:S(2)}) copy-start(bf16[2048]{0:T(1024)(128)(2,1)} %param.11) | copy-start | bytes 12292
  5.3 4.9 %copy-start = (bf16[1024,2048]{1,0:T(8,128)(2,1)S(1)}, bf16[1024,2048]{1,0:T(8,128)(2,1)}, u32[]{:S(2)}) copy-start(bf16[1024,2048]{1,0:T(8,128)(2,1)} %refs_7_.1) | copy-start | bytes 12582916
  6.3 14.3 %copy-start.2 = (f32[512,256]{1,0:T(8,128)S(1)}, f32[512,256]{1,0:T(8,128)}, u32[]{:S(2)}) copy-start(f32[512,256]{1,0:T(8,128)} %refs_0_.3) | copy-start | bytes 1572868
  6.3 9.3 %collective-permute-start.1 = (bf16[264,256]{1,0:T(8,128)(2,1)S(1)}, bf16[264,256]{1,0:T(8,128)(2,1)S(1)}, u32[]{:S(2)}, u32[]{:S(2)}) collective-permute-start(bf16[264,256]{1,0:T(8,128)(2,1)S(1)} %get-tuple-element.27), channel_id=1, source_target_pairs={{0,12},{1,13},{4,0},{5,1},{8,4},{9,5},{12,8},{13,9},{2,14},{3,15},... | collective-permute-start | bytes 405512 | tf_op jit(solution)/shard_map/ppermute | solution.py:229
  8.4 17.2 %collective-permute-start.2 = (bf16[264,256]{1,0:T(8,128)(2,1)S(1)}, bf16[264,256]{1,0:T(8,128)(2,1)S(1)}, u32[]{:S(2)}, u32[]{:S(2)}) collective-permute-start(bf16[264,256]{1,0:T(8,128)(2,1)S(1)} %get-tuple-element.33), channel_id=1, source_target_pairs={{0,8},{1,9},{4,12},{5,13},{8,0},{9,1},{12,4},{13,5},{2,10},{3,11},... | collective-permute-start | bytes 405512 | tf_op jit(solution)/shard_map/ppermute | solution.py:229
  9.4 18.7 %collective-permute-start.3 = (bf16[264,256]{1,0:T(8,128)(2,1)S(1)}, bf16[264,256]{1,0:T(8,128)(2,1)S(1)}, u32[]{:S(2)}, u32[]{:S(2)}) collective-permute-start(bf16[264,256]{1,0:T(8,128)(2,1)S(1)} %get-tuple-element.34), channel_id=1, source_target_pairs={{0,9},{1,8},{4,13},{5,12},{8,1},{9,0},{12,5},{13,4},{2,11},{3,10},... | collective-permute-start | bytes 405512 | tf_op jit(solution)/shard_map/ppermute | solution.py:229
  12.6 16.0 %collective-permute-start.4 = (bf16[264,256]{1,0:T(8,128)(2,1)S(1)}, bf16[264,256]{1,0:T(8,128)(2,1)S(1)}, u32[]{:S(2)}, u32[]{:S(2)}) collective-permute-start(bf16[264,256]{1,0:T(8,128)(2,1)S(1)} %get-tuple-element.37), channel_id=1, source_target_pairs={{0,13},{1,12},{4,1},{5,0},{8,5},{9,4},{12,9},{13,8},{2,15},{3,14},... | collective-permute-start | bytes 405512 | tf_op jit(solution)/shard_map/ppermute | solution.py:229
  15.5 13.1 %collective-permute-start.5 = (bf16[264,256]{1,0:T(8,128)(2,1)S(1)}, bf16[264,256]{1,0:T(8,128)(2,1)S(1)}, u32[]{:S(2)}, u32[]{:S(2)}) collective-permute-start(bf16[264,256]{1,0:T(8,128)(2,1)S(1)} %get-tuple-element.38), channel_id=1, source_target_pairs={{0,5},{1,4},{4,9},{5,8},{8,13},{9,12},{12,1},{13,0},{2,7},{3,6},{6... | collective-permute-start | bytes 405512 | tf_op jit(solution)/shard_map/ppermute | solution.py:229
  15.5 13.1 %collective-permute-start.6 = (bf16[264,256]{1,0:T(8,128)(2,1)S(1)}, bf16[264,256]{1,0:T(8,128)(2,1)S(1)}, u32[]{:S(2)}, u32[]{:S(2)}) collective-permute-start(bf16[264,256]{1,0:T(8,128)(2,1)S(1)} %get-tuple-element.39), channel_id=1, source_target_pairs={{0,1},{1,0},{4,5},{5,4},{8,9},{9,8},{12,13},{13,12},{2,3},{3,2},{6... | collective-permute-start | bytes 405512 | tf_op jit(solution)/shard_map/ppermute | solution.py:229
  28.6 12.7 %copy-start.1 = (bf16[1024,2048]{1,0:T(8,128)(2,1)S(1)}, bf16[1024,2048]{1,0:T(8,128)(2,1)}, u32[]{:S(2)}) copy-start(bf16[1024,2048]{1,0:T(8,128)(2,1)} %refs_7_.1) | copy-start | bytes 12582916
  28.6 12.7 %copy-start.3 = (s32[1024,1]{0,1:T(1,128)S(1)}, s32[1024,1]{0,1:T(1,128)}, u32[]{:S(2)}) copy-start(s32[1024,1]{0,1:T(1,128)} %param.14) | copy-start | bytes 12292
  28.6 12.7 %copy-start.4 = (s32[1024,1]{0,1:T(1,128)S(1)}, s32[1024,1]{0,1:T(1,128)}, u32[]{:S(2)}) copy-start(s32[1024,1]{0,1:T(1,128)} %param.16) | copy-start | bytes 12292
  28.7 12.7 %copy-start.5 = (s32[1024]{0:T(1024)S(1)}, s32[1024]{0:T(1024)}, u32[]{:S(2)}) copy-start(s32[1024]{0:T(1024)} %param.18) | copy-start | bytes 12292
  28.7 12.7 %copy-start.6 = (s32[1024]{0:T(1024)S(1)}, s32[1024]{0:T(1024)}, u32[]{:S(2)}) copy-start(s32[1024]{0:T(1024)} %param.19) | copy-start | bytes 12292

commit v28 on v20

--- a/solution.py
+++ b/solution.py
@@ -323,7 +323,7 @@
     near_chunks = [shift_send(x, n_rows, n_ent, k) for k, x in zip(near, near_chunks)]
     chunks = dict(zip(first + second + near, chunks + near_chunks))
     early = away[:n_ent] + near[-1:]
-    later, late = away[n_ent:-2], near[:-1]
+    later, late = away[n_ent:-2] + near[2:-1], near[:2]
     order = early + later + late
     table, *scores = call(
         partial(early_kernel, capacity, len(early)),

time: 53.1 us -> 53.2 us (level)
  no operation moved by 1% of the time
where the time goes in v28:
time: 53.2 us; the launch traced here: 52.9 us
  blocking collectives  25.2 us (47%)
  starting transfers between devices  11.8 us (22%)
  Pallas kernels  9.81 us (18%)
  waiting for transfers between devices  5.18 us (10%)
  between operations  0.77 us (1%)
    all_to_all x1, blocking collectives, body(): lax.all_to_all(scores, EVERY, split_axis=0, concat_axis=0, tiled=True)  11.9 us
    ppermute x7, starting transfers between devices, shift_send(): return lax.ppermute(x, HOME, pairs)  11.8 us
    pallas_call x9, Pallas kernels, call(): pl.pallas_call(kernel, out_shape=out_shape, in_specs=in_specs, out_specs=...  9.81 us
    all_to_all x1, blocking collectives, body(): came = lax.all_to_all(sent, HOME, split_axis=0, concat_axis=0, tiled=True)  8.4 us
    ppermute x7, waiting for transfers between devices, shift_send(): return lax.ppermute(x, HOME, pairs)  5.18 us
    psum x1, blocking collectives, body(): global_total = lax.psum(global_part, 'feat')  4.91 us
  transfers between devices with their start and end apart: 7, of which 2 were waited for; matrix products, arithmetic and copies ran while one was open for 0% of the time, Pallas kernels for 9%

profile of v28, /device:TPU:0, one launch (start us, length us, event | category | flops | bytes accessed | tf_op | source)
XLA Modules:
  0.0 52.9 jit_solution(4575797007506177095)
XLA Ops:
  0.6 1.6 %shard_map.113 = (s32[2,1024]{1,0:T(2,128)S(1)}, s32[1,1024]{1,0:T(1,128)S(1)}, bf16[8,1024]{1,0:T(8,128)(2,1)S(1)}, bf16[1024,256]{1,0:T(8,128)(2,1)S(1)}, bf16[264,256]{1,0:T(8,128)(2,1)S(1)}) custom-call(s32[1,1024]{1,0:T(1,128)} %bitcast.10, s32[1,1024]{1,0:T(1,128)} %bitcast.12, s32[1,1024]{1,0:T(1,128)} %bitcast.16, s32[1,1024]{1,0:T(1,128)} %bitcast.17, ...), custom_call_target="tpu_custom_call" | custom-call | flops 134217728 | bytes 1228800 | tf_op jit(solution)/shard_map/pallas_call | solution.py:234
  2.2 3.1 %collective-permute-start = (bf16[264,256]{1,0:T(8,128)(2,1)S(1)}, bf16[264,256]{1,0:T(8,128)(2,1)S(1)}, u32[]{:S(2)}, u32[]{:S(2)}) collective-permute-start(bf16[264,256]{1,0:T(8,128)(2,1)S(1)} %get-tuple-element.25), channel_id=1, source_target_pairs={{0,4},{1,5},{4,8},{5,9},{8,12},{9,13},{12,0},{13,1},{2,6},{3,7},{6... | collective-permute-start | bytes 405512 | tf_op jit(solution)/shard_map/ppermute | solution.py:229
  5.3 0.0 copy-start.7
  5.3 0.0 copy-start
  5.3 1.0 %shard_map.115 = (bf16[264,256]{1,0:T(8,128)(2,1)S(1)}, bf16[264,256]{1,0:T(8,128)(2,1)S(1)}, bf16[264,256]{1,0:T(8,128)(2,1)S(1)}) custom-call(s32[1,1024]{1,0:T(1,128)S(1)} %get-tuple-element.24.place.refs_0_, bf16[8,1024]{1,0:T(8,128)(2,1)S(1)} %get-tuple-element.26.refs_1_, bf16[1024,256]{1,0:T(8,128)(2,1)S(1)} %get-tuple-element.27.refs_2_), custom_call_target="tpu_custom_call" | custom-call | flops 4294967296 | bytes 950272 | tf_op jit(solution)/shard_map/pallas_call | solution.py:234
  6.3 0.0 copy-start.2
  6.3 2.1 %collective-permute-start.1 = (bf16[264,256]{1,0:T(8,128)(2,1)S(1)}, bf16[264,256]{1,0:T(8,128)(2,1)S(1)}, u32[]{:S(2)}, u32[]{:S(2)}) collective-permute-start(bf16[264,256]{1,0:T(8,128)(2,1)S(1)} %get-tuple-element.28), channel_id=1, source_target_pairs={{0,12},{1,13},{4,0},{5,1},{8,4},{9,5},{12,8},{13,9},{2,14},{3,15},... | collective-permute-start | bytes 405512 | tf_op jit(solution)/shard_map/ppermute | solution.py:229
  8.4 1.0 %collective-permute-start.2 = (bf16[264,256]{1,0:T(8,128)(2,1)S(1)}, bf16[264,256]{1,0:T(8,128)(2,1)S(1)}, u32[]{:S(2)}, u32[]{:S(2)}) collective-permute-start(bf16[264,256]{1,0:T(8,128)(2,1)S(1)} %get-tuple-element.34), channel_id=1, source_target_pairs={{0,8},{1,9},{4,12},{5,13},{8,0},{9,1},{12,4},{13,5},{2,10},{3,11},... | collective-permute-start | bytes 405512 | tf_op jit(solution)/shard_map/ppermute | solution.py:229
  9.4 0.8 %collective-permute-start.3 = (bf16[264,256]{1,0:T(8,128)(2,1)S(1)}, bf16[264,256]{1,0:T(8,128)(2,1)S(1)}, u32[]{:S(2)}, u32[]{:S(2)}) collective-permute-start(bf16[264,256]{1,0:T(8,128)(2,1)S(1)} %get-tuple-element.35), channel_id=1, source_target_pairs={{0,9},{1,8},{4,13},{5,12},{8,1},{9,0},{12,5},{13,4},{2,11},{3,10},... | collective-permute-start | bytes 405512 | tf_op jit(solution)/shard_map/ppermute | solution.py:229
  10.2 0.0 copy-done.7
  10.2 0.0 copy-done
  10.2 1.2 %shard_map.114.refs_3_ = f32[1,1024]{1,0:T(1,128)S(1)} custom-call(s32[1,1024]{1,0:T(1,128)S(1)} %get-tuple-element.24.place.refs_0_, f32[1,2048]{1,0:T(1,128)S(1)} %bitcast.8, bf16[1024,2048]{1,0:T(8,128)(2,1)S(1)} %copy-done), custom_call_target="tpu_custom_call" | custom-call | tf_op jit(solution)/shard_map/pallas_call | solution.py:234
  11.4 1.2 %shard_map.116 = (bf16[264,256]{1,0:T(8,128)(2,1)S(1)}, bf16[264,256]{1,0:T(8,128)(2,1)S(1)}, bf16[264,256]{1,0:T(8,128)(2,1)S(1)}, bf16[264,256]{1,0:T(8,128)(2,1)S(1)}) custom-call(s32[1,1024]{1,0:T(1,128)S(1)} %get-tuple-element.24.place.refs_0_, bf16[8,1024]{1,0:T(8,128)(2,1)S(1)} %get-tuple-element.26.refs_1_, ...), custom_call_target="tpu_custom_call" | custom-call | tf_op jit(solution)/shard_map/pallas_call | solution.py:234
  12.6 1.3 %collective-permute-start.4 = (bf16[264,256]{1,0:T(8,128)(2,1)S(1)}, bf16[264,256]{1,0:T(8,128)(2,1)S(1)}, u32[]{:S(2)}, u32[]{:S(2)}) collective-permute-start(bf16[264,256]{1,0:T(8,128)(2,1)S(1)} %get-tuple-element.36), channel_id=1, source_target_pairs={{0,1},{1,0},{4,5},{5,4},{8,9},{9,8},{12,13},{13,12},{2,3},{3,2},{6... | collective-permute-start | bytes 405512 | tf_op jit(solution)/shard_map/ppermute | solution.py:229
  13.9 0.0 collective-permute-done.refs_1_.refs_3_
  13.9 0.0 collective-permute-start.5
  13.9 0.0 collective-permute-done.1.refs_2_.refs_4_
  14.0 3.5 %collective-permute-start.6 = (bf16[264,256]{1,0:T(8,128)(2,1)S(1)}, bf16[264,256]{1,0:T(8,128)(2,1)S(1)}, u32[]{:S(2)}, u32[]{:S(2)}) collective-permute-start(bf16[264,256]{1,0:T(8,128)(2,1)S(1)} %get-tuple-element.41), channel_id=1, source_target_pairs={{0,13},{1,12},{4,1},{5,0},{8,5},{9,4},{12,9},{13,8},{2,15},{3,14},... | collective-permute-start | bytes 405512 | tf_op jit(solution)/shard_map/ppermute | solution.py:229
  17.5 4.9 %psum.7.refs_4_.refs_5_ = f32[1,1024]{1,0:T(1,128)S(1)} all-reduce(f32[1,1024]{1,0:T(1,128)S(1)} %shard_map.114.refs_3_), channel_id=1, replica_groups=mesh['groups'=2,'rows'=4,'feat'=2,'ent'=2] {'feat'}, use_global_device_ids=true, to_apply=%region_0.0 | all-reduce | flops 1024 | bytes 8192 | tf_op jit(solution)/shard_map/psum | solution.py:315
  22.4 0.0 copy-done.2
  22.4 0.6 %shard_map.117 = (bf16[1024,256]{1,0:T(8,128)(2,1)S(1)}, f32[1,256]{1,0:T(1,128)S(1)}, f32[1,256]{1,0:T(1,128)S(1)}, f32[1,256]{1,0:T(1,128)S(1)}) custom-call(f32[512,256]{1,0:T(8,128)S(1)} %copy-done.2, bf16[264,256]{1,0:T(8,128)(2,1)S(1)} %collective-permute-done.refs_1_.refs_3_, bf16[264,256]{1,0:T(8,128)(2,1)S(1)} %collective-permute-done.1.refs_2_.refs_4_, ...), custom_call_target="tpu_custom_call" | custom-call | tf_op jit(solution)/shard_map/pallas_call | solution.py:234
  23.0 2.6 %collective-permute-done.2.refs_1_.refs_6_ = bf16[264,256]{1,0:T(8,128)(2,1)S(1)} collective-permute-done((bf16[264,256]{1,0:T(8,128)(2,1)S(1)}, bf16[264,256]{1,0:T(8,128)(2,1)S(1)}, u32[]{:S(2)}, u32[]{:S(2)}) %collective-permute-start.2) | collective-permute-done | bytes 135200 | tf_op jit(solution)/shard_map/ppermute | solution.py:229
  25.6 2.6 %collective-permute-done.3.refs_2_.refs_7_ = bf16[264,256]{1,0:T(8,128)(2,1)S(1)} collective-permute-done((bf16[264,256]{1,0:T(8,128)(2,1)S(1)}, bf16[264,256]{1,0:T(8,128)(2,1)S(1)}, u32[]{:S(2)}, u32[]{:S(2)}) %collective-permute-start.3) | collective-permute-done | bytes 135200 | tf_op jit(solution)/shard_map/ppermute | solution.py:229
  28.2 0.0 collective-permute-done.4.refs_3_.refs_8_
  28.2 0.6 %shard_map.118 = (f32[1,256]{1,0:T(1,128)S(1)}, f32[1,256]{1,0:T(1,128)S(1)}, f32[1,256]{1,0:T(1,128)S(1)}) custom-call(bf16[1024,256]{1,0:T(8,128)(2,1)S(1)} %get-tuple-element.30.refs_0_, bf16[264,256]{1,0:T(8,128)(2,1)S(1)} %collective-permute-done.2.refs_1_.refs_6_, bf16[264,256]{1,0:T(8,128)(2,1)S(1)} %collective-permute-done.3.refs_2_.refs_7_, ...), custom_call_target="tpu_custom_call" | custom-call | tf_op jit(solution)/shard_map/pallas_call | solution.py:234
  28.8 0.0 collective-permute-done.5.refs_7_.refs_9_
  28.8 0.0 collective-permute-done.6.refs_8_.refs_10_
  28.9 0.0 copy-start.1
  28.9 0.0 copy-start.3
  28.9 0.0 copy-start.4
  28.9 0.0 copy-start.5
  28.9 0.0 copy-start.6
  28.9 0.5 shard_map.119
  29.4 11.9 %all_to_all.10.refs_6_ = f32[16,1,256]{2,1,0:T(1,128)S(1)} all-to-all(f32[16,1,256]{2,1,0:T(1,128)S(1)} %shard_map.119), channel_id=1, replica_groups=mesh['groups'=2,'rows'=4,'feat'=2,'ent'=2] {'rows','feat','ent'}, dimensions={0} | all-to-all | bytes 32768 | tf_op jit(solution)/shard_map/all_to_all | solution.py:349
  41.3 0.0 copy-done.1
  41.4 0.0 copy-done.3
  41.4 0.0 copy-done.4
  41.4 0.0 copy-done.5
  41.4 0.0 copy-done.6
  41.4 1.0 %shard_map.120 = f32[8,1,2304]{2,1,0:T(1,128)S(1)} custom-call(s32[1,1024]{1,0:T(1,128)S(1)} %bitcast.11, s32[1,1024]{1,0:T(1,128)S(1)} %bitcast.13, s32[2,1024]{1,0:T(2,128)S(1)} %get-tuple-element.23.refs_2_, s32[1,1024]{1,0:T(1,128)S(1)} %bitcast.14, s32[1,1024]{1,0:T(1,128)S(1)} %bitcast.15, f32[1,1024]{1,0:T(1,128)S(1)} %psum.7.refs_4_.refs_5_, ...), custom_call_target="tpu_custom_call" | custom-call | flops 67108864 | bytes 4313088 | tf_op jit(solution)/shard_map/pallas_call | solution.py:234
  42.4 8.4 %all_to_all.11.refs_2_ = f32[8,1,2304]{2,1,0:T(1,128)S(1)} all-to-all(f32[8,1,2304]{2,1,0:T(1,128)S(1)} %shard_map.120), channel_id=1, replica_groups=mesh['groups'=2,'rows'=4,'feat'=2,'ent'=2] {'rows','ent'}, dimensions={0} | all-to-all | bytes 147456 | tf_op jit(solution)/shard_map/all_to_all | solution.py:366
  50.8 2.1 %shard_map.121 = (f32[1,2048]{1,0:T(1,128)}, f32[512,256]{1,0:T(8,128)}) custom-call(f32[512,256]{1,0:T(8,128)S(1)} %copy-done.2, f32[1,2048]{1,0:T(1,128)S(1)} %bitcast.9, f32[8,1,2304]{2,1,0:T(1,128)S(1)} %all_to_all.11.refs_2_, bf16[264,256]{1,0:T(8,128)(2,1)S(1)} %collective-permute-done.refs_1_.refs_3_, ...), custom_call_target="tpu_custom_call" | custom-call | flops 1073741824 | bytes 2220032 | tf_op jit(solution)/shard_map/pallas_call | solution.py:234
  (1 shorter events, 0.0 us)
Async XLA Ops:
  2.2 11.7 %collective-permute-start = (bf16[264,256]{1,0:T(8,128)(2,1)S(1)}, bf16[264,256]{1,0:T(8,128)(2,1)S(1)}, u32[]{:S(2)}, u32[]{:S(2)}) collective-permute-start(bf16[264,256]{1,0:T(8,128)(2,1)S(1)} %get-tuple-element.25), channel_id=1, source_target_pairs={{0,4},{1,5},{4,8},{5,9},{8,12},{9,13},{12,0},{13,1},{2,6},{3,7},{6... | collective-permute-start | bytes 405512 | tf_op jit(solution)/shard_map/ppermute | solution.py:229
  5.3 4.9 %copy-start.7 = (bf16[2048]{0:T(1024)(128)(2,1)S(1)}, bf16[2048]{0:T(1024)(128)(2,1)}, u32[]{:S(2)}) copy-start(bf16[2048]{0:T(1024)(128)(2,1)} %param.11) | copy-start | bytes 12292
  5.3 4.9 %copy-start = (bf16[1024,2048]{1,0:T(8,128)(2,1)S(1)}, bf16[1024,2048]{1,0:T(8,128)(2,1)}, u32[]{:S(2)}) copy-start(bf16[1024,2048]{1,0:T(8,128)(2,1)} %refs_7_.1) | copy-start | bytes 12582916
  6.3 16.2 %copy-start.2 = (f32[512,256]{1,0:T(8,128)S(1)}, f32[512,256]{1,0:T(8,128)}, u32[]{:S(2)}) copy-start(f32[512,256]{1,0:T(8,128)} %refs_0_.3) | copy-start | bytes 1572868
  6.3 7.7 %collective-permute-start.1 = (bf16[264,256]{1,0:T(8,128)(2,1)S(1)}, bf16[264,256]{1,0:T(8,128)(2,1)S(1)}, u32[]{:S(2)}, u32[]{:S(2)}) collective-permute-start(bf16[264,256]{1,0:T(8,128)(2,1)S(1)} %get-tuple-element.28), channel_id=1, source_target_pairs={{0,12},{1,13},{4,0},{5,1},{8,4},{9,5},{12,8},{13,9},{2,14},{3,15},... | collective-permute-start | bytes 405512 | tf_op jit(solution)/shard_map/ppermute | solution.py:229
  8.4 17.3 %collective-permute-start.2 = (bf16[264,256]{1,0:T(8,128)(2,1)S(1)}, bf16[264,256]{1,0:T(8,128)(2,1)S(1)}, u32[]{:S(2)}, u32[]{:S(2)}) collective-permute-start(bf16[264,256]{1,0:T(8,128)(2,1)S(1)} %get-tuple-element.34), channel_id=1, source_target_pairs={{0,8},{1,9},{4,12},{5,13},{8,0},{9,1},{12,4},{13,5},{2,10},{3,11},... | collective-permute-start | bytes 405512 | tf_op jit(solution)/shard_map/ppermute | solution.py:229
  9.4 18.8 %collective-permute-start.3 = (bf16[264,256]{1,0:T(8,128)(2,1)S(1)}, bf16[264,256]{1,0:T(8,128)(2,1)S(1)}, u32[]{:S(2)}, u32[]{:S(2)}) collective-permute-start(bf16[264,256]{1,0:T(8,128)(2,1)S(1)} %get-tuple-element.35), channel_id=1, source_target_pairs={{0,9},{1,8},{4,13},{5,12},{8,1},{9,0},{12,5},{13,4},{2,11},{3,10},... | collective-permute-start | bytes 405512 | tf_op jit(solution)/shard_map/ppermute | solution.py:229
  12.6 15.6 %collective-permute-start.4 = (bf16[264,256]{1,0:T(8,128)(2,1)S(1)}, bf16[264,256]{1,0:T(8,128)(2,1)S(1)}, u32[]{:S(2)}, u32[]{:S(2)}) collective-permute-start(bf16[264,256]{1,0:T(8,128)(2,1)S(1)} %get-tuple-element.36), channel_id=1, source_target_pairs={{0,1},{1,0},{4,5},{5,4},{8,9},{9,8},{12,13},{13,12},{2,3},{3,2},{6... | collective-permute-start | bytes 405512 | tf_op jit(solution)/shard_map/ppermute | solution.py:229
  13.9 14.9 %collective-permute-start.5 = (bf16[264,256]{1,0:T(8,128)(2,1)S(1)}, bf16[264,256]{1,0:T(8,128)(2,1)S(1)}, u32[]{:S(2)}, u32[]{:S(2)}) collective-permute-start(bf16[264,256]{1,0:T(8,128)(2,1)S(1)} %get-tuple-element.40), channel_id=1, source_target_pairs={{0,5},{1,4},{4,9},{5,8},{8,13},{9,12},{12,1},{13,0},{2,7},{3,6},{6... | collective-permute-start | bytes 405512 | tf_op jit(solution)/shard_map/ppermute | solution.py:229
  14.0 14.9 %collective-permute-start.6 = (bf16[264,256]{1,0:T(8,128)(2,1)S(1)}, bf16[264,256]{1,0:T(8,128)(2,1)S(1)}, u32[]{:S(2)}, u32[]{:S(2)}) collective-permute-start(bf16[264,256]{1,0:T(8,128)(2,1)S(1)} %get-tuple-element.41), channel_id=1, source_target_pairs={{0,13},{1,12},{4,1},{5,0},{8,5},{9,4},{12,9},{13,8},{2,15},{3,14},... | collective-permute-start | bytes 405512 | tf_op jit(solution)/shard_map/ppermute | solution.py:229
  28.9 12.5 %copy-start.1 = (bf16[1024,2048]{1,0:T(8,128)(2,1)S(1)}, bf16[1024,2048]{1,0:T(8,128)(2,1)}, u32[]{:S(2)}) copy-start(bf16[1024,2048]{1,0:T(8,128)(2,1)} %refs_7_.1) | copy-start | bytes 12582916
  28.9 12.5 %copy-start.3 = (s32[1024,1]{0,1:T(1,128)S(1)}, s32[1024,1]{0,1:T(1,128)}, u32[]{:S(2)}) copy-start(s32[1024,1]{0,1:T(1,128)} %param.14) | copy-start | bytes 12292
  28.9 12.5 %copy-start.4 = (s32[1024,1]{0,1:T(1,128)S(1)}, s32[1024,1]{0,1:T(1,128)}, u32[]{:S(2)}) copy-start(s32[1024,1]{0,1:T(1,128)} %param.16) | copy-start | bytes 12292
  28.9 12.5 %copy-start.5 = (s32[1024]{0:T(1024)S(1)}, s32[1024]{0:T(1024)}, u32[]{:S(2)}) copy-start(s32[1024]{0:T(1024)} %param.18) | copy-start | bytes 12292
  28.9 12.5 %copy-start.6 = (s32[1024]{0:T(1024)S(1)}, s32[1024]{0:T(1024)}, u32[]{:S(2)}) copy-start(s32[1024]{0:T(1024)} %param.19) | copy-start | bytes 12292

commit v29 on v21

--- a/solution.py
+++ b/solution.py
@@ -272,7 +272,7 @@
     middle = n_rows // 2
     away = [up * n_ent for half in range(1, middle) for up in (half, n_rows - half)]
     away += [middle * n_ent + c for c in range(n_ent)]
-    away += [up * n_ent + c for c in range(1, n_ent) for half in range(1, middle) for up in (half, n_rows - half)]
+    away += [up * n_ent + c for c in range(1, n_ent) for half in range(1, middle) for up in (n_rows - half, half)]
     first, second, near = away[:1], away[1:-2], [*away[-2:], *reversed(range(n_ent))]
     chunk = shape(capacity + IDS, width, dtype=BF16)
     flops = len(first) * 2 * capacity * rows_here * width

time: 53.1 us -> 53.1 us (level)
  transfers between devices with their start and end apart: 7 -> 7, of which waited for: 3 -> 2; matrix products, arithmetic and copies ran while one was open for 0% -> 0% of each run, Pallas kernels for 9% -> 9%
where the time goes in v29:
time: 53.1 us; the launch traced here: 52.8 us
  blocking collectives  25.3 us (48%)
  starting transfers between devices  10.4 us (20%)
  Pallas kernels  9.78 us (18%)
  waiting for transfers between devices  6.55 us (12%)
  between operations  0.76 us (1%)
    all_to_all x1, blocking collectives, body(): lax.all_to_all(scores, EVERY, split_axis=0, concat_axis=0, tiled=True)  12 us
    ppermute x7, starting transfers between devices, shift_send(): return lax.ppermute(x, HOME, pairs)  10.4 us
    pallas_call x9, Pallas kernels, call(): pl.pallas_call(kernel, out_shape=out_shape, in_specs=in_specs, out_specs=...  9.78 us
    all_to_all x1, blocking collectives, body(): came = lax.all_to_all(sent, HOME, split_axis=0, concat_axis=0, tiled=True)  8.4 us
    ppermute x7, waiting for transfers between devices, shift_send(): return lax.ppermute(x, HOME, pairs)  6.55 us
    psum x1, blocking collectives, body(): global_total = lax.psum(global_part, 'feat')  4.93 us
  transfers between devices with their start and end apart: 7, of which 2 were waited for; matrix products, arithmetic and copies ran while one was open for 0% of the time, Pallas kernels for 9%

profile of v29, /device:TPU:0, one launch (start us, length us, event | category | flops | bytes accessed | tf_op | source)
XLA Modules:
  0.0 52.8 jit_solution(15784153040373921686)
XLA Ops:
  0.6 1.6 %shard_map.113 = (s32[2,1024]{1,0:T(2,128)S(1)}, s32[1,1024]{1,0:T(1,128)S(1)}, bf16[8,1024]{1,0:T(8,128)(2,1)S(1)}, bf16[1024,256]{1,0:T(8,128)(2,1)S(1)}, bf16[264,256]{1,0:T(8,128)(2,1)S(1)}) custom-call(s32[1,1024]{1,0:T(1,128)} %bitcast.10, s32[1,1024]{1,0:T(1,128)} %bitcast.12, s32[1,1024]{1,0:T(1,128)} %bitcast.16, s32[1,1024]{1,0:T(1,128)} %bitcast.17, ...), custom_call_target="tpu_custom_call" | custom-call | flops 134217728 | bytes 1228800 | tf_op jit(solution)/shard_map/pallas_call | solution.py:234
  2.2 3.1 %collective-permute-start = (bf16[264,256]{1,0:T(8,128)(2,1)S(1)}, bf16[264,256]{1,0:T(8,128)(2,1)S(1)}, u32[]{:S(2)}, u32[]{:S(2)}) collective-permute-start(bf16[264,256]{1,0:T(8,128)(2,1)S(1)} %get-tuple-element.28), channel_id=1, source_target_pairs={{0,4},{1,5},{4,8},{5,9},{8,12},{9,13},{12,0},{13,1},{2,6},{3,7},{6... | collective-permute-start | bytes 405512 | tf_op jit(solution)/shard_map/ppermute | solution.py:229
  5.3 0.0 copy-start.7
  5.3 0.0 copy-start
  5.3 1.0 %shard_map.116 = (bf16[264,256]{1,0:T(8,128)(2,1)S(1)}, bf16[264,256]{1,0:T(8,128)(2,1)S(1)}, bf16[264,256]{1,0:T(8,128)(2,1)S(1)}) custom-call(s32[1,1024]{1,0:T(1,128)S(1)} %get-tuple-element.24.refs_0_, bf16[8,1024]{1,0:T(8,128)(2,1)S(1)} %get-tuple-element.25.refs_1_, bf16[1024,256]{1,0:T(8,128)(2,1)S(1)} %get-tuple-element.26.refs_2_), custom_call_target="tpu_custom_call" | custom-call | flops 4294967296 | bytes 950272 | tf_op jit(solution)/shard_map/pallas_call | solution.py:234
  6.3 0.0 copy-start.2
  6.3 2.1 %collective-permute-start.1 = (bf16[264,256]{1,0:T(8,128)(2,1)S(1)}, bf16[264,256]{1,0:T(8,128)(2,1)S(1)}, u32[]{:S(2)}, u32[]{:S(2)}) collective-permute-start(bf16[264,256]{1,0:T(8,128)(2,1)S(1)} %get-tuple-element.29), channel_id=1, source_target_pairs={{0,12},{1,13},{4,0},{5,1},{8,4},{9,5},{12,8},{13,9},{2,14},{3,15},... | collective-permute-start | bytes 405512 | tf_op jit(solution)/shard_map/ppermute | solution.py:229
  8.4 1.0 %collective-permute-start.2 = (bf16[264,256]{1,0:T(8,128)(2,1)S(1)}, bf16[264,256]{1,0:T(8,128)(2,1)S(1)}, u32[]{:S(2)}, u32[]{:S(2)}) collective-permute-start(bf16[264,256]{1,0:T(8,128)(2,1)S(1)} %get-tuple-element.34), channel_id=1, source_target_pairs={{0,8},{1,9},{4,12},{5,13},{8,0},{9,1},{12,4},{13,5},{2,10},{3,11},... | collective-permute-start | bytes 405512 | tf_op jit(solution)/shard_map/ppermute | solution.py:229
  9.4 0.8 %collective-permute-start.3 = (bf16[264,256]{1,0:T(8,128)(2,1)S(1)}, bf16[264,256]{1,0:T(8,128)(2,1)S(1)}, u32[]{:S(2)}, u32[]{:S(2)}) collective-permute-start(bf16[264,256]{1,0:T(8,128)(2,1)S(1)} %get-tuple-element.35), channel_id=1, source_target_pairs={{0,9},{1,8},{4,13},{5,12},{8,1},{9,0},{12,5},{13,4},{2,11},{3,10},... | collective-permute-start | bytes 405512 | tf_op jit(solution)/shard_map/ppermute | solution.py:229
  10.2 1.2 %shard_map.114 = (bf16[264,256]{1,0:T(8,128)(2,1)S(1)}, bf16[264,256]{1,0:T(8,128)(2,1)S(1)}, bf16[264,256]{1,0:T(8,128)(2,1)S(1)}, bf16[264,256]{1,0:T(8,128)(2,1)S(1)}) custom-call(s32[1,1024]{1,0:T(1,128)S(1)} %get-tuple-element.24.refs_0_, bf16[8,1024]{1,0:T(8,128)(2,1)S(1)} %get-tuple-element.25.refs_1_, bf16[1024,256]{1,0:T(8,128)(2,1)S(1)} %get-tuple-element.26.refs_2_), custom_call_target="tpu_custom_call" | custom-call | tf_op jit(solution)/shard_map/pallas_call | solution.py:234
  11.4 1.3 %collective-permute-start.4 = (bf16[264,256]{1,0:T(8,128)(2,1)S(1)}, bf16[264,256]{1,0:T(8,128)(2,1)S(1)}, u32[]{:S(2)}, u32[]{:S(2)}) collective-permute-start(bf16[264,256]{1,0:T(8,128)(2,1)S(1)} %get-tuple-element.36), channel_id=1, source_target_pairs={{0,1},{1,0},{4,5},{5,4},{8,9},{9,8},{12,13},{13,12},{2,3},{3,2},{6... | collective-permute-start | bytes 405512 | tf_op jit(solution)/shard_map/ppermute | solution.py:229
  12.7 0.0 collective-permute-done.refs_1_.refs_3_
  12.7 1.7 %collective-permute-start.5 = (bf16[264,256]{1,0:T(8,128)(2,1)S(1)}, bf16[264,256]{1,0:T(8,128)(2,1)S(1)}, u32[]{:S(2)}, u32[]{:S(2)}) collective-permute-start(bf16[264,256]{1,0:T(8,128)(2,1)S(1)} %get-tuple-element.40), channel_id=1, source_target_pairs={{0,13},{1,12},{4,1},{5,0},{8,5},{9,4},{12,9},{13,8},{2,15},{3,14},... | collective-permute-start | bytes 405512 | tf_op jit(solution)/shard_map/ppermute | solution.py:229
  14.4 0.0 collective-permute-done.1.refs_2_.refs_4_
  14.4 0.4 collective-permute-start.6
  14.8 0.0 copy-done.7
  14.8 0.0 copy-done
  14.8 1.2 %shard_map.115 = f32[1,1024]{1,0:T(1,128)S(1)} custom-call(bf16[264,256]{1,0:T(8,128)(2,1)S(1)} %get-tuple-element.27.place.refs_3_.refs_5_, f32[1,2048]{1,0:T(1,128)S(1)} %bitcast.8, bf16[1024,2048]{1,0:T(8,128)(2,1)S(1)} %copy-done), custom_call_target="tpu_custom_call" | custom-call | tf_op jit(solution)/shard_map/pallas_call | solution.py:234
  16.0 4.9 %psum.7.refs_4_.refs_5_ = f32[1,1024]{1,0:T(1,128)S(1)} all-reduce(f32[1,1024]{1,0:T(1,128)S(1)} %shard_map.115), channel_id=1, replica_groups=mesh['groups'=2,'rows'=4,'feat'=2,'ent'=2] {'feat'}, use_global_device_ids=true, to_apply=%region_0.0 | all-reduce | flops 1024 | bytes 8192 | tf_op jit(solution)/shard_map/psum | solution.py:322
  20.9 0.0 copy-done.2
  20.9 0.6 %shard_map.117 = (bf16[1024,256]{1,0:T(8,128)(2,1)S(1)}, f32[1,256]{1,0:T(1,128)S(1)}, f32[1,256]{1,0:T(1,128)S(1)}, f32[1,256]{1,0:T(1,128)S(1)}) custom-call(f32[512,256]{1,0:T(8,128)S(1)} %copy-done.2, bf16[264,256]{1,0:T(8,128)(2,1)S(1)} %collective-permute-done.refs_1_.refs_3_, bf16[264,256]{1,0:T(8,128)(2,1)S(1)} %collective-permute-done.1.refs_2_.refs_4_, ...), custom_call_target="tpu_custom_call" | custom-call | tf_op jit(solution)/shard_map/pallas_call | solution.py:234
  21.6 4.0 %collective-permute-done.2.refs_1_.refs_6_ = bf16[264,256]{1,0:T(8,128)(2,1)S(1)} collective-permute-done((bf16[264,256]{1,0:T(8,128)(2,1)S(1)}, bf16[264,256]{1,0:T(8,128)(2,1)S(1)}, u32[]{:S(2)}, u32[]{:S(2)}) %collective-permute-start.2) | collective-permute-done | bytes 135200 | tf_op jit(solution)/shard_map/ppermute | solution.py:229
  25.5 2.6 %collective-permute-done.3.refs_2_.refs_7_ = bf16[264,256]{1,0:T(8,128)(2,1)S(1)} collective-permute-done((bf16[264,256]{1,0:T(8,128)(2,1)S(1)}, bf16[264,256]{1,0:T(8,128)(2,1)S(1)}, u32[]{:S(2)}, u32[]{:S(2)}) %collective-permute-start.3) | collective-permute-done | bytes 135200 | tf_op jit(solution)/shard_map/ppermute | solution.py:229
  28.1 0.0 collective-permute-done.4.refs_3_.refs_8_
  28.1 0.6 %shard_map.118 = (f32[1,256]{1,0:T(1,128)S(1)}, f32[1,256]{1,0:T(1,128)S(1)}, f32[1,256]{1,0:T(1,128)S(1)}) custom-call(bf16[1024,256]{1,0:T(8,128)(2,1)S(1)} %get-tuple-element.30.refs_0_, bf16[264,256]{1,0:T(8,128)(2,1)S(1)} %collective-permute-done.2.refs_1_.refs_6_, bf16[264,256]{1,0:T(8,128)(2,1)S(1)} %collective-permute-done.3.refs_2_.refs_7_, ...), custom_call_target="tpu_custom_call" | custom-call | tf_op jit(solution)/shard_map/pallas_call | solution.py:234
  28.7 0.0 collective-permute-done.5.refs_7_.refs_9_
  28.7 0.0 collective-permute-done.6.refs_8_.refs_10_
  28.8 0.0 copy-start.1
  28.8 0.0 copy-start.3
  28.8 0.0 copy-start.4
  28.8 0.0 copy-start.5
  28.8 0.0 copy-start.6
  28.8 0.5 shard_map.119
  29.3 12.0 %all_to_all.10.refs_6_ = f32[16,1,256]{2,1,0:T(1,128)S(1)} all-to-all(f32[16,1,256]{2,1,0:T(1,128)S(1)} %shard_map.119), channel_id=1, replica_groups=mesh['groups'=2,'rows'=4,'feat'=2,'ent'=2] {'rows','feat','ent'}, dimensions={0} | all-to-all | bytes 32768 | tf_op jit(solution)/shard_map/all_to_all | solution.py:349
  41.3 0.0 copy-done.1
  41.3 0.0 copy-done.3
  41.3 0.0 copy-done.4
  41.3 0.0 copy-done.5
  41.3 0.0 copy-done.6
  41.3 1.0 %shard_map.120 = f32[8,1,2304]{2,1,0:T(1,128)S(1)} custom-call(s32[1,1024]{1,0:T(1,128)S(1)} %bitcast.11, s32[1,1024]{1,0:T(1,128)S(1)} %bitcast.13, s32[2,1024]{1,0:T(2,128)S(1)} %get-tuple-element.23.refs_2_, s32[1,1024]{1,0:T(1,128)S(1)} %bitcast.14, s32[1,1024]{1,0:T(1,128)S(1)} %bitcast.15, f32[1,1024]{1,0:T(1,128)S(1)} %psum.7.refs_4_.refs_5_, ...), custom_call_target="tpu_custom_call" | custom-call | flops 67108864 | bytes 4313088 | tf_op jit(solution)/shard_map/pallas_call | solution.py:234
  42.4 8.4 %all_to_all.11.refs_2_ = f32[8,1,2304]{2,1,0:T(1,128)S(1)} all-to-all(f32[8,1,2304]{2,1,0:T(1,128)S(1)} %shard_map.120), channel_id=1, replica_groups=mesh['groups'=2,'rows'=4,'feat'=2,'ent'=2] {'rows','ent'}, dimensions={0} | all-to-all | bytes 147456 | tf_op jit(solution)/shard_map/all_to_all | solution.py:366
  50.8 2.1 %shard_map.121 = (f32[1,2048]{1,0:T(1,128)}, f32[512,256]{1,0:T(8,128)}) custom-call(f32[512,256]{1,0:T(8,128)S(1)} %copy-done.2, f32[1,2048]{1,0:T(1,128)S(1)} %bitcast.9, f32[8,1,2304]{2,1,0:T(1,128)S(1)} %all_to_all.11.refs_2_, bf16[264,256]{1,0:T(8,128)(2,1)S(1)} %collective-permute-done.refs_1_.refs_3_, ...), custom_call_target="tpu_custom_call" | custom-call | flops 1073741824 | bytes 2220032 | tf_op jit(solution)/shard_map/pallas_call | solution.py:234
  (1 shorter events, 0.0 us)
Async XLA Ops:
  2.2 10.5 %collective-permute-start = (bf16[264,256]{1,0:T(8,128)(2,1)S(1)}, bf16[264,256]{1,0:T(8,128)(2,1)S(1)}, u32[]{:S(2)}, u32[]{:S(2)}) collective-permute-start(bf16[264,256]{1,0:T(8,128)(2,1)S(1)} %get-tuple-element.28), channel_id=1, source_target_pairs={{0,4},{1,5},{4,8},{5,9},{8,12},{9,13},{12,0},{13,1},{2,6},{3,7},{6... | collective-permute-start | bytes 405512 | tf_op jit(solution)/shard_map/ppermute | solution.py:229
  5.3 9.5 %copy-start.7 = (bf16[2048]{0:T(1024)(128)(2,1)S(1)}, bf16[2048]{0:T(1024)(128)(2,1)}, u32[]{:S(2)}) copy-start(bf16[2048]{0:T(1024)(128)(2,1)} %param.11) | copy-start | bytes 12292
  5.3 9.5 %copy-start = (bf16[1024,2048]{1,0:T(8,128)(2,1)S(1)}, bf16[1024,2048]{1,0:T(8,128)(2,1)}, u32[]{:S(2)}) copy-start(bf16[1024,2048]{1,0:T(8,128)(2,1)} %refs_7_.1) | copy-start | bytes 12582916
  6.3 14.7 %copy-start.2 = (f32[512,256]{1,0:T(8,128)S(1)}, f32[512,256]{1,0:T(8,128)}, u32[]{:S(2)}) copy-start(f32[512,256]{1,0:T(8,128)} %refs_0_.3) | copy-start | bytes 1572868
  6.3 8.1 %collective-permute-start.1 = (bf16[264,256]{1,0:T(8,128)(2,1)S(1)}, bf16[264,256]{1,0:T(8,128)(2,1)S(1)}, u32[]{:S(2)}, u32[]{:S(2)}) collective-permute-start(bf16[264,256]{1,0:T(8,128)(2,1)S(1)} %get-tuple-element.29), channel_id=1, source_target_pairs={{0,12},{1,13},{4,0},{5,1},{8,4},{9,5},{12,8},{13,9},{2,14},{3,15},... | collective-permute-start | bytes 405512 | tf_op jit(solution)/shard_map/ppermute | solution.py:229
  8.4 17.2 %collective-permute-start.2 = (bf16[264,256]{1,0:T(8,128)(2,1)S(1)}, bf16[264,256]{1,0:T(8,128)(2,1)S(1)}, u32[]{:S(2)}, u32[]{:S(2)}) collective-permute-start(bf16[264,256]{1,0:T(8,128)(2,1)S(1)} %get-tuple-element.34), channel_id=1, source_target_pairs={{0,8},{1,9},{4,12},{5,13},{8,0},{9,1},{12,4},{13,5},{2,10},{3,11},... | collective-permute-start | bytes 405512 | tf_op jit(solution)/shard_map/ppermute | solution.py:229
  9.4 18.7 %collective-permute-start.3 = (bf16[264,256]{1,0:T(8,128)(2,1)S(1)}, bf16[264,256]{1,0:T(8,128)(2,1)S(1)}, u32[]{:S(2)}, u32[]{:S(2)}) collective-permute-start(bf16[264,256]{1,0:T(8,128)(2,1)S(1)} %get-tuple-element.35), channel_id=1, source_target_pairs={{0,9},{1,8},{4,13},{5,12},{8,1},{9,0},{12,5},{13,4},{2,11},{3,10},... | collective-permute-start | bytes 405512 | tf_op jit(solution)/shard_map/ppermute | solution.py:229
  11.4 16.7 %collective-permute-start.4 = (bf16[264,256]{1,0:T(8,128)(2,1)S(1)}, bf16[264,256]{1,0:T(8,128)(2,1)S(1)}, u32[]{:S(2)}, u32[]{:S(2)}) collective-permute-start(bf16[264,256]{1,0:T(8,128)(2,1)S(1)} %get-tuple-element.36), channel_id=1, source_target_pairs={{0,1},{1,0},{4,5},{5,4},{8,9},{9,8},{12,13},{13,12},{2,3},{3,2},{6... | collective-permute-start | bytes 405512 | tf_op jit(solution)/shard_map/ppermute | solution.py:229
  12.7 16.0 %collective-permute-start.5 = (bf16[264,256]{1,0:T(8,128)(2,1)S(1)}, bf16[264,256]{1,0:T(8,128)(2,1)S(1)}, u32[]{:S(2)}, u32[]{:S(2)}) collective-permute-start(bf16[264,256]{1,0:T(8,128)(2,1)S(1)} %get-tuple-element.40), channel_id=1, source_target_pairs={{0,13},{1,12},{4,1},{5,0},{8,5},{9,4},{12,9},{13,8},{2,15},{3,14},... | collective-permute-start | bytes 405512 | tf_op jit(solution)/shard_map/ppermute | solution.py:229
  14.4 14.3 %collective-permute-start.6 = (bf16[264,256]{1,0:T(8,128)(2,1)S(1)}, bf16[264,256]{1,0:T(8,128)(2,1)S(1)}, u32[]{:S(2)}, u32[]{:S(2)}) collective-permute-start(bf16[264,256]{1,0:T(8,128)(2,1)S(1)} %get-tuple-element.41), channel_id=1, source_target_pairs={{0,5},{1,4},{4,9},{5,8},{8,13},{9,12},{12,1},{13,0},{2,7},{3,6},{6... | collective-permute-start | bytes 405512 | tf_op jit(solution)/shard_map/ppermute | solution.py:229
  28.8 12.5 %copy-start.1 = (bf16[1024,2048]{1,0:T(8,128)(2,1)S(1)}, bf16[1024,2048]{1,0:T(8,128)(2,1)}, u32[]{:S(2)}) copy-start(bf16[1024,2048]{1,0:T(8,128)(2,1)} %refs_7_.1) | copy-start | bytes 12582916
  28.8 12.5 %copy-start.3 = (s32[1024,1]{0,1:T(1,128)S(1)}, s32[1024,1]{0,1:T(1,128)}, u32[]{:S(2)}) copy-start(s32[1024,1]{0,1:T(1,128)} %param.14) | copy-start | bytes 12292
  28.8 12.5 %copy-start.4 = (s32[1024,1]{0,1:T(1,128)S(1)}, s32[1024,1]{0,1:T(1,128)}, u32[]{:S(2)}) copy-start(s32[1024,1]{0,1:T(1,128)} %param.16) | copy-start | bytes 12292
  28.8 12.5 %copy-start.5 = (s32[1024]{0:T(1024)S(1)}, s32[1024]{0:T(1024)}, u32[]{:S(2)}) copy-start(s32[1024]{0:T(1024)} %param.18) | copy-start | bytes 12292
  28.8 12.5 %copy-start.6 = (s32[1024]{0:T(1024)S(1)}, s32[1024]{0:T(1024)}, u32[]{:S(2)}) copy-start(s32[1024]{0:T(1024)} %param.19) | copy-start | bytes 12292
